TPU v7x, 128 devices: a whole 4x4x4 slice. The times are simulated.
128 devices in a mesh: dp: 16 (over z, x), mp: 8 (over y, core).
Axes of the slice: x: 4, y: 4, z: 4, core: 2. Of those that a mesh axis runs over, the one named last changes fastest.
Arguments:
- gradient: bfloat16 [16, 2560, 10240], P('dp', 'mp')
- error: bfloat16 [16, 2560, 10240], P('dp', 'mp'), may hold values from -3 to 3
- q_start: bfloat16 [64, 10240], replicated, may hold values from -6 to 6
Outputs:
- new_error: bfloat16 [16, 2560, 10240], P('dp', 'mp')
- p_hat: float32 [64, 2560], P(None, 'mp')
- q_new: float32 [64, 10240], replicated
All inputs are finite; a program needn't handle non-finite values.
Results may differ from a plain program's by a relative error of at most 0.012.
Values sent between devices are 32-bit elements; how exact they have to be, the bound alone decides.
No kernel may reach another device: no remote copies, remote signals or barrier semaphores. Data moves between devices by JAX's collectives and lax.ppermute only.
A program may use at most 64 MiB of HBM per device.

v0:
```python
import jax
import jax.numpy as jnp
from jax import lax
from jax.sharding import PartitionSpec as P


def body(gradient, error, q_start):
    merged = (gradient[0].astype(jnp.float32) + error[0].astype(jnp.float32)).astype(jnp.bfloat16)
    replicas = lax.axis_size("dp")
    local_left = lax.dot_general(
        q_start, merged, (((1,), (1,)), ((), ())), preferred_element_type=jnp.float32
    )
    p_mean = lax.psum(local_left, "dp") / replicas
    own_gram = jnp.dot(p_mean, p_mean.T, precision=lax.Precision.HIGHEST)
    gram = lax.psum(own_gram, "mp")
    lower = jnp.linalg.cholesky(gram)
    p_hat = lax.linalg.triangular_solve(lower, p_mean, left_side=True, lower=True)
    p_low = p_hat.astype(jnp.bfloat16)
    local_right = jnp.dot(p_low, merged, preferred_element_type=jnp.float32)
    q_new = lax.psum(local_right, ("dp", "mp")) / replicas
    q_low = q_new.astype(jnp.bfloat16)
    decoded = lax.dot_general(
        p_low, q_low, (((0,), (0,)), ((), ())), preferred_element_type=jnp.float32
    )
    new_error = (merged.astype(jnp.float32) - decoded).astype(jnp.bfloat16)
    return (new_error[None], p_hat, q_new)


def solution(mesh):
    return jax.shard_map(
        body,
        mesh=mesh,
        in_specs=(P("dp", "mp", None), P("dp", "mp", None), P()),
        out_specs=(P("dp", "mp", None), P(None, "mp"), P()),
        check_vma=False,
    )
```

profile of v0, /device:TPU:1, one launch (start us, length us, event | category | flops | bytes accessed | tf_op | source)
XLA Modules:
  0.0 313.9 jit_solution(10044238528964253917)
XLA Ops:
  7.2 0.0 copy-start
  7.2 0.0 all-reduce.3.cloned.1.call-start
  7.2 1.3 copy-done
  8.5 7.4 %convolution_bitcast_fusion = f32[64,320]{1,0:T(8,128)} fusion(bf16[64,10240]{1,0:T(8,128)(2,1)S(1)} %copy-done, bf16[1,320,10240]{2,1,0:T(8,128)(2,1)} %param.4, bf16[1,320,10240]{2,1,0:T(8,128)(2,1)} %param.3), kind=kOutput, calls=%fused_computation.7 | convolution fusion | flops 432537600 | bytes 14499840 | tf_op jit(solution)/shard_map/dot_general | solution.py:10
  15.9 0.0 all-reduce.3.cloned.1.call-update
  15.9 0.0 all-reduce.5.cloned.1.call-start
  16.0 83.8 %all-reduce.3.cloned.1.call-done = f32[64,320]{1,0:T(8,128)} async-done(((f32[64,320]{1,0:T(8,128)}), f32[64,320]{1,0:T(8,128)}) %all-reduce.3.cloned.1.call-update) | async-done | bytes 81936 | tf_op jit(solution)/shard_map/psum | solution.py:13
  99.8 1.2 fusion.6
  101.0 22.7 %psum.22 = f32[64,64]{0,1:T(8,128)S(1)} all-reduce(f32[64,64]{0,1:T(8,128)S(1)} %fusion.6), channel_id=1, replica_groups=mesh['dp'=16,'mp'=8] {'mp'}, use_global_device_ids=true, to_apply=%region_1.0 | all-reduce | flops 4096 | bytes 32768 | tf_op jit(solution)/shard_map/psum | solution.py:15
  123.7 0.1 copy.7
  123.8 5.8 %cholesky.16 = f32[64,64]{1,0:T(8,128)S(1)} custom-call(f32[64,64]{1,0:T(8,128)S(1)} %fusion.12), custom_call_target="Cholesky" | custom-call | tf_op jit(solution)/shard_map/jit(cholesky)/cholesky | solution.py:16
  129.7 0.6 compare_reduce_fusion
  130.3 0.7 fusion.10
  131.0 4.9 %custom-call.6 = f32[1,64,64]{1,2,0:T(8,128)S(1)} custom-call(f32[1,64,64]{2,1,0:T(8,128)S(1)} %fusion.10), custom_call_target="InvertDiagBlocksLowerTriangular" | custom-call | tf_op jit(solution)/shard_map/triangular_solve | solution.py:17
  135.9 1.2 fusion.4
  137.1 0.0 copy-start.2
  137.1 8.3 %fusion.14 = f32[64,10240]{1,0:T(8,128)} fusion(f32[64,320]{1,0:T(8,128)S(1)} %fusion.4, bf16[1,320,10240]{2,1,0:T(8,128)(2,1)} %param.4, bf16[1,320,10240]{2,1,0:T(8,128)(2,1)} %param.3), kind=kOutput, calls=%fused_computation.23 | convolution fusion | flops 432558080 | bytes 15810560 | tf_op jit(solution)/shard_map/dot_general | solution.py:19
  145.4 0.0 all-reduce.5.cloned.1.call-update
  145.4 151.0 %all-reduce.5.cloned.1.call-done = f32[64,10240]{1,0:T(8,128)} async-done(((f32[64,10240]{1,0:T(8,128)}), f32[64,10240]{1,0:T(8,128)}) %all-reduce.5.cloned.1.call-update) | async-done | bytes 2621456 | tf_op jit(solution)/shard_map/psum | solution.py:20
  296.4 1.9 broadcast_multiply_fusion
  298.4 0.0 copy-done.2
  298.4 0.0 copy-start.1
  298.4 8.6 %fusion.1 = bf16[1,320,10240]{2,1,0:T(8,128)(2,1)} fusion(f32[64,10240]{1,0:T(8,128)S(1)} %broadcast_multiply_fusion, f32[64,320]{1,0:T(8,128)S(1)} %fusion.4, bf16[1,320,10240]{2,1,0:T(8,128)(2,1)} %param.4, bf16[1,320,10240]{2,1,0:T(8,128)(2,1)} %param.3), kind=kOutput, calls=%fused_computation.3 | convolution fusion | flops 443043840 | bytes 22364160 | tf_op jit(solution)/shard_map/dot_general | solution.py:22
  307.0 0.0 copy-done.1
  (2 shorter events, 0.0 us)
Async XLA Ops:
  7.2 1.3 copy-start
  7.2 92.6 %all-reduce.3.cloned.1.call-start = ((), (), s32[]{:S(2)}) async-start(), calls=%async_computation | async-start | bytes 196608 | tf_op jit(solution)/shard_map/psum | solution.py:13
  15.9 280.5 %all-reduce.5.cloned.1.call-start = ((), (), s32[]{:S(2)}) async-start(), calls=%async_computation.1 | async-start | bytes 5242880 | tf_op jit(solution)/shard_map/psum | solution.py:20
  137.1 161.3 %copy-start.2 = (f32[64,320]{1,0:T(8,128)}, f32[64,320]{1,0:T(8,128)S(1)}, u32[]{:S(2)}) copy-start(f32[64,320]{1,0:T(8,128)S(1)} %fusion.4) | copy-start | bytes 245764
  298.4 8.6 %copy-start.1 = (f32[64,10240]{1,0:T(8,128)}, f32[64,10240]{1,0:T(8,128)S(1)}, u32[]{:S(2)}) copy-start(f32[64,10240]{1,0:T(8,128)S(1)} %broadcast_multiply_fusion) | copy-start | bytes 7864324
Sparse Core Ops, SparseCore 0:
  16.0 83.6 all-reduce.2
  145.5 150.8 all-reduce.4
where the time goes:
time: 314 us
  waiting for transfers between devices  235 us (75%)
  matrix products  26.7 us (9%)
  blocking collectives  22.7 us (7%)
  between operations  14.1 us (4%)
  other arithmetic  14 us (4%)
    psum x1, waiting for transfers between devices, body(): q_new = lax.psum(local_right, ('dp', 'mp')) / replicas  151 us
    psum x1, waiting for transfers between devices, body(): p_mean = lax.psum(local_left, 'dp') / replicas  83.8 us
    psum x1, blocking collectives, body(): gram = lax.psum(own_gram, 'mp')  22.7 us
    dot_general x1, matrix products, body(): lax.dot_general(p_low, q_low, (((0,), (0,)), ((), ())), preferred_element...  8.63 us
    dot_general x1, matrix products, body(): local_right = jnp.dot(p_low, merged, preferred_element_type=jnp.float32)  8.25 us
    dot_general x1, matrix products, body(): lax.dot_general(q_start, merged, (((1,), (1,)), ((), ())), preferred_elem...  7.4 us
    another operation x3, other arithmetic, body(): lower = jnp.linalg.cholesky(gram)  6.52 us
  transfers between devices with their start and end apart: 2, of which 2 were waited for; matrix products, arithmetic and copies ran while one was open for 0% of the time, Pallas kernels for 0%

commit v1 on v0

v1 whole, which is shorter than its diff:
```python
import jax
import jax.numpy as jnp
from jax import lax
from jax.sharding import Mesh, PartitionSpec as P

DP = ("z", "x")
HIGHEST = lax.Precision.HIGHEST


def shifts(value, axis):
    n = lax.axis_size(axis)
    return [
        lax.ppermute(value, axis, [(i, (i + k) % n) for i in range(n)]) for k in range(1, n)
    ]


def swap(value):
    return lax.ppermute(value, "c", [(0, 1), (1, 0)])


def body(gradient, error, q_start):
    merged = (gradient[0].astype(jnp.float32) + error[0].astype(jnp.float32)).astype(jnp.bfloat16)
    rank, columns = q_start.shape
    replicas = lax.axis_size(DP)
    half = columns // 2
    core = lax.axis_index("c")
    rows = 8
    groups = rank // rows
    cuts = replicas // groups

    p = lax.dot_general(
        q_start, merged, (((1,), (1,)), ((), ())), preferred_element_type=jnp.float32
    )
    p = p + sum(shifts(p, "x"))
    p = (p + sum(shifts(p, "z"))) / replicas

    peak = jnp.max(jnp.abs(p))
    peak = jnp.where(peak > 0, peak, 1.0)
    own_gram = jnp.dot(p, p.T, precision=HIGHEST)
    packed = jnp.concatenate([own_gram, jnp.full_like(own_gram, peak)], axis=1)
    other = swap(packed)
    other_peak = other[0, rank]
    pair_peak = jnp.maximum(peak, other_peak)
    packed = jnp.concatenate(
        [own_gram + other[:, :rank], jnp.full_like(own_gram, pair_peak)], axis=1
    )
    across = shifts(packed, "y")
    gram = packed[:, :rank] + sum(a[:, :rank] for a in across)
    peaks = [a[0, rank] for a in across]
    top = pair_peak
    for a in peaks:
        top = jnp.maximum(top, a)
    lower = jnp.linalg.cholesky(gram)
    inverse = lax.linalg.triangular_solve(
        lower, jnp.eye(rank, dtype=jnp.float32), left_side=True, lower=True
    )
    p_hat = jnp.dot(inverse, p, precision=HIGHEST)

    scaled = p / peak
    sent = lax.dynamic_slice_in_dim(merged, (1 - core) * half, half, axis=1)
    kept = lax.dynamic_slice_in_dim(merged, core * half, half, axis=1)
    right_sent = jnp.dot(scaled, sent.astype(jnp.float32), precision=HIGHEST)
    received = swap(right_sent)
    right_kept = jnp.dot(scaled, kept.astype(jnp.float32), precision=HIGHEST)
    right = right_kept * (peak / pair_peak) + received * (other_peak / pair_peak)
    right = right.reshape(groups, rows, cuts, half // cuts).transpose(0, 2, 1, 3)
    right = lax.all_to_all(right.reshape(replicas, rows, half // cuts), DP, 0, 0)
    right = jnp.sum(right, axis=0)
    total = right * (pair_peak / top)
    for a, b in zip(shifts(right, "y"), peaks):
        total = total + a * (b / top)
    total = lax.all_to_all(jnp.broadcast_to(total[None], (replicas,) + total.shape), DP, 0, 0)
    mine = total.reshape(groups, cuts, rows, half // cuts).transpose(0, 2, 1, 3).reshape(rank, half)
    theirs = swap(mine)
    solve = inverse * (top / replicas)
    q_mine = jnp.dot(solve, mine, precision=HIGHEST)
    q_theirs = jnp.dot(solve, theirs, precision=HIGHEST)
    q_new = jnp.where(
        core == 0,
        jnp.concatenate([q_mine, q_theirs], axis=1),
        jnp.concatenate([q_theirs, q_mine], axis=1),
    )
    decoded = lax.dot_general(
        p_hat.astype(jnp.bfloat16),
        q_new.astype(jnp.bfloat16),
        (((0,), (0,)), ((), ())),
        preferred_element_type=jnp.float32,
    )
    new_error = (merged.astype(jnp.float32) - decoded).astype(jnp.bfloat16)
    return (new_error[None], p_hat, q_new)


def solution(mesh):
    fine = Mesh(mesh.devices.reshape(4, 4, 4, 2), ("z", "x", "y", "c"))
    return jax.shard_map(
        body,
        mesh=fine,
        in_specs=(P(DP, ("y", "c"), None), P(DP, ("y", "c"), None), P()),
        out_specs=(P(DP, ("y", "c"), None), P(None, ("y", "c")), P()),
        check_vma=False,
    )
```

time: 314 us -> 146 us (0.46)
  waiting for transfers between devices: 235 us -> 36.5 us
  starting transfers between devices: 0.08 us -> 26.6 us
  other arithmetic: 14 us -> 23.4 us
  between operations: 14.1 us -> 7.41 us
    psum x2 -> x0, waiting for transfers between devices: 235 us -> none  [the longest x1 151 us: body(): q_new = lax.psum(local_right, ('dp', 'mp')) / replicas]
    ppermute x0 -> x15, starting transfers between devices: none -> 22.9 us  [the longest x12 16.1 us: shifts(): lax.ppermute(value, axis, [(i, (i + k) % n) for i in range(n)])]
    psum x1 -> x0, blocking collectives: 22.7 us -> none  [body(): gram = lax.psum(own_gram, 'mp')]
    all_to_all x0 -> x1, blocking collectives: none -> 22.2 us  [body(): lax.all_to_all(right.reshape(replicas, rows, half // cuts), DP, 0, 0)]
    ppermute x0 -> x15, waiting for transfers between devices: none -> 19.3 us  [the longest x12 16.9 us: shifts(): lax.ppermute(value, axis, [(i, (i + k) % n) for i in range(n)])]
    all_to_all x0 -> x1, waiting for transfers between devices: none -> 17.2 us  [body(): lax.all_to_all(jnp.broadcast_to(total[None], (replicas,) + total.shape),...]
    convert_element_type x0 -> x1, other arithmetic: none -> 10.3 us  [body(): (gradient[0].astype(jnp.float32) + error[0].astype(jnp.float32)).astype(j...]
    all_to_all x0 -> x1, starting transfers between devices: none -> 3.7 us  [body(): lax.all_to_all(jnp.broadcast_to(total[None], (replicas,) + total.shape),...]
  transfers between devices with their start and end apart: 2 -> 16, of which waited for: 2 -> 10; matrix products, arithmetic and copies ran while one was open for 0% -> 11% of each run, Pallas kernels for 0% -> 0%
where the time goes in v1:
time: 146 us
  waiting for transfers between devices  36.5 us (25%)
  starting transfers between devices  26.6 us (18%)
  matrix products  26.2 us (18%)
  other arithmetic  23.4 us (16%)
  blocking collectives  22.2 us (15%)
  between operations  7.41 us (5%)
  local copies, waits for them, and re-layouts  3.39 us (2%)
    all_to_all x1, blocking collectives, body(): lax.all_to_all(right.reshape(replicas, rows, half // cuts), DP, 0, 0)  22.2 us
    all_to_all x1, waiting for transfers between devices, body(): lax.all_to_all(jnp.broadcast_to(total[None], (replicas,) + total.shape),...  17.2 us
    ppermute x12, waiting for transfers between devices, shifts(): lax.ppermute(value, axis, [(i, (i + k) % n) for i in range(n)])  16.9 us
    ppermute x12, starting transfers between devices, shifts(): lax.ppermute(value, axis, [(i, (i + k) % n) for i in range(n)])  16.1 us
    convert_element_type x1, other arithmetic, body(): (gradient[0].astype(jnp.float32) + error[0].astype(jnp.float32)).astype(j...  10.3 us
    dot_general x1, matrix products, body(): lax.dot_general(p_hat.astype(jnp.bfloat16), q_new.astype(jnp.bfloat16), (...  8.49 us
    ppermute x3, starting transfers between devices, swap(): return lax.ppermute(value, 'c', [(0, 1), (1, 0)])  6.75 us
    another operation x3, other arithmetic, body(): lower = jnp.linalg.cholesky(gram)  6.52 us
  transfers between devices with their start and end apart: 16, of which 10 were waited for; matrix products, arithmetic and copies ran while one was open for 11% of the time, Pallas kernels for 0%

profile of v1, /device:TPU:1, one launch (start us, length us, event | category | flops | bytes accessed | tf_op | source)
XLA Modules:
  0.0 145.7 jit_solution(10819947603543983662)
XLA Ops:
  0.6 0.0 copy-start
  0.6 10.3 %add_convert_fusion = bf16[1,320,10240]{2,1,0:T(8,128)(2,1)} fusion(bf16[1,320,10240]{2,1,0:T(8,128)(2,1)} %param.4, bf16[1,320,10240]{2,1,0:T(8,128)(2,1)} %param.3), kind=kLoop, calls=%fused_computation.2 | loop fusion | flops 13107200 | bytes 19660800 | tf_op jit(solution)/shard_map/convert_element_type | solution.py:22
  10.9 0.0 copy-done
  10.9 4.9 %fusion.11 = f32[64,320]{1,0:T(8,128)S(1)} fusion(bf16[64,10240]{1,0:T(8,128)(2,1)S(1)} %copy-done, bf16[1,320,10240]{2,1,0:T(8,128)(2,1)} %add_convert_fusion), kind=kOutput, calls=%fused_computation.15 | convolution fusion | flops 419430400 | bytes 7946240 | tf_op jit(solution)/shard_map/dot_general | solution.py:31
  15.8 3.4 %collective-permute-start.2 = (f32[64,320]{1,0:T(8,128)S(1)}, f32[64,320]{1,0:T(8,128)S(1)}, u32[]{:S(2)}, u32[]{:S(2)}) collective-permute-start(f32[64,320]{1,0:T(8,128)S(1)} %fusion.11), channel_id=1, source_target_pairs={{0,24},{8,0},{16,8},{24,16},{1,25},{9,1},{17,9},{25,17},{2,26},{10... | collective-permute-start | bytes 245768 | tf_op jit(solution)/shard_map/ppermute | solution.py:13
  19.2 0.5 collective-permute-start.1
  19.7 0.6 collective-permute-start
  20.3 0.5 collective-permute-done.2
  20.8 3.4 %collective-permute-done.1 = f32[64,320]{1,0:T(8,128)S(1)} collective-permute-done((f32[64,320]{1,0:T(8,128)S(1)}, f32[64,320]{1,0:T(8,128)S(1)}, u32[]{:S(2)}, u32[]{:S(2)}) %collective-permute-start.1) | collective-permute-done | bytes 81952 | tf_op jit(solution)/shard_map/ppermute | solution.py:13
  24.3 2.7 %collective-permute-done = f32[64,320]{1,0:T(8,128)S(1)} collective-permute-done((f32[64,320]{1,0:T(8,128)S(1)}, f32[64,320]{1,0:T(8,128)S(1)}, u32[]{:S(2)}, u32[]{:S(2)}) %collective-permute-start) | collective-permute-done | bytes 81952 | tf_op jit(solution)/shard_map/ppermute | solution.py:13
  26.9 3.8 %collective-permute-start.5 = (f32[64,320]{1,0:T(8,128)S(1)}, f32[64,320]{1,0:T(8,128)S(1)}, u32[]{:S(2)}, u32[]{:S(2)}) collective-permute-start(f32[64,320]{1,0:T(8,128)S(1)} %add_add_fusion), channel_id=1, source_target_pairs={{0,96},{32,0},{64,32},{96,64},{1,97},{33,1},{65,33},{97,65},{2,98}... | collective-permute-start | bytes 245768 | tf_op jit(solution)/shard_map/ppermute | solution.py:13
  30.8 0.0 collective-permute-start.4
  30.8 0.7 collective-permute-start.3
  31.5 2.2 %collective-permute-done.5 = f32[64,320]{1,0:T(8,128)S(1)} collective-permute-done((f32[64,320]{1,0:T(8,128)S(1)}, f32[64,320]{1,0:T(8,128)S(1)}, u32[]{:S(2)}, u32[]{:S(2)}) %collective-permute-start.5) | collective-permute-done | bytes 81952 | tf_op jit(solution)/shard_map/ppermute | solution.py:13
  33.7 2.1 %collective-permute-done.4 = f32[64,320]{1,0:T(8,128)S(1)} collective-permute-done((f32[64,320]{1,0:T(8,128)S(1)}, f32[64,320]{1,0:T(8,128)S(1)}, u32[]{:S(2)}, u32[]{:S(2)}) %collective-permute-start.4) | collective-permute-done | bytes 81952 | tf_op jit(solution)/shard_map/ppermute | solution.py:13
  35.8 1.3 collective-permute-done.3
  37.1 0.6 abs_reduce_fusion
  39.0 3.9 %fusion.5 = f32[64,5120]{1,0:T(8,128)S(1)} fusion(bf16[1,320,10240]{2,1,0:T(8,128)(2,1)} %add_convert_fusion, s32[]{:T(128)S(6)} %select_n.26, f32[64,320]{1,0:T(8,128)S(1)} %get-tuple-element.4, f32[]{:T(128)S(6)} %select_n.22), kind=kOutput, calls=%fused_computation.8 | convolution fusion | flops 1258311680 | bytes 4669448 | tf_op jit(solution)/shard_map/dot_general | solution.py:62
  43.0 2.3 %collective-permute-start.10 = (f32[64,5120]{1,0:T(8,128)S(1)}, f32[64,5120]{1,0:T(8,128)}, u32[]{:S(2)}, u32[]{:S(2)}) collective-permute-start(f32[64,5120]{1,0:T(8,128)S(1)} %fusion.5), channel_id=1, source_target_pairs={{0,1},{1,0},{2,3},{3,2},{4,5},{5,4},{6,7},{7,6},{8,9},{9,8},{10,11... | collective-permute-start | bytes 3932168 | tf_op jit(solution)/shard_map/ppermute | solution.py:18
  45.3 0.3 fusion.28
  45.5 0.1 collective-permute-start.6
  45.6 2.4 %collective-permute-done.6 = f32[64,128]{0,1:T(8,128)S(1)} collective-permute-done((f32[64,128]{0,1:T(8,128)S(1)}, f32[64,128]{0,1:T(8,128)S(1)}, u32[]{:S(2)}, u32[]{:S(2)}) %collective-permute-start.6) | collective-permute-done | bytes 32800 | tf_op jit(solution)/shard_map/ppermute | solution.py:18
  48.0 0.5 slice.43
  49.9 0.0 collective-permute-done.10
  49.9 4.4 %fusion.4 = f32[64,5120]{1,0:T(8,128)S(1)} fusion(bf16[1,320,10240]{2,1,0:T(8,128)(2,1)} %add_convert_fusion, s32[]{:T(128)S(6)} %select_n.25, f32[64,5120]{1,0:T(8,128)} %collective-permute-done.10, f32[]{:T(128)S(6)} %div.49, f32[]{:T(128)S(6)} %div.48, f32[64,320]{1,0:T(8,128)S(1)} %get-tuple-element.4, f32[]{:T(128)S(6)} %select_n.22), kind=kOutput, calls=%fused_computation.7 | convolution fusion | flops 1259294720 | bytes 5980176 | tf_op jit(solution)/shard_map/dot_general | solution.py:64
  54.3 22.2 %all_to_all.10 = f32[16,8,2560]{2,1,0:T(8,128)S(1)} all-to-all(f32[16,8,2560]{2,1,0:T(8,128)S(1)} %bitcast.48), channel_id=1, replica_groups=mesh['z'=4,'x'=4,'y'=4,'c'=2] {'z','x'}, dimensions={0} | all-to-all | bytes 2621440 | tf_op jit(solution)/shard_map/all_to_all | solution.py:67
  76.5 0.1 reduce_sum.9
  76.6 2.8 %collective-permute-start.13 = (f32[8,2560]{1,0:T(8,128)S(1)}, f32[8,2560]{1,0:T(8,128)S(1)}, u32[]{:S(2)}, u32[]{:S(2)}) collective-permute-start(f32[8,2560]{1,0:T(8,128)S(1)} %reduce_sum.9), channel_id=1, source_target_pairs={{0,6},{2,0},{4,2},{6,4},{1,7},{3,1},{5,3},{7,5},{8,14},{10,8},{12,... | collective-permute-start | bytes 245768 | tf_op jit(solution)/shard_map/ppermute | solution.py:13
  79.4 0.4 collective-permute-start.12
  79.8 0.7 collective-permute-start.11
  80.4 1.7 %collective-permute-start.7 = (f32[64,128]{0,1:T(8,128)S(1)}, f32[64,128]{0,1:T(8,128)S(1)}, u32[]{:S(2)}, u32[]{:S(2)}) collective-permute-start(f32[64,128]{0,1:T(8,128)S(1)} %concatenate.13), channel_id=1, source_target_pairs={{0,2},{2,4},{4,6},{6,0},{1,3},{3,5},{5,7},{7,1},{8,10},{10,12},{12... | collective-permute-start | bytes 98312 | tf_op jit(solution)/shard_map/ppermute | solution.py:13
  82.1 1.6 %collective-permute-start.8 = (f32[64,128]{0,1:T(8,128)S(1)}, f32[64,128]{0,1:T(8,128)S(1)}, u32[]{:S(2)}, u32[]{:S(2)}) collective-permute-start(f32[64,128]{0,1:T(8,128)S(1)} %concatenate.13), channel_id=1, source_target_pairs={{0,4},{2,6},{4,0},{6,2},{1,5},{3,7},{5,1},{7,3},{8,12},{10,14},{12... | collective-permute-start | bytes 98312 | tf_op jit(solution)/shard_map/ppermute | solution.py:13
  83.7 4.0 %collective-permute-done.7 = f32[64,128]{0,1:T(8,128)S(1)} collective-permute-done((f32[64,128]{0,1:T(8,128)S(1)}, f32[64,128]{0,1:T(8,128)S(1)}, u32[]{:S(2)}, u32[]{:S(2)}) %collective-permute-start.7) | collective-permute-done | bytes 32800 | tf_op jit(solution)/shard_map/ppermute | solution.py:13
  87.7 0.0 collective-permute-start.9
  87.7 0.5 slice.47
  88.8 0.0 collective-permute-done.8
  88.9 0.6 slice.48
  90.0 0.7 collective-permute-done.9
  90.8 0.5 slice.49
  93.9 0.0 collective-permute-done.13
  93.9 0.0 collective-permute-done.12
  94.0 0.0 collective-permute-done.11
  94.0 1.2 broadcast_in_dim.6
  95.2 3.7 %all-to-all-start.1 = ((f32[16,8,2560]{2,1,0:T(8,128)}), f32[16,8,2560]{2,1,0:T(8,128)S(1)}, u32[]{:S(2)}, u32[]{:S(2)}) async-start(f32[16,8,2560]{2,1,0:T(8,128)} %broadcast_in_dim.6), calls=%async_computation.1 | async-start | bytes 2621440 | tf_op jit(solution)/shard_map/all_to_all | solution.py:72
  98.9 0.1 copy.8
  99.0 17.2 %all-to-all-done.1 = f32[16,8,2560]{2,1,0:T(8,128)S(1)} async-done(((f32[16,8,2560]{2,1,0:T(8,128)}), f32[16,8,2560]{2,1,0:T(8,128)S(1)}, u32[]{:S(2)}, u32[]{:S(2)}) %all-to-all-start.1) | async-done | bytes 1310752 | tf_op jit(solution)/shard_map/all_to_all | solution.py:72
  116.2 4.4 %collective-permute-start.14 = (f32[64,5120]{1,0:T(8,128)S(1)}, f32[64,5120]{1,0:T(8,128)}, u32[]{:S(2)}, u32[]{:S(2)}) collective-permute-start(f32[64,5120]{1,0:T(8,128)S(1)} %bitcast.46), channel_id=1, source_target_pairs={{0,1},{1,0},{2,3},{3,2},{4,5},{5,4},{6,7},{7,6},{8,9},{9,8},{10,11... | collective-permute-start | bytes 3932168 | tf_op jit(solution)/shard_map/ppermute | solution.py:18
  120.5 5.8 %cholesky.17 = f32[64,64]{1,0:T(8,128)S(1)} custom-call(f32[64,64]{1,0:T(8,128)S(1)} %fusion.19), custom_call_target="Cholesky" | custom-call | tf_op jit(solution)/shard_map/jit(cholesky)/cholesky | solution.py:53
  126.4 0.6 compare_reduce_fusion
  127.0 0.7 fusion.15
  127.7 4.9 %custom-call.6 = f32[1,64,64]{1,2,0:T(8,128)S(1)} custom-call(f32[1,64,64]{2,1,0:T(8,128)S(1)} %fusion.15), custom_call_target="InvertDiagBlocksLowerTriangular" | custom-call | tf_op jit(solution)/shard_map/triangular_solve | solution.py:54
  132.6 0.2 fusion.17
  132.8 0.2 fusion.29
  133.1 0.0 copy-start.2
  133.1 1.3 fusion.22
  134.3 0.0 collective-permute-done.14
  134.4 2.5 %fusion.20 = f32[64,5120]{1,0:T(8,128)S(1)} fusion(f32[64,5120]{1,0:T(8,128)} %collective-permute-done.14, f32[64,64]{1,0:T(8,128)S(1)} %fusion.17, f32[]{:T(128)S(6)} %div.45), kind=kOutput, calls=%fused_computation.35 | convolution fusion | flops 251662336 | bytes 2637828 | tf_op jit(solution)/shard_map/dot_general | solution.py:77
  136.9 0.3 maximum_select_fusion
  137.2 0.0 copy-done.2
  137.2 0.0 copy-start.1
  137.2 8.5 %fusion.1 = bf16[1,320,10240]{2,1,0:T(8,128)(2,1)} fusion(bf16[1,320,10240]{2,1,0:T(8,128)(2,1)} %add_convert_fusion, f32[64,10240]{1,0:T(8,128)S(1)} %maximum_select_fusion, f32[64,320]{1,0:T(8,128)S(1)} %fusion.29), kind=kOutput, calls=%fused_computation.3 | convolution fusion | flops 429936640 | bytes 15810560 | tf_op jit(solution)/shard_map/dot_general | solution.py:83
  145.7 0.0 copy-done.1
  (8 shorter events, 0.1 us)
Async XLA Ops:
  0.6 10.3 %copy-start = (bf16[64,10240]{1,0:T(8,128)(2,1)S(1)}, bf16[64,10240]{1,0:T(8,128)(2,1)}, u32[]{:S(2)}) copy-start(bf16[64,10240]{1,0:T(8,128)(2,1)} %param.5) | copy-start | bytes 3932164
  15.8 5.0 %collective-permute-start.2 = (f32[64,320]{1,0:T(8,128)S(1)}, f32[64,320]{1,0:T(8,128)S(1)}, u32[]{:S(2)}, u32[]{:S(2)}) collective-permute-start(f32[64,320]{1,0:T(8,128)S(1)} %fusion.11), channel_id=1, source_target_pairs={{0,24},{8,0},{16,8},{24,16},{1,25},{9,1},{17,9},{25,17},{2,26},{10... | collective-permute-start | bytes 245768 | tf_op jit(solution)/shard_map/ppermute | solution.py:13
  19.2 5.1 %collective-permute-start.1 = (f32[64,320]{1,0:T(8,128)S(1)}, f32[64,320]{1,0:T(8,128)S(1)}, u32[]{:S(2)}, u32[]{:S(2)}) collective-permute-start(f32[64,320]{1,0:T(8,128)S(1)} %fusion.11), channel_id=1, source_target_pairs={{0,16},{8,24},{16,0},{24,8},{1,17},{9,25},{17,1},{25,9},{2,18},{10... | collective-permute-start | bytes 245768 | tf_op jit(solution)/shard_map/ppermute | solution.py:13
  19.7 7.2 %collective-permute-start = (f32[64,320]{1,0:T(8,128)S(1)}, f32[64,320]{1,0:T(8,128)S(1)}, u32[]{:S(2)}, u32[]{:S(2)}) collective-permute-start(f32[64,320]{1,0:T(8,128)S(1)} %fusion.11), channel_id=1, source_target_pairs={{0,8},{8,16},{16,24},{24,0},{1,9},{9,17},{17,25},{25,1},{2,10},{10... | collective-permute-start | bytes 245768 | tf_op jit(solution)/shard_map/ppermute | solution.py:13
  26.9 6.8 %collective-permute-start.5 = (f32[64,320]{1,0:T(8,128)S(1)}, f32[64,320]{1,0:T(8,128)S(1)}, u32[]{:S(2)}, u32[]{:S(2)}) collective-permute-start(f32[64,320]{1,0:T(8,128)S(1)} %add_add_fusion), channel_id=1, source_target_pairs={{0,96},{32,0},{64,32},{96,64},{1,97},{33,1},{65,33},{97,65},{2,98}... | collective-permute-start | bytes 245768 | tf_op jit(solution)/shard_map/ppermute | solution.py:13
  30.8 5.1 %collective-permute-start.4 = (f32[64,320]{1,0:T(8,128)S(1)}, f32[64,320]{1,0:T(8,128)S(1)}, u32[]{:S(2)}, u32[]{:S(2)}) collective-permute-start(f32[64,320]{1,0:T(8,128)S(1)} %add_add_fusion), channel_id=1, source_target_pairs={{0,64},{32,96},{64,0},{96,32},{1,65},{33,97},{65,1},{97,33},{2,66}... | collective-permute-start | bytes 245768 | tf_op jit(solution)/shard_map/ppermute | solution.py:13
  30.8 6.3 %collective-permute-start.3 = (f32[64,320]{1,0:T(8,128)S(1)}, f32[64,320]{1,0:T(8,128)S(1)}, u32[]{:S(2)}, u32[]{:S(2)}) collective-permute-start(f32[64,320]{1,0:T(8,128)S(1)} %add_add_fusion), channel_id=1, source_target_pairs={{0,32},{32,64},{64,96},{96,0},{1,33},{33,65},{65,97},{97,1},{2,34}... | collective-permute-start | bytes 245768 | tf_op jit(solution)/shard_map/ppermute | solution.py:13
  43.0 6.9 %collective-permute-start.10 = (f32[64,5120]{1,0:T(8,128)S(1)}, f32[64,5120]{1,0:T(8,128)}, u32[]{:S(2)}, u32[]{:S(2)}) collective-permute-start(f32[64,5120]{1,0:T(8,128)S(1)} %fusion.5), channel_id=1, source_target_pairs={{0,1},{1,0},{2,3},{3,2},{4,5},{5,4},{6,7},{7,6},{8,9},{9,8},{10,11... | collective-permute-start | bytes 3932168 | tf_op jit(solution)/shard_map/ppermute | solution.py:18
  45.5 2.5 %collective-permute-start.6 = (f32[64,128]{0,1:T(8,128)S(1)}, f32[64,128]{0,1:T(8,128)S(1)}, u32[]{:S(2)}, u32[]{:S(2)}) collective-permute-start(f32[64,128]{0,1:T(8,128)S(1)} %concatenate.12), channel_id=1, source_target_pairs={{0,1},{1,0},{2,3},{3,2},{4,5},{5,4},{6,7},{7,6},{8,9},{9,8},{10,11... | collective-permute-start | bytes 98312 | tf_op jit(solution)/shard_map/ppermute | solution.py:18
  76.6 17.3 %collective-permute-start.13 = (f32[8,2560]{1,0:T(8,128)S(1)}, f32[8,2560]{1,0:T(8,128)S(1)}, u32[]{:S(2)}, u32[]{:S(2)}) collective-permute-start(f32[8,2560]{1,0:T(8,128)S(1)} %reduce_sum.9), channel_id=1, source_target_pairs={{0,6},{2,0},{4,2},{6,4},{1,7},{3,1},{5,3},{7,5},{8,14},{10,8},{12,... | collective-permute-start | bytes 245768 | tf_op jit(solution)/shard_map/ppermute | solution.py:13
  79.4 14.6 %collective-permute-start.12 = (f32[8,2560]{1,0:T(8,128)S(1)}, f32[8,2560]{1,0:T(8,128)S(1)}, u32[]{:S(2)}, u32[]{:S(2)}) collective-permute-start(f32[8,2560]{1,0:T(8,128)S(1)} %reduce_sum.9), channel_id=1, source_target_pairs={{0,4},{2,6},{4,0},{6,2},{1,5},{3,7},{5,1},{7,3},{8,12},{10,14},{12... | collective-permute-start | bytes 245768 | tf_op jit(solution)/shard_map/ppermute | solution.py:13
  79.8 14.2 %collective-permute-start.11 = (f32[8,2560]{1,0:T(8,128)S(1)}, f32[8,2560]{1,0:T(8,128)S(1)}, u32[]{:S(2)}, u32[]{:S(2)}) collective-permute-start(f32[8,2560]{1,0:T(8,128)S(1)} %reduce_sum.9), channel_id=1, source_target_pairs={{0,2},{2,4},{4,6},{6,0},{1,3},{3,5},{5,7},{7,1},{8,10},{10,12},{12... | collective-permute-start | bytes 245768 | tf_op jit(solution)/shard_map/ppermute | solution.py:13
  80.4 7.2 %collective-permute-start.7 = (f32[64,128]{0,1:T(8,128)S(1)}, f32[64,128]{0,1:T(8,128)S(1)}, u32[]{:S(2)}, u32[]{:S(2)}) collective-permute-start(f32[64,128]{0,1:T(8,128)S(1)} %concatenate.13), channel_id=1, source_target_pairs={{0,2},{2,4},{4,6},{6,0},{1,3},{3,5},{5,7},{7,1},{8,10},{10,12},{12... | collective-permute-start | bytes 98312 | tf_op jit(solution)/shard_map/ppermute | solution.py:13
  82.1 6.7 %collective-permute-start.8 = (f32[64,128]{0,1:T(8,128)S(1)}, f32[64,128]{0,1:T(8,128)S(1)}, u32[]{:S(2)}, u32[]{:S(2)}) collective-permute-start(f32[64,128]{0,1:T(8,128)S(1)} %concatenate.13), channel_id=1, source_target_pairs={{0,4},{2,6},{4,0},{6,2},{1,5},{3,7},{5,1},{7,3},{8,12},{10,14},{12... | collective-permute-start | bytes 98312 | tf_op jit(solution)/shard_map/ppermute | solution.py:13
  87.7 3.1 %collective-permute-start.9 = (f32[64,128]{0,1:T(8,128)S(1)}, f32[64,128]{0,1:T(8,128)S(1)}, u32[]{:S(2)}, u32[]{:S(2)}) collective-permute-start(f32[64,128]{0,1:T(8,128)S(1)} %concatenate.13), channel_id=1, source_target_pairs={{0,6},{2,0},{4,2},{6,4},{1,7},{3,1},{5,3},{7,5},{8,14},{10,8},{12,... | collective-permute-start | bytes 98312 | tf_op jit(solution)/shard_map/ppermute | solution.py:13
  95.2 21.0 %all-to-all-start.1 = ((f32[16,8,2560]{2,1,0:T(8,128)}), f32[16,8,2560]{2,1,0:T(8,128)S(1)}, u32[]{:S(2)}, u32[]{:S(2)}) async-start(f32[16,8,2560]{2,1,0:T(8,128)} %broadcast_in_dim.6), calls=%async_computation.1 | async-start | bytes 2621440 | tf_op jit(solution)/shard_map/all_to_all | solution.py:72
  116.2 18.2 %collective-permute-start.14 = (f32[64,5120]{1,0:T(8,128)S(1)}, f32[64,5120]{1,0:T(8,128)}, u32[]{:S(2)}, u32[]{:S(2)}) collective-permute-start(f32[64,5120]{1,0:T(8,128)S(1)} %bitcast.46), channel_id=1, source_target_pairs={{0,1},{1,0},{2,3},{3,2},{4,5},{5,4},{6,7},{7,6},{8,9},{9,8},{10,11... | collective-permute-start | bytes 3932168 | tf_op jit(solution)/shard_map/ppermute | solution.py:18
  133.1 4.1 %copy-start.2 = (f32[64,320]{1,0:T(8,128)}, f32[64,320]{1,0:T(8,128)S(1)}, u32[]{:S(2)}) copy-start(f32[64,320]{1,0:T(8,128)S(1)} %fusion.29) | copy-start | bytes 245764
  137.2 8.5 %copy-start.1 = (f32[64,10240]{1,0:T(8,128)}, f32[64,10240]{1,0:T(8,128)S(1)}, u32[]{:S(2)}) copy-start(f32[64,10240]{1,0:T(8,128)S(1)} %maximum_select_fusion) | copy-start | bytes 7864324

commit v2 on v0

v2 whole, which is shorter than its diff:
```python
import functools

import jax
import jax.numpy as jnp
from jax import lax
from jax.experimental import pallas as pl
from jax.experimental.pallas import tpu as pltpu
from jax.sharding import Mesh, PartitionSpec as P

DP = ("z", "x")
AXES = ("z", "x", "y", "c")
SIZES = (4, 4, 4, 2)
HIGHEST = lax.Precision.HIGHEST
F32 = jnp.float32
BF16 = jnp.bfloat16
MIB = 1 << 20
ROWS = 8
ANY = pl.BlockSpec(memory_space=pl.ANY)
WHOLE = pl.BlockSpec(memory_space=pltpu.VMEM)
SCALAR = pl.BlockSpec(memory_space=pltpu.SMEM)


def params(mib):
    return pltpu.CompilerParams(vmem_limit_bytes=mib * MIB)


def cost(flops, nbytes):
    return pl.CostEstimate(flops=flops, bytes_accessed=nbytes, transcendentals=0)


def index(z, x, y, c):
    return ((z * SIZES[1] + x) * SIZES[2] + y) * SIZES[3] + c


def everyone():
    return [
        (z, x, y, c)
        for z in range(SIZES[0])
        for x in range(SIZES[1])
        for y in range(SIZES[2])
        for c in range(SIZES[3])
    ]


def ring_x_or_z(value, phase):
    out = []
    for k in (1, 3, 2):
        pairs = []
        for z, x, y, c in everyone():
            to = (z, (x + k) % SIZES[1], y, c) if c == phase else ((z + k) % SIZES[0], x, y, c)
            pairs.append((index(z, x, y, c), index(*to)))
        out.append(lax.ppermute(value, AXES, pairs))
    return out


def ring_y(value):
    n = SIZES[2]
    return [lax.ppermute(value, "y", [(i, (i + k) % n) for i in range(n)]) for k in (1, 3, 2)]


def swap(value):
    return lax.ppermute(value, "c", [(0, 1), (1, 0)])


def merge_kernel(width, g_ref, e_ref, q_ref, m_ref, p_ref, acc):
    rows, columns = g_ref.shape
    rank = q_ref.shape[0]
    acc[...] = jnp.zeros_like(acc)

    def step(g, e, q):
        at = pl.multiple_of(pl.program_id(0) * width, width)
        m = (g[...].astype(F32) + e[...].astype(F32)).astype(BF16)
        m_ref[:, pl.ds(at, width)] = m
        acc[...] += lax.dot_general(
            m, q[...], (((1,), (1,)), ((), ())), preferred_element_type=F32
        )

    def spec(n):
        return pl.BlockSpec((n, width), lambda i: (0, i))

    pltpu.emit_pipeline(
        step, grid=(columns // width,), in_specs=[spec(rows), spec(rows), spec(rank)]
    )(g_ref, e_ref, q_ref)
    p_ref[...] = acc[...].T


def merge(gradient, error, q_start):
    rows, columns = gradient.shape
    rank = q_start.shape[0]
    gradient, error, q_start = (
        pltpu.with_memory_space_constraint(a, pltpu.HBM) for a in (gradient, error, q_start)
    )
    return pl.pallas_call(
        functools.partial(merge_kernel, 1024),
        out_shape=[pltpu.VMEM((rows, columns), BF16), pltpu.VMEM((rank, rows), F32)],
        in_specs=[ANY, ANY, ANY],
        out_specs=[WHOLE, WHOLE],
        scratch_shapes=[pltpu.VMEM((rows, rank), F32)],
        compiler_params=params(20),
        cost_estimate=cost(2 * rank * rows * columns, 4 * rows * columns),
        name="merge",
    )(gradient, error, q_start)


def right_tiles(half, pieces, m_ref, out_ref, width):
    rank = pieces.shape[0] // 3
    cut = out_ref.shape[2]
    steps = cut // width
    cuts = m_ref.shape[1] // 2 // cut

    def step(i, carry):
        j, k = i // steps, i % steps
        at = pl.multiple_of(half * (cuts * cut) + i * width, width)
        t = jnp.dot(pieces, m_ref[:, pl.ds(at, width)], preferred_element_type=F32)
        t = t[:rank] + (t[rank : 2 * rank] + t[2 * rank :])
        to = pl.ds(pl.multiple_of(k * width, width), width)
        for g in range(rank // ROWS):
            out_ref[g * cuts + j, :, to] = t[g * ROWS : (g + 1) * ROWS]
        return carry

    lax.fori_loop(0, cuts * steps, step, 0)


def first_right_kernel(replicas, half_ref, a_ref, b_ref, c_ref, d_ref, m_ref, out_ref, ext_ref, p_ref, pieces_ref):
    p = (a_ref[...] + b_ref[...] + (c_ref[...] + d_ref[...])) * (1.0 / replicas)
    p_ref[...] = p
    rank = p.shape[0]
    peak = jnp.max(jnp.abs(p), axis=(0, 1), keepdims=True)
    peak = jnp.where(peak > 0, peak, 1.0)
    gram = lax.dot_general(
        p, p, (((1,), (1,)), ((), ())), precision=HIGHEST, preferred_element_type=F32
    )
    ext = jnp.concatenate(
        [gram[g * ROWS : (g + 1) * ROWS] for g in range(rank // ROWS)]
        + [jnp.broadcast_to(peak, (ROWS, 128))],
        axis=1,
    )
    ext_ref[...] = ext
    out_ref[out_ref.shape[0] - 1, :, : ext.shape[1]] = ext
    n = p / peak
    high = n.astype(BF16)
    n = n - high.astype(F32)
    middle = n.astype(BF16)
    low = (n - middle.astype(F32)).astype(BF16)
    pieces = jnp.concatenate([high, middle, low], axis=0)
    pieces_ref[...] = pieces
    right_tiles(half_ref[0], pieces, m_ref, out_ref, 512)


def second_right_kernel(half_ref, pieces_ref, m_ref, out_ref):
    right_tiles(half_ref[0], pieces_ref[...], m_ref, out_ref, 512)


def first_right(half, parts, merged, replicas, cut):
    rank, rows = parts[0].shape
    width = rank * ROWS + 128
    return pl.pallas_call(
        functools.partial(first_right_kernel, replicas),
        out_shape=[
            jax.ShapeDtypeStruct((replicas + 1, ROWS, cut), F32),
            pltpu.VMEM((ROWS, width), F32),
            pltpu.VMEM((rank, rows), F32),
            pltpu.VMEM((3 * rank, rows), BF16),
        ],
        in_specs=[SCALAR] + [WHOLE] * 5,
        out_specs=[WHOLE] * 4,
        compiler_params=params(12),
        cost_estimate=cost(3 * rank * rows * cut * replicas // ROWS, 4 * rank * cut * 2),
        name="first_right",
    )(half, *parts, merged)


def second_right(half, pieces, merged, replicas, cut):
    return pl.pallas_call(
        second_right_kernel,
        out_shape=pltpu.VMEM((replicas, ROWS, cut), F32),
        in_specs=[SCALAR, WHOLE, WHOLE],
        out_specs=WHOLE,
        compiler_params=params(12),
        cost_estimate=cost(pieces.shape[0] * pieces.shape[1] * cut * 4, replicas * ROWS * cut * 4),
        name="second_right",
    )(half, pieces, merged)


def pair_kernel(kept_ref, got_ref, ext_ref, out_ref, pair_ref):
    width = ext_ref.shape[1]
    last = got_ref.shape[0] - 1
    mine, other = ext_ref[...], got_ref[last, :, :width]
    own, its = mine[:1, width - 1 :], other[:1, width - 1 :]
    top = jnp.maximum(own, its)
    lane = lax.broadcasted_iota(jnp.int32, mine.shape, 1)
    pair_ref[...] = jnp.where(lane < width - 128, mine + other, top)
    for i in range(last):
        out_ref[i] = kept_ref[i] * (own / top) + got_ref[i] * (its / top)


def pair(kept, got, ext):
    return pl.pallas_call(
        pair_kernel,
        out_shape=[jax.ShapeDtypeStruct(kept.shape, F32), pltpu.VMEM(ext.shape, F32)],
        in_specs=[WHOLE] * 3,
        out_specs=[WHOLE] * 2,
        compiler_params=params(8),
        name="pair",
    )(kept, got, ext)


def gather_kernel(parts_ref, ext_ref, out_ref):
    total = parts_ref[0]
    for i in range(1, parts_ref.shape[0]):
        total = total + parts_ref[i]
    cut = total.shape[1]
    out_ref[:, :cut] = total
    out_ref[:, cut:] = ext_ref[...]


def add_parts(parts, ext):
    n, rows, cut = parts.shape
    return pl.pallas_call(
        gather_kernel,
        out_shape=jax.ShapeDtypeStruct((rows, cut + ext.shape[1]), F32),
        in_specs=[WHOLE] * 2,
        out_specs=WHOLE,
        compiler_params=params(8),
        name="add_parts",
    )(parts, ext)


def across_kernel(a_ref, b_ref, c_ref, d_ref, out_ref, ext_ref):
    copies, _, cut = out_ref.shape
    width = ext_ref.shape[1]
    refs = (a_ref, b_ref, c_ref, d_ref)
    peaks = [r[:1, cut + width - 1 :] for r in refs]
    top = jnp.maximum(jnp.maximum(peaks[0], peaks[1]), jnp.maximum(peaks[2], peaks[3]))
    total = sum(r[:, :cut] * (k / top) for r, k in zip(refs, peaks))
    for i in range(copies):
        out_ref[i] = total
    ext = (a_ref[:, cut:] + b_ref[:, cut:]) + (c_ref[:, cut:] + d_ref[:, cut:])
    lane = lax.broadcasted_iota(jnp.int32, ext.shape, 1)
    ext_ref[...] = jnp.where(lane < width - 128, ext, top)


def across(parts, replicas, cut):
    rows, width = parts[0].shape
    return pl.pallas_call(
        across_kernel,
        out_shape=[
            jax.ShapeDtypeStruct((replicas, rows, cut), F32),
            pltpu.VMEM((rows, width - cut), F32),
        ],
        in_specs=[WHOLE] * 4,
        out_specs=[WHOLE] * 2,
        compiler_params=params(8),
        name="across",
    )(*parts)


def result_kernel(width, half_ref, t_ref, m_ref, solve_ref, p_ref, *refs):
    error_ref, q_ref = refs[-2:]
    rank = solve_ref.shape[0]
    groups = rank // ROWS
    cut = t_ref.shape[2]
    cuts = t_ref.shape[0] // groups
    steps = cuts * (cut // width)
    base = half_ref[0] * steps
    left = p_ref[...].T.astype(BF16)
    solve = solve_ref[...]

    def step(e, q):
        i = pl.program_id(0)
        j, k = i // (cut // width), i % (cut // width)
        at = pl.ds(pl.multiple_of(k * width, width), width)
        t = jnp.concatenate([t_ref[g * cuts + j, :, at] for g in range(groups)], axis=0)
        new = jnp.dot(solve, t, precision=HIGHEST, preferred_element_type=F32)
        q[...] = new
        decoded = jnp.dot(left, new.astype(BF16), preferred_element_type=F32)
        m = m_ref[:, pl.ds(pl.multiple_of((base + i) * width, width), width)]
        e[...] = (m.astype(F32) - decoded).astype(BF16)

    pltpu.emit_pipeline(
        step,
        grid=(steps,),
        out_specs=[
            pl.BlockSpec((m_ref.shape[0], width), lambda i: (0, base + i)),
            pl.BlockSpec((rank, width), lambda i: (0, base + i)),
        ],
    )(error_ref, q_ref)


def result(half, totals, merged, solve, p_hat, before):
    rank = solve.shape[0]
    rows, columns = merged.shape
    held = [] if before is None else list(before)
    return pl.pallas_call(
        functools.partial(result_kernel, 1280),
        out_shape=[pltpu.HBM((rows, columns), BF16), pltpu.HBM((rank, columns), F32)],
        in_specs=[SCALAR] + [WHOLE] * 4 + [ANY] * len(held),
        out_specs=[ANY, ANY],
        input_output_aliases={5 + i: i for i in range(len(held))},
        compiler_params=params(16),
        cost_estimate=cost(rank * rows * columns, rows * columns + 2 * rank * columns),
        name="result",
    )(half, totals, merged, solve, p_hat, *held)


def body(gradient, error, q_start):
    rank, columns = q_start.shape
    replicas = SIZES[0] * SIZES[1]
    cut = columns * rank // (2 * replicas * ROWS)
    core = lax.axis_index("c").reshape(1)

    merged, p = merge(gradient[0], error[0], q_start)
    a, b, c = ring_x_or_z(p, 0)
    p = (p + a) + (b + c)
    sent, ext, p_mean, pieces = first_right(
        1 - core, (p, *ring_x_or_z(p, 1)), merged, replicas, cut
    )
    got = swap(sent)
    kept = second_right(core, pieces, merged, replicas, cut)
    parts, ext = pair(kept, got, ext)
    parts = lax.all_to_all(parts, DP, 0, 0)
    parts = add_parts(parts, ext)
    totals, ext = across((parts, *ring_y(parts)), replicas, cut)
    totals = lax.all_to_all(totals, DP, 0, 0)

    gram = ext[:, : rank * ROWS].reshape(ROWS, rank // ROWS, rank)
    gram = gram.transpose(1, 0, 2).reshape(rank, rank)
    lower = jnp.linalg.cholesky(gram)
    inverse = lax.linalg.triangular_solve(
        lower, jnp.eye(rank, dtype=F32), left_side=True, lower=True
    )
    p_hat = jnp.dot(inverse, p_mean, precision=HIGHEST)
    solve = inverse * (ext[:1, rank * ROWS : rank * ROWS + 1] / replicas)

    others = swap(totals)
    first = result(core, totals, merged, solve, p_hat, None)
    new_error, q_new = result(1 - core, others, merged, solve, p_hat, first)
    return (new_error[None], p_hat, q_new)


def solution(mesh):
    fine = Mesh(mesh.devices.reshape(SIZES), AXES)
    return jax.shard_map(
        body,
        mesh=fine,
        in_specs=(P(DP, ("y", "c"), None), P(DP, ("y", "c"), None), P()),
        out_specs=(P(DP, ("y", "c"), None), P(None, ("y", "c")), P()),
        check_vma=False,
    )
```

time: 314 us -> 124 us (0.39)
  waiting for transfers between devices: 235 us -> 12 us
  matrix products: 26.7 us -> 0.43 us
  Pallas kernels: 0 us -> 23.7 us
  starting transfers between devices: 0.08 us -> 22.7 us
  blocking collectives: 22.7 us -> 42.1 us
  between operations: 14.1 us -> 1.41 us
  local copies, waits for them, and re-layouts: 1.36 us -> 9.23 us
    psum x2 -> x0, waiting for transfers between devices: 235 us -> none  [the longest x1 151 us: body(): q_new = lax.psum(local_right, ('dp', 'mp')) / replicas]
    all_to_all x0 -> x2, blocking collectives: none -> 42.1 us  [the longest x1 22.2 us: body(): parts = lax.all_to_all(parts, DP, 0, 0)]
    dot_general x4 -> x1, matrix products: 25.5 us -> 0.22 us  [body(): p_hat = jnp.dot(inverse, p_mean, precision=HIGHEST)]
    pallas_call x0 -> x8, Pallas kernels: none -> 23.7 us  [the longest x1 9.43 us: merge(): pl.pallas_call(functools.partial(merge_kernel, 1024), out_shape=[pltpu.VM...]
    psum x1 -> x0, blocking collectives: 22.7 us -> none  [body(): gram = lax.psum(own_gram, 'mp')]
    ppermute x0 -> x11, starting transfers between devices: none -> 22.7 us  [the longest x6 10.2 us: ring_x_or_z(): out.append(lax.ppermute(value, AXES, pairs))]
    ppermute x0 -> x11, waiting for transfers between devices: none -> 12 us  [the longest x6 7.72 us: ring_x_or_z(): out.append(lax.ppermute(value, AXES, pairs))]
    unnamed x6 -> x8, local copies, waits for them, and re-layouts: 1.28 us -> 8.55 us
  transfers between devices with their start and end apart: 2 -> 11, of which waited for: 2 -> 10; matrix products, arithmetic and copies ran while one was open for 0% -> 11% of each run, Pallas kernels for 0% -> 5%
where the time goes in v2:
time: 124 us
  blocking collectives  42.1 us (34%)
  Pallas kernels  23.7 us (19%)
  starting transfers between devices  22.7 us (18%)
  other arithmetic  12.1 us (10%)
  waiting for transfers between devices  12 us (10%)
  local copies, waits for them, and re-layouts  9.23 us (7%)
  between operations  1.41 us (1%)
    all_to_all x1, blocking collectives, body(): parts = lax.all_to_all(parts, DP, 0, 0)  22.2 us
    all_to_all x1, blocking collectives, body(): totals = lax.all_to_all(totals, DP, 0, 0)  19.8 us
    ppermute x6, starting transfers between devices, ring_x_or_z(): out.append(lax.ppermute(value, AXES, pairs))  10.2 us
    pallas_call x1, Pallas kernels, merge(): pl.pallas_call(functools.partial(merge_kernel, 1024), out_shape=[pltpu.VM...  9.43 us
    unnamed x8, local copies, waits for them, and re-layouts  8.55 us
    pallas_call x2, Pallas kernels, result(): pl.pallas_call(functools.partial(result_kernel, 1280), out_shape=[pltpu.H...  8.2 us
    ppermute x2, starting transfers between devices, swap(): return lax.ppermute(value, 'c', [(0, 1), (1, 0)])  8.06 us
    ppermute x6, waiting for transfers between devices, ring_x_or_z(): out.append(lax.ppermute(value, AXES, pairs))  7.72 us
  transfers between devices with their start and end apart: 11, of which 10 were waited for; matrix products, arithmetic and copies ran while one was open for 11% of the time, Pallas kernels for 5%

profile of v2, /device:TPU:1, one launch (start us, length us, event | category | flops | bytes accessed | tf_op | source)
XLA Modules:
  0.0 123.7 jit_solution(9530752336905563861)
XLA Ops:
  0.6 9.4 %merge.1 = (bf16[320,10240]{1,0:T(8,128)(2,1)S(1)}, f32[64,320]{1,0:T(8,128)S(1)}) custom-call(bf16[320,10240]{1,0:T(8,128)(2,1)} %bitcast.25, bf16[320,10240]{1,0:T(8,128)(2,1)} %bitcast.26, bf16[64,10240]{1,0:T(8,128)(2,1)} %q_ref.1), custom_call_target="tpu_custom_call" | custom-call | flops 419430400 | bytes 13107200 | tf_op jit(solution)/shard_map/merge/pallas_call | solution.py:93
  10.1 0.0 copy-start
  10.1 2.8 %copy-done = bf16[320,10240]{1,0:T(8,128)(2,1)} copy-done((bf16[320,10240]{1,0:T(8,128)(2,1)}, bf16[320,10240]{1,0:T(8,128)(2,1)S(1)}, u32[]{:S(2)}) %copy-start) | copy-done | bytes 6553624
  12.9 4.4 %collective-permute-start.2 = (f32[64,320]{1,0:T(8,128)S(1)}, f32[64,320]{1,0:T(8,128)S(1)}, u32[]{:S(2)}, u32[]{:S(2)}) collective-permute-start(f32[64,320]{1,0:T(8,128)S(1)} %get-tuple-element.17), channel_id=1, source_target_pairs={{0,16},{1,65},{2,18},{3,67},{4,20},{5,69},{6,22},{7,71},{8,24},{9,... | collective-permute-start | bytes 245768 | tf_op jit(solution)/shard_map/ppermute | solution.py:52
  17.3 0.4 collective-permute-start.1
  17.7 1.0 collective-permute-start
  18.8 0.8 collective-permute-done.2
  19.6 1.8 %collective-permute-done.1 = f32[64,320]{1,0:T(8,128)S(1)} collective-permute-done((f32[64,320]{1,0:T(8,128)S(1)}, f32[64,320]{1,0:T(8,128)S(1)}, u32[]{:S(2)}, u32[]{:S(2)}) %collective-permute-start.1) | collective-permute-done | bytes 81952 | tf_op jit(solution)/shard_map/ppermute | solution.py:52
  21.4 1.0 collective-permute-done
  22.4 2.8 %collective-permute-start.5 = (f32[64,320]{1,0:T(8,128)S(1)}, f32[64,320]{1,0:T(8,128)S(1)}, u32[]{:S(2)}, u32[]{:S(2)}) collective-permute-start(f32[64,320]{1,0:T(8,128)S(1)} %add_add_fusion.a_ref), channel_id=1, source_target_pairs={{0,64},{1,17},{2,66},{3,19},{4,68},{5,21},{6,70},{7,23},{8,72},{9,... | collective-permute-start | bytes 245768 | tf_op jit(solution)/shard_map/ppermute | solution.py:52
  25.2 0.9 collective-permute-start.4
  26.1 0.6 collective-permute-start.3
  26.7 0.8 collective-permute-done.5.d_ref
  27.5 1.2 collective-permute-done.4.c_ref
  28.7 2.1 %collective-permute-done.3.b_ref = f32[64,320]{1,0:T(8,128)S(1)} collective-permute-done((f32[64,320]{1,0:T(8,128)S(1)}, f32[64,320]{1,0:T(8,128)S(1)}, u32[]{:S(2)}, u32[]{:S(2)}) %collective-permute-start.3) | collective-permute-done | bytes 81952 | tf_op jit(solution)/shard_map/ppermute | solution.py:52
  30.8 0.0 copy-start.1
  30.8 2.9 %copy-done.1 = bf16[320,10240]{1,0:T(8,128)(2,1)S(1)} copy-done((bf16[320,10240]{1,0:T(8,128)(2,1)S(1)}, bf16[320,10240]{1,0:T(8,128)(2,1)}, u32[]{:S(2)}) %copy-start.1) | copy-done | bytes 6553624
  33.7 2.9 %first_right.1 = (f32[17,8,2560]{2,1,0:T(8,128)S(1)}, f32[8,640]{1,0:T(8,128)S(1)}, f32[64,320]{1,0:T(8,128)S(1)}, bf16[192,320]{1,0:T(8,128)(2,1)S(1)}) custom-call(s32[1]{0:T(128)S(6)} %sub.4.half_ref, f32[64,320]{1,0:T(8,128)S(1)} %add_add_fusion.a_ref, f32[64,320]{1,0:T(8,128)S(1)} %collective-permute-done.3.b_ref, ...), custom_call_target="tpu_custom_call" | custom-call | flops 314572800 | bytes 1310720 | tf_op jit(solution)/shard_map/first_right/pallas_call | solution.py:157
  36.6 4.2 %collective-permute-start.6 = (f32[17,8,2560]{2,1,0:T(8,128)S(1)}, f32[17,8,2560]{2,1,0:T(8,128)S(1)}, u32[]{:S(2)}, u32[]{:S(2)}) collective-permute-start(f32[17,8,2560]{2,1,0:T(8,128)S(1)} %get-tuple-element.20), channel_id=1, source_target_pairs={{0,1},{1,0},{2,3},{3,2},{4,5},{5,4},{6,7},{7,6},{8,9},{9,8},{10,11... | collective-permute-start | bytes 4177928 | tf_op jit(solution)/shard_map/ppermute | solution.py:62
  40.8 2.7 %second_right.1.kept_ref = f32[16,8,2560]{2,1,0:T(8,128)S(1)} custom-call(s32[1]{0:T(128)} %bitcast.half_ref, bf16[192,320]{1,0:T(8,128)(2,1)S(1)} %get-tuple-element.19.pieces_ref, bf16[320,10240]{1,0:T(8,128)(2,1)S(1)} %copy-done.1), custom_call_target="tpu_custom_call" | custom-call | flops 629145600 | bytes 1310720 | tf_op jit(solution)/shard_map/second_right/pallas_call | solution.py:174
  43.4 0.1 collective-permute-done.6.got_ref
  43.6 0.3 pair.1
  43.8 22.2 %all_to_all.10.parts_ref = f32[16,8,2560]{2,1,0:T(8,128)S(1)} all-to-all(f32[16,8,2560]{2,1,0:T(8,128)S(1)} %get-tuple-element.22), channel_id=1, replica_groups=mesh['z'=4,'x'=4,'y'=4,'c'=2] {'z','x'}, dimensions={0} | all-to-all | bytes 2621440 | tf_op jit(solution)/shard_map/all_to_all | solution.py:321
  66.1 0.1 add_parts.1.a_ref
  66.1 3.0 %collective-permute-start.9 = (f32[8,3200]{1,0:T(8,128)S(1)}, f32[8,3200]{1,0:T(8,128)S(1)}, u32[]{:S(2)}, u32[]{:S(2)}) collective-permute-start(f32[8,3200]{1,0:T(8,128)S(1)} %add_parts.1.a_ref), channel_id=1, source_target_pairs={{0,4},{2,6},{4,0},{6,2},{1,5},{3,7},{5,1},{7,3},{8,12},{10,14},{12... | collective-permute-start | bytes 307208 | tf_op jit(solution)/shard_map/ppermute | solution.py:58
  69.1 0.8 collective-permute-start.8
  69.9 0.7 collective-permute-start.7
  70.6 0.6 collective-permute-done.9.d_ref
  71.2 2.1 %collective-permute-done.8.c_ref = f32[8,3200]{1,0:T(8,128)S(1)} collective-permute-done((f32[8,3200]{1,0:T(8,128)S(1)}, f32[8,3200]{1,0:T(8,128)S(1)}, u32[]{:S(2)}, u32[]{:S(2)}) %collective-permute-start.8) | collective-permute-done | bytes 102432 | tf_op jit(solution)/shard_map/ppermute | solution.py:58
  73.3 1.5 %collective-permute-done.7.b_ref = f32[8,3200]{1,0:T(8,128)S(1)} collective-permute-done((f32[8,3200]{1,0:T(8,128)S(1)}, f32[8,3200]{1,0:T(8,128)S(1)}, u32[]{:S(2)}, u32[]{:S(2)}) %collective-permute-start.7) | collective-permute-done | bytes 102432 | tf_op jit(solution)/shard_map/ppermute | solution.py:58
  74.8 0.2 across.1
  75.0 19.8 %all_to_all.11.t_ref = f32[16,8,2560]{2,1,0:T(8,128)S(1)} all-to-all(f32[16,8,2560]{2,1,0:T(8,128)S(1)} %get-tuple-element.24), channel_id=1, replica_groups=mesh['z'=4,'x'=4,'y'=4,'c'=2] {'z','x'}, dimensions={0} | all-to-all | bytes 2621440 | tf_op jit(solution)/shard_map/all_to_all | solution.py:324
  94.8 3.9 %collective-permute-start.10 = (f32[16,8,2560]{2,1,0:T(8,128)S(1)}, f32[16,8,2560]{2,1,0:T(8,128)S(1)}, u32[]{:S(2)}, u32[]{:S(2)}) collective-permute-start(f32[16,8,2560]{2,1,0:T(8,128)S(1)} %all_to_all.11.t_ref), channel_id=1, source_target_pairs={{0,1},{1,0},{2,3},{3,2},{4,5},{5,4},{6,7},{7,6},{8,9},{9,8},{10,11... | collective-permute-start | bytes 3932168 | tf_op jit(solution)/shard_map/ppermute | solution.py:62
  98.7 0.5 slice.17
  99.2 0.1 reshape.25
  99.3 0.1 copy.11
  99.4 5.8 %cholesky.17 = f32[64,64]{1,0:T(8,128)S(1)} custom-call(f32[64,64]{1,0:T(8,128)S(1)} %fusion.3), custom_call_target="Cholesky" | custom-call | tf_op jit(solution)/shard_map/jit(cholesky)/cholesky | solution.py:328
  105.3 0.6 compare_reduce_fusion
  105.9 0.7 fusion
  106.6 4.9 %custom-call.6 = f32[1,64,64]{1,2,0:T(8,128)S(1)} custom-call(f32[1,64,64]{2,1,0:T(8,128)S(1)} %fusion), custom_call_target="InvertDiagBlocksLowerTriangular" | custom-call | tf_op jit(solution)/shard_map/triangular_solve | solution.py:329
  112.2 0.2 broadcast_multiply_fusion
  112.4 0.2 fusion.4.p_ref
  112.6 0.0 copy-start.3
  112.6 0.0 copy-start.2
  112.6 2.9 %copy-done.2 = bf16[320,10240]{1,0:T(8,128)(2,1)S(1)} copy-done((bf16[320,10240]{1,0:T(8,128)(2,1)S(1)}, bf16[320,10240]{1,0:T(8,128)(2,1)}, u32[]{:S(2)}) %copy-start.2) | copy-done | bytes 6553624
  115.5 4.1 %result.2 = (bf16[320,10240]{1,0:T(8,128)(2,1)}, f32[64,10240]{1,0:T(8,128)}) custom-call(s32[1]{0:T(128)} %bitcast.half_ref, f32[16,8,2560]{2,1,0:T(8,128)S(1)} %all_to_all.11.t_ref, bf16[320,10240]{1,0:T(8,128)(2,1)S(1)} %copy-done.2, f32[64,64]{1,0:T(8,128)S(1)} %get-tuple-element.31.solve_ref, f32[64,320]{1,0:T(8,128)S(1)} %fusion.4.p_ref), custom_call_target="tpu_custom_call" | custom-call | flops 209715200 | bytes 4587520 | tf_op jit(solution)/shard_map/result/pallas_call | solution.py:294
  119.6 0.0 collective-permute-done.10.t_ref
  119.6 0.0 copy-done.3
  119.6 4.1 %result.3 = (bf16[320,10240]{1,0:T(8,128)(2,1)}, f32[64,10240]{1,0:T(8,128)}) custom-call(s32[1]{0:T(128)S(6)} %sub.4.half_ref, f32[16,8,2560]{2,1,0:T(8,128)S(1)} %collective-permute-done.10.t_ref, bf16[320,10240]{1,0:T(8,128)(2,1)S(1)} %copy-done.2, f32[64,64]{1,0:T(8,128)S(1)} %get-tuple-element.31.solve_ref, ...), custom_call_target="tpu_custom_call", output_to_operand_aliasing={{0}: (5, {}), {1}: (6, {})} | custom-call | flops 209715200 | bytes 4587520 | tf_op jit(solution)/shard_map/result/pallas_call | solution.py:294
  (5 shorter events, 0.1 us)
Async XLA Ops:
  10.1 2.8 %copy-start = (bf16[320,10240]{1,0:T(8,128)(2,1)}, bf16[320,10240]{1,0:T(8,128)(2,1)S(1)}, u32[]{:S(2)}) copy-start(bf16[320,10240]{1,0:T(8,128)(2,1)S(1)} %get-tuple-element.18.m_ref) | copy-start | bytes 19660804
  12.9 6.7 %collective-permute-start.2 = (f32[64,320]{1,0:T(8,128)S(1)}, f32[64,320]{1,0:T(8,128)S(1)}, u32[]{:S(2)}, u32[]{:S(2)}) collective-permute-start(f32[64,320]{1,0:T(8,128)S(1)} %get-tuple-element.17), channel_id=1, source_target_pairs={{0,16},{1,65},{2,18},{3,67},{4,20},{5,69},{6,22},{7,71},{8,24},{9,... | collective-permute-start | bytes 245768 | tf_op jit(solution)/shard_map/ppermute | solution.py:52
  17.3 4.1 %collective-permute-start.1 = (f32[64,320]{1,0:T(8,128)S(1)}, f32[64,320]{1,0:T(8,128)S(1)}, u32[]{:S(2)}, u32[]{:S(2)}) collective-permute-start(f32[64,320]{1,0:T(8,128)S(1)} %get-tuple-element.17), channel_id=1, source_target_pairs={{0,24},{1,97},{2,26},{3,99},{4,28},{5,101},{6,30},{7,103},{8,0},{9... | collective-permute-start | bytes 245768 | tf_op jit(solution)/shard_map/ppermute | solution.py:52
  17.7 4.7 %collective-permute-start = (f32[64,320]{1,0:T(8,128)S(1)}, f32[64,320]{1,0:T(8,128)S(1)}, u32[]{:S(2)}, u32[]{:S(2)}) collective-permute-start(f32[64,320]{1,0:T(8,128)S(1)} %get-tuple-element.17), channel_id=1, source_target_pairs={{0,8},{1,33},{2,10},{3,35},{4,12},{5,37},{6,14},{7,39},{8,16},{9,4... | collective-permute-start | bytes 245768 | tf_op jit(solution)/shard_map/ppermute | solution.py:52
  22.4 5.1 %collective-permute-start.5 = (f32[64,320]{1,0:T(8,128)S(1)}, f32[64,320]{1,0:T(8,128)S(1)}, u32[]{:S(2)}, u32[]{:S(2)}) collective-permute-start(f32[64,320]{1,0:T(8,128)S(1)} %add_add_fusion.a_ref), channel_id=1, source_target_pairs={{0,64},{1,17},{2,66},{3,19},{4,68},{5,21},{6,70},{7,23},{8,72},{9,... | collective-permute-start | bytes 245768 | tf_op jit(solution)/shard_map/ppermute | solution.py:52
  25.2 3.5 %collective-permute-start.4 = (f32[64,320]{1,0:T(8,128)S(1)}, f32[64,320]{1,0:T(8,128)S(1)}, u32[]{:S(2)}, u32[]{:S(2)}) collective-permute-start(f32[64,320]{1,0:T(8,128)S(1)} %add_add_fusion.a_ref), channel_id=1, source_target_pairs={{0,96},{1,25},{2,98},{3,27},{4,100},{5,29},{6,102},{7,31},{8,104},... | collective-permute-start | bytes 245768 | tf_op jit(solution)/shard_map/ppermute | solution.py:52
  26.1 4.7 %collective-permute-start.3 = (f32[64,320]{1,0:T(8,128)S(1)}, f32[64,320]{1,0:T(8,128)S(1)}, u32[]{:S(2)}, u32[]{:S(2)}) collective-permute-start(f32[64,320]{1,0:T(8,128)S(1)} %add_add_fusion.a_ref), channel_id=1, source_target_pairs={{0,32},{1,9},{2,34},{3,11},{4,36},{5,13},{6,38},{7,15},{8,40},{9,1... | collective-permute-start | bytes 245768 | tf_op jit(solution)/shard_map/ppermute | solution.py:52
  30.8 2.9 %copy-start.1 = (bf16[320,10240]{1,0:T(8,128)(2,1)S(1)}, bf16[320,10240]{1,0:T(8,128)(2,1)}, u32[]{:S(2)}) copy-start(bf16[320,10240]{1,0:T(8,128)(2,1)} %copy-done) | copy-start | bytes 19660804
  36.6 7.0 %collective-permute-start.6 = (f32[17,8,2560]{2,1,0:T(8,128)S(1)}, f32[17,8,2560]{2,1,0:T(8,128)S(1)}, u32[]{:S(2)}, u32[]{:S(2)}) collective-permute-start(f32[17,8,2560]{2,1,0:T(8,128)S(1)} %get-tuple-element.20), channel_id=1, source_target_pairs={{0,1},{1,0},{2,3},{3,2},{4,5},{5,4},{6,7},{7,6},{8,9},{9,8},{10,11... | collective-permute-start | bytes 4177928 | tf_op jit(solution)/shard_map/ppermute | solution.py:62
  66.1 5.1 %collective-permute-start.9 = (f32[8,3200]{1,0:T(8,128)S(1)}, f32[8,3200]{1,0:T(8,128)S(1)}, u32[]{:S(2)}, u32[]{:S(2)}) collective-permute-start(f32[8,3200]{1,0:T(8,128)S(1)} %add_parts.1.a_ref), channel_id=1, source_target_pairs={{0,4},{2,6},{4,0},{6,2},{1,5},{3,7},{5,1},{7,3},{8,12},{10,14},{12... | collective-permute-start | bytes 307208 | tf_op jit(solution)/shard_map/ppermute | solution.py:58
  69.1 4.2 %collective-permute-start.8 = (f32[8,3200]{1,0:T(8,128)S(1)}, f32[8,3200]{1,0:T(8,128)S(1)}, u32[]{:S(2)}, u32[]{:S(2)}) collective-permute-start(f32[8,3200]{1,0:T(8,128)S(1)} %add_parts.1.a_ref), channel_id=1, source_target_pairs={{0,6},{2,0},{4,2},{6,4},{1,7},{3,1},{5,3},{7,5},{8,14},{10,8},{12,... | collective-permute-start | bytes 307208 | tf_op jit(solution)/shard_map/ppermute | solution.py:58
  69.9 4.9 %collective-permute-start.7 = (f32[8,3200]{1,0:T(8,128)S(1)}, f32[8,3200]{1,0:T(8,128)S(1)}, u32[]{:S(2)}, u32[]{:S(2)}) collective-permute-start(f32[8,3200]{1,0:T(8,128)S(1)} %add_parts.1.a_ref), channel_id=1, source_target_pairs={{0,2},{2,4},{4,6},{6,0},{1,3},{3,5},{5,7},{7,1},{8,10},{10,12},{12... | collective-permute-start | bytes 307208 | tf_op jit(solution)/shard_map/ppermute | solution.py:58
  94.8 24.8 %collective-permute-start.10 = (f32[16,8,2560]{2,1,0:T(8,128)S(1)}, f32[16,8,2560]{2,1,0:T(8,128)S(1)}, u32[]{:S(2)}, u32[]{:S(2)}) collective-permute-start(f32[16,8,2560]{2,1,0:T(8,128)S(1)} %all_to_all.11.t_ref), channel_id=1, source_target_pairs={{0,1},{1,0},{2,3},{3,2},{4,5},{5,4},{6,7},{7,6},{8,9},{9,8},{10,11... | collective-permute-start | bytes 3932168 | tf_op jit(solution)/shard_map/ppermute | solution.py:62
  112.6 7.0 %copy-start.3 = (f32[64,320]{1,0:T(8,128)}, f32[64,320]{1,0:T(8,128)S(1)}, u32[]{:S(2)}) copy-start(f32[64,320]{1,0:T(8,128)S(1)} %fusion.4.p_ref) | copy-start | bytes 245764
  112.6 2.9 %copy-start.2 = (bf16[320,10240]{1,0:T(8,128)(2,1)S(1)}, bf16[320,10240]{1,0:T(8,128)(2,1)}, u32[]{:S(2)}) copy-start(bf16[320,10240]{1,0:T(8,128)(2,1)} %copy-done) | copy-start | bytes 19660804

commit v3 on v2

v3 whole, which is shorter than its diff:
```python
import functools

import jax
import jax.numpy as jnp
from jax import lax
from jax.experimental import pallas as pl
from jax.experimental.pallas import tpu as pltpu
from jax.sharding import Mesh, PartitionSpec as P

DP = ("z", "x")
AXES = ("z", "x", "y", "c")
SIZES = (4, 4, 4, 2)
HIGHEST = lax.Precision.HIGHEST
F32 = jnp.float32
BF16 = jnp.bfloat16
MIB = 1 << 20
ROWS = 8
ANY = pl.BlockSpec(memory_space=pl.ANY)
WHOLE = pl.BlockSpec(memory_space=pltpu.VMEM)
SCALAR = pl.BlockSpec(memory_space=pltpu.SMEM)


def params(mib):
    return pltpu.CompilerParams(vmem_limit_bytes=mib * MIB)


def cost(flops, nbytes):
    return pl.CostEstimate(flops=flops, bytes_accessed=nbytes, transcendentals=0)


def index(z, x, y, c):
    return ((z * SIZES[1] + x) * SIZES[2] + y) * SIZES[3] + c


def everyone():
    return [
        (z, x, y, c)
        for z in range(SIZES[0])
        for x in range(SIZES[1])
        for y in range(SIZES[2])
        for c in range(SIZES[3])
    ]


def ring_x_or_z(value, phase):
    out = []
    for k in (1, 3, 2):
        pairs = []
        for z, x, y, c in everyone():
            to = (z, (x + k) % SIZES[1], y, c) if c == phase else ((z + k) % SIZES[0], x, y, c)
            pairs.append((index(z, x, y, c), index(*to)))
        out.append(lax.ppermute(value, AXES, pairs))
    return out


def ring_y(value):
    n = SIZES[2]
    return [lax.ppermute(value, "y", [(i, (i + k) % n) for i in range(n)]) for k in (1, 3, 2)]


def swap(value):
    return lax.ppermute(value, "c", [(0, 1), (1, 0)])


def merge_kernel(width, core_ref, g_hbm, e_hbm, q_hbm, m_ref, p_ref, g_ref, e_ref, q_ref, sems):
    rows, columns = g_ref.shape
    rank = q_ref.shape[0]
    steps = columns // width
    del core_ref

    def copies(i):
        at = pl.ds(i * width, width)
        return [
            pltpu.make_async_copy(src.at[:, at], dst.at[:, at], sems.at[n, i])
            for n, (src, dst) in enumerate(((g_hbm, g_ref), (e_hbm, e_ref), (q_hbm, q_ref)))
        ]

    for i in range(steps):
        for c in copies(i):
            c.start()
    acc = jnp.zeros((rows, rank), F32)
    for i in range(steps):
        for c in copies(i):
            c.wait()
        at = pl.ds(i * width, width)
        m = (g_ref[:, at].astype(F32) + e_ref[:, at].astype(F32)).astype(BF16)
        m_ref[:, at] = m
        acc = acc + lax.dot_general(
            m, q_ref[:, at], (((1,), (1,)), ((), ())), preferred_element_type=F32
        )
    p_ref[...] = pack(acc.T)


def pack(p):
    rank, rows = p.shape
    full = rows // 128
    half = rank // 2
    parts = [p[:, i * 128 : (i + 1) * 128] for i in range(full)]
    rest = p[:, full * 128 :]
    return jnp.concatenate(parts + [jnp.concatenate([rest[:half], rest[half:]], axis=1)], axis=0)


def unpack(packed, rank):
    full = packed.shape[0] // rank
    last = packed[full * rank :]
    rest = jnp.concatenate([last[:, :64], last[:, 64:]], axis=0)
    return jnp.concatenate(
        [packed[i * rank : (i + 1) * rank] for i in range(full)] + [rest], axis=1
    )


def merge(core, gradient, error, q_start):
    rows, columns = gradient.shape
    rank = q_start.shape[0]
    width = 1024
    gradient, error, q_start = (
        pltpu.with_memory_space_constraint(a, pltpu.HBM) for a in (gradient, error, q_start)
    )
    return pl.pallas_call(
        functools.partial(merge_kernel, width),
        out_shape=[pltpu.VMEM((rows, columns), BF16), pltpu.VMEM((rank * rows // 128, 128), F32)],
        in_specs=[SCALAR, ANY, ANY, ANY],
        out_specs=[WHOLE, WHOLE],
        scratch_shapes=[
            pltpu.VMEM((rows, columns), BF16),
            pltpu.VMEM((rows, columns), BF16),
            pltpu.VMEM((rank, columns), BF16),
            pltpu.SemaphoreType.DMA((3, columns // width)),
        ],
        compiler_params=params(24),
        cost_estimate=cost(2 * rank * rows * columns, 4 * rows * columns),
        name="merge",
    )(core, gradient, error, q_start)


def right_tiles(half, pieces, m_ref, out_ref, width):
    rank = pieces.shape[0] // 3
    groups = rank // ROWS
    tiles = width // 128
    cut = out_ref.shape[1] // ROWS * 128
    steps = cut // width
    cuts = m_ref.shape[1] // 2 // cut

    def step(i, carry):
        j, k = i // steps, i % steps
        at = pl.multiple_of(half * (cuts * cut) + i * width, width)
        t = jnp.dot(pieces, m_ref[:, pl.ds(at, width)], preferred_element_type=F32)
        t = t[:rank] + (t[rank : 2 * rank] + t[2 * rank :])
        for g in range(groups):
            for n in range(tiles):
                to = pl.ds(pl.multiple_of((k * tiles + n) * ROWS, ROWS), ROWS)
                out_ref[g * cuts + j, to, :] = t[g * ROWS : (g + 1) * ROWS, n * 128 : (n + 1) * 128]
        return carry

    lax.fori_loop(0, cuts * steps, step, 0)


def split(n):
    high = n.astype(BF16)
    n = n - high.astype(F32)
    middle = n.astype(BF16)
    return high, middle, (n - middle.astype(F32)).astype(BF16)


def first_right_kernel(replicas, rank, core_ref, a_ref, b_ref, c_ref, d_ref, m_ref, out_ref, ext_ref, p_ref, pieces_ref):
    p = (a_ref[...] + b_ref[...] + (c_ref[...] + d_ref[...])) * (1.0 / replicas)
    peak = jnp.max(jnp.abs(p), axis=(0, 1), keepdims=True)
    peak = jnp.where(peak > 0, peak, 1.0)
    p = unpack(p, rank)
    p_ref[...] = p
    gram = lax.dot_general(
        p, p, (((1,), (1,)), ((), ())), precision=HIGHEST, preferred_element_type=F32
    )
    two = 2 * ROWS
    ext = jnp.concatenate(
        [
            jnp.concatenate([gram[i : i + ROWS], gram[i + ROWS : i + two]], axis=1)
            for i in range(0, rank, two)
        ]
        + [jnp.broadcast_to(peak, (ROWS, 128))],
        axis=0,
    )
    ext_ref[...] = ext
    out_ref[out_ref.shape[0] - 1, : ext.shape[0], :] = ext
    pieces = jnp.concatenate(split(p / peak), axis=0)
    pieces_ref[...] = pieces
    right_tiles(1 - core_ref[0], pieces, m_ref, out_ref, 512)


def second_right_kernel(core_ref, pieces_ref, m_ref, out_ref):
    right_tiles(core_ref[0], pieces_ref[...], m_ref, out_ref, 512)


def first_right(core, parts, merged, rank, replicas, size):
    rows = merged.shape[0]
    return pl.pallas_call(
        functools.partial(first_right_kernel, replicas, rank),
        out_shape=[
            jax.ShapeDtypeStruct((replicas + 1, size, 128), F32),
            pltpu.VMEM((rank * rank // 128 + ROWS, 128), F32),
            pltpu.VMEM((rank, rows), F32),
            pltpu.VMEM((3 * rank, rows), BF16),
        ],
        in_specs=[SCALAR] + [WHOLE] * 5,
        out_specs=[WHOLE] * 4,
        compiler_params=params(12),
        cost_estimate=cost(6 * rows * replicas * size * 128, 8 * replicas * size * 128),
        name="first_right",
    )(core, *parts, merged)


def second_right(core, pieces, merged, replicas, size):
    return pl.pallas_call(
        second_right_kernel,
        out_shape=pltpu.VMEM((replicas, size, 128), F32),
        in_specs=[SCALAR, WHOLE, WHOLE],
        out_specs=WHOLE,
        compiler_params=params(12),
        cost_estimate=cost(6 * pieces.shape[1] * replicas * size * 128, 8 * replicas * size * 128),
        name="second_right",
    )(core, pieces, merged)


def pair_kernel(kept_ref, got_ref, ext_ref, out_ref, pair_ref):
    grams = ext_ref.shape[0] - ROWS
    last = got_ref.shape[0] - 1
    own, its = ext_ref[grams : grams + 1, :1], got_ref[last, grams : grams + 1, :1]
    top = jnp.maximum(own, its)
    pair_ref[:grams] = ext_ref[:grams] + got_ref[last, :grams]
    pair_ref[grams:] = jnp.broadcast_to(top, (ROWS, 128))
    own, its = own / top, its / top
    for i in range(last):
        out_ref[i] = kept_ref[i] * own + got_ref[i] * its


def pair(kept, got, ext):
    return pl.pallas_call(
        pair_kernel,
        out_shape=[jax.ShapeDtypeStruct(kept.shape, F32), pltpu.VMEM(ext.shape, F32)],
        in_specs=[WHOLE] * 3,
        out_specs=[WHOLE] * 2,
        compiler_params=params(8),
        name="pair",
    )(kept, got, ext)


def add_parts_kernel(parts_ref, ext_ref, out_ref):
    total = parts_ref[0]
    for i in range(1, parts_ref.shape[0]):
        total = total + parts_ref[i]
    out_ref[: total.shape[0]] = total
    out_ref[total.shape[0] :] = ext_ref[...]


def add_parts(parts, ext):
    _, size, lanes = parts.shape
    return pl.pallas_call(
        add_parts_kernel,
        out_shape=jax.ShapeDtypeStruct((size + ext.shape[0], lanes), F32),
        in_specs=[WHOLE] * 2,
        out_specs=WHOLE,
        compiler_params=params(8),
        name="add_parts",
    )(parts, ext)


def across_kernel(a_ref, b_ref, c_ref, d_ref, out_ref, ext_ref):
    copies, size, _ = out_ref.shape
    grams = ext_ref.shape[0] - ROWS
    refs = (a_ref, b_ref, c_ref, d_ref)
    peaks = [r[size + grams : size + grams + 1, :1] for r in refs]
    top = jnp.maximum(jnp.maximum(peaks[0], peaks[1]), jnp.maximum(peaks[2], peaks[3]))
    weights = [k / top for k in peaks]
    for n in range(0, size, ROWS):
        at = slice(n, n + ROWS)
        total = (a_ref[at] * weights[0] + b_ref[at] * weights[1]) + (
            c_ref[at] * weights[2] + d_ref[at] * weights[3]
        )
        for i in range(copies):
            out_ref[i, at, :] = total
    at = slice(size, size + grams)
    ext_ref[:grams] = (a_ref[at] + b_ref[at]) + (c_ref[at] + d_ref[at])
    ext_ref[grams:] = jnp.broadcast_to(top, (ROWS, 128))


def across(parts, replicas, size):
    rows, lanes = parts[0].shape
    return pl.pallas_call(
        across_kernel,
        out_shape=[
            jax.ShapeDtypeStruct((replicas, size, lanes), F32),
            pltpu.VMEM((rows - size, lanes), F32),
        ],
        in_specs=[WHOLE] * 4,
        out_specs=[WHOLE] * 2,
        compiler_params=params(8),
        name="across",
    )(*parts)


def factor_kernel(replicas, ext_ref, p_ref, solve_ref, hat_ref):
    rank = p_ref.shape[0]
    groups = rank // ROWS
    sub = lax.broadcasted_iota(jnp.int32, (ROWS, 2 * rank), 0)
    lane = lax.broadcasted_iota(jnp.int32, (ROWS, 2 * rank), 1)
    blocks = []
    for g in range(groups):
        tile = ext_ref[g // 2 * ROWS : (g // 2 + 1) * ROWS, (g % 2) * rank : (g % 2 + 1) * rank]
        unit = jnp.where(lane[:, :rank] == sub[:, :rank] + g * ROWS, 1.0, 0.0)
        blocks.append(jnp.concatenate([tile, unit], axis=1))
    for j in range(rank):
        own, at = j // ROWS, j % ROWS
        row = blocks[own][at : at + 1]
        row = row / row[:, j : j + 1]
        for g in range(own, groups):
            column = blocks[g][:, j : j + 1]
            if g == own:
                column = jnp.where(sub[:, :1] > at, column, 0.0)
            blocks[g] = blocks[g] - column * row
    inverse = []
    for g in range(groups):
        diagonal = jnp.sum(
            jnp.where(lane == sub + g * ROWS, blocks[g], 0.0), axis=1, keepdims=True
        )
        inverse.append(blocks[g][:, rank:] / jnp.sqrt(diagonal))
    inverse = jnp.concatenate(inverse, axis=0)
    grams = ext_ref.shape[0] - ROWS
    solve_ref[...] = inverse * (ext_ref[grams : grams + 1, :1] * (1.0 / replicas))
    hat_ref[...] = jnp.dot(inverse, p_ref[...], precision=HIGHEST, preferred_element_type=F32)


def factor(ext, p_mean, replicas):
    rank, rows = p_mean.shape
    return pl.pallas_call(
        functools.partial(factor_kernel, replicas),
        out_shape=[
            jax.ShapeDtypeStruct((rank, rank), F32),
            jax.ShapeDtypeStruct((rank, rows), F32),
        ],
        in_specs=[WHOLE] * 2,
        out_specs=[WHOLE] * 2,
        compiler_params=params(8),
        cost_estimate=cost(1 << 32, 1 << 20),
        name="factor",
    )(ext, p_mean)


def result_kernel(own, width, core_ref, t_ref, m_ref, solve_ref, p_ref, *refs):
    error_hbm, q_hbm, error_ref, q_ref, sems = refs[-5:]
    rank = solve_ref.shape[0]
    groups = rank // ROWS
    tiles = width // 128
    cuts = t_ref.shape[0] // groups
    steps = t_ref.shape[1] // ROWS * 128 // width
    half = cuts * steps * width
    base = pl.multiple_of((core_ref[0] if own else 1 - core_ref[0]) * half, half)
    left = p_ref[...].T.astype(BF16)
    s1, s2, s3 = split(solve_ref[...])
    solve = jnp.concatenate([s1, s1, s2, s2, s1, s3], axis=1)

    def out(at, size):
        to = pl.ds(pl.multiple_of(base + at, width), size)
        here = pl.ds(at, size)
        return (
            pltpu.make_async_copy(error_ref.at[:, here], error_hbm.at[:, to], sems.at[0]),
            pltpu.make_async_copy(q_ref.at[:, here], q_hbm.at[:, to], sems.at[1]),
        )

    def step(i, carry):
        j, k = i // steps, i % steps
        t = jnp.concatenate(
            [
                jnp.concatenate(
                    [
                        t_ref[g * cuts + j, pl.ds(pl.multiple_of((k * tiles + n) * ROWS, ROWS), ROWS), :]
                        for n in range(tiles)
                    ],
                    axis=1,
                )
                for g in range(groups)
            ],
            axis=0,
        )
        t1, t2, t3 = split(t)
        t = jnp.concatenate([t1, t2, t1, t2, t3, t1], axis=0)
        new = jnp.dot(solve, t, preferred_element_type=F32)
        at = pl.multiple_of(i * width, width)
        here = pl.ds(at, width)
        q_ref[:, here] = new
        decoded = jnp.dot(left, new.astype(BF16), preferred_element_type=F32)
        m = m_ref[:, pl.ds(pl.multiple_of(base + at, width), width)]
        error_ref[:, here] = (m.astype(F32) - decoded).astype(BF16)
        for c in out(at, width):
            c.start()
        return carry

    lax.fori_loop(0, cuts * steps, step, 0)
    for c in out(0, half):
        c.wait()


def result(core, own, totals, merged, solve, p_hat, before):
    rank = solve.shape[0]
    rows, columns = merged.shape
    held = [] if before is None else list(before)
    return pl.pallas_call(
        functools.partial(result_kernel, own, 512),
        out_shape=[pltpu.HBM((rows, columns), BF16), pltpu.HBM((rank, columns), F32)],
        in_specs=[SCALAR] + [WHOLE] * 4 + [ANY] * len(held),
        out_specs=[ANY, ANY],
        scratch_shapes=[
            pltpu.VMEM((rows, columns // 2), BF16),
            pltpu.VMEM((rank, columns // 2), F32),
            pltpu.SemaphoreType.DMA((2,)),
        ],
        input_output_aliases={5 + i: i for i in range(len(held))},
        compiler_params=params(16),
        cost_estimate=cost(rank * rows * columns, rows * columns + 2 * rank * columns),
        name="result",
    )(core, totals, merged, solve, p_hat, *held)


def tie_kernel(value_ref, after_ref, out_ref):
    del value_ref, after_ref, out_ref


def tie(value, after):
    return pl.pallas_call(
        tie_kernel,
        out_shape=jax.ShapeDtypeStruct(value.shape, value.dtype),
        in_specs=[ANY] * 2,
        out_specs=ANY,
        input_output_aliases={0: 0},
        compiler_params=params(4),
        name="tie",
    )(value, after)


def body(gradient, error, q_start):
    rank, columns = q_start.shape
    replicas = SIZES[0] * SIZES[1]
    size = rank * columns // (2 * replicas * 128)
    core = lax.axis_index("c").reshape(1)

    merged, p = merge(core, gradient[0], error[0], q_start)
    a, b, c = ring_x_or_z(p, 0)
    p = (p + a) + (b + c)
    sent, ext, p_mean, pieces = first_right(
        core, (p, *ring_x_or_z(p, 1)), merged, rank, replicas, size
    )
    got = swap(sent)
    kept = second_right(core, pieces, merged, replicas, size)
    parts, ext = pair(kept, got, ext)
    parts = lax.all_to_all(parts, DP, 0, 0)
    parts = add_parts(parts, ext)
    totals, ext = across((parts, *ring_y(parts)), replicas, size)
    totals = lax.all_to_all(totals, DP, 0, 0)
    solve, p_hat = factor(ext, p_mean, replicas)
    totals = tie(totals, solve)
    others = swap(totals)
    first = result(core, True, totals, merged, solve, p_hat, None)
    new_error, q_new = result(core, False, others, merged, solve, p_hat, first)
    return (new_error[None], p_hat, q_new)


def solution(mesh):
    fine = Mesh(mesh.devices.reshape(SIZES), AXES)
    return jax.shard_map(
        body,
        mesh=fine,
        in_specs=(P(DP, ("y", "c"), None), P(DP, ("y", "c"), None), P()),
        out_specs=(P(DP, ("y", "c"), None), P(None, ("y", "c")), P()),
        check_vma=False,
    )
```

time: 124 us -> 105 us (0.85)
  blocking collectives: 42.1 us -> 22.2 us
  other arithmetic: 12.1 us -> 0.02 us
  waiting for transfers between devices: 12 us -> 22.5 us
  local copies, waits for them, and re-layouts: 9.23 us -> 2.87 us
  Pallas kernels: 23.7 us -> 29.7 us
  starting transfers between devices: 22.7 us -> 27 us
    all_to_all x1 -> x0, blocking collectives: 19.8 us -> none  [body(): totals = lax.all_to_all(totals, DP, 0, 0)]
    another operation x5 -> x0, other arithmetic: 12.1 us -> none  [the longest x3 6.52 us: body(): lower = jnp.linalg.cholesky(gram)]
    all_to_all x0 -> x1, waiting for transfers between devices: none -> 10.9 us  [body(): totals = lax.all_to_all(totals, DP, 0, 0)]
    unnamed x8 -> x6, local copies, waits for them, and re-layouts: 8.55 us -> 2.87 us
    pallas_call x6 -> x8, Pallas kernels: 23.3 us -> 28.3 us  [the longest x2 10.2 us: result(): pl.pallas_call(functools.partial(result_kernel, own, 512), out_shape=[plt...]
    all_to_all x0 -> x1, starting transfers between devices: none -> 3.7 us  [body(): totals = lax.all_to_all(totals, DP, 0, 0)]
  transfers between devices with their start and end apart: 11 -> 12, of which waited for: 10 -> 11; matrix products, arithmetic and copies ran while one was open for 11% -> 0% of each run, Pallas kernels for 5% -> 13%
where the time goes in v3:
time: 105 us
  Pallas kernels  29.7 us (28%)
  starting transfers between devices  27 us (26%)
  waiting for transfers between devices  22.5 us (21%)
  blocking collectives  22.2 us (21%)
  local copies, waits for them, and re-layouts  2.87 us (3%)
    all_to_all x1, blocking collectives, body(): parts = lax.all_to_all(parts, DP, 0, 0)  22.2 us
    all_to_all x1, waiting for transfers between devices, body(): totals = lax.all_to_all(totals, DP, 0, 0)  10.9 us
    ppermute x6, starting transfers between devices, ring_x_or_z(): out.append(lax.ppermute(value, AXES, pairs))  10.3 us
    pallas_call x2, Pallas kernels, result(): pl.pallas_call(functools.partial(result_kernel, own, 512), out_shape=[plt...  10.2 us
    ppermute x2, starting transfers between devices, swap(): return lax.ppermute(value, 'c', [(0, 1), (1, 0)])  8.54 us
    ppermute x6, waiting for transfers between devices, ring_x_or_z(): out.append(lax.ppermute(value, AXES, pairs))  7.37 us
    pallas_call x1, Pallas kernels, factor(): pl.pallas_call(functools.partial(factor_kernel, replicas), out_shape=[jax...  6.38 us
    pallas_call x1, Pallas kernels, merge(): pl.pallas_call(functools.partial(merge_kernel, width), out_shape=[pltpu.V...  6.03 us
  transfers between devices with their start and end apart: 12, of which 11 were waited for; matrix products, arithmetic and copies ran while one was open for 0% of the time, Pallas kernels for 13%

profile of v3, /device:TPU:1, one launch (start us, length us, event | category | flops | bytes accessed | tf_op | source)
XLA Modules:
  0.0 105.1 jit_solution(7801384501788362237)
XLA Ops:
  0.6 6.0 %merge.1 = (bf16[320,10240]{1,0:T(8,128)(2,1)S(1)}, f32[160,128]{1,0:T(8,128)S(1)}) custom-call(s32[1]{0:T(128)} %bitcast.core_ref, bf16[320,10240]{1,0:T(8,128)(2,1)} %bitcast.5, bf16[320,10240]{1,0:T(8,128)(2,1)} %bitcast.6, bf16[64,10240]{1,0:T(8,128)(2,1)} %q_hbm.1), custom_call_target="tpu_custom_call" | custom-call | flops 419430400 | bytes 13107200 | tf_op jit(solution)/shard_map/merge/pallas_call | solution.py:119
  6.7 0.0 copy-start
  6.7 4.5 %collective-permute-start.2 = (f32[160,128]{1,0:T(8,128)S(1)}, f32[160,128]{1,0:T(8,128)S(1)}, u32[]{:S(2)}, u32[]{:S(2)}) collective-permute-start(f32[160,128]{1,0:T(8,128)S(1)} %get-tuple-element.19), channel_id=1, source_target_pairs={{0,16},{1,65},{2,18},{3,67},{4,20},{5,69},{6,22},{7,71},{8,24},{9,... | collective-permute-start | bytes 245768 | tf_op jit(solution)/shard_map/ppermute | solution.py:52
  11.2 0.4 collective-permute-start.1
  11.6 1.0 collective-permute-start
  12.7 0.7 collective-permute-done.2
  13.3 1.6 %collective-permute-done.1 = f32[160,128]{1,0:T(8,128)S(1)} collective-permute-done((f32[160,128]{1,0:T(8,128)S(1)}, f32[160,128]{1,0:T(8,128)S(1)}, u32[]{:S(2)}, u32[]{:S(2)}) %collective-permute-start.1) | collective-permute-done | bytes 81952 | tf_op jit(solution)/shard_map/ppermute | solution.py:52
  14.9 1.2 %collective-permute-done = f32[160,128]{1,0:T(8,128)S(1)} collective-permute-done((f32[160,128]{1,0:T(8,128)S(1)}, f32[160,128]{1,0:T(8,128)S(1)}, u32[]{:S(2)}, u32[]{:S(2)}) %collective-permute-start) | collective-permute-done | bytes 81952 | tf_op jit(solution)/shard_map/ppermute | solution.py:52
  16.2 2.8 %collective-permute-start.5 = (f32[160,128]{1,0:T(8,128)S(1)}, f32[160,128]{1,0:T(8,128)S(1)}, u32[]{:S(2)}, u32[]{:S(2)}) collective-permute-start(f32[160,128]{1,0:T(8,128)S(1)} %add_add_fusion.a_ref), channel_id=1, source_target_pairs={{0,64},{1,17},{2,66},{3,19},{4,68},{5,21},{6,70},{7,23},{8,72},{9,... | collective-permute-start | bytes 245768 | tf_op jit(solution)/shard_map/ppermute | solution.py:52
  19.0 0.9 collective-permute-start.4
  19.8 0.6 collective-permute-start.3
  20.4 0.6 collective-permute-done.5.d_ref
  21.0 1.2 %collective-permute-done.4.c_ref = f32[160,128]{1,0:T(8,128)S(1)} collective-permute-done((f32[160,128]{1,0:T(8,128)S(1)}, f32[160,128]{1,0:T(8,128)S(1)}, u32[]{:S(2)}, u32[]{:S(2)}) %collective-permute-start.4) | collective-permute-done | bytes 81952 | tf_op jit(solution)/shard_map/ppermute | solution.py:52
  22.3 2.1 %collective-permute-done.3.b_ref = f32[160,128]{1,0:T(8,128)S(1)} collective-permute-done((f32[160,128]{1,0:T(8,128)S(1)}, f32[160,128]{1,0:T(8,128)S(1)}, u32[]{:S(2)}, u32[]{:S(2)}) %collective-permute-start.3) | collective-permute-done | bytes 81952 | tf_op jit(solution)/shard_map/ppermute | solution.py:52
  24.3 3.0 %first_right.1 = (f32[17,160,128]{2,1,0:T(8,128)S(1)}, f32[40,128]{1,0:T(8,128)S(1)}, f32[64,320]{1,0:T(8,128)S(1)}, bf16[192,320]{1,0:T(8,128)(2,1)S(1)}) custom-call(s32[1]{0:T(128)} %bitcast.core_ref, f32[160,128]{1,0:T(8,128)S(1)} %add_add_fusion.a_ref, f32[160,128]{1,0:T(8,128)S(1)} %collective-permute-done.3.b_ref, ...), custom_call_target="tpu_custom_call" | custom-call | flops 629145600 | bytes 2621440 | tf_op jit(solution)/shard_map/first_right/pallas_call | solution.py:196
  27.4 4.2 %collective-permute-start.6 = (f32[17,160,128]{2,1,0:T(8,128)S(1)}, f32[17,160,128]{2,1,0:T(8,128)S(1)}, u32[]{:S(2)}, u32[]{:S(2)}) collective-permute-start(f32[17,160,128]{2,1,0:T(8,128)S(1)} %get-tuple-element.22), channel_id=1, source_target_pairs={{0,1},{1,0},{2,3},{3,2},{4,5},{5,4},{6,7},{7,6},{8,9},{9,8},{10,11... | collective-permute-start | bytes 4177928 | tf_op jit(solution)/shard_map/ppermute | solution.py:62
  31.5 0.0 copy-done
  31.5 2.6 %second_right.1.kept_ref = f32[16,160,128]{2,1,0:T(8,128)S(1)} custom-call(s32[1]{0:T(128)} %bitcast.core_ref, bf16[192,320]{1,0:T(8,128)(2,1)S(1)} %get-tuple-element.21.pieces_ref, bf16[320,10240]{1,0:T(8,128)(2,1)S(1)} %get-tuple-element.20.m_ref), custom_call_target="tpu_custom_call" | custom-call | flops 629145600 | bytes 2621440 | tf_op jit(solution)/shard_map/second_right/pallas_call | solution.py:213
  34.2 0.1 collective-permute-done.6.got_ref
  34.3 0.2 pair.1
  34.5 22.2 %all_to_all.10.parts_ref = f32[16,160,128]{2,1,0:T(8,128)S(1)} all-to-all(f32[16,160,128]{2,1,0:T(8,128)S(1)} %get-tuple-element.24), channel_id=1, replica_groups=mesh['z'=4,'x'=4,'y'=4,'c'=2] {'z','x'}, dimensions={0} | all-to-all | bytes 2621440 | tf_op jit(solution)/shard_map/all_to_all | solution.py:454
  56.7 0.1 add_parts.1.a_ref
  56.8 3.0 %collective-permute-start.9 = (f32[200,128]{1,0:T(8,128)S(1)}, f32[200,128]{1,0:T(8,128)S(1)}, u32[]{:S(2)}, u32[]{:S(2)}) collective-permute-start(f32[200,128]{1,0:T(8,128)S(1)} %add_parts.1.a_ref), channel_id=1, source_target_pairs={{0,4},{2,6},{4,0},{6,2},{1,5},{3,7},{5,1},{7,3},{8,12},{10,14},{12... | collective-permute-start | bytes 307208 | tf_op jit(solution)/shard_map/ppermute | solution.py:58
  59.8 0.8 collective-permute-start.8
  60.6 0.7 collective-permute-start.7
  61.3 0.6 collective-permute-done.9.d_ref
  61.9 2.1 %collective-permute-done.8.c_ref = f32[200,128]{1,0:T(8,128)S(1)} collective-permute-done((f32[200,128]{1,0:T(8,128)S(1)}, f32[200,128]{1,0:T(8,128)S(1)}, u32[]{:S(2)}, u32[]{:S(2)}) %collective-permute-start.8) | collective-permute-done | bytes 102432 | tf_op jit(solution)/shard_map/ppermute | solution.py:58
  64.0 1.5 %collective-permute-done.7.b_ref = f32[200,128]{1,0:T(8,128)S(1)} collective-permute-done((f32[200,128]{1,0:T(8,128)S(1)}, f32[200,128]{1,0:T(8,128)S(1)}, u32[]{:S(2)}, u32[]{:S(2)}) %collective-permute-start.7) | collective-permute-done | bytes 102432 | tf_op jit(solution)/shard_map/ppermute | solution.py:58
  65.5 1.2 %across.1 = (f32[16,160,128]{2,1,0:T(8,128)}, f32[40,128]{1,0:T(8,128)S(1)}) custom-call(f32[200,128]{1,0:T(8,128)S(1)} %add_parts.1.a_ref, f32[200,128]{1,0:T(8,128)S(1)} %collective-permute-done.7.b_ref, f32[200,128]{1,0:T(8,128)S(1)} %collective-permute-done.8.c_ref, f32[200,128]{1,0:T(8,128)S(1)} %collective-permute-done.9.d_ref), custom_call_target="tpu_custom_call" | custom-call | tf_op jit(solution)/shard_map/across/pallas_call | solution.py:288
  66.7 3.7 %all-to-all-start.1 = ((f32[16,160,128]{2,1,0:T(8,128)}), f32[16,160,128]{2,1,0:T(8,128)S(1)}, u32[]{:S(2)}, u32[]{:S(2)}) async-start(f32[16,160,128]{2,1,0:T(8,128)} %get-tuple-element.26), calls=%async_computation.1 | async-start | bytes 2621440 | tf_op jit(solution)/shard_map/all_to_all | solution.py:457
  70.4 6.4 %factor.1 = (f32[64,64]{1,0:T(8,128)S(1)}, f32[64,320]{1,0:T(8,128)}) custom-call(f32[40,128]{1,0:T(8,128)S(1)} %get-tuple-element.27.ext_ref, f32[64,320]{1,0:T(8,128)S(1)} %get-tuple-element.28.p_ref), custom_call_target="tpu_custom_call" | custom-call | flops 4294967296 | bytes 1048576 | tf_op jit(solution)/shard_map/factor/pallas_call | solution.py:334
  76.8 0.0 copy-start.2
  76.8 10.9 %all-to-all-done.1.value_ref = f32[16,160,128]{2,1,0:T(8,128)S(1)} async-done(((f32[16,160,128]{2,1,0:T(8,128)}), f32[16,160,128]{2,1,0:T(8,128)S(1)}, u32[]{:S(2)}, u32[]{:S(2)}) %all-to-all-start.1) | async-done | bytes 1310752 | tf_op jit(solution)/shard_map/all_to_all | solution.py:457
  87.7 4.4 %collective-permute-start.10 = (f32[16,160,128]{2,1,0:T(8,128)S(1)}, f32[16,160,128]{2,1,0:T(8,128)S(1)}, u32[]{:S(2)}, u32[]{:S(2)}) collective-permute-start(f32[16,160,128]{2,1,0:T(8,128)S(1)} %tie.1.t_ref), channel_id=1, source_target_pairs={{0,1},{1,0},{2,3},{3,2},{4,5},{5,4},{6,7},{7,6},{8,9},{9,8},{10,11... | collective-permute-start | bytes 3932168 | tf_op jit(solution)/shard_map/ppermute | solution.py:62
  92.0 0.0 copy-done.2
  92.0 0.0 copy-start.1
  92.1 2.9 %copy-done.1 = bf16[320,10240]{1,0:T(8,128)(2,1)S(1)} copy-done((bf16[320,10240]{1,0:T(8,128)(2,1)S(1)}, bf16[320,10240]{1,0:T(8,128)(2,1)}, u32[]{:S(2)}) %copy-start.1) | copy-done | bytes 6553624
  94.9 5.1 %result.2 = (bf16[320,10240]{1,0:T(8,128)(2,1)}, f32[64,10240]{1,0:T(8,128)}) custom-call(s32[1]{0:T(128)} %bitcast.core_ref, f32[16,160,128]{2,1,0:T(8,128)S(1)} %tie.1.t_ref, bf16[320,10240]{1,0:T(8,128)(2,1)S(1)} %copy-done.1, f32[64,64]{1,0:T(8,128)S(1)} %get-tuple-element.29.after_ref.solve_ref, f32[64,320]{1,0:T(8,128)S(1)} %copy-done.2), custom_call_target="tpu_custom_call" | custom-call | flops 209715200 | bytes 4587520 | tf_op jit(solution)/shard_map/result/pallas_call | solution.py:406
  100.0 0.0 collective-permute-done.10.t_ref
  100.0 5.1 %result.3 = (bf16[320,10240]{1,0:T(8,128)(2,1)}, f32[64,10240]{1,0:T(8,128)}) custom-call(s32[1]{0:T(128)} %bitcast.core_ref, f32[16,160,128]{2,1,0:T(8,128)S(1)} %collective-permute-done.10.t_ref, bf16[320,10240]{1,0:T(8,128)(2,1)S(1)} %copy-done.1, ...), custom_call_target="tpu_custom_call", output_to_operand_aliasing={{0}: (5, {}), {1}: (6, {})} | custom-call | flops 209715200 | bytes 4587520 | tf_op jit(solution)/shard_map/result/pallas_call | solution.py:406
  (2 shorter events, 0.0 us)
Async XLA Ops:
  6.7 24.9 %copy-start = (bf16[320,10240]{1,0:T(8,128)(2,1)}, bf16[320,10240]{1,0:T(8,128)(2,1)S(1)}, u32[]{:S(2)}) copy-start(bf16[320,10240]{1,0:T(8,128)(2,1)S(1)} %get-tuple-element.20.m_ref) | copy-start | bytes 19660804
  6.7 6.6 %collective-permute-start.2 = (f32[160,128]{1,0:T(8,128)S(1)}, f32[160,128]{1,0:T(8,128)S(1)}, u32[]{:S(2)}, u32[]{:S(2)}) collective-permute-start(f32[160,128]{1,0:T(8,128)S(1)} %get-tuple-element.19), channel_id=1, source_target_pairs={{0,16},{1,65},{2,18},{3,67},{4,20},{5,69},{6,22},{7,71},{8,24},{9,... | collective-permute-start | bytes 245768 | tf_op jit(solution)/shard_map/ppermute | solution.py:52
  11.2 3.7 %collective-permute-start.1 = (f32[160,128]{1,0:T(8,128)S(1)}, f32[160,128]{1,0:T(8,128)S(1)}, u32[]{:S(2)}, u32[]{:S(2)}) collective-permute-start(f32[160,128]{1,0:T(8,128)S(1)} %get-tuple-element.19), channel_id=1, source_target_pairs={{0,24},{1,97},{2,26},{3,99},{4,28},{5,101},{6,30},{7,103},{8,0},{9... | collective-permute-start | bytes 245768 | tf_op jit(solution)/shard_map/ppermute | solution.py:52
  11.6 4.5 %collective-permute-start = (f32[160,128]{1,0:T(8,128)S(1)}, f32[160,128]{1,0:T(8,128)S(1)}, u32[]{:S(2)}, u32[]{:S(2)}) collective-permute-start(f32[160,128]{1,0:T(8,128)S(1)} %get-tuple-element.19), channel_id=1, source_target_pairs={{0,8},{1,33},{2,10},{3,35},{4,12},{5,37},{6,14},{7,39},{8,16},{9,4... | collective-permute-start | bytes 245768 | tf_op jit(solution)/shard_map/ppermute | solution.py:52
  16.2 4.9 %collective-permute-start.5 = (f32[160,128]{1,0:T(8,128)S(1)}, f32[160,128]{1,0:T(8,128)S(1)}, u32[]{:S(2)}, u32[]{:S(2)}) collective-permute-start(f32[160,128]{1,0:T(8,128)S(1)} %add_add_fusion.a_ref), channel_id=1, source_target_pairs={{0,64},{1,17},{2,66},{3,19},{4,68},{5,21},{6,70},{7,23},{8,72},{9,... | collective-permute-start | bytes 245768 | tf_op jit(solution)/shard_map/ppermute | solution.py:52
  19.0 3.3 %collective-permute-start.4 = (f32[160,128]{1,0:T(8,128)S(1)}, f32[160,128]{1,0:T(8,128)S(1)}, u32[]{:S(2)}, u32[]{:S(2)}) collective-permute-start(f32[160,128]{1,0:T(8,128)S(1)} %add_add_fusion.a_ref), channel_id=1, source_target_pairs={{0,96},{1,25},{2,98},{3,27},{4,100},{5,29},{6,102},{7,31},{8,104},... | collective-permute-start | bytes 245768 | tf_op jit(solution)/shard_map/ppermute | solution.py:52
  19.8 4.5 %collective-permute-start.3 = (f32[160,128]{1,0:T(8,128)S(1)}, f32[160,128]{1,0:T(8,128)S(1)}, u32[]{:S(2)}, u32[]{:S(2)}) collective-permute-start(f32[160,128]{1,0:T(8,128)S(1)} %add_add_fusion.a_ref), channel_id=1, source_target_pairs={{0,32},{1,9},{2,34},{3,11},{4,36},{5,13},{6,38},{7,15},{8,40},{9,1... | collective-permute-start | bytes 245768 | tf_op jit(solution)/shard_map/ppermute | solution.py:52
  27.4 6.9 %collective-permute-start.6 = (f32[17,160,128]{2,1,0:T(8,128)S(1)}, f32[17,160,128]{2,1,0:T(8,128)S(1)}, u32[]{:S(2)}, u32[]{:S(2)}) collective-permute-start(f32[17,160,128]{2,1,0:T(8,128)S(1)} %get-tuple-element.22), channel_id=1, source_target_pairs={{0,1},{1,0},{2,3},{3,2},{4,5},{5,4},{6,7},{7,6},{8,9},{9,8},{10,11... | collective-permute-start | bytes 4177928 | tf_op jit(solution)/shard_map/ppermute | solution.py:62
  56.8 5.1 %collective-permute-start.9 = (f32[200,128]{1,0:T(8,128)S(1)}, f32[200,128]{1,0:T(8,128)S(1)}, u32[]{:S(2)}, u32[]{:S(2)}) collective-permute-start(f32[200,128]{1,0:T(8,128)S(1)} %add_parts.1.a_ref), channel_id=1, source_target_pairs={{0,4},{2,6},{4,0},{6,2},{1,5},{3,7},{5,1},{7,3},{8,12},{10,14},{12... | collective-permute-start | bytes 307208 | tf_op jit(solution)/shard_map/ppermute | solution.py:58
  59.8 4.2 %collective-permute-start.8 = (f32[200,128]{1,0:T(8,128)S(1)}, f32[200,128]{1,0:T(8,128)S(1)}, u32[]{:S(2)}, u32[]{:S(2)}) collective-permute-start(f32[200,128]{1,0:T(8,128)S(1)} %add_parts.1.a_ref), channel_id=1, source_target_pairs={{0,6},{2,0},{4,2},{6,4},{1,7},{3,1},{5,3},{7,5},{8,14},{10,8},{12,... | collective-permute-start | bytes 307208 | tf_op jit(solution)/shard_map/ppermute | solution.py:58
  60.6 4.9 %collective-permute-start.7 = (f32[200,128]{1,0:T(8,128)S(1)}, f32[200,128]{1,0:T(8,128)S(1)}, u32[]{:S(2)}, u32[]{:S(2)}) collective-permute-start(f32[200,128]{1,0:T(8,128)S(1)} %add_parts.1.a_ref), channel_id=1, source_target_pairs={{0,2},{2,4},{4,6},{6,0},{1,3},{3,5},{5,7},{7,1},{8,10},{10,12},{12... | collective-permute-start | bytes 307208 | tf_op jit(solution)/shard_map/ppermute | solution.py:58
  66.7 21.0 %all-to-all-start.1 = ((f32[16,160,128]{2,1,0:T(8,128)}), f32[16,160,128]{2,1,0:T(8,128)S(1)}, u32[]{:S(2)}, u32[]{:S(2)}) async-start(f32[16,160,128]{2,1,0:T(8,128)} %get-tuple-element.26), calls=%async_computation.1 | async-start | bytes 2621440 | tf_op jit(solution)/shard_map/all_to_all | solution.py:457
  76.8 15.2 %copy-start.2 = (f32[64,320]{1,0:T(8,128)S(1)}, f32[64,320]{1,0:T(8,128)}, u32[]{:S(2)}) copy-start(f32[64,320]{1,0:T(8,128)} %get-tuple-element.17.p_ref) | copy-start | bytes 245764
  87.7 12.3 %collective-permute-start.10 = (f32[16,160,128]{2,1,0:T(8,128)S(1)}, f32[16,160,128]{2,1,0:T(8,128)S(1)}, u32[]{:S(2)}, u32[]{:S(2)}) collective-permute-start(f32[16,160,128]{2,1,0:T(8,128)S(1)} %tie.1.t_ref), channel_id=1, source_target_pairs={{0,1},{1,0},{2,3},{3,2},{4,5},{5,4},{6,7},{7,6},{8,9},{9,8},{10,11... | collective-permute-start | bytes 3932168 | tf_op jit(solution)/shard_map/ppermute | solution.py:62
  92.0 2.9 %copy-start.1 = (bf16[320,10240]{1,0:T(8,128)(2,1)S(1)}, bf16[320,10240]{1,0:T(8,128)(2,1)}, u32[]{:S(2)}) copy-start(bf16[320,10240]{1,0:T(8,128)(2,1)} %copy-done) | copy-start | bytes 19660804

commit v4 on v3

v4 whole, which is shorter than its diff:
```python
import functools

import jax
import jax.numpy as jnp
from jax import lax
from jax.experimental import pallas as pl
from jax.experimental.pallas import tpu as pltpu
from jax.sharding import Mesh, PartitionSpec as P

DP = ("z", "x")
AXES = ("z", "x", "y", "c")
SIZES = (4, 4, 4, 2)
HIGHEST = lax.Precision.HIGHEST
F32 = jnp.float32
BF16 = jnp.bfloat16
MIB = 1 << 20
ROWS = 8
QUARTERS = 4
SHIFTS = (1, 3, 2)
ANY = pl.BlockSpec(memory_space=pl.ANY)
WHOLE = pl.BlockSpec(memory_space=pltpu.VMEM)
SCALAR = pl.BlockSpec(memory_space=pltpu.SMEM)


def params(mib):
    return pltpu.CompilerParams(vmem_limit_bytes=mib * MIB)


def cost(flops, nbytes):
    return pl.CostEstimate(flops=flops, bytes_accessed=nbytes, transcendentals=0)


def index(z, x, y, c):
    return ((z * SIZES[1] + x) * SIZES[2] + y) * SIZES[3] + c


def everyone():
    return [
        (z, x, y, c)
        for z in range(SIZES[0])
        for x in range(SIZES[1])
        for y in range(SIZES[2])
        for c in range(SIZES[3])
    ]


def ring_x_or_z(values, phase):
    out = []
    for k, value in zip(SHIFTS, values):
        pairs = []
        for z, x, y, c in everyone():
            to = (z, (x + k) % SIZES[1], y, c) if c == phase else ((z + k) % SIZES[0], x, y, c)
            pairs.append((index(z, x, y, c), index(*to)))
        out.append(lax.ppermute(value, AXES, pairs))
    return out


def ring_y(value):
    n = SIZES[2]
    return [lax.ppermute(value, "y", [(i, (i + k) % n) for i in range(n)]) for k in SHIFTS]


def swap(value):
    return lax.ppermute(value, "c", [(0, 1), (1, 0)])


def merge_kernel(width, meta_ref, g_hbm, e_hbm, q_hbm, m_ref, p_ref, g_ref, e_ref, q_ref, sems):
    rows, columns = g_ref.shape
    rank = q_ref.shape[0]
    steps = columns // width
    del meta_ref

    def copies(i):
        at = pl.ds(i * width, width)
        return [
            pltpu.make_async_copy(src.at[:, at], dst.at[:, at], sems.at[n, i])
            for n, (src, dst) in enumerate(((g_hbm, g_ref), (e_hbm, e_ref), (q_hbm, q_ref)))
        ]

    for i in range(steps):
        for c in copies(i):
            c.start()
    acc = jnp.zeros((rows, rank), F32)
    for i in range(steps):
        for c in copies(i):
            c.wait()
        at = pl.ds(i * width, width)
        m = (g_ref[:, at].astype(F32) + e_ref[:, at].astype(F32)).astype(BF16)
        m_ref[:, at] = m
        acc = acc + lax.dot_general(
            m, q_ref[:, at], (((1,), (1,)), ((), ())), preferred_element_type=F32
        )
    p_ref[...] = pack(acc.T)


def pack(p):
    rank, rows = p.shape
    full = rows // 128
    half = rank // 2
    parts = [p[:, i * 128 : (i + 1) * 128] for i in range(full)]
    rest = p[:, full * 128 :]
    return jnp.concatenate(parts + [jnp.concatenate([rest[:half], rest[half:]], axis=1)], axis=0)


def unpack(packed, rank):
    full = packed.shape[0] // rank
    last = packed[full * rank :]
    rest = jnp.concatenate([last[:, :64], last[:, 64:]], axis=0)
    return jnp.concatenate(
        [packed[i * rank : (i + 1) * rank] for i in range(full)] + [rest], axis=1
    )


def merge(meta, gradient, error, q_start):
    rows, columns = gradient.shape
    rank = q_start.shape[0]
    width = 1024
    gradient, error, q_start = (
        pltpu.with_memory_space_constraint(a, pltpu.HBM) for a in (gradient, error, q_start)
    )
    return pl.pallas_call(
        functools.partial(merge_kernel, width),
        out_shape=[pltpu.VMEM((rows, columns), BF16), pltpu.VMEM((rank * rows // 128, 128), F32)],
        in_specs=[SCALAR, ANY, ANY, ANY],
        out_specs=[WHOLE, WHOLE],
        scratch_shapes=[
            pltpu.VMEM((rows, columns), BF16),
            pltpu.VMEM((rows, columns), BF16),
            pltpu.VMEM((rank, columns), BF16),
            pltpu.SemaphoreType.DMA((3, columns // width)),
        ],
        compiler_params=params(24),
        cost_estimate=cost(2 * rank * rows * columns, 4 * rows * columns),
        name="merge",
    )(meta, gradient, error, q_start)


def right_tiles(half, pieces, m_ref, out_ref):
    rank = pieces.shape[0] // 3
    width = m_ref.shape[1] // 2 // QUARTERS
    for a in range(QUARTERS):
        at = pl.multiple_of(half * (QUARTERS * width) + a * width, width)
        t = jnp.dot(pieces, m_ref[:, pl.ds(at, width)], preferred_element_type=F32)
        t = t[:rank] + (t[rank : 2 * rank] + t[2 * rank :])
        to = a * (rank * width // 128)
        for g in range(rank // ROWS):
            for n in range(width // 128):
                out_ref[to : to + ROWS, :] = t[g * ROWS : (g + 1) * ROWS, n * 128 : (n + 1) * 128]
                to += ROWS


def split(n):
    high = n.astype(BF16)
    n = n - high.astype(F32)
    middle = n.astype(BF16)
    return high, middle, (n - middle.astype(F32)).astype(BF16)


def first_right_kernel(replicas, rank, meta_ref, a_ref, b_ref, c_ref, d_ref, m_ref, out_ref, ext_ref, p_ref, pieces_ref):
    p = (a_ref[...] + b_ref[...] + (c_ref[...] + d_ref[...])) * (1.0 / replicas)
    peak = jnp.max(jnp.abs(p), axis=(0, 1), keepdims=True)
    peak = jnp.where(peak > 0, peak, 1.0)
    p = unpack(p, rank)
    p_ref[...] = p
    gram = lax.dot_general(
        p, p, (((1,), (1,)), ((), ())), precision=HIGHEST, preferred_element_type=F32
    )
    two = 2 * ROWS
    ext = jnp.concatenate(
        [
            jnp.concatenate([gram[i : i + ROWS], gram[i + ROWS : i + two]], axis=1)
            for i in range(0, rank, two)
        ]
        + [jnp.broadcast_to(peak, (ROWS, 128))],
        axis=0,
    )
    ext_ref[...] = ext
    out_ref[out_ref.shape[0] - ext.shape[0] :, :] = ext
    pieces = jnp.concatenate(split(p / peak), axis=0)
    pieces_ref[...] = pieces
    right_tiles(1 - meta_ref[0], pieces, m_ref, out_ref)


def second_right_kernel(meta_ref, pieces_ref, m_ref, out_ref):
    right_tiles(meta_ref[0], pieces_ref[...], m_ref, out_ref)


def first_right(meta, parts, merged, rank, replicas):
    rows, columns = merged.shape
    size = rank * columns // 256
    extra = rank * rank // 128 + ROWS
    return pl.pallas_call(
        functools.partial(first_right_kernel, replicas, rank),
        out_shape=[
            jax.ShapeDtypeStruct((size + extra, 128), F32),
            pltpu.VMEM((extra, 128), F32),
            pltpu.VMEM((rank, rows), F32),
            pltpu.VMEM((3 * rank, rows), BF16),
        ],
        in_specs=[SCALAR] + [WHOLE] * 5,
        out_specs=[WHOLE] * 4,
        compiler_params=params(12),
        cost_estimate=cost(3 * rank * rows * columns, 512 * size),
        name="first_right",
    )(meta, *parts, merged)


def second_right(meta, pieces, merged):
    size = pieces.shape[0] // 3 * merged.shape[1] // 256
    return pl.pallas_call(
        second_right_kernel,
        out_shape=pltpu.VMEM((size, 128), F32),
        in_specs=[SCALAR, WHOLE, WHOLE],
        out_specs=WHOLE,
        compiler_params=params(12),
        cost_estimate=cost(pieces.shape[0] * merged.size, 512 * size),
        name="second_right",
    )(meta, pieces, merged)


def pair_kernel(meta_ref, kept_ref, got_ref, ext_ref, *out):
    pair_ref = out[-1]
    grams = ext_ref.shape[0] - ROWS
    ext = kept_ref.shape[0]
    size = ext // QUARTERS
    own, its = ext_ref[grams : grams + 1, :1], got_ref[ext + grams : ext + grams + 1, :1]
    top = jnp.maximum(own, its)
    pair_ref[:grams] = ext_ref[:grams] + got_ref[ext : ext + grams]
    pair_ref[grams:] = jnp.broadcast_to(top, (ROWS, 128))
    own, its = own / top, its / top
    for k, ref in zip((0,) + SHIFTS, out):
        at = pl.ds(pl.multiple_of((meta_ref[1] + k) % QUARTERS * size, size), size)
        ref[...] = kept_ref[at] * own + got_ref[at] * its


def pair(meta, kept, got, ext):
    size = kept.shape[0] // QUARTERS
    return pl.pallas_call(
        pair_kernel,
        out_shape=[jax.ShapeDtypeStruct((size, 128), F32)] * QUARTERS
        + [pltpu.VMEM(ext.shape, F32)],
        in_specs=[SCALAR] + [WHOLE] * 3,
        out_specs=[WHOLE] * (QUARTERS + 1),
        compiler_params=params(8),
        name="pair",
    )(meta, kept, got, ext)


def add_quarters_kernel(meta_ref, a_ref, b_ref, c_ref, d_ref, *out):
    size = a_ref.shape[0] // QUARTERS
    for k, ref in zip((0,) + SHIFTS, out):
        at = pl.ds(pl.multiple_of((meta_ref[2] + k) % QUARTERS * size, size), size)
        ref[...] = (a_ref[at] + b_ref[at]) + (c_ref[at] + d_ref[at])


def add_quarters(meta, parts):
    size = parts[0].shape[0] // QUARTERS
    return pl.pallas_call(
        add_quarters_kernel,
        out_shape=[jax.ShapeDtypeStruct((size, 128), F32)] * QUARTERS,
        in_specs=[SCALAR] + [WHOLE] * QUARTERS,
        out_specs=[WHOLE] * QUARTERS,
        compiler_params=params(8),
        name="add_quarters",
    )(meta, *parts)


def add_parts_kernel(a_ref, b_ref, c_ref, d_ref, ext_ref, out_ref):
    size = a_ref.shape[0]
    out_ref[:size] = (a_ref[...] + b_ref[...]) + (c_ref[...] + d_ref[...])
    out_ref[size:] = ext_ref[...]


def add_parts(parts, ext):
    return pl.pallas_call(
        add_parts_kernel,
        out_shape=jax.ShapeDtypeStruct((parts[0].shape[0] + ext.shape[0], 128), F32),
        in_specs=[WHOLE] * 5,
        out_specs=WHOLE,
        compiler_params=params(8),
        name="add_parts",
    )(*parts, ext)


def across_kernel(a_ref, b_ref, c_ref, d_ref, out_ref, ext_ref):
    size = out_ref.shape[0]
    grams = ext_ref.shape[0] - ROWS
    refs = (a_ref, b_ref, c_ref, d_ref)
    peaks = [r[size + grams : size + grams + 1, :1] for r in refs]
    top = jnp.maximum(jnp.maximum(peaks[0], peaks[1]), jnp.maximum(peaks[2], peaks[3]))
    a, b, c, d = (r[:size] * (k / top) for r, k in zip(refs, peaks))
    out_ref[...] = (a + b) + (c + d)
    a, b, c, d = (r[size : size + grams] for r in refs)
    ext_ref[:grams] = (a + b) + (c + d)
    ext_ref[grams:] = jnp.broadcast_to(top, (ROWS, 128))


def across(parts, extra):
    return pl.pallas_call(
        across_kernel,
        out_shape=[
            jax.ShapeDtypeStruct((parts[0].shape[0] - extra, 128), F32),
            pltpu.VMEM((extra, 128), F32),
        ],
        in_specs=[WHOLE] * 4,
        out_specs=[WHOLE] * 2,
        compiler_params=params(8),
        name="across",
    )(*parts)


def assemble_kernel(meta_ref, a_ref, b_ref, c_ref, d_ref, out_ref):
    size = a_ref.shape[0]
    for k, ref in zip((0,) + SHIFTS, (a_ref, b_ref, c_ref, d_ref)):
        at = pl.multiple_of((meta_ref[2] + QUARTERS - k) % QUARTERS * size, size)
        out_ref[pl.ds(at, size)] = ref[...]


def assemble(meta, parts):
    return pl.pallas_call(
        assemble_kernel,
        out_shape=jax.ShapeDtypeStruct((parts[0].shape[0] * QUARTERS, 128), F32),
        in_specs=[SCALAR] + [WHOLE] * 4,
        out_specs=WHOLE,
        compiler_params=params(8),
        name="assemble",
    )(meta, *parts)


def factor_kernel(replicas, ext_ref, p_ref, solve_ref, hat_ref):
    rank = p_ref.shape[0]
    groups = rank // ROWS
    sub = lax.broadcasted_iota(jnp.int32, (ROWS, 2 * rank), 0)
    lane = lax.broadcasted_iota(jnp.int32, (ROWS, 2 * rank), 1)
    blocks = []
    for g in range(groups):
        tile = ext_ref[g // 2 * ROWS : (g // 2 + 1) * ROWS, (g % 2) * rank : (g % 2 + 1) * rank]
        unit = jnp.where(lane[:, :rank] == sub[:, :rank] + g * ROWS, 1.0, 0.0)
        blocks.append(jnp.concatenate([tile, unit], axis=1))
    for j in range(rank):
        own, at = j // ROWS, j % ROWS
        row = blocks[own][at : at + 1]
        row = row / row[:, j : j + 1]
        for g in range(own, groups):
            column = blocks[g][:, j : j + 1]
            if g == own:
                column = jnp.where(sub[:, :1] > at, column, 0.0)
            blocks[g] = blocks[g] - column * row
    inverse = []
    for g in range(groups):
        diagonal = jnp.sum(
            jnp.where(lane == sub + g * ROWS, blocks[g], 0.0), axis=1, keepdims=True
        )
        inverse.append(blocks[g][:, rank:] / jnp.sqrt(diagonal))
    inverse = jnp.concatenate(inverse, axis=0)
    grams = ext_ref.shape[0] - ROWS
    solve_ref[...] = inverse * (ext_ref[grams : grams + 1, :1] * (1.0 / replicas))
    hat_ref[...] = jnp.dot(inverse, p_ref[...], precision=HIGHEST, preferred_element_type=F32)


def factor(ext, p_mean, replicas):
    rank, rows = p_mean.shape
    return pl.pallas_call(
        functools.partial(factor_kernel, replicas),
        out_shape=[
            jax.ShapeDtypeStruct((rank, rank), F32),
            jax.ShapeDtypeStruct((rank, rows), F32),
        ],
        in_specs=[WHOLE] * 2,
        out_specs=[WHOLE] * 2,
        compiler_params=params(8),
        cost_estimate=cost(1 << 32, 1 << 20),
        name="factor",
    )(ext, p_mean)


def result_kernel(sources, width, meta_ref, solve_ref, p_ref, m_ref, *refs):
    error_hbm, q_hbm, error_ref, q_ref, sems = refs[-5:]
    rank = solve_ref.shape[0]
    columns = q_ref.shape[2]
    left = p_ref[...].T.astype(BF16)
    s1, s2, s3 = split(solve_ref[...])
    solve = jnp.concatenate([s1, s1, s2, s2, s1, s3], axis=1)

    def copies(n, base, at, size):
        to, here = pl.ds(pl.multiple_of(base + at, 128), size), pl.ds(at, size)
        return (
            pltpu.make_async_copy(error_ref.at[n, :, here], error_hbm.at[:, to], sems.at[0, n]),
            pltpu.make_async_copy(q_ref.at[n, :, here], q_hbm.at[:, to], sems.at[1, n]),
        )

    bases = []
    for n, (own, k) in enumerate(sources):
        t_ref = refs[n]
        core = meta_ref[0] if own else 1 - meta_ref[0]
        quarter = (meta_ref[1 if own else 2] + QUARTERS - k) % QUARTERS
        base = (core * QUARTERS + quarter) * columns
        bases.append(base)
        for at in range(0, columns, width):
            t = jnp.concatenate(
                [
                    jnp.concatenate(
                        [
                            t_ref[(g * columns + i) // 128 * ROWS : (g * columns + i) // 128 * ROWS + ROWS, :]
                            for i in range(at, at + width, 128)
                        ],
                        axis=1,
                    )
                    for g in range(rank // ROWS)
                ],
                axis=0,
            )
            t1, t2, t3 = split(t)
            t = jnp.concatenate([t1, t2, t1, t2, t3, t1], axis=0)
            new = jnp.dot(solve, t, preferred_element_type=F32)
            q_ref[n, :, at : at + width] = new
            decoded = jnp.dot(left, new.astype(BF16), preferred_element_type=F32)
            m = m_ref[:, pl.ds(pl.multiple_of(base + at, 128), width)]
            error_ref[n, :, at : at + width] = (m.astype(F32) - decoded).astype(BF16)
            for c in copies(n, base, at, width):
                c.start()
    for n, base in enumerate(bases):
        for c in copies(n, base, 0, columns):
            c.wait()


def result(meta, sources, totals, merged, solve, p_hat, before):
    rank = solve.shape[0]
    rows, columns = merged.shape
    quarter = columns // 2 // QUARTERS
    n = len(sources)
    held = [] if before is None else list(before)
    return pl.pallas_call(
        functools.partial(result_kernel, sources, quarter // 2),
        out_shape=[pltpu.HBM((rows, columns), BF16), pltpu.HBM((rank, columns), F32)],
        in_specs=[SCALAR] + [WHOLE] * (3 + n) + [ANY] * len(held),
        out_specs=[ANY, ANY],
        scratch_shapes=[
            pltpu.VMEM((n, rows, quarter), BF16),
            pltpu.VMEM((n, rank, quarter), F32),
            pltpu.SemaphoreType.DMA((2, n)),
        ],
        input_output_aliases={4 + n + i: i for i in range(len(held))},
        compiler_params=params(12),
        cost_estimate=cost(2 * n * rank * rows * quarter, 4 * n * rows * quarter),
        name="result",
    )(meta, solve, p_hat, merged, *totals, *held)


def body(gradient, error, q_start):
    rank = q_start.shape[0]
    replicas = SIZES[0] * SIZES[1]
    core, x, z = (lax.axis_index(a) for a in ("c", "x", "z"))
    meta = jnp.stack([core, jnp.where(core == 0, x, z), jnp.where(core == 0, z, x)])

    merged, p = merge(meta, gradient[0], error[0], q_start)
    a, b, c = ring_x_or_z([p] * 3, 0)
    p = (p + a) + (b + c)
    sent, ext, p_mean, pieces = first_right(
        meta, (p, *ring_x_or_z([p] * 3, 1)), merged, rank, replicas
    )
    got = swap(sent)
    kept = second_right(meta, pieces, merged)
    own, *sent, ext = pair(meta, kept, got, ext)
    own, *sent = add_quarters(meta, (own, *ring_x_or_z(sent, 0)))
    part = add_parts((own, *ring_x_or_z(sent, 1)), ext)
    total, ext = across((part, *ring_y(part)), ext.shape[0])
    solve, p_hat = factor(ext, p_mean, replicas)
    total = assemble(meta, (total, *ring_x_or_z([total] * 3, 1)))
    totals = dict(zip((0,) + SHIFTS, (total, *ring_x_or_z([total] * 3, 0))))
    out = None
    for own, turns in ((True, (0,)), (False, (0,)), (True, (1, 3)), (False, (1, 3)), (True, (2,)), (False, (2,))):
        sources = tuple((own, k) for k in turns)
        held = [totals[k] if own else swap(totals[k]) for k in turns]
        out = result(meta, sources, held, merged, solve, p_hat, out)
    new_error, q_new = out
    return (new_error[None], p_hat, q_new)


def solution(mesh):
    fine = Mesh(mesh.devices.reshape(SIZES), AXES)
    return jax.shard_map(
        body,
        mesh=fine,
        in_specs=(P(DP, ("y", "c"), None), P(DP, ("y", "c"), None), P()),
        out_specs=(P(DP, ("y", "c"), None), P(None, ("y", "c")), P()),
        check_vma=False,
    )
```

time: 105 us -> 111 us (1.057)
  blocking collectives: 22.2 us -> 0 us
  starting transfers between devices: 27 us -> 46.7 us
  waiting for transfers between devices: 22.5 us -> 29.7 us
  Pallas kernels: 29.7 us -> 32.6 us
  local copies, waits for them, and re-layouts: 2.87 us -> 0.89 us
    all_to_all x1 -> x0, blocking collectives: 22.2 us -> none  [body(): parts = lax.all_to_all(parts, DP, 0, 0)]
    ppermute x6 -> x18, waiting for transfers between devices: 7.37 us -> 25.1 us  [ring_x_or_z(): out.append(lax.ppermute(value, AXES, pairs))]
    ppermute x6 -> x18, starting transfers between devices: 10.3 us -> 22.6 us  [ring_x_or_z(): out.append(lax.ppermute(value, AXES, pairs))]
    ppermute x2 -> x5, starting transfers between devices: 8.54 us -> 19.6 us  [swap(): return lax.ppermute(value, 'c', [(0, 1), (1, 0)])]
    all_to_all x1 -> x0, waiting for transfers between devices: 10.9 us -> none  [body(): totals = lax.all_to_all(totals, DP, 0, 0)]
    all_to_all x1 -> x0, starting transfers between devices: 3.7 us -> none  [body(): totals = lax.all_to_all(totals, DP, 0, 0)]
    pallas_call x7 -> x12, Pallas kernels: 14.3 us -> 17.7 us  [the longest x6 13.9 us: result(): pl.pallas_call(functools.partial(result_kernel, sources, quarter // 2), o...]
    unnamed x6 -> x2, local copies, waits for them, and re-layouts: 2.87 us -> 0.89 us
  transfers between devices with their start and end apart: 12 -> 26, of which waited for: 11 -> 16; matrix products, arithmetic and copies ran while one was open for 0% -> 0% of each run, Pallas kernels for 13% -> 18%
where the time goes in v4:
time: 111 us
  starting transfers between devices  46.7 us (42%)
  Pallas kernels  32.6 us (29%)
  waiting for transfers between devices  29.7 us (27%)
    ppermute x18, waiting for transfers between devices, ring_x_or_z(): out.append(lax.ppermute(value, AXES, pairs))  25.1 us
    ppermute x18, starting transfers between devices, ring_x_or_z(): out.append(lax.ppermute(value, AXES, pairs))  22.6 us
    ppermute x5, starting transfers between devices, swap(): return lax.ppermute(value, 'c', [(0, 1), (1, 0)])  19.6 us
    pallas_call x6, Pallas kernels, result(): pl.pallas_call(functools.partial(result_kernel, sources, quarter // 2), o...  13.9 us
    pallas_call x1, Pallas kernels, merge(): pl.pallas_call(functools.partial(merge_kernel, width), out_shape=[pltpu.V...  6.57 us
    pallas_call x1, Pallas kernels, factor(): pl.pallas_call(functools.partial(factor_kernel, replicas), out_shape=[jax...  6.37 us
    ppermute x3, starting transfers between devices, ring_y(): lax.ppermute(value, 'y', [(i, (i + k) % n) for i in range(n)])  4.45 us
    ppermute x3, waiting for transfers between devices, ring_y(): lax.ppermute(value, 'y', [(i, (i + k) % n) for i in range(n)])  3.55 us
  transfers between devices with their start and end apart: 26, of which 16 were waited for; matrix products, arithmetic and copies ran while one was open for 0% of the time, Pallas kernels for 18%

profile of v4, /device:TPU:1, one launch (start us, length us, event | category | flops | bytes accessed | tf_op | source)
XLA Modules:
  0.0 110.9 jit_solution(1235864887547534146)
XLA Ops:
  0.6 0.1 pad_add_fusion.meta_ref
  0.7 6.6 %merge.1 = (bf16[320,10240]{1,0:T(8,128)(2,1)S(1)}, f32[160,128]{1,0:T(8,128)S(1)}) custom-call(s32[3]{0:T(128)S(1)} %pad_add_fusion.meta_ref, bf16[320,10240]{1,0:T(8,128)(2,1)} %bitcast.7, bf16[320,10240]{1,0:T(8,128)(2,1)} %bitcast.8, bf16[64,10240]{1,0:T(8,128)(2,1)} %q_hbm.1), custom_call_target="tpu_custom_call" | custom-call | flops 419430400 | bytes 13107200 | tf_op jit(solution)/shard_map/merge/pallas_call | solution.py:121
  7.3 2.5 %collective-permute-start = (f32[160,128]{1,0:T(8,128)S(1)}, f32[160,128]{1,0:T(8,128)S(1)}, u32[]{:S(2)}, u32[]{:S(2)}) collective-permute-start(f32[160,128]{1,0:T(8,128)S(1)} %get-tuple-element.34), channel_id=1, source_target_pairs={{0,8},{1,33},{2,10},{3,35},{4,12},{5,37},{6,14},{7,39},{8,16},{9,4... | collective-permute-start | bytes 245768 | tf_op jit(solution)/shard_map/ppermute | solution.py:54
  9.8 2.2 %collective-permute-start.1 = (f32[160,128]{1,0:T(8,128)S(1)}, f32[160,128]{1,0:T(8,128)S(1)}, u32[]{:S(2)}, u32[]{:S(2)}) collective-permute-start(f32[160,128]{1,0:T(8,128)S(1)} %get-tuple-element.34), channel_id=1, source_target_pairs={{0,24},{1,97},{2,26},{3,99},{4,28},{5,101},{6,30},{7,103},{8,0},{9... | collective-permute-start | bytes 245768 | tf_op jit(solution)/shard_map/ppermute | solution.py:54
  12.0 1.2 %collective-permute-start.2 = (f32[160,128]{1,0:T(8,128)S(1)}, f32[160,128]{1,0:T(8,128)S(1)}, u32[]{:S(2)}, u32[]{:S(2)}) collective-permute-start(f32[160,128]{1,0:T(8,128)S(1)} %get-tuple-element.34), channel_id=1, source_target_pairs={{0,16},{1,65},{2,18},{3,67},{4,20},{5,69},{6,22},{7,71},{8,24},{9,... | collective-permute-start | bytes 245768 | tf_op jit(solution)/shard_map/ppermute | solution.py:54
  13.3 0.8 collective-permute-done
  14.0 0.0 collective-permute-done.1
  14.0 3.1 %collective-permute-done.2 = f32[160,128]{1,0:T(8,128)S(1)} collective-permute-done((f32[160,128]{1,0:T(8,128)S(1)}, f32[160,128]{1,0:T(8,128)S(1)}, u32[]{:S(2)}, u32[]{:S(2)}) %collective-permute-start.2) | collective-permute-done | bytes 81952 | tf_op jit(solution)/shard_map/ppermute | solution.py:54
  17.2 1.0 collective-permute-start.3
  18.1 1.8 %collective-permute-start.4 = (f32[160,128]{1,0:T(8,128)S(1)}, f32[160,128]{1,0:T(8,128)S(1)}, u32[]{:S(2)}, u32[]{:S(2)}) collective-permute-start(f32[160,128]{1,0:T(8,128)S(1)} %add_add_fusion.a_ref), channel_id=1, source_target_pairs={{0,96},{1,25},{2,98},{3,27},{4,100},{5,29},{6,102},{7,31},{8,104},... | collective-permute-start | bytes 245768 | tf_op jit(solution)/shard_map/ppermute | solution.py:54
  19.9 1.2 %collective-permute-start.5 = (f32[160,128]{1,0:T(8,128)S(1)}, f32[160,128]{1,0:T(8,128)S(1)}, u32[]{:S(2)}, u32[]{:S(2)}) collective-permute-start(f32[160,128]{1,0:T(8,128)S(1)} %add_add_fusion.a_ref), channel_id=1, source_target_pairs={{0,64},{1,17},{2,66},{3,19},{4,68},{5,21},{6,70},{7,23},{8,72},{9,... | collective-permute-start | bytes 245768 | tf_op jit(solution)/shard_map/ppermute | solution.py:54
  21.1 0.6 collective-permute-done.3.b_ref
  21.7 0.0 collective-permute-done.4.c_ref
  21.7 3.0 %collective-permute-done.5.d_ref = f32[160,128]{1,0:T(8,128)S(1)} collective-permute-done((f32[160,128]{1,0:T(8,128)S(1)}, f32[160,128]{1,0:T(8,128)S(1)}, u32[]{:S(2)}, u32[]{:S(2)}) %collective-permute-start.5) | collective-permute-done | bytes 81952 | tf_op jit(solution)/shard_map/ppermute | solution.py:54
  24.7 1.9 %first_right.1 = (f32[2600,128]{1,0:T(8,128)S(1)}, f32[40,128]{1,0:T(8,128)S(1)}, f32[64,320]{1,0:T(8,128)S(1)}, bf16[192,320]{1,0:T(8,128)(2,1)S(1)}) custom-call(s32[3]{0:T(128)S(1)} %pad_add_fusion.meta_ref, f32[160,128]{1,0:T(8,128)S(1)} %add_add_fusion.a_ref, f32[160,128]{1,0:T(8,128)S(1)} %collective-permute-done.3.b_ref, ...), custom_call_target="tpu_custom_call" | custom-call | flops 629145600 | bytes 1310720 | tf_op jit(solution)/shard_map/first_right/pallas_call | solution.py:192
  26.6 3.6 %collective-permute-start.6 = (f32[2600,128]{1,0:T(8,128)S(1)}, f32[2600,128]{1,0:T(8,128)S(1)}, u32[]{:S(2)}, u32[]{:S(2)}) collective-permute-start(f32[2600,128]{1,0:T(8,128)S(1)} %get-tuple-element.37), channel_id=1, source_target_pairs={{0,1},{1,0},{2,3},{3,2},{4,5},{5,4},{6,7},{7,6},{8,9},{9,8},{10,11... | collective-permute-start | bytes 3993608 | tf_op jit(solution)/shard_map/ppermute | solution.py:64
  30.2 1.7 %second_right.1.kept_ref = f32[2560,128]{1,0:T(8,128)S(1)} custom-call(s32[3]{0:T(128)S(1)} %pad_add_fusion.meta_ref, bf16[192,320]{1,0:T(8,128)(2,1)S(1)} %get-tuple-element.36.pieces_ref, bf16[320,10240]{1,0:T(8,128)(2,1)S(1)} %get-tuple-element.35.m_ref), custom_call_target="tpu_custom_call" | custom-call | flops 629145600 | bytes 1310720 | tf_op jit(solution)/shard_map/second_right/pallas_call | solution.py:210
  31.9 1.0 collective-permute-done.6.got_ref
  32.9 0.8 pair.1
  33.7 0.1 collective-permute-start.7
  33.8 2.7 %collective-permute-start.8 = (f32[640,128]{1,0:T(8,128)S(1)}, f32[640,128]{1,0:T(8,128)S(1)}, u32[]{:S(2)}, u32[]{:S(2)}) collective-permute-start(f32[640,128]{1,0:T(8,128)S(1)} %get-tuple-element.41), channel_id=1, source_target_pairs={{0,24},{1,97},{2,26},{3,99},{4,28},{5,101},{6,30},{7,103},{8,0},{9... | collective-permute-start | bytes 983048 | tf_op jit(solution)/shard_map/ppermute | solution.py:54
  36.5 0.3 collective-permute-start.9
  36.8 4.5 %collective-permute-done.7.b_ref = f32[640,128]{1,0:T(8,128)S(1)} collective-permute-done((f32[640,128]{1,0:T(8,128)S(1)}, f32[640,128]{1,0:T(8,128)S(1)}, u32[]{:S(2)}, u32[]{:S(2)}) %collective-permute-start.7) | collective-permute-done | bytes 327712 | tf_op jit(solution)/shard_map/ppermute | solution.py:54
  41.2 2.8 %collective-permute-done.8.c_ref = f32[640,128]{1,0:T(8,128)S(1)} collective-permute-done((f32[640,128]{1,0:T(8,128)S(1)}, f32[640,128]{1,0:T(8,128)S(1)}, u32[]{:S(2)}, u32[]{:S(2)}) %collective-permute-start.8) | collective-permute-done | bytes 327712 | tf_op jit(solution)/shard_map/ppermute | solution.py:54
  44.0 0.9 collective-permute-done.9.d_ref
  44.9 0.6 add_quarters.1
  45.5 0.1 collective-permute-start.10
  45.6 2.7 %collective-permute-start.11 = (f32[160,128]{1,0:T(8,128)S(1)}, f32[160,128]{1,0:T(8,128)S(1)}, u32[]{:S(2)}, u32[]{:S(2)}) collective-permute-start(f32[160,128]{1,0:T(8,128)S(1)} %get-tuple-element.45), channel_id=1, source_target_pairs={{0,96},{1,25},{2,98},{3,27},{4,100},{5,29},{6,102},{7,31},{8,104},... | collective-permute-start | bytes 245768 | tf_op jit(solution)/shard_map/ppermute | solution.py:54
  48.3 0.0 collective-permute-start.12
  48.3 1.8 %collective-permute-done.10.b_ref = f32[160,128]{1,0:T(8,128)S(1)} collective-permute-done((f32[160,128]{1,0:T(8,128)S(1)}, f32[160,128]{1,0:T(8,128)S(1)}, u32[]{:S(2)}, u32[]{:S(2)}) %collective-permute-start.10) | collective-permute-done | bytes 81952 | tf_op jit(solution)/shard_map/ppermute | solution.py:54
  50.1 0.4 collective-permute-done.11.c_ref
  50.5 2.5 %collective-permute-done.12.d_ref = f32[160,128]{1,0:T(8,128)S(1)} collective-permute-done((f32[160,128]{1,0:T(8,128)S(1)}, f32[160,128]{1,0:T(8,128)S(1)}, u32[]{:S(2)}, u32[]{:S(2)}) %collective-permute-start.12) | collective-permute-done | bytes 81952 | tf_op jit(solution)/shard_map/ppermute | solution.py:54
  53.1 1.4 %collective-permute-start.13 = (f32[200,128]{1,0:T(8,128)S(1)}, f32[200,128]{1,0:T(8,128)S(1)}, u32[]{:S(2)}, u32[]{:S(2)}) collective-permute-start(f32[200,128]{1,0:T(8,128)S(1)} %add_parts.1.a_ref), channel_id=1, source_target_pairs={{0,2},{2,4},{4,6},{6,0},{1,3},{3,5},{5,7},{7,1},{8,10},{10,12},{12... | collective-permute-start | bytes 307208 | tf_op jit(solution)/shard_map/ppermute | solution.py:60
  54.4 1.5 %collective-permute-start.14 = (f32[200,128]{1,0:T(8,128)S(1)}, f32[200,128]{1,0:T(8,128)S(1)}, u32[]{:S(2)}, u32[]{:S(2)}) collective-permute-start(f32[200,128]{1,0:T(8,128)S(1)} %add_parts.1.a_ref), channel_id=1, source_target_pairs={{0,6},{2,0},{4,2},{6,4},{1,7},{3,1},{5,3},{7,5},{8,14},{10,8},{12,... | collective-permute-start | bytes 307208 | tf_op jit(solution)/shard_map/ppermute | solution.py:60
  56.0 1.6 %collective-permute-start.15 = (f32[200,128]{1,0:T(8,128)S(1)}, f32[200,128]{1,0:T(8,128)S(1)}, u32[]{:S(2)}, u32[]{:S(2)}) collective-permute-start(f32[200,128]{1,0:T(8,128)S(1)} %add_parts.1.a_ref), channel_id=1, source_target_pairs={{0,4},{2,6},{4,0},{6,2},{1,5},{3,7},{5,1},{7,3},{8,12},{10,14},{12... | collective-permute-start | bytes 307208 | tf_op jit(solution)/shard_map/ppermute | solution.py:60
  57.5 0.4 collective-permute-done.13.b_ref
  57.9 0.0 collective-permute-done.14.c_ref
  58.0 3.1 %collective-permute-done.15.d_ref = f32[200,128]{1,0:T(8,128)S(1)} collective-permute-done((f32[200,128]{1,0:T(8,128)S(1)}, f32[200,128]{1,0:T(8,128)S(1)}, u32[]{:S(2)}, u32[]{:S(2)}) %collective-permute-start.15) | collective-permute-done | bytes 102432 | tf_op jit(solution)/shard_map/ppermute | solution.py:60
  61.1 0.1 across.1
  61.2 0.1 collective-permute-start.16
  61.2 2.7 %collective-permute-start.17 = (f32[160,128]{1,0:T(8,128)S(1)}, f32[160,128]{1,0:T(8,128)S(1)}, u32[]{:S(2)}, u32[]{:S(2)}) collective-permute-start(f32[160,128]{1,0:T(8,128)S(1)} %get-tuple-element.52.a_ref), channel_id=1, source_target_pairs={{0,96},{1,25},{2,98},{3,27},{4,100},{5,29},{6,102},{7,31},{8,104},... | collective-permute-start | bytes 245768 | tf_op jit(solution)/shard_map/ppermute | solution.py:54
  63.9 0.0 collective-permute-start.18
  63.9 1.8 %collective-permute-done.16.b_ref = f32[160,128]{1,0:T(8,128)S(1)} collective-permute-done((f32[160,128]{1,0:T(8,128)S(1)}, f32[160,128]{1,0:T(8,128)S(1)}, u32[]{:S(2)}, u32[]{:S(2)}) %collective-permute-start.16) | collective-permute-done | bytes 81952 | tf_op jit(solution)/shard_map/ppermute | solution.py:54
  65.7 0.4 collective-permute-done.17.c_ref
  66.2 2.5 %collective-permute-done.18.d_ref = f32[160,128]{1,0:T(8,128)S(1)} collective-permute-done((f32[160,128]{1,0:T(8,128)S(1)}, f32[160,128]{1,0:T(8,128)S(1)}, u32[]{:S(2)}, u32[]{:S(2)}) %collective-permute-start.18) | collective-permute-done | bytes 81952 | tf_op jit(solution)/shard_map/ppermute | solution.py:54
  68.7 0.6 assemble.1.refs_0_
  69.3 1.1 collective-permute-start.21
  70.4 1.9 %collective-permute-start.23 = (f32[640,128]{1,0:T(8,128)S(1)}, f32[640,128]{1,0:T(8,128)S(1)}, u32[]{:S(2)}, u32[]{:S(2)}) collective-permute-start(f32[640,128]{1,0:T(8,128)S(1)} %assemble.1.refs_0_), channel_id=1, source_target_pairs={{0,24},{1,97},{2,26},{3,99},{4,28},{5,101},{6,30},{7,103},{8,0},{9... | collective-permute-start | bytes 983048 | tf_op jit(solution)/shard_map/ppermute | solution.py:54
  72.3 1.1 collective-permute-start.19
  73.4 7.5 %collective-permute-start.25 = (f32[640,128]{1,0:T(8,128)S(1)}, f32[640,128]{1,0:T(8,128)S(1)}, u32[]{:S(2)}, u32[]{:S(2)}) collective-permute-start(f32[640,128]{1,0:T(8,128)S(1)} %assemble.1.refs_0_), channel_id=1, source_target_pairs={{0,1},{1,0},{2,3},{3,2},{4,5},{5,4},{6,7},{7,6},{8,9},{9,8},{10,11... | collective-permute-start | bytes 983048 | tf_op jit(solution)/shard_map/ppermute | solution.py:64
  80.9 0.0 collective-permute-done.21.refs_0_
  80.9 3.6 %collective-permute-start.22 = (f32[640,128]{1,0:T(8,128)S(1)}, f32[640,128]{1,0:T(8,128)S(1)}, u32[]{:S(2)}, u32[]{:S(2)}) collective-permute-start(f32[640,128]{1,0:T(8,128)S(1)} %collective-permute-done.21.refs_0_), channel_id=1, source_target_pairs={{0,1},{1,0},{2,3},{3,2},{4,5},{5,4},{6,7},{7,6},{8,9},{9,8},{10,11... | collective-permute-start | bytes 983048 | tf_op jit(solution)/shard_map/ppermute | solution.py:64
  84.5 0.0 collective-permute-done.23.refs_1_
  84.5 3.2 %collective-permute-start.24 = (f32[640,128]{1,0:T(8,128)S(1)}, f32[640,128]{1,0:T(8,128)S(1)}, u32[]{:S(2)}, u32[]{:S(2)}) collective-permute-start(f32[640,128]{1,0:T(8,128)S(1)} %collective-permute-done.23.refs_1_), channel_id=1, source_target_pairs={{0,1},{1,0},{2,3},{3,2},{4,5},{5,4},{6,7},{7,6},{8,9},{9,8},{10,11... | collective-permute-start | bytes 983048 | tf_op jit(solution)/shard_map/ppermute | solution.py:64
  87.6 0.0 collective-permute-done.19.refs_0_
  87.7 1.8 %collective-permute-start.20 = (f32[640,128]{1,0:T(8,128)S(1)}, f32[640,128]{1,0:T(8,128)S(1)}, u32[]{:S(2)}, u32[]{:S(2)}) collective-permute-start(f32[640,128]{1,0:T(8,128)S(1)} %collective-permute-done.19.refs_0_), channel_id=1, source_target_pairs={{0,1},{1,0},{2,3},{3,2},{4,5},{5,4},{6,7},{7,6},{8,9},{9,8},{10,11... | collective-permute-start | bytes 983048 | tf_op jit(solution)/shard_map/ppermute | solution.py:64
  89.5 6.4 %factor.1 = (f32[64,64]{1,0:T(8,128)S(1)}, f32[64,320]{1,0:T(8,128)}) custom-call(f32[40,128]{1,0:T(8,128)S(1)} %get-tuple-element.48.ext_ref, f32[64,320]{1,0:T(8,128)S(1)} %get-tuple-element.49.p_ref), custom_call_target="tpu_custom_call" | custom-call | flops 4294967296 | bytes 1048576 | tf_op jit(solution)/shard_map/factor/pallas_call | solution.py:363
  95.8 0.9 copy-done
  96.7 2.1 %result.6 = (bf16[320,10240]{1,0:T(8,128)(2,1)}, f32[64,10240]{1,0:T(8,128)}) custom-call(s32[3]{0:T(128)S(1)} %pad_add_fusion.meta_ref, f32[64,64]{1,0:T(8,128)S(1)} %get-tuple-element.50.solve_ref, f32[64,320]{1,0:T(8,128)S(1)} %copy-done, bf16[320,10240]{1,0:T(8,128)(2,1)S(1)} %get-tuple-element.35.m_ref, f32[640,128]{1,0:T(8,128)S(1)} %assemble.1.refs_0_), custom_call_target="tpu_custom_call" | custom-call | flops 52428800 | bytes 1638400 | tf_op jit(solution)/shard_map/result/pallas_call | solution.py:433
  98.9 2.1 %result.7 = (bf16[320,10240]{1,0:T(8,128)(2,1)}, f32[64,10240]{1,0:T(8,128)}) custom-call(s32[3]{0:T(128)S(1)} %pad_add_fusion.meta_ref, f32[64,64]{1,0:T(8,128)S(1)} %get-tuple-element.50.solve_ref, f32[64,320]{1,0:T(8,128)S(1)} %copy-done, bf16[320,10240]{1,0:T(8,128)(2,1)S(1)} %get-tuple-element.35.m_ref, ...), custom_call_target="tpu_custom_call", output_to_operand_aliasing={{0}: (5, {}), {1}: (6, {})} | custom-call | flops 52428800 | bytes 1638400 | tf_op jit(solution)/shard_map/result/pallas_call | solution.py:433
  101.0 2.7 %result.8 = (bf16[320,10240]{1,0:T(8,128)(2,1)}, f32[64,10240]{1,0:T(8,128)}) custom-call(s32[3]{0:T(128)S(1)} %pad_add_fusion.meta_ref, f32[64,64]{1,0:T(8,128)S(1)} %get-tuple-element.50.solve_ref, f32[64,320]{1,0:T(8,128)S(1)} %copy-done, bf16[320,10240]{1,0:T(8,128)(2,1)S(1)} %get-tuple-element.35.m_ref, ...), custom_call_target="tpu_custom_call", output_to_operand_aliasing={{0}: (6, {}), {1}: (7, {})} | custom-call | flops 104857600 | bytes 3276800 | tf_op jit(solution)/shard_map/result/pallas_call | solution.py:433
  103.7 2.7 %result.9 = (bf16[320,10240]{1,0:T(8,128)(2,1)}, f32[64,10240]{1,0:T(8,128)}) custom-call(s32[3]{0:T(128)S(1)} %pad_add_fusion.meta_ref, f32[64,64]{1,0:T(8,128)S(1)} %get-tuple-element.50.solve_ref, f32[64,320]{1,0:T(8,128)S(1)} %copy-done, bf16[320,10240]{1,0:T(8,128)(2,1)S(1)} %get-tuple-element.35.m_ref, ...), custom_call_target="tpu_custom_call", output_to_operand_aliasing={{0}: (6, {}), {1}: (7, {})} | custom-call | flops 104857600 | bytes 3276800 | tf_op jit(solution)/shard_map/result/pallas_call | solution.py:433
  106.4 2.1 %result.10 = (bf16[320,10240]{1,0:T(8,128)(2,1)}, f32[64,10240]{1,0:T(8,128)}) custom-call(s32[3]{0:T(128)S(1)} %pad_add_fusion.meta_ref, f32[64,64]{1,0:T(8,128)S(1)} %get-tuple-element.50.solve_ref, f32[64,320]{1,0:T(8,128)S(1)} %copy-done, bf16[320,10240]{1,0:T(8,128)(2,1)S(1)} %get-tuple-element.35.m_ref, ...), custom_call_target="tpu_custom_call", output_to_operand_aliasing={{0}: (5, {}), {1}: (6, {})} | custom-call | flops 52428800 | bytes 1638400 | tf_op jit(solution)/shard_map/result/pallas_call | solution.py:433
  108.6 2.1 %result.11 = (bf16[320,10240]{1,0:T(8,128)(2,1)}, f32[64,10240]{1,0:T(8,128)}) custom-call(s32[3]{0:T(128)S(1)} %pad_add_fusion.meta_ref, f32[64,64]{1,0:T(8,128)S(1)} %get-tuple-element.50.solve_ref, f32[64,320]{1,0:T(8,128)S(1)} %copy-done, bf16[320,10240]{1,0:T(8,128)(2,1)S(1)} %get-tuple-element.35.m_ref, ...), custom_call_target="tpu_custom_call", output_to_operand_aliasing={{0}: (5, {}), {1}: (6, {})} | custom-call | flops 52428800 | bytes 1638400 | tf_op jit(solution)/shard_map/result/pallas_call | solution.py:433
  (7 shorter events, 0.1 us)
Async XLA Ops:
  7.3 6.7 %collective-permute-start = (f32[160,128]{1,0:T(8,128)S(1)}, f32[160,128]{1,0:T(8,128)S(1)}, u32[]{:S(2)}, u32[]{:S(2)}) collective-permute-start(f32[160,128]{1,0:T(8,128)S(1)} %get-tuple-element.34), channel_id=1, source_target_pairs={{0,8},{1,33},{2,10},{3,35},{4,12},{5,37},{6,14},{7,39},{8,16},{9,4... | collective-permute-start | bytes 245768 | tf_op jit(solution)/shard_map/ppermute | solution.py:54
  9.8 4.2 %collective-permute-start.1 = (f32[160,128]{1,0:T(8,128)S(1)}, f32[160,128]{1,0:T(8,128)S(1)}, u32[]{:S(2)}, u32[]{:S(2)}) collective-permute-start(f32[160,128]{1,0:T(8,128)S(1)} %get-tuple-element.34), channel_id=1, source_target_pairs={{0,24},{1,97},{2,26},{3,99},{4,28},{5,101},{6,30},{7,103},{8,0},{9... | collective-permute-start | bytes 245768 | tf_op jit(solution)/shard_map/ppermute | solution.py:54
  12.0 5.1 %collective-permute-start.2 = (f32[160,128]{1,0:T(8,128)S(1)}, f32[160,128]{1,0:T(8,128)S(1)}, u32[]{:S(2)}, u32[]{:S(2)}) collective-permute-start(f32[160,128]{1,0:T(8,128)S(1)} %get-tuple-element.34), channel_id=1, source_target_pairs={{0,16},{1,65},{2,18},{3,67},{4,20},{5,69},{6,22},{7,71},{8,24},{9,... | collective-permute-start | bytes 245768 | tf_op jit(solution)/shard_map/ppermute | solution.py:54
  17.2 4.6 %collective-permute-start.3 = (f32[160,128]{1,0:T(8,128)S(1)}, f32[160,128]{1,0:T(8,128)S(1)}, u32[]{:S(2)}, u32[]{:S(2)}) collective-permute-start(f32[160,128]{1,0:T(8,128)S(1)} %add_add_fusion.a_ref), channel_id=1, source_target_pairs={{0,32},{1,9},{2,34},{3,11},{4,36},{5,13},{6,38},{7,15},{8,40},{9,1... | collective-permute-start | bytes 245768 | tf_op jit(solution)/shard_map/ppermute | solution.py:54
  18.1 3.6 %collective-permute-start.4 = (f32[160,128]{1,0:T(8,128)S(1)}, f32[160,128]{1,0:T(8,128)S(1)}, u32[]{:S(2)}, u32[]{:S(2)}) collective-permute-start(f32[160,128]{1,0:T(8,128)S(1)} %add_add_fusion.a_ref), channel_id=1, source_target_pairs={{0,96},{1,25},{2,98},{3,27},{4,100},{5,29},{6,102},{7,31},{8,104},... | collective-permute-start | bytes 245768 | tf_op jit(solution)/shard_map/ppermute | solution.py:54
  19.9 4.8 %collective-permute-start.5 = (f32[160,128]{1,0:T(8,128)S(1)}, f32[160,128]{1,0:T(8,128)S(1)}, u32[]{:S(2)}, u32[]{:S(2)}) collective-permute-start(f32[160,128]{1,0:T(8,128)S(1)} %add_add_fusion.a_ref), channel_id=1, source_target_pairs={{0,64},{1,17},{2,66},{3,19},{4,68},{5,21},{6,70},{7,23},{8,72},{9,... | collective-permute-start | bytes 245768 | tf_op jit(solution)/shard_map/ppermute | solution.py:54
  26.6 6.3 %collective-permute-start.6 = (f32[2600,128]{1,0:T(8,128)S(1)}, f32[2600,128]{1,0:T(8,128)S(1)}, u32[]{:S(2)}, u32[]{:S(2)}) collective-permute-start(f32[2600,128]{1,0:T(8,128)S(1)} %get-tuple-element.37), channel_id=1, source_target_pairs={{0,1},{1,0},{2,3},{3,2},{4,5},{5,4},{6,7},{7,6},{8,9},{9,8},{10,11... | collective-permute-start | bytes 3993608 | tf_op jit(solution)/shard_map/ppermute | solution.py:64
  33.7 7.5 %collective-permute-start.7 = (f32[640,128]{1,0:T(8,128)S(1)}, f32[640,128]{1,0:T(8,128)S(1)}, u32[]{:S(2)}, u32[]{:S(2)}) collective-permute-start(f32[640,128]{1,0:T(8,128)S(1)} %get-tuple-element.40), channel_id=1, source_target_pairs={{0,8},{1,33},{2,10},{3,35},{4,12},{5,37},{6,14},{7,39},{8,16},{9,4... | collective-permute-start | bytes 983048 | tf_op jit(solution)/shard_map/ppermute | solution.py:54
  33.8 10.2 %collective-permute-start.8 = (f32[640,128]{1,0:T(8,128)S(1)}, f32[640,128]{1,0:T(8,128)S(1)}, u32[]{:S(2)}, u32[]{:S(2)}) collective-permute-start(f32[640,128]{1,0:T(8,128)S(1)} %get-tuple-element.41), channel_id=1, source_target_pairs={{0,24},{1,97},{2,26},{3,99},{4,28},{5,101},{6,30},{7,103},{8,0},{9... | collective-permute-start | bytes 983048 | tf_op jit(solution)/shard_map/ppermute | solution.py:54
  36.5 8.4 %collective-permute-start.9 = (f32[640,128]{1,0:T(8,128)S(1)}, f32[640,128]{1,0:T(8,128)S(1)}, u32[]{:S(2)}, u32[]{:S(2)}) collective-permute-start(f32[640,128]{1,0:T(8,128)S(1)} %get-tuple-element.42), channel_id=1, source_target_pairs={{0,16},{1,65},{2,18},{3,67},{4,20},{5,69},{6,22},{7,71},{8,24},{9,... | collective-permute-start | bytes 983048 | tf_op jit(solution)/shard_map/ppermute | solution.py:54
  45.5 4.6 %collective-permute-start.10 = (f32[160,128]{1,0:T(8,128)S(1)}, f32[160,128]{1,0:T(8,128)S(1)}, u32[]{:S(2)}, u32[]{:S(2)}) collective-permute-start(f32[160,128]{1,0:T(8,128)S(1)} %get-tuple-element.44), channel_id=1, source_target_pairs={{0,32},{1,9},{2,34},{3,11},{4,36},{5,13},{6,38},{7,15},{8,40},{9,1... | collective-permute-start | bytes 245768 | tf_op jit(solution)/shard_map/ppermute | solution.py:54
  45.6 4.9 %collective-permute-start.11 = (f32[160,128]{1,0:T(8,128)S(1)}, f32[160,128]{1,0:T(8,128)S(1)}, u32[]{:S(2)}, u32[]{:S(2)}) collective-permute-start(f32[160,128]{1,0:T(8,128)S(1)} %get-tuple-element.45), channel_id=1, source_target_pairs={{0,96},{1,25},{2,98},{3,27},{4,100},{5,29},{6,102},{7,31},{8,104},... | collective-permute-start | bytes 245768 | tf_op jit(solution)/shard_map/ppermute | solution.py:54
  48.3 4.8 %collective-permute-start.12 = (f32[160,128]{1,0:T(8,128)S(1)}, f32[160,128]{1,0:T(8,128)S(1)}, u32[]{:S(2)}, u32[]{:S(2)}) collective-permute-start(f32[160,128]{1,0:T(8,128)S(1)} %get-tuple-element.46), channel_id=1, source_target_pairs={{0,64},{1,17},{2,66},{3,19},{4,68},{5,21},{6,70},{7,23},{8,72},{9,... | collective-permute-start | bytes 245768 | tf_op jit(solution)/shard_map/ppermute | solution.py:54
  53.1 4.9 %collective-permute-start.13 = (f32[200,128]{1,0:T(8,128)S(1)}, f32[200,128]{1,0:T(8,128)S(1)}, u32[]{:S(2)}, u32[]{:S(2)}) collective-permute-start(f32[200,128]{1,0:T(8,128)S(1)} %add_parts.1.a_ref), channel_id=1, source_target_pairs={{0,2},{2,4},{4,6},{6,0},{1,3},{3,5},{5,7},{7,1},{8,10},{10,12},{12... | collective-permute-start | bytes 307208 | tf_op jit(solution)/shard_map/ppermute | solution.py:60
  54.4 3.5 %collective-permute-start.14 = (f32[200,128]{1,0:T(8,128)S(1)}, f32[200,128]{1,0:T(8,128)S(1)}, u32[]{:S(2)}, u32[]{:S(2)}) collective-permute-start(f32[200,128]{1,0:T(8,128)S(1)} %add_parts.1.a_ref), channel_id=1, source_target_pairs={{0,6},{2,0},{4,2},{6,4},{1,7},{3,1},{5,3},{7,5},{8,14},{10,8},{12,... | collective-permute-start | bytes 307208 | tf_op jit(solution)/shard_map/ppermute | solution.py:60
  56.0 5.1 %collective-permute-start.15 = (f32[200,128]{1,0:T(8,128)S(1)}, f32[200,128]{1,0:T(8,128)S(1)}, u32[]{:S(2)}, u32[]{:S(2)}) collective-permute-start(f32[200,128]{1,0:T(8,128)S(1)} %add_parts.1.a_ref), channel_id=1, source_target_pairs={{0,4},{2,6},{4,0},{6,2},{1,5},{3,7},{5,1},{7,3},{8,12},{10,14},{12... | collective-permute-start | bytes 307208 | tf_op jit(solution)/shard_map/ppermute | solution.py:60
  61.2 4.6 %collective-permute-start.16 = (f32[160,128]{1,0:T(8,128)S(1)}, f32[160,128]{1,0:T(8,128)S(1)}, u32[]{:S(2)}, u32[]{:S(2)}) collective-permute-start(f32[160,128]{1,0:T(8,128)S(1)} %get-tuple-element.52.a_ref), channel_id=1, source_target_pairs={{0,32},{1,9},{2,34},{3,11},{4,36},{5,13},{6,38},{7,15},{8,40},{9,1... | collective-permute-start | bytes 245768 | tf_op jit(solution)/shard_map/ppermute | solution.py:54
  61.2 4.9 %collective-permute-start.17 = (f32[160,128]{1,0:T(8,128)S(1)}, f32[160,128]{1,0:T(8,128)S(1)}, u32[]{:S(2)}, u32[]{:S(2)}) collective-permute-start(f32[160,128]{1,0:T(8,128)S(1)} %get-tuple-element.52.a_ref), channel_id=1, source_target_pairs={{0,96},{1,25},{2,98},{3,27},{4,100},{5,29},{6,102},{7,31},{8,104},... | collective-permute-start | bytes 245768 | tf_op jit(solution)/shard_map/ppermute | solution.py:54
  63.9 4.8 %collective-permute-start.18 = (f32[160,128]{1,0:T(8,128)S(1)}, f32[160,128]{1,0:T(8,128)S(1)}, u32[]{:S(2)}, u32[]{:S(2)}) collective-permute-start(f32[160,128]{1,0:T(8,128)S(1)} %get-tuple-element.52.a_ref), channel_id=1, source_target_pairs={{0,64},{1,17},{2,66},{3,19},{4,68},{5,21},{6,70},{7,23},{8,72},{9,... | collective-permute-start | bytes 245768 | tf_op jit(solution)/shard_map/ppermute | solution.py:54
  69.3 11.6 %collective-permute-start.21 = (f32[640,128]{1,0:T(8,128)S(1)}, f32[640,128]{1,0:T(8,128)S(1)}, u32[]{:S(2)}, u32[]{:S(2)}) collective-permute-start(f32[640,128]{1,0:T(8,128)S(1)} %assemble.1.refs_0_), channel_id=1, source_target_pairs={{0,8},{1,33},{2,10},{3,35},{4,12},{5,37},{6,14},{7,39},{8,16},{9,4... | collective-permute-start | bytes 983048 | tf_op jit(solution)/shard_map/ppermute | solution.py:54
  70.4 14.1 %collective-permute-start.23 = (f32[640,128]{1,0:T(8,128)S(1)}, f32[640,128]{1,0:T(8,128)S(1)}, u32[]{:S(2)}, u32[]{:S(2)}) collective-permute-start(f32[640,128]{1,0:T(8,128)S(1)} %assemble.1.refs_0_), channel_id=1, source_target_pairs={{0,24},{1,97},{2,26},{3,99},{4,28},{5,101},{6,30},{7,103},{8,0},{9... | collective-permute-start | bytes 983048 | tf_op jit(solution)/shard_map/ppermute | solution.py:54
  72.3 15.3 %collective-permute-start.19 = (f32[640,128]{1,0:T(8,128)S(1)}, f32[640,128]{1,0:T(8,128)S(1)}, u32[]{:S(2)}, u32[]{:S(2)}) collective-permute-start(f32[640,128]{1,0:T(8,128)S(1)} %assemble.1.refs_0_), channel_id=1, source_target_pairs={{0,16},{1,65},{2,18},{3,67},{4,20},{5,69},{6,22},{7,71},{8,24},{9,... | collective-permute-start | bytes 983048 | tf_op jit(solution)/shard_map/ppermute | solution.py:54
  73.4 25.4 %collective-permute-start.25 = (f32[640,128]{1,0:T(8,128)S(1)}, f32[640,128]{1,0:T(8,128)S(1)}, u32[]{:S(2)}, u32[]{:S(2)}) collective-permute-start(f32[640,128]{1,0:T(8,128)S(1)} %assemble.1.refs_0_), channel_id=1, source_target_pairs={{0,1},{1,0},{2,3},{3,2},{4,5},{5,4},{6,7},{7,6},{8,9},{9,8},{10,11... | collective-permute-start | bytes 983048 | tf_op jit(solution)/shard_map/ppermute | solution.py:64
  80.9 22.8 %collective-permute-start.22 = (f32[640,128]{1,0:T(8,128)S(1)}, f32[640,128]{1,0:T(8,128)S(1)}, u32[]{:S(2)}, u32[]{:S(2)}) collective-permute-start(f32[640,128]{1,0:T(8,128)S(1)} %collective-permute-done.21.refs_0_), channel_id=1, source_target_pairs={{0,1},{1,0},{2,3},{3,2},{4,5},{5,4},{6,7},{7,6},{8,9},{9,8},{10,11... | collective-permute-start | bytes 983048 | tf_op jit(solution)/shard_map/ppermute | solution.py:64
  84.5 19.2 %collective-permute-start.24 = (f32[640,128]{1,0:T(8,128)S(1)}, f32[640,128]{1,0:T(8,128)S(1)}, u32[]{:S(2)}, u32[]{:S(2)}) collective-permute-start(f32[640,128]{1,0:T(8,128)S(1)} %collective-permute-done.23.refs_1_), channel_id=1, source_target_pairs={{0,1},{1,0},{2,3},{3,2},{4,5},{5,4},{6,7},{7,6},{8,9},{9,8},{10,11... | collective-permute-start | bytes 983048 | tf_op jit(solution)/shard_map/ppermute | solution.py:64
  87.7 20.9 %collective-permute-start.20 = (f32[640,128]{1,0:T(8,128)S(1)}, f32[640,128]{1,0:T(8,128)S(1)}, u32[]{:S(2)}, u32[]{:S(2)}) collective-permute-start(f32[640,128]{1,0:T(8,128)S(1)} %collective-permute-done.19.refs_0_), channel_id=1, source_target_pairs={{0,1},{1,0},{2,3},{3,2},{4,5},{5,4},{6,7},{7,6},{8,9},{9,8},{10,11... | collective-permute-start | bytes 983048 | tf_op jit(solution)/shard_map/ppermute | solution.py:64
  95.8 0.9 copy-start

commit v5 on v4

--- a/solution.py
+++ b/solution.py
@@ -138,15 +138,21 @@
 def right_tiles(half, pieces, m_ref, out_ref):
     rank = pieces.shape[0] // 3
     width = m_ref.shape[1] // 2 // QUARTERS
-    for a in range(QUARTERS):
-        at = pl.multiple_of(half * (QUARTERS * width) + a * width, width)
+    size = rank * width // 128
+
+    def step(a, carry):
+        at = pl.multiple_of((half * QUARTERS + a) * width, width)
         t = jnp.dot(pieces, m_ref[:, pl.ds(at, width)], preferred_element_type=F32)
         t = t[:rank] + (t[rank : 2 * rank] + t[2 * rank :])
-        to = a * (rank * width // 128)
+        to = 0
         for g in range(rank // ROWS):
             for n in range(width // 128):
-                out_ref[to : to + ROWS, :] = t[g * ROWS : (g + 1) * ROWS, n * 128 : (n + 1) * 128]
+                here = pl.ds(pl.multiple_of(a * size + to, ROWS), ROWS)
+                out_ref[here, :] = t[g * ROWS : (g + 1) * ROWS, n * 128 : (n + 1) * 128]
                 to += ROWS
+        return carry
+
+    lax.fori_loop(0, QUARTERS, step, 0, unroll=2)
 
 
 def split(n):
@@ -309,22 +315,23 @@
     )(*parts)
 
 
-def assemble_kernel(meta_ref, a_ref, b_ref, c_ref, d_ref, out_ref):
+def assemble_kernel(meta_ref, a_ref, b_ref, c_ref, d_ref, after_ref, out_ref):
+    del after_ref
     size = a_ref.shape[0]
     for k, ref in zip((0,) + SHIFTS, (a_ref, b_ref, c_ref, d_ref)):
         at = pl.multiple_of((meta_ref[2] + QUARTERS - k) % QUARTERS * size, size)
         out_ref[pl.ds(at, size)] = ref[...]
 
 
-def assemble(meta, parts):
+def assemble(meta, parts, after):
     return pl.pallas_call(
         assemble_kernel,
         out_shape=jax.ShapeDtypeStruct((parts[0].shape[0] * QUARTERS, 128), F32),
-        in_specs=[SCALAR] + [WHOLE] * 4,
+        in_specs=[SCALAR] + [WHOLE] * 4 + [ANY],
         out_specs=WHOLE,
         compiler_params=params(8),
         name="assemble",
-    )(meta, *parts)
+    )(meta, *parts, after)
 
 
 def factor_kernel(replicas, ext_ref, p_ref, solve_ref, hat_ref):
@@ -375,7 +382,8 @@
 
 
 def result_kernel(sources, width, meta_ref, solve_ref, p_ref, m_ref, *refs):
-    error_hbm, q_hbm, error_ref, q_ref, sems = refs[-5:]
+    error_hbm, q_hbm, token_ref, error_ref, q_ref, sems = refs[-6:]
+    token_ref[...] = jnp.zeros_like(token_ref)
     rank = solve_ref.shape[0]
     columns = q_ref.shape[2]
     left = p_ref[...].T.astype(BF16)
@@ -432,9 +440,13 @@
     held = [] if before is None else list(before)
     return pl.pallas_call(
         functools.partial(result_kernel, sources, quarter // 2),
-        out_shape=[pltpu.HBM((rows, columns), BF16), pltpu.HBM((rank, columns), F32)],
+        out_shape=[
+            pltpu.HBM((rows, columns), BF16),
+            pltpu.HBM((rank, columns), F32),
+            pltpu.VMEM((ROWS, 128), F32),
+        ],
         in_specs=[SCALAR] + [WHOLE] * (3 + n) + [ANY] * len(held),
-        out_specs=[ANY, ANY],
+        out_specs=[ANY, ANY, WHOLE],
         scratch_shapes=[
             pltpu.VMEM((n, rows, quarter), BF16),
             pltpu.VMEM((n, rank, quarter), F32),
@@ -445,6 +457,22 @@
         cost_estimate=cost(2 * n * rank * rows * quarter, 4 * n * rows * quarter),
         name="result",
     )(meta, solve, p_hat, merged, *totals, *held)
+
+
+def tie_kernel(value_ref, after_ref, out_ref):
+    del value_ref, after_ref, out_ref
+
+
+def tie(value, after):
+    return pl.pallas_call(
+        tie_kernel,
+        out_shape=jax.ShapeDtypeStruct(value.shape, value.dtype),
+        in_specs=[ANY] * 2,
+        out_specs=ANY,
+        input_output_aliases={0: 0},
+        compiler_params=params(4),
+        name="tie",
+    )(value, after)
 
 
 def body(gradient, error, q_start):
@@ -466,14 +494,19 @@
     part = add_parts((own, *ring_x_or_z(sent, 1)), ext)
     total, ext = across((part, *ring_y(part)), ext.shape[0])
     solve, p_hat = factor(ext, p_mean, replicas)
-    total = assemble(meta, (total, *ring_x_or_z([total] * 3, 1)))
-    totals = dict(zip((0,) + SHIFTS, (total, *ring_x_or_z([total] * 3, 0))))
-    out = None
-    for own, turns in ((True, (0,)), (False, (0,)), (True, (1, 3)), (False, (1, 3)), (True, (2,)), (False, (2,))):
-        sources = tuple((own, k) for k in turns)
-        held = [totals[k] if own else swap(totals[k]) for k in turns]
-        out = result(meta, sources, held, merged, solve, p_hat, out)
-    new_error, q_new = out
+    total = assemble(meta, (total, *ring_x_or_z([total] * 3, 1)), solve)
+    one, three, two = ring_x_or_z([total] * 3, 0)
+
+    def write(sources, totals, before):
+        return result(meta, sources, totals, merged, solve, p_hat, before)
+
+    *out, token = write(((True, 0), (False, 0)), (total, swap(total)), None)
+    one, three = tie(one, token), tie(three, token)
+    *out, _ = write(((True, 1), (True, 3)), (one, three), out)
+    *out, token = write(((False, 1), (False, 3)), (swap(one), swap(three)), out)
+    two = tie(two, token)
+    *out, _ = write(((True, 2),), (two,), out)
+    new_error, q_new, _ = write(((False, 2),), (swap(two),), out)
     return (new_error[None], p_hat, q_new)
 
 

time: 111 us -> 100 us (0.901)
  starting transfers between devices: 46.7 us -> 37.4 us
  waiting for transfers between devices: 29.7 us -> 27.5 us
    ppermute x5, starting transfers between devices: 19.6 us -> 9.7 us  [swap(): return lax.ppermute(value, 'c', [(0, 1), (1, 0)])]
    ppermute x18, waiting for transfers between devices: 25.1 us -> 21.6 us  [ring_x_or_z(): out.append(lax.ppermute(value, AXES, pairs))]
    ppermute x3, waiting for transfers between devices: 3.55 us -> 5.12 us  [ring_y(): lax.ppermute(value, 'y', [(i, (i + k) % n) for i in range(n)])]
    pallas_call x6 -> x5, Pallas kernels: 13.9 us -> 14 us  [result(): pl.pallas_call(functools.partial(result_kernel, sources, quarter // 2), o...]
  transfers between devices with their start and end apart: 26 -> 26, of which waited for: 16 -> 15; matrix products, arithmetic and copies ran while one was open for 0% -> 0% of each run, Pallas kernels for 18% -> 20%
where the time goes in v5:
time: 100 us
  starting transfers between devices  37.4 us (37%)
  Pallas kernels  33.3 us (33%)
  waiting for transfers between devices  27.5 us (28%)
    ppermute x18, starting transfers between devices, ring_x_or_z(): out.append(lax.ppermute(value, AXES, pairs))  23.2 us
    ppermute x18, waiting for transfers between devices, ring_x_or_z(): out.append(lax.ppermute(value, AXES, pairs))  21.6 us
    pallas_call x5, Pallas kernels, result(): pl.pallas_call(functools.partial(result_kernel, sources, quarter // 2), o...  14 us
    ppermute x5, starting transfers between devices, swap(): return lax.ppermute(value, 'c', [(0, 1), (1, 0)])  9.7 us
    pallas_call x1, Pallas kernels, merge(): pl.pallas_call(functools.partial(merge_kernel, width), out_shape=[pltpu.V...  6.57 us
    pallas_call x1, Pallas kernels, factor(): pl.pallas_call(functools.partial(factor_kernel, replicas), out_shape=[jax...  6.37 us
    ppermute x3, waiting for transfers between devices, ring_y(): lax.ppermute(value, 'y', [(i, (i + k) % n) for i in range(n)])  5.12 us
    ppermute x3, starting transfers between devices, ring_y(): lax.ppermute(value, 'y', [(i, (i + k) % n) for i in range(n)])  4.46 us
  transfers between devices with their start and end apart: 26, of which 15 were waited for; matrix products, arithmetic and copies ran while one was open for 0% of the time, Pallas kernels for 20%

profile of v5, /device:TPU:1, one launch (start us, length us, event | category | flops | bytes accessed | tf_op | source)
XLA Modules:
  0.0 100.1 jit_solution(719603648497064019)
XLA Ops:
  0.6 0.1 pad_add_fusion.meta_ref
  0.7 6.6 %merge.1 = (bf16[320,10240]{1,0:T(8,128)(2,1)S(1)}, f32[160,128]{1,0:T(8,128)S(1)}) custom-call(s32[3]{0:T(128)S(1)} %pad_add_fusion.meta_ref, bf16[320,10240]{1,0:T(8,128)(2,1)} %bitcast.7, bf16[320,10240]{1,0:T(8,128)(2,1)} %bitcast.8, bf16[64,10240]{1,0:T(8,128)(2,1)} %q_hbm.1), custom_call_target="tpu_custom_call" | custom-call | flops 419430400 | bytes 13107200 | tf_op jit(solution)/shard_map/merge/pallas_call | solution.py:121
  7.3 4.5 %collective-permute-start.2 = (f32[160,128]{1,0:T(8,128)S(1)}, f32[160,128]{1,0:T(8,128)S(1)}, u32[]{:S(2)}, u32[]{:S(2)}) collective-permute-start(f32[160,128]{1,0:T(8,128)S(1)} %get-tuple-element.34), channel_id=1, source_target_pairs={{0,16},{1,65},{2,18},{3,67},{4,20},{5,69},{6,22},{7,71},{8,24},{9,... | collective-permute-start | bytes 245768 | tf_op jit(solution)/shard_map/ppermute | solution.py:54
  11.8 0.4 collective-permute-start.1
  12.2 1.0 %collective-permute-start = (f32[160,128]{1,0:T(8,128)S(1)}, f32[160,128]{1,0:T(8,128)S(1)}, u32[]{:S(2)}, u32[]{:S(2)}) collective-permute-start(f32[160,128]{1,0:T(8,128)S(1)} %get-tuple-element.34), channel_id=1, source_target_pairs={{0,8},{1,33},{2,10},{3,35},{4,12},{5,37},{6,14},{7,39},{8,16},{9,4... | collective-permute-start | bytes 245768 | tf_op jit(solution)/shard_map/ppermute | solution.py:54
  13.3 0.7 collective-permute-done.2
  13.9 1.6 %collective-permute-done.1 = f32[160,128]{1,0:T(8,128)S(1)} collective-permute-done((f32[160,128]{1,0:T(8,128)S(1)}, f32[160,128]{1,0:T(8,128)S(1)}, u32[]{:S(2)}, u32[]{:S(2)}) %collective-permute-start.1) | collective-permute-done | bytes 81952 | tf_op jit(solution)/shard_map/ppermute | solution.py:54
  15.5 1.2 %collective-permute-done = f32[160,128]{1,0:T(8,128)S(1)} collective-permute-done((f32[160,128]{1,0:T(8,128)S(1)}, f32[160,128]{1,0:T(8,128)S(1)}, u32[]{:S(2)}, u32[]{:S(2)}) %collective-permute-start) | collective-permute-done | bytes 81952 | tf_op jit(solution)/shard_map/ppermute | solution.py:54
  16.8 2.8 %collective-permute-start.5 = (f32[160,128]{1,0:T(8,128)S(1)}, f32[160,128]{1,0:T(8,128)S(1)}, u32[]{:S(2)}, u32[]{:S(2)}) collective-permute-start(f32[160,128]{1,0:T(8,128)S(1)} %add_add_fusion.a_ref), channel_id=1, source_target_pairs={{0,64},{1,17},{2,66},{3,19},{4,68},{5,21},{6,70},{7,23},{8,72},{9,... | collective-permute-start | bytes 245768 | tf_op jit(solution)/shard_map/ppermute | solution.py:54
  19.6 0.9 collective-permute-start.4
  20.4 0.6 collective-permute-start.3
  21.1 0.6 collective-permute-done.5.d_ref
  21.6 1.2 %collective-permute-done.4.c_ref = f32[160,128]{1,0:T(8,128)S(1)} collective-permute-done((f32[160,128]{1,0:T(8,128)S(1)}, f32[160,128]{1,0:T(8,128)S(1)}, u32[]{:S(2)}, u32[]{:S(2)}) %collective-permute-start.4) | collective-permute-done | bytes 81952 | tf_op jit(solution)/shard_map/ppermute | solution.py:54
  22.9 2.1 %collective-permute-done.3.b_ref = f32[160,128]{1,0:T(8,128)S(1)} collective-permute-done((f32[160,128]{1,0:T(8,128)S(1)}, f32[160,128]{1,0:T(8,128)S(1)}, u32[]{:S(2)}, u32[]{:S(2)}) %collective-permute-start.3) | collective-permute-done | bytes 81952 | tf_op jit(solution)/shard_map/ppermute | solution.py:54
  24.9 2.3 %first_right.1 = (f32[2600,128]{1,0:T(8,128)S(1)}, f32[40,128]{1,0:T(8,128)S(1)}, f32[64,320]{1,0:T(8,128)S(1)}, bf16[192,320]{1,0:T(8,128)(2,1)S(1)}) custom-call(s32[3]{0:T(128)S(1)} %pad_add_fusion.meta_ref, f32[160,128]{1,0:T(8,128)S(1)} %add_add_fusion.a_ref, f32[160,128]{1,0:T(8,128)S(1)} %collective-permute-done.3.b_ref, ...), custom_call_target="tpu_custom_call" | custom-call | flops 629145600 | bytes 1310720 | tf_op jit(solution)/shard_map/first_right/pallas_call | solution.py:198
  27.2 4.2 %collective-permute-start.6 = (f32[2600,128]{1,0:T(8,128)S(1)}, f32[2600,128]{1,0:T(8,128)S(1)}, u32[]{:S(2)}, u32[]{:S(2)}) collective-permute-start(f32[2600,128]{1,0:T(8,128)S(1)} %get-tuple-element.37), channel_id=1, source_target_pairs={{0,1},{1,0},{2,3},{3,2},{4,5},{5,4},{6,7},{7,6},{8,9},{9,8},{10,11... | collective-permute-start | bytes 3993608 | tf_op jit(solution)/shard_map/ppermute | solution.py:64
  31.4 1.9 %second_right.1.kept_ref = f32[2560,128]{1,0:T(8,128)S(1)} custom-call(s32[3]{0:T(128)S(1)} %pad_add_fusion.meta_ref, bf16[192,320]{1,0:T(8,128)(2,1)S(1)} %get-tuple-element.36.pieces_ref, bf16[320,10240]{1,0:T(8,128)(2,1)S(1)} %get-tuple-element.35.m_ref), custom_call_target="tpu_custom_call" | custom-call | flops 629145600 | bytes 1310720 | tf_op jit(solution)/shard_map/second_right/pallas_call | solution.py:216
  33.3 0.8 collective-permute-done.6.got_ref
  34.1 0.8 pair.1
  34.9 0.1 collective-permute-start.7
  35.0 2.7 %collective-permute-start.8 = (f32[640,128]{1,0:T(8,128)S(1)}, f32[640,128]{1,0:T(8,128)S(1)}, u32[]{:S(2)}, u32[]{:S(2)}) collective-permute-start(f32[640,128]{1,0:T(8,128)S(1)} %get-tuple-element.41), channel_id=1, source_target_pairs={{0,24},{1,97},{2,26},{3,99},{4,28},{5,101},{6,30},{7,103},{8,0},{9... | collective-permute-start | bytes 983048 | tf_op jit(solution)/shard_map/ppermute | solution.py:54
  37.7 0.0 collective-permute-start.9
  37.7 8.3 %collective-permute-done.7.b_ref = f32[640,128]{1,0:T(8,128)S(1)} collective-permute-done((f32[640,128]{1,0:T(8,128)S(1)}, f32[640,128]{1,0:T(8,128)S(1)}, u32[]{:S(2)}, u32[]{:S(2)}) %collective-permute-start.7) | collective-permute-done | bytes 327712 | tf_op jit(solution)/shard_map/ppermute | solution.py:54
  45.9 0.0 collective-permute-done.8.c_ref
  45.9 0.0 collective-permute-done.9.d_ref
  45.9 0.6 add_quarters.1
  46.5 0.1 collective-permute-start.10
  46.6 2.7 %collective-permute-start.11 = (f32[160,128]{1,0:T(8,128)S(1)}, f32[160,128]{1,0:T(8,128)S(1)}, u32[]{:S(2)}, u32[]{:S(2)}) collective-permute-start(f32[160,128]{1,0:T(8,128)S(1)} %get-tuple-element.45), channel_id=1, source_target_pairs={{0,96},{1,25},{2,98},{3,27},{4,100},{5,29},{6,102},{7,31},{8,104},... | collective-permute-start | bytes 245768 | tf_op jit(solution)/shard_map/ppermute | solution.py:54
  49.3 0.0 collective-permute-start.12
  49.3 1.8 %collective-permute-done.10.b_ref = f32[160,128]{1,0:T(8,128)S(1)} collective-permute-done((f32[160,128]{1,0:T(8,128)S(1)}, f32[160,128]{1,0:T(8,128)S(1)}, u32[]{:S(2)}, u32[]{:S(2)}) %collective-permute-start.10) | collective-permute-done | bytes 81952 | tf_op jit(solution)/shard_map/ppermute | solution.py:54
  51.1 0.4 collective-permute-done.11.c_ref
  51.6 2.5 %collective-permute-done.12.d_ref = f32[160,128]{1,0:T(8,128)S(1)} collective-permute-done((f32[160,128]{1,0:T(8,128)S(1)}, f32[160,128]{1,0:T(8,128)S(1)}, u32[]{:S(2)}, u32[]{:S(2)}) %collective-permute-start.12) | collective-permute-done | bytes 81952 | tf_op jit(solution)/shard_map/ppermute | solution.py:54
  54.1 3.0 %collective-permute-start.15 = (f32[200,128]{1,0:T(8,128)S(1)}, f32[200,128]{1,0:T(8,128)S(1)}, u32[]{:S(2)}, u32[]{:S(2)}) collective-permute-start(f32[200,128]{1,0:T(8,128)S(1)} %add_parts.1.a_ref), channel_id=1, source_target_pairs={{0,4},{2,6},{4,0},{6,2},{1,5},{3,7},{5,1},{7,3},{8,12},{10,14},{12... | collective-permute-start | bytes 307208 | tf_op jit(solution)/shard_map/ppermute | solution.py:60
  57.1 0.8 collective-permute-start.14
  57.9 0.7 collective-permute-start.13
  58.6 0.6 collective-permute-done.15.d_ref
  59.2 1.4 %collective-permute-done.14.c_ref = f32[200,128]{1,0:T(8,128)S(1)} collective-permute-done((f32[200,128]{1,0:T(8,128)S(1)}, f32[200,128]{1,0:T(8,128)S(1)}, u32[]{:S(2)}, u32[]{:S(2)}) %collective-permute-start.14) | collective-permute-done | bytes 102432 | tf_op jit(solution)/shard_map/ppermute | solution.py:60
  60.7 3.1 %collective-permute-done.13.b_ref = f32[200,128]{1,0:T(8,128)S(1)} collective-permute-done((f32[200,128]{1,0:T(8,128)S(1)}, f32[200,128]{1,0:T(8,128)S(1)}, u32[]{:S(2)}, u32[]{:S(2)}) %collective-permute-start.13) | collective-permute-done | bytes 102432 | tf_op jit(solution)/shard_map/ppermute | solution.py:60
  63.7 0.1 across.1
  63.8 0.1 collective-permute-start.18
  63.9 0.4 collective-permute-start.17
  64.3 1.1 %collective-permute-start.16 = (f32[160,128]{1,0:T(8,128)S(1)}, f32[160,128]{1,0:T(8,128)S(1)}, u32[]{:S(2)}, u32[]{:S(2)}) collective-permute-start(f32[160,128]{1,0:T(8,128)S(1)} %get-tuple-element.52.a_ref), channel_id=1, source_target_pairs={{0,32},{1,9},{2,34},{3,11},{4,36},{5,13},{6,38},{7,15},{8,40},{9,1... | collective-permute-start | bytes 245768 | tf_op jit(solution)/shard_map/ppermute | solution.py:54
  65.4 6.4 %factor.1 = (f32[64,64]{1,0:T(8,128)S(1)}, f32[64,320]{1,0:T(8,128)}) custom-call(f32[40,128]{1,0:T(8,128)S(1)} %get-tuple-element.48.ext_ref, f32[64,320]{1,0:T(8,128)S(1)} %get-tuple-element.49.p_ref), custom_call_target="tpu_custom_call" | custom-call | flops 4294967296 | bytes 1048576 | tf_op jit(solution)/shard_map/factor/pallas_call | solution.py:370
  71.8 0.0 collective-permute-done.18.d_ref
  71.8 0.0 collective-permute-done.17.c_ref
  71.8 0.0 collective-permute-done.16.b_ref
  71.8 0.6 assemble.1.refs_0_
  72.4 4.2 %collective-permute-start.21 = (f32[640,128]{1,0:T(8,128)S(1)}, f32[640,128]{1,0:T(8,128)S(1)}, u32[]{:S(2)}, u32[]{:S(2)}) collective-permute-start(f32[640,128]{1,0:T(8,128)S(1)} %assemble.1.refs_0_), channel_id=1, source_target_pairs={{0,1},{1,0},{2,3},{3,2},{4,5},{5,4},{6,7},{7,6},{8,9},{9,8},{10,11... | collective-permute-start | bytes 983048 | tf_op jit(solution)/shard_map/ppermute | solution.py:64
  76.6 1.1 %collective-permute-start.20 = (f32[640,128]{1,0:T(8,128)S(1)}, f32[640,128]{1,0:T(8,128)S(1)}, u32[]{:S(2)}, u32[]{:S(2)}) collective-permute-start(f32[640,128]{1,0:T(8,128)S(1)} %assemble.1.refs_0_), channel_id=1, source_target_pairs={{0,8},{1,33},{2,10},{3,35},{4,12},{5,37},{6,14},{7,39},{8,16},{9,4... | collective-permute-start | bytes 983048 | tf_op jit(solution)/shard_map/ppermute | solution.py:54
  77.7 1.6 %collective-permute-start.23 = (f32[640,128]{1,0:T(8,128)S(1)}, f32[640,128]{1,0:T(8,128)S(1)}, u32[]{:S(2)}, u32[]{:S(2)}) collective-permute-start(f32[640,128]{1,0:T(8,128)S(1)} %assemble.1.refs_0_), channel_id=1, source_target_pairs={{0,24},{1,97},{2,26},{3,99},{4,28},{5,101},{6,30},{7,103},{8,0},{9... | collective-permute-start | bytes 983048 | tf_op jit(solution)/shard_map/ppermute | solution.py:54
  79.3 0.9 copy-done
  80.2 2.7 %result.5 = (bf16[320,10240]{1,0:T(8,128)(2,1)}, f32[64,10240]{1,0:T(8,128)}, f32[8,128]{1,0:T(8,128)S(1)}) custom-call(s32[3]{0:T(128)S(1)} %pad_add_fusion.meta_ref, f32[64,64]{1,0:T(8,128)S(1)} %get-tuple-element.50.after_ref.solve_ref, f32[64,320]{1,0:T(8,128)S(1)} %copy-done, bf16[320,10240]{1,0:T(8,128)(2,1)S(1)} %get-tuple-element.35.m_ref, ...), custom_call_target="tpu_custom_call" | custom-call | flops 104857600 | bytes 3276800 | tf_op jit(solution)/shard_map/result/pallas_call | solution.py:441
  82.8 1.2 %collective-permute-done.20.value_ref = f32[640,128]{1,0:T(8,128)S(1)} collective-permute-done((f32[640,128]{1,0:T(8,128)S(1)}, f32[640,128]{1,0:T(8,128)S(1)}, u32[]{:S(2)}, u32[]{:S(2)}) %collective-permute-start.20) | collective-permute-done | bytes 327712 | tf_op jit(solution)/shard_map/ppermute | solution.py:54
  84.0 0.9 collective-permute-start.22
  85.0 0.0 collective-permute-done.23.value_ref
  85.0 0.1 collective-permute-start.24
  85.0 3.2 %collective-permute-start.19 = (f32[640,128]{1,0:T(8,128)S(1)}, f32[640,128]{1,0:T(8,128)S(1)}, u32[]{:S(2)}, u32[]{:S(2)}) collective-permute-start(f32[640,128]{1,0:T(8,128)S(1)} %assemble.1.refs_0_), channel_id=1, source_target_pairs={{0,16},{1,65},{2,18},{3,67},{4,20},{5,69},{6,22},{7,71},{8,24},{9,... | collective-permute-start | bytes 983048 | tf_op jit(solution)/shard_map/ppermute | solution.py:54
  88.2 3.3 %result.6 = (bf16[320,10240]{1,0:T(8,128)(2,1)}, f32[64,10240]{1,0:T(8,128)}, f32[8,128]{1,0:T(8,128)}) custom-call(s32[3]{0:T(128)S(1)} %pad_add_fusion.meta_ref, f32[64,64]{1,0:T(8,128)S(1)} %get-tuple-element.50.after_ref.solve_ref, f32[64,320]{1,0:T(8,128)S(1)} %copy-done, ...), custom_call_target="tpu_custom_call", output_to_operand_aliasing={{0}: (6, {}), {1}: (7, {})} | custom-call | flops 104857600 | bytes 3276800 | tf_op jit(solution)/shard_map/result/pallas_call | solution.py:441
  91.5 0.0 collective-permute-done.24.refs_1_
  91.5 2.7 %result.7 = (bf16[320,10240]{1,0:T(8,128)(2,1)}, f32[64,10240]{1,0:T(8,128)}, f32[8,128]{1,0:T(8,128)S(1)}) custom-call(s32[3]{0:T(128)S(1)} %pad_add_fusion.meta_ref, f32[64,64]{1,0:T(8,128)S(1)} %get-tuple-element.50.after_ref.solve_ref, f32[64,320]{1,0:T(8,128)S(1)} %copy-done, ...), custom_call_target="tpu_custom_call", output_to_operand_aliasing={{0}: (6, {}), {1}: (7, {})} | custom-call | flops 104857600 | bytes 3276800 | tf_op jit(solution)/shard_map/result/pallas_call | solution.py:441
  94.2 0.0 collective-permute-done.19.value_ref
  94.2 0.3 collective-permute-start.25
  94.5 2.7 %result.8 = (bf16[320,10240]{1,0:T(8,128)(2,1)}, f32[64,10240]{1,0:T(8,128)}, f32[8,128]{1,0:T(8,128)}) custom-call(s32[3]{0:T(128)S(1)} %pad_add_fusion.meta_ref, f32[64,64]{1,0:T(8,128)S(1)} %get-tuple-element.50.after_ref.solve_ref, f32[64,320]{1,0:T(8,128)S(1)} %copy-done, ...), custom_call_target="tpu_custom_call", output_to_operand_aliasing={{0}: (5, {}), {1}: (6, {})} | custom-call | flops 52428800 | bytes 1638400 | tf_op jit(solution)/shard_map/result/pallas_call | solution.py:441
  97.2 2.7 %result.9 = (bf16[320,10240]{1,0:T(8,128)(2,1)}, f32[64,10240]{1,0:T(8,128)}, f32[8,128]{1,0:T(8,128)}) custom-call(s32[3]{0:T(128)S(1)} %pad_add_fusion.meta_ref, f32[64,64]{1,0:T(8,128)S(1)} %get-tuple-element.50.after_ref.solve_ref, f32[64,320]{1,0:T(8,128)S(1)} %copy-done, ...), custom_call_target="tpu_custom_call", output_to_operand_aliasing={{0}: (5, {}), {1}: (6, {})} | custom-call | flops 52428800 | bytes 1638400 | tf_op jit(solution)/shard_map/result/pallas_call | solution.py:441
  (9 shorter events, 0.1 us)
Async XLA Ops:
  7.3 6.6 %collective-permute-start.2 = (f32[160,128]{1,0:T(8,128)S(1)}, f32[160,128]{1,0:T(8,128)S(1)}, u32[]{:S(2)}, u32[]{:S(2)}) collective-permute-start(f32[160,128]{1,0:T(8,128)S(1)} %get-tuple-element.34), channel_id=1, source_target_pairs={{0,16},{1,65},{2,18},{3,67},{4,20},{5,69},{6,22},{7,71},{8,24},{9,... | collective-permute-start | bytes 245768 | tf_op jit(solution)/shard_map/ppermute | solution.py:54
  11.8 3.7 %collective-permute-start.1 = (f32[160,128]{1,0:T(8,128)S(1)}, f32[160,128]{1,0:T(8,128)S(1)}, u32[]{:S(2)}, u32[]{:S(2)}) collective-permute-start(f32[160,128]{1,0:T(8,128)S(1)} %get-tuple-element.34), channel_id=1, source_target_pairs={{0,24},{1,97},{2,26},{3,99},{4,28},{5,101},{6,30},{7,103},{8,0},{9... | collective-permute-start | bytes 245768 | tf_op jit(solution)/shard_map/ppermute | solution.py:54
  12.2 4.5 %collective-permute-start = (f32[160,128]{1,0:T(8,128)S(1)}, f32[160,128]{1,0:T(8,128)S(1)}, u32[]{:S(2)}, u32[]{:S(2)}) collective-permute-start(f32[160,128]{1,0:T(8,128)S(1)} %get-tuple-element.34), channel_id=1, source_target_pairs={{0,8},{1,33},{2,10},{3,35},{4,12},{5,37},{6,14},{7,39},{8,16},{9,4... | collective-permute-start | bytes 245768 | tf_op jit(solution)/shard_map/ppermute | solution.py:54
  16.8 4.9 %collective-permute-start.5 = (f32[160,128]{1,0:T(8,128)S(1)}, f32[160,128]{1,0:T(8,128)S(1)}, u32[]{:S(2)}, u32[]{:S(2)}) collective-permute-start(f32[160,128]{1,0:T(8,128)S(1)} %add_add_fusion.a_ref), channel_id=1, source_target_pairs={{0,64},{1,17},{2,66},{3,19},{4,68},{5,21},{6,70},{7,23},{8,72},{9,... | collective-permute-start | bytes 245768 | tf_op jit(solution)/shard_map/ppermute | solution.py:54
  19.6 3.3 %collective-permute-start.4 = (f32[160,128]{1,0:T(8,128)S(1)}, f32[160,128]{1,0:T(8,128)S(1)}, u32[]{:S(2)}, u32[]{:S(2)}) collective-permute-start(f32[160,128]{1,0:T(8,128)S(1)} %add_add_fusion.a_ref), channel_id=1, source_target_pairs={{0,96},{1,25},{2,98},{3,27},{4,100},{5,29},{6,102},{7,31},{8,104},... | collective-permute-start | bytes 245768 | tf_op jit(solution)/shard_map/ppermute | solution.py:54
  20.4 4.5 %collective-permute-start.3 = (f32[160,128]{1,0:T(8,128)S(1)}, f32[160,128]{1,0:T(8,128)S(1)}, u32[]{:S(2)}, u32[]{:S(2)}) collective-permute-start(f32[160,128]{1,0:T(8,128)S(1)} %add_add_fusion.a_ref), channel_id=1, source_target_pairs={{0,32},{1,9},{2,34},{3,11},{4,36},{5,13},{6,38},{7,15},{8,40},{9,1... | collective-permute-start | bytes 245768 | tf_op jit(solution)/shard_map/ppermute | solution.py:54
  27.2 6.9 %collective-permute-start.6 = (f32[2600,128]{1,0:T(8,128)S(1)}, f32[2600,128]{1,0:T(8,128)S(1)}, u32[]{:S(2)}, u32[]{:S(2)}) collective-permute-start(f32[2600,128]{1,0:T(8,128)S(1)} %get-tuple-element.37), channel_id=1, source_target_pairs={{0,1},{1,0},{2,3},{3,2},{4,5},{5,4},{6,7},{7,6},{8,9},{9,8},{10,11... | collective-permute-start | bytes 3993608 | tf_op jit(solution)/shard_map/ppermute | solution.py:64
  34.9 11.0 %collective-permute-start.7 = (f32[640,128]{1,0:T(8,128)S(1)}, f32[640,128]{1,0:T(8,128)S(1)}, u32[]{:S(2)}, u32[]{:S(2)}) collective-permute-start(f32[640,128]{1,0:T(8,128)S(1)} %get-tuple-element.40), channel_id=1, source_target_pairs={{0,8},{1,33},{2,10},{3,35},{4,12},{5,37},{6,14},{7,39},{8,16},{9,4... | collective-permute-start | bytes 983048 | tf_op jit(solution)/shard_map/ppermute | solution.py:54
  35.0 10.9 %collective-permute-start.8 = (f32[640,128]{1,0:T(8,128)S(1)}, f32[640,128]{1,0:T(8,128)S(1)}, u32[]{:S(2)}, u32[]{:S(2)}) collective-permute-start(f32[640,128]{1,0:T(8,128)S(1)} %get-tuple-element.41), channel_id=1, source_target_pairs={{0,24},{1,97},{2,26},{3,99},{4,28},{5,101},{6,30},{7,103},{8,0},{9... | collective-permute-start | bytes 983048 | tf_op jit(solution)/shard_map/ppermute | solution.py:54
  37.7 8.3 %collective-permute-start.9 = (f32[640,128]{1,0:T(8,128)S(1)}, f32[640,128]{1,0:T(8,128)S(1)}, u32[]{:S(2)}, u32[]{:S(2)}) collective-permute-start(f32[640,128]{1,0:T(8,128)S(1)} %get-tuple-element.42), channel_id=1, source_target_pairs={{0,16},{1,65},{2,18},{3,67},{4,20},{5,69},{6,22},{7,71},{8,24},{9,... | collective-permute-start | bytes 983048 | tf_op jit(solution)/shard_map/ppermute | solution.py:54
  46.5 4.6 %collective-permute-start.10 = (f32[160,128]{1,0:T(8,128)S(1)}, f32[160,128]{1,0:T(8,128)S(1)}, u32[]{:S(2)}, u32[]{:S(2)}) collective-permute-start(f32[160,128]{1,0:T(8,128)S(1)} %get-tuple-element.44), channel_id=1, source_target_pairs={{0,32},{1,9},{2,34},{3,11},{4,36},{5,13},{6,38},{7,15},{8,40},{9,1... | collective-permute-start | bytes 245768 | tf_op jit(solution)/shard_map/ppermute | solution.py:54
  46.6 4.9 %collective-permute-start.11 = (f32[160,128]{1,0:T(8,128)S(1)}, f32[160,128]{1,0:T(8,128)S(1)}, u32[]{:S(2)}, u32[]{:S(2)}) collective-permute-start(f32[160,128]{1,0:T(8,128)S(1)} %get-tuple-element.45), channel_id=1, source_target_pairs={{0,96},{1,25},{2,98},{3,27},{4,100},{5,29},{6,102},{7,31},{8,104},... | collective-permute-start | bytes 245768 | tf_op jit(solution)/shard_map/ppermute | solution.py:54
  49.3 4.8 %collective-permute-start.12 = (f32[160,128]{1,0:T(8,128)S(1)}, f32[160,128]{1,0:T(8,128)S(1)}, u32[]{:S(2)}, u32[]{:S(2)}) collective-permute-start(f32[160,128]{1,0:T(8,128)S(1)} %get-tuple-element.46), channel_id=1, source_target_pairs={{0,64},{1,17},{2,66},{3,19},{4,68},{5,21},{6,70},{7,23},{8,72},{9,... | collective-permute-start | bytes 245768 | tf_op jit(solution)/shard_map/ppermute | solution.py:54
  54.1 5.1 %collective-permute-start.15 = (f32[200,128]{1,0:T(8,128)S(1)}, f32[200,128]{1,0:T(8,128)S(1)}, u32[]{:S(2)}, u32[]{:S(2)}) collective-permute-start(f32[200,128]{1,0:T(8,128)S(1)} %add_parts.1.a_ref), channel_id=1, source_target_pairs={{0,4},{2,6},{4,0},{6,2},{1,5},{3,7},{5,1},{7,3},{8,12},{10,14},{12... | collective-permute-start | bytes 307208 | tf_op jit(solution)/shard_map/ppermute | solution.py:60
  57.1 3.5 %collective-permute-start.14 = (f32[200,128]{1,0:T(8,128)S(1)}, f32[200,128]{1,0:T(8,128)S(1)}, u32[]{:S(2)}, u32[]{:S(2)}) collective-permute-start(f32[200,128]{1,0:T(8,128)S(1)} %add_parts.1.a_ref), channel_id=1, source_target_pairs={{0,6},{2,0},{4,2},{6,4},{1,7},{3,1},{5,3},{7,5},{8,14},{10,8},{12,... | collective-permute-start | bytes 307208 | tf_op jit(solution)/shard_map/ppermute | solution.py:60
  57.9 5.8 %collective-permute-start.13 = (f32[200,128]{1,0:T(8,128)S(1)}, f32[200,128]{1,0:T(8,128)S(1)}, u32[]{:S(2)}, u32[]{:S(2)}) collective-permute-start(f32[200,128]{1,0:T(8,128)S(1)} %add_parts.1.a_ref), channel_id=1, source_target_pairs={{0,2},{2,4},{4,6},{6,0},{1,3},{3,5},{5,7},{7,1},{8,10},{10,12},{12... | collective-permute-start | bytes 307208 | tf_op jit(solution)/shard_map/ppermute | solution.py:60
  63.8 8.0 %collective-permute-start.18 = (f32[160,128]{1,0:T(8,128)S(1)}, f32[160,128]{1,0:T(8,128)S(1)}, u32[]{:S(2)}, u32[]{:S(2)}) collective-permute-start(f32[160,128]{1,0:T(8,128)S(1)} %get-tuple-element.52.a_ref), channel_id=1, source_target_pairs={{0,64},{1,17},{2,66},{3,19},{4,68},{5,21},{6,70},{7,23},{8,72},{9,... | collective-permute-start | bytes 245768 | tf_op jit(solution)/shard_map/ppermute | solution.py:54
  63.9 7.9 %collective-permute-start.17 = (f32[160,128]{1,0:T(8,128)S(1)}, f32[160,128]{1,0:T(8,128)S(1)}, u32[]{:S(2)}, u32[]{:S(2)}) collective-permute-start(f32[160,128]{1,0:T(8,128)S(1)} %get-tuple-element.52.a_ref), channel_id=1, source_target_pairs={{0,96},{1,25},{2,98},{3,27},{4,100},{5,29},{6,102},{7,31},{8,104},... | collective-permute-start | bytes 245768 | tf_op jit(solution)/shard_map/ppermute | solution.py:54
  64.3 7.5 %collective-permute-start.16 = (f32[160,128]{1,0:T(8,128)S(1)}, f32[160,128]{1,0:T(8,128)S(1)}, u32[]{:S(2)}, u32[]{:S(2)}) collective-permute-start(f32[160,128]{1,0:T(8,128)S(1)} %get-tuple-element.52.a_ref), channel_id=1, source_target_pairs={{0,32},{1,9},{2,34},{3,11},{4,36},{5,13},{6,38},{7,15},{8,40},{9,1... | collective-permute-start | bytes 245768 | tf_op jit(solution)/shard_map/ppermute | solution.py:54
  72.4 6.9 %collective-permute-start.21 = (f32[640,128]{1,0:T(8,128)S(1)}, f32[640,128]{1,0:T(8,128)S(1)}, u32[]{:S(2)}, u32[]{:S(2)}) collective-permute-start(f32[640,128]{1,0:T(8,128)S(1)} %assemble.1.refs_0_), channel_id=1, source_target_pairs={{0,1},{1,0},{2,3},{3,2},{4,5},{5,4},{6,7},{7,6},{8,9},{9,8},{10,11... | collective-permute-start | bytes 983048 | tf_op jit(solution)/shard_map/ppermute | solution.py:64
  76.6 7.4 %collective-permute-start.20 = (f32[640,128]{1,0:T(8,128)S(1)}, f32[640,128]{1,0:T(8,128)S(1)}, u32[]{:S(2)}, u32[]{:S(2)}) collective-permute-start(f32[640,128]{1,0:T(8,128)S(1)} %assemble.1.refs_0_), channel_id=1, source_target_pairs={{0,8},{1,33},{2,10},{3,35},{4,12},{5,37},{6,14},{7,39},{8,16},{9,4... | collective-permute-start | bytes 983048 | tf_op jit(solution)/shard_map/ppermute | solution.py:54
  77.7 7.3 %collective-permute-start.23 = (f32[640,128]{1,0:T(8,128)S(1)}, f32[640,128]{1,0:T(8,128)S(1)}, u32[]{:S(2)}, u32[]{:S(2)}) collective-permute-start(f32[640,128]{1,0:T(8,128)S(1)} %assemble.1.refs_0_), channel_id=1, source_target_pairs={{0,24},{1,97},{2,26},{3,99},{4,28},{5,101},{6,30},{7,103},{8,0},{9... | collective-permute-start | bytes 983048 | tf_op jit(solution)/shard_map/ppermute | solution.py:54
  79.3 0.9 copy-start
  84.0 7.5 %collective-permute-start.22 = (f32[640,128]{1,0:T(8,128)S(1)}, f32[640,128]{1,0:T(8,128)S(1)}, u32[]{:S(2)}, u32[]{:S(2)}) collective-permute-start(f32[640,128]{1,0:T(8,128)S(1)} %tie.3.refs_0_), channel_id=1, source_target_pairs={{0,1},{1,0},{2,3},{3,2},{4,5},{5,4},{6,7},{7,6},{8,9},{9,8},{10,11... | collective-permute-start | bytes 983048 | tf_op jit(solution)/shard_map/ppermute | solution.py:64
  85.0 6.5 %collective-permute-start.24 = (f32[640,128]{1,0:T(8,128)S(1)}, f32[640,128]{1,0:T(8,128)S(1)}, u32[]{:S(2)}, u32[]{:S(2)}) collective-permute-start(f32[640,128]{1,0:T(8,128)S(1)} %tie.4.refs_1_), channel_id=1, source_target_pairs={{0,1},{1,0},{2,3},{3,2},{4,5},{5,4},{6,7},{7,6},{8,9},{9,8},{10,11... | collective-permute-start | bytes 983048 | tf_op jit(solution)/shard_map/ppermute | solution.py:64
  85.0 9.2 %collective-permute-start.19 = (f32[640,128]{1,0:T(8,128)S(1)}, f32[640,128]{1,0:T(8,128)S(1)}, u32[]{:S(2)}, u32[]{:S(2)}) collective-permute-start(f32[640,128]{1,0:T(8,128)S(1)} %assemble.1.refs_0_), channel_id=1, source_target_pairs={{0,16},{1,65},{2,18},{3,67},{4,20},{5,69},{6,22},{7,71},{8,24},{9,... | collective-permute-start | bytes 983048 | tf_op jit(solution)/shard_map/ppermute | solution.py:54
  94.2 3.0 %collective-permute-start.25 = (f32[640,128]{1,0:T(8,128)S(1)}, f32[640,128]{1,0:T(8,128)S(1)}, u32[]{:S(2)}, u32[]{:S(2)}) collective-permute-start(f32[640,128]{1,0:T(8,128)S(1)} %tie.5.refs_0_), channel_id=1, source_target_pairs={{0,1},{1,0},{2,3},{3,2},{4,5},{5,4},{6,7},{7,6},{8,9},{9,8},{10,11... | collective-permute-start | bytes 983048 | tf_op jit(solution)/shard_map/ppermute | solution.py:64

commit v6 on v5

--- a/solution.py
+++ b/solution.py
@@ -19,7 +19,6 @@
 SHIFTS = (1, 3, 2)
 ANY = pl.BlockSpec(memory_space=pl.ANY)
 WHOLE = pl.BlockSpec(memory_space=pltpu.VMEM)
-SCALAR = pl.BlockSpec(memory_space=pltpu.SMEM)
 
 
 def params(mib):
@@ -28,6 +27,11 @@
 
 def cost(flops, nbytes):
     return pl.CostEstimate(flops=flops, bytes_accessed=nbytes, transcendentals=0)
+
+
+def place():
+    core, x, z = (lax.axis_index(a) for a in ("c", "x", "z"))
+    return core, jnp.where(core == 0, x, z), jnp.where(core == 0, z, x)
 
 
 def index(z, x, y, c):
@@ -64,11 +68,10 @@
     return lax.ppermute(value, "c", [(0, 1), (1, 0)])
 
 
-def merge_kernel(width, meta_ref, g_hbm, e_hbm, q_hbm, m_ref, p_ref, g_ref, e_ref, q_ref, sems):
+def merge_kernel(width, g_hbm, e_hbm, q_hbm, m_ref, p_ref, g_ref, e_ref, q_ref, sems):
     rows, columns = g_ref.shape
     rank = q_ref.shape[0]
     steps = columns // width
-    del meta_ref
 
     def copies(i):
         at = pl.ds(i * width, width)
@@ -111,7 +114,7 @@
     )
 
 
-def merge(meta, gradient, error, q_start):
+def merge(gradient, error, q_start):
     rows, columns = gradient.shape
     rank = q_start.shape[0]
     width = 1024
@@ -121,7 +124,7 @@
     return pl.pallas_call(
         functools.partial(merge_kernel, width),
         out_shape=[pltpu.VMEM((rows, columns), BF16), pltpu.VMEM((rank * rows // 128, 128), F32)],
-        in_specs=[SCALAR, ANY, ANY, ANY],
+        in_specs=[ANY, ANY, ANY],
         out_specs=[WHOLE, WHOLE],
         scratch_shapes=[
             pltpu.VMEM((rows, columns), BF16),
@@ -132,7 +135,7 @@
         compiler_params=params(24),
         cost_estimate=cost(2 * rank * rows * columns, 4 * rows * columns),
         name="merge",
-    )(meta, gradient, error, q_start)
+    )(gradient, error, q_start)
 
 
 def right_tiles(half, pieces, m_ref, out_ref):
@@ -162,7 +165,7 @@
     return high, middle, (n - middle.astype(F32)).astype(BF16)
 
 
-def first_right_kernel(replicas, rank, meta_ref, a_ref, b_ref, c_ref, d_ref, m_ref, out_ref, ext_ref, p_ref, pieces_ref):
+def first_right_kernel(replicas, rank, a_ref, b_ref, c_ref, d_ref, m_ref, out_ref, ext_ref, p_ref, pieces_ref):
     p = (a_ref[...] + b_ref[...] + (c_ref[...] + d_ref[...])) * (1.0 / replicas)
     peak = jnp.max(jnp.abs(p), axis=(0, 1), keepdims=True)
     peak = jnp.where(peak > 0, peak, 1.0)
@@ -184,14 +187,14 @@
     out_ref[out_ref.shape[0] - ext.shape[0] :, :] = ext
     pieces = jnp.concatenate(split(p / peak), axis=0)
     pieces_ref[...] = pieces
-    right_tiles(1 - meta_ref[0], pieces, m_ref, out_ref)
-
-
-def second_right_kernel(meta_ref, pieces_ref, m_ref, out_ref):
-    right_tiles(meta_ref[0], pieces_ref[...], m_ref, out_ref)
-
-
-def first_right(meta, parts, merged, rank, replicas):
+    right_tiles(1 - place()[0], pieces, m_ref, out_ref)
+
+
+def second_right_kernel(pieces_ref, m_ref, out_ref):
+    right_tiles(place()[0], pieces_ref[...], m_ref, out_ref)
+
+
+def first_right(parts, merged, rank, replicas):
     rows, columns = merged.shape
     size = rank * columns // 256
     extra = rank * rank // 128 + ROWS
@@ -203,28 +206,28 @@
             pltpu.VMEM((rank, rows), F32),
             pltpu.VMEM((3 * rank, rows), BF16),
         ],
-        in_specs=[SCALAR] + [WHOLE] * 5,
+        in_specs=[WHOLE] * 5,
         out_specs=[WHOLE] * 4,
         compiler_params=params(12),
         cost_estimate=cost(3 * rank * rows * columns, 512 * size),
         name="first_right",
-    )(meta, *parts, merged)
-
-
-def second_right(meta, pieces, merged):
+    )(*parts, merged)
+
+
+def second_right(pieces, merged):
     size = pieces.shape[0] // 3 * merged.shape[1] // 256
     return pl.pallas_call(
         second_right_kernel,
         out_shape=pltpu.VMEM((size, 128), F32),
-        in_specs=[SCALAR, WHOLE, WHOLE],
+        in_specs=[WHOLE, WHOLE],
         out_specs=WHOLE,
         compiler_params=params(12),
         cost_estimate=cost(pieces.shape[0] * merged.size, 512 * size),
         name="second_right",
-    )(meta, pieces, merged)
-
-
-def pair_kernel(meta_ref, kept_ref, got_ref, ext_ref, *out):
+    )(pieces, merged)
+
+
+def pair_kernel(kept_ref, got_ref, ext_ref, *out):
     pair_ref = out[-1]
     grams = ext_ref.shape[0] - ROWS
     ext = kept_ref.shape[0]
@@ -235,40 +238,40 @@
     pair_ref[grams:] = jnp.broadcast_to(top, (ROWS, 128))
     own, its = own / top, its / top
     for k, ref in zip((0,) + SHIFTS, out):
-        at = pl.ds(pl.multiple_of((meta_ref[1] + k) % QUARTERS * size, size), size)
+        at = pl.ds(pl.multiple_of((place()[1] + k) % QUARTERS * size, size), size)
         ref[...] = kept_ref[at] * own + got_ref[at] * its
 
 
-def pair(meta, kept, got, ext):
+def pair(kept, got, ext):
     size = kept.shape[0] // QUARTERS
     return pl.pallas_call(
         pair_kernel,
         out_shape=[jax.ShapeDtypeStruct((size, 128), F32)] * QUARTERS
         + [pltpu.VMEM(ext.shape, F32)],
-        in_specs=[SCALAR] + [WHOLE] * 3,
+        in_specs=[WHOLE] * 3,
         out_specs=[WHOLE] * (QUARTERS + 1),
         compiler_params=params(8),
         name="pair",
-    )(meta, kept, got, ext)
-
-
-def add_quarters_kernel(meta_ref, a_ref, b_ref, c_ref, d_ref, *out):
+    )(kept, got, ext)
+
+
+def add_quarters_kernel(a_ref, b_ref, c_ref, d_ref, *out):
     size = a_ref.shape[0] // QUARTERS
     for k, ref in zip((0,) + SHIFTS, out):
-        at = pl.ds(pl.multiple_of((meta_ref[2] + k) % QUARTERS * size, size), size)
+        at = pl.ds(pl.multiple_of((place()[2] + k) % QUARTERS * size, size), size)
         ref[...] = (a_ref[at] + b_ref[at]) + (c_ref[at] + d_ref[at])
 
 
-def add_quarters(meta, parts):
+def add_quarters(parts):
     size = parts[0].shape[0] // QUARTERS
     return pl.pallas_call(
         add_quarters_kernel,
         out_shape=[jax.ShapeDtypeStruct((size, 128), F32)] * QUARTERS,
-        in_specs=[SCALAR] + [WHOLE] * QUARTERS,
+        in_specs=[WHOLE] * QUARTERS,
         out_specs=[WHOLE] * QUARTERS,
         compiler_params=params(8),
         name="add_quarters",
-    )(meta, *parts)
+    )(*parts)
 
 
 def add_parts_kernel(a_ref, b_ref, c_ref, d_ref, ext_ref, out_ref):
@@ -315,23 +318,23 @@
     )(*parts)
 
 
-def assemble_kernel(meta_ref, a_ref, b_ref, c_ref, d_ref, after_ref, out_ref):
+def assemble_kernel(a_ref, b_ref, c_ref, d_ref, after_ref, out_ref):
     del after_ref
     size = a_ref.shape[0]
     for k, ref in zip((0,) + SHIFTS, (a_ref, b_ref, c_ref, d_ref)):
-        at = pl.multiple_of((meta_ref[2] + QUARTERS - k) % QUARTERS * size, size)
+        at = pl.multiple_of((place()[2] + QUARTERS - k) % QUARTERS * size, size)
         out_ref[pl.ds(at, size)] = ref[...]
 
 
-def assemble(meta, parts, after):
+def assemble(parts, after):
     return pl.pallas_call(
         assemble_kernel,
         out_shape=jax.ShapeDtypeStruct((parts[0].shape[0] * QUARTERS, 128), F32),
-        in_specs=[SCALAR] + [WHOLE] * 4 + [ANY],
+        in_specs=[WHOLE] * 4 + [ANY],
         out_specs=WHOLE,
         compiler_params=params(8),
         name="assemble",
-    )(meta, *parts, after)
+    )(*parts, after)
 
 
 def factor_kernel(replicas, ext_ref, p_ref, solve_ref, hat_ref):
@@ -344,15 +347,29 @@
         tile = ext_ref[g // 2 * ROWS : (g // 2 + 1) * ROWS, (g % 2) * rank : (g % 2 + 1) * rank]
         unit = jnp.where(lane[:, :rank] == sub[:, :rank] + g * ROWS, 1.0, 0.0)
         blocks.append(jnp.concatenate([tile, unit], axis=1))
-    for j in range(rank):
-        own, at = j // ROWS, j % ROWS
-        row = blocks[own][at : at + 1]
-        row = row / row[:, j : j + 1]
-        for g in range(own, groups):
-            column = blocks[g][:, j : j + 1]
-            if g == own:
-                column = jnp.where(sub[:, :1] > at, column, 0.0)
-            blocks[g] = blocks[g] - column * row
+    for own in range(groups):
+        spread = lambda g: [
+            jnp.broadcast_to(blocks[g][:, own * ROWS + k : own * ROWS + k + 1], (ROWS, 2 * rank))
+            for k in range(ROWS)
+        ]
+        columns = spread(own)
+        rows, heads = [], []
+        for k in range(ROWS):
+            scale = 1.0 / columns[k][k : k + 1]
+            row = blocks[own][k : k + 1] * scale
+            head = {m: columns[m][k : k + 1] * scale for m in range(k + 1, ROWS)}
+            factors = jnp.where(sub > k, columns[k], 0.0)
+            blocks[own] = blocks[own] - factors * row
+            for m, h in head.items():
+                columns[m] = columns[m] - factors * h
+            rows.append(row)
+            heads.append(head)
+        for g in range(own + 1, groups):
+            columns = spread(g)
+            for k in range(ROWS):
+                blocks[g] = blocks[g] - columns[k] * rows[k]
+                for m, h in heads[k].items():
+                    columns[m] = columns[m] - columns[k] * h
     inverse = []
     for g in range(groups):
         diagonal = jnp.sum(
@@ -381,7 +398,11 @@
     )(ext, p_mean)
 
 
-def result_kernel(sources, width, meta_ref, solve_ref, p_ref, m_ref, *refs):
+def result_kernel(sources, last, width, solve_ref, p_ref, m_ref, *refs):
+    if last:
+        hat_hbm, refs = refs[-4], refs[:-4] + refs[-3:]
+        hat = pltpu.make_async_copy(p_ref, hat_hbm, refs[-1].at[0, len(sources)])
+        hat.start()
     error_hbm, q_hbm, token_ref, error_ref, q_ref, sems = refs[-6:]
     token_ref[...] = jnp.zeros_like(token_ref)
     rank = solve_ref.shape[0]
@@ -400,8 +421,9 @@
     bases = []
     for n, (own, k) in enumerate(sources):
         t_ref = refs[n]
-        core = meta_ref[0] if own else 1 - meta_ref[0]
-        quarter = (meta_ref[1 if own else 2] + QUARTERS - k) % QUARTERS
+        core, one, two = place()
+        core, turn = (core, one) if own else (1 - core, two)
+        quarter = (turn + QUARTERS - k) % QUARTERS
         base = (core * QUARTERS + quarter) * columns
         bases.append(base)
         for at in range(0, columns, width):
@@ -430,33 +452,36 @@
     for n, base in enumerate(bases):
         for c in copies(n, base, 0, columns):
             c.wait()
-
-
-def result(meta, sources, totals, merged, solve, p_hat, before):
+    if last:
+        hat.wait()
+
+
+def result(sources, last, totals, merged, solve, p_hat, before):
     rank = solve.shape[0]
     rows, columns = merged.shape
     quarter = columns // 2 // QUARTERS
     n = len(sources)
     held = [] if before is None else list(before)
     return pl.pallas_call(
-        functools.partial(result_kernel, sources, quarter // 2),
+        functools.partial(result_kernel, sources, last, quarter // 2),
         out_shape=[
             pltpu.HBM((rows, columns), BF16),
             pltpu.HBM((rank, columns), F32),
             pltpu.VMEM((ROWS, 128), F32),
-        ],
-        in_specs=[SCALAR] + [WHOLE] * (3 + n) + [ANY] * len(held),
-        out_specs=[ANY, ANY, WHOLE],
+        ]
+        + [pltpu.HBM(p_hat.shape, F32)] * last,
+        in_specs=[WHOLE] * (3 + n) + [ANY] * len(held),
+        out_specs=[ANY, ANY, WHOLE] + [ANY] * last,
         scratch_shapes=[
             pltpu.VMEM((n, rows, quarter), BF16),
             pltpu.VMEM((n, rank, quarter), F32),
-            pltpu.SemaphoreType.DMA((2, n)),
+            pltpu.SemaphoreType.DMA((2, n + 1)),
         ],
-        input_output_aliases={4 + n + i: i for i in range(len(held))},
+        input_output_aliases={3 + n + i: i for i in range(len(held))},
         compiler_params=params(12),
-        cost_estimate=cost(2 * n * rank * rows * quarter, 4 * n * rows * quarter),
+        cost_estimate=cost(1<<33, 1<<20),
         name="result",
-    )(meta, solve, p_hat, merged, *totals, *held)
+    )(solve, p_hat, merged, *totals, *held)
 
 
 def tie_kernel(value_ref, after_ref, out_ref):
@@ -478,27 +503,24 @@
 def body(gradient, error, q_start):
     rank = q_start.shape[0]
     replicas = SIZES[0] * SIZES[1]
-    core, x, z = (lax.axis_index(a) for a in ("c", "x", "z"))
-    meta = jnp.stack([core, jnp.where(core == 0, x, z), jnp.where(core == 0, z, x)])
-
-    merged, p = merge(meta, gradient[0], error[0], q_start)
+    merged, p = merge(gradient[0], error[0], q_start)
     a, b, c = ring_x_or_z([p] * 3, 0)
     p = (p + a) + (b + c)
     sent, ext, p_mean, pieces = first_right(
-        meta, (p, *ring_x_or_z([p] * 3, 1)), merged, rank, replicas
+        (p, *ring_x_or_z([p] * 3, 1)), merged, rank, replicas
     )
     got = swap(sent)
-    kept = second_right(meta, pieces, merged)
-    own, *sent, ext = pair(meta, kept, got, ext)
-    own, *sent = add_quarters(meta, (own, *ring_x_or_z(sent, 0)))
+    kept = second_right(pieces, merged)
+    own, *sent, ext = pair(kept, got, ext)
+    own, *sent = add_quarters((own, *ring_x_or_z(sent, 0)))
     part = add_parts((own, *ring_x_or_z(sent, 1)), ext)
     total, ext = across((part, *ring_y(part)), ext.shape[0])
     solve, p_hat = factor(ext, p_mean, replicas)
-    total = assemble(meta, (total, *ring_x_or_z([total] * 3, 1)), solve)
+    total = assemble((total, *ring_x_or_z([total] * 3, 1)), solve)
     one, three, two = ring_x_or_z([total] * 3, 0)
 
-    def write(sources, totals, before):
-        return result(meta, sources, totals, merged, solve, p_hat, before)
+    def write(sources, totals, before, last=False):
+        return result(sources, last, totals, merged, solve, p_hat, before)
 
     *out, token = write(((True, 0), (False, 0)), (total, swap(total)), None)
     one, three = tie(one, token), tie(three, token)
@@ -506,7 +528,7 @@
     *out, token = write(((False, 1), (False, 3)), (swap(one), swap(three)), out)
     two = tie(two, token)
     *out, _ = write(((True, 2),), (two,), out)
-    new_error, q_new, _ = write(((False, 2),), (swap(two),), out)
+    new_error, q_new, _, p_hat = write(((False, 2),), (swap(two),), out, True)
     return (new_error[None], p_hat, q_new)
 
 

time: 100 us -> 98 us (0.980)
  Pallas kernels: 33.3 us -> 23.1 us
  waiting for transfers between devices: 27.5 us -> 36.6 us
    ppermute x18, waiting for transfers between devices: 21.6 us -> 30.2 us  [ring_x_or_z(): out.append(lax.ppermute(value, AXES, pairs))]
    pallas_call x1, Pallas kernels: 6.37 us -> 1.93 us  [factor(): pl.pallas_call(functools.partial(factor_kernel, replicas), out_shape=[jax...]
    ppermute x18, starting transfers between devices: 23.2 us -> 19.6 us  [ring_x_or_z(): out.append(lax.ppermute(value, AXES, pairs))]
    ppermute x5, starting transfers between devices: 9.7 us -> 13.1 us  [swap(): return lax.ppermute(value, 'c', [(0, 1), (1, 0)])]
    pallas_call x5, Pallas kernels: 14 us -> 11.5 us  [result(): pl.pallas_call(functools.partial(result_kernel, sources, last, quarter //...]
  transfers between devices with their start and end apart: 26 -> 26, of which waited for: 15 -> 17; matrix products, arithmetic and copies ran while one was open for 0% -> 0% of each run, Pallas kernels for 20% -> 13%
where the time goes in v6:
time: 98 us; the launch traced here: 97.9 us
  starting transfers between devices  37.1 us (38%)
  waiting for transfers between devices  36.6 us (37%)
  Pallas kernels  23.1 us (24%)
    ppermute x18, waiting for transfers between devices, ring_x_or_z(): out.append(lax.ppermute(value, AXES, pairs))  30.2 us
    ppermute x18, starting transfers between devices, ring_x_or_z(): out.append(lax.ppermute(value, AXES, pairs))  19.6 us
    ppermute x5, starting transfers between devices, swap(): return lax.ppermute(value, 'c', [(0, 1), (1, 0)])  13.1 us
    pallas_call x5, Pallas kernels, result(): pl.pallas_call(functools.partial(result_kernel, sources, last, quarter //...  11.5 us
    pallas_call x1, Pallas kernels, merge(): pl.pallas_call(functools.partial(merge_kernel, width), out_shape=[pltpu.V...  6.14 us
    ppermute x3, waiting for transfers between devices, ring_y(): lax.ppermute(value, 'y', [(i, (i + k) % n) for i in range(n)])  5.11 us
    ppermute x3, starting transfers between devices, ring_y(): lax.ppermute(value, 'y', [(i, (i + k) % n) for i in range(n)])  4.47 us
  transfers between devices with their start and end apart: 26, of which 17 were waited for; matrix products, arithmetic and copies ran while one was open for 0% of the time, Pallas kernels for 13%

profile of v6, /device:TPU:1, one launch (start us, length us, event | category | flops | bytes accessed | tf_op | source)
XLA Modules:
  0.0 97.9 jit_solution(3571466654608039041)
XLA Ops:
  0.6 6.1 %merge.1 = (bf16[320,10240]{1,0:T(8,128)(2,1)S(1)}, f32[160,128]{1,0:T(8,128)S(1)}) custom-call(bf16[320,10240]{1,0:T(8,128)(2,1)} %bitcast.3, bf16[320,10240]{1,0:T(8,128)(2,1)} %bitcast.4, bf16[64,10240]{1,0:T(8,128)(2,1)} %q_hbm.1), custom_call_target="tpu_custom_call" | custom-call | flops 419430400 | bytes 13107200 | tf_op jit(solution)/shard_map/merge/pallas_call | solution.py:124
  6.8 4.5 %collective-permute-start.2 = (f32[160,128]{1,0:T(8,128)S(1)}, f32[160,128]{1,0:T(8,128)S(1)}, u32[]{:S(2)}, u32[]{:S(2)}) collective-permute-start(f32[160,128]{1,0:T(8,128)S(1)} %get-tuple-element.35), channel_id=1, source_target_pairs={{0,16},{1,65},{2,18},{3,67},{4,20},{5,69},{6,22},{7,71},{8,24},{9,... | collective-permute-start | bytes 245768 | tf_op jit(solution)/shard_map/ppermute | solution.py:58
  11.3 0.4 collective-permute-start.1
  11.7 1.0 %collective-permute-start = (f32[160,128]{1,0:T(8,128)S(1)}, f32[160,128]{1,0:T(8,128)S(1)}, u32[]{:S(2)}, u32[]{:S(2)}) collective-permute-start(f32[160,128]{1,0:T(8,128)S(1)} %get-tuple-element.35), channel_id=1, source_target_pairs={{0,8},{1,33},{2,10},{3,35},{4,12},{5,37},{6,14},{7,39},{8,16},{9,4... | collective-permute-start | bytes 245768 | tf_op jit(solution)/shard_map/ppermute | solution.py:58
  12.7 0.7 collective-permute-done.2
  13.4 1.6 %collective-permute-done.1 = f32[160,128]{1,0:T(8,128)S(1)} collective-permute-done((f32[160,128]{1,0:T(8,128)S(1)}, f32[160,128]{1,0:T(8,128)S(1)}, u32[]{:S(2)}, u32[]{:S(2)}) %collective-permute-start.1) | collective-permute-done | bytes 81952 | tf_op jit(solution)/shard_map/ppermute | solution.py:58
  15.0 1.2 %collective-permute-done = f32[160,128]{1,0:T(8,128)S(1)} collective-permute-done((f32[160,128]{1,0:T(8,128)S(1)}, f32[160,128]{1,0:T(8,128)S(1)}, u32[]{:S(2)}, u32[]{:S(2)}) %collective-permute-start) | collective-permute-done | bytes 81952 | tf_op jit(solution)/shard_map/ppermute | solution.py:58
  16.2 2.8 %collective-permute-start.5 = (f32[160,128]{1,0:T(8,128)S(1)}, f32[160,128]{1,0:T(8,128)S(1)}, u32[]{:S(2)}, u32[]{:S(2)}) collective-permute-start(f32[160,128]{1,0:T(8,128)S(1)} %add_add_fusion.a_ref), channel_id=1, source_target_pairs={{0,64},{1,17},{2,66},{3,19},{4,68},{5,21},{6,70},{7,23},{8,72},{9,... | collective-permute-start | bytes 245768 | tf_op jit(solution)/shard_map/ppermute | solution.py:58
  19.1 0.9 collective-permute-start.4
  19.9 0.6 collective-permute-start.3
  20.5 0.6 collective-permute-done.5.d_ref
  21.1 1.2 %collective-permute-done.4.c_ref = f32[160,128]{1,0:T(8,128)S(1)} collective-permute-done((f32[160,128]{1,0:T(8,128)S(1)}, f32[160,128]{1,0:T(8,128)S(1)}, u32[]{:S(2)}, u32[]{:S(2)}) %collective-permute-start.4) | collective-permute-done | bytes 81952 | tf_op jit(solution)/shard_map/ppermute | solution.py:58
  22.4 2.1 %collective-permute-done.3.b_ref = f32[160,128]{1,0:T(8,128)S(1)} collective-permute-done((f32[160,128]{1,0:T(8,128)S(1)}, f32[160,128]{1,0:T(8,128)S(1)}, u32[]{:S(2)}, u32[]{:S(2)}) %collective-permute-start.3) | collective-permute-done | bytes 81952 | tf_op jit(solution)/shard_map/ppermute | solution.py:58
  24.4 1.7 %first_right.1 = (f32[2600,128]{1,0:T(8,128)S(1)}, f32[40,128]{1,0:T(8,128)S(1)}, f32[64,320]{1,0:T(8,128)S(1)}, bf16[192,320]{1,0:T(8,128)(2,1)S(1)}) custom-call(f32[160,128]{1,0:T(8,128)S(1)} %add_add_fusion.a_ref, f32[160,128]{1,0:T(8,128)S(1)} %collective-permute-done.3.b_ref, f32[160,128]{1,0:T(8,128)S(1)} %collective-permute-done.4.c_ref, ...), custom_call_target="tpu_custom_call" | custom-call | flops 629145600 | bytes 1310720 | tf_op jit(solution)/shard_map/first_right/pallas_call | solution.py:201
  26.1 4.2 %collective-permute-start.6 = (f32[2600,128]{1,0:T(8,128)S(1)}, f32[2600,128]{1,0:T(8,128)S(1)}, u32[]{:S(2)}, u32[]{:S(2)}) collective-permute-start(f32[2600,128]{1,0:T(8,128)S(1)} %get-tuple-element.38), channel_id=1, source_target_pairs={{0,1},{1,0},{2,3},{3,2},{4,5},{5,4},{6,7},{7,6},{8,9},{9,8},{10,11... | collective-permute-start | bytes 3993608 | tf_op jit(solution)/shard_map/ppermute | solution.py:68
  30.3 1.4 %second_right.1.kept_ref = f32[2560,128]{1,0:T(8,128)S(1)} custom-call(bf16[192,320]{1,0:T(8,128)(2,1)S(1)} %get-tuple-element.37.pieces_ref, bf16[320,10240]{1,0:T(8,128)(2,1)S(1)} %get-tuple-element.36.m_ref), custom_call_target="tpu_custom_call" | custom-call | flops 629145600 | bytes 1310720 | tf_op jit(solution)/shard_map/second_right/pallas_call | solution.py:219
  31.7 1.3 %collective-permute-done.6.got_ref = f32[2600,128]{1,0:T(8,128)S(1)} collective-permute-done((f32[2600,128]{1,0:T(8,128)S(1)}, f32[2600,128]{1,0:T(8,128)S(1)}, u32[]{:S(2)}, u32[]{:S(2)}) %collective-permute-start.6) | collective-permute-done | bytes 1331232 | tf_op jit(solution)/shard_map/ppermute | solution.py:68
  33.0 0.3 pair.1
  33.3 0.1 collective-permute-start.7
  33.4 2.7 %collective-permute-start.8 = (f32[640,128]{1,0:T(8,128)S(1)}, f32[640,128]{1,0:T(8,128)S(1)}, u32[]{:S(2)}, u32[]{:S(2)}) collective-permute-start(f32[640,128]{1,0:T(8,128)S(1)} %get-tuple-element.42), channel_id=1, source_target_pairs={{0,24},{1,97},{2,26},{3,99},{4,28},{5,101},{6,30},{7,103},{8,0},{9... | collective-permute-start | bytes 983048 | tf_op jit(solution)/shard_map/ppermute | solution.py:58
  36.0 0.0 collective-permute-start.9
  36.0 8.3 %collective-permute-done.7.b_ref = f32[640,128]{1,0:T(8,128)S(1)} collective-permute-done((f32[640,128]{1,0:T(8,128)S(1)}, f32[640,128]{1,0:T(8,128)S(1)}, u32[]{:S(2)}, u32[]{:S(2)}) %collective-permute-start.7) | collective-permute-done | bytes 327712 | tf_op jit(solution)/shard_map/ppermute | solution.py:58
  44.3 0.0 collective-permute-done.8.c_ref
  44.3 0.0 collective-permute-done.9.d_ref
  44.3 0.1 add_quarters.1
  44.4 0.1 collective-permute-start.10
  44.5 2.7 %collective-permute-start.11 = (f32[160,128]{1,0:T(8,128)S(1)}, f32[160,128]{1,0:T(8,128)S(1)}, u32[]{:S(2)}, u32[]{:S(2)}) collective-permute-start(f32[160,128]{1,0:T(8,128)S(1)} %get-tuple-element.46), channel_id=1, source_target_pairs={{0,96},{1,25},{2,98},{3,27},{4,100},{5,29},{6,102},{7,31},{8,104},... | collective-permute-start | bytes 245768 | tf_op jit(solution)/shard_map/ppermute | solution.py:58
  47.1 0.0 collective-permute-start.12
  47.1 1.8 %collective-permute-done.10.b_ref = f32[160,128]{1,0:T(8,128)S(1)} collective-permute-done((f32[160,128]{1,0:T(8,128)S(1)}, f32[160,128]{1,0:T(8,128)S(1)}, u32[]{:S(2)}, u32[]{:S(2)}) %collective-permute-start.10) | collective-permute-done | bytes 81952 | tf_op jit(solution)/shard_map/ppermute | solution.py:58
  49.0 0.4 collective-permute-done.11.c_ref
  49.4 2.5 %collective-permute-done.12.d_ref = f32[160,128]{1,0:T(8,128)S(1)} collective-permute-done((f32[160,128]{1,0:T(8,128)S(1)}, f32[160,128]{1,0:T(8,128)S(1)}, u32[]{:S(2)}, u32[]{:S(2)}) %collective-permute-start.12) | collective-permute-done | bytes 81952 | tf_op jit(solution)/shard_map/ppermute | solution.py:58
  51.9 3.0 %collective-permute-start.15 = (f32[200,128]{1,0:T(8,128)S(1)}, f32[200,128]{1,0:T(8,128)S(1)}, u32[]{:S(2)}, u32[]{:S(2)}) collective-permute-start(f32[200,128]{1,0:T(8,128)S(1)} %add_parts.1.a_ref), channel_id=1, source_target_pairs={{0,4},{2,6},{4,0},{6,2},{1,5},{3,7},{5,1},{7,3},{8,12},{10,14},{12... | collective-permute-start | bytes 307208 | tf_op jit(solution)/shard_map/ppermute | solution.py:64
  55.0 0.8 collective-permute-start.14
  55.7 0.7 collective-permute-start.13
  56.4 0.6 collective-permute-done.15.d_ref
  57.0 1.5 %collective-permute-done.14.c_ref = f32[200,128]{1,0:T(8,128)S(1)} collective-permute-done((f32[200,128]{1,0:T(8,128)S(1)}, f32[200,128]{1,0:T(8,128)S(1)}, u32[]{:S(2)}, u32[]{:S(2)}) %collective-permute-start.14) | collective-permute-done | bytes 102432 | tf_op jit(solution)/shard_map/ppermute | solution.py:64
  58.5 3.0 %collective-permute-done.13.b_ref = f32[200,128]{1,0:T(8,128)S(1)} collective-permute-done((f32[200,128]{1,0:T(8,128)S(1)}, f32[200,128]{1,0:T(8,128)S(1)}, u32[]{:S(2)}, u32[]{:S(2)}) %collective-permute-start.13) | collective-permute-done | bytes 102432 | tf_op jit(solution)/shard_map/ppermute | solution.py:64
  61.5 0.1 across.1
  61.6 0.1 collective-permute-start.18
  61.7 0.4 collective-permute-start.17
  62.2 1.1 %collective-permute-start.16 = (f32[160,128]{1,0:T(8,128)S(1)}, f32[160,128]{1,0:T(8,128)S(1)}, u32[]{:S(2)}, u32[]{:S(2)}) collective-permute-start(f32[160,128]{1,0:T(8,128)S(1)} %get-tuple-element.53.a_ref), channel_id=1, source_target_pairs={{0,32},{1,9},{2,34},{3,11},{4,36},{5,13},{6,38},{7,15},{8,40},{9,1... | collective-permute-start | bytes 245768 | tf_op jit(solution)/shard_map/ppermute | solution.py:58
  63.2 1.9 %factor.1 = (f32[64,64]{1,0:T(8,128)S(1)}, f32[64,320]{1,0:T(8,128)S(1)}) custom-call(f32[40,128]{1,0:T(8,128)S(1)} %get-tuple-element.49.ext_ref, f32[64,320]{1,0:T(8,128)S(1)} %get-tuple-element.50.p_ref), custom_call_target="tpu_custom_call" | custom-call | flops 4294967296 | bytes 1048576 | tf_op jit(solution)/shard_map/factor/pallas_call | solution.py:387
  65.2 1.4 %collective-permute-done.18.d_ref = f32[160,128]{1,0:T(8,128)S(1)} collective-permute-done((f32[160,128]{1,0:T(8,128)S(1)}, f32[160,128]{1,0:T(8,128)S(1)}, u32[]{:S(2)}, u32[]{:S(2)}) %collective-permute-start.18) | collective-permute-done | bytes 81952 | tf_op jit(solution)/shard_map/ppermute | solution.py:58
  66.6 0.0 collective-permute-done.17.c_ref
  66.6 0.8 collective-permute-done.16.b_ref
  67.4 5.2 %collective-permute-start.21 = (f32[640,128]{1,0:T(8,128)S(1)}, f32[640,128]{1,0:T(8,128)S(1)}, u32[]{:S(2)}, u32[]{:S(2)}) collective-permute-start(f32[640,128]{1,0:T(8,128)S(1)} %assemble.1.refs_0_), channel_id=1, source_target_pairs={{0,1},{1,0},{2,3},{3,2},{4,5},{5,4},{6,7},{7,6},{8,9},{9,8},{10,11... | collective-permute-start | bytes 983048 | tf_op jit(solution)/shard_map/ppermute | solution.py:68
  72.6 1.0 %collective-permute-start.23 = (f32[640,128]{1,0:T(8,128)S(1)}, f32[640,128]{1,0:T(8,128)S(1)}, u32[]{:S(2)}, u32[]{:S(2)}) collective-permute-start(f32[640,128]{1,0:T(8,128)S(1)} %assemble.1.refs_0_), channel_id=1, source_target_pairs={{0,24},{1,97},{2,26},{3,99},{4,28},{5,101},{6,30},{7,103},{8,0},{9... | collective-permute-start | bytes 983048 | tf_op jit(solution)/shard_map/ppermute | solution.py:58
  73.6 0.4 collective-permute-start.20
  74.1 0.7 collective-permute-start.19
  74.8 0.0 collective-permute-done.21.refs_1_
  74.8 2.2 %result.5 = (bf16[320,10240]{1,0:T(8,128)(2,1)}, f32[64,10240]{1,0:T(8,128)}, f32[8,128]{1,0:T(8,128)S(1)}) custom-call(f32[64,64]{1,0:T(8,128)S(1)} %get-tuple-element.51.after_ref.solve_ref, f32[64,320]{1,0:T(8,128)S(1)} %get-tuple-element.52.p_ref, bf16[320,10240]{1,0:T(8,128)(2,1)S(1)} %get-tuple-element.36.m_ref, f32[640,128]{1,0:T(8,128)S(1)} %assemble.1.refs_0_, ...), custom_call_target="tpu_custom_call" | custom-call | flops 8589934592 | bytes 1048576 | tf_op jit(solution)/shard_map/result/pallas_call | solution.py:465
  77.0 7.6 %collective-permute-done.20.value_ref = f32[640,128]{1,0:T(8,128)S(1)} collective-permute-done((f32[640,128]{1,0:T(8,128)S(1)}, f32[640,128]{1,0:T(8,128)S(1)}, u32[]{:S(2)}, u32[]{:S(2)}) %collective-permute-start.20) | collective-permute-done | bytes 327712 | tf_op jit(solution)/shard_map/ppermute | solution.py:58
  84.6 3.1 %collective-permute-start.22 = (f32[640,128]{1,0:T(8,128)S(1)}, f32[640,128]{1,0:T(8,128)S(1)}, u32[]{:S(2)}, u32[]{:S(2)}) collective-permute-start(f32[640,128]{1,0:T(8,128)S(1)} %tie.3.refs_0_), channel_id=1, source_target_pairs={{0,1},{1,0},{2,3},{3,2},{4,5},{5,4},{6,7},{7,6},{8,9},{9,8},{10,11... | collective-permute-start | bytes 983048 | tf_op jit(solution)/shard_map/ppermute | solution.py:68
  87.7 0.0 collective-permute-done.23.value_ref
  87.7 0.1 collective-permute-start.24
  87.8 2.8 %result.6 = (bf16[320,10240]{1,0:T(8,128)(2,1)}, f32[64,10240]{1,0:T(8,128)}, f32[8,128]{1,0:T(8,128)}) custom-call(f32[64,64]{1,0:T(8,128)S(1)} %get-tuple-element.51.after_ref.solve_ref, f32[64,320]{1,0:T(8,128)S(1)} %get-tuple-element.52.p_ref, bf16[320,10240]{1,0:T(8,128)(2,1)S(1)} %get-tuple-element.36.m_ref, ...), custom_call_target="tpu_custom_call", output_to_operand_aliasing={{0}: (5, {}), {1}: (6, {})} | custom-call | flops 8589934592 | bytes 1048576 | tf_op jit(solution)/shard_map/result/pallas_call | solution.py:465
  90.6 0.0 collective-permute-done.22.refs_0_
  90.6 0.0 collective-permute-done.24.refs_1_
  90.6 2.2 %result.7 = (bf16[320,10240]{1,0:T(8,128)(2,1)}, f32[64,10240]{1,0:T(8,128)}, f32[8,128]{1,0:T(8,128)S(1)}) custom-call(f32[64,64]{1,0:T(8,128)S(1)} %get-tuple-element.51.after_ref.solve_ref, f32[64,320]{1,0:T(8,128)S(1)} %get-tuple-element.52.p_ref, bf16[320,10240]{1,0:T(8,128)(2,1)S(1)} %get-tuple-element.36.m_ref, ...), custom_call_target="tpu_custom_call", output_to_operand_aliasing={{0}: (5, {}), {1}: (6, {})} | custom-call | flops 8589934592 | bytes 1048576 | tf_op jit(solution)/shard_map/result/pallas_call | solution.py:465
  92.8 0.0 collective-permute-done.19.value_ref
  92.8 0.5 collective-permute-start.25
  93.3 2.2 %result.8 = (bf16[320,10240]{1,0:T(8,128)(2,1)}, f32[64,10240]{1,0:T(8,128)}, f32[8,128]{1,0:T(8,128)}) custom-call(f32[64,64]{1,0:T(8,128)S(1)} %get-tuple-element.51.after_ref.solve_ref, f32[64,320]{1,0:T(8,128)S(1)} %get-tuple-element.52.p_ref, bf16[320,10240]{1,0:T(8,128)(2,1)S(1)} %get-tuple-element.36.m_ref, ...), custom_call_target="tpu_custom_call", output_to_operand_aliasing={{0}: (4, {}), {1}: (5, {})} | custom-call | flops 8589934592 | bytes 1048576 | tf_op jit(solution)/shard_map/result/pallas_call | solution.py:465
  95.5 0.0 collective-permute-done.25.refs_0_
  95.5 2.2 %result.9 = (bf16[320,10240]{1,0:T(8,128)(2,1)}, f32[64,10240]{1,0:T(8,128)}, f32[8,128]{1,0:T(8,128)}, f32[64,320]{1,0:T(8,128)}) custom-call(f32[64,64]{1,0:T(8,128)S(1)} %get-tuple-element.51.after_ref.solve_ref, f32[64,320]{1,0:T(8,128)S(1)} %get-tuple-element.52.p_ref, ...), custom_call_target="tpu_custom_call", output_to_operand_aliasing={{0}: (4, {}), {1}: (5, {})} | custom-call | flops 8589934592 | bytes 1048576 | tf_op jit(solution)/shard_map/result/pallas_call | solution.py:465
  (6 shorter events, 0.1 us)
Async XLA Ops:
  6.8 6.6 %collective-permute-start.2 = (f32[160,128]{1,0:T(8,128)S(1)}, f32[160,128]{1,0:T(8,128)S(1)}, u32[]{:S(2)}, u32[]{:S(2)}) collective-permute-start(f32[160,128]{1,0:T(8,128)S(1)} %get-tuple-element.35), channel_id=1, source_target_pairs={{0,16},{1,65},{2,18},{3,67},{4,20},{5,69},{6,22},{7,71},{8,24},{9,... | collective-permute-start | bytes 245768 | tf_op jit(solution)/shard_map/ppermute | solution.py:58
  11.3 3.7 %collective-permute-start.1 = (f32[160,128]{1,0:T(8,128)S(1)}, f32[160,128]{1,0:T(8,128)S(1)}, u32[]{:S(2)}, u32[]{:S(2)}) collective-permute-start(f32[160,128]{1,0:T(8,128)S(1)} %get-tuple-element.35), channel_id=1, source_target_pairs={{0,24},{1,97},{2,26},{3,99},{4,28},{5,101},{6,30},{7,103},{8,0},{9... | collective-permute-start | bytes 245768 | tf_op jit(solution)/shard_map/ppermute | solution.py:58
  11.7 4.5 %collective-permute-start = (f32[160,128]{1,0:T(8,128)S(1)}, f32[160,128]{1,0:T(8,128)S(1)}, u32[]{:S(2)}, u32[]{:S(2)}) collective-permute-start(f32[160,128]{1,0:T(8,128)S(1)} %get-tuple-element.35), channel_id=1, source_target_pairs={{0,8},{1,33},{2,10},{3,35},{4,12},{5,37},{6,14},{7,39},{8,16},{9,4... | collective-permute-start | bytes 245768 | tf_op jit(solution)/shard_map/ppermute | solution.py:58
  16.2 4.9 %collective-permute-start.5 = (f32[160,128]{1,0:T(8,128)S(1)}, f32[160,128]{1,0:T(8,128)S(1)}, u32[]{:S(2)}, u32[]{:S(2)}) collective-permute-start(f32[160,128]{1,0:T(8,128)S(1)} %add_add_fusion.a_ref), channel_id=1, source_target_pairs={{0,64},{1,17},{2,66},{3,19},{4,68},{5,21},{6,70},{7,23},{8,72},{9,... | collective-permute-start | bytes 245768 | tf_op jit(solution)/shard_map/ppermute | solution.py:58
  19.1 3.3 %collective-permute-start.4 = (f32[160,128]{1,0:T(8,128)S(1)}, f32[160,128]{1,0:T(8,128)S(1)}, u32[]{:S(2)}, u32[]{:S(2)}) collective-permute-start(f32[160,128]{1,0:T(8,128)S(1)} %add_add_fusion.a_ref), channel_id=1, source_target_pairs={{0,96},{1,25},{2,98},{3,27},{4,100},{5,29},{6,102},{7,31},{8,104},... | collective-permute-start | bytes 245768 | tf_op jit(solution)/shard_map/ppermute | solution.py:58
  19.9 4.5 %collective-permute-start.3 = (f32[160,128]{1,0:T(8,128)S(1)}, f32[160,128]{1,0:T(8,128)S(1)}, u32[]{:S(2)}, u32[]{:S(2)}) collective-permute-start(f32[160,128]{1,0:T(8,128)S(1)} %add_add_fusion.a_ref), channel_id=1, source_target_pairs={{0,32},{1,9},{2,34},{3,11},{4,36},{5,13},{6,38},{7,15},{8,40},{9,1... | collective-permute-start | bytes 245768 | tf_op jit(solution)/shard_map/ppermute | solution.py:58
  26.1 6.9 %collective-permute-start.6 = (f32[2600,128]{1,0:T(8,128)S(1)}, f32[2600,128]{1,0:T(8,128)S(1)}, u32[]{:S(2)}, u32[]{:S(2)}) collective-permute-start(f32[2600,128]{1,0:T(8,128)S(1)} %get-tuple-element.38), channel_id=1, source_target_pairs={{0,1},{1,0},{2,3},{3,2},{4,5},{5,4},{6,7},{7,6},{8,9},{9,8},{10,11... | collective-permute-start | bytes 3993608 | tf_op jit(solution)/shard_map/ppermute | solution.py:68
  33.3 11.0 %collective-permute-start.7 = (f32[640,128]{1,0:T(8,128)S(1)}, f32[640,128]{1,0:T(8,128)S(1)}, u32[]{:S(2)}, u32[]{:S(2)}) collective-permute-start(f32[640,128]{1,0:T(8,128)S(1)} %get-tuple-element.41), channel_id=1, source_target_pairs={{0,8},{1,33},{2,10},{3,35},{4,12},{5,37},{6,14},{7,39},{8,16},{9,4... | collective-permute-start | bytes 983048 | tf_op jit(solution)/shard_map/ppermute | solution.py:58
  33.4 10.9 %collective-permute-start.8 = (f32[640,128]{1,0:T(8,128)S(1)}, f32[640,128]{1,0:T(8,128)S(1)}, u32[]{:S(2)}, u32[]{:S(2)}) collective-permute-start(f32[640,128]{1,0:T(8,128)S(1)} %get-tuple-element.42), channel_id=1, source_target_pairs={{0,24},{1,97},{2,26},{3,99},{4,28},{5,101},{6,30},{7,103},{8,0},{9... | collective-permute-start | bytes 983048 | tf_op jit(solution)/shard_map/ppermute | solution.py:58
  36.0 8.3 %collective-permute-start.9 = (f32[640,128]{1,0:T(8,128)S(1)}, f32[640,128]{1,0:T(8,128)S(1)}, u32[]{:S(2)}, u32[]{:S(2)}) collective-permute-start(f32[640,128]{1,0:T(8,128)S(1)} %get-tuple-element.43), channel_id=1, source_target_pairs={{0,16},{1,65},{2,18},{3,67},{4,20},{5,69},{6,22},{7,71},{8,24},{9,... | collective-permute-start | bytes 983048 | tf_op jit(solution)/shard_map/ppermute | solution.py:58
  44.4 4.6 %collective-permute-start.10 = (f32[160,128]{1,0:T(8,128)S(1)}, f32[160,128]{1,0:T(8,128)S(1)}, u32[]{:S(2)}, u32[]{:S(2)}) collective-permute-start(f32[160,128]{1,0:T(8,128)S(1)} %get-tuple-element.45), channel_id=1, source_target_pairs={{0,32},{1,9},{2,34},{3,11},{4,36},{5,13},{6,38},{7,15},{8,40},{9,1... | collective-permute-start | bytes 245768 | tf_op jit(solution)/shard_map/ppermute | solution.py:58
  44.5 4.9 %collective-permute-start.11 = (f32[160,128]{1,0:T(8,128)S(1)}, f32[160,128]{1,0:T(8,128)S(1)}, u32[]{:S(2)}, u32[]{:S(2)}) collective-permute-start(f32[160,128]{1,0:T(8,128)S(1)} %get-tuple-element.46), channel_id=1, source_target_pairs={{0,96},{1,25},{2,98},{3,27},{4,100},{5,29},{6,102},{7,31},{8,104},... | collective-permute-start | bytes 245768 | tf_op jit(solution)/shard_map/ppermute | solution.py:58
  47.1 4.8 %collective-permute-start.12 = (f32[160,128]{1,0:T(8,128)S(1)}, f32[160,128]{1,0:T(8,128)S(1)}, u32[]{:S(2)}, u32[]{:S(2)}) collective-permute-start(f32[160,128]{1,0:T(8,128)S(1)} %get-tuple-element.47), channel_id=1, source_target_pairs={{0,64},{1,17},{2,66},{3,19},{4,68},{5,21},{6,70},{7,23},{8,72},{9,... | collective-permute-start | bytes 245768 | tf_op jit(solution)/shard_map/ppermute | solution.py:58
  51.9 5.1 %collective-permute-start.15 = (f32[200,128]{1,0:T(8,128)S(1)}, f32[200,128]{1,0:T(8,128)S(1)}, u32[]{:S(2)}, u32[]{:S(2)}) collective-permute-start(f32[200,128]{1,0:T(8,128)S(1)} %add_parts.1.a_ref), channel_id=1, source_target_pairs={{0,4},{2,6},{4,0},{6,2},{1,5},{3,7},{5,1},{7,3},{8,12},{10,14},{12... | collective-permute-start | bytes 307208 | tf_op jit(solution)/shard_map/ppermute | solution.py:64
  55.0 3.5 %collective-permute-start.14 = (f32[200,128]{1,0:T(8,128)S(1)}, f32[200,128]{1,0:T(8,128)S(1)}, u32[]{:S(2)}, u32[]{:S(2)}) collective-permute-start(f32[200,128]{1,0:T(8,128)S(1)} %add_parts.1.a_ref), channel_id=1, source_target_pairs={{0,6},{2,0},{4,2},{6,4},{1,7},{3,1},{5,3},{7,5},{8,14},{10,8},{12,... | collective-permute-start | bytes 307208 | tf_op jit(solution)/shard_map/ppermute | solution.py:64
  55.7 5.8 %collective-permute-start.13 = (f32[200,128]{1,0:T(8,128)S(1)}, f32[200,128]{1,0:T(8,128)S(1)}, u32[]{:S(2)}, u32[]{:S(2)}) collective-permute-start(f32[200,128]{1,0:T(8,128)S(1)} %add_parts.1.a_ref), channel_id=1, source_target_pairs={{0,2},{2,4},{4,6},{6,0},{1,3},{3,5},{5,7},{7,1},{8,10},{10,12},{12... | collective-permute-start | bytes 307208 | tf_op jit(solution)/shard_map/ppermute | solution.py:64
  61.6 4.9 %collective-permute-start.18 = (f32[160,128]{1,0:T(8,128)S(1)}, f32[160,128]{1,0:T(8,128)S(1)}, u32[]{:S(2)}, u32[]{:S(2)}) collective-permute-start(f32[160,128]{1,0:T(8,128)S(1)} %get-tuple-element.53.a_ref), channel_id=1, source_target_pairs={{0,64},{1,17},{2,66},{3,19},{4,68},{5,21},{6,70},{7,23},{8,72},{9,... | collective-permute-start | bytes 245768 | tf_op jit(solution)/shard_map/ppermute | solution.py:58
  61.7 4.8 %collective-permute-start.17 = (f32[160,128]{1,0:T(8,128)S(1)}, f32[160,128]{1,0:T(8,128)S(1)}, u32[]{:S(2)}, u32[]{:S(2)}) collective-permute-start(f32[160,128]{1,0:T(8,128)S(1)} %get-tuple-element.53.a_ref), channel_id=1, source_target_pairs={{0,96},{1,25},{2,98},{3,27},{4,100},{5,29},{6,102},{7,31},{8,104},... | collective-permute-start | bytes 245768 | tf_op jit(solution)/shard_map/ppermute | solution.py:58
  62.2 5.2 %collective-permute-start.16 = (f32[160,128]{1,0:T(8,128)S(1)}, f32[160,128]{1,0:T(8,128)S(1)}, u32[]{:S(2)}, u32[]{:S(2)}) collective-permute-start(f32[160,128]{1,0:T(8,128)S(1)} %get-tuple-element.53.a_ref), channel_id=1, source_target_pairs={{0,32},{1,9},{2,34},{3,11},{4,36},{5,13},{6,38},{7,15},{8,40},{9,1... | collective-permute-start | bytes 245768 | tf_op jit(solution)/shard_map/ppermute | solution.py:58
  67.4 7.4 %collective-permute-start.21 = (f32[640,128]{1,0:T(8,128)S(1)}, f32[640,128]{1,0:T(8,128)S(1)}, u32[]{:S(2)}, u32[]{:S(2)}) collective-permute-start(f32[640,128]{1,0:T(8,128)S(1)} %assemble.1.refs_0_), channel_id=1, source_target_pairs={{0,1},{1,0},{2,3},{3,2},{4,5},{5,4},{6,7},{7,6},{8,9},{9,8},{10,11... | collective-permute-start | bytes 983048 | tf_op jit(solution)/shard_map/ppermute | solution.py:68
  72.6 15.1 %collective-permute-start.23 = (f32[640,128]{1,0:T(8,128)S(1)}, f32[640,128]{1,0:T(8,128)S(1)}, u32[]{:S(2)}, u32[]{:S(2)}) collective-permute-start(f32[640,128]{1,0:T(8,128)S(1)} %assemble.1.refs_0_), channel_id=1, source_target_pairs={{0,24},{1,97},{2,26},{3,99},{4,28},{5,101},{6,30},{7,103},{8,0},{9... | collective-permute-start | bytes 983048 | tf_op jit(solution)/shard_map/ppermute | solution.py:58
  73.6 10.9 %collective-permute-start.20 = (f32[640,128]{1,0:T(8,128)S(1)}, f32[640,128]{1,0:T(8,128)S(1)}, u32[]{:S(2)}, u32[]{:S(2)}) collective-permute-start(f32[640,128]{1,0:T(8,128)S(1)} %assemble.1.refs_0_), channel_id=1, source_target_pairs={{0,8},{1,33},{2,10},{3,35},{4,12},{5,37},{6,14},{7,39},{8,16},{9,4... | collective-permute-start | bytes 983048 | tf_op jit(solution)/shard_map/ppermute | solution.py:58
  74.1 18.7 %collective-permute-start.19 = (f32[640,128]{1,0:T(8,128)S(1)}, f32[640,128]{1,0:T(8,128)S(1)}, u32[]{:S(2)}, u32[]{:S(2)}) collective-permute-start(f32[640,128]{1,0:T(8,128)S(1)} %assemble.1.refs_0_), channel_id=1, source_target_pairs={{0,16},{1,65},{2,18},{3,67},{4,20},{5,69},{6,22},{7,71},{8,24},{9,... | collective-permute-start | bytes 983048 | tf_op jit(solution)/shard_map/ppermute | solution.py:58
  84.6 6.0 %collective-permute-start.22 = (f32[640,128]{1,0:T(8,128)S(1)}, f32[640,128]{1,0:T(8,128)S(1)}, u32[]{:S(2)}, u32[]{:S(2)}) collective-permute-start(f32[640,128]{1,0:T(8,128)S(1)} %tie.3.refs_0_), channel_id=1, source_target_pairs={{0,1},{1,0},{2,3},{3,2},{4,5},{5,4},{6,7},{7,6},{8,9},{9,8},{10,11... | collective-permute-start | bytes 983048 | tf_op jit(solution)/shard_map/ppermute | solution.py:68
  87.7 2.9 %collective-permute-start.24 = (f32[640,128]{1,0:T(8,128)S(1)}, f32[640,128]{1,0:T(8,128)S(1)}, u32[]{:S(2)}, u32[]{:S(2)}) collective-permute-start(f32[640,128]{1,0:T(8,128)S(1)} %tie.4.refs_1_), channel_id=1, source_target_pairs={{0,1},{1,0},{2,3},{3,2},{4,5},{5,4},{6,7},{7,6},{8,9},{9,8},{10,11... | collective-permute-start | bytes 983048 | tf_op jit(solution)/shard_map/ppermute | solution.py:68
  92.8 2.7 %collective-permute-start.25 = (f32[640,128]{1,0:T(8,128)S(1)}, f32[640,128]{1,0:T(8,128)S(1)}, u32[]{:S(2)}, u32[]{:S(2)}) collective-permute-start(f32[640,128]{1,0:T(8,128)S(1)} %tie.5.refs_0_), channel_id=1, source_target_pairs={{0,1},{1,0},{2,3},{3,2},{4,5},{5,4},{6,7},{7,6},{8,9},{9,8},{10,11... | collective-permute-start | bytes 983048 | tf_op jit(solution)/shard_map/ppermute | solution.py:68

commit v7 on v6

--- a/solution.py
+++ b/solution.py
@@ -48,9 +48,9 @@
     ]
 
 
-def ring_x_or_z(values, phase):
+def ring_x_or_z(values, phase, shifts=SHIFTS):
     out = []
-    for k, value in zip(SHIFTS, values):
+    for k, value in zip(shifts, values):
         pairs = []
         for z, x, y, c in everyone():
             to = (z, (x + k) % SIZES[1], y, c) if c == phase else ((z + k) % SIZES[0], x, y, c)
@@ -484,6 +484,42 @@
     )(solve, p_hat, merged, *totals, *held)
 
 
+def halves_kernel(a_ref, b_ref, after_ref, low_ref, high_ref):
+    del after_ref
+    half = low_ref.shape[0]
+    low_ref[...] = a_ref[:half]
+    high_ref[...] = b_ref[half:]
+
+
+def halves(a, b, after):
+    return pl.pallas_call(
+        halves_kernel,
+        out_shape=[jax.ShapeDtypeStruct((a.shape[0] // 2, 128), F32)] * 2,
+        in_specs=[WHOLE, WHOLE, ANY],
+        out_specs=[WHOLE, WHOLE],
+        compiler_params=params(4),
+        name="halves",
+    )(a, b, after)
+
+
+def join_kernel(low_ref, high_ref, after_ref, out_ref):
+    del after_ref
+    half = low_ref.shape[0]
+    out_ref[:half] = low_ref[...]
+    out_ref[half:] = high_ref[...]
+
+
+def join(low, high, after):
+    return pl.pallas_call(
+        join_kernel,
+        out_shape=jax.ShapeDtypeStruct((low.shape[0] * 2, 128), F32),
+        in_specs=[WHOLE, WHOLE, ANY],
+        out_specs=WHOLE,
+        compiler_params=params(4),
+        name="join",
+    )(low, high, after)
+
+
 def tie_kernel(value_ref, after_ref, out_ref):
     del value_ref, after_ref, out_ref
 
@@ -517,16 +553,17 @@
     total, ext = across((part, *ring_y(part)), ext.shape[0])
     solve, p_hat = factor(ext, p_mean, replicas)
     total = assemble((total, *ring_x_or_z([total] * 3, 1)), solve)
-    one, three, two = ring_x_or_z([total] * 3, 0)
+    one, three = ring_x_or_z([total] * 2, 0, (1, 3))
 
     def write(sources, totals, before, last=False):
         return result(sources, last, totals, merged, solve, p_hat, before)
 
     *out, token = write(((True, 0), (False, 0)), (total, swap(total)), None)
+    low, high = ring_x_or_z(halves(one, three, token), 0, (1, 3))
     one, three = tie(one, token), tie(three, token)
     *out, _ = write(((True, 1), (True, 3)), (one, three), out)
     *out, token = write(((False, 1), (False, 3)), (swap(one), swap(three)), out)
-    two = tie(two, token)
+    two = join(low, high, token)
     *out, _ = write(((True, 2),), (two,), out)
     new_error, q_new, _, p_hat = write(((False, 2),), (swap(two),), out, True)
     return (new_error[None], p_hat, q_new)

time: 98 us -> 97.8 us (level)
  waiting for transfers between devices: 36.6 us -> 33.9 us
  starting transfers between devices: 37.1 us -> 39.7 us
    ppermute x18 -> x19, waiting for transfers between devices: 30.2 us -> 27.4 us  [ring_x_or_z(): out.append(lax.ppermute(value, AXES, pairs))]
    ppermute x18 -> x19, starting transfers between devices: 19.6 us -> 21.6 us  [ring_x_or_z(): out.append(lax.ppermute(value, AXES, pairs))]
  transfers between devices with their start and end apart: 26 -> 27, of which waited for: 17 -> 18; matrix products, arithmetic and copies ran while one was open for 0% -> 0% of each run, Pallas kernels for 13% -> 13%
where the time goes in v7:
time: 97.8 us; the launch traced here: 97.7 us
  starting transfers between devices  39.7 us (41%)
  waiting for transfers between devices  33.9 us (35%)
  Pallas kernels  23.1 us (24%)
  between operations  0.99 us (1%)
    ppermute x19, waiting for transfers between devices, ring_x_or_z(): out.append(lax.ppermute(value, AXES, pairs))  27.4 us
    ppermute x19, starting transfers between devices, ring_x_or_z(): out.append(lax.ppermute(value, AXES, pairs))  21.6 us
    ppermute x5, starting transfers between devices, swap(): return lax.ppermute(value, 'c', [(0, 1), (1, 0)])  13.6 us
    pallas_call x5, Pallas kernels, result(): pl.pallas_call(functools.partial(result_kernel, sources, last, quarter //...  11.5 us
    pallas_call x1, Pallas kernels, merge(): pl.pallas_call(functools.partial(merge_kernel, width), out_shape=[pltpu.V...  6.14 us
    ppermute x3, waiting for transfers between devices, ring_y(): lax.ppermute(value, 'y', [(i, (i + k) % n) for i in range(n)])  5.11 us
    ppermute x3, starting transfers between devices, ring_y(): lax.ppermute(value, 'y', [(i, (i + k) % n) for i in range(n)])  4.47 us
  transfers between devices with their start and end apart: 27, of which 18 were waited for; matrix products, arithmetic and copies ran while one was open for 0% of the time, Pallas kernels for 13%

profile of v7, /device:TPU:1, one launch (start us, length us, event | category | flops | bytes accessed | tf_op | source)
XLA Modules:
  0.0 97.7 jit_solution(1298279852805646196)
XLA Ops:
  0.6 6.1 %merge.1 = (bf16[320,10240]{1,0:T(8,128)(2,1)S(1)}, f32[160,128]{1,0:T(8,128)S(1)}) custom-call(bf16[320,10240]{1,0:T(8,128)(2,1)} %bitcast.3, bf16[320,10240]{1,0:T(8,128)(2,1)} %bitcast.4, bf16[64,10240]{1,0:T(8,128)(2,1)} %q_hbm.1), custom_call_target="tpu_custom_call" | custom-call | flops 419430400 | bytes 13107200 | tf_op jit(solution)/shard_map/merge/pallas_call | solution.py:124
  6.8 4.5 %collective-permute-start.2 = (f32[160,128]{1,0:T(8,128)S(1)}, f32[160,128]{1,0:T(8,128)S(1)}, u32[]{:S(2)}, u32[]{:S(2)}) collective-permute-start(f32[160,128]{1,0:T(8,128)S(1)} %get-tuple-element.37), channel_id=1, source_target_pairs={{0,16},{1,65},{2,18},{3,67},{4,20},{5,69},{6,22},{7,71},{8,24},{9,... | collective-permute-start | bytes 245768 | tf_op jit(solution)/shard_map/ppermute | solution.py:58
  11.3 0.4 collective-permute-start.1
  11.7 1.0 %collective-permute-start = (f32[160,128]{1,0:T(8,128)S(1)}, f32[160,128]{1,0:T(8,128)S(1)}, u32[]{:S(2)}, u32[]{:S(2)}) collective-permute-start(f32[160,128]{1,0:T(8,128)S(1)} %get-tuple-element.37), channel_id=1, source_target_pairs={{0,8},{1,33},{2,10},{3,35},{4,12},{5,37},{6,14},{7,39},{8,16},{9,4... | collective-permute-start | bytes 245768 | tf_op jit(solution)/shard_map/ppermute | solution.py:58
  12.7 0.7 collective-permute-done.2
  13.4 1.6 %collective-permute-done.1 = f32[160,128]{1,0:T(8,128)S(1)} collective-permute-done((f32[160,128]{1,0:T(8,128)S(1)}, f32[160,128]{1,0:T(8,128)S(1)}, u32[]{:S(2)}, u32[]{:S(2)}) %collective-permute-start.1) | collective-permute-done | bytes 81952 | tf_op jit(solution)/shard_map/ppermute | solution.py:58
  15.0 1.2 %collective-permute-done = f32[160,128]{1,0:T(8,128)S(1)} collective-permute-done((f32[160,128]{1,0:T(8,128)S(1)}, f32[160,128]{1,0:T(8,128)S(1)}, u32[]{:S(2)}, u32[]{:S(2)}) %collective-permute-start) | collective-permute-done | bytes 81952 | tf_op jit(solution)/shard_map/ppermute | solution.py:58
  16.2 2.8 %collective-permute-start.5 = (f32[160,128]{1,0:T(8,128)S(1)}, f32[160,128]{1,0:T(8,128)S(1)}, u32[]{:S(2)}, u32[]{:S(2)}) collective-permute-start(f32[160,128]{1,0:T(8,128)S(1)} %add_add_fusion.a_ref), channel_id=1, source_target_pairs={{0,64},{1,17},{2,66},{3,19},{4,68},{5,21},{6,70},{7,23},{8,72},{9,... | collective-permute-start | bytes 245768 | tf_op jit(solution)/shard_map/ppermute | solution.py:58
  19.1 0.9 collective-permute-start.4
  19.9 0.6 collective-permute-start.3
  20.5 0.6 collective-permute-done.5.d_ref
  21.1 1.2 %collective-permute-done.4.c_ref = f32[160,128]{1,0:T(8,128)S(1)} collective-permute-done((f32[160,128]{1,0:T(8,128)S(1)}, f32[160,128]{1,0:T(8,128)S(1)}, u32[]{:S(2)}, u32[]{:S(2)}) %collective-permute-start.4) | collective-permute-done | bytes 81952 | tf_op jit(solution)/shard_map/ppermute | solution.py:58
  22.4 2.1 %collective-permute-done.3.b_ref = f32[160,128]{1,0:T(8,128)S(1)} collective-permute-done((f32[160,128]{1,0:T(8,128)S(1)}, f32[160,128]{1,0:T(8,128)S(1)}, u32[]{:S(2)}, u32[]{:S(2)}) %collective-permute-start.3) | collective-permute-done | bytes 81952 | tf_op jit(solution)/shard_map/ppermute | solution.py:58
  24.4 1.7 %first_right.1 = (f32[2600,128]{1,0:T(8,128)S(1)}, f32[40,128]{1,0:T(8,128)S(1)}, f32[64,320]{1,0:T(8,128)S(1)}, bf16[192,320]{1,0:T(8,128)(2,1)S(1)}) custom-call(f32[160,128]{1,0:T(8,128)S(1)} %add_add_fusion.a_ref, f32[160,128]{1,0:T(8,128)S(1)} %collective-permute-done.3.b_ref, f32[160,128]{1,0:T(8,128)S(1)} %collective-permute-done.4.c_ref, ...), custom_call_target="tpu_custom_call" | custom-call | flops 629145600 | bytes 1310720 | tf_op jit(solution)/shard_map/first_right/pallas_call | solution.py:201
  26.1 4.2 %collective-permute-start.6 = (f32[2600,128]{1,0:T(8,128)S(1)}, f32[2600,128]{1,0:T(8,128)S(1)}, u32[]{:S(2)}, u32[]{:S(2)}) collective-permute-start(f32[2600,128]{1,0:T(8,128)S(1)} %get-tuple-element.40), channel_id=1, source_target_pairs={{0,1},{1,0},{2,3},{3,2},{4,5},{5,4},{6,7},{7,6},{8,9},{9,8},{10,11... | collective-permute-start | bytes 3993608 | tf_op jit(solution)/shard_map/ppermute | solution.py:68
  30.3 1.4 %second_right.1.kept_ref = f32[2560,128]{1,0:T(8,128)S(1)} custom-call(bf16[192,320]{1,0:T(8,128)(2,1)S(1)} %get-tuple-element.39.pieces_ref, bf16[320,10240]{1,0:T(8,128)(2,1)S(1)} %get-tuple-element.38.m_ref), custom_call_target="tpu_custom_call" | custom-call | flops 629145600 | bytes 1310720 | tf_op jit(solution)/shard_map/second_right/pallas_call | solution.py:219
  31.7 1.3 %collective-permute-done.6.got_ref = f32[2600,128]{1,0:T(8,128)S(1)} collective-permute-done((f32[2600,128]{1,0:T(8,128)S(1)}, f32[2600,128]{1,0:T(8,128)S(1)}, u32[]{:S(2)}, u32[]{:S(2)}) %collective-permute-start.6) | collective-permute-done | bytes 1331232 | tf_op jit(solution)/shard_map/ppermute | solution.py:68
  33.0 0.3 pair.1
  33.3 0.1 collective-permute-start.7
  33.4 2.7 %collective-permute-start.8 = (f32[640,128]{1,0:T(8,128)S(1)}, f32[640,128]{1,0:T(8,128)S(1)}, u32[]{:S(2)}, u32[]{:S(2)}) collective-permute-start(f32[640,128]{1,0:T(8,128)S(1)} %get-tuple-element.44), channel_id=1, source_target_pairs={{0,24},{1,97},{2,26},{3,99},{4,28},{5,101},{6,30},{7,103},{8,0},{9... | collective-permute-start | bytes 983048 | tf_op jit(solution)/shard_map/ppermute | solution.py:58
  36.0 0.0 collective-permute-start.9
  36.0 8.3 %collective-permute-done.7.b_ref = f32[640,128]{1,0:T(8,128)S(1)} collective-permute-done((f32[640,128]{1,0:T(8,128)S(1)}, f32[640,128]{1,0:T(8,128)S(1)}, u32[]{:S(2)}, u32[]{:S(2)}) %collective-permute-start.7) | collective-permute-done | bytes 327712 | tf_op jit(solution)/shard_map/ppermute | solution.py:58
  44.3 0.0 collective-permute-done.8.c_ref
  44.3 0.0 collective-permute-done.9.d_ref
  44.3 0.1 add_quarters.1
  44.4 0.1 collective-permute-start.10
  44.5 2.7 %collective-permute-start.11 = (f32[160,128]{1,0:T(8,128)S(1)}, f32[160,128]{1,0:T(8,128)S(1)}, u32[]{:S(2)}, u32[]{:S(2)}) collective-permute-start(f32[160,128]{1,0:T(8,128)S(1)} %get-tuple-element.48), channel_id=1, source_target_pairs={{0,96},{1,25},{2,98},{3,27},{4,100},{5,29},{6,102},{7,31},{8,104},... | collective-permute-start | bytes 245768 | tf_op jit(solution)/shard_map/ppermute | solution.py:58
  47.1 0.0 collective-permute-start.12
  47.1 1.8 %collective-permute-done.10.b_ref = f32[160,128]{1,0:T(8,128)S(1)} collective-permute-done((f32[160,128]{1,0:T(8,128)S(1)}, f32[160,128]{1,0:T(8,128)S(1)}, u32[]{:S(2)}, u32[]{:S(2)}) %collective-permute-start.10) | collective-permute-done | bytes 81952 | tf_op jit(solution)/shard_map/ppermute | solution.py:58
  49.0 0.4 collective-permute-done.11.c_ref
  49.4 2.5 %collective-permute-done.12.d_ref = f32[160,128]{1,0:T(8,128)S(1)} collective-permute-done((f32[160,128]{1,0:T(8,128)S(1)}, f32[160,128]{1,0:T(8,128)S(1)}, u32[]{:S(2)}, u32[]{:S(2)}) %collective-permute-start.12) | collective-permute-done | bytes 81952 | tf_op jit(solution)/shard_map/ppermute | solution.py:58
  51.9 3.0 %collective-permute-start.15 = (f32[200,128]{1,0:T(8,128)S(1)}, f32[200,128]{1,0:T(8,128)S(1)}, u32[]{:S(2)}, u32[]{:S(2)}) collective-permute-start(f32[200,128]{1,0:T(8,128)S(1)} %add_parts.1.a_ref), channel_id=1, source_target_pairs={{0,4},{2,6},{4,0},{6,2},{1,5},{3,7},{5,1},{7,3},{8,12},{10,14},{12... | collective-permute-start | bytes 307208 | tf_op jit(solution)/shard_map/ppermute | solution.py:64
  55.0 0.8 collective-permute-start.14
  55.7 0.7 collective-permute-start.13
  56.4 0.6 collective-permute-done.15.d_ref
  57.0 1.5 %collective-permute-done.14.c_ref = f32[200,128]{1,0:T(8,128)S(1)} collective-permute-done((f32[200,128]{1,0:T(8,128)S(1)}, f32[200,128]{1,0:T(8,128)S(1)}, u32[]{:S(2)}, u32[]{:S(2)}) %collective-permute-start.14) | collective-permute-done | bytes 102432 | tf_op jit(solution)/shard_map/ppermute | solution.py:64
  58.5 3.0 %collective-permute-done.13.b_ref = f32[200,128]{1,0:T(8,128)S(1)} collective-permute-done((f32[200,128]{1,0:T(8,128)S(1)}, f32[200,128]{1,0:T(8,128)S(1)}, u32[]{:S(2)}, u32[]{:S(2)}) %collective-permute-start.13) | collective-permute-done | bytes 102432 | tf_op jit(solution)/shard_map/ppermute | solution.py:64
  61.5 0.1 across.1
  61.6 0.1 collective-permute-start.18
  61.7 0.4 collective-permute-start.17
  62.2 1.1 %collective-permute-start.16 = (f32[160,128]{1,0:T(8,128)S(1)}, f32[160,128]{1,0:T(8,128)S(1)}, u32[]{:S(2)}, u32[]{:S(2)}) collective-permute-start(f32[160,128]{1,0:T(8,128)S(1)} %get-tuple-element.55.a_ref), channel_id=1, source_target_pairs={{0,32},{1,9},{2,34},{3,11},{4,36},{5,13},{6,38},{7,15},{8,40},{9,1... | collective-permute-start | bytes 245768 | tf_op jit(solution)/shard_map/ppermute | solution.py:58
  63.2 1.9 %factor.1 = (f32[64,64]{1,0:T(8,128)S(1)}, f32[64,320]{1,0:T(8,128)S(1)}) custom-call(f32[40,128]{1,0:T(8,128)S(1)} %get-tuple-element.51.ext_ref, f32[64,320]{1,0:T(8,128)S(1)} %get-tuple-element.52.p_ref), custom_call_target="tpu_custom_call" | custom-call | flops 4294967296 | bytes 1048576 | tf_op jit(solution)/shard_map/factor/pallas_call | solution.py:387
  65.2 1.4 %collective-permute-done.18.d_ref = f32[160,128]{1,0:T(8,128)S(1)} collective-permute-done((f32[160,128]{1,0:T(8,128)S(1)}, f32[160,128]{1,0:T(8,128)S(1)}, u32[]{:S(2)}, u32[]{:S(2)}) %collective-permute-start.18) | collective-permute-done | bytes 81952 | tf_op jit(solution)/shard_map/ppermute | solution.py:58
  66.6 0.8 collective-permute-done.16.b_ref
  67.4 5.2 %collective-permute-start.21 = (f32[640,128]{1,0:T(8,128)S(1)}, f32[640,128]{1,0:T(8,128)S(1)}, u32[]{:S(2)}, u32[]{:S(2)}) collective-permute-start(f32[640,128]{1,0:T(8,128)S(1)} %assemble.1.refs_0_), channel_id=1, source_target_pairs={{0,1},{1,0},{2,3},{3,2},{4,5},{5,4},{6,7},{7,6},{8,9},{9,8},{10,11... | collective-permute-start | bytes 983048 | tf_op jit(solution)/shard_map/ppermute | solution.py:68
  72.6 1.0 %collective-permute-start.20 = (f32[640,128]{1,0:T(8,128)S(1)}, f32[640,128]{1,0:T(8,128)S(1)}, u32[]{:S(2)}, u32[]{:S(2)}) collective-permute-start(f32[640,128]{1,0:T(8,128)S(1)} %assemble.1.refs_0_), channel_id=1, source_target_pairs={{0,24},{1,97},{2,26},{3,99},{4,28},{5,101},{6,30},{7,103},{8,0},{9... | collective-permute-start | bytes 983048 | tf_op jit(solution)/shard_map/ppermute | solution.py:58
  73.6 0.4 collective-permute-start.19
  74.1 0.0 collective-permute-done.21.refs_1_
  74.1 2.2 %result.5 = (bf16[320,10240]{1,0:T(8,128)(2,1)}, f32[64,10240]{1,0:T(8,128)}, f32[8,128]{1,0:T(8,128)S(1)}) custom-call(f32[64,64]{1,0:T(8,128)S(1)} %get-tuple-element.53.after_ref.solve_ref, f32[64,320]{1,0:T(8,128)S(1)} %get-tuple-element.54.p_ref, bf16[320,10240]{1,0:T(8,128)(2,1)S(1)} %get-tuple-element.38.m_ref, f32[640,128]{1,0:T(8,128)S(1)} %assemble.1.refs_0_, ...), custom_call_target="tpu_custom_call" | custom-call | flops 8589934592 | bytes 1048576 | tf_op jit(solution)/shard_map/result/pallas_call | solution.py:465
  76.3 2.6 %collective-permute-done.20.b_ref.value_ref = f32[640,128]{1,0:T(8,128)S(1)} collective-permute-done((f32[640,128]{1,0:T(8,128)S(1)}, f32[640,128]{1,0:T(8,128)S(1)}, u32[]{:S(2)}, u32[]{:S(2)}) %collective-permute-start.20) | collective-permute-done | bytes 327712 | tf_op jit(solution)/shard_map/ppermute | solution.py:58
  78.8 2.2 %collective-permute-done.19.a_ref.value_ref = f32[640,128]{1,0:T(8,128)S(1)} collective-permute-done((f32[640,128]{1,0:T(8,128)S(1)}, f32[640,128]{1,0:T(8,128)S(1)}, u32[]{:S(2)}, u32[]{:S(2)}) %collective-permute-start.19) | collective-permute-done | bytes 327712 | tf_op jit(solution)/shard_map/ppermute | solution.py:58
  81.1 0.1 collective-permute-start.22
  81.2 2.7 %collective-permute-start.23 = (f32[320,128]{1,0:T(8,128)S(1)}, f32[320,128]{1,0:T(8,128)S(1)}, u32[]{:S(2)}, u32[]{:S(2)}) collective-permute-start(f32[320,128]{1,0:T(8,128)S(1)} %get-tuple-element.58), channel_id=1, source_target_pairs={{0,24},{1,97},{2,26},{3,99},{4,28},{5,101},{6,30},{7,103},{8,0},{9... | collective-permute-start | bytes 491528 | tf_op jit(solution)/shard_map/ppermute | solution.py:58
  83.8 3.7 %collective-permute-start.24 = (f32[640,128]{1,0:T(8,128)S(1)}, f32[640,128]{1,0:T(8,128)S(1)}, u32[]{:S(2)}, u32[]{:S(2)}) collective-permute-start(f32[640,128]{1,0:T(8,128)S(1)} %tie.2.refs_0_), channel_id=1, source_target_pairs={{0,1},{1,0},{2,3},{3,2},{4,5},{5,4},{6,7},{7,6},{8,9},{9,8},{10,11... | collective-permute-start | bytes 983048 | tf_op jit(solution)/shard_map/ppermute | solution.py:68
  87.5 2.8 %result.6 = (bf16[320,10240]{1,0:T(8,128)(2,1)}, f32[64,10240]{1,0:T(8,128)}, f32[8,128]{1,0:T(8,128)}) custom-call(f32[64,64]{1,0:T(8,128)S(1)} %get-tuple-element.53.after_ref.solve_ref, f32[64,320]{1,0:T(8,128)S(1)} %get-tuple-element.54.p_ref, bf16[320,10240]{1,0:T(8,128)(2,1)S(1)} %get-tuple-element.38.m_ref, ...), custom_call_target="tpu_custom_call", output_to_operand_aliasing={{0}: (5, {}), {1}: (6, {})} | custom-call | flops 8589934592 | bytes 1048576 | tf_op jit(solution)/shard_map/result/pallas_call | solution.py:465
  90.3 0.0 collective-permute-done.24.refs_0_
  90.3 0.0 collective-permute-done.25.refs_1_
  90.3 2.2 %result.7 = (bf16[320,10240]{1,0:T(8,128)(2,1)}, f32[64,10240]{1,0:T(8,128)}, f32[8,128]{1,0:T(8,128)S(1)}) custom-call(f32[64,64]{1,0:T(8,128)S(1)} %get-tuple-element.53.after_ref.solve_ref, f32[64,320]{1,0:T(8,128)S(1)} %get-tuple-element.54.p_ref, bf16[320,10240]{1,0:T(8,128)(2,1)S(1)} %get-tuple-element.38.m_ref, ...), custom_call_target="tpu_custom_call", output_to_operand_aliasing={{0}: (5, {}), {1}: (6, {})} | custom-call | flops 8589934592 | bytes 1048576 | tf_op jit(solution)/shard_map/result/pallas_call | solution.py:465
  92.5 0.0 collective-permute-done.22.low_ref
  92.5 0.0 collective-permute-done.23.high_ref
  92.5 0.6 collective-permute-start.26
  93.1 2.2 %result.8 = (bf16[320,10240]{1,0:T(8,128)(2,1)}, f32[64,10240]{1,0:T(8,128)}, f32[8,128]{1,0:T(8,128)}) custom-call(f32[64,64]{1,0:T(8,128)S(1)} %get-tuple-element.53.after_ref.solve_ref, f32[64,320]{1,0:T(8,128)S(1)} %get-tuple-element.54.p_ref, bf16[320,10240]{1,0:T(8,128)(2,1)S(1)} %get-tuple-element.38.m_ref, ...), custom_call_target="tpu_custom_call", output_to_operand_aliasing={{0}: (4, {}), {1}: (5, {})} | custom-call | flops 8589934592 | bytes 1048576 | tf_op jit(solution)/shard_map/result/pallas_call | solution.py:465
  95.3 0.0 collective-permute-done.26.refs_0_
  95.3 2.2 %result.9 = (bf16[320,10240]{1,0:T(8,128)(2,1)}, f32[64,10240]{1,0:T(8,128)}, f32[8,128]{1,0:T(8,128)}, f32[64,320]{1,0:T(8,128)}) custom-call(f32[64,64]{1,0:T(8,128)S(1)} %get-tuple-element.53.after_ref.solve_ref, f32[64,320]{1,0:T(8,128)S(1)} %get-tuple-element.54.p_ref, ...), custom_call_target="tpu_custom_call", output_to_operand_aliasing={{0}: (4, {}), {1}: (5, {})} | custom-call | flops 8589934592 | bytes 1048576 | tf_op jit(solution)/shard_map/result/pallas_call | solution.py:465
  (9 shorter events, 0.1 us)
Async XLA Ops:
  6.8 6.6 %collective-permute-start.2 = (f32[160,128]{1,0:T(8,128)S(1)}, f32[160,128]{1,0:T(8,128)S(1)}, u32[]{:S(2)}, u32[]{:S(2)}) collective-permute-start(f32[160,128]{1,0:T(8,128)S(1)} %get-tuple-element.37), channel_id=1, source_target_pairs={{0,16},{1,65},{2,18},{3,67},{4,20},{5,69},{6,22},{7,71},{8,24},{9,... | collective-permute-start | bytes 245768 | tf_op jit(solution)/shard_map/ppermute | solution.py:58
  11.3 3.7 %collective-permute-start.1 = (f32[160,128]{1,0:T(8,128)S(1)}, f32[160,128]{1,0:T(8,128)S(1)}, u32[]{:S(2)}, u32[]{:S(2)}) collective-permute-start(f32[160,128]{1,0:T(8,128)S(1)} %get-tuple-element.37), channel_id=1, source_target_pairs={{0,24},{1,97},{2,26},{3,99},{4,28},{5,101},{6,30},{7,103},{8,0},{9... | collective-permute-start | bytes 245768 | tf_op jit(solution)/shard_map/ppermute | solution.py:58
  11.7 4.5 %collective-permute-start = (f32[160,128]{1,0:T(8,128)S(1)}, f32[160,128]{1,0:T(8,128)S(1)}, u32[]{:S(2)}, u32[]{:S(2)}) collective-permute-start(f32[160,128]{1,0:T(8,128)S(1)} %get-tuple-element.37), channel_id=1, source_target_pairs={{0,8},{1,33},{2,10},{3,35},{4,12},{5,37},{6,14},{7,39},{8,16},{9,4... | collective-permute-start | bytes 245768 | tf_op jit(solution)/shard_map/ppermute | solution.py:58
  16.2 4.9 %collective-permute-start.5 = (f32[160,128]{1,0:T(8,128)S(1)}, f32[160,128]{1,0:T(8,128)S(1)}, u32[]{:S(2)}, u32[]{:S(2)}) collective-permute-start(f32[160,128]{1,0:T(8,128)S(1)} %add_add_fusion.a_ref), channel_id=1, source_target_pairs={{0,64},{1,17},{2,66},{3,19},{4,68},{5,21},{6,70},{7,23},{8,72},{9,... | collective-permute-start | bytes 245768 | tf_op jit(solution)/shard_map/ppermute | solution.py:58
  19.1 3.3 %collective-permute-start.4 = (f32[160,128]{1,0:T(8,128)S(1)}, f32[160,128]{1,0:T(8,128)S(1)}, u32[]{:S(2)}, u32[]{:S(2)}) collective-permute-start(f32[160,128]{1,0:T(8,128)S(1)} %add_add_fusion.a_ref), channel_id=1, source_target_pairs={{0,96},{1,25},{2,98},{3,27},{4,100},{5,29},{6,102},{7,31},{8,104},... | collective-permute-start | bytes 245768 | tf_op jit(solution)/shard_map/ppermute | solution.py:58
  19.9 4.5 %collective-permute-start.3 = (f32[160,128]{1,0:T(8,128)S(1)}, f32[160,128]{1,0:T(8,128)S(1)}, u32[]{:S(2)}, u32[]{:S(2)}) collective-permute-start(f32[160,128]{1,0:T(8,128)S(1)} %add_add_fusion.a_ref), channel_id=1, source_target_pairs={{0,32},{1,9},{2,34},{3,11},{4,36},{5,13},{6,38},{7,15},{8,40},{9,1... | collective-permute-start | bytes 245768 | tf_op jit(solution)/shard_map/ppermute | solution.py:58
  26.1 6.9 %collective-permute-start.6 = (f32[2600,128]{1,0:T(8,128)S(1)}, f32[2600,128]{1,0:T(8,128)S(1)}, u32[]{:S(2)}, u32[]{:S(2)}) collective-permute-start(f32[2600,128]{1,0:T(8,128)S(1)} %get-tuple-element.40), channel_id=1, source_target_pairs={{0,1},{1,0},{2,3},{3,2},{4,5},{5,4},{6,7},{7,6},{8,9},{9,8},{10,11... | collective-permute-start | bytes 3993608 | tf_op jit(solution)/shard_map/ppermute | solution.py:68
  33.3 11.0 %collective-permute-start.7 = (f32[640,128]{1,0:T(8,128)S(1)}, f32[640,128]{1,0:T(8,128)S(1)}, u32[]{:S(2)}, u32[]{:S(2)}) collective-permute-start(f32[640,128]{1,0:T(8,128)S(1)} %get-tuple-element.43), channel_id=1, source_target_pairs={{0,8},{1,33},{2,10},{3,35},{4,12},{5,37},{6,14},{7,39},{8,16},{9,4... | collective-permute-start | bytes 983048 | tf_op jit(solution)/shard_map/ppermute | solution.py:58
  33.4 10.9 %collective-permute-start.8 = (f32[640,128]{1,0:T(8,128)S(1)}, f32[640,128]{1,0:T(8,128)S(1)}, u32[]{:S(2)}, u32[]{:S(2)}) collective-permute-start(f32[640,128]{1,0:T(8,128)S(1)} %get-tuple-element.44), channel_id=1, source_target_pairs={{0,24},{1,97},{2,26},{3,99},{4,28},{5,101},{6,30},{7,103},{8,0},{9... | collective-permute-start | bytes 983048 | tf_op jit(solution)/shard_map/ppermute | solution.py:58
  36.0 8.3 %collective-permute-start.9 = (f32[640,128]{1,0:T(8,128)S(1)}, f32[640,128]{1,0:T(8,128)S(1)}, u32[]{:S(2)}, u32[]{:S(2)}) collective-permute-start(f32[640,128]{1,0:T(8,128)S(1)} %get-tuple-element.45), channel_id=1, source_target_pairs={{0,16},{1,65},{2,18},{3,67},{4,20},{5,69},{6,22},{7,71},{8,24},{9,... | collective-permute-start | bytes 983048 | tf_op jit(solution)/shard_map/ppermute | solution.py:58
  44.4 4.6 %collective-permute-start.10 = (f32[160,128]{1,0:T(8,128)S(1)}, f32[160,128]{1,0:T(8,128)S(1)}, u32[]{:S(2)}, u32[]{:S(2)}) collective-permute-start(f32[160,128]{1,0:T(8,128)S(1)} %get-tuple-element.47), channel_id=1, source_target_pairs={{0,32},{1,9},{2,34},{3,11},{4,36},{5,13},{6,38},{7,15},{8,40},{9,1... | collective-permute-start | bytes 245768 | tf_op jit(solution)/shard_map/ppermute | solution.py:58
  44.5 4.9 %collective-permute-start.11 = (f32[160,128]{1,0:T(8,128)S(1)}, f32[160,128]{1,0:T(8,128)S(1)}, u32[]{:S(2)}, u32[]{:S(2)}) collective-permute-start(f32[160,128]{1,0:T(8,128)S(1)} %get-tuple-element.48), channel_id=1, source_target_pairs={{0,96},{1,25},{2,98},{3,27},{4,100},{5,29},{6,102},{7,31},{8,104},... | collective-permute-start | bytes 245768 | tf_op jit(solution)/shard_map/ppermute | solution.py:58
  47.1 4.8 %collective-permute-start.12 = (f32[160,128]{1,0:T(8,128)S(1)}, f32[160,128]{1,0:T(8,128)S(1)}, u32[]{:S(2)}, u32[]{:S(2)}) collective-permute-start(f32[160,128]{1,0:T(8,128)S(1)} %get-tuple-element.49), channel_id=1, source_target_pairs={{0,64},{1,17},{2,66},{3,19},{4,68},{5,21},{6,70},{7,23},{8,72},{9,... | collective-permute-start | bytes 245768 | tf_op jit(solution)/shard_map/ppermute | solution.py:58
  51.9 5.1 %collective-permute-start.15 = (f32[200,128]{1,0:T(8,128)S(1)}, f32[200,128]{1,0:T(8,128)S(1)}, u32[]{:S(2)}, u32[]{:S(2)}) collective-permute-start(f32[200,128]{1,0:T(8,128)S(1)} %add_parts.1.a_ref), channel_id=1, source_target_pairs={{0,4},{2,6},{4,0},{6,2},{1,5},{3,7},{5,1},{7,3},{8,12},{10,14},{12... | collective-permute-start | bytes 307208 | tf_op jit(solution)/shard_map/ppermute | solution.py:64
  55.0 3.5 %collective-permute-start.14 = (f32[200,128]{1,0:T(8,128)S(1)}, f32[200,128]{1,0:T(8,128)S(1)}, u32[]{:S(2)}, u32[]{:S(2)}) collective-permute-start(f32[200,128]{1,0:T(8,128)S(1)} %add_parts.1.a_ref), channel_id=1, source_target_pairs={{0,6},{2,0},{4,2},{6,4},{1,7},{3,1},{5,3},{7,5},{8,14},{10,8},{12,... | collective-permute-start | bytes 307208 | tf_op jit(solution)/shard_map/ppermute | solution.py:64
  55.7 5.8 %collective-permute-start.13 = (f32[200,128]{1,0:T(8,128)S(1)}, f32[200,128]{1,0:T(8,128)S(1)}, u32[]{:S(2)}, u32[]{:S(2)}) collective-permute-start(f32[200,128]{1,0:T(8,128)S(1)} %add_parts.1.a_ref), channel_id=1, source_target_pairs={{0,2},{2,4},{4,6},{6,0},{1,3},{3,5},{5,7},{7,1},{8,10},{10,12},{12... | collective-permute-start | bytes 307208 | tf_op jit(solution)/shard_map/ppermute | solution.py:64
  61.6 4.9 %collective-permute-start.18 = (f32[160,128]{1,0:T(8,128)S(1)}, f32[160,128]{1,0:T(8,128)S(1)}, u32[]{:S(2)}, u32[]{:S(2)}) collective-permute-start(f32[160,128]{1,0:T(8,128)S(1)} %get-tuple-element.55.a_ref), channel_id=1, source_target_pairs={{0,64},{1,17},{2,66},{3,19},{4,68},{5,21},{6,70},{7,23},{8,72},{9,... | collective-permute-start | bytes 245768 | tf_op jit(solution)/shard_map/ppermute | solution.py:58
  61.7 4.8 %collective-permute-start.17 = (f32[160,128]{1,0:T(8,128)S(1)}, f32[160,128]{1,0:T(8,128)S(1)}, u32[]{:S(2)}, u32[]{:S(2)}) collective-permute-start(f32[160,128]{1,0:T(8,128)S(1)} %get-tuple-element.55.a_ref), channel_id=1, source_target_pairs={{0,96},{1,25},{2,98},{3,27},{4,100},{5,29},{6,102},{7,31},{8,104},... | collective-permute-start | bytes 245768 | tf_op jit(solution)/shard_map/ppermute | solution.py:58
  62.2 5.2 %collective-permute-start.16 = (f32[160,128]{1,0:T(8,128)S(1)}, f32[160,128]{1,0:T(8,128)S(1)}, u32[]{:S(2)}, u32[]{:S(2)}) collective-permute-start(f32[160,128]{1,0:T(8,128)S(1)} %get-tuple-element.55.a_ref), channel_id=1, source_target_pairs={{0,32},{1,9},{2,34},{3,11},{4,36},{5,13},{6,38},{7,15},{8,40},{9,1... | collective-permute-start | bytes 245768 | tf_op jit(solution)/shard_map/ppermute | solution.py:58
  67.4 6.7 %collective-permute-start.21 = (f32[640,128]{1,0:T(8,128)S(1)}, f32[640,128]{1,0:T(8,128)S(1)}, u32[]{:S(2)}, u32[]{:S(2)}) collective-permute-start(f32[640,128]{1,0:T(8,128)S(1)} %assemble.1.refs_0_), channel_id=1, source_target_pairs={{0,1},{1,0},{2,3},{3,2},{4,5},{5,4},{6,7},{7,6},{8,9},{9,8},{10,11... | collective-permute-start | bytes 983048 | tf_op jit(solution)/shard_map/ppermute | solution.py:68
  72.6 6.2 %collective-permute-start.20 = (f32[640,128]{1,0:T(8,128)S(1)}, f32[640,128]{1,0:T(8,128)S(1)}, u32[]{:S(2)}, u32[]{:S(2)}) collective-permute-start(f32[640,128]{1,0:T(8,128)S(1)} %assemble.1.refs_0_), channel_id=1, source_target_pairs={{0,24},{1,97},{2,26},{3,99},{4,28},{5,101},{6,30},{7,103},{8,0},{9... | collective-permute-start | bytes 983048 | tf_op jit(solution)/shard_map/ppermute | solution.py:58
  73.6 7.4 %collective-permute-start.19 = (f32[640,128]{1,0:T(8,128)S(1)}, f32[640,128]{1,0:T(8,128)S(1)}, u32[]{:S(2)}, u32[]{:S(2)}) collective-permute-start(f32[640,128]{1,0:T(8,128)S(1)} %assemble.1.refs_0_), channel_id=1, source_target_pairs={{0,8},{1,33},{2,10},{3,35},{4,12},{5,37},{6,14},{7,39},{8,16},{9,4... | collective-permute-start | bytes 983048 | tf_op jit(solution)/shard_map/ppermute | solution.py:58
  81.1 11.4 %collective-permute-start.22 = (f32[320,128]{1,0:T(8,128)S(1)}, f32[320,128]{1,0:T(8,128)S(1)}, u32[]{:S(2)}, u32[]{:S(2)}) collective-permute-start(f32[320,128]{1,0:T(8,128)S(1)} %get-tuple-element.57), channel_id=1, source_target_pairs={{0,8},{1,33},{2,10},{3,35},{4,12},{5,37},{6,14},{7,39},{8,16},{9,4... | collective-permute-start | bytes 491528 | tf_op jit(solution)/shard_map/ppermute | solution.py:58
  81.2 11.3 %collective-permute-start.23 = (f32[320,128]{1,0:T(8,128)S(1)}, f32[320,128]{1,0:T(8,128)S(1)}, u32[]{:S(2)}, u32[]{:S(2)}) collective-permute-start(f32[320,128]{1,0:T(8,128)S(1)} %get-tuple-element.58), channel_id=1, source_target_pairs={{0,24},{1,97},{2,26},{3,99},{4,28},{5,101},{6,30},{7,103},{8,0},{9... | collective-permute-start | bytes 491528 | tf_op jit(solution)/shard_map/ppermute | solution.py:58
  83.8 6.5 %collective-permute-start.24 = (f32[640,128]{1,0:T(8,128)S(1)}, f32[640,128]{1,0:T(8,128)S(1)}, u32[]{:S(2)}, u32[]{:S(2)}) collective-permute-start(f32[640,128]{1,0:T(8,128)S(1)} %tie.2.refs_0_), channel_id=1, source_target_pairs={{0,1},{1,0},{2,3},{3,2},{4,5},{5,4},{6,7},{7,6},{8,9},{9,8},{10,11... | collective-permute-start | bytes 983048 | tf_op jit(solution)/shard_map/ppermute | solution.py:68
  87.5 2.8 %collective-permute-start.25 = (f32[640,128]{1,0:T(8,128)S(1)}, f32[640,128]{1,0:T(8,128)S(1)}, u32[]{:S(2)}, u32[]{:S(2)}) collective-permute-start(f32[640,128]{1,0:T(8,128)S(1)} %tie.3.refs_1_), channel_id=1, source_target_pairs={{0,1},{1,0},{2,3},{3,2},{4,5},{5,4},{6,7},{7,6},{8,9},{9,8},{10,11... | collective-permute-start | bytes 983048 | tf_op jit(solution)/shard_map/ppermute | solution.py:68
  92.5 2.8 %collective-permute-start.26 = (f32[640,128]{1,0:T(8,128)S(1)}, f32[640,128]{1,0:T(8,128)S(1)}, u32[]{:S(2)}, u32[]{:S(2)}) collective-permute-start(f32[640,128]{1,0:T(8,128)S(1)} %join.1.refs_0_), channel_id=1, source_target_pairs={{0,1},{1,0},{2,3},{3,2},{4,5},{5,4},{6,7},{7,6},{8,9},{9,8},{10,11... | collective-permute-start | bytes 983048 | tf_op jit(solution)/shard_map/ppermute | solution.py:68

commit v8 on v7

--- a/solution.py
+++ b/solution.py
@@ -16,6 +16,7 @@
 MIB = 1 << 20
 ROWS = 8
 QUARTERS = 4
+RIGHT = 1 << 33
 SHIFTS = (1, 3, 2)
 ANY = pl.BlockSpec(memory_space=pl.ANY)
 WHOLE = pl.BlockSpec(memory_space=pltpu.VMEM)
@@ -138,24 +139,24 @@
     )(gradient, error, q_start)
 
 
-def right_tiles(half, pieces, m_ref, out_ref):
+def right_tiles(quarters, pieces, m_ref, out_ref):
     rank = pieces.shape[0] // 3
     width = m_ref.shape[1] // 2 // QUARTERS
-    size = rank * width // 128
-
-    def step(a, carry):
-        at = pl.multiple_of((half * QUARTERS + a) * width, width)
+    to = 0
+    for quarter in quarters:
+        at = pl.multiple_of(quarter * width, width)
         t = jnp.dot(pieces, m_ref[:, pl.ds(at, width)], preferred_element_type=F32)
         t = t[:rank] + (t[rank : 2 * rank] + t[2 * rank :])
-        to = 0
         for g in range(rank // ROWS):
             for n in range(width // 128):
-                here = pl.ds(pl.multiple_of(a * size + to, ROWS), ROWS)
-                out_ref[here, :] = t[g * ROWS : (g + 1) * ROWS, n * 128 : (n + 1) * 128]
+                out_ref[to : to + ROWS, :] = t[g * ROWS : (g + 1) * ROWS, n * 128 : (n + 1) * 128]
                 to += ROWS
-        return carry
-
-    lax.fori_loop(0, QUARTERS, step, 0, unroll=2)
+
+
+def quarters_of(own, turns):
+    core, one, two = place()
+    core, turn = (core, one) if own else (1 - core, two)
+    return [core * QUARTERS + (turn + k) % QUARTERS for k in turns]
 
 
 def split(n):
@@ -165,12 +166,15 @@
     return high, middle, (n - middle.astype(F32)).astype(BF16)
 
 
-def first_right_kernel(replicas, rank, a_ref, b_ref, c_ref, d_ref, m_ref, out_ref, ext_ref, p_ref, pieces_ref):
+def first_right_kernel(replicas, rank, turns, a_ref, b_ref, c_ref, d_ref, m_ref, out_ref, ext_ref, p_ref, pieces_ref):
     p = (a_ref[...] + b_ref[...] + (c_ref[...] + d_ref[...])) * (1.0 / replicas)
     peak = jnp.max(jnp.abs(p), axis=(0, 1), keepdims=True)
     peak = jnp.where(peak > 0, peak, 1.0)
     p = unpack(p, rank)
     p_ref[...] = p
+    pieces = jnp.concatenate(split(p / peak), axis=0)
+    pieces_ref[...] = pieces
+    right_tiles(quarters_of(False, turns), pieces, m_ref, out_ref)
     gram = lax.dot_general(
         p, p, (((1,), (1,)), ((), ())), precision=HIGHEST, preferred_element_type=F32
     )
@@ -185,21 +189,19 @@
     )
     ext_ref[...] = ext
     out_ref[out_ref.shape[0] - ext.shape[0] :, :] = ext
-    pieces = jnp.concatenate(split(p / peak), axis=0)
-    pieces_ref[...] = pieces
-    right_tiles(1 - place()[0], pieces, m_ref, out_ref)
-
-
-def second_right_kernel(pieces_ref, m_ref, out_ref):
-    right_tiles(place()[0], pieces_ref[...], m_ref, out_ref)
-
-
-def first_right(parts, merged, rank, replicas):
+
+
+def next_right_kernel(own, turns, pieces_ref, m_ref, after_ref, out_ref):
+    del after_ref
+    right_tiles(quarters_of(own, turns), pieces_ref[...], m_ref, out_ref)
+
+
+def first_right(turns, parts, merged, rank, replicas):
     rows, columns = merged.shape
-    size = rank * columns // 256
+    size = rank * columns // 1024
     extra = rank * rank // 128 + ROWS
     return pl.pallas_call(
-        functools.partial(first_right_kernel, replicas, rank),
+        functools.partial(first_right_kernel, replicas, rank, turns),
         out_shape=[
             jax.ShapeDtypeStruct((size + extra, 128), F32),
             pltpu.VMEM((extra, 128), F32),
@@ -209,57 +211,83 @@
         in_specs=[WHOLE] * 5,
         out_specs=[WHOLE] * 4,
         compiler_params=params(12),
-        cost_estimate=cost(3 * rank * rows * columns, 512 * size),
+        cost_estimate=cost(RIGHT, 1 << 20),
         name="first_right",
     )(*parts, merged)
 
 
-def second_right(pieces, merged):
-    size = pieces.shape[0] // 3 * merged.shape[1] // 256
-    return pl.pallas_call(
-        second_right_kernel,
-        out_shape=pltpu.VMEM((size, 128), F32),
-        in_specs=[WHOLE, WHOLE],
+def next_right(own, turns, pieces, merged, after):
+    size = pieces.shape[0] // 3 * merged.shape[1] // 1024 * len(turns)
+    return pl.pallas_call(
+        functools.partial(next_right_kernel, own, turns),
+        out_shape=jax.ShapeDtypeStruct((size, 128), F32),
+        in_specs=[WHOLE, WHOLE, ANY],
         out_specs=WHOLE,
         compiler_params=params(12),
-        cost_estimate=cost(pieces.shape[0] * merged.size, 512 * size),
-        name="second_right",
-    )(pieces, merged)
-
-
-def pair_kernel(kept_ref, got_ref, ext_ref, *out):
-    pair_ref = out[-1]
+        cost_estimate=cost(RIGHT, 1 << 20),
+        name="next_right",
+    )(pieces, merged, after)
+
+
+def first_pair_kernel(kept_ref, got_ref, ext_ref, low_ref, high_ref, pair_ref, weight_ref):
     grams = ext_ref.shape[0] - ROWS
-    ext = kept_ref.shape[0]
-    size = ext // QUARTERS
-    own, its = ext_ref[grams : grams + 1, :1], got_ref[ext + grams : ext + grams + 1, :1]
+    size = kept_ref.shape[0]
+    half = size // 2
+    own, its = ext_ref[grams : grams + 1, :1], got_ref[size + grams : size + grams + 1, :1]
     top = jnp.maximum(own, its)
-    pair_ref[:grams] = ext_ref[:grams] + got_ref[ext : ext + grams]
+    pair_ref[:grams] = ext_ref[:grams] + got_ref[size : size + grams]
     pair_ref[grams:] = jnp.broadcast_to(top, (ROWS, 128))
     own, its = own / top, its / top
-    for k, ref in zip((0,) + SHIFTS, out):
-        at = pl.ds(pl.multiple_of((place()[1] + k) % QUARTERS * size, size), size)
-        ref[...] = kept_ref[at] * own + got_ref[at] * its
-
-
-def pair(kept, got, ext):
-    size = kept.shape[0] // QUARTERS
-    return pl.pallas_call(
-        pair_kernel,
-        out_shape=[jax.ShapeDtypeStruct((size, 128), F32)] * QUARTERS
-        + [pltpu.VMEM(ext.shape, F32)],
+    weight_ref[:ROWS] = jnp.broadcast_to(own, (ROWS, 128))
+    weight_ref[ROWS:] = jnp.broadcast_to(its, (ROWS, 128))
+    low_ref[...] = kept_ref[:half] * own + got_ref[:half] * its
+    high_ref[...] = kept_ref[half:] * own + got_ref[half:size] * its
+
+
+def first_pair(kept, got, ext):
+    half = jax.ShapeDtypeStruct((kept.shape[0] // 2, 128), F32)
+    return pl.pallas_call(
+        first_pair_kernel,
+        out_shape=[half, half, pltpu.VMEM(ext.shape, F32), pltpu.VMEM((2 * ROWS, 128), F32)],
         in_specs=[WHOLE] * 3,
-        out_specs=[WHOLE] * (QUARTERS + 1),
+        out_specs=[WHOLE] * 4,
         compiler_params=params(8),
-        name="pair",
+        name="first_pair",
     )(kept, got, ext)
 
 
-def add_quarters_kernel(a_ref, b_ref, c_ref, d_ref, *out):
+def next_pair_kernel(kept_ref, got_ref, weight_ref, low_ref, high_ref, *out):
+    own, its = weight_ref[:1, :1], weight_ref[ROWS : ROWS + 1, :1]
+    size = out[0].shape[0]
+    half = size // 2
+    for n, ref in enumerate(out):
+        for part in (0, 1):
+            at = slice(n * size + part * half, n * size + (part + 1) * half)
+            x = kept_ref[at] * own + got_ref[at] * its
+            if (n, part) == (0, 0):
+                x = x + low_ref[...]
+            if (n, part) == (1, 1):
+                x = x + high_ref[...]
+            ref[part * half : (part + 1) * half] = x
+
+
+def next_pair(kept, got, weight, low, high):
+    size = kept.shape[0] // 3
+    return pl.pallas_call(
+        next_pair_kernel,
+        out_shape=[jax.ShapeDtypeStruct((size, 128), F32)] * 3,
+        in_specs=[WHOLE] * 5,
+        out_specs=[WHOLE] * 3,
+        compiler_params=params(8),
+        name="next_pair",
+    )(kept, got, weight, low, high)
+
+
+def add_quarters_kernel(a_ref, b_ref, c_ref, *out):
     size = a_ref.shape[0] // QUARTERS
     for k, ref in zip((0,) + SHIFTS, out):
         at = pl.ds(pl.multiple_of((place()[2] + k) % QUARTERS * size, size), size)
-        ref[...] = (a_ref[at] + b_ref[at]) + (c_ref[at] + d_ref[at])
+        ref[...] = a_ref[at] + (b_ref[at] + c_ref[at])
 
 
 def add_quarters(parts):
@@ -267,7 +295,7 @@
     return pl.pallas_call(
         add_quarters_kernel,
         out_shape=[jax.ShapeDtypeStruct((size, 128), F32)] * QUARTERS,
-        in_specs=[WHOLE] * QUARTERS,
+        in_specs=[WHOLE] * 3,
         out_specs=[WHOLE] * QUARTERS,
         compiler_params=params(8),
         name="add_quarters",
@@ -543,12 +571,17 @@
     a, b, c = ring_x_or_z([p] * 3, 0)
     p = (p + a) + (b + c)
     sent, ext, p_mean, pieces = first_right(
-        (p, *ring_x_or_z([p] * 3, 1)), merged, rank, replicas
+        (2,), (p, *ring_x_or_z([p] * 3, 1)), merged, rank, replicas
     )
     got = swap(sent)
-    kept = second_right(pieces, merged)
-    own, *sent, ext = pair(kept, got, ext)
-    own, *sent = add_quarters((own, *ring_x_or_z(sent, 0)))
+    sent = next_right(False, (1, 3, 0), pieces, merged, ext)
+    got_next = swap(sent)
+    kept = next_right(True, (2,), pieces, merged, sent)
+    low, high, ext, weight = first_pair(kept, got, ext)
+    kept = next_right(True, (1, 3, 0), pieces, merged, weight)
+    low, high = ring_x_or_z((low, high), 0, (1, 3))
+    up, down, own = next_pair(kept, got_next, weight, low, high)
+    own, *sent = add_quarters((own, *ring_x_or_z((up, down), 0, (1, 3))))
     part = add_parts((own, *ring_x_or_z(sent, 1)), ext)
     total, ext = across((part, *ring_y(part)), ext.shape[0])
     solve, p_hat = factor(ext, p_mean, replicas)

time: 97.8 us -> 98.8 us (1.010)
  starting transfers between devices: 39.7 us -> 43.3 us
  waiting for transfers between devices: 33.9 us -> 31.3 us
    ppermute x19 -> x20, starting transfers between devices: 21.6 us -> 24.3 us  [ring_x_or_z(): out.append(lax.ppermute(value, AXES, pairs))]
    ppermute x19 -> x20, waiting for transfers between devices: 27.4 us -> 26 us  [ring_x_or_z(): out.append(lax.ppermute(value, AXES, pairs))]
    ppermute x5 -> x6, waiting for transfers between devices: 1.32 us -> 0.02 us  [swap(): return lax.ppermute(value, 'c', [(0, 1), (1, 0)])]
    ppermute x5 -> x6, starting transfers between devices: 13.6 us -> 14.5 us  [swap(): return lax.ppermute(value, 'c', [(0, 1), (1, 0)])]
    pallas_call x3 -> x6, Pallas kernels: 3.36 us -> 3.27 us  [the longest x3 2.25 us: next_right(): pl.pallas_call(functools.partial(next_right_kernel, own, turns), out_shap...]
  transfers between devices with their start and end apart: 27 -> 29, of which waited for: 18 -> 18; matrix products, arithmetic and copies ran while one was open for 0% -> 0% of each run, Pallas kernels for 13% -> 14%
where the time goes in v8:
time: 98.8 us; the launch traced here: 98.7 us
  starting transfers between devices  43.3 us (44%)
  waiting for transfers between devices  31.3 us (32%)
  Pallas kernels  23 us (23%)
  between operations  1.02 us (1%)
    ppermute x20, waiting for transfers between devices, ring_x_or_z(): out.append(lax.ppermute(value, AXES, pairs))  26 us
    ppermute x20, starting transfers between devices, ring_x_or_z(): out.append(lax.ppermute(value, AXES, pairs))  24.3 us
    ppermute x6, starting transfers between devices, swap(): return lax.ppermute(value, 'c', [(0, 1), (1, 0)])  14.5 us
    pallas_call x5, Pallas kernels, result(): pl.pallas_call(functools.partial(result_kernel, sources, last, quarter //...  11.5 us
    pallas_call x1, Pallas kernels, merge(): pl.pallas_call(functools.partial(merge_kernel, width), out_shape=[pltpu.V...  6.14 us
    ppermute x3, waiting for transfers between devices, ring_y(): lax.ppermute(value, 'y', [(i, (i + k) % n) for i in range(n)])  5.32 us
    ppermute x3, starting transfers between devices, ring_y(): lax.ppermute(value, 'y', [(i, (i + k) % n) for i in range(n)])  4.47 us
    pallas_call x3, Pallas kernels, next_right(): pl.pallas_call(functools.partial(next_right_kernel, own, turns), out_shap...  2.25 us
  transfers between devices with their start and end apart: 29, of which 18 were waited for; matrix products, arithmetic and copies ran while one was open for 0% of the time, Pallas kernels for 14%

profile of v8, /device:TPU:1, one launch (start us, length us, event | category | flops | bytes accessed | tf_op | source)
XLA Modules:
  0.0 98.7 jit_solution(12893515330740622834)
XLA Ops:
  0.6 6.1 %merge.1 = (bf16[320,10240]{1,0:T(8,128)(2,1)S(1)}, f32[160,128]{1,0:T(8,128)S(1)}) custom-call(bf16[320,10240]{1,0:T(8,128)(2,1)} %bitcast.3, bf16[320,10240]{1,0:T(8,128)(2,1)} %bitcast.4, bf16[64,10240]{1,0:T(8,128)(2,1)} %q_hbm.1), custom_call_target="tpu_custom_call" | custom-call | flops 419430400 | bytes 13107200 | tf_op jit(solution)/shard_map/merge/pallas_call | solution.py:125
  6.8 4.5 %collective-permute-start.2 = (f32[160,128]{1,0:T(8,128)S(1)}, f32[160,128]{1,0:T(8,128)S(1)}, u32[]{:S(2)}, u32[]{:S(2)}) collective-permute-start(f32[160,128]{1,0:T(8,128)S(1)} %get-tuple-element.39), channel_id=1, source_target_pairs={{0,16},{1,65},{2,18},{3,67},{4,20},{5,69},{6,22},{7,71},{8,24},{9,... | collective-permute-start | bytes 245768 | tf_op jit(solution)/shard_map/ppermute | solution.py:59
  11.3 0.4 collective-permute-start.1
  11.7 1.0 %collective-permute-start = (f32[160,128]{1,0:T(8,128)S(1)}, f32[160,128]{1,0:T(8,128)S(1)}, u32[]{:S(2)}, u32[]{:S(2)}) collective-permute-start(f32[160,128]{1,0:T(8,128)S(1)} %get-tuple-element.39), channel_id=1, source_target_pairs={{0,8},{1,33},{2,10},{3,35},{4,12},{5,37},{6,14},{7,39},{8,16},{9,4... | collective-permute-start | bytes 245768 | tf_op jit(solution)/shard_map/ppermute | solution.py:59
  12.7 0.7 collective-permute-done.2
  13.4 1.6 %collective-permute-done.1 = f32[160,128]{1,0:T(8,128)S(1)} collective-permute-done((f32[160,128]{1,0:T(8,128)S(1)}, f32[160,128]{1,0:T(8,128)S(1)}, u32[]{:S(2)}, u32[]{:S(2)}) %collective-permute-start.1) | collective-permute-done | bytes 81952 | tf_op jit(solution)/shard_map/ppermute | solution.py:59
  15.0 1.2 %collective-permute-done = f32[160,128]{1,0:T(8,128)S(1)} collective-permute-done((f32[160,128]{1,0:T(8,128)S(1)}, f32[160,128]{1,0:T(8,128)S(1)}, u32[]{:S(2)}, u32[]{:S(2)}) %collective-permute-start) | collective-permute-done | bytes 81952 | tf_op jit(solution)/shard_map/ppermute | solution.py:59
  16.2 2.8 %collective-permute-start.5 = (f32[160,128]{1,0:T(8,128)S(1)}, f32[160,128]{1,0:T(8,128)S(1)}, u32[]{:S(2)}, u32[]{:S(2)}) collective-permute-start(f32[160,128]{1,0:T(8,128)S(1)} %add_add_fusion.a_ref), channel_id=1, source_target_pairs={{0,64},{1,17},{2,66},{3,19},{4,68},{5,21},{6,70},{7,23},{8,72},{9,... | collective-permute-start | bytes 245768 | tf_op jit(solution)/shard_map/ppermute | solution.py:59
  19.1 0.9 collective-permute-start.4
  19.9 0.6 collective-permute-start.3
  20.5 0.6 collective-permute-done.5.d_ref
  21.1 1.2 %collective-permute-done.4.c_ref = f32[160,128]{1,0:T(8,128)S(1)} collective-permute-done((f32[160,128]{1,0:T(8,128)S(1)}, f32[160,128]{1,0:T(8,128)S(1)}, u32[]{:S(2)}, u32[]{:S(2)}) %collective-permute-start.4) | collective-permute-done | bytes 81952 | tf_op jit(solution)/shard_map/ppermute | solution.py:59
  22.4 2.1 %collective-permute-done.3.b_ref = f32[160,128]{1,0:T(8,128)S(1)} collective-permute-done((f32[160,128]{1,0:T(8,128)S(1)}, f32[160,128]{1,0:T(8,128)S(1)}, u32[]{:S(2)}, u32[]{:S(2)}) %collective-permute-start.3) | collective-permute-done | bytes 81952 | tf_op jit(solution)/shard_map/ppermute | solution.py:59
  24.4 0.7 first_right.1
  25.1 4.1 %collective-permute-start.6 = (f32[680,128]{1,0:T(8,128)S(1)}, f32[680,128]{1,0:T(8,128)S(1)}, u32[]{:S(2)}, u32[]{:S(2)}) collective-permute-start(f32[680,128]{1,0:T(8,128)S(1)} %get-tuple-element.43), channel_id=1, source_target_pairs={{0,1},{1,0},{2,3},{3,2},{4,5},{5,4},{6,7},{7,6},{8,9},{9,8},{10,11... | collective-permute-start | bytes 1044488 | tf_op jit(solution)/shard_map/ppermute | solution.py:69
  29.2 0.9 next_right.3.after_ref
  30.2 0.1 collective-permute-start.7
  30.3 0.4 next_right.4.kept_ref
  30.7 0.0 collective-permute-done.6.got_ref
  30.7 0.1 first_pair.1
  30.8 0.1 collective-permute-start.8
  30.9 2.7 %collective-permute-start.9 = (f32[320,128]{1,0:T(8,128)S(1)}, f32[320,128]{1,0:T(8,128)S(1)}, u32[]{:S(2)}, u32[]{:S(2)}) collective-permute-start(f32[320,128]{1,0:T(8,128)S(1)} %get-tuple-element.46), channel_id=1, source_target_pairs={{0,24},{1,97},{2,26},{3,99},{4,28},{5,101},{6,30},{7,103},{8,0},{9... | collective-permute-start | bytes 491528 | tf_op jit(solution)/shard_map/ppermute | solution.py:59
  33.6 0.9 next_right.5.kept_ref
  34.5 2.1 %collective-permute-done.8.low_ref = f32[320,128]{1,0:T(8,128)S(1)} collective-permute-done((f32[320,128]{1,0:T(8,128)S(1)}, f32[320,128]{1,0:T(8,128)S(1)}, u32[]{:S(2)}, u32[]{:S(2)}) %collective-permute-start.8) | collective-permute-done | bytes 163872 | tf_op jit(solution)/shard_map/ppermute | solution.py:59
  36.6 0.0 collective-permute-done.9.high_ref
  36.6 0.0 collective-permute-done.7.got_ref
  36.6 0.2 next_pair.1
  36.8 0.1 collective-permute-start.10
  36.9 2.7 %collective-permute-start.11 = (f32[640,128]{1,0:T(8,128)S(1)}, f32[640,128]{1,0:T(8,128)S(1)}, u32[]{:S(2)}, u32[]{:S(2)}) collective-permute-start(f32[640,128]{1,0:T(8,128)S(1)} %get-tuple-element.49), channel_id=1, source_target_pairs={{0,24},{1,97},{2,26},{3,99},{4,28},{5,101},{6,30},{7,103},{8,0},{9... | collective-permute-start | bytes 983048 | tf_op jit(solution)/shard_map/ppermute | solution.py:59
  39.5 4.8 %collective-permute-done.10.b_ref = f32[640,128]{1,0:T(8,128)S(1)} collective-permute-done((f32[640,128]{1,0:T(8,128)S(1)}, f32[640,128]{1,0:T(8,128)S(1)}, u32[]{:S(2)}, u32[]{:S(2)}) %collective-permute-start.10) | collective-permute-done | bytes 327712 | tf_op jit(solution)/shard_map/ppermute | solution.py:59
  44.3 0.1 collective-permute-start.12
  44.4 2.7 %collective-permute-start.13 = (f32[160,128]{1,0:T(8,128)S(1)}, f32[160,128]{1,0:T(8,128)S(1)}, u32[]{:S(2)}, u32[]{:S(2)}) collective-permute-start(f32[160,128]{1,0:T(8,128)S(1)} %get-tuple-element.52), channel_id=1, source_target_pairs={{0,96},{1,25},{2,98},{3,27},{4,100},{5,29},{6,102},{7,31},{8,104},... | collective-permute-start | bytes 245768 | tf_op jit(solution)/shard_map/ppermute | solution.py:59
  47.1 1.8 %collective-permute-done.12.b_ref = f32[160,128]{1,0:T(8,128)S(1)} collective-permute-done((f32[160,128]{1,0:T(8,128)S(1)}, f32[160,128]{1,0:T(8,128)S(1)}, u32[]{:S(2)}, u32[]{:S(2)}) %collective-permute-start.12) | collective-permute-done | bytes 81952 | tf_op jit(solution)/shard_map/ppermute | solution.py:59
  48.9 0.4 collective-permute-done.13.c_ref
  49.4 2.5 %collective-permute-done.14.d_ref = f32[160,128]{1,0:T(8,128)S(1)} collective-permute-done((f32[160,128]{1,0:T(8,128)S(1)}, f32[160,128]{1,0:T(8,128)S(1)}, u32[]{:S(2)}, u32[]{:S(2)}) %collective-permute-start.14) | collective-permute-done | bytes 81952 | tf_op jit(solution)/shard_map/ppermute | solution.py:59
  51.9 3.0 %collective-permute-start.17 = (f32[200,128]{1,0:T(8,128)S(1)}, f32[200,128]{1,0:T(8,128)S(1)}, u32[]{:S(2)}, u32[]{:S(2)}) collective-permute-start(f32[200,128]{1,0:T(8,128)S(1)} %add_parts.1.a_ref), channel_id=1, source_target_pairs={{0,4},{2,6},{4,0},{6,2},{1,5},{3,7},{5,1},{7,3},{8,12},{10,14},{12... | collective-permute-start | bytes 307208 | tf_op jit(solution)/shard_map/ppermute | solution.py:65
  54.9 0.8 collective-permute-start.16
  55.7 0.7 collective-permute-start.15
  56.4 0.6 collective-permute-done.17.d_ref
  57.0 1.4 %collective-permute-done.16.c_ref = f32[200,128]{1,0:T(8,128)S(1)} collective-permute-done((f32[200,128]{1,0:T(8,128)S(1)}, f32[200,128]{1,0:T(8,128)S(1)}, u32[]{:S(2)}, u32[]{:S(2)}) %collective-permute-start.16) | collective-permute-done | bytes 102432 | tf_op jit(solution)/shard_map/ppermute | solution.py:65
  58.5 3.2 %collective-permute-done.15.b_ref = f32[200,128]{1,0:T(8,128)S(1)} collective-permute-done((f32[200,128]{1,0:T(8,128)S(1)}, f32[200,128]{1,0:T(8,128)S(1)}, u32[]{:S(2)}, u32[]{:S(2)}) %collective-permute-start.15) | collective-permute-done | bytes 102432 | tf_op jit(solution)/shard_map/ppermute | solution.py:65
  61.7 0.1 across.1
  61.8 0.1 collective-permute-start.20
  61.9 0.1 collective-permute-start.19
  62.0 1.5 %collective-permute-start.18 = (f32[160,128]{1,0:T(8,128)S(1)}, f32[160,128]{1,0:T(8,128)S(1)}, u32[]{:S(2)}, u32[]{:S(2)}) collective-permute-start(f32[160,128]{1,0:T(8,128)S(1)} %get-tuple-element.59.a_ref), channel_id=1, source_target_pairs={{0,32},{1,9},{2,34},{3,11},{4,36},{5,13},{6,38},{7,15},{8,40},{9,1... | collective-permute-start | bytes 245768 | tf_op jit(solution)/shard_map/ppermute | solution.py:59
  63.4 1.9 %factor.1 = (f32[64,64]{1,0:T(8,128)S(1)}, f32[64,320]{1,0:T(8,128)S(1)}) custom-call(f32[40,128]{1,0:T(8,128)S(1)} %get-tuple-element.55.ext_ref, f32[64,320]{1,0:T(8,128)S(1)} %get-tuple-element.56.p_ref), custom_call_target="tpu_custom_call" | custom-call | flops 4294967296 | bytes 1048576 | tf_op jit(solution)/shard_map/factor/pallas_call | solution.py:415
  65.4 1.4 %collective-permute-done.20.d_ref = f32[160,128]{1,0:T(8,128)S(1)} collective-permute-done((f32[160,128]{1,0:T(8,128)S(1)}, f32[160,128]{1,0:T(8,128)S(1)}, u32[]{:S(2)}, u32[]{:S(2)}) %collective-permute-start.20) | collective-permute-done | bytes 81952 | tf_op jit(solution)/shard_map/ppermute | solution.py:59
  66.7 0.0 collective-permute-done.19.c_ref
  66.7 0.8 collective-permute-done.18.b_ref
  67.6 5.9 %collective-permute-start.23 = (f32[640,128]{1,0:T(8,128)S(1)}, f32[640,128]{1,0:T(8,128)S(1)}, u32[]{:S(2)}, u32[]{:S(2)}) collective-permute-start(f32[640,128]{1,0:T(8,128)S(1)} %assemble.1.refs_0_), channel_id=1, source_target_pairs={{0,1},{1,0},{2,3},{3,2},{4,5},{5,4},{6,7},{7,6},{8,9},{9,8},{10,11... | collective-permute-start | bytes 983048 | tf_op jit(solution)/shard_map/ppermute | solution.py:69
  73.5 1.0 %collective-permute-start.22 = (f32[640,128]{1,0:T(8,128)S(1)}, f32[640,128]{1,0:T(8,128)S(1)}, u32[]{:S(2)}, u32[]{:S(2)}) collective-permute-start(f32[640,128]{1,0:T(8,128)S(1)} %assemble.1.refs_0_), channel_id=1, source_target_pairs={{0,24},{1,97},{2,26},{3,99},{4,28},{5,101},{6,30},{7,103},{8,0},{9... | collective-permute-start | bytes 983048 | tf_op jit(solution)/shard_map/ppermute | solution.py:59
  74.6 0.4 collective-permute-start.21
  75.0 2.2 %result.5 = (bf16[320,10240]{1,0:T(8,128)(2,1)}, f32[64,10240]{1,0:T(8,128)}, f32[8,128]{1,0:T(8,128)S(1)}) custom-call(f32[64,64]{1,0:T(8,128)S(1)} %get-tuple-element.57.after_ref.solve_ref, f32[64,320]{1,0:T(8,128)S(1)} %get-tuple-element.58.p_ref, bf16[320,10240]{1,0:T(8,128)(2,1)S(1)} %get-tuple-element.40.m_ref, f32[640,128]{1,0:T(8,128)S(1)} %assemble.1.refs_0_, ...), custom_call_target="tpu_custom_call" | custom-call | flops 8589934592 | bytes 1048576 | tf_op jit(solution)/shard_map/result/pallas_call | solution.py:493
  77.1 2.6 %collective-permute-done.22.b_ref.value_ref = f32[640,128]{1,0:T(8,128)S(1)} collective-permute-done((f32[640,128]{1,0:T(8,128)S(1)}, f32[640,128]{1,0:T(8,128)S(1)}, u32[]{:S(2)}, u32[]{:S(2)}) %collective-permute-start.22) | collective-permute-done | bytes 327712 | tf_op jit(solution)/shard_map/ppermute | solution.py:59
  79.7 2.3 %collective-permute-done.21.a_ref.value_ref = f32[640,128]{1,0:T(8,128)S(1)} collective-permute-done((f32[640,128]{1,0:T(8,128)S(1)}, f32[640,128]{1,0:T(8,128)S(1)}, u32[]{:S(2)}, u32[]{:S(2)}) %collective-permute-start.21) | collective-permute-done | bytes 327712 | tf_op jit(solution)/shard_map/ppermute | solution.py:59
  82.0 0.1 collective-permute-start.24
  82.1 2.7 %collective-permute-start.25 = (f32[320,128]{1,0:T(8,128)S(1)}, f32[320,128]{1,0:T(8,128)S(1)}, u32[]{:S(2)}, u32[]{:S(2)}) collective-permute-start(f32[320,128]{1,0:T(8,128)S(1)} %get-tuple-element.62), channel_id=1, source_target_pairs={{0,24},{1,97},{2,26},{3,99},{4,28},{5,101},{6,30},{7,103},{8,0},{9... | collective-permute-start | bytes 491528 | tf_op jit(solution)/shard_map/ppermute | solution.py:59
  84.8 3.8 %collective-permute-start.26 = (f32[640,128]{1,0:T(8,128)S(1)}, f32[640,128]{1,0:T(8,128)S(1)}, u32[]{:S(2)}, u32[]{:S(2)}) collective-permute-start(f32[640,128]{1,0:T(8,128)S(1)} %tie.2.refs_0_), channel_id=1, source_target_pairs={{0,1},{1,0},{2,3},{3,2},{4,5},{5,4},{6,7},{7,6},{8,9},{9,8},{10,11... | collective-permute-start | bytes 983048 | tf_op jit(solution)/shard_map/ppermute | solution.py:69
  88.5 2.8 %result.6 = (bf16[320,10240]{1,0:T(8,128)(2,1)}, f32[64,10240]{1,0:T(8,128)}, f32[8,128]{1,0:T(8,128)}) custom-call(f32[64,64]{1,0:T(8,128)S(1)} %get-tuple-element.57.after_ref.solve_ref, f32[64,320]{1,0:T(8,128)S(1)} %get-tuple-element.58.p_ref, bf16[320,10240]{1,0:T(8,128)(2,1)S(1)} %get-tuple-element.40.m_ref, ...), custom_call_target="tpu_custom_call", output_to_operand_aliasing={{0}: (5, {}), {1}: (6, {})} | custom-call | flops 8589934592 | bytes 1048576 | tf_op jit(solution)/shard_map/result/pallas_call | solution.py:493
  91.3 2.2 %result.7 = (bf16[320,10240]{1,0:T(8,128)(2,1)}, f32[64,10240]{1,0:T(8,128)}, f32[8,128]{1,0:T(8,128)S(1)}) custom-call(f32[64,64]{1,0:T(8,128)S(1)} %get-tuple-element.57.after_ref.solve_ref, f32[64,320]{1,0:T(8,128)S(1)} %get-tuple-element.58.p_ref, bf16[320,10240]{1,0:T(8,128)(2,1)S(1)} %get-tuple-element.40.m_ref, ...), custom_call_target="tpu_custom_call", output_to_operand_aliasing={{0}: (5, {}), {1}: (6, {})} | custom-call | flops 8589934592 | bytes 1048576 | tf_op jit(solution)/shard_map/result/pallas_call | solution.py:493
  93.5 0.0 collective-permute-done.24.low_ref
  93.5 0.6 collective-permute-start.28
  94.1 2.2 %result.8 = (bf16[320,10240]{1,0:T(8,128)(2,1)}, f32[64,10240]{1,0:T(8,128)}, f32[8,128]{1,0:T(8,128)}) custom-call(f32[64,64]{1,0:T(8,128)S(1)} %get-tuple-element.57.after_ref.solve_ref, f32[64,320]{1,0:T(8,128)S(1)} %get-tuple-element.58.p_ref, bf16[320,10240]{1,0:T(8,128)(2,1)S(1)} %get-tuple-element.40.m_ref, ...), custom_call_target="tpu_custom_call", output_to_operand_aliasing={{0}: (4, {}), {1}: (5, {})} | custom-call | flops 8589934592 | bytes 1048576 | tf_op jit(solution)/shard_map/result/pallas_call | solution.py:493
  96.3 2.2 %result.9 = (bf16[320,10240]{1,0:T(8,128)(2,1)}, f32[64,10240]{1,0:T(8,128)}, f32[8,128]{1,0:T(8,128)}, f32[64,320]{1,0:T(8,128)}) custom-call(f32[64,64]{1,0:T(8,128)S(1)} %get-tuple-element.57.after_ref.solve_ref, f32[64,320]{1,0:T(8,128)S(1)} %get-tuple-element.58.p_ref, ...), custom_call_target="tpu_custom_call", output_to_operand_aliasing={{0}: (4, {}), {1}: (5, {})} | custom-call | flops 8589934592 | bytes 1048576 | tf_op jit(solution)/shard_map/result/pallas_call | solution.py:493
  (16 shorter events, 0.2 us)
Async XLA Ops:
  6.8 6.6 %collective-permute-start.2 = (f32[160,128]{1,0:T(8,128)S(1)}, f32[160,128]{1,0:T(8,128)S(1)}, u32[]{:S(2)}, u32[]{:S(2)}) collective-permute-start(f32[160,128]{1,0:T(8,128)S(1)} %get-tuple-element.39), channel_id=1, source_target_pairs={{0,16},{1,65},{2,18},{3,67},{4,20},{5,69},{6,22},{7,71},{8,24},{9,... | collective-permute-start | bytes 245768 | tf_op jit(solution)/shard_map/ppermute | solution.py:59
  11.3 3.7 %collective-permute-start.1 = (f32[160,128]{1,0:T(8,128)S(1)}, f32[160,128]{1,0:T(8,128)S(1)}, u32[]{:S(2)}, u32[]{:S(2)}) collective-permute-start(f32[160,128]{1,0:T(8,128)S(1)} %get-tuple-element.39), channel_id=1, source_target_pairs={{0,24},{1,97},{2,26},{3,99},{4,28},{5,101},{6,30},{7,103},{8,0},{9... | collective-permute-start | bytes 245768 | tf_op jit(solution)/shard_map/ppermute | solution.py:59
  11.7 4.5 %collective-permute-start = (f32[160,128]{1,0:T(8,128)S(1)}, f32[160,128]{1,0:T(8,128)S(1)}, u32[]{:S(2)}, u32[]{:S(2)}) collective-permute-start(f32[160,128]{1,0:T(8,128)S(1)} %get-tuple-element.39), channel_id=1, source_target_pairs={{0,8},{1,33},{2,10},{3,35},{4,12},{5,37},{6,14},{7,39},{8,16},{9,4... | collective-permute-start | bytes 245768 | tf_op jit(solution)/shard_map/ppermute | solution.py:59
  16.2 4.9 %collective-permute-start.5 = (f32[160,128]{1,0:T(8,128)S(1)}, f32[160,128]{1,0:T(8,128)S(1)}, u32[]{:S(2)}, u32[]{:S(2)}) collective-permute-start(f32[160,128]{1,0:T(8,128)S(1)} %add_add_fusion.a_ref), channel_id=1, source_target_pairs={{0,64},{1,17},{2,66},{3,19},{4,68},{5,21},{6,70},{7,23},{8,72},{9,... | collective-permute-start | bytes 245768 | tf_op jit(solution)/shard_map/ppermute | solution.py:59
  19.1 3.3 %collective-permute-start.4 = (f32[160,128]{1,0:T(8,128)S(1)}, f32[160,128]{1,0:T(8,128)S(1)}, u32[]{:S(2)}, u32[]{:S(2)}) collective-permute-start(f32[160,128]{1,0:T(8,128)S(1)} %add_add_fusion.a_ref), channel_id=1, source_target_pairs={{0,96},{1,25},{2,98},{3,27},{4,100},{5,29},{6,102},{7,31},{8,104},... | collective-permute-start | bytes 245768 | tf_op jit(solution)/shard_map/ppermute | solution.py:59
  19.9 4.5 %collective-permute-start.3 = (f32[160,128]{1,0:T(8,128)S(1)}, f32[160,128]{1,0:T(8,128)S(1)}, u32[]{:S(2)}, u32[]{:S(2)}) collective-permute-start(f32[160,128]{1,0:T(8,128)S(1)} %add_add_fusion.a_ref), channel_id=1, source_target_pairs={{0,32},{1,9},{2,34},{3,11},{4,36},{5,13},{6,38},{7,15},{8,40},{9,1... | collective-permute-start | bytes 245768 | tf_op jit(solution)/shard_map/ppermute | solution.py:59
  25.1 5.6 %collective-permute-start.6 = (f32[680,128]{1,0:T(8,128)S(1)}, f32[680,128]{1,0:T(8,128)S(1)}, u32[]{:S(2)}, u32[]{:S(2)}) collective-permute-start(f32[680,128]{1,0:T(8,128)S(1)} %get-tuple-element.43), channel_id=1, source_target_pairs={{0,1},{1,0},{2,3},{3,2},{4,5},{5,4},{6,7},{7,6},{8,9},{9,8},{10,11... | collective-permute-start | bytes 1044488 | tf_op jit(solution)/shard_map/ppermute | solution.py:69
  30.2 6.4 %collective-permute-start.7 = (f32[1920,128]{1,0:T(8,128)S(1)}, f32[1920,128]{1,0:T(8,128)S(1)}, u32[]{:S(2)}, u32[]{:S(2)}) collective-permute-start(f32[1920,128]{1,0:T(8,128)S(1)} %next_right.3.after_ref), channel_id=1, source_target_pairs={{0,1},{1,0},{2,3},{3,2},{4,5},{5,4},{6,7},{7,6},{8,9},{9,8},{10,11... | collective-permute-start | bytes 2949128 | tf_op jit(solution)/shard_map/ppermute | solution.py:69
  30.8 5.7 %collective-permute-start.8 = (f32[320,128]{1,0:T(8,128)S(1)}, f32[320,128]{1,0:T(8,128)S(1)}, u32[]{:S(2)}, u32[]{:S(2)}) collective-permute-start(f32[320,128]{1,0:T(8,128)S(1)} %get-tuple-element.45), channel_id=1, source_target_pairs={{0,8},{1,33},{2,10},{3,35},{4,12},{5,37},{6,14},{7,39},{8,16},{9,4... | collective-permute-start | bytes 491528 | tf_op jit(solution)/shard_map/ppermute | solution.py:59
  30.9 5.7 %collective-permute-start.9 = (f32[320,128]{1,0:T(8,128)S(1)}, f32[320,128]{1,0:T(8,128)S(1)}, u32[]{:S(2)}, u32[]{:S(2)}) collective-permute-start(f32[320,128]{1,0:T(8,128)S(1)} %get-tuple-element.46), channel_id=1, source_target_pairs={{0,24},{1,97},{2,26},{3,99},{4,28},{5,101},{6,30},{7,103},{8,0},{9... | collective-permute-start | bytes 491528 | tf_op jit(solution)/shard_map/ppermute | solution.py:59
  36.8 7.5 %collective-permute-start.10 = (f32[640,128]{1,0:T(8,128)S(1)}, f32[640,128]{1,0:T(8,128)S(1)}, u32[]{:S(2)}, u32[]{:S(2)}) collective-permute-start(f32[640,128]{1,0:T(8,128)S(1)} %get-tuple-element.48), channel_id=1, source_target_pairs={{0,8},{1,33},{2,10},{3,35},{4,12},{5,37},{6,14},{7,39},{8,16},{9,4... | collective-permute-start | bytes 983048 | tf_op jit(solution)/shard_map/ppermute | solution.py:59
  36.9 7.4 %collective-permute-start.11 = (f32[640,128]{1,0:T(8,128)S(1)}, f32[640,128]{1,0:T(8,128)S(1)}, u32[]{:S(2)}, u32[]{:S(2)}) collective-permute-start(f32[640,128]{1,0:T(8,128)S(1)} %get-tuple-element.49), channel_id=1, source_target_pairs={{0,24},{1,97},{2,26},{3,99},{4,28},{5,101},{6,30},{7,103},{8,0},{9... | collective-permute-start | bytes 983048 | tf_op jit(solution)/shard_map/ppermute | solution.py:59
  44.3 4.6 %collective-permute-start.12 = (f32[160,128]{1,0:T(8,128)S(1)}, f32[160,128]{1,0:T(8,128)S(1)}, u32[]{:S(2)}, u32[]{:S(2)}) collective-permute-start(f32[160,128]{1,0:T(8,128)S(1)} %get-tuple-element.51), channel_id=1, source_target_pairs={{0,32},{1,9},{2,34},{3,11},{4,36},{5,13},{6,38},{7,15},{8,40},{9,1... | collective-permute-start | bytes 245768 | tf_op jit(solution)/shard_map/ppermute | solution.py:59
  44.4 4.9 %collective-permute-start.13 = (f32[160,128]{1,0:T(8,128)S(1)}, f32[160,128]{1,0:T(8,128)S(1)}, u32[]{:S(2)}, u32[]{:S(2)}) collective-permute-start(f32[160,128]{1,0:T(8,128)S(1)} %get-tuple-element.52), channel_id=1, source_target_pairs={{0,96},{1,25},{2,98},{3,27},{4,100},{5,29},{6,102},{7,31},{8,104},... | collective-permute-start | bytes 245768 | tf_op jit(solution)/shard_map/ppermute | solution.py:59
  47.1 4.8 %collective-permute-start.14 = (f32[160,128]{1,0:T(8,128)S(1)}, f32[160,128]{1,0:T(8,128)S(1)}, u32[]{:S(2)}, u32[]{:S(2)}) collective-permute-start(f32[160,128]{1,0:T(8,128)S(1)} %get-tuple-element.53), channel_id=1, source_target_pairs={{0,64},{1,17},{2,66},{3,19},{4,68},{5,21},{6,70},{7,23},{8,72},{9,... | collective-permute-start | bytes 245768 | tf_op jit(solution)/shard_map/ppermute | solution.py:59
  51.9 5.1 %collective-permute-start.17 = (f32[200,128]{1,0:T(8,128)S(1)}, f32[200,128]{1,0:T(8,128)S(1)}, u32[]{:S(2)}, u32[]{:S(2)}) collective-permute-start(f32[200,128]{1,0:T(8,128)S(1)} %add_parts.1.a_ref), channel_id=1, source_target_pairs={{0,4},{2,6},{4,0},{6,2},{1,5},{3,7},{5,1},{7,3},{8,12},{10,14},{12... | collective-permute-start | bytes 307208 | tf_op jit(solution)/shard_map/ppermute | solution.py:65
  54.9 3.5 %collective-permute-start.16 = (f32[200,128]{1,0:T(8,128)S(1)}, f32[200,128]{1,0:T(8,128)S(1)}, u32[]{:S(2)}, u32[]{:S(2)}) collective-permute-start(f32[200,128]{1,0:T(8,128)S(1)} %add_parts.1.a_ref), channel_id=1, source_target_pairs={{0,6},{2,0},{4,2},{6,4},{1,7},{3,1},{5,3},{7,5},{8,14},{10,8},{12,... | collective-permute-start | bytes 307208 | tf_op jit(solution)/shard_map/ppermute | solution.py:65
  55.7 6.0 %collective-permute-start.15 = (f32[200,128]{1,0:T(8,128)S(1)}, f32[200,128]{1,0:T(8,128)S(1)}, u32[]{:S(2)}, u32[]{:S(2)}) collective-permute-start(f32[200,128]{1,0:T(8,128)S(1)} %add_parts.1.a_ref), channel_id=1, source_target_pairs={{0,2},{2,4},{4,6},{6,0},{1,3},{3,5},{5,7},{7,1},{8,10},{10,12},{12... | collective-permute-start | bytes 307208 | tf_op jit(solution)/shard_map/ppermute | solution.py:65
  61.8 4.9 %collective-permute-start.20 = (f32[160,128]{1,0:T(8,128)S(1)}, f32[160,128]{1,0:T(8,128)S(1)}, u32[]{:S(2)}, u32[]{:S(2)}) collective-permute-start(f32[160,128]{1,0:T(8,128)S(1)} %get-tuple-element.59.a_ref), channel_id=1, source_target_pairs={{0,64},{1,17},{2,66},{3,19},{4,68},{5,21},{6,70},{7,23},{8,72},{9,... | collective-permute-start | bytes 245768 | tf_op jit(solution)/shard_map/ppermute | solution.py:59
  61.9 4.8 %collective-permute-start.19 = (f32[160,128]{1,0:T(8,128)S(1)}, f32[160,128]{1,0:T(8,128)S(1)}, u32[]{:S(2)}, u32[]{:S(2)}) collective-permute-start(f32[160,128]{1,0:T(8,128)S(1)} %get-tuple-element.59.a_ref), channel_id=1, source_target_pairs={{0,96},{1,25},{2,98},{3,27},{4,100},{5,29},{6,102},{7,31},{8,104},... | collective-permute-start | bytes 245768 | tf_op jit(solution)/shard_map/ppermute | solution.py:59
  62.0 5.6 %collective-permute-start.18 = (f32[160,128]{1,0:T(8,128)S(1)}, f32[160,128]{1,0:T(8,128)S(1)}, u32[]{:S(2)}, u32[]{:S(2)}) collective-permute-start(f32[160,128]{1,0:T(8,128)S(1)} %get-tuple-element.59.a_ref), channel_id=1, source_target_pairs={{0,32},{1,9},{2,34},{3,11},{4,36},{5,13},{6,38},{7,15},{8,40},{9,1... | collective-permute-start | bytes 245768 | tf_op jit(solution)/shard_map/ppermute | solution.py:59
  67.6 7.4 %collective-permute-start.23 = (f32[640,128]{1,0:T(8,128)S(1)}, f32[640,128]{1,0:T(8,128)S(1)}, u32[]{:S(2)}, u32[]{:S(2)}) collective-permute-start(f32[640,128]{1,0:T(8,128)S(1)} %assemble.1.refs_0_), channel_id=1, source_target_pairs={{0,1},{1,0},{2,3},{3,2},{4,5},{5,4},{6,7},{7,6},{8,9},{9,8},{10,11... | collective-permute-start | bytes 983048 | tf_op jit(solution)/shard_map/ppermute | solution.py:69
  73.5 6.2 %collective-permute-start.22 = (f32[640,128]{1,0:T(8,128)S(1)}, f32[640,128]{1,0:T(8,128)S(1)}, u32[]{:S(2)}, u32[]{:S(2)}) collective-permute-start(f32[640,128]{1,0:T(8,128)S(1)} %assemble.1.refs_0_), channel_id=1, source_target_pairs={{0,24},{1,97},{2,26},{3,99},{4,28},{5,101},{6,30},{7,103},{8,0},{9... | collective-permute-start | bytes 983048 | tf_op jit(solution)/shard_map/ppermute | solution.py:59
  74.6 7.4 %collective-permute-start.21 = (f32[640,128]{1,0:T(8,128)S(1)}, f32[640,128]{1,0:T(8,128)S(1)}, u32[]{:S(2)}, u32[]{:S(2)}) collective-permute-start(f32[640,128]{1,0:T(8,128)S(1)} %assemble.1.refs_0_), channel_id=1, source_target_pairs={{0,8},{1,33},{2,10},{3,35},{4,12},{5,37},{6,14},{7,39},{8,16},{9,4... | collective-permute-start | bytes 983048 | tf_op jit(solution)/shard_map/ppermute | solution.py:59
  82.0 11.5 %collective-permute-start.24 = (f32[320,128]{1,0:T(8,128)S(1)}, f32[320,128]{1,0:T(8,128)S(1)}, u32[]{:S(2)}, u32[]{:S(2)}) collective-permute-start(f32[320,128]{1,0:T(8,128)S(1)} %get-tuple-element.61), channel_id=1, source_target_pairs={{0,8},{1,33},{2,10},{3,35},{4,12},{5,37},{6,14},{7,39},{8,16},{9,4... | collective-permute-start | bytes 491528 | tf_op jit(solution)/shard_map/ppermute | solution.py:59
  82.1 11.4 %collective-permute-start.25 = (f32[320,128]{1,0:T(8,128)S(1)}, f32[320,128]{1,0:T(8,128)S(1)}, u32[]{:S(2)}, u32[]{:S(2)}) collective-permute-start(f32[320,128]{1,0:T(8,128)S(1)} %get-tuple-element.62), channel_id=1, source_target_pairs={{0,24},{1,97},{2,26},{3,99},{4,28},{5,101},{6,30},{7,103},{8,0},{9... | collective-permute-start | bytes 491528 | tf_op jit(solution)/shard_map/ppermute | solution.py:59
  84.8 6.5 %collective-permute-start.26 = (f32[640,128]{1,0:T(8,128)S(1)}, f32[640,128]{1,0:T(8,128)S(1)}, u32[]{:S(2)}, u32[]{:S(2)}) collective-permute-start(f32[640,128]{1,0:T(8,128)S(1)} %tie.2.refs_0_), channel_id=1, source_target_pairs={{0,1},{1,0},{2,3},{3,2},{4,5},{5,4},{6,7},{7,6},{8,9},{9,8},{10,11... | collective-permute-start | bytes 983048 | tf_op jit(solution)/shard_map/ppermute | solution.py:69
  88.5 2.8 %collective-permute-start.27 = (f32[640,128]{1,0:T(8,128)S(1)}, f32[640,128]{1,0:T(8,128)S(1)}, u32[]{:S(2)}, u32[]{:S(2)}) collective-permute-start(f32[640,128]{1,0:T(8,128)S(1)} %tie.3.refs_1_), channel_id=1, source_target_pairs={{0,1},{1,0},{2,3},{3,2},{4,5},{5,4},{6,7},{7,6},{8,9},{9,8},{10,11... | collective-permute-start | bytes 983048 | tf_op jit(solution)/shard_map/ppermute | solution.py:69
  93.5 2.8 %collective-permute-start.28 = (f32[640,128]{1,0:T(8,128)S(1)}, f32[640,128]{1,0:T(8,128)S(1)}, u32[]{:S(2)}, u32[]{:S(2)}) collective-permute-start(f32[640,128]{1,0:T(8,128)S(1)} %join.1.refs_0_), channel_id=1, source_target_pairs={{0,1},{1,0},{2,3},{3,2},{4,5},{5,4},{6,7},{7,6},{8,9},{9,8},{10,11... | collective-permute-start | bytes 983048 | tf_op jit(solution)/shard_map/ppermute | solution.py:69

commit v9 on v8

--- a/solution.py
+++ b/solution.py
@@ -229,10 +229,9 @@
     )(pieces, merged, after)
 
 
-def first_pair_kernel(kept_ref, got_ref, ext_ref, low_ref, high_ref, pair_ref, weight_ref):
+def first_pair_kernel(kept_ref, got_ref, ext_ref, out_ref, pair_ref, weight_ref):
     grams = ext_ref.shape[0] - ROWS
     size = kept_ref.shape[0]
-    half = size // 2
     own, its = ext_ref[grams : grams + 1, :1], got_ref[size + grams : size + grams + 1, :1]
     top = jnp.maximum(own, its)
     pair_ref[:grams] = ext_ref[:grams] + got_ref[size : size + grams]
@@ -240,54 +239,49 @@
     own, its = own / top, its / top
     weight_ref[:ROWS] = jnp.broadcast_to(own, (ROWS, 128))
     weight_ref[ROWS:] = jnp.broadcast_to(its, (ROWS, 128))
-    low_ref[...] = kept_ref[:half] * own + got_ref[:half] * its
-    high_ref[...] = kept_ref[half:] * own + got_ref[half:size] * its
+    out_ref[...] = kept_ref[...] * own + got_ref[:size] * its
 
 
 def first_pair(kept, got, ext):
-    half = jax.ShapeDtypeStruct((kept.shape[0] // 2, 128), F32)
     return pl.pallas_call(
         first_pair_kernel,
-        out_shape=[half, half, pltpu.VMEM(ext.shape, F32), pltpu.VMEM((2 * ROWS, 128), F32)],
+        out_shape=[
+            jax.ShapeDtypeStruct(kept.shape, F32),
+            pltpu.VMEM(ext.shape, F32),
+            pltpu.VMEM((2 * ROWS, 128), F32),
+        ],
         in_specs=[WHOLE] * 3,
-        out_specs=[WHOLE] * 4,
+        out_specs=[WHOLE] * 3,
         compiler_params=params(8),
         name="first_pair",
     )(kept, got, ext)
 
 
-def next_pair_kernel(kept_ref, got_ref, weight_ref, low_ref, high_ref, *out):
+def next_pair_kernel(kept_ref, got_ref, weight_ref, *out):
     own, its = weight_ref[:1, :1], weight_ref[ROWS : ROWS + 1, :1]
     size = out[0].shape[0]
-    half = size // 2
     for n, ref in enumerate(out):
-        for part in (0, 1):
-            at = slice(n * size + part * half, n * size + (part + 1) * half)
-            x = kept_ref[at] * own + got_ref[at] * its
-            if (n, part) == (0, 0):
-                x = x + low_ref[...]
-            if (n, part) == (1, 1):
-                x = x + high_ref[...]
-            ref[part * half : (part + 1) * half] = x
-
-
-def next_pair(kept, got, weight, low, high):
+        at = slice(n * size, (n + 1) * size)
+        ref[...] = kept_ref[at] * own + got_ref[at] * its
+
+
+def next_pair(kept, got, weight):
     size = kept.shape[0] // 3
     return pl.pallas_call(
         next_pair_kernel,
         out_shape=[jax.ShapeDtypeStruct((size, 128), F32)] * 3,
-        in_specs=[WHOLE] * 5,
+        in_specs=[WHOLE] * 3,
         out_specs=[WHOLE] * 3,
         compiler_params=params(8),
         name="next_pair",
-    )(kept, got, weight, low, high)
-
-
-def add_quarters_kernel(a_ref, b_ref, c_ref, *out):
+    )(kept, got, weight)
+
+
+def add_quarters_kernel(a_ref, b_ref, c_ref, d_ref, *out):
     size = a_ref.shape[0] // QUARTERS
     for k, ref in zip((0,) + SHIFTS, out):
         at = pl.ds(pl.multiple_of((place()[2] + k) % QUARTERS * size, size), size)
-        ref[...] = a_ref[at] + (b_ref[at] + c_ref[at])
+        ref[...] = (a_ref[at] + b_ref[at]) + (c_ref[at] + d_ref[at])
 
 
 def add_quarters(parts):
@@ -295,7 +289,7 @@
     return pl.pallas_call(
         add_quarters_kernel,
         out_shape=[jax.ShapeDtypeStruct((size, 128), F32)] * QUARTERS,
-        in_specs=[WHOLE] * 3,
+        in_specs=[WHOLE] * QUARTERS,
         out_specs=[WHOLE] * QUARTERS,
         compiler_params=params(8),
         name="add_quarters",
@@ -512,42 +506,6 @@
     )(solve, p_hat, merged, *totals, *held)
 
 
-def halves_kernel(a_ref, b_ref, after_ref, low_ref, high_ref):
-    del after_ref
-    half = low_ref.shape[0]
-    low_ref[...] = a_ref[:half]
-    high_ref[...] = b_ref[half:]
-
-
-def halves(a, b, after):
-    return pl.pallas_call(
-        halves_kernel,
-        out_shape=[jax.ShapeDtypeStruct((a.shape[0] // 2, 128), F32)] * 2,
-        in_specs=[WHOLE, WHOLE, ANY],
-        out_specs=[WHOLE, WHOLE],
-        compiler_params=params(4),
-        name="halves",
-    )(a, b, after)
-
-
-def join_kernel(low_ref, high_ref, after_ref, out_ref):
-    del after_ref
-    half = low_ref.shape[0]
-    out_ref[:half] = low_ref[...]
-    out_ref[half:] = high_ref[...]
-
-
-def join(low, high, after):
-    return pl.pallas_call(
-        join_kernel,
-        out_shape=jax.ShapeDtypeStruct((low.shape[0] * 2, 128), F32),
-        in_specs=[WHOLE, WHOLE, ANY],
-        out_specs=WHOLE,
-        compiler_params=params(4),
-        name="join",
-    )(low, high, after)
-
-
 def tie_kernel(value_ref, after_ref, out_ref):
     del value_ref, after_ref, out_ref
 
@@ -577,28 +535,26 @@
     sent = next_right(False, (1, 3, 0), pieces, merged, ext)
     got_next = swap(sent)
     kept = next_right(True, (2,), pieces, merged, sent)
-    low, high, ext, weight = first_pair(kept, got, ext)
+    two, ext, weight = first_pair(kept, got, ext)
+    (two,) = ring_x_or_z((two,), 0, (2,))
     kept = next_right(True, (1, 3, 0), pieces, merged, weight)
-    low, high = ring_x_or_z((low, high), 0, (1, 3))
-    up, down, own = next_pair(kept, got_next, weight, low, high)
-    own, *sent = add_quarters((own, *ring_x_or_z((up, down), 0, (1, 3))))
+    *near, own = next_pair(kept, got_next, weight)
+    own, *sent = add_quarters((own, *ring_x_or_z(near, 0, (1, 3)), two))
     part = add_parts((own, *ring_x_or_z(sent, 1)), ext)
     total, ext = across((part, *ring_y(part)), ext.shape[0])
     solve, p_hat = factor(ext, p_mean, replicas)
     total = assemble((total, *ring_x_or_z([total] * 3, 1)), solve)
-    one, three = ring_x_or_z([total] * 2, 0, (1, 3))
-
-    def write(sources, totals, before, last=False):
+    others = ring_x_or_z([total] * 3, 0)
+
+    def write(own, turns, totals, before, last=False):
+        sources = tuple((own, k) for k in turns)
         return result(sources, last, totals, merged, solve, p_hat, before)
 
-    *out, token = write(((True, 0), (False, 0)), (total, swap(total)), None)
-    low, high = ring_x_or_z(halves(one, three, token), 0, (1, 3))
-    one, three = tie(one, token), tie(three, token)
-    *out, _ = write(((True, 1), (True, 3)), (one, three), out)
-    *out, token = write(((False, 1), (False, 3)), (swap(one), swap(three)), out)
-    two = join(low, high, token)
-    *out, _ = write(((True, 2),), (two,), out)
-    new_error, q_new, _, p_hat = write(((False, 2),), (swap(two),), out, True)
+    *out, token = write(True, (0,), (total,), None)
+    *out, token = write(False, (0,), (swap(total),), out)
+    others = [tie(a, token) for a in others]
+    *out, _ = write(True, SHIFTS, others, out)
+    new_error, q_new, _, p_hat = write(False, SHIFTS, [swap(a) for a in others], out, True)
     return (new_error[None], p_hat, q_new)
 
 

time: 98.8 us -> 90.2 us (0.913)
  waiting for transfers between devices: 31.3 us -> 27.3 us
  starting transfers between devices: 43.3 us -> 39.8 us
  Pallas kernels: 23 us -> 22 us
    ppermute x20 -> x18, starting transfers between devices: 24.3 us -> 21.4 us  [ring_x_or_z(): out.append(lax.ppermute(value, AXES, pairs))]
    ppermute x20 -> x18, waiting for transfers between devices: 26 us -> 23.8 us  [ring_x_or_z(): out.append(lax.ppermute(value, AXES, pairs))]
    ppermute x3, waiting for transfers between devices: 5.32 us -> 3.52 us  [ring_y(): lax.ppermute(value, 'y', [(i, (i + k) % n) for i in range(n)])]
    pallas_call x5 -> x4, Pallas kernels: 11.5 us -> 10.4 us  [result(): pl.pallas_call(functools.partial(result_kernel, sources, last, quarter //...]
  transfers between devices with their start and end apart: 29 -> 27, of which waited for: 18 -> 15; matrix products, arithmetic and copies ran while one was open for 0% -> 0% of each run, Pallas kernels for 14% -> 13%
where the time goes in v9:
time: 90.2 us; the launch traced here: 90.1 us
  starting transfers between devices  39.8 us (44%)
  waiting for transfers between devices  27.3 us (30%)
  Pallas kernels  22 us (24%)
  between operations  0.98 us (1%)
    ppermute x18, waiting for transfers between devices, ring_x_or_z(): out.append(lax.ppermute(value, AXES, pairs))  23.8 us
    ppermute x18, starting transfers between devices, ring_x_or_z(): out.append(lax.ppermute(value, AXES, pairs))  21.4 us
    ppermute x6, starting transfers between devices, swap(): return lax.ppermute(value, 'c', [(0, 1), (1, 0)])  14 us
    pallas_call x4, Pallas kernels, result(): pl.pallas_call(functools.partial(result_kernel, sources, last, quarter //...  10.4 us
    pallas_call x1, Pallas kernels, merge(): pl.pallas_call(functools.partial(merge_kernel, width), out_shape=[pltpu.V...  6.14 us
    ppermute x3, starting transfers between devices, ring_y(): lax.ppermute(value, 'y', [(i, (i + k) % n) for i in range(n)])  4.44 us
    ppermute x3, waiting for transfers between devices, ring_y(): lax.ppermute(value, 'y', [(i, (i + k) % n) for i in range(n)])  3.52 us
    pallas_call x3, Pallas kernels, next_right(): pl.pallas_call(functools.partial(next_right_kernel, own, turns), out_shap...  2.25 us
  transfers between devices with their start and end apart: 27, of which 15 were waited for; matrix products, arithmetic and copies ran while one was open for 0% of the time, Pallas kernels for 13%

profile of v9, /device:TPU:1, one launch (start us, length us, event | category | flops | bytes accessed | tf_op | source)
XLA Modules:
  0.0 90.1 jit_solution(12743053818496993754)
XLA Ops:
  0.6 6.1 %merge.1 = (bf16[320,10240]{1,0:T(8,128)(2,1)S(1)}, f32[160,128]{1,0:T(8,128)S(1)}) custom-call(bf16[320,10240]{1,0:T(8,128)(2,1)} %bitcast.3, bf16[320,10240]{1,0:T(8,128)(2,1)} %bitcast.4, bf16[64,10240]{1,0:T(8,128)(2,1)} %q_hbm.1), custom_call_target="tpu_custom_call" | custom-call | flops 419430400 | bytes 13107200 | tf_op jit(solution)/shard_map/merge/pallas_call | solution.py:125
  6.8 2.5 %collective-permute-start = (f32[160,128]{1,0:T(8,128)S(1)}, f32[160,128]{1,0:T(8,128)S(1)}, u32[]{:S(2)}, u32[]{:S(2)}) collective-permute-start(f32[160,128]{1,0:T(8,128)S(1)} %get-tuple-element.33), channel_id=1, source_target_pairs={{0,8},{1,33},{2,10},{3,35},{4,12},{5,37},{6,14},{7,39},{8,16},{9,4... | collective-permute-start | bytes 245768 | tf_op jit(solution)/shard_map/ppermute | solution.py:59
  9.3 2.2 %collective-permute-start.1 = (f32[160,128]{1,0:T(8,128)S(1)}, f32[160,128]{1,0:T(8,128)S(1)}, u32[]{:S(2)}, u32[]{:S(2)}) collective-permute-start(f32[160,128]{1,0:T(8,128)S(1)} %get-tuple-element.33), channel_id=1, source_target_pairs={{0,24},{1,97},{2,26},{3,99},{4,28},{5,101},{6,30},{7,103},{8,0},{9... | collective-permute-start | bytes 245768 | tf_op jit(solution)/shard_map/ppermute | solution.py:59
  11.5 1.2 %collective-permute-start.2 = (f32[160,128]{1,0:T(8,128)S(1)}, f32[160,128]{1,0:T(8,128)S(1)}, u32[]{:S(2)}, u32[]{:S(2)}) collective-permute-start(f32[160,128]{1,0:T(8,128)S(1)} %get-tuple-element.33), channel_id=1, source_target_pairs={{0,16},{1,65},{2,18},{3,67},{4,20},{5,69},{6,22},{7,71},{8,24},{9,... | collective-permute-start | bytes 245768 | tf_op jit(solution)/shard_map/ppermute | solution.py:59
  12.7 0.8 collective-permute-done
  13.5 0.0 collective-permute-done.1
  13.5 3.1 %collective-permute-done.2 = f32[160,128]{1,0:T(8,128)S(1)} collective-permute-done((f32[160,128]{1,0:T(8,128)S(1)}, f32[160,128]{1,0:T(8,128)S(1)}, u32[]{:S(2)}, u32[]{:S(2)}) %collective-permute-start.2) | collective-permute-done | bytes 81952 | tf_op jit(solution)/shard_map/ppermute | solution.py:59
  16.6 1.0 %collective-permute-start.3 = (f32[160,128]{1,0:T(8,128)S(1)}, f32[160,128]{1,0:T(8,128)S(1)}, u32[]{:S(2)}, u32[]{:S(2)}) collective-permute-start(f32[160,128]{1,0:T(8,128)S(1)} %add_add_fusion.a_ref), channel_id=1, source_target_pairs={{0,32},{1,9},{2,34},{3,11},{4,36},{5,13},{6,38},{7,15},{8,40},{9,1... | collective-permute-start | bytes 245768 | tf_op jit(solution)/shard_map/ppermute | solution.py:59
  17.6 1.8 %collective-permute-start.4 = (f32[160,128]{1,0:T(8,128)S(1)}, f32[160,128]{1,0:T(8,128)S(1)}, u32[]{:S(2)}, u32[]{:S(2)}) collective-permute-start(f32[160,128]{1,0:T(8,128)S(1)} %add_add_fusion.a_ref), channel_id=1, source_target_pairs={{0,96},{1,25},{2,98},{3,27},{4,100},{5,29},{6,102},{7,31},{8,104},... | collective-permute-start | bytes 245768 | tf_op jit(solution)/shard_map/ppermute | solution.py:59
  19.4 1.2 %collective-permute-start.5 = (f32[160,128]{1,0:T(8,128)S(1)}, f32[160,128]{1,0:T(8,128)S(1)}, u32[]{:S(2)}, u32[]{:S(2)}) collective-permute-start(f32[160,128]{1,0:T(8,128)S(1)} %add_add_fusion.a_ref), channel_id=1, source_target_pairs={{0,64},{1,17},{2,66},{3,19},{4,68},{5,21},{6,70},{7,23},{8,72},{9,... | collective-permute-start | bytes 245768 | tf_op jit(solution)/shard_map/ppermute | solution.py:59
  20.6 0.6 collective-permute-done.3.b_ref
  21.2 0.0 collective-permute-done.4.c_ref
  21.2 3.0 %collective-permute-done.5.d_ref = f32[160,128]{1,0:T(8,128)S(1)} collective-permute-done((f32[160,128]{1,0:T(8,128)S(1)}, f32[160,128]{1,0:T(8,128)S(1)}, u32[]{:S(2)}, u32[]{:S(2)}) %collective-permute-start.5) | collective-permute-done | bytes 81952 | tf_op jit(solution)/shard_map/ppermute | solution.py:59
  24.2 0.7 first_right.1
  24.9 3.5 %collective-permute-start.6 = (f32[680,128]{1,0:T(8,128)S(1)}, f32[680,128]{1,0:T(8,128)S(1)}, u32[]{:S(2)}, u32[]{:S(2)}) collective-permute-start(f32[680,128]{1,0:T(8,128)S(1)} %get-tuple-element.37), channel_id=1, source_target_pairs={{0,1},{1,0},{2,3},{3,2},{4,5},{5,4},{6,7},{7,6},{8,9},{9,8},{10,11... | collective-permute-start | bytes 1044488 | tf_op jit(solution)/shard_map/ppermute | solution.py:69
  28.4 0.9 %next_right.3.after_ref = f32[1920,128]{1,0:T(8,128)S(1)} custom-call(bf16[192,320]{1,0:T(8,128)(2,1)S(1)} %get-tuple-element.35.pieces_ref, bf16[320,10240]{1,0:T(8,128)(2,1)S(1)} %get-tuple-element.34.m_ref, f32[40,128]{1,0:T(8,128)S(1)} %get-tuple-element.36.after_ref.ext_ref), custom_call_target="tpu_custom_call" | custom-call | flops 8589934592 | bytes 1048576 | tf_op jit(solution)/shard_map/next_right/pallas_call | solution.py:221
  29.3 0.1 collective-permute-start.7
  29.5 0.4 next_right.4.kept_ref
  29.9 0.0 collective-permute-done.6.got_ref
  29.9 0.1 first_pair.1
  30.0 1.6 %collective-permute-start.10 = (f32[640,128]{1,0:T(8,128)S(1)}, f32[640,128]{1,0:T(8,128)S(1)}, u32[]{:S(2)}, u32[]{:S(2)}) collective-permute-start(f32[640,128]{1,0:T(8,128)S(1)} %get-tuple-element.42), channel_id=1, source_target_pairs={{0,16},{1,65},{2,18},{3,67},{4,20},{5,69},{6,22},{7,71},{8,24},{9,... | collective-permute-start | bytes 983048 | tf_op jit(solution)/shard_map/ppermute | solution.py:59
  31.6 0.9 %next_right.5.kept_ref = f32[1920,128]{1,0:T(8,128)S(1)} custom-call(bf16[192,320]{1,0:T(8,128)(2,1)S(1)} %get-tuple-element.35.pieces_ref, bf16[320,10240]{1,0:T(8,128)(2,1)S(1)} %get-tuple-element.34.m_ref, f32[16,128]{1,0:T(8,128)S(1)} %get-tuple-element.38.after_ref.weight_ref), custom_call_target="tpu_custom_call" | custom-call | flops 8589934592 | bytes 1048576 | tf_op jit(solution)/shard_map/next_right/pallas_call | solution.py:221
  32.5 0.0 collective-permute-done.7.got_ref
  32.5 0.2 next_pair.1
  32.7 0.8 collective-permute-start.8
  33.5 1.9 %collective-permute-start.9 = (f32[640,128]{1,0:T(8,128)S(1)}, f32[640,128]{1,0:T(8,128)S(1)}, u32[]{:S(2)}, u32[]{:S(2)}) collective-permute-start(f32[640,128]{1,0:T(8,128)S(1)} %get-tuple-element.41), channel_id=1, source_target_pairs={{0,24},{1,97},{2,26},{3,99},{4,28},{5,101},{6,30},{7,103},{8,0},{9... | collective-permute-start | bytes 983048 | tf_op jit(solution)/shard_map/ppermute | solution.py:59
  35.5 2.3 %collective-permute-done.10.d_ref = f32[640,128]{1,0:T(8,128)S(1)} collective-permute-done((f32[640,128]{1,0:T(8,128)S(1)}, f32[640,128]{1,0:T(8,128)S(1)}, u32[]{:S(2)}, u32[]{:S(2)}) %collective-permute-start.10) | collective-permute-done | bytes 327712 | tf_op jit(solution)/shard_map/ppermute | solution.py:59
  37.8 3.5 %collective-permute-done.8.b_ref = f32[640,128]{1,0:T(8,128)S(1)} collective-permute-done((f32[640,128]{1,0:T(8,128)S(1)}, f32[640,128]{1,0:T(8,128)S(1)}, u32[]{:S(2)}, u32[]{:S(2)}) %collective-permute-start.8) | collective-permute-done | bytes 327712 | tf_op jit(solution)/shard_map/ppermute | solution.py:59
  41.3 0.1 add_quarters.1
  41.4 0.1 collective-permute-start.11
  41.5 2.7 %collective-permute-start.12 = (f32[160,128]{1,0:T(8,128)S(1)}, f32[160,128]{1,0:T(8,128)S(1)}, u32[]{:S(2)}, u32[]{:S(2)}) collective-permute-start(f32[160,128]{1,0:T(8,128)S(1)} %get-tuple-element.45), channel_id=1, source_target_pairs={{0,96},{1,25},{2,98},{3,27},{4,100},{5,29},{6,102},{7,31},{8,104},... | collective-permute-start | bytes 245768 | tf_op jit(solution)/shard_map/ppermute | solution.py:59
  44.1 0.0 collective-permute-start.13
  44.1 1.8 %collective-permute-done.11.b_ref = f32[160,128]{1,0:T(8,128)S(1)} collective-permute-done((f32[160,128]{1,0:T(8,128)S(1)}, f32[160,128]{1,0:T(8,128)S(1)}, u32[]{:S(2)}, u32[]{:S(2)}) %collective-permute-start.11) | collective-permute-done | bytes 81952 | tf_op jit(solution)/shard_map/ppermute | solution.py:59
  46.0 0.4 collective-permute-done.12.c_ref
  46.4 2.5 %collective-permute-done.13.d_ref = f32[160,128]{1,0:T(8,128)S(1)} collective-permute-done((f32[160,128]{1,0:T(8,128)S(1)}, f32[160,128]{1,0:T(8,128)S(1)}, u32[]{:S(2)}, u32[]{:S(2)}) %collective-permute-start.13) | collective-permute-done | bytes 81952 | tf_op jit(solution)/shard_map/ppermute | solution.py:59
  48.9 1.4 %collective-permute-start.14 = (f32[200,128]{1,0:T(8,128)S(1)}, f32[200,128]{1,0:T(8,128)S(1)}, u32[]{:S(2)}, u32[]{:S(2)}) collective-permute-start(f32[200,128]{1,0:T(8,128)S(1)} %add_parts.1.a_ref), channel_id=1, source_target_pairs={{0,2},{2,4},{4,6},{6,0},{1,3},{3,5},{5,7},{7,1},{8,10},{10,12},{12... | collective-permute-start | bytes 307208 | tf_op jit(solution)/shard_map/ppermute | solution.py:65
  50.3 1.5 %collective-permute-start.15 = (f32[200,128]{1,0:T(8,128)S(1)}, f32[200,128]{1,0:T(8,128)S(1)}, u32[]{:S(2)}, u32[]{:S(2)}) collective-permute-start(f32[200,128]{1,0:T(8,128)S(1)} %add_parts.1.a_ref), channel_id=1, source_target_pairs={{0,6},{2,0},{4,2},{6,4},{1,7},{3,1},{5,3},{7,5},{8,14},{10,8},{12,... | collective-permute-start | bytes 307208 | tf_op jit(solution)/shard_map/ppermute | solution.py:65
  51.8 1.6 %collective-permute-start.16 = (f32[200,128]{1,0:T(8,128)S(1)}, f32[200,128]{1,0:T(8,128)S(1)}, u32[]{:S(2)}, u32[]{:S(2)}) collective-permute-start(f32[200,128]{1,0:T(8,128)S(1)} %add_parts.1.a_ref), channel_id=1, source_target_pairs={{0,4},{2,6},{4,0},{6,2},{1,5},{3,7},{5,1},{7,3},{8,12},{10,14},{12... | collective-permute-start | bytes 307208 | tf_op jit(solution)/shard_map/ppermute | solution.py:65
  53.4 0.4 collective-permute-done.14.b_ref
  53.8 0.0 collective-permute-done.15.c_ref
  53.8 3.1 %collective-permute-done.16.d_ref = f32[200,128]{1,0:T(8,128)S(1)} collective-permute-done((f32[200,128]{1,0:T(8,128)S(1)}, f32[200,128]{1,0:T(8,128)S(1)}, u32[]{:S(2)}, u32[]{:S(2)}) %collective-permute-start.16) | collective-permute-done | bytes 102432 | tf_op jit(solution)/shard_map/ppermute | solution.py:65
  56.9 0.1 across.1
  57.0 0.3 collective-permute-start.17
  57.3 2.7 %collective-permute-start.18 = (f32[160,128]{1,0:T(8,128)S(1)}, f32[160,128]{1,0:T(8,128)S(1)}, u32[]{:S(2)}, u32[]{:S(2)}) collective-permute-start(f32[160,128]{1,0:T(8,128)S(1)} %get-tuple-element.52.a_ref), channel_id=1, source_target_pairs={{0,96},{1,25},{2,98},{3,27},{4,100},{5,29},{6,102},{7,31},{8,104},... | collective-permute-start | bytes 245768 | tf_op jit(solution)/shard_map/ppermute | solution.py:59
  59.9 1.9 %factor.1 = (f32[64,64]{1,0:T(8,128)S(1)}, f32[64,320]{1,0:T(8,128)S(1)}) custom-call(f32[40,128]{1,0:T(8,128)S(1)} %get-tuple-element.48.ext_ref, f32[64,320]{1,0:T(8,128)S(1)} %get-tuple-element.49.p_ref), custom_call_target="tpu_custom_call" | custom-call | flops 4294967296 | bytes 1048576 | tf_op jit(solution)/shard_map/factor/pallas_call | solution.py:409
  61.9 0.0 collective-permute-done.17.b_ref
  61.9 0.3 collective-permute-done.18.c_ref
  62.2 2.5 %collective-permute-done.19.d_ref = f32[160,128]{1,0:T(8,128)S(1)} collective-permute-done((f32[160,128]{1,0:T(8,128)S(1)}, f32[160,128]{1,0:T(8,128)S(1)}, u32[]{:S(2)}, u32[]{:S(2)}) %collective-permute-start.19) | collective-permute-done | bytes 81952 | tf_op jit(solution)/shard_map/ppermute | solution.py:59
  64.8 6.3 %collective-permute-start.21 = (f32[640,128]{1,0:T(8,128)S(1)}, f32[640,128]{1,0:T(8,128)S(1)}, u32[]{:S(2)}, u32[]{:S(2)}) collective-permute-start(f32[640,128]{1,0:T(8,128)S(1)} %assemble.1.refs_0_), channel_id=1, source_target_pairs={{0,1},{1,0},{2,3},{3,2},{4,5},{5,4},{6,7},{7,6},{8,9},{9,8},{10,11... | collective-permute-start | bytes 983048 | tf_op jit(solution)/shard_map/ppermute | solution.py:69
  71.1 0.0 collective-permute-start.25
  71.1 1.0 %collective-permute-start.23 = (f32[640,128]{1,0:T(8,128)S(1)}, f32[640,128]{1,0:T(8,128)S(1)}, u32[]{:S(2)}, u32[]{:S(2)}) collective-permute-start(f32[640,128]{1,0:T(8,128)S(1)} %assemble.1.refs_0_), channel_id=1, source_target_pairs={{0,24},{1,97},{2,26},{3,99},{4,28},{5,101},{6,30},{7,103},{8,0},{9... | collective-permute-start | bytes 983048 | tf_op jit(solution)/shard_map/ppermute | solution.py:59
  72.1 0.5 collective-permute-start.20
  72.6 2.2 %result.4 = (bf16[320,10240]{1,0:T(8,128)(2,1)}, f32[64,10240]{1,0:T(8,128)}, f32[8,128]{1,0:T(8,128)}) custom-call(f32[64,64]{1,0:T(8,128)S(1)} %get-tuple-element.50.after_ref.solve_ref, f32[64,320]{1,0:T(8,128)S(1)} %get-tuple-element.51.p_ref, bf16[320,10240]{1,0:T(8,128)(2,1)S(1)} %get-tuple-element.34.m_ref, f32[640,128]{1,0:T(8,128)S(1)} %assemble.1.refs_0_), custom_call_target="tpu_custom_call" | custom-call | flops 8589934592 | bytes 1048576 | tf_op jit(solution)/shard_map/result/pallas_call | solution.py:487
  74.8 1.6 %result.5 = (bf16[320,10240]{1,0:T(8,128)(2,1)}, f32[64,10240]{1,0:T(8,128)}, f32[8,128]{1,0:T(8,128)S(1)}) custom-call(f32[64,64]{1,0:T(8,128)S(1)} %get-tuple-element.50.after_ref.solve_ref, f32[64,320]{1,0:T(8,128)S(1)} %get-tuple-element.51.p_ref, bf16[320,10240]{1,0:T(8,128)(2,1)S(1)} %get-tuple-element.34.m_ref, ...), custom_call_target="tpu_custom_call", output_to_operand_aliasing={{0}: (4, {}), {1}: (5, {})} | custom-call | flops 8589934592 | bytes 1048576 | tf_op jit(solution)/shard_map/result/pallas_call | solution.py:487
  76.4 2.5 %collective-permute-done.25.value_ref = f32[640,128]{1,0:T(8,128)S(1)} collective-permute-done((f32[640,128]{1,0:T(8,128)S(1)}, f32[640,128]{1,0:T(8,128)S(1)}, u32[]{:S(2)}, u32[]{:S(2)}) %collective-permute-start.25) | collective-permute-done | bytes 327712 | tf_op jit(solution)/shard_map/ppermute | solution.py:59
  78.9 1.0 %collective-permute-start.26 = (f32[640,128]{1,0:T(8,128)S(1)}, f32[640,128]{1,0:T(8,128)S(1)}, u32[]{:S(2)}, u32[]{:S(2)}) collective-permute-start(f32[640,128]{1,0:T(8,128)S(1)} %tie.5.refs_2_), channel_id=1, source_target_pairs={{0,1},{1,0},{2,3},{3,2},{4,5},{5,4},{6,7},{7,6},{8,9},{9,8},{10,11... | collective-permute-start | bytes 983048 | tf_op jit(solution)/shard_map/ppermute | solution.py:69
  79.9 0.4 collective-permute-done.23.value_ref
  80.3 2.8 %collective-permute-start.24 = (f32[640,128]{1,0:T(8,128)S(1)}, f32[640,128]{1,0:T(8,128)S(1)}, u32[]{:S(2)}, u32[]{:S(2)}) collective-permute-start(f32[640,128]{1,0:T(8,128)S(1)} %tie.4.refs_1_), channel_id=1, source_target_pairs={{0,1},{1,0},{2,3},{3,2},{4,5},{5,4},{6,7},{7,6},{8,9},{9,8},{10,11... | collective-permute-start | bytes 983048 | tf_op jit(solution)/shard_map/ppermute | solution.py:69
  83.1 0.0 collective-permute-done.20.value_ref
  83.1 0.2 collective-permute-start.22
  83.3 3.3 %result.6 = (bf16[320,10240]{1,0:T(8,128)(2,1)}, f32[64,10240]{1,0:T(8,128)}, f32[8,128]{1,0:T(8,128)}) custom-call(f32[64,64]{1,0:T(8,128)S(1)} %get-tuple-element.50.after_ref.solve_ref, f32[64,320]{1,0:T(8,128)S(1)} %get-tuple-element.51.p_ref, bf16[320,10240]{1,0:T(8,128)(2,1)S(1)} %get-tuple-element.34.m_ref, ...), custom_call_target="tpu_custom_call", output_to_operand_aliasing={{0}: (6, {}), {1}: (7, {})} | custom-call | flops 8589934592 | bytes 1048576 | tf_op jit(solution)/shard_map/result/pallas_call | solution.py:487
  86.6 0.0 collective-permute-done.26.refs_2_
  86.6 0.0 collective-permute-done.24.refs_1_
  86.6 3.3 %result.7 = (bf16[320,10240]{1,0:T(8,128)(2,1)}, f32[64,10240]{1,0:T(8,128)}, f32[8,128]{1,0:T(8,128)}, f32[64,320]{1,0:T(8,128)}) custom-call(f32[64,64]{1,0:T(8,128)S(1)} %get-tuple-element.50.after_ref.solve_ref, f32[64,320]{1,0:T(8,128)S(1)} %get-tuple-element.51.p_ref, ...), custom_call_target="tpu_custom_call", output_to_operand_aliasing={{0}: (6, {}), {1}: (7, {})} | custom-call | flops 8589934592 | bytes 1048576 | tf_op jit(solution)/shard_map/result/pallas_call | solution.py:487
  (10 shorter events, 0.1 us)
Async XLA Ops:
  6.8 6.7 %collective-permute-start = (f32[160,128]{1,0:T(8,128)S(1)}, f32[160,128]{1,0:T(8,128)S(1)}, u32[]{:S(2)}, u32[]{:S(2)}) collective-permute-start(f32[160,128]{1,0:T(8,128)S(1)} %get-tuple-element.33), channel_id=1, source_target_pairs={{0,8},{1,33},{2,10},{3,35},{4,12},{5,37},{6,14},{7,39},{8,16},{9,4... | collective-permute-start | bytes 245768 | tf_op jit(solution)/shard_map/ppermute | solution.py:59
  9.3 4.2 %collective-permute-start.1 = (f32[160,128]{1,0:T(8,128)S(1)}, f32[160,128]{1,0:T(8,128)S(1)}, u32[]{:S(2)}, u32[]{:S(2)}) collective-permute-start(f32[160,128]{1,0:T(8,128)S(1)} %get-tuple-element.33), channel_id=1, source_target_pairs={{0,24},{1,97},{2,26},{3,99},{4,28},{5,101},{6,30},{7,103},{8,0},{9... | collective-permute-start | bytes 245768 | tf_op jit(solution)/shard_map/ppermute | solution.py:59
  11.5 5.1 %collective-permute-start.2 = (f32[160,128]{1,0:T(8,128)S(1)}, f32[160,128]{1,0:T(8,128)S(1)}, u32[]{:S(2)}, u32[]{:S(2)}) collective-permute-start(f32[160,128]{1,0:T(8,128)S(1)} %get-tuple-element.33), channel_id=1, source_target_pairs={{0,16},{1,65},{2,18},{3,67},{4,20},{5,69},{6,22},{7,71},{8,24},{9,... | collective-permute-start | bytes 245768 | tf_op jit(solution)/shard_map/ppermute | solution.py:59
  16.6 4.6 %collective-permute-start.3 = (f32[160,128]{1,0:T(8,128)S(1)}, f32[160,128]{1,0:T(8,128)S(1)}, u32[]{:S(2)}, u32[]{:S(2)}) collective-permute-start(f32[160,128]{1,0:T(8,128)S(1)} %add_add_fusion.a_ref), channel_id=1, source_target_pairs={{0,32},{1,9},{2,34},{3,11},{4,36},{5,13},{6,38},{7,15},{8,40},{9,1... | collective-permute-start | bytes 245768 | tf_op jit(solution)/shard_map/ppermute | solution.py:59
  17.6 3.6 %collective-permute-start.4 = (f32[160,128]{1,0:T(8,128)S(1)}, f32[160,128]{1,0:T(8,128)S(1)}, u32[]{:S(2)}, u32[]{:S(2)}) collective-permute-start(f32[160,128]{1,0:T(8,128)S(1)} %add_add_fusion.a_ref), channel_id=1, source_target_pairs={{0,96},{1,25},{2,98},{3,27},{4,100},{5,29},{6,102},{7,31},{8,104},... | collective-permute-start | bytes 245768 | tf_op jit(solution)/shard_map/ppermute | solution.py:59
  19.4 4.8 %collective-permute-start.5 = (f32[160,128]{1,0:T(8,128)S(1)}, f32[160,128]{1,0:T(8,128)S(1)}, u32[]{:S(2)}, u32[]{:S(2)}) collective-permute-start(f32[160,128]{1,0:T(8,128)S(1)} %add_add_fusion.a_ref), channel_id=1, source_target_pairs={{0,64},{1,17},{2,66},{3,19},{4,68},{5,21},{6,70},{7,23},{8,72},{9,... | collective-permute-start | bytes 245768 | tf_op jit(solution)/shard_map/ppermute | solution.py:59
  24.9 5.0 %collective-permute-start.6 = (f32[680,128]{1,0:T(8,128)S(1)}, f32[680,128]{1,0:T(8,128)S(1)}, u32[]{:S(2)}, u32[]{:S(2)}) collective-permute-start(f32[680,128]{1,0:T(8,128)S(1)} %get-tuple-element.37), channel_id=1, source_target_pairs={{0,1},{1,0},{2,3},{3,2},{4,5},{5,4},{6,7},{7,6},{8,9},{9,8},{10,11... | collective-permute-start | bytes 1044488 | tf_op jit(solution)/shard_map/ppermute | solution.py:69
  29.3 3.2 %collective-permute-start.7 = (f32[1920,128]{1,0:T(8,128)S(1)}, f32[1920,128]{1,0:T(8,128)S(1)}, u32[]{:S(2)}, u32[]{:S(2)}) collective-permute-start(f32[1920,128]{1,0:T(8,128)S(1)} %next_right.3.after_ref), channel_id=1, source_target_pairs={{0,1},{1,0},{2,3},{3,2},{4,5},{5,4},{6,7},{7,6},{8,9},{9,8},{10,11... | collective-permute-start | bytes 2949128 | tf_op jit(solution)/shard_map/ppermute | solution.py:69
  30.0 7.8 %collective-permute-start.10 = (f32[640,128]{1,0:T(8,128)S(1)}, f32[640,128]{1,0:T(8,128)S(1)}, u32[]{:S(2)}, u32[]{:S(2)}) collective-permute-start(f32[640,128]{1,0:T(8,128)S(1)} %get-tuple-element.42), channel_id=1, source_target_pairs={{0,16},{1,65},{2,18},{3,67},{4,20},{5,69},{6,22},{7,71},{8,24},{9,... | collective-permute-start | bytes 983048 | tf_op jit(solution)/shard_map/ppermute | solution.py:59
  32.7 8.6 %collective-permute-start.8 = (f32[640,128]{1,0:T(8,128)S(1)}, f32[640,128]{1,0:T(8,128)S(1)}, u32[]{:S(2)}, u32[]{:S(2)}) collective-permute-start(f32[640,128]{1,0:T(8,128)S(1)} %get-tuple-element.40), channel_id=1, source_target_pairs={{0,8},{1,33},{2,10},{3,35},{4,12},{5,37},{6,14},{7,39},{8,16},{9,4... | collective-permute-start | bytes 983048 | tf_op jit(solution)/shard_map/ppermute | solution.py:59
  33.5 7.8 %collective-permute-start.9 = (f32[640,128]{1,0:T(8,128)S(1)}, f32[640,128]{1,0:T(8,128)S(1)}, u32[]{:S(2)}, u32[]{:S(2)}) collective-permute-start(f32[640,128]{1,0:T(8,128)S(1)} %get-tuple-element.41), channel_id=1, source_target_pairs={{0,24},{1,97},{2,26},{3,99},{4,28},{5,101},{6,30},{7,103},{8,0},{9... | collective-permute-start | bytes 983048 | tf_op jit(solution)/shard_map/ppermute | solution.py:59
  41.4 4.6 %collective-permute-start.11 = (f32[160,128]{1,0:T(8,128)S(1)}, f32[160,128]{1,0:T(8,128)S(1)}, u32[]{:S(2)}, u32[]{:S(2)}) collective-permute-start(f32[160,128]{1,0:T(8,128)S(1)} %get-tuple-element.44), channel_id=1, source_target_pairs={{0,32},{1,9},{2,34},{3,11},{4,36},{5,13},{6,38},{7,15},{8,40},{9,1... | collective-permute-start | bytes 245768 | tf_op jit(solution)/shard_map/ppermute | solution.py:59
  41.5 4.9 %collective-permute-start.12 = (f32[160,128]{1,0:T(8,128)S(1)}, f32[160,128]{1,0:T(8,128)S(1)}, u32[]{:S(2)}, u32[]{:S(2)}) collective-permute-start(f32[160,128]{1,0:T(8,128)S(1)} %get-tuple-element.45), channel_id=1, source_target_pairs={{0,96},{1,25},{2,98},{3,27},{4,100},{5,29},{6,102},{7,31},{8,104},... | collective-permute-start | bytes 245768 | tf_op jit(solution)/shard_map/ppermute | solution.py:59
  44.1 4.8 %collective-permute-start.13 = (f32[160,128]{1,0:T(8,128)S(1)}, f32[160,128]{1,0:T(8,128)S(1)}, u32[]{:S(2)}, u32[]{:S(2)}) collective-permute-start(f32[160,128]{1,0:T(8,128)S(1)} %get-tuple-element.46), channel_id=1, source_target_pairs={{0,64},{1,17},{2,66},{3,19},{4,68},{5,21},{6,70},{7,23},{8,72},{9,... | collective-permute-start | bytes 245768 | tf_op jit(solution)/shard_map/ppermute | solution.py:59
  48.9 4.8 %collective-permute-start.14 = (f32[200,128]{1,0:T(8,128)S(1)}, f32[200,128]{1,0:T(8,128)S(1)}, u32[]{:S(2)}, u32[]{:S(2)}) collective-permute-start(f32[200,128]{1,0:T(8,128)S(1)} %add_parts.1.a_ref), channel_id=1, source_target_pairs={{0,2},{2,4},{4,6},{6,0},{1,3},{3,5},{5,7},{7,1},{8,10},{10,12},{12... | collective-permute-start | bytes 307208 | tf_op jit(solution)/shard_map/ppermute | solution.py:65
  50.3 3.5 %collective-permute-start.15 = (f32[200,128]{1,0:T(8,128)S(1)}, f32[200,128]{1,0:T(8,128)S(1)}, u32[]{:S(2)}, u32[]{:S(2)}) collective-permute-start(f32[200,128]{1,0:T(8,128)S(1)} %add_parts.1.a_ref), channel_id=1, source_target_pairs={{0,6},{2,0},{4,2},{6,4},{1,7},{3,1},{5,3},{7,5},{8,14},{10,8},{12,... | collective-permute-start | bytes 307208 | tf_op jit(solution)/shard_map/ppermute | solution.py:65
  51.8 5.1 %collective-permute-start.16 = (f32[200,128]{1,0:T(8,128)S(1)}, f32[200,128]{1,0:T(8,128)S(1)}, u32[]{:S(2)}, u32[]{:S(2)}) collective-permute-start(f32[200,128]{1,0:T(8,128)S(1)} %add_parts.1.a_ref), channel_id=1, source_target_pairs={{0,4},{2,6},{4,0},{6,2},{1,5},{3,7},{5,1},{7,3},{8,12},{10,14},{12... | collective-permute-start | bytes 307208 | tf_op jit(solution)/shard_map/ppermute | solution.py:65
  57.0 4.9 %collective-permute-start.17 = (f32[160,128]{1,0:T(8,128)S(1)}, f32[160,128]{1,0:T(8,128)S(1)}, u32[]{:S(2)}, u32[]{:S(2)}) collective-permute-start(f32[160,128]{1,0:T(8,128)S(1)} %get-tuple-element.52.a_ref), channel_id=1, source_target_pairs={{0,32},{1,9},{2,34},{3,11},{4,36},{5,13},{6,38},{7,15},{8,40},{9,1... | collective-permute-start | bytes 245768 | tf_op jit(solution)/shard_map/ppermute | solution.py:59
  57.3 4.9 %collective-permute-start.18 = (f32[160,128]{1,0:T(8,128)S(1)}, f32[160,128]{1,0:T(8,128)S(1)}, u32[]{:S(2)}, u32[]{:S(2)}) collective-permute-start(f32[160,128]{1,0:T(8,128)S(1)} %get-tuple-element.52.a_ref), channel_id=1, source_target_pairs={{0,96},{1,25},{2,98},{3,27},{4,100},{5,29},{6,102},{7,31},{8,104},... | collective-permute-start | bytes 245768 | tf_op jit(solution)/shard_map/ppermute | solution.py:59
  59.9 4.8 %collective-permute-start.19 = (f32[160,128]{1,0:T(8,128)S(1)}, f32[160,128]{1,0:T(8,128)S(1)}, u32[]{:S(2)}, u32[]{:S(2)}) collective-permute-start(f32[160,128]{1,0:T(8,128)S(1)} %get-tuple-element.52.a_ref), channel_id=1, source_target_pairs={{0,64},{1,17},{2,66},{3,19},{4,68},{5,21},{6,70},{7,23},{8,72},{9,... | collective-permute-start | bytes 245768 | tf_op jit(solution)/shard_map/ppermute | solution.py:59
  64.8 10.0 %collective-permute-start.21 = (f32[640,128]{1,0:T(8,128)S(1)}, f32[640,128]{1,0:T(8,128)S(1)}, u32[]{:S(2)}, u32[]{:S(2)}) collective-permute-start(f32[640,128]{1,0:T(8,128)S(1)} %assemble.1.refs_0_), channel_id=1, source_target_pairs={{0,1},{1,0},{2,3},{3,2},{4,5},{5,4},{6,7},{7,6},{8,9},{9,8},{10,11... | collective-permute-start | bytes 983048 | tf_op jit(solution)/shard_map/ppermute | solution.py:69
  71.1 7.8 %collective-permute-start.25 = (f32[640,128]{1,0:T(8,128)S(1)}, f32[640,128]{1,0:T(8,128)S(1)}, u32[]{:S(2)}, u32[]{:S(2)}) collective-permute-start(f32[640,128]{1,0:T(8,128)S(1)} %assemble.1.refs_0_), channel_id=1, source_target_pairs={{0,16},{1,65},{2,18},{3,67},{4,20},{5,69},{6,22},{7,71},{8,24},{9,... | collective-permute-start | bytes 983048 | tf_op jit(solution)/shard_map/ppermute | solution.py:59
  71.1 9.2 %collective-permute-start.23 = (f32[640,128]{1,0:T(8,128)S(1)}, f32[640,128]{1,0:T(8,128)S(1)}, u32[]{:S(2)}, u32[]{:S(2)}) collective-permute-start(f32[640,128]{1,0:T(8,128)S(1)} %assemble.1.refs_0_), channel_id=1, source_target_pairs={{0,24},{1,97},{2,26},{3,99},{4,28},{5,101},{6,30},{7,103},{8,0},{9... | collective-permute-start | bytes 983048 | tf_op jit(solution)/shard_map/ppermute | solution.py:59
  72.1 11.0 %collective-permute-start.20 = (f32[640,128]{1,0:T(8,128)S(1)}, f32[640,128]{1,0:T(8,128)S(1)}, u32[]{:S(2)}, u32[]{:S(2)}) collective-permute-start(f32[640,128]{1,0:T(8,128)S(1)} %assemble.1.refs_0_), channel_id=1, source_target_pairs={{0,8},{1,33},{2,10},{3,35},{4,12},{5,37},{6,14},{7,39},{8,16},{9,4... | collective-permute-start | bytes 983048 | tf_op jit(solution)/shard_map/ppermute | solution.py:59
  78.9 7.7 %collective-permute-start.26 = (f32[640,128]{1,0:T(8,128)S(1)}, f32[640,128]{1,0:T(8,128)S(1)}, u32[]{:S(2)}, u32[]{:S(2)}) collective-permute-start(f32[640,128]{1,0:T(8,128)S(1)} %tie.5.refs_2_), channel_id=1, source_target_pairs={{0,1},{1,0},{2,3},{3,2},{4,5},{5,4},{6,7},{7,6},{8,9},{9,8},{10,11... | collective-permute-start | bytes 983048 | tf_op jit(solution)/shard_map/ppermute | solution.py:69
  80.3 6.3 %collective-permute-start.24 = (f32[640,128]{1,0:T(8,128)S(1)}, f32[640,128]{1,0:T(8,128)S(1)}, u32[]{:S(2)}, u32[]{:S(2)}) collective-permute-start(f32[640,128]{1,0:T(8,128)S(1)} %tie.4.refs_1_), channel_id=1, source_target_pairs={{0,1},{1,0},{2,3},{3,2},{4,5},{5,4},{6,7},{7,6},{8,9},{9,8},{10,11... | collective-permute-start | bytes 983048 | tf_op jit(solution)/shard_map/ppermute | solution.py:69
  83.1 3.5 %collective-permute-start.22 = (f32[640,128]{1,0:T(8,128)S(1)}, f32[640,128]{1,0:T(8,128)S(1)}, u32[]{:S(2)}, u32[]{:S(2)}) collective-permute-start(f32[640,128]{1,0:T(8,128)S(1)} %tie.3.refs_0_), channel_id=1, source_target_pairs={{0,1},{1,0},{2,3},{3,2},{4,5},{5,4},{6,7},{7,6},{8,9},{9,8},{10,11... | collective-permute-start | bytes 983048 | tf_op jit(solution)/shard_map/ppermute | solution.py:69

commit v10 on v9

--- a/solution.py
+++ b/solution.py
@@ -359,7 +359,7 @@
     )(*parts, after)
 
 
-def factor_kernel(replicas, ext_ref, p_ref, solve_ref, hat_ref):
+def factor_kernel(replicas, ext_ref, p_ref, solve_ref, left_ref, hat_ref):
     rank = p_ref.shape[0]
     groups = rank // ROWS
     sub = lax.broadcasted_iota(jnp.int32, (ROWS, 2 * rank), 0)
@@ -400,8 +400,11 @@
         inverse.append(blocks[g][:, rank:] / jnp.sqrt(diagonal))
     inverse = jnp.concatenate(inverse, axis=0)
     grams = ext_ref.shape[0] - ROWS
-    solve_ref[...] = inverse * (ext_ref[grams : grams + 1, :1] * (1.0 / replicas))
-    hat_ref[...] = jnp.dot(inverse, p_ref[...], precision=HIGHEST, preferred_element_type=F32)
+    s1, s2, s3 = split(inverse * (ext_ref[grams : grams + 1, :1] * (1.0 / replicas)))
+    solve_ref[...] = jnp.concatenate([s1, s1, s2, s2, s1, s3], axis=1)
+    hat = jnp.dot(inverse, p_ref[...], precision=HIGHEST, preferred_element_type=F32)
+    hat_ref[...] = hat
+    left_ref[...] = hat.T.astype(BF16)
 
 
 def factor(ext, p_mean, replicas):
@@ -409,29 +412,29 @@
     return pl.pallas_call(
         functools.partial(factor_kernel, replicas),
         out_shape=[
-            jax.ShapeDtypeStruct((rank, rank), F32),
+            jax.ShapeDtypeStruct((rank, 6 * rank), BF16),
+            jax.ShapeDtypeStruct((rows, rank), BF16),
             jax.ShapeDtypeStruct((rank, rows), F32),
         ],
         in_specs=[WHOLE] * 2,
-        out_specs=[WHOLE] * 2,
+        out_specs=[WHOLE] * 3,
         compiler_params=params(8),
         cost_estimate=cost(1 << 32, 1 << 20),
         name="factor",
     )(ext, p_mean)
 
 
-def result_kernel(sources, last, width, solve_ref, p_ref, m_ref, *refs):
+def result_kernel(sources, last, width, solve_ref, left_ref, m_ref, *refs):
     if last:
         hat_hbm, refs = refs[-4], refs[:-4] + refs[-3:]
-        hat = pltpu.make_async_copy(p_ref, hat_hbm, refs[-1].at[0, len(sources)])
+        hat = pltpu.make_async_copy(refs[len(sources)], hat_hbm, refs[-1].at[0, len(sources)])
         hat.start()
     error_hbm, q_hbm, token_ref, error_ref, q_ref, sems = refs[-6:]
     token_ref[...] = jnp.zeros_like(token_ref)
     rank = solve_ref.shape[0]
     columns = q_ref.shape[2]
-    left = p_ref[...].T.astype(BF16)
-    s1, s2, s3 = split(solve_ref[...])
-    solve = jnp.concatenate([s1, s1, s2, s2, s1, s3], axis=1)
+    left = left_ref[...]
+    solve = solve_ref[...]
 
     def copies(n, base, at, size):
         to, here = pl.ds(pl.multiple_of(base + at, 128), size), pl.ds(at, size)
@@ -478,32 +481,33 @@
         hat.wait()
 
 
-def result(sources, last, totals, merged, solve, p_hat, before):
+def result(sources, totals, merged, solve, left, before, p_hat=None):
     rank = solve.shape[0]
     rows, columns = merged.shape
     quarter = columns // 2 // QUARTERS
     n = len(sources)
     held = [] if before is None else list(before)
-    return pl.pallas_call(
-        functools.partial(result_kernel, sources, last, quarter // 2),
+    last = [] if p_hat is None else [p_hat]
+    return pl.pallas_call(
+        functools.partial(result_kernel, sources, bool(last), quarter // 2),
         out_shape=[
             pltpu.HBM((rows, columns), BF16),
             pltpu.HBM((rank, columns), F32),
             pltpu.VMEM((ROWS, 128), F32),
         ]
-        + [pltpu.HBM(p_hat.shape, F32)] * last,
-        in_specs=[WHOLE] * (3 + n) + [ANY] * len(held),
-        out_specs=[ANY, ANY, WHOLE] + [ANY] * last,
+        + [pltpu.HBM(a.shape, F32) for a in last],
+        in_specs=[WHOLE] * (3 + n + len(last)) + [ANY] * len(held),
+        out_specs=[ANY, ANY, WHOLE] + [ANY] * len(last),
         scratch_shapes=[
             pltpu.VMEM((n, rows, quarter), BF16),
             pltpu.VMEM((n, rank, quarter), F32),
             pltpu.SemaphoreType.DMA((2, n + 1)),
         ],
-        input_output_aliases={3 + n + i: i for i in range(len(held))},
+        input_output_aliases={3 + n + len(last) + i: i for i in range(len(held))},
         compiler_params=params(12),
         cost_estimate=cost(1<<33, 1<<20),
         name="result",
-    )(solve, p_hat, merged, *totals, *held)
+    )(solve, left, merged, *totals, *last, *held)
 
 
 def tie_kernel(value_ref, after_ref, out_ref):
@@ -542,19 +546,23 @@
     own, *sent = add_quarters((own, *ring_x_or_z(near, 0, (1, 3)), two))
     part = add_parts((own, *ring_x_or_z(sent, 1)), ext)
     total, ext = across((part, *ring_y(part)), ext.shape[0])
-    solve, p_hat = factor(ext, p_mean, replicas)
+    solve, left, p_hat = factor(ext, p_mean, replicas)
     total = assemble((total, *ring_x_or_z([total] * 3, 1)), solve)
-    others = ring_x_or_z([total] * 3, 0)
-
-    def write(own, turns, totals, before, last=False):
-        sources = tuple((own, k) for k in turns)
-        return result(sources, last, totals, merged, solve, p_hat, before)
-
-    *out, token = write(True, (0,), (total,), None)
-    *out, token = write(False, (0,), (swap(total),), out)
-    others = [tie(a, token) for a in others]
-    *out, _ = write(True, SHIFTS, others, out)
-    new_error, q_new, _, p_hat = write(False, SHIFTS, [swap(a) for a in others], out, True)
+    two, one, three = ring_x_or_z([total] * 3, 0, (2, 1, 3))
+
+    def write(sources, totals, *after):
+        return result(sources, totals, merged, solve, left, *after)
+
+    own, other = True, False
+    *out, _ = write(((own, 0),), (total,), None)
+    *out, token = write(((other, 0),), (swap(total),), out)
+    two = tie(two, token)
+    *out, token = write(((own, 2),), (two,), out)
+    one, three = tie(one, token), tie(three, token)
+    *out, _ = write(((own, 1), (own, 3), (other, 2)), (one, three, swap(two)), out)
+    new_error, q_new, _, p_hat = write(
+        ((other, 1), (other, 3)), (swap(one), swap(three)), out, p_hat
+    )
     return (new_error[None], p_hat, q_new)
 
 

time: 90.2 us -> 89.6 us (level)
  starting transfers between devices: 39.8 us -> 38.7 us
    ppermute x6, starting transfers between devices: 14 us -> 12.8 us  [swap(): return lax.ppermute(value, 'c', [(0, 1), (1, 0)])]
    pallas_call x4 -> x5, Pallas kernels: 10.4 us -> 11.3 us  [result(): pl.pallas_call(functools.partial(result_kernel, sources, bool(last), quar...]
  transfers between devices with their start and end apart: 27 -> 27, of which waited for: 15 -> 14; matrix products, arithmetic and copies ran while one was open for 0% -> 0% of each run, Pallas kernels for 13% -> 15%
where the time goes in v10:
time: 89.6 us; the launch traced here: 89.5 us
  starting transfers between devices  38.7 us (43%)
  waiting for transfers between devices  26.9 us (30%)
  Pallas kernels  22.9 us (26%)
  between operations  1 us (1%)
    ppermute x18, waiting for transfers between devices, ring_x_or_z(): out.append(lax.ppermute(value, AXES, pairs))  23.3 us
    ppermute x18, starting transfers between devices, ring_x_or_z(): out.append(lax.ppermute(value, AXES, pairs))  21.4 us
    ppermute x6, starting transfers between devices, swap(): return lax.ppermute(value, 'c', [(0, 1), (1, 0)])  12.8 us
    pallas_call x5, Pallas kernels, result(): pl.pallas_call(functools.partial(result_kernel, sources, bool(last), quar...  11.3 us
    pallas_call x1, Pallas kernels, merge(): pl.pallas_call(functools.partial(merge_kernel, width), out_shape=[pltpu.V...  6.14 us
    ppermute x3, starting transfers between devices, ring_y(): lax.ppermute(value, 'y', [(i, (i + k) % n) for i in range(n)])  4.44 us
    ppermute x3, waiting for transfers between devices, ring_y(): lax.ppermute(value, 'y', [(i, (i + k) % n) for i in range(n)])  3.52 us
    pallas_call x3, Pallas kernels, next_right(): pl.pallas_call(functools.partial(next_right_kernel, own, turns), out_shap...  2.25 us
  transfers between devices with their start and end apart: 27, of which 14 were waited for; matrix products, arithmetic and copies ran while one was open for 0% of the time, Pallas kernels for 15%

profile of v10, /device:TPU:1, one launch (start us, length us, event | category | flops | bytes accessed | tf_op | source)
XLA Modules:
  0.0 89.5 jit_solution(4318084070543208168)
XLA Ops:
  0.6 6.1 %merge.1 = (bf16[320,10240]{1,0:T(8,128)(2,1)S(1)}, f32[160,128]{1,0:T(8,128)S(1)}) custom-call(bf16[320,10240]{1,0:T(8,128)(2,1)} %bitcast.3, bf16[320,10240]{1,0:T(8,128)(2,1)} %bitcast.4, bf16[64,10240]{1,0:T(8,128)(2,1)} %q_hbm.1), custom_call_target="tpu_custom_call" | custom-call | flops 419430400 | bytes 13107200 | tf_op jit(solution)/shard_map/merge/pallas_call | solution.py:125
  6.8 2.5 %collective-permute-start = (f32[160,128]{1,0:T(8,128)S(1)}, f32[160,128]{1,0:T(8,128)S(1)}, u32[]{:S(2)}, u32[]{:S(2)}) collective-permute-start(f32[160,128]{1,0:T(8,128)S(1)} %get-tuple-element.37), channel_id=1, source_target_pairs={{0,8},{1,33},{2,10},{3,35},{4,12},{5,37},{6,14},{7,39},{8,16},{9,4... | collective-permute-start | bytes 245768 | tf_op jit(solution)/shard_map/ppermute | solution.py:59
  9.3 2.2 %collective-permute-start.1 = (f32[160,128]{1,0:T(8,128)S(1)}, f32[160,128]{1,0:T(8,128)S(1)}, u32[]{:S(2)}, u32[]{:S(2)}) collective-permute-start(f32[160,128]{1,0:T(8,128)S(1)} %get-tuple-element.37), channel_id=1, source_target_pairs={{0,24},{1,97},{2,26},{3,99},{4,28},{5,101},{6,30},{7,103},{8,0},{9... | collective-permute-start | bytes 245768 | tf_op jit(solution)/shard_map/ppermute | solution.py:59
  11.5 1.2 %collective-permute-start.2 = (f32[160,128]{1,0:T(8,128)S(1)}, f32[160,128]{1,0:T(8,128)S(1)}, u32[]{:S(2)}, u32[]{:S(2)}) collective-permute-start(f32[160,128]{1,0:T(8,128)S(1)} %get-tuple-element.37), channel_id=1, source_target_pairs={{0,16},{1,65},{2,18},{3,67},{4,20},{5,69},{6,22},{7,71},{8,24},{9,... | collective-permute-start | bytes 245768 | tf_op jit(solution)/shard_map/ppermute | solution.py:59
  12.7 0.8 collective-permute-done
  13.5 3.1 %collective-permute-done.2 = f32[160,128]{1,0:T(8,128)S(1)} collective-permute-done((f32[160,128]{1,0:T(8,128)S(1)}, f32[160,128]{1,0:T(8,128)S(1)}, u32[]{:S(2)}, u32[]{:S(2)}) %collective-permute-start.2) | collective-permute-done | bytes 81952 | tf_op jit(solution)/shard_map/ppermute | solution.py:59
  16.6 1.0 %collective-permute-start.3 = (f32[160,128]{1,0:T(8,128)S(1)}, f32[160,128]{1,0:T(8,128)S(1)}, u32[]{:S(2)}, u32[]{:S(2)}) collective-permute-start(f32[160,128]{1,0:T(8,128)S(1)} %add_add_fusion.a_ref), channel_id=1, source_target_pairs={{0,32},{1,9},{2,34},{3,11},{4,36},{5,13},{6,38},{7,15},{8,40},{9,1... | collective-permute-start | bytes 245768 | tf_op jit(solution)/shard_map/ppermute | solution.py:59
  17.6 1.8 %collective-permute-start.4 = (f32[160,128]{1,0:T(8,128)S(1)}, f32[160,128]{1,0:T(8,128)S(1)}, u32[]{:S(2)}, u32[]{:S(2)}) collective-permute-start(f32[160,128]{1,0:T(8,128)S(1)} %add_add_fusion.a_ref), channel_id=1, source_target_pairs={{0,96},{1,25},{2,98},{3,27},{4,100},{5,29},{6,102},{7,31},{8,104},... | collective-permute-start | bytes 245768 | tf_op jit(solution)/shard_map/ppermute | solution.py:59
  19.4 1.2 %collective-permute-start.5 = (f32[160,128]{1,0:T(8,128)S(1)}, f32[160,128]{1,0:T(8,128)S(1)}, u32[]{:S(2)}, u32[]{:S(2)}) collective-permute-start(f32[160,128]{1,0:T(8,128)S(1)} %add_add_fusion.a_ref), channel_id=1, source_target_pairs={{0,64},{1,17},{2,66},{3,19},{4,68},{5,21},{6,70},{7,23},{8,72},{9,... | collective-permute-start | bytes 245768 | tf_op jit(solution)/shard_map/ppermute | solution.py:59
  20.6 0.6 collective-permute-done.3.b_ref
  21.2 0.0 collective-permute-done.4.c_ref
  21.2 3.0 %collective-permute-done.5.d_ref = f32[160,128]{1,0:T(8,128)S(1)} collective-permute-done((f32[160,128]{1,0:T(8,128)S(1)}, f32[160,128]{1,0:T(8,128)S(1)}, u32[]{:S(2)}, u32[]{:S(2)}) %collective-permute-start.5) | collective-permute-done | bytes 81952 | tf_op jit(solution)/shard_map/ppermute | solution.py:59
  24.2 0.7 first_right.1
  24.9 3.5 %collective-permute-start.6 = (f32[680,128]{1,0:T(8,128)S(1)}, f32[680,128]{1,0:T(8,128)S(1)}, u32[]{:S(2)}, u32[]{:S(2)}) collective-permute-start(f32[680,128]{1,0:T(8,128)S(1)} %get-tuple-element.41), channel_id=1, source_target_pairs={{0,1},{1,0},{2,3},{3,2},{4,5},{5,4},{6,7},{7,6},{8,9},{9,8},{10,11... | collective-permute-start | bytes 1044488 | tf_op jit(solution)/shard_map/ppermute | solution.py:69
  28.4 0.9 %next_right.3.after_ref = f32[1920,128]{1,0:T(8,128)S(1)} custom-call(bf16[192,320]{1,0:T(8,128)(2,1)S(1)} %get-tuple-element.39.pieces_ref, bf16[320,10240]{1,0:T(8,128)(2,1)S(1)} %get-tuple-element.38.m_ref, f32[40,128]{1,0:T(8,128)S(1)} %get-tuple-element.40.after_ref.ext_ref), custom_call_target="tpu_custom_call" | custom-call | flops 8589934592 | bytes 1048576 | tf_op jit(solution)/shard_map/next_right/pallas_call | solution.py:221
  29.3 0.1 collective-permute-start.7
  29.5 0.4 next_right.4.kept_ref
  29.9 0.0 collective-permute-done.6.got_ref
  29.9 0.1 first_pair.1
  30.0 1.6 %collective-permute-start.10 = (f32[640,128]{1,0:T(8,128)S(1)}, f32[640,128]{1,0:T(8,128)S(1)}, u32[]{:S(2)}, u32[]{:S(2)}) collective-permute-start(f32[640,128]{1,0:T(8,128)S(1)} %get-tuple-element.46), channel_id=1, source_target_pairs={{0,16},{1,65},{2,18},{3,67},{4,20},{5,69},{6,22},{7,71},{8,24},{9,... | collective-permute-start | bytes 983048 | tf_op jit(solution)/shard_map/ppermute | solution.py:59
  31.6 0.9 %next_right.5.kept_ref = f32[1920,128]{1,0:T(8,128)S(1)} custom-call(bf16[192,320]{1,0:T(8,128)(2,1)S(1)} %get-tuple-element.39.pieces_ref, bf16[320,10240]{1,0:T(8,128)(2,1)S(1)} %get-tuple-element.38.m_ref, f32[16,128]{1,0:T(8,128)S(1)} %get-tuple-element.42.after_ref.weight_ref), custom_call_target="tpu_custom_call" | custom-call | flops 8589934592 | bytes 1048576 | tf_op jit(solution)/shard_map/next_right/pallas_call | solution.py:221
  32.5 0.0 collective-permute-done.7.got_ref
  32.5 0.2 next_pair.1
  32.7 0.8 collective-permute-start.8
  33.5 1.9 %collective-permute-start.9 = (f32[640,128]{1,0:T(8,128)S(1)}, f32[640,128]{1,0:T(8,128)S(1)}, u32[]{:S(2)}, u32[]{:S(2)}) collective-permute-start(f32[640,128]{1,0:T(8,128)S(1)} %get-tuple-element.45), channel_id=1, source_target_pairs={{0,24},{1,97},{2,26},{3,99},{4,28},{5,101},{6,30},{7,103},{8,0},{9... | collective-permute-start | bytes 983048 | tf_op jit(solution)/shard_map/ppermute | solution.py:59
  35.5 2.3 %collective-permute-done.10.d_ref = f32[640,128]{1,0:T(8,128)S(1)} collective-permute-done((f32[640,128]{1,0:T(8,128)S(1)}, f32[640,128]{1,0:T(8,128)S(1)}, u32[]{:S(2)}, u32[]{:S(2)}) %collective-permute-start.10) | collective-permute-done | bytes 327712 | tf_op jit(solution)/shard_map/ppermute | solution.py:59
  37.8 3.5 %collective-permute-done.8.b_ref = f32[640,128]{1,0:T(8,128)S(1)} collective-permute-done((f32[640,128]{1,0:T(8,128)S(1)}, f32[640,128]{1,0:T(8,128)S(1)}, u32[]{:S(2)}, u32[]{:S(2)}) %collective-permute-start.8) | collective-permute-done | bytes 327712 | tf_op jit(solution)/shard_map/ppermute | solution.py:59
  41.3 0.0 collective-permute-done.9.c_ref
  41.3 0.1 add_quarters.1
  41.4 0.1 collective-permute-start.11
  41.5 2.7 %collective-permute-start.12 = (f32[160,128]{1,0:T(8,128)S(1)}, f32[160,128]{1,0:T(8,128)S(1)}, u32[]{:S(2)}, u32[]{:S(2)}) collective-permute-start(f32[160,128]{1,0:T(8,128)S(1)} %get-tuple-element.49), channel_id=1, source_target_pairs={{0,96},{1,25},{2,98},{3,27},{4,100},{5,29},{6,102},{7,31},{8,104},... | collective-permute-start | bytes 245768 | tf_op jit(solution)/shard_map/ppermute | solution.py:59
  44.1 0.0 collective-permute-start.13
  44.1 1.8 %collective-permute-done.11.b_ref = f32[160,128]{1,0:T(8,128)S(1)} collective-permute-done((f32[160,128]{1,0:T(8,128)S(1)}, f32[160,128]{1,0:T(8,128)S(1)}, u32[]{:S(2)}, u32[]{:S(2)}) %collective-permute-start.11) | collective-permute-done | bytes 81952 | tf_op jit(solution)/shard_map/ppermute | solution.py:59
  46.0 0.4 collective-permute-done.12.c_ref
  46.4 2.5 %collective-permute-done.13.d_ref = f32[160,128]{1,0:T(8,128)S(1)} collective-permute-done((f32[160,128]{1,0:T(8,128)S(1)}, f32[160,128]{1,0:T(8,128)S(1)}, u32[]{:S(2)}, u32[]{:S(2)}) %collective-permute-start.13) | collective-permute-done | bytes 81952 | tf_op jit(solution)/shard_map/ppermute | solution.py:59
  48.9 1.4 %collective-permute-start.14 = (f32[200,128]{1,0:T(8,128)S(1)}, f32[200,128]{1,0:T(8,128)S(1)}, u32[]{:S(2)}, u32[]{:S(2)}) collective-permute-start(f32[200,128]{1,0:T(8,128)S(1)} %add_parts.1.a_ref), channel_id=1, source_target_pairs={{0,2},{2,4},{4,6},{6,0},{1,3},{3,5},{5,7},{7,1},{8,10},{10,12},{12... | collective-permute-start | bytes 307208 | tf_op jit(solution)/shard_map/ppermute | solution.py:65
  50.3 1.5 %collective-permute-start.15 = (f32[200,128]{1,0:T(8,128)S(1)}, f32[200,128]{1,0:T(8,128)S(1)}, u32[]{:S(2)}, u32[]{:S(2)}) collective-permute-start(f32[200,128]{1,0:T(8,128)S(1)} %add_parts.1.a_ref), channel_id=1, source_target_pairs={{0,6},{2,0},{4,2},{6,4},{1,7},{3,1},{5,3},{7,5},{8,14},{10,8},{12,... | collective-permute-start | bytes 307208 | tf_op jit(solution)/shard_map/ppermute | solution.py:65
  51.8 1.6 %collective-permute-start.16 = (f32[200,128]{1,0:T(8,128)S(1)}, f32[200,128]{1,0:T(8,128)S(1)}, u32[]{:S(2)}, u32[]{:S(2)}) collective-permute-start(f32[200,128]{1,0:T(8,128)S(1)} %add_parts.1.a_ref), channel_id=1, source_target_pairs={{0,4},{2,6},{4,0},{6,2},{1,5},{3,7},{5,1},{7,3},{8,12},{10,14},{12... | collective-permute-start | bytes 307208 | tf_op jit(solution)/shard_map/ppermute | solution.py:65
  53.4 0.4 collective-permute-done.14.b_ref
  53.8 0.0 collective-permute-done.15.c_ref
  53.8 3.1 %collective-permute-done.16.d_ref = f32[200,128]{1,0:T(8,128)S(1)} collective-permute-done((f32[200,128]{1,0:T(8,128)S(1)}, f32[200,128]{1,0:T(8,128)S(1)}, u32[]{:S(2)}, u32[]{:S(2)}) %collective-permute-start.16) | collective-permute-done | bytes 102432 | tf_op jit(solution)/shard_map/ppermute | solution.py:65
  56.9 0.1 across.1
  57.0 0.3 collective-permute-start.17
  57.3 2.7 %collective-permute-start.18 = (f32[160,128]{1,0:T(8,128)S(1)}, f32[160,128]{1,0:T(8,128)S(1)}, u32[]{:S(2)}, u32[]{:S(2)}) collective-permute-start(f32[160,128]{1,0:T(8,128)S(1)} %get-tuple-element.56.a_ref), channel_id=1, source_target_pairs={{0,96},{1,25},{2,98},{3,27},{4,100},{5,29},{6,102},{7,31},{8,104},... | collective-permute-start | bytes 245768 | tf_op jit(solution)/shard_map/ppermute | solution.py:59
  59.9 0.0 collective-permute-start.19
  59.9 2.0 %factor.1 = (bf16[64,384]{1,0:T(8,128)(2,1)S(1)}, bf16[320,64]{1,0:T(8,128)(2,1)S(1)}, f32[64,320]{1,0:T(8,128)S(1)}) custom-call(f32[40,128]{1,0:T(8,128)S(1)} %get-tuple-element.52.ext_ref, f32[64,320]{1,0:T(8,128)S(1)} %get-tuple-element.53.p_ref), custom_call_target="tpu_custom_call" | custom-call | flops 4294967296 | bytes 1048576 | tf_op jit(solution)/shard_map/factor/pallas_call | solution.py:412
  61.9 0.0 collective-permute-done.17.b_ref
  62.0 0.2 collective-permute-done.18.c_ref
  62.2 2.5 %collective-permute-done.19.d_ref = f32[160,128]{1,0:T(8,128)S(1)} collective-permute-done((f32[160,128]{1,0:T(8,128)S(1)}, f32[160,128]{1,0:T(8,128)S(1)}, u32[]{:S(2)}, u32[]{:S(2)}) %collective-permute-start.19) | collective-permute-done | bytes 81952 | tf_op jit(solution)/shard_map/ppermute | solution.py:59
  64.8 6.3 %collective-permute-start.22 = (f32[640,128]{1,0:T(8,128)S(1)}, f32[640,128]{1,0:T(8,128)S(1)}, u32[]{:S(2)}, u32[]{:S(2)}) collective-permute-start(f32[640,128]{1,0:T(8,128)S(1)} %assemble.1.refs_0_), channel_id=1, source_target_pairs={{0,1},{1,0},{2,3},{3,2},{4,5},{5,4},{6,7},{7,6},{8,9},{9,8},{10,11... | collective-permute-start | bytes 983048 | tf_op jit(solution)/shard_map/ppermute | solution.py:69
  71.1 0.0 collective-permute-start.21
  71.1 1.0 %collective-permute-start.24 = (f32[640,128]{1,0:T(8,128)S(1)}, f32[640,128]{1,0:T(8,128)S(1)}, u32[]{:S(2)}, u32[]{:S(2)}) collective-permute-start(f32[640,128]{1,0:T(8,128)S(1)} %assemble.1.refs_0_), channel_id=1, source_target_pairs={{0,24},{1,97},{2,26},{3,99},{4,28},{5,101},{6,30},{7,103},{8,0},{9... | collective-permute-start | bytes 983048 | tf_op jit(solution)/shard_map/ppermute | solution.py:59
  72.1 0.5 collective-permute-start.20
  72.6 2.2 %result.5 = (bf16[320,10240]{1,0:T(8,128)(2,1)}, f32[64,10240]{1,0:T(8,128)}, f32[8,128]{1,0:T(8,128)}) custom-call(bf16[64,384]{1,0:T(8,128)(2,1)S(1)} %get-tuple-element.54.after_ref.solve_ref, bf16[320,64]{1,0:T(8,128)(2,1)S(1)} %get-tuple-element.55.left_ref, bf16[320,10240]{1,0:T(8,128)(2,1)S(1)} %get-tuple-element.38.m_ref, f32[640,128]{1,0:T(8,128)S(1)} %assemble.1.refs_0_), custom_call_target="tpu_custom_call" | custom-call | flops 8589934592 | bytes 1048576 | tf_op jit(solution)/shard_map/result/pallas_call | solution.py:491
  74.7 1.6 %result.6 = (bf16[320,10240]{1,0:T(8,128)(2,1)}, f32[64,10240]{1,0:T(8,128)}, f32[8,128]{1,0:T(8,128)S(1)}) custom-call(bf16[64,384]{1,0:T(8,128)(2,1)S(1)} %get-tuple-element.54.after_ref.solve_ref, bf16[320,64]{1,0:T(8,128)(2,1)S(1)} %get-tuple-element.55.left_ref, ...), custom_call_target="tpu_custom_call", output_to_operand_aliasing={{0}: (4, {}), {1}: (5, {})} | custom-call | flops 8589934592 | bytes 1048576 | tf_op jit(solution)/shard_map/result/pallas_call | solution.py:491
  76.3 2.6 %collective-permute-done.21.value_ref = f32[640,128]{1,0:T(8,128)S(1)} collective-permute-done((f32[640,128]{1,0:T(8,128)S(1)}, f32[640,128]{1,0:T(8,128)S(1)}, u32[]{:S(2)}, u32[]{:S(2)}) %collective-permute-start.21) | collective-permute-done | bytes 327712 | tf_op jit(solution)/shard_map/ppermute | solution.py:59
  78.9 1.0 %collective-permute-start.26 = (f32[640,128]{1,0:T(8,128)S(1)}, f32[640,128]{1,0:T(8,128)S(1)}, u32[]{:S(2)}, u32[]{:S(2)}) collective-permute-start(f32[640,128]{1,0:T(8,128)S(1)} %tie.3.refs_0_), channel_id=1, source_target_pairs={{0,1},{1,0},{2,3},{3,2},{4,5},{5,4},{6,7},{7,6},{8,9},{9,8},{10,11... | collective-permute-start | bytes 983048 | tf_op jit(solution)/shard_map/ppermute | solution.py:69
  79.9 1.6 %result.7 = (bf16[320,10240]{1,0:T(8,128)(2,1)}, f32[64,10240]{1,0:T(8,128)}, f32[8,128]{1,0:T(8,128)S(1)}) custom-call(bf16[64,384]{1,0:T(8,128)(2,1)S(1)} %get-tuple-element.54.after_ref.solve_ref, bf16[320,64]{1,0:T(8,128)(2,1)S(1)} %get-tuple-element.55.left_ref, ...), custom_call_target="tpu_custom_call", output_to_operand_aliasing={{0}: (4, {}), {1}: (5, {})} | custom-call | flops 8589934592 | bytes 1048576 | tf_op jit(solution)/shard_map/result/pallas_call | solution.py:491
  81.4 1.7 %collective-permute-start.25 = (f32[640,128]{1,0:T(8,128)S(1)}, f32[640,128]{1,0:T(8,128)S(1)}, u32[]{:S(2)}, u32[]{:S(2)}) collective-permute-start(f32[640,128]{1,0:T(8,128)S(1)} %tie.5.refs_1_), channel_id=1, source_target_pairs={{0,1},{1,0},{2,3},{3,2},{4,5},{5,4},{6,7},{7,6},{8,9},{9,8},{10,11... | collective-permute-start | bytes 983048 | tf_op jit(solution)/shard_map/ppermute | solution.py:69
  83.1 0.2 collective-permute-start.23
  83.3 0.0 collective-permute-done.26.refs_2_
  83.3 3.3 %result.8 = (bf16[320,10240]{1,0:T(8,128)(2,1)}, f32[64,10240]{1,0:T(8,128)}, f32[8,128]{1,0:T(8,128)}) custom-call(bf16[64,384]{1,0:T(8,128)(2,1)S(1)} %get-tuple-element.54.after_ref.solve_ref, bf16[320,64]{1,0:T(8,128)(2,1)S(1)} %get-tuple-element.55.left_ref, ...), custom_call_target="tpu_custom_call", output_to_operand_aliasing={{0}: (6, {}), {1}: (7, {})} | custom-call | flops 8589934592 | bytes 1048576 | tf_op jit(solution)/shard_map/result/pallas_call | solution.py:491
  86.6 0.0 collective-permute-done.23.refs_0_
  86.6 2.7 %result.9 = (bf16[320,10240]{1,0:T(8,128)(2,1)}, f32[64,10240]{1,0:T(8,128)}, f32[8,128]{1,0:T(8,128)}, f32[64,320]{1,0:T(8,128)}) custom-call(bf16[64,384]{1,0:T(8,128)(2,1)S(1)} %get-tuple-element.54.after_ref.solve_ref, bf16[320,64]{1,0:T(8,128)(2,1)S(1)} %get-tuple-element.55.left_ref, ...), custom_call_target="tpu_custom_call", output_to_operand_aliasing={{0}: (6, {}), {1}: (7, {})} | custom-call | flops 8589934592 | bytes 1048576 | tf_op jit(solution)/shard_map/result/pallas_call | solution.py:491
  (11 shorter events, 0.1 us)
Async XLA Ops:
  6.8 6.7 %collective-permute-start = (f32[160,128]{1,0:T(8,128)S(1)}, f32[160,128]{1,0:T(8,128)S(1)}, u32[]{:S(2)}, u32[]{:S(2)}) collective-permute-start(f32[160,128]{1,0:T(8,128)S(1)} %get-tuple-element.37), channel_id=1, source_target_pairs={{0,8},{1,33},{2,10},{3,35},{4,12},{5,37},{6,14},{7,39},{8,16},{9,4... | collective-permute-start | bytes 245768 | tf_op jit(solution)/shard_map/ppermute | solution.py:59
  9.3 4.2 %collective-permute-start.1 = (f32[160,128]{1,0:T(8,128)S(1)}, f32[160,128]{1,0:T(8,128)S(1)}, u32[]{:S(2)}, u32[]{:S(2)}) collective-permute-start(f32[160,128]{1,0:T(8,128)S(1)} %get-tuple-element.37), channel_id=1, source_target_pairs={{0,24},{1,97},{2,26},{3,99},{4,28},{5,101},{6,30},{7,103},{8,0},{9... | collective-permute-start | bytes 245768 | tf_op jit(solution)/shard_map/ppermute | solution.py:59
  11.5 5.1 %collective-permute-start.2 = (f32[160,128]{1,0:T(8,128)S(1)}, f32[160,128]{1,0:T(8,128)S(1)}, u32[]{:S(2)}, u32[]{:S(2)}) collective-permute-start(f32[160,128]{1,0:T(8,128)S(1)} %get-tuple-element.37), channel_id=1, source_target_pairs={{0,16},{1,65},{2,18},{3,67},{4,20},{5,69},{6,22},{7,71},{8,24},{9,... | collective-permute-start | bytes 245768 | tf_op jit(solution)/shard_map/ppermute | solution.py:59
  16.6 4.6 %collective-permute-start.3 = (f32[160,128]{1,0:T(8,128)S(1)}, f32[160,128]{1,0:T(8,128)S(1)}, u32[]{:S(2)}, u32[]{:S(2)}) collective-permute-start(f32[160,128]{1,0:T(8,128)S(1)} %add_add_fusion.a_ref), channel_id=1, source_target_pairs={{0,32},{1,9},{2,34},{3,11},{4,36},{5,13},{6,38},{7,15},{8,40},{9,1... | collective-permute-start | bytes 245768 | tf_op jit(solution)/shard_map/ppermute | solution.py:59
  17.6 3.6 %collective-permute-start.4 = (f32[160,128]{1,0:T(8,128)S(1)}, f32[160,128]{1,0:T(8,128)S(1)}, u32[]{:S(2)}, u32[]{:S(2)}) collective-permute-start(f32[160,128]{1,0:T(8,128)S(1)} %add_add_fusion.a_ref), channel_id=1, source_target_pairs={{0,96},{1,25},{2,98},{3,27},{4,100},{5,29},{6,102},{7,31},{8,104},... | collective-permute-start | bytes 245768 | tf_op jit(solution)/shard_map/ppermute | solution.py:59
  19.4 4.8 %collective-permute-start.5 = (f32[160,128]{1,0:T(8,128)S(1)}, f32[160,128]{1,0:T(8,128)S(1)}, u32[]{:S(2)}, u32[]{:S(2)}) collective-permute-start(f32[160,128]{1,0:T(8,128)S(1)} %add_add_fusion.a_ref), channel_id=1, source_target_pairs={{0,64},{1,17},{2,66},{3,19},{4,68},{5,21},{6,70},{7,23},{8,72},{9,... | collective-permute-start | bytes 245768 | tf_op jit(solution)/shard_map/ppermute | solution.py:59
  24.9 5.0 %collective-permute-start.6 = (f32[680,128]{1,0:T(8,128)S(1)}, f32[680,128]{1,0:T(8,128)S(1)}, u32[]{:S(2)}, u32[]{:S(2)}) collective-permute-start(f32[680,128]{1,0:T(8,128)S(1)} %get-tuple-element.41), channel_id=1, source_target_pairs={{0,1},{1,0},{2,3},{3,2},{4,5},{5,4},{6,7},{7,6},{8,9},{9,8},{10,11... | collective-permute-start | bytes 1044488 | tf_op jit(solution)/shard_map/ppermute | solution.py:69
  29.3 3.2 %collective-permute-start.7 = (f32[1920,128]{1,0:T(8,128)S(1)}, f32[1920,128]{1,0:T(8,128)S(1)}, u32[]{:S(2)}, u32[]{:S(2)}) collective-permute-start(f32[1920,128]{1,0:T(8,128)S(1)} %next_right.3.after_ref), channel_id=1, source_target_pairs={{0,1},{1,0},{2,3},{3,2},{4,5},{5,4},{6,7},{7,6},{8,9},{9,8},{10,11... | collective-permute-start | bytes 2949128 | tf_op jit(solution)/shard_map/ppermute | solution.py:69
  30.0 7.8 %collective-permute-start.10 = (f32[640,128]{1,0:T(8,128)S(1)}, f32[640,128]{1,0:T(8,128)S(1)}, u32[]{:S(2)}, u32[]{:S(2)}) collective-permute-start(f32[640,128]{1,0:T(8,128)S(1)} %get-tuple-element.46), channel_id=1, source_target_pairs={{0,16},{1,65},{2,18},{3,67},{4,20},{5,69},{6,22},{7,71},{8,24},{9,... | collective-permute-start | bytes 983048 | tf_op jit(solution)/shard_map/ppermute | solution.py:59
  32.7 8.6 %collective-permute-start.8 = (f32[640,128]{1,0:T(8,128)S(1)}, f32[640,128]{1,0:T(8,128)S(1)}, u32[]{:S(2)}, u32[]{:S(2)}) collective-permute-start(f32[640,128]{1,0:T(8,128)S(1)} %get-tuple-element.44), channel_id=1, source_target_pairs={{0,8},{1,33},{2,10},{3,35},{4,12},{5,37},{6,14},{7,39},{8,16},{9,4... | collective-permute-start | bytes 983048 | tf_op jit(solution)/shard_map/ppermute | solution.py:59
  33.5 7.8 %collective-permute-start.9 = (f32[640,128]{1,0:T(8,128)S(1)}, f32[640,128]{1,0:T(8,128)S(1)}, u32[]{:S(2)}, u32[]{:S(2)}) collective-permute-start(f32[640,128]{1,0:T(8,128)S(1)} %get-tuple-element.45), channel_id=1, source_target_pairs={{0,24},{1,97},{2,26},{3,99},{4,28},{5,101},{6,30},{7,103},{8,0},{9... | collective-permute-start | bytes 983048 | tf_op jit(solution)/shard_map/ppermute | solution.py:59
  41.4 4.6 %collective-permute-start.11 = (f32[160,128]{1,0:T(8,128)S(1)}, f32[160,128]{1,0:T(8,128)S(1)}, u32[]{:S(2)}, u32[]{:S(2)}) collective-permute-start(f32[160,128]{1,0:T(8,128)S(1)} %get-tuple-element.48), channel_id=1, source_target_pairs={{0,32},{1,9},{2,34},{3,11},{4,36},{5,13},{6,38},{7,15},{8,40},{9,1... | collective-permute-start | bytes 245768 | tf_op jit(solution)/shard_map/ppermute | solution.py:59
  41.5 4.9 %collective-permute-start.12 = (f32[160,128]{1,0:T(8,128)S(1)}, f32[160,128]{1,0:T(8,128)S(1)}, u32[]{:S(2)}, u32[]{:S(2)}) collective-permute-start(f32[160,128]{1,0:T(8,128)S(1)} %get-tuple-element.49), channel_id=1, source_target_pairs={{0,96},{1,25},{2,98},{3,27},{4,100},{5,29},{6,102},{7,31},{8,104},... | collective-permute-start | bytes 245768 | tf_op jit(solution)/shard_map/ppermute | solution.py:59
  44.1 4.8 %collective-permute-start.13 = (f32[160,128]{1,0:T(8,128)S(1)}, f32[160,128]{1,0:T(8,128)S(1)}, u32[]{:S(2)}, u32[]{:S(2)}) collective-permute-start(f32[160,128]{1,0:T(8,128)S(1)} %get-tuple-element.50), channel_id=1, source_target_pairs={{0,64},{1,17},{2,66},{3,19},{4,68},{5,21},{6,70},{7,23},{8,72},{9,... | collective-permute-start | bytes 245768 | tf_op jit(solution)/shard_map/ppermute | solution.py:59
  48.9 4.8 %collective-permute-start.14 = (f32[200,128]{1,0:T(8,128)S(1)}, f32[200,128]{1,0:T(8,128)S(1)}, u32[]{:S(2)}, u32[]{:S(2)}) collective-permute-start(f32[200,128]{1,0:T(8,128)S(1)} %add_parts.1.a_ref), channel_id=1, source_target_pairs={{0,2},{2,4},{4,6},{6,0},{1,3},{3,5},{5,7},{7,1},{8,10},{10,12},{12... | collective-permute-start | bytes 307208 | tf_op jit(solution)/shard_map/ppermute | solution.py:65
  50.3 3.5 %collective-permute-start.15 = (f32[200,128]{1,0:T(8,128)S(1)}, f32[200,128]{1,0:T(8,128)S(1)}, u32[]{:S(2)}, u32[]{:S(2)}) collective-permute-start(f32[200,128]{1,0:T(8,128)S(1)} %add_parts.1.a_ref), channel_id=1, source_target_pairs={{0,6},{2,0},{4,2},{6,4},{1,7},{3,1},{5,3},{7,5},{8,14},{10,8},{12,... | collective-permute-start | bytes 307208 | tf_op jit(solution)/shard_map/ppermute | solution.py:65
  51.8 5.1 %collective-permute-start.16 = (f32[200,128]{1,0:T(8,128)S(1)}, f32[200,128]{1,0:T(8,128)S(1)}, u32[]{:S(2)}, u32[]{:S(2)}) collective-permute-start(f32[200,128]{1,0:T(8,128)S(1)} %add_parts.1.a_ref), channel_id=1, source_target_pairs={{0,4},{2,6},{4,0},{6,2},{1,5},{3,7},{5,1},{7,3},{8,12},{10,14},{12... | collective-permute-start | bytes 307208 | tf_op jit(solution)/shard_map/ppermute | solution.py:65
  57.0 5.0 %collective-permute-start.17 = (f32[160,128]{1,0:T(8,128)S(1)}, f32[160,128]{1,0:T(8,128)S(1)}, u32[]{:S(2)}, u32[]{:S(2)}) collective-permute-start(f32[160,128]{1,0:T(8,128)S(1)} %get-tuple-element.56.a_ref), channel_id=1, source_target_pairs={{0,32},{1,9},{2,34},{3,11},{4,36},{5,13},{6,38},{7,15},{8,40},{9,1... | collective-permute-start | bytes 245768 | tf_op jit(solution)/shard_map/ppermute | solution.py:59
  57.3 4.9 %collective-permute-start.18 = (f32[160,128]{1,0:T(8,128)S(1)}, f32[160,128]{1,0:T(8,128)S(1)}, u32[]{:S(2)}, u32[]{:S(2)}) collective-permute-start(f32[160,128]{1,0:T(8,128)S(1)} %get-tuple-element.56.a_ref), channel_id=1, source_target_pairs={{0,96},{1,25},{2,98},{3,27},{4,100},{5,29},{6,102},{7,31},{8,104},... | collective-permute-start | bytes 245768 | tf_op jit(solution)/shard_map/ppermute | solution.py:59
  59.9 4.8 %collective-permute-start.19 = (f32[160,128]{1,0:T(8,128)S(1)}, f32[160,128]{1,0:T(8,128)S(1)}, u32[]{:S(2)}, u32[]{:S(2)}) collective-permute-start(f32[160,128]{1,0:T(8,128)S(1)} %get-tuple-element.56.a_ref), channel_id=1, source_target_pairs={{0,64},{1,17},{2,66},{3,19},{4,68},{5,21},{6,70},{7,23},{8,72},{9,... | collective-permute-start | bytes 245768 | tf_op jit(solution)/shard_map/ppermute | solution.py:59
  64.8 10.0 %collective-permute-start.22 = (f32[640,128]{1,0:T(8,128)S(1)}, f32[640,128]{1,0:T(8,128)S(1)}, u32[]{:S(2)}, u32[]{:S(2)}) collective-permute-start(f32[640,128]{1,0:T(8,128)S(1)} %assemble.1.refs_0_), channel_id=1, source_target_pairs={{0,1},{1,0},{2,3},{3,2},{4,5},{5,4},{6,7},{7,6},{8,9},{9,8},{10,11... | collective-permute-start | bytes 983048 | tf_op jit(solution)/shard_map/ppermute | solution.py:69
  71.1 7.8 %collective-permute-start.21 = (f32[640,128]{1,0:T(8,128)S(1)}, f32[640,128]{1,0:T(8,128)S(1)}, u32[]{:S(2)}, u32[]{:S(2)}) collective-permute-start(f32[640,128]{1,0:T(8,128)S(1)} %assemble.1.refs_0_), channel_id=1, source_target_pairs={{0,16},{1,65},{2,18},{3,67},{4,20},{5,69},{6,22},{7,71},{8,24},{9,... | collective-permute-start | bytes 983048 | tf_op jit(solution)/shard_map/ppermute | solution.py:59
  71.1 10.3 %collective-permute-start.24 = (f32[640,128]{1,0:T(8,128)S(1)}, f32[640,128]{1,0:T(8,128)S(1)}, u32[]{:S(2)}, u32[]{:S(2)}) collective-permute-start(f32[640,128]{1,0:T(8,128)S(1)} %assemble.1.refs_0_), channel_id=1, source_target_pairs={{0,24},{1,97},{2,26},{3,99},{4,28},{5,101},{6,30},{7,103},{8,0},{9... | collective-permute-start | bytes 983048 | tf_op jit(solution)/shard_map/ppermute | solution.py:59
  72.1 11.0 %collective-permute-start.20 = (f32[640,128]{1,0:T(8,128)S(1)}, f32[640,128]{1,0:T(8,128)S(1)}, u32[]{:S(2)}, u32[]{:S(2)}) collective-permute-start(f32[640,128]{1,0:T(8,128)S(1)} %assemble.1.refs_0_), channel_id=1, source_target_pairs={{0,8},{1,33},{2,10},{3,35},{4,12},{5,37},{6,14},{7,39},{8,16},{9,4... | collective-permute-start | bytes 983048 | tf_op jit(solution)/shard_map/ppermute | solution.py:59
  78.9 4.4 %collective-permute-start.26 = (f32[640,128]{1,0:T(8,128)S(1)}, f32[640,128]{1,0:T(8,128)S(1)}, u32[]{:S(2)}, u32[]{:S(2)}) collective-permute-start(f32[640,128]{1,0:T(8,128)S(1)} %tie.3.refs_0_), channel_id=1, source_target_pairs={{0,1},{1,0},{2,3},{3,2},{4,5},{5,4},{6,7},{7,6},{8,9},{9,8},{10,11... | collective-permute-start | bytes 983048 | tf_op jit(solution)/shard_map/ppermute | solution.py:69
  81.4 5.1 %collective-permute-start.25 = (f32[640,128]{1,0:T(8,128)S(1)}, f32[640,128]{1,0:T(8,128)S(1)}, u32[]{:S(2)}, u32[]{:S(2)}) collective-permute-start(f32[640,128]{1,0:T(8,128)S(1)} %tie.5.refs_1_), channel_id=1, source_target_pairs={{0,1},{1,0},{2,3},{3,2},{4,5},{5,4},{6,7},{7,6},{8,9},{9,8},{10,11... | collective-permute-start | bytes 983048 | tf_op jit(solution)/shard_map/ppermute | solution.py:69
  83.1 3.5 %collective-permute-start.23 = (f32[640,128]{1,0:T(8,128)S(1)}, f32[640,128]{1,0:T(8,128)S(1)}, u32[]{:S(2)}, u32[]{:S(2)}) collective-permute-start(f32[640,128]{1,0:T(8,128)S(1)} %tie.4.refs_0_), channel_id=1, source_target_pairs={{0,1},{1,0},{2,3},{3,2},{4,5},{5,4},{6,7},{7,6},{8,9},{9,8},{10,11... | collective-permute-start | bytes 983048 | tf_op jit(solution)/shard_map/ppermute | solution.py:69

commit v11 on v10

--- a/solution.py
+++ b/solution.py
@@ -30,9 +30,14 @@
     return pl.CostEstimate(flops=flops, bytes_accessed=nbytes, transcendentals=0)
 
 
+def half_of(x, y, z, c):
+    return (x + y + z + c) % 2
+
+
 def place():
-    core, x, z = (lax.axis_index(a) for a in ("c", "x", "z"))
-    return core, jnp.where(core == 0, x, z), jnp.where(core == 0, z, x)
+    x, y, z, c = (lax.axis_index(a) for a in ("x", "y", "z", "c"))
+    half = half_of(x, y, z, c)
+    return half, jnp.where(half == 0, x, z), jnp.where(half == 0, z, x)
 
 
 def index(z, x, y, c):
@@ -49,20 +54,27 @@
     ]
 
 
-def ring_x_or_z(values, phase, shifts=SHIFTS):
+def ring_x_or_z(values, phase, shifts=SHIFTS, halves=True):
     out = []
     for k, value in zip(shifts, values):
         pairs = []
         for z, x, y, c in everyone():
-            to = (z, (x + k) % SIZES[1], y, c) if c == phase else ((z + k) % SIZES[0], x, y, c)
-            pairs.append((index(z, x, y, c), index(*to)))
+            along_x = (half_of(x, y, z, c) if halves else c) == phase
+            to = (z, (x + k) % SIZES[1], y) if along_x else ((z + k) % SIZES[0], x, y)
+            pairs.append((index(z, x, y, c), index(*to, (c + k) % 2 if halves else c)))
         out.append(lax.ppermute(value, AXES, pairs))
     return out
 
 
 def ring_y(value):
-    n = SIZES[2]
-    return [lax.ppermute(value, "y", [(i, (i + k) % n) for i in range(n)]) for k in SHIFTS]
+    out = []
+    for k in SHIFTS:
+        pairs = [
+            (index(z, x, y, c), index(z, x, (y + k) % SIZES[2], (c + k) % 2))
+            for z, x, y, c in everyone()
+        ]
+        out.append(lax.ppermute(value, AXES, pairs))
+    return out
 
 
 def swap(value):
@@ -154,9 +166,9 @@
 
 
 def quarters_of(own, turns):
-    core, one, two = place()
-    core, turn = (core, one) if own else (1 - core, two)
-    return [core * QUARTERS + (turn + k) % QUARTERS for k in turns]
+    half, one, two = place()
+    half, turn = (half, one) if own else (1 - half, two)
+    return [half * QUARTERS + (turn + k) % QUARTERS for k in turns]
 
 
 def split(n):
@@ -446,10 +458,10 @@
     bases = []
     for n, (own, k) in enumerate(sources):
         t_ref = refs[n]
-        core, one, two = place()
-        core, turn = (core, one) if own else (1 - core, two)
+        half, one, two = place()
+        half, turn = (half, one) if own else (1 - half, two)
         quarter = (turn + QUARTERS - k) % QUARTERS
-        base = (core * QUARTERS + quarter) * columns
+        base = (half * QUARTERS + quarter) * columns
         bases.append(base)
         for at in range(0, columns, width):
             t = jnp.concatenate(
@@ -530,10 +542,10 @@
     rank = q_start.shape[0]
     replicas = SIZES[0] * SIZES[1]
     merged, p = merge(gradient[0], error[0], q_start)
-    a, b, c = ring_x_or_z([p] * 3, 0)
+    a, b, c = ring_x_or_z([p] * 3, 0, halves=False)
     p = (p + a) + (b + c)
     sent, ext, p_mean, pieces = first_right(
-        (2,), (p, *ring_x_or_z([p] * 3, 1)), merged, rank, replicas
+        (2,), (p, *ring_x_or_z([p] * 3, 1, halves=False)), merged, rank, replicas
     )
     got = swap(sent)
     sent = next_right(False, (1, 3, 0), pieces, merged, ext)

time: 89.6 us -> 89.1 us (level)
  starting transfers between devices: 38.7 us -> 37.6 us
    ppermute x6, starting transfers between devices: 12.8 us -> 7.97 us  [swap(): return lax.ppermute(value, 'c', [(0, 1), (1, 0)])]
    ppermute x18, starting transfers between devices: 21.4 us -> 23.4 us  [ring_x_or_z(): out.append(lax.ppermute(value, AXES, pairs))]
    ppermute x3, starting transfers between devices: 4.44 us -> 6.15 us  [ring_y(): out.append(lax.ppermute(value, AXES, pairs))]
    ppermute x3, waiting for transfers between devices: 3.52 us -> 4.62 us  [ring_y(): out.append(lax.ppermute(value, AXES, pairs))]
  transfers between devices with their start and end apart: 27 -> 27, of which waited for: 14 -> 17; matrix products, arithmetic and copies ran while one was open for 0% -> 0% of each run, Pallas kernels for 15% -> 15%
where the time goes in v11:
time: 89.1 us; the launch traced here: 89 us
  starting transfers between devices  37.6 us (42%)
  waiting for transfers between devices  27.6 us (31%)
  Pallas kernels  22.9 us (26%)
  between operations  0.96 us (1%)
    ppermute x18, starting transfers between devices, ring_x_or_z(): out.append(lax.ppermute(value, AXES, pairs))  23.4 us
    ppermute x18, waiting for transfers between devices, ring_x_or_z(): out.append(lax.ppermute(value, AXES, pairs))  22.9 us
    pallas_call x5, Pallas kernels, result(): pl.pallas_call(functools.partial(result_kernel, sources, bool(last), quar...  11.3 us
    ppermute x6, starting transfers between devices, swap(): return lax.ppermute(value, 'c', [(0, 1), (1, 0)])  7.97 us
    ppermute x3, starting transfers between devices, ring_y(): out.append(lax.ppermute(value, AXES, pairs))  6.15 us
    pallas_call x1, Pallas kernels, merge(): pl.pallas_call(functools.partial(merge_kernel, width), out_shape=[pltpu.V...  6.14 us
    ppermute x3, waiting for transfers between devices, ring_y(): out.append(lax.ppermute(value, AXES, pairs))  4.62 us
    pallas_call x3, Pallas kernels, next_right(): pl.pallas_call(functools.partial(next_right_kernel, own, turns), out_shap...  2.25 us
  transfers between devices with their start and end apart: 27, of which 17 were waited for; matrix products, arithmetic and copies ran while one was open for 0% of the time, Pallas kernels for 15%

profile of v11, /device:TPU:1, one launch (start us, length us, event | category | flops | bytes accessed | tf_op | source)
XLA Modules:
  0.0 89.0 jit_solution(5870215200883607300)
XLA Ops:
  0.6 6.1 %merge.1 = (bf16[320,10240]{1,0:T(8,128)(2,1)S(1)}, f32[160,128]{1,0:T(8,128)S(1)}) custom-call(bf16[320,10240]{1,0:T(8,128)(2,1)} %bitcast.3, bf16[320,10240]{1,0:T(8,128)(2,1)} %bitcast.4, bf16[64,10240]{1,0:T(8,128)(2,1)} %q_hbm.1), custom_call_target="tpu_custom_call" | custom-call | flops 419430400 | bytes 13107200 | tf_op jit(solution)/shard_map/merge/pallas_call | solution.py:137
  6.8 2.5 %collective-permute-start = (f32[160,128]{1,0:T(8,128)S(1)}, f32[160,128]{1,0:T(8,128)S(1)}, u32[]{:S(2)}, u32[]{:S(2)}) collective-permute-start(f32[160,128]{1,0:T(8,128)S(1)} %get-tuple-element.37), channel_id=1, source_target_pairs={{0,8},{1,33},{2,10},{3,35},{4,12},{5,37},{6,14},{7,39},{8,16},{9,4... | collective-permute-start | bytes 245768 | tf_op jit(solution)/shard_map/ppermute | solution.py:65
  9.3 2.2 %collective-permute-start.1 = (f32[160,128]{1,0:T(8,128)S(1)}, f32[160,128]{1,0:T(8,128)S(1)}, u32[]{:S(2)}, u32[]{:S(2)}) collective-permute-start(f32[160,128]{1,0:T(8,128)S(1)} %get-tuple-element.37), channel_id=1, source_target_pairs={{0,24},{1,97},{2,26},{3,99},{4,28},{5,101},{6,30},{7,103},{8,0},{9... | collective-permute-start | bytes 245768 | tf_op jit(solution)/shard_map/ppermute | solution.py:65
  11.5 1.2 %collective-permute-start.2 = (f32[160,128]{1,0:T(8,128)S(1)}, f32[160,128]{1,0:T(8,128)S(1)}, u32[]{:S(2)}, u32[]{:S(2)}) collective-permute-start(f32[160,128]{1,0:T(8,128)S(1)} %get-tuple-element.37), channel_id=1, source_target_pairs={{0,16},{1,65},{2,18},{3,67},{4,20},{5,69},{6,22},{7,71},{8,24},{9,... | collective-permute-start | bytes 245768 | tf_op jit(solution)/shard_map/ppermute | solution.py:65
  12.7 0.8 collective-permute-done
  13.5 0.0 collective-permute-done.1
  13.5 3.1 %collective-permute-done.2 = f32[160,128]{1,0:T(8,128)S(1)} collective-permute-done((f32[160,128]{1,0:T(8,128)S(1)}, f32[160,128]{1,0:T(8,128)S(1)}, u32[]{:S(2)}, u32[]{:S(2)}) %collective-permute-start.2) | collective-permute-done | bytes 81952 | tf_op jit(solution)/shard_map/ppermute | solution.py:65
  16.6 1.0 %collective-permute-start.3 = (f32[160,128]{1,0:T(8,128)S(1)}, f32[160,128]{1,0:T(8,128)S(1)}, u32[]{:S(2)}, u32[]{:S(2)}) collective-permute-start(f32[160,128]{1,0:T(8,128)S(1)} %add_add_fusion.a_ref), channel_id=1, source_target_pairs={{0,32},{1,9},{2,34},{3,11},{4,36},{5,13},{6,38},{7,15},{8,40},{9,1... | collective-permute-start | bytes 245768 | tf_op jit(solution)/shard_map/ppermute | solution.py:65
  17.6 1.8 %collective-permute-start.4 = (f32[160,128]{1,0:T(8,128)S(1)}, f32[160,128]{1,0:T(8,128)S(1)}, u32[]{:S(2)}, u32[]{:S(2)}) collective-permute-start(f32[160,128]{1,0:T(8,128)S(1)} %add_add_fusion.a_ref), channel_id=1, source_target_pairs={{0,96},{1,25},{2,98},{3,27},{4,100},{5,29},{6,102},{7,31},{8,104},... | collective-permute-start | bytes 245768 | tf_op jit(solution)/shard_map/ppermute | solution.py:65
  19.4 1.2 %collective-permute-start.5 = (f32[160,128]{1,0:T(8,128)S(1)}, f32[160,128]{1,0:T(8,128)S(1)}, u32[]{:S(2)}, u32[]{:S(2)}) collective-permute-start(f32[160,128]{1,0:T(8,128)S(1)} %add_add_fusion.a_ref), channel_id=1, source_target_pairs={{0,64},{1,17},{2,66},{3,19},{4,68},{5,21},{6,70},{7,23},{8,72},{9,... | collective-permute-start | bytes 245768 | tf_op jit(solution)/shard_map/ppermute | solution.py:65
  20.6 0.6 collective-permute-done.3.b_ref
  21.2 0.0 collective-permute-done.4.c_ref
  21.2 3.0 %collective-permute-done.5.d_ref = f32[160,128]{1,0:T(8,128)S(1)} collective-permute-done((f32[160,128]{1,0:T(8,128)S(1)}, f32[160,128]{1,0:T(8,128)S(1)}, u32[]{:S(2)}, u32[]{:S(2)}) %collective-permute-start.5) | collective-permute-done | bytes 81952 | tf_op jit(solution)/shard_map/ppermute | solution.py:65
  24.2 0.7 first_right.1
  24.9 3.5 %collective-permute-start.6 = (f32[680,128]{1,0:T(8,128)S(1)}, f32[680,128]{1,0:T(8,128)S(1)}, u32[]{:S(2)}, u32[]{:S(2)}) collective-permute-start(f32[680,128]{1,0:T(8,128)S(1)} %get-tuple-element.41), channel_id=1, source_target_pairs={{0,1},{1,0},{2,3},{3,2},{4,5},{5,4},{6,7},{7,6},{8,9},{9,8},{10,11... | collective-permute-start | bytes 1044488 | tf_op jit(solution)/shard_map/ppermute | solution.py:81
  28.4 0.9 %next_right.3.after_ref = f32[1920,128]{1,0:T(8,128)S(1)} custom-call(bf16[192,320]{1,0:T(8,128)(2,1)S(1)} %get-tuple-element.39.pieces_ref, bf16[320,10240]{1,0:T(8,128)(2,1)S(1)} %get-tuple-element.38.m_ref, f32[40,128]{1,0:T(8,128)S(1)} %get-tuple-element.40.after_ref.ext_ref), custom_call_target="tpu_custom_call" | custom-call | flops 8589934592 | bytes 1048576 | tf_op jit(solution)/shard_map/next_right/pallas_call | solution.py:233
  29.3 0.1 collective-permute-start.7
  29.5 0.4 next_right.4.kept_ref
  29.9 0.0 collective-permute-done.6.got_ref
  29.9 0.1 first_pair.1
  30.0 1.6 %collective-permute-start.10 = (f32[640,128]{1,0:T(8,128)S(1)}, f32[640,128]{1,0:T(8,128)S(1)}, u32[]{:S(2)}, u32[]{:S(2)}) collective-permute-start(f32[640,128]{1,0:T(8,128)S(1)} %get-tuple-element.46), channel_id=1, source_target_pairs={{0,16},{1,65},{2,66},{3,19},{4,20},{5,69},{6,70},{7,23},{8,72},{9,... | collective-permute-start | bytes 983048 | tf_op jit(solution)/shard_map/ppermute | solution.py:65
  31.6 0.9 %next_right.5.kept_ref = f32[1920,128]{1,0:T(8,128)S(1)} custom-call(bf16[192,320]{1,0:T(8,128)(2,1)S(1)} %get-tuple-element.39.pieces_ref, bf16[320,10240]{1,0:T(8,128)(2,1)S(1)} %get-tuple-element.38.m_ref, f32[16,128]{1,0:T(8,128)S(1)} %get-tuple-element.42.after_ref.weight_ref), custom_call_target="tpu_custom_call" | custom-call | flops 8589934592 | bytes 1048576 | tf_op jit(solution)/shard_map/next_right/pallas_call | solution.py:233
  32.5 0.0 collective-permute-done.7.got_ref
  32.5 0.2 next_pair.1
  32.7 1.4 %collective-permute-start.8 = (f32[640,128]{1,0:T(8,128)S(1)}, f32[640,128]{1,0:T(8,128)S(1)}, u32[]{:S(2)}, u32[]{:S(2)}) collective-permute-start(f32[640,128]{1,0:T(8,128)S(1)} %get-tuple-element.44), channel_id=1, source_target_pairs={{0,9},{1,32},{2,35},{3,10},{4,13},{5,36},{6,39},{7,14},{8,41},{9,1... | collective-permute-start | bytes 983048 | tf_op jit(solution)/shard_map/ppermute | solution.py:65
  34.2 1.6 %collective-permute-start.9 = (f32[640,128]{1,0:T(8,128)S(1)}, f32[640,128]{1,0:T(8,128)S(1)}, u32[]{:S(2)}, u32[]{:S(2)}) collective-permute-start(f32[640,128]{1,0:T(8,128)S(1)} %get-tuple-element.45), channel_id=1, source_target_pairs={{0,25},{1,96},{2,99},{3,26},{4,29},{5,100},{6,103},{7,30},{8,105},... | collective-permute-start | bytes 983048 | tf_op jit(solution)/shard_map/ppermute | solution.py:65
  35.8 2.0 %collective-permute-done.10.d_ref = f32[640,128]{1,0:T(8,128)S(1)} collective-permute-done((f32[640,128]{1,0:T(8,128)S(1)}, f32[640,128]{1,0:T(8,128)S(1)}, u32[]{:S(2)}, u32[]{:S(2)}) %collective-permute-start.10) | collective-permute-done | bytes 327712 | tf_op jit(solution)/shard_map/ppermute | solution.py:65
  37.8 3.5 %collective-permute-done.8.b_ref = f32[640,128]{1,0:T(8,128)S(1)} collective-permute-done((f32[640,128]{1,0:T(8,128)S(1)}, f32[640,128]{1,0:T(8,128)S(1)}, u32[]{:S(2)}, u32[]{:S(2)}) %collective-permute-start.8) | collective-permute-done | bytes 327712 | tf_op jit(solution)/shard_map/ppermute | solution.py:65
  41.3 0.2 collective-permute-done.9.c_ref
  41.5 0.1 add_quarters.1
  41.6 1.1 %collective-permute-start.11 = (f32[160,128]{1,0:T(8,128)S(1)}, f32[160,128]{1,0:T(8,128)S(1)}, u32[]{:S(2)}, u32[]{:S(2)}) collective-permute-start(f32[160,128]{1,0:T(8,128)S(1)} %get-tuple-element.48), channel_id=1, source_target_pairs={{0,33},{1,8},{2,11},{3,34},{4,37},{5,12},{6,15},{7,38},{8,17},{9,4... | collective-permute-start | bytes 245768 | tf_op jit(solution)/shard_map/ppermute | solution.py:65
  42.7 1.9 %collective-permute-start.12 = (f32[160,128]{1,0:T(8,128)S(1)}, f32[160,128]{1,0:T(8,128)S(1)}, u32[]{:S(2)}, u32[]{:S(2)}) collective-permute-start(f32[160,128]{1,0:T(8,128)S(1)} %get-tuple-element.49), channel_id=1, source_target_pairs={{0,97},{1,24},{2,27},{3,98},{4,101},{5,28},{6,31},{7,102},{8,1},{9... | collective-permute-start | bytes 245768 | tf_op jit(solution)/shard_map/ppermute | solution.py:65
  44.6 0.5 collective-permute-start.13
  45.1 1.9 %collective-permute-done.11.b_ref = f32[160,128]{1,0:T(8,128)S(1)} collective-permute-done((f32[160,128]{1,0:T(8,128)S(1)}, f32[160,128]{1,0:T(8,128)S(1)}, u32[]{:S(2)}, u32[]{:S(2)}) %collective-permute-start.11) | collective-permute-done | bytes 81952 | tf_op jit(solution)/shard_map/ppermute | solution.py:65
  47.0 0.0 collective-permute-done.12.c_ref
  47.0 2.4 %collective-permute-done.13.d_ref = f32[160,128]{1,0:T(8,128)S(1)} collective-permute-done((f32[160,128]{1,0:T(8,128)S(1)}, f32[160,128]{1,0:T(8,128)S(1)}, u32[]{:S(2)}, u32[]{:S(2)}) %collective-permute-start.13) | collective-permute-done | bytes 81952 | tf_op jit(solution)/shard_map/ppermute | solution.py:65
  49.4 3.5 %collective-permute-start.14 = (f32[200,128]{1,0:T(8,128)S(1)}, f32[200,128]{1,0:T(8,128)S(1)}, u32[]{:S(2)}, u32[]{:S(2)}) collective-permute-start(f32[200,128]{1,0:T(8,128)S(1)} %add_parts.1.a_ref), channel_id=1, source_target_pairs={{0,3},{1,2},{2,5},{3,4},{4,7},{5,6},{6,1},{7,0},{8,11},{9,10},{10,... | collective-permute-start | bytes 307208 | tf_op jit(solution)/shard_map/ppermute | solution.py:76
  53.0 1.5 %collective-permute-start.15 = (f32[200,128]{1,0:T(8,128)S(1)}, f32[200,128]{1,0:T(8,128)S(1)}, u32[]{:S(2)}, u32[]{:S(2)}) collective-permute-start(f32[200,128]{1,0:T(8,128)S(1)} %add_parts.1.a_ref), channel_id=1, source_target_pairs={{0,7},{1,6},{2,1},{3,0},{4,3},{5,2},{6,5},{7,4},{8,15},{9,14},{10,... | collective-permute-start | bytes 307208 | tf_op jit(solution)/shard_map/ppermute | solution.py:76
  54.5 1.1 %collective-permute-start.16 = (f32[200,128]{1,0:T(8,128)S(1)}, f32[200,128]{1,0:T(8,128)S(1)}, u32[]{:S(2)}, u32[]{:S(2)}) collective-permute-start(f32[200,128]{1,0:T(8,128)S(1)} %add_parts.1.a_ref), channel_id=1, source_target_pairs={{0,4},{1,5},{2,6},{3,7},{4,0},{5,1},{6,2},{7,3},{8,12},{9,13},{10,... | collective-permute-start | bytes 307208 | tf_op jit(solution)/shard_map/ppermute | solution.py:76
  55.6 1.9 %collective-permute-done.14.b_ref = f32[200,128]{1,0:T(8,128)S(1)} collective-permute-done((f32[200,128]{1,0:T(8,128)S(1)}, f32[200,128]{1,0:T(8,128)S(1)}, u32[]{:S(2)}, u32[]{:S(2)}) %collective-permute-start.14) | collective-permute-done | bytes 102432 | tf_op jit(solution)/shard_map/ppermute | solution.py:76
  57.5 0.6 collective-permute-done.15.c_ref
  58.1 2.1 %collective-permute-done.16.d_ref = f32[200,128]{1,0:T(8,128)S(1)} collective-permute-done((f32[200,128]{1,0:T(8,128)S(1)}, f32[200,128]{1,0:T(8,128)S(1)}, u32[]{:S(2)}, u32[]{:S(2)}) %collective-permute-start.16) | collective-permute-done | bytes 102432 | tf_op jit(solution)/shard_map/ppermute | solution.py:76
  60.2 0.1 across.1
  60.3 0.3 collective-permute-start.17
  60.6 2.9 %collective-permute-start.18 = (f32[160,128]{1,0:T(8,128)S(1)}, f32[160,128]{1,0:T(8,128)S(1)}, u32[]{:S(2)}, u32[]{:S(2)}) collective-permute-start(f32[160,128]{1,0:T(8,128)S(1)} %get-tuple-element.56.a_ref), channel_id=1, source_target_pairs={{0,97},{1,24},{2,27},{3,98},{4,101},{5,28},{6,31},{7,102},{8,1},{9... | collective-permute-start | bytes 245768 | tf_op jit(solution)/shard_map/ppermute | solution.py:65
  63.5 0.0 collective-permute-start.19
  63.5 2.0 %factor.1 = (bf16[64,384]{1,0:T(8,128)(2,1)S(1)}, bf16[320,64]{1,0:T(8,128)(2,1)S(1)}, f32[64,320]{1,0:T(8,128)S(1)}) custom-call(f32[40,128]{1,0:T(8,128)S(1)} %get-tuple-element.52.ext_ref, f32[64,320]{1,0:T(8,128)S(1)} %get-tuple-element.53.p_ref), custom_call_target="tpu_custom_call" | custom-call | flops 4294967296 | bytes 1048576 | tf_op jit(solution)/shard_map/factor/pallas_call | solution.py:424
  65.5 0.4 collective-permute-done.17.b_ref
  65.9 2.4 %collective-permute-done.19.d_ref = f32[160,128]{1,0:T(8,128)S(1)} collective-permute-done((f32[160,128]{1,0:T(8,128)S(1)}, f32[160,128]{1,0:T(8,128)S(1)}, u32[]{:S(2)}, u32[]{:S(2)}) %collective-permute-start.19) | collective-permute-done | bytes 81952 | tf_op jit(solution)/shard_map/ppermute | solution.py:65
  68.3 2.3 %collective-permute-start.22 = (f32[640,128]{1,0:T(8,128)S(1)}, f32[640,128]{1,0:T(8,128)S(1)}, u32[]{:S(2)}, u32[]{:S(2)}) collective-permute-start(f32[640,128]{1,0:T(8,128)S(1)} %assemble.1.refs_0_), channel_id=1, source_target_pairs={{0,1},{1,0},{2,3},{3,2},{4,5},{5,4},{6,7},{7,6},{8,9},{9,8},{10,11... | collective-permute-start | bytes 983048 | tf_op jit(solution)/shard_map/ppermute | solution.py:81
  70.6 2.1 %collective-permute-start.24 = (f32[640,128]{1,0:T(8,128)S(1)}, f32[640,128]{1,0:T(8,128)S(1)}, u32[]{:S(2)}, u32[]{:S(2)}) collective-permute-start(f32[640,128]{1,0:T(8,128)S(1)} %assemble.1.refs_0_), channel_id=1, source_target_pairs={{0,25},{1,96},{2,99},{3,26},{4,29},{5,100},{6,103},{7,30},{8,105},... | collective-permute-start | bytes 983048 | tf_op jit(solution)/shard_map/ppermute | solution.py:65
  72.8 2.2 %result.5 = (bf16[320,10240]{1,0:T(8,128)(2,1)}, f32[64,10240]{1,0:T(8,128)}, f32[8,128]{1,0:T(8,128)}) custom-call(bf16[64,384]{1,0:T(8,128)(2,1)S(1)} %get-tuple-element.54.after_ref.solve_ref, bf16[320,64]{1,0:T(8,128)(2,1)S(1)} %get-tuple-element.55.left_ref, bf16[320,10240]{1,0:T(8,128)(2,1)S(1)} %get-tuple-element.38.m_ref, f32[640,128]{1,0:T(8,128)S(1)} %assemble.1.refs_0_), custom_call_target="tpu_custom_call" | custom-call | flops 8589934592 | bytes 1048576 | tf_op jit(solution)/shard_map/result/pallas_call | solution.py:503
  74.9 0.0 collective-permute-done.22.refs_0_
  74.9 1.6 %result.6 = (bf16[320,10240]{1,0:T(8,128)(2,1)}, f32[64,10240]{1,0:T(8,128)}, f32[8,128]{1,0:T(8,128)S(1)}) custom-call(bf16[64,384]{1,0:T(8,128)(2,1)S(1)} %get-tuple-element.54.after_ref.solve_ref, bf16[320,64]{1,0:T(8,128)(2,1)S(1)} %get-tuple-element.55.left_ref, ...), custom_call_target="tpu_custom_call", output_to_operand_aliasing={{0}: (4, {}), {1}: (5, {})} | custom-call | flops 8589934592 | bytes 1048576 | tf_op jit(solution)/shard_map/result/pallas_call | solution.py:503
  76.5 1.8 %collective-permute-done.21.value_ref = f32[640,128]{1,0:T(8,128)S(1)} collective-permute-done((f32[640,128]{1,0:T(8,128)S(1)}, f32[640,128]{1,0:T(8,128)S(1)}, u32[]{:S(2)}, u32[]{:S(2)}) %collective-permute-start.21) | collective-permute-done | bytes 327712 | tf_op jit(solution)/shard_map/ppermute | solution.py:65
  78.4 1.1 %collective-permute-start.26 = (f32[640,128]{1,0:T(8,128)S(1)}, f32[640,128]{1,0:T(8,128)S(1)}, u32[]{:S(2)}, u32[]{:S(2)}) collective-permute-start(f32[640,128]{1,0:T(8,128)S(1)} %tie.3.refs_0_), channel_id=1, source_target_pairs={{0,1},{1,0},{2,3},{3,2},{4,5},{5,4},{6,7},{7,6},{8,9},{9,8},{10,11... | collective-permute-start | bytes 983048 | tf_op jit(solution)/shard_map/ppermute | solution.py:81
  79.4 1.6 %result.7 = (bf16[320,10240]{1,0:T(8,128)(2,1)}, f32[64,10240]{1,0:T(8,128)}, f32[8,128]{1,0:T(8,128)S(1)}) custom-call(bf16[64,384]{1,0:T(8,128)(2,1)S(1)} %get-tuple-element.54.after_ref.solve_ref, bf16[320,64]{1,0:T(8,128)(2,1)S(1)} %get-tuple-element.55.left_ref, ...), custom_call_target="tpu_custom_call", output_to_operand_aliasing={{0}: (4, {}), {1}: (5, {})} | custom-call | flops 8589934592 | bytes 1048576 | tf_op jit(solution)/shard_map/result/pallas_call | solution.py:503
  81.0 0.4 collective-permute-done.24.value_ref
  81.4 0.5 collective-permute-done.20.value_ref
  81.9 0.9 %collective-permute-start.23 = (f32[640,128]{1,0:T(8,128)S(1)}, f32[640,128]{1,0:T(8,128)S(1)}, u32[]{:S(2)}, u32[]{:S(2)}) collective-permute-start(f32[640,128]{1,0:T(8,128)S(1)} %tie.4.refs_0_), channel_id=1, source_target_pairs={{0,1},{1,0},{2,3},{3,2},{4,5},{5,4},{6,7},{7,6},{8,9},{9,8},{10,11... | collective-permute-start | bytes 983048 | tf_op jit(solution)/shard_map/ppermute | solution.py:81
  82.8 0.0 collective-permute-done.26.refs_2_
  82.8 3.3 %result.8 = (bf16[320,10240]{1,0:T(8,128)(2,1)}, f32[64,10240]{1,0:T(8,128)}, f32[8,128]{1,0:T(8,128)}) custom-call(bf16[64,384]{1,0:T(8,128)(2,1)S(1)} %get-tuple-element.54.after_ref.solve_ref, bf16[320,64]{1,0:T(8,128)(2,1)S(1)} %get-tuple-element.55.left_ref, ...), custom_call_target="tpu_custom_call", output_to_operand_aliasing={{0}: (6, {}), {1}: (7, {})} | custom-call | flops 8589934592 | bytes 1048576 | tf_op jit(solution)/shard_map/result/pallas_call | solution.py:503
  86.1 0.0 collective-permute-done.25.refs_1_
  86.1 2.7 %result.9 = (bf16[320,10240]{1,0:T(8,128)(2,1)}, f32[64,10240]{1,0:T(8,128)}, f32[8,128]{1,0:T(8,128)}, f32[64,320]{1,0:T(8,128)}) custom-call(bf16[64,384]{1,0:T(8,128)(2,1)S(1)} %get-tuple-element.54.after_ref.solve_ref, bf16[320,64]{1,0:T(8,128)(2,1)S(1)} %get-tuple-element.55.left_ref, ...), custom_call_target="tpu_custom_call", output_to_operand_aliasing={{0}: (6, {}), {1}: (7, {})} | custom-call | flops 8589934592 | bytes 1048576 | tf_op jit(solution)/shard_map/result/pallas_call | solution.py:503
  (11 shorter events, 0.1 us)
Async XLA Ops:
  6.8 6.7 %collective-permute-start = (f32[160,128]{1,0:T(8,128)S(1)}, f32[160,128]{1,0:T(8,128)S(1)}, u32[]{:S(2)}, u32[]{:S(2)}) collective-permute-start(f32[160,128]{1,0:T(8,128)S(1)} %get-tuple-element.37), channel_id=1, source_target_pairs={{0,8},{1,33},{2,10},{3,35},{4,12},{5,37},{6,14},{7,39},{8,16},{9,4... | collective-permute-start | bytes 245768 | tf_op jit(solution)/shard_map/ppermute | solution.py:65
  9.3 4.2 %collective-permute-start.1 = (f32[160,128]{1,0:T(8,128)S(1)}, f32[160,128]{1,0:T(8,128)S(1)}, u32[]{:S(2)}, u32[]{:S(2)}) collective-permute-start(f32[160,128]{1,0:T(8,128)S(1)} %get-tuple-element.37), channel_id=1, source_target_pairs={{0,24},{1,97},{2,26},{3,99},{4,28},{5,101},{6,30},{7,103},{8,0},{9... | collective-permute-start | bytes 245768 | tf_op jit(solution)/shard_map/ppermute | solution.py:65
  11.5 5.1 %collective-permute-start.2 = (f32[160,128]{1,0:T(8,128)S(1)}, f32[160,128]{1,0:T(8,128)S(1)}, u32[]{:S(2)}, u32[]{:S(2)}) collective-permute-start(f32[160,128]{1,0:T(8,128)S(1)} %get-tuple-element.37), channel_id=1, source_target_pairs={{0,16},{1,65},{2,18},{3,67},{4,20},{5,69},{6,22},{7,71},{8,24},{9,... | collective-permute-start | bytes 245768 | tf_op jit(solution)/shard_map/ppermute | solution.py:65
  16.6 4.6 %collective-permute-start.3 = (f32[160,128]{1,0:T(8,128)S(1)}, f32[160,128]{1,0:T(8,128)S(1)}, u32[]{:S(2)}, u32[]{:S(2)}) collective-permute-start(f32[160,128]{1,0:T(8,128)S(1)} %add_add_fusion.a_ref), channel_id=1, source_target_pairs={{0,32},{1,9},{2,34},{3,11},{4,36},{5,13},{6,38},{7,15},{8,40},{9,1... | collective-permute-start | bytes 245768 | tf_op jit(solution)/shard_map/ppermute | solution.py:65
  17.6 3.6 %collective-permute-start.4 = (f32[160,128]{1,0:T(8,128)S(1)}, f32[160,128]{1,0:T(8,128)S(1)}, u32[]{:S(2)}, u32[]{:S(2)}) collective-permute-start(f32[160,128]{1,0:T(8,128)S(1)} %add_add_fusion.a_ref), channel_id=1, source_target_pairs={{0,96},{1,25},{2,98},{3,27},{4,100},{5,29},{6,102},{7,31},{8,104},... | collective-permute-start | bytes 245768 | tf_op jit(solution)/shard_map/ppermute | solution.py:65
  19.4 4.8 %collective-permute-start.5 = (f32[160,128]{1,0:T(8,128)S(1)}, f32[160,128]{1,0:T(8,128)S(1)}, u32[]{:S(2)}, u32[]{:S(2)}) collective-permute-start(f32[160,128]{1,0:T(8,128)S(1)} %add_add_fusion.a_ref), channel_id=1, source_target_pairs={{0,64},{1,17},{2,66},{3,19},{4,68},{5,21},{6,70},{7,23},{8,72},{9,... | collective-permute-start | bytes 245768 | tf_op jit(solution)/shard_map/ppermute | solution.py:65
  24.9 5.0 %collective-permute-start.6 = (f32[680,128]{1,0:T(8,128)S(1)}, f32[680,128]{1,0:T(8,128)S(1)}, u32[]{:S(2)}, u32[]{:S(2)}) collective-permute-start(f32[680,128]{1,0:T(8,128)S(1)} %get-tuple-element.41), channel_id=1, source_target_pairs={{0,1},{1,0},{2,3},{3,2},{4,5},{5,4},{6,7},{7,6},{8,9},{9,8},{10,11... | collective-permute-start | bytes 1044488 | tf_op jit(solution)/shard_map/ppermute | solution.py:81
  29.3 3.2 %collective-permute-start.7 = (f32[1920,128]{1,0:T(8,128)S(1)}, f32[1920,128]{1,0:T(8,128)S(1)}, u32[]{:S(2)}, u32[]{:S(2)}) collective-permute-start(f32[1920,128]{1,0:T(8,128)S(1)} %next_right.3.after_ref), channel_id=1, source_target_pairs={{0,1},{1,0},{2,3},{3,2},{4,5},{5,4},{6,7},{7,6},{8,9},{9,8},{10,11... | collective-permute-start | bytes 2949128 | tf_op jit(solution)/shard_map/ppermute | solution.py:81
  30.0 7.8 %collective-permute-start.10 = (f32[640,128]{1,0:T(8,128)S(1)}, f32[640,128]{1,0:T(8,128)S(1)}, u32[]{:S(2)}, u32[]{:S(2)}) collective-permute-start(f32[640,128]{1,0:T(8,128)S(1)} %get-tuple-element.46), channel_id=1, source_target_pairs={{0,16},{1,65},{2,66},{3,19},{4,20},{5,69},{6,70},{7,23},{8,72},{9,... | collective-permute-start | bytes 983048 | tf_op jit(solution)/shard_map/ppermute | solution.py:65
  32.7 8.6 %collective-permute-start.8 = (f32[640,128]{1,0:T(8,128)S(1)}, f32[640,128]{1,0:T(8,128)S(1)}, u32[]{:S(2)}, u32[]{:S(2)}) collective-permute-start(f32[640,128]{1,0:T(8,128)S(1)} %get-tuple-element.44), channel_id=1, source_target_pairs={{0,9},{1,32},{2,35},{3,10},{4,13},{5,36},{6,39},{7,14},{8,41},{9,1... | collective-permute-start | bytes 983048 | tf_op jit(solution)/shard_map/ppermute | solution.py:65
  34.2 7.3 %collective-permute-start.9 = (f32[640,128]{1,0:T(8,128)S(1)}, f32[640,128]{1,0:T(8,128)S(1)}, u32[]{:S(2)}, u32[]{:S(2)}) collective-permute-start(f32[640,128]{1,0:T(8,128)S(1)} %get-tuple-element.45), channel_id=1, source_target_pairs={{0,25},{1,96},{2,99},{3,26},{4,29},{5,100},{6,103},{7,30},{8,105},... | collective-permute-start | bytes 983048 | tf_op jit(solution)/shard_map/ppermute | solution.py:65
  41.6 5.4 %collective-permute-start.11 = (f32[160,128]{1,0:T(8,128)S(1)}, f32[160,128]{1,0:T(8,128)S(1)}, u32[]{:S(2)}, u32[]{:S(2)}) collective-permute-start(f32[160,128]{1,0:T(8,128)S(1)} %get-tuple-element.48), channel_id=1, source_target_pairs={{0,33},{1,8},{2,11},{3,34},{4,37},{5,12},{6,15},{7,38},{8,17},{9,4... | collective-permute-start | bytes 245768 | tf_op jit(solution)/shard_map/ppermute | solution.py:65
  42.7 4.4 %collective-permute-start.12 = (f32[160,128]{1,0:T(8,128)S(1)}, f32[160,128]{1,0:T(8,128)S(1)}, u32[]{:S(2)}, u32[]{:S(2)}) collective-permute-start(f32[160,128]{1,0:T(8,128)S(1)} %get-tuple-element.49), channel_id=1, source_target_pairs={{0,97},{1,24},{2,27},{3,98},{4,101},{5,28},{6,31},{7,102},{8,1},{9... | collective-permute-start | bytes 245768 | tf_op jit(solution)/shard_map/ppermute | solution.py:65
  44.6 4.8 %collective-permute-start.13 = (f32[160,128]{1,0:T(8,128)S(1)}, f32[160,128]{1,0:T(8,128)S(1)}, u32[]{:S(2)}, u32[]{:S(2)}) collective-permute-start(f32[160,128]{1,0:T(8,128)S(1)} %get-tuple-element.50), channel_id=1, source_target_pairs={{0,64},{1,17},{2,18},{3,67},{4,68},{5,21},{6,22},{7,71},{8,24},{9,... | collective-permute-start | bytes 245768 | tf_op jit(solution)/shard_map/ppermute | solution.py:65
  49.4 8.1 %collective-permute-start.14 = (f32[200,128]{1,0:T(8,128)S(1)}, f32[200,128]{1,0:T(8,128)S(1)}, u32[]{:S(2)}, u32[]{:S(2)}) collective-permute-start(f32[200,128]{1,0:T(8,128)S(1)} %add_parts.1.a_ref), channel_id=1, source_target_pairs={{0,3},{1,2},{2,5},{3,4},{4,7},{5,6},{6,1},{7,0},{8,11},{9,10},{10,... | collective-permute-start | bytes 307208 | tf_op jit(solution)/shard_map/ppermute | solution.py:76
  53.0 5.1 %collective-permute-start.15 = (f32[200,128]{1,0:T(8,128)S(1)}, f32[200,128]{1,0:T(8,128)S(1)}, u32[]{:S(2)}, u32[]{:S(2)}) collective-permute-start(f32[200,128]{1,0:T(8,128)S(1)} %add_parts.1.a_ref), channel_id=1, source_target_pairs={{0,7},{1,6},{2,1},{3,0},{4,3},{5,2},{6,5},{7,4},{8,15},{9,14},{10,... | collective-permute-start | bytes 307208 | tf_op jit(solution)/shard_map/ppermute | solution.py:76
  54.5 5.7 %collective-permute-start.16 = (f32[200,128]{1,0:T(8,128)S(1)}, f32[200,128]{1,0:T(8,128)S(1)}, u32[]{:S(2)}, u32[]{:S(2)}) collective-permute-start(f32[200,128]{1,0:T(8,128)S(1)} %add_parts.1.a_ref), channel_id=1, source_target_pairs={{0,4},{1,5},{2,6},{3,7},{4,0},{5,1},{6,2},{7,3},{8,12},{9,13},{10,... | collective-permute-start | bytes 307208 | tf_op jit(solution)/shard_map/ppermute | solution.py:76
  60.3 5.6 %collective-permute-start.17 = (f32[160,128]{1,0:T(8,128)S(1)}, f32[160,128]{1,0:T(8,128)S(1)}, u32[]{:S(2)}, u32[]{:S(2)}) collective-permute-start(f32[160,128]{1,0:T(8,128)S(1)} %get-tuple-element.56.a_ref), channel_id=1, source_target_pairs={{0,33},{1,8},{2,11},{3,34},{4,37},{5,12},{6,15},{7,38},{8,17},{9,4... | collective-permute-start | bytes 245768 | tf_op jit(solution)/shard_map/ppermute | solution.py:65
  60.6 5.3 %collective-permute-start.18 = (f32[160,128]{1,0:T(8,128)S(1)}, f32[160,128]{1,0:T(8,128)S(1)}, u32[]{:S(2)}, u32[]{:S(2)}) collective-permute-start(f32[160,128]{1,0:T(8,128)S(1)} %get-tuple-element.56.a_ref), channel_id=1, source_target_pairs={{0,97},{1,24},{2,27},{3,98},{4,101},{5,28},{6,31},{7,102},{8,1},{9... | collective-permute-start | bytes 245768 | tf_op jit(solution)/shard_map/ppermute | solution.py:65
  63.5 4.8 %collective-permute-start.19 = (f32[160,128]{1,0:T(8,128)S(1)}, f32[160,128]{1,0:T(8,128)S(1)}, u32[]{:S(2)}, u32[]{:S(2)}) collective-permute-start(f32[160,128]{1,0:T(8,128)S(1)} %get-tuple-element.56.a_ref), channel_id=1, source_target_pairs={{0,64},{1,17},{2,18},{3,67},{4,68},{5,21},{6,22},{7,71},{8,24},{9,... | collective-permute-start | bytes 245768 | tf_op jit(solution)/shard_map/ppermute | solution.py:65
  68.3 6.6 %collective-permute-start.22 = (f32[640,128]{1,0:T(8,128)S(1)}, f32[640,128]{1,0:T(8,128)S(1)}, u32[]{:S(2)}, u32[]{:S(2)}) collective-permute-start(f32[640,128]{1,0:T(8,128)S(1)} %assemble.1.refs_0_), channel_id=1, source_target_pairs={{0,1},{1,0},{2,3},{3,2},{4,5},{5,4},{6,7},{7,6},{8,9},{9,8},{10,11... | collective-permute-start | bytes 983048 | tf_op jit(solution)/shard_map/ppermute | solution.py:81
  70.6 7.7 %collective-permute-start.21 = (f32[640,128]{1,0:T(8,128)S(1)}, f32[640,128]{1,0:T(8,128)S(1)}, u32[]{:S(2)}, u32[]{:S(2)}) collective-permute-start(f32[640,128]{1,0:T(8,128)S(1)} %assemble.1.refs_0_), channel_id=1, source_target_pairs={{0,16},{1,65},{2,66},{3,19},{4,20},{5,69},{6,70},{7,23},{8,72},{9,... | collective-permute-start | bytes 983048 | tf_op jit(solution)/shard_map/ppermute | solution.py:65
  70.6 10.7 %collective-permute-start.24 = (f32[640,128]{1,0:T(8,128)S(1)}, f32[640,128]{1,0:T(8,128)S(1)}, u32[]{:S(2)}, u32[]{:S(2)}) collective-permute-start(f32[640,128]{1,0:T(8,128)S(1)} %assemble.1.refs_0_), channel_id=1, source_target_pairs={{0,25},{1,96},{2,99},{3,26},{4,29},{5,100},{6,103},{7,30},{8,105},... | collective-permute-start | bytes 983048 | tf_op jit(solution)/shard_map/ppermute | solution.py:65
  72.8 9.1 %collective-permute-start.20 = (f32[640,128]{1,0:T(8,128)S(1)}, f32[640,128]{1,0:T(8,128)S(1)}, u32[]{:S(2)}, u32[]{:S(2)}) collective-permute-start(f32[640,128]{1,0:T(8,128)S(1)} %assemble.1.refs_0_), channel_id=1, source_target_pairs={{0,9},{1,32},{2,35},{3,10},{4,13},{5,36},{6,39},{7,14},{8,41},{9,1... | collective-permute-start | bytes 983048 | tf_op jit(solution)/shard_map/ppermute | solution.py:65
  78.4 4.5 %collective-permute-start.26 = (f32[640,128]{1,0:T(8,128)S(1)}, f32[640,128]{1,0:T(8,128)S(1)}, u32[]{:S(2)}, u32[]{:S(2)}) collective-permute-start(f32[640,128]{1,0:T(8,128)S(1)} %tie.3.refs_0_), channel_id=1, source_target_pairs={{0,1},{1,0},{2,3},{3,2},{4,5},{5,4},{6,7},{7,6},{8,9},{9,8},{10,11... | collective-permute-start | bytes 983048 | tf_op jit(solution)/shard_map/ppermute | solution.py:81
  81.4 4.8 %collective-permute-start.25 = (f32[640,128]{1,0:T(8,128)S(1)}, f32[640,128]{1,0:T(8,128)S(1)}, u32[]{:S(2)}, u32[]{:S(2)}) collective-permute-start(f32[640,128]{1,0:T(8,128)S(1)} %tie.5.refs_1_), channel_id=1, source_target_pairs={{0,1},{1,0},{2,3},{3,2},{4,5},{5,4},{6,7},{7,6},{8,9},{9,8},{10,11... | collective-permute-start | bytes 983048 | tf_op jit(solution)/shard_map/ppermute | solution.py:81
  81.9 4.2 %collective-permute-start.23 = (f32[640,128]{1,0:T(8,128)S(1)}, f32[640,128]{1,0:T(8,128)S(1)}, u32[]{:S(2)}, u32[]{:S(2)}) collective-permute-start(f32[640,128]{1,0:T(8,128)S(1)} %tie.4.refs_0_), channel_id=1, source_target_pairs={{0,1},{1,0},{2,3},{3,2},{4,5},{5,4},{6,7},{7,6},{8,9},{9,8},{10,11... | collective-permute-start | bytes 983048 | tf_op jit(solution)/shard_map/ppermute | solution.py:81

commit v12 on v11

--- a/solution.py
+++ b/solution.py
@@ -34,10 +34,20 @@
     return (x + y + z + c) % 2
 
 
+def core_of(x, y, z, c):
+    return c
+
+
 def place():
     x, y, z, c = (lax.axis_index(a) for a in ("x", "y", "z", "c"))
     half = half_of(x, y, z, c)
-    return half, jnp.where(half == 0, x, z), jnp.where(half == 0, z, x)
+    return half, jnp.where(half == 0, x, z), jnp.where(half == 0, z, y)
+
+
+def other_place():
+    x, y, z, c = (lax.axis_index(a) for a in ("x", "y", "z", "c"))
+    half = 1 - half_of(x, y, z, c)
+    return half, jnp.where(half == 0, x, z), jnp.where(half == 0, z, y)
 
 
 def index(z, x, y, c):
@@ -54,53 +64,43 @@
     ]
 
 
-def ring_x_or_z(values, phase, shifts=SHIFTS, halves=True):
+def ring(values, phase, shifts=SHIFTS, orders=("xzy", "zyx"), group=half_of):
     out = []
     for k, value in zip(shifts, values):
         pairs = []
         for z, x, y, c in everyone():
-            along_x = (half_of(x, y, z, c) if halves else c) == phase
-            to = (z, (x + k) % SIZES[1], y) if along_x else ((z + k) % SIZES[0], x, y)
-            pairs.append((index(z, x, y, c), index(*to, (c + k) % 2 if halves else c)))
+            to = {"z": z, "x": x, "y": y}
+            axis = orders[group(x, y, z, c)][phase]
+            to[axis] = (to[axis] + k) % SIZES[AXES.index(axis)]
+            core = c if group is core_of else (c + k) % 2
+            pairs.append((index(z, x, y, c), index(*to.values(), core)))
         out.append(lax.ppermute(value, AXES, pairs))
     return out
 
 
-def ring_y(value):
-    out = []
-    for k in SHIFTS:
-        pairs = [
-            (index(z, x, y, c), index(z, x, (y + k) % SIZES[2], (c + k) % 2))
-            for z, x, y, c in everyone()
-        ]
-        out.append(lax.ppermute(value, AXES, pairs))
-    return out
-
-
 def swap(value):
     return lax.ppermute(value, "c", [(0, 1), (1, 0)])
 
 
-def merge_kernel(width, g_hbm, e_hbm, q_hbm, m_ref, p_ref, g_ref, e_ref, q_ref, sems):
-    rows, columns = g_ref.shape
+def merge_kernel(cuts, g_hbm, e_hbm, q_hbm, m_ref, p_ref, g_ref, e_ref, q_ref, sems):
+    rows = g_ref.shape[0]
     rank = q_ref.shape[0]
-    steps = columns // width
 
     def copies(i):
-        at = pl.ds(i * width, width)
+        at = pl.ds(cuts[i], cuts[i + 1] - cuts[i])
         return [
             pltpu.make_async_copy(src.at[:, at], dst.at[:, at], sems.at[n, i])
             for n, (src, dst) in enumerate(((g_hbm, g_ref), (e_hbm, e_ref), (q_hbm, q_ref)))
         ]
 
-    for i in range(steps):
+    for i in range(len(cuts) - 1):
         for c in copies(i):
             c.start()
     acc = jnp.zeros((rows, rank), F32)
-    for i in range(steps):
+    for i in range(len(cuts) - 1):
         for c in copies(i):
             c.wait()
-        at = pl.ds(i * width, width)
+        at = pl.ds(cuts[i], cuts[i + 1] - cuts[i])
         m = (g_ref[:, at].astype(F32) + e_ref[:, at].astype(F32)).astype(BF16)
         m_ref[:, at] = m
         acc = acc + lax.dot_general(
@@ -130,12 +130,13 @@
 def merge(gradient, error, q_start):
     rows, columns = gradient.shape
     rank = q_start.shape[0]
-    width = 1024
+    step = columns // 20
+    cuts = [n * step for n in (0, 2, 4, 6, 8, 10, 12, 14, 16, 18, 19, 20)]
     gradient, error, q_start = (
         pltpu.with_memory_space_constraint(a, pltpu.HBM) for a in (gradient, error, q_start)
     )
     return pl.pallas_call(
-        functools.partial(merge_kernel, width),
+        functools.partial(merge_kernel, cuts),
         out_shape=[pltpu.VMEM((rows, columns), BF16), pltpu.VMEM((rank * rows // 128, 128), F32)],
         in_specs=[ANY, ANY, ANY],
         out_specs=[WHOLE, WHOLE],
@@ -143,7 +144,7 @@
             pltpu.VMEM((rows, columns), BF16),
             pltpu.VMEM((rows, columns), BF16),
             pltpu.VMEM((rank, columns), BF16),
-            pltpu.SemaphoreType.DMA((3, columns // width)),
+            pltpu.SemaphoreType.DMA((3, len(cuts) - 1)),
         ],
         compiler_params=params(24),
         cost_estimate=cost(2 * rank * rows * columns, 4 * rows * columns),
@@ -166,8 +167,7 @@
 
 
 def quarters_of(own, turns):
-    half, one, two = place()
-    half, turn = (half, one) if own else (1 - half, two)
+    half, turn, _ = place() if own else other_place()
     return [half * QUARTERS + (turn + k) % QUARTERS for k in turns]
 
 
@@ -289,60 +289,49 @@
     )(kept, got, weight)
 
 
-def add_quarters_kernel(a_ref, b_ref, c_ref, d_ref, *out):
+def add_quarters_kernel(a_ref, b_ref, c_ref, d_ref, ext_ref, *out):
     size = a_ref.shape[0] // QUARTERS
     for k, ref in zip((0,) + SHIFTS, out):
         at = pl.ds(pl.multiple_of((place()[2] + k) % QUARTERS * size, size), size)
-        ref[...] = (a_ref[at] + b_ref[at]) + (c_ref[at] + d_ref[at])
-
-
-def add_quarters(parts):
+        ref[:size] = (a_ref[at] + b_ref[at]) + (c_ref[at] + d_ref[at])
+        ref[size:] = ext_ref[...]
+
+
+def add_quarters(parts, ext):
     size = parts[0].shape[0] // QUARTERS
     return pl.pallas_call(
         add_quarters_kernel,
-        out_shape=[jax.ShapeDtypeStruct((size, 128), F32)] * QUARTERS,
-        in_specs=[WHOLE] * QUARTERS,
+        out_shape=[jax.ShapeDtypeStruct((size + ext.shape[0], 128), F32)] * QUARTERS,
+        in_specs=[WHOLE] * (QUARTERS + 1),
         out_specs=[WHOLE] * QUARTERS,
         compiler_params=params(8),
         name="add_quarters",
-    )(*parts)
-
-
-def add_parts_kernel(a_ref, b_ref, c_ref, d_ref, ext_ref, out_ref):
-    size = a_ref.shape[0]
-    out_ref[:size] = (a_ref[...] + b_ref[...]) + (c_ref[...] + d_ref[...])
-    out_ref[size:] = ext_ref[...]
-
-
-def add_parts(parts, ext):
-    return pl.pallas_call(
-        add_parts_kernel,
-        out_shape=jax.ShapeDtypeStruct((parts[0].shape[0] + ext.shape[0], 128), F32),
-        in_specs=[WHOLE] * 5,
-        out_specs=WHOLE,
-        compiler_params=params(8),
-        name="add_parts",
     )(*parts, ext)
 
 
-def across_kernel(a_ref, b_ref, c_ref, d_ref, out_ref, ext_ref):
-    size = out_ref.shape[0]
+def across_kernel(half_along_y, a_ref, b_ref, c_ref, d_ref, out_ref, ext_ref):
     grams = ext_ref.shape[0] - ROWS
+    size = a_ref.shape[0] - grams - ROWS
     refs = (a_ref, b_ref, c_ref, d_ref)
     peaks = [r[size + grams : size + grams + 1, :1] for r in refs]
     top = jnp.maximum(jnp.maximum(peaks[0], peaks[1]), jnp.maximum(peaks[2], peaks[3]))
     a, b, c, d = (r[:size] * (k / top) for r, k in zip(refs, peaks))
-    out_ref[...] = (a + b) + (c + d)
+    out_ref[:size] = (a + b) + (c + d)
     a, b, c, d = (r[size : size + grams] for r in refs)
-    ext_ref[:grams] = (a + b) + (c + d)
+    gram = jnp.where(place()[0] == half_along_y, (a + b) + (c + d), a)
+    ext_ref[:grams] = gram
     ext_ref[grams:] = jnp.broadcast_to(top, (ROWS, 128))
-
-
-def across(parts, extra):
-    return pl.pallas_call(
-        across_kernel,
+    if out_ref.shape[0] > size:
+        out_ref[size : size + grams] = gram
+        out_ref[size + grams :] = jnp.broadcast_to(top, (ROWS, 128))
+
+
+def across(half_along_y, parts, extra, keep):
+    rows = parts[0].shape[0]
+    return pl.pallas_call(
+        functools.partial(across_kernel, half_along_y),
         out_shape=[
-            jax.ShapeDtypeStruct((parts[0].shape[0] - extra, 128), F32),
+            jax.ShapeDtypeStruct((rows if keep else rows - extra, 128), F32),
             pltpu.VMEM((extra, 128), F32),
         ],
         in_specs=[WHOLE] * 4,
@@ -458,8 +447,7 @@
     bases = []
     for n, (own, k) in enumerate(sources):
         t_ref = refs[n]
-        half, one, two = place()
-        half, turn = (half, one) if own else (1 - half, two)
+        half, turn, _ = place() if own else other_place()
         quarter = (turn + QUARTERS - k) % QUARTERS
         base = (half * QUARTERS + quarter) * columns
         bases.append(base)
@@ -542,25 +530,26 @@
     rank = q_start.shape[0]
     replicas = SIZES[0] * SIZES[1]
     merged, p = merge(gradient[0], error[0], q_start)
-    a, b, c = ring_x_or_z([p] * 3, 0, halves=False)
+    a, b, c = ring([p] * 3, 0, orders=("xz", "zx"), group=core_of)
     p = (p + a) + (b + c)
     sent, ext, p_mean, pieces = first_right(
-        (2,), (p, *ring_x_or_z([p] * 3, 1, halves=False)), merged, rank, replicas
+        (2,), (p, *ring([p] * 3, 1, orders=("xz", "zx"), group=core_of)), merged, rank, replicas
     )
     got = swap(sent)
     sent = next_right(False, (1, 3, 0), pieces, merged, ext)
     got_next = swap(sent)
     kept = next_right(True, (2,), pieces, merged, sent)
     two, ext, weight = first_pair(kept, got, ext)
-    (two,) = ring_x_or_z((two,), 0, (2,))
+    (two,) = ring((two,), 0, (2,))
     kept = next_right(True, (1, 3, 0), pieces, merged, weight)
     *near, own = next_pair(kept, got_next, weight)
-    own, *sent = add_quarters((own, *ring_x_or_z(near, 0, (1, 3)), two))
-    part = add_parts((own, *ring_x_or_z(sent, 1)), ext)
-    total, ext = across((part, *ring_y(part)), ext.shape[0])
+    own, *sent = add_quarters((own, *ring(near, 0, (1, 3)), two), ext)
+    extra = ext.shape[0]
+    part, _ = across(1, (own, *ring(sent, 1)), extra, True)
+    total, ext = across(0, (part, *ring([part] * 3, 2)), extra, False)
     solve, left, p_hat = factor(ext, p_mean, replicas)
-    total = assemble((total, *ring_x_or_z([total] * 3, 1)), solve)
-    two, one, three = ring_x_or_z([total] * 3, 0, (2, 1, 3))
+    total = assemble((total, *ring([total] * 3, 1)), solve)
+    two, one, three = ring([total] * 3, 0, (2, 1, 3))
 
     def write(sources, totals, *after):
         return result(sources, totals, merged, solve, left, *after)

time: 89.1 us -> 89.6 us (level)
  waiting for transfers between devices: 27.6 us -> 25.9 us
  starting transfers between devices: 37.6 us -> 39 us
    ppermute x21, waiting for transfers between devices: 27.6 us -> 25.9 us  [ring(): out.append(lax.ppermute(value, AXES, pairs))]
    ppermute x21, starting transfers between devices: 29.6 us -> 30.6 us  [ring(): out.append(lax.ppermute(value, AXES, pairs))]
  transfers between devices with their start and end apart: 27 -> 27, of which waited for: 17 -> 16; matrix products, arithmetic and copies ran while one was open for 0% -> 0% of each run, Pallas kernels for 15% -> 15%
where the time goes in v12:
time: 89.6 us; the launch traced here: 89.5 us
  starting transfers between devices  39 us (44%)
  waiting for transfers between devices  25.9 us (29%)
  Pallas kernels  23.6 us (26%)
  between operations  0.97 us (1%)
    ppermute x21, starting transfers between devices, ring(): out.append(lax.ppermute(value, AXES, pairs))  30.6 us
    ppermute x21, waiting for transfers between devices, ring(): out.append(lax.ppermute(value, AXES, pairs))  25.9 us
    pallas_call x5, Pallas kernels, result(): pl.pallas_call(functools.partial(result_kernel, sources, bool(last), quar...  11.3 us
    ppermute x6, starting transfers between devices, swap(): return lax.ppermute(value, 'c', [(0, 1), (1, 0)])  8.35 us
    pallas_call x1, Pallas kernels, merge(): pl.pallas_call(functools.partial(merge_kernel, cuts), out_shape=[pltpu.VM...  6.21 us
    pallas_call x3, Pallas kernels, next_right(): pl.pallas_call(functools.partial(next_right_kernel, own, turns), out_shap...  2.25 us
    pallas_call x1, Pallas kernels, factor(): pl.pallas_call(functools.partial(factor_kernel, replicas), out_shape=[jax...  2.01 us
  transfers between devices with their start and end apart: 27, of which 16 were waited for; matrix products, arithmetic and copies ran while one was open for 0% of the time, Pallas kernels for 15%

profile of v12, /device:TPU:1, one launch (start us, length us, event | category | flops | bytes accessed | tf_op | source)
XLA Modules:
  0.0 89.5 jit_solution(1533307404873769617)
XLA Ops:
  0.6 6.2 %merge.1 = (bf16[320,10240]{1,0:T(8,128)(2,1)S(1)}, f32[160,128]{1,0:T(8,128)S(1)}) custom-call(bf16[320,10240]{1,0:T(8,128)(2,1)} %bitcast.3, bf16[320,10240]{1,0:T(8,128)(2,1)} %bitcast.4, bf16[64,10240]{1,0:T(8,128)(2,1)} %q_hbm.1), custom_call_target="tpu_custom_call" | custom-call | flops 419430400 | bytes 13107200 | tf_op jit(solution)/shard_map/merge/pallas_call | solution.py:138
  6.8 2.5 %collective-permute-start = (f32[160,128]{1,0:T(8,128)S(1)}, f32[160,128]{1,0:T(8,128)S(1)}, u32[]{:S(2)}, u32[]{:S(2)}) collective-permute-start(f32[160,128]{1,0:T(8,128)S(1)} %get-tuple-element.38), channel_id=1, source_target_pairs={{0,8},{1,33},{2,10},{3,35},{4,12},{5,37},{6,14},{7,39},{8,16},{9,4... | collective-permute-start | bytes 245768 | tf_op jit(solution)/shard_map/ppermute | solution.py:77
  9.4 2.2 %collective-permute-start.1 = (f32[160,128]{1,0:T(8,128)S(1)}, f32[160,128]{1,0:T(8,128)S(1)}, u32[]{:S(2)}, u32[]{:S(2)}) collective-permute-start(f32[160,128]{1,0:T(8,128)S(1)} %get-tuple-element.38), channel_id=1, source_target_pairs={{0,24},{1,97},{2,26},{3,99},{4,28},{5,101},{6,30},{7,103},{8,0},{9... | collective-permute-start | bytes 245768 | tf_op jit(solution)/shard_map/ppermute | solution.py:77
  11.6 1.2 %collective-permute-start.2 = (f32[160,128]{1,0:T(8,128)S(1)}, f32[160,128]{1,0:T(8,128)S(1)}, u32[]{:S(2)}, u32[]{:S(2)}) collective-permute-start(f32[160,128]{1,0:T(8,128)S(1)} %get-tuple-element.38), channel_id=1, source_target_pairs={{0,16},{1,65},{2,18},{3,67},{4,20},{5,69},{6,22},{7,71},{8,24},{9,... | collective-permute-start | bytes 245768 | tf_op jit(solution)/shard_map/ppermute | solution.py:77
  12.8 0.8 collective-permute-done
  13.6 0.0 collective-permute-done.1
  13.6 3.1 %collective-permute-done.2 = f32[160,128]{1,0:T(8,128)S(1)} collective-permute-done((f32[160,128]{1,0:T(8,128)S(1)}, f32[160,128]{1,0:T(8,128)S(1)}, u32[]{:S(2)}, u32[]{:S(2)}) %collective-permute-start.2) | collective-permute-done | bytes 81952 | tf_op jit(solution)/shard_map/ppermute | solution.py:77
  16.7 1.0 %collective-permute-start.3 = (f32[160,128]{1,0:T(8,128)S(1)}, f32[160,128]{1,0:T(8,128)S(1)}, u32[]{:S(2)}, u32[]{:S(2)}) collective-permute-start(f32[160,128]{1,0:T(8,128)S(1)} %add_add_fusion.a_ref), channel_id=1, source_target_pairs={{0,32},{1,9},{2,34},{3,11},{4,36},{5,13},{6,38},{7,15},{8,40},{9,1... | collective-permute-start | bytes 245768 | tf_op jit(solution)/shard_map/ppermute | solution.py:77
  17.7 1.8 %collective-permute-start.4 = (f32[160,128]{1,0:T(8,128)S(1)}, f32[160,128]{1,0:T(8,128)S(1)}, u32[]{:S(2)}, u32[]{:S(2)}) collective-permute-start(f32[160,128]{1,0:T(8,128)S(1)} %add_add_fusion.a_ref), channel_id=1, source_target_pairs={{0,96},{1,25},{2,98},{3,27},{4,100},{5,29},{6,102},{7,31},{8,104},... | collective-permute-start | bytes 245768 | tf_op jit(solution)/shard_map/ppermute | solution.py:77
  19.4 1.2 %collective-permute-start.5 = (f32[160,128]{1,0:T(8,128)S(1)}, f32[160,128]{1,0:T(8,128)S(1)}, u32[]{:S(2)}, u32[]{:S(2)}) collective-permute-start(f32[160,128]{1,0:T(8,128)S(1)} %add_add_fusion.a_ref), channel_id=1, source_target_pairs={{0,64},{1,17},{2,66},{3,19},{4,68},{5,21},{6,70},{7,23},{8,72},{9,... | collective-permute-start | bytes 245768 | tf_op jit(solution)/shard_map/ppermute | solution.py:77
  20.7 0.6 collective-permute-done.3.b_ref
  21.3 0.0 collective-permute-done.4.c_ref
  21.3 3.0 %collective-permute-done.5.d_ref = f32[160,128]{1,0:T(8,128)S(1)} collective-permute-done((f32[160,128]{1,0:T(8,128)S(1)}, f32[160,128]{1,0:T(8,128)S(1)}, u32[]{:S(2)}, u32[]{:S(2)}) %collective-permute-start.5) | collective-permute-done | bytes 81952 | tf_op jit(solution)/shard_map/ppermute | solution.py:77
  24.2 0.7 first_right.1
  24.9 3.5 %collective-permute-start.6 = (f32[680,128]{1,0:T(8,128)S(1)}, f32[680,128]{1,0:T(8,128)S(1)}, u32[]{:S(2)}, u32[]{:S(2)}) collective-permute-start(f32[680,128]{1,0:T(8,128)S(1)} %get-tuple-element.42), channel_id=1, source_target_pairs={{0,1},{1,0},{2,3},{3,2},{4,5},{5,4},{6,7},{7,6},{8,9},{9,8},{10,11... | collective-permute-start | bytes 1044488 | tf_op jit(solution)/shard_map/ppermute | solution.py:82
  28.5 0.9 %next_right.3.after_ref = f32[1920,128]{1,0:T(8,128)S(1)} custom-call(bf16[192,320]{1,0:T(8,128)(2,1)S(1)} %get-tuple-element.40.pieces_ref, bf16[320,10240]{1,0:T(8,128)(2,1)S(1)} %get-tuple-element.39.m_ref, f32[40,128]{1,0:T(8,128)S(1)} %get-tuple-element.41.after_ref.ext_ref), custom_call_target="tpu_custom_call" | custom-call | flops 8589934592 | bytes 1048576 | tf_op jit(solution)/shard_map/next_right/pallas_call | solution.py:233
  29.4 0.1 collective-permute-start.7
  29.5 0.4 next_right.4.kept_ref
  29.9 0.0 collective-permute-done.6.got_ref
  30.0 0.1 first_pair.1
  30.1 1.6 %collective-permute-start.10 = (f32[640,128]{1,0:T(8,128)S(1)}, f32[640,128]{1,0:T(8,128)S(1)}, u32[]{:S(2)}, u32[]{:S(2)}) collective-permute-start(f32[640,128]{1,0:T(8,128)S(1)} %get-tuple-element.47), channel_id=1, source_target_pairs={{0,16},{1,65},{2,66},{3,19},{4,20},{5,69},{6,70},{7,23},{8,72},{9,... | collective-permute-start | bytes 983048 | tf_op jit(solution)/shard_map/ppermute | solution.py:77
  31.6 0.9 %next_right.5.kept_ref = f32[1920,128]{1,0:T(8,128)S(1)} custom-call(bf16[192,320]{1,0:T(8,128)(2,1)S(1)} %get-tuple-element.40.pieces_ref, bf16[320,10240]{1,0:T(8,128)(2,1)S(1)} %get-tuple-element.39.m_ref, f32[16,128]{1,0:T(8,128)S(1)} %get-tuple-element.43.after_ref.weight_ref), custom_call_target="tpu_custom_call" | custom-call | flops 8589934592 | bytes 1048576 | tf_op jit(solution)/shard_map/next_right/pallas_call | solution.py:233
  32.6 0.2 next_pair.1
  32.8 1.4 %collective-permute-start.8 = (f32[640,128]{1,0:T(8,128)S(1)}, f32[640,128]{1,0:T(8,128)S(1)}, u32[]{:S(2)}, u32[]{:S(2)}) collective-permute-start(f32[640,128]{1,0:T(8,128)S(1)} %get-tuple-element.45), channel_id=1, source_target_pairs={{0,9},{1,32},{2,35},{3,10},{4,13},{5,36},{6,39},{7,14},{8,41},{9,1... | collective-permute-start | bytes 983048 | tf_op jit(solution)/shard_map/ppermute | solution.py:77
  34.3 1.6 %collective-permute-start.9 = (f32[640,128]{1,0:T(8,128)S(1)}, f32[640,128]{1,0:T(8,128)S(1)}, u32[]{:S(2)}, u32[]{:S(2)}) collective-permute-start(f32[640,128]{1,0:T(8,128)S(1)} %get-tuple-element.46), channel_id=1, source_target_pairs={{0,25},{1,96},{2,99},{3,26},{4,29},{5,100},{6,103},{7,30},{8,105},... | collective-permute-start | bytes 983048 | tf_op jit(solution)/shard_map/ppermute | solution.py:77
  35.8 2.0 %collective-permute-done.10.d_ref = f32[640,128]{1,0:T(8,128)S(1)} collective-permute-done((f32[640,128]{1,0:T(8,128)S(1)}, f32[640,128]{1,0:T(8,128)S(1)}, u32[]{:S(2)}, u32[]{:S(2)}) %collective-permute-start.10) | collective-permute-done | bytes 327712 | tf_op jit(solution)/shard_map/ppermute | solution.py:77
  37.9 3.5 %collective-permute-done.8.b_ref = f32[640,128]{1,0:T(8,128)S(1)} collective-permute-done((f32[640,128]{1,0:T(8,128)S(1)}, f32[640,128]{1,0:T(8,128)S(1)}, u32[]{:S(2)}, u32[]{:S(2)}) %collective-permute-start.8) | collective-permute-done | bytes 327712 | tf_op jit(solution)/shard_map/ppermute | solution.py:77
  41.4 0.2 collective-permute-done.9.c_ref
  41.6 0.1 add_quarters.1
  41.7 2.4 %collective-permute-start.11 = (f32[200,128]{1,0:T(8,128)S(1)}, f32[200,128]{1,0:T(8,128)S(1)}, u32[]{:S(2)}, u32[]{:S(2)}) collective-permute-start(f32[200,128]{1,0:T(8,128)S(1)} %get-tuple-element.50), channel_id=1, source_target_pairs={{0,33},{1,2},{2,5},{3,34},{4,37},{5,6},{6,1},{7,38},{8,11},{9,40},... | collective-permute-start | bytes 307208 | tf_op jit(solution)/shard_map/ppermute | solution.py:77
  44.0 1.5 %collective-permute-start.12 = (f32[200,128]{1,0:T(8,128)S(1)}, f32[200,128]{1,0:T(8,128)S(1)}, u32[]{:S(2)}, u32[]{:S(2)}) collective-permute-start(f32[200,128]{1,0:T(8,128)S(1)} %get-tuple-element.51), channel_id=1, source_target_pairs={{0,97},{1,6},{2,1},{3,98},{4,101},{5,2},{6,5},{7,102},{8,15},{9,10... | collective-permute-start | bytes 307208 | tf_op jit(solution)/shard_map/ppermute | solution.py:77
  45.6 1.1 %collective-permute-start.13 = (f32[200,128]{1,0:T(8,128)S(1)}, f32[200,128]{1,0:T(8,128)S(1)}, u32[]{:S(2)}, u32[]{:S(2)}) collective-permute-start(f32[200,128]{1,0:T(8,128)S(1)} %get-tuple-element.52), channel_id=1, source_target_pairs={{0,64},{1,5},{2,6},{3,67},{4,68},{5,1},{6,2},{7,71},{8,12},{9,73},... | collective-permute-start | bytes 307208 | tf_op jit(solution)/shard_map/ppermute | solution.py:77
  46.7 1.2 %collective-permute-done.11.b_ref = f32[200,128]{1,0:T(8,128)S(1)} collective-permute-done((f32[200,128]{1,0:T(8,128)S(1)}, f32[200,128]{1,0:T(8,128)S(1)}, u32[]{:S(2)}, u32[]{:S(2)}) %collective-permute-start.11) | collective-permute-done | bytes 102432 | tf_op jit(solution)/shard_map/ppermute | solution.py:77
  47.8 0.3 collective-permute-done.12.c_ref
  48.1 2.8 %collective-permute-done.13.d_ref = f32[200,128]{1,0:T(8,128)S(1)} collective-permute-done((f32[200,128]{1,0:T(8,128)S(1)}, f32[200,128]{1,0:T(8,128)S(1)}, u32[]{:S(2)}, u32[]{:S(2)}) %collective-permute-start.13) | collective-permute-done | bytes 102432 | tf_op jit(solution)/shard_map/ppermute | solution.py:77
  50.9 0.7 across.2
  51.5 1.0 %collective-permute-start.14 = (f32[200,128]{1,0:T(8,128)S(1)}, f32[200,128]{1,0:T(8,128)S(1)}, u32[]{:S(2)}, u32[]{:S(2)}) collective-permute-start(f32[200,128]{1,0:T(8,128)S(1)} %get-tuple-element.53.a_ref), channel_id=1, source_target_pairs={{0,3},{1,8},{2,11},{3,4},{4,7},{5,12},{6,15},{7,0},{8,17},{9,10},{... | collective-permute-start | bytes 307208 | tf_op jit(solution)/shard_map/ppermute | solution.py:77
  52.5 2.0 %collective-permute-start.15 = (f32[200,128]{1,0:T(8,128)S(1)}, f32[200,128]{1,0:T(8,128)S(1)}, u32[]{:S(2)}, u32[]{:S(2)}) collective-permute-start(f32[200,128]{1,0:T(8,128)S(1)} %get-tuple-element.53.a_ref), channel_id=1, source_target_pairs={{0,7},{1,24},{2,27},{3,0},{4,3},{5,28},{6,31},{7,4},{8,1},{9,14},{... | collective-permute-start | bytes 307208 | tf_op jit(solution)/shard_map/ppermute | solution.py:77
  54.5 0.5 collective-permute-start.16
  55.0 2.1 %collective-permute-done.14.b_ref = f32[200,128]{1,0:T(8,128)S(1)} collective-permute-done((f32[200,128]{1,0:T(8,128)S(1)}, f32[200,128]{1,0:T(8,128)S(1)}, u32[]{:S(2)}, u32[]{:S(2)}) %collective-permute-start.14) | collective-permute-done | bytes 102432 | tf_op jit(solution)/shard_map/ppermute | solution.py:77
  57.1 2.4 %collective-permute-done.16.d_ref = f32[200,128]{1,0:T(8,128)S(1)} collective-permute-done((f32[200,128]{1,0:T(8,128)S(1)}, f32[200,128]{1,0:T(8,128)S(1)}, u32[]{:S(2)}, u32[]{:S(2)}) %collective-permute-start.16) | collective-permute-done | bytes 102432 | tf_op jit(solution)/shard_map/ppermute | solution.py:77
  59.5 0.1 across.3
  59.6 2.5 %collective-permute-start.17 = (f32[160,128]{1,0:T(8,128)S(1)}, f32[160,128]{1,0:T(8,128)S(1)}, u32[]{:S(2)}, u32[]{:S(2)}) collective-permute-start(f32[160,128]{1,0:T(8,128)S(1)} %get-tuple-element.58.a_ref), channel_id=1, source_target_pairs={{0,33},{1,2},{2,5},{3,34},{4,37},{5,6},{6,1},{7,38},{8,11},{9,40},... | collective-permute-start | bytes 245768 | tf_op jit(solution)/shard_map/ppermute | solution.py:77
  62.1 1.5 %collective-permute-start.18 = (f32[160,128]{1,0:T(8,128)S(1)}, f32[160,128]{1,0:T(8,128)S(1)}, u32[]{:S(2)}, u32[]{:S(2)}) collective-permute-start(f32[160,128]{1,0:T(8,128)S(1)} %get-tuple-element.58.a_ref), channel_id=1, source_target_pairs={{0,97},{1,6},{2,1},{3,98},{4,101},{5,2},{6,5},{7,102},{8,15},{9,10... | collective-permute-start | bytes 245768 | tf_op jit(solution)/shard_map/ppermute | solution.py:77
  63.6 1.1 %collective-permute-start.19 = (f32[160,128]{1,0:T(8,128)S(1)}, f32[160,128]{1,0:T(8,128)S(1)}, u32[]{:S(2)}, u32[]{:S(2)}) collective-permute-start(f32[160,128]{1,0:T(8,128)S(1)} %get-tuple-element.58.a_ref), channel_id=1, source_target_pairs={{0,64},{1,5},{2,6},{3,67},{4,68},{5,1},{6,2},{7,71},{8,12},{9,73},... | collective-permute-start | bytes 245768 | tf_op jit(solution)/shard_map/ppermute | solution.py:77
  64.7 2.0 %factor.1 = (bf16[64,384]{1,0:T(8,128)(2,1)S(1)}, bf16[320,64]{1,0:T(8,128)(2,1)S(1)}, f32[64,320]{1,0:T(8,128)S(1)}) custom-call(f32[40,128]{1,0:T(8,128)S(1)} %get-tuple-element.54.ext_ref, f32[64,320]{1,0:T(8,128)S(1)} %get-tuple-element.55.p_ref), custom_call_target="tpu_custom_call" | custom-call | flops 4294967296 | bytes 1048576 | tf_op jit(solution)/shard_map/factor/pallas_call | solution.py:413
  66.7 0.0 collective-permute-done.17.b_ref
  66.7 0.0 collective-permute-done.18.c_ref
  66.7 1.7 %collective-permute-done.19.d_ref = f32[160,128]{1,0:T(8,128)S(1)} collective-permute-done((f32[160,128]{1,0:T(8,128)S(1)}, f32[160,128]{1,0:T(8,128)S(1)}, u32[]{:S(2)}, u32[]{:S(2)}) %collective-permute-start.19) | collective-permute-done | bytes 81952 | tf_op jit(solution)/shard_map/ppermute | solution.py:77
  68.4 2.7 %collective-permute-start.22 = (f32[640,128]{1,0:T(8,128)S(1)}, f32[640,128]{1,0:T(8,128)S(1)}, u32[]{:S(2)}, u32[]{:S(2)}) collective-permute-start(f32[640,128]{1,0:T(8,128)S(1)} %assemble.1.refs_0_), channel_id=1, source_target_pairs={{0,1},{1,0},{2,3},{3,2},{4,5},{5,4},{6,7},{7,6},{8,9},{9,8},{10,11... | collective-permute-start | bytes 983048 | tf_op jit(solution)/shard_map/ppermute | solution.py:82
  71.1 2.5 %collective-permute-start.24 = (f32[640,128]{1,0:T(8,128)S(1)}, f32[640,128]{1,0:T(8,128)S(1)}, u32[]{:S(2)}, u32[]{:S(2)}) collective-permute-start(f32[640,128]{1,0:T(8,128)S(1)} %assemble.1.refs_0_), channel_id=1, source_target_pairs={{0,25},{1,96},{2,99},{3,26},{4,29},{5,100},{6,103},{7,30},{8,105},... | collective-permute-start | bytes 983048 | tf_op jit(solution)/shard_map/ppermute | solution.py:77
  73.6 0.0 collective-permute-start.20
  73.6 2.2 %result.5 = (bf16[320,10240]{1,0:T(8,128)(2,1)}, f32[64,10240]{1,0:T(8,128)}, f32[8,128]{1,0:T(8,128)}) custom-call(bf16[64,384]{1,0:T(8,128)(2,1)S(1)} %get-tuple-element.56.after_ref.solve_ref, bf16[320,64]{1,0:T(8,128)(2,1)S(1)} %get-tuple-element.57.left_ref, bf16[320,10240]{1,0:T(8,128)(2,1)S(1)} %get-tuple-element.39.m_ref, f32[640,128]{1,0:T(8,128)S(1)} %assemble.1.refs_0_), custom_call_target="tpu_custom_call" | custom-call | flops 8589934592 | bytes 1048576 | tf_op jit(solution)/shard_map/result/pallas_call | solution.py:491
  75.8 1.6 %result.6 = (bf16[320,10240]{1,0:T(8,128)(2,1)}, f32[64,10240]{1,0:T(8,128)}, f32[8,128]{1,0:T(8,128)S(1)}) custom-call(bf16[64,384]{1,0:T(8,128)(2,1)S(1)} %get-tuple-element.56.after_ref.solve_ref, bf16[320,64]{1,0:T(8,128)(2,1)S(1)} %get-tuple-element.57.left_ref, ...), custom_call_target="tpu_custom_call", output_to_operand_aliasing={{0}: (4, {}), {1}: (5, {})} | custom-call | flops 8589934592 | bytes 1048576 | tf_op jit(solution)/shard_map/result/pallas_call | solution.py:491
  77.4 1.5 %collective-permute-done.21.value_ref = f32[640,128]{1,0:T(8,128)S(1)} collective-permute-done((f32[640,128]{1,0:T(8,128)S(1)}, f32[640,128]{1,0:T(8,128)S(1)}, u32[]{:S(2)}, u32[]{:S(2)}) %collective-permute-start.21) | collective-permute-done | bytes 327712 | tf_op jit(solution)/shard_map/ppermute | solution.py:77
  78.9 1.1 %collective-permute-start.26 = (f32[640,128]{1,0:T(8,128)S(1)}, f32[640,128]{1,0:T(8,128)S(1)}, u32[]{:S(2)}, u32[]{:S(2)}) collective-permute-start(f32[640,128]{1,0:T(8,128)S(1)} %tie.3.refs_0_), channel_id=1, source_target_pairs={{0,1},{1,0},{2,3},{3,2},{4,5},{5,4},{6,7},{7,6},{8,9},{9,8},{10,11... | collective-permute-start | bytes 983048 | tf_op jit(solution)/shard_map/ppermute | solution.py:82
  79.9 1.6 %result.7 = (bf16[320,10240]{1,0:T(8,128)(2,1)}, f32[64,10240]{1,0:T(8,128)}, f32[8,128]{1,0:T(8,128)S(1)}) custom-call(bf16[64,384]{1,0:T(8,128)(2,1)S(1)} %get-tuple-element.56.after_ref.solve_ref, bf16[320,64]{1,0:T(8,128)(2,1)S(1)} %get-tuple-element.57.left_ref, ...), custom_call_target="tpu_custom_call", output_to_operand_aliasing={{0}: (4, {}), {1}: (5, {})} | custom-call | flops 8589934592 | bytes 1048576 | tf_op jit(solution)/shard_map/result/pallas_call | solution.py:491
  81.5 0.7 collective-permute-done.24.value_ref
  82.2 0.1 collective-permute-done.20.value_ref
  82.4 0.9 %collective-permute-start.23 = (f32[640,128]{1,0:T(8,128)S(1)}, f32[640,128]{1,0:T(8,128)S(1)}, u32[]{:S(2)}, u32[]{:S(2)}) collective-permute-start(f32[640,128]{1,0:T(8,128)S(1)} %tie.4.refs_0_), channel_id=1, source_target_pairs={{0,1},{1,0},{2,3},{3,2},{4,5},{5,4},{6,7},{7,6},{8,9},{9,8},{10,11... | collective-permute-start | bytes 983048 | tf_op jit(solution)/shard_map/ppermute | solution.py:82
  83.3 0.0 collective-permute-done.26.refs_2_
  83.3 3.3 %result.8 = (bf16[320,10240]{1,0:T(8,128)(2,1)}, f32[64,10240]{1,0:T(8,128)}, f32[8,128]{1,0:T(8,128)}) custom-call(bf16[64,384]{1,0:T(8,128)(2,1)S(1)} %get-tuple-element.56.after_ref.solve_ref, bf16[320,64]{1,0:T(8,128)(2,1)S(1)} %get-tuple-element.57.left_ref, ...), custom_call_target="tpu_custom_call", output_to_operand_aliasing={{0}: (6, {}), {1}: (7, {})} | custom-call | flops 8589934592 | bytes 1048576 | tf_op jit(solution)/shard_map/result/pallas_call | solution.py:491
  86.6 0.0 collective-permute-done.23.refs_0_
  86.6 2.7 %result.9 = (bf16[320,10240]{1,0:T(8,128)(2,1)}, f32[64,10240]{1,0:T(8,128)}, f32[8,128]{1,0:T(8,128)}, f32[64,320]{1,0:T(8,128)}) custom-call(bf16[64,384]{1,0:T(8,128)(2,1)S(1)} %get-tuple-element.56.after_ref.solve_ref, bf16[320,64]{1,0:T(8,128)(2,1)S(1)} %get-tuple-element.57.left_ref, ...), custom_call_target="tpu_custom_call", output_to_operand_aliasing={{0}: (6, {}), {1}: (7, {})} | custom-call | flops 8589934592 | bytes 1048576 | tf_op jit(solution)/shard_map/result/pallas_call | solution.py:491
  (11 shorter events, 0.1 us)
Async XLA Ops:
  6.8 6.7 %collective-permute-start = (f32[160,128]{1,0:T(8,128)S(1)}, f32[160,128]{1,0:T(8,128)S(1)}, u32[]{:S(2)}, u32[]{:S(2)}) collective-permute-start(f32[160,128]{1,0:T(8,128)S(1)} %get-tuple-element.38), channel_id=1, source_target_pairs={{0,8},{1,33},{2,10},{3,35},{4,12},{5,37},{6,14},{7,39},{8,16},{9,4... | collective-permute-start | bytes 245768 | tf_op jit(solution)/shard_map/ppermute | solution.py:77
  9.4 4.2 %collective-permute-start.1 = (f32[160,128]{1,0:T(8,128)S(1)}, f32[160,128]{1,0:T(8,128)S(1)}, u32[]{:S(2)}, u32[]{:S(2)}) collective-permute-start(f32[160,128]{1,0:T(8,128)S(1)} %get-tuple-element.38), channel_id=1, source_target_pairs={{0,24},{1,97},{2,26},{3,99},{4,28},{5,101},{6,30},{7,103},{8,0},{9... | collective-permute-start | bytes 245768 | tf_op jit(solution)/shard_map/ppermute | solution.py:77
  11.6 5.1 %collective-permute-start.2 = (f32[160,128]{1,0:T(8,128)S(1)}, f32[160,128]{1,0:T(8,128)S(1)}, u32[]{:S(2)}, u32[]{:S(2)}) collective-permute-start(f32[160,128]{1,0:T(8,128)S(1)} %get-tuple-element.38), channel_id=1, source_target_pairs={{0,16},{1,65},{2,18},{3,67},{4,20},{5,69},{6,22},{7,71},{8,24},{9,... | collective-permute-start | bytes 245768 | tf_op jit(solution)/shard_map/ppermute | solution.py:77
  16.7 4.6 %collective-permute-start.3 = (f32[160,128]{1,0:T(8,128)S(1)}, f32[160,128]{1,0:T(8,128)S(1)}, u32[]{:S(2)}, u32[]{:S(2)}) collective-permute-start(f32[160,128]{1,0:T(8,128)S(1)} %add_add_fusion.a_ref), channel_id=1, source_target_pairs={{0,32},{1,9},{2,34},{3,11},{4,36},{5,13},{6,38},{7,15},{8,40},{9,1... | collective-permute-start | bytes 245768 | tf_op jit(solution)/shard_map/ppermute | solution.py:77
  17.7 3.6 %collective-permute-start.4 = (f32[160,128]{1,0:T(8,128)S(1)}, f32[160,128]{1,0:T(8,128)S(1)}, u32[]{:S(2)}, u32[]{:S(2)}) collective-permute-start(f32[160,128]{1,0:T(8,128)S(1)} %add_add_fusion.a_ref), channel_id=1, source_target_pairs={{0,96},{1,25},{2,98},{3,27},{4,100},{5,29},{6,102},{7,31},{8,104},... | collective-permute-start | bytes 245768 | tf_op jit(solution)/shard_map/ppermute | solution.py:77
  19.4 4.8 %collective-permute-start.5 = (f32[160,128]{1,0:T(8,128)S(1)}, f32[160,128]{1,0:T(8,128)S(1)}, u32[]{:S(2)}, u32[]{:S(2)}) collective-permute-start(f32[160,128]{1,0:T(8,128)S(1)} %add_add_fusion.a_ref), channel_id=1, source_target_pairs={{0,64},{1,17},{2,66},{3,19},{4,68},{5,21},{6,70},{7,23},{8,72},{9,... | collective-permute-start | bytes 245768 | tf_op jit(solution)/shard_map/ppermute | solution.py:77
  24.9 5.0 %collective-permute-start.6 = (f32[680,128]{1,0:T(8,128)S(1)}, f32[680,128]{1,0:T(8,128)S(1)}, u32[]{:S(2)}, u32[]{:S(2)}) collective-permute-start(f32[680,128]{1,0:T(8,128)S(1)} %get-tuple-element.42), channel_id=1, source_target_pairs={{0,1},{1,0},{2,3},{3,2},{4,5},{5,4},{6,7},{7,6},{8,9},{9,8},{10,11... | collective-permute-start | bytes 1044488 | tf_op jit(solution)/shard_map/ppermute | solution.py:82
  29.4 3.2 %collective-permute-start.7 = (f32[1920,128]{1,0:T(8,128)S(1)}, f32[1920,128]{1,0:T(8,128)S(1)}, u32[]{:S(2)}, u32[]{:S(2)}) collective-permute-start(f32[1920,128]{1,0:T(8,128)S(1)} %next_right.3.after_ref), channel_id=1, source_target_pairs={{0,1},{1,0},{2,3},{3,2},{4,5},{5,4},{6,7},{7,6},{8,9},{9,8},{10,11... | collective-permute-start | bytes 2949128 | tf_op jit(solution)/shard_map/ppermute | solution.py:82
  30.1 7.8 %collective-permute-start.10 = (f32[640,128]{1,0:T(8,128)S(1)}, f32[640,128]{1,0:T(8,128)S(1)}, u32[]{:S(2)}, u32[]{:S(2)}) collective-permute-start(f32[640,128]{1,0:T(8,128)S(1)} %get-tuple-element.47), channel_id=1, source_target_pairs={{0,16},{1,65},{2,66},{3,19},{4,20},{5,69},{6,70},{7,23},{8,72},{9,... | collective-permute-start | bytes 983048 | tf_op jit(solution)/shard_map/ppermute | solution.py:77
  32.8 8.6 %collective-permute-start.8 = (f32[640,128]{1,0:T(8,128)S(1)}, f32[640,128]{1,0:T(8,128)S(1)}, u32[]{:S(2)}, u32[]{:S(2)}) collective-permute-start(f32[640,128]{1,0:T(8,128)S(1)} %get-tuple-element.45), channel_id=1, source_target_pairs={{0,9},{1,32},{2,35},{3,10},{4,13},{5,36},{6,39},{7,14},{8,41},{9,1... | collective-permute-start | bytes 983048 | tf_op jit(solution)/shard_map/ppermute | solution.py:77
  34.3 7.3 %collective-permute-start.9 = (f32[640,128]{1,0:T(8,128)S(1)}, f32[640,128]{1,0:T(8,128)S(1)}, u32[]{:S(2)}, u32[]{:S(2)}) collective-permute-start(f32[640,128]{1,0:T(8,128)S(1)} %get-tuple-element.46), channel_id=1, source_target_pairs={{0,25},{1,96},{2,99},{3,26},{4,29},{5,100},{6,103},{7,30},{8,105},... | collective-permute-start | bytes 983048 | tf_op jit(solution)/shard_map/ppermute | solution.py:77
  41.7 6.2 %collective-permute-start.11 = (f32[200,128]{1,0:T(8,128)S(1)}, f32[200,128]{1,0:T(8,128)S(1)}, u32[]{:S(2)}, u32[]{:S(2)}) collective-permute-start(f32[200,128]{1,0:T(8,128)S(1)} %get-tuple-element.50), channel_id=1, source_target_pairs={{0,33},{1,2},{2,5},{3,34},{4,37},{5,6},{6,1},{7,38},{8,11},{9,40},... | collective-permute-start | bytes 307208 | tf_op jit(solution)/shard_map/ppermute | solution.py:77
  44.0 4.1 %collective-permute-start.12 = (f32[200,128]{1,0:T(8,128)S(1)}, f32[200,128]{1,0:T(8,128)S(1)}, u32[]{:S(2)}, u32[]{:S(2)}) collective-permute-start(f32[200,128]{1,0:T(8,128)S(1)} %get-tuple-element.51), channel_id=1, source_target_pairs={{0,97},{1,6},{2,1},{3,98},{4,101},{5,2},{6,5},{7,102},{8,15},{9,10... | collective-permute-start | bytes 307208 | tf_op jit(solution)/shard_map/ppermute | solution.py:77
  45.6 5.3 %collective-permute-start.13 = (f32[200,128]{1,0:T(8,128)S(1)}, f32[200,128]{1,0:T(8,128)S(1)}, u32[]{:S(2)}, u32[]{:S(2)}) collective-permute-start(f32[200,128]{1,0:T(8,128)S(1)} %get-tuple-element.52), channel_id=1, source_target_pairs={{0,64},{1,5},{2,6},{3,67},{4,68},{5,1},{6,2},{7,71},{8,12},{9,73},... | collective-permute-start | bytes 307208 | tf_op jit(solution)/shard_map/ppermute | solution.py:77
  51.5 5.6 %collective-permute-start.14 = (f32[200,128]{1,0:T(8,128)S(1)}, f32[200,128]{1,0:T(8,128)S(1)}, u32[]{:S(2)}, u32[]{:S(2)}) collective-permute-start(f32[200,128]{1,0:T(8,128)S(1)} %get-tuple-element.53.a_ref), channel_id=1, source_target_pairs={{0,3},{1,8},{2,11},{3,4},{4,7},{5,12},{6,15},{7,0},{8,17},{9,10},{... | collective-permute-start | bytes 307208 | tf_op jit(solution)/shard_map/ppermute | solution.py:77
  52.5 4.6 %collective-permute-start.15 = (f32[200,128]{1,0:T(8,128)S(1)}, f32[200,128]{1,0:T(8,128)S(1)}, u32[]{:S(2)}, u32[]{:S(2)}) collective-permute-start(f32[200,128]{1,0:T(8,128)S(1)} %get-tuple-element.53.a_ref), channel_id=1, source_target_pairs={{0,7},{1,24},{2,27},{3,0},{4,3},{5,28},{6,31},{7,4},{8,1},{9,14},{... | collective-permute-start | bytes 307208 | tf_op jit(solution)/shard_map/ppermute | solution.py:77
  54.5 5.0 %collective-permute-start.16 = (f32[200,128]{1,0:T(8,128)S(1)}, f32[200,128]{1,0:T(8,128)S(1)}, u32[]{:S(2)}, u32[]{:S(2)}) collective-permute-start(f32[200,128]{1,0:T(8,128)S(1)} %get-tuple-element.53.a_ref), channel_id=1, source_target_pairs={{0,4},{1,17},{2,18},{3,7},{4,0},{5,21},{6,22},{7,3},{8,24},{9,13},... | collective-permute-start | bytes 307208 | tf_op jit(solution)/shard_map/ppermute | solution.py:77
  59.6 7.1 %collective-permute-start.17 = (f32[160,128]{1,0:T(8,128)S(1)}, f32[160,128]{1,0:T(8,128)S(1)}, u32[]{:S(2)}, u32[]{:S(2)}) collective-permute-start(f32[160,128]{1,0:T(8,128)S(1)} %get-tuple-element.58.a_ref), channel_id=1, source_target_pairs={{0,33},{1,2},{2,5},{3,34},{4,37},{5,6},{6,1},{7,38},{8,11},{9,40},... | collective-permute-start | bytes 245768 | tf_op jit(solution)/shard_map/ppermute | solution.py:77
  62.1 4.7 %collective-permute-start.18 = (f32[160,128]{1,0:T(8,128)S(1)}, f32[160,128]{1,0:T(8,128)S(1)}, u32[]{:S(2)}, u32[]{:S(2)}) collective-permute-start(f32[160,128]{1,0:T(8,128)S(1)} %get-tuple-element.58.a_ref), channel_id=1, source_target_pairs={{0,97},{1,6},{2,1},{3,98},{4,101},{5,2},{6,5},{7,102},{8,15},{9,10... | collective-permute-start | bytes 245768 | tf_op jit(solution)/shard_map/ppermute | solution.py:77
  63.6 4.8 %collective-permute-start.19 = (f32[160,128]{1,0:T(8,128)S(1)}, f32[160,128]{1,0:T(8,128)S(1)}, u32[]{:S(2)}, u32[]{:S(2)}) collective-permute-start(f32[160,128]{1,0:T(8,128)S(1)} %get-tuple-element.58.a_ref), channel_id=1, source_target_pairs={{0,64},{1,5},{2,6},{3,67},{4,68},{5,1},{6,2},{7,71},{8,12},{9,73},... | collective-permute-start | bytes 245768 | tf_op jit(solution)/shard_map/ppermute | solution.py:77
  68.4 7.3 %collective-permute-start.22 = (f32[640,128]{1,0:T(8,128)S(1)}, f32[640,128]{1,0:T(8,128)S(1)}, u32[]{:S(2)}, u32[]{:S(2)}) collective-permute-start(f32[640,128]{1,0:T(8,128)S(1)} %assemble.1.refs_0_), channel_id=1, source_target_pairs={{0,1},{1,0},{2,3},{3,2},{4,5},{5,4},{6,7},{7,6},{8,9},{9,8},{10,11... | collective-permute-start | bytes 983048 | tf_op jit(solution)/shard_map/ppermute | solution.py:82
  71.1 7.7 %collective-permute-start.21 = (f32[640,128]{1,0:T(8,128)S(1)}, f32[640,128]{1,0:T(8,128)S(1)}, u32[]{:S(2)}, u32[]{:S(2)}) collective-permute-start(f32[640,128]{1,0:T(8,128)S(1)} %assemble.1.refs_0_), channel_id=1, source_target_pairs={{0,16},{1,65},{2,66},{3,19},{4,20},{5,69},{6,70},{7,23},{8,72},{9,... | collective-permute-start | bytes 983048 | tf_op jit(solution)/shard_map/ppermute | solution.py:77
  71.1 11.1 %collective-permute-start.24 = (f32[640,128]{1,0:T(8,128)S(1)}, f32[640,128]{1,0:T(8,128)S(1)}, u32[]{:S(2)}, u32[]{:S(2)}) collective-permute-start(f32[640,128]{1,0:T(8,128)S(1)} %assemble.1.refs_0_), channel_id=1, source_target_pairs={{0,25},{1,96},{2,99},{3,26},{4,29},{5,100},{6,103},{7,30},{8,105},... | collective-permute-start | bytes 983048 | tf_op jit(solution)/shard_map/ppermute | solution.py:77
  73.6 8.7 %collective-permute-start.20 = (f32[640,128]{1,0:T(8,128)S(1)}, f32[640,128]{1,0:T(8,128)S(1)}, u32[]{:S(2)}, u32[]{:S(2)}) collective-permute-start(f32[640,128]{1,0:T(8,128)S(1)} %assemble.1.refs_0_), channel_id=1, source_target_pairs={{0,9},{1,32},{2,35},{3,10},{4,13},{5,36},{6,39},{7,14},{8,41},{9,1... | collective-permute-start | bytes 983048 | tf_op jit(solution)/shard_map/ppermute | solution.py:77
  78.9 4.5 %collective-permute-start.26 = (f32[640,128]{1,0:T(8,128)S(1)}, f32[640,128]{1,0:T(8,128)S(1)}, u32[]{:S(2)}, u32[]{:S(2)}) collective-permute-start(f32[640,128]{1,0:T(8,128)S(1)} %tie.3.refs_0_), channel_id=1, source_target_pairs={{0,1},{1,0},{2,3},{3,2},{4,5},{5,4},{6,7},{7,6},{8,9},{9,8},{10,11... | collective-permute-start | bytes 983048 | tf_op jit(solution)/shard_map/ppermute | solution.py:82
  82.2 4.4 %collective-permute-start.25 = (f32[640,128]{1,0:T(8,128)S(1)}, f32[640,128]{1,0:T(8,128)S(1)}, u32[]{:S(2)}, u32[]{:S(2)}) collective-permute-start(f32[640,128]{1,0:T(8,128)S(1)} %tie.5.refs_1_), channel_id=1, source_target_pairs={{0,1},{1,0},{2,3},{3,2},{4,5},{5,4},{6,7},{7,6},{8,9},{9,8},{10,11... | collective-permute-start | bytes 983048 | tf_op jit(solution)/shard_map/ppermute | solution.py:82
  82.4 4.2 %collective-permute-start.23 = (f32[640,128]{1,0:T(8,128)S(1)}, f32[640,128]{1,0:T(8,128)S(1)}, u32[]{:S(2)}, u32[]{:S(2)}) collective-permute-start(f32[640,128]{1,0:T(8,128)S(1)} %tie.4.refs_0_), channel_id=1, source_target_pairs={{0,1},{1,0},{2,3},{3,2},{4,5},{5,4},{6,7},{7,6},{8,9},{9,8},{10,11... | collective-permute-start | bytes 983048 | tf_op jit(solution)/shard_map/ppermute | solution.py:82

commit v13 on v12

--- a/solution.py
+++ b/solution.py
@@ -309,9 +309,9 @@
     )(*parts, ext)
 
 
-def across_kernel(half_along_y, a_ref, b_ref, c_ref, d_ref, out_ref, ext_ref):
-    grams = ext_ref.shape[0] - ROWS
-    size = a_ref.shape[0] - grams - ROWS
+def across_kernel(half_along_y, extra, a_ref, b_ref, c_ref, d_ref, out_ref, *ext_ref):
+    grams = extra - ROWS
+    size = a_ref.shape[0] - extra
     refs = (a_ref, b_ref, c_ref, d_ref)
     peaks = [r[size + grams : size + grams + 1, :1] for r in refs]
     top = jnp.maximum(jnp.maximum(peaks[0], peaks[1]), jnp.maximum(peaks[2], peaks[3]))
@@ -319,23 +319,21 @@
     out_ref[:size] = (a + b) + (c + d)
     a, b, c, d = (r[size : size + grams] for r in refs)
     gram = jnp.where(place()[0] == half_along_y, (a + b) + (c + d), a)
-    ext_ref[:grams] = gram
-    ext_ref[grams:] = jnp.broadcast_to(top, (ROWS, 128))
-    if out_ref.shape[0] > size:
-        out_ref[size : size + grams] = gram
-        out_ref[size + grams :] = jnp.broadcast_to(top, (ROWS, 128))
+    ext = out_ref.at[size:] if not ext_ref else ext_ref[0]
+    ext[:grams] = gram
+    ext[grams:] = jnp.broadcast_to(top, (ROWS, 128))
 
 
 def across(half_along_y, parts, extra, keep):
     rows = parts[0].shape[0]
-    return pl.pallas_call(
-        functools.partial(across_kernel, half_along_y),
-        out_shape=[
-            jax.ShapeDtypeStruct((rows if keep else rows - extra, 128), F32),
-            pltpu.VMEM((extra, 128), F32),
-        ],
+    out = [jax.ShapeDtypeStruct((rows, 128), F32)]
+    if not keep:
+        out = [jax.ShapeDtypeStruct((rows - extra, 128), F32), pltpu.VMEM((extra, 128), F32)]
+    return pl.pallas_call(
+        functools.partial(across_kernel, half_along_y, extra),
+        out_shape=out,
         in_specs=[WHOLE] * 4,
-        out_specs=[WHOLE] * 2,
+        out_specs=[WHOLE] * len(out),
         compiler_params=params(8),
         name="across",
     )(*parts)
@@ -425,13 +423,14 @@
     )(ext, p_mean)
 
 
-def result_kernel(sources, last, width, solve_ref, left_ref, m_ref, *refs):
-    if last:
-        hat_hbm, refs = refs[-4], refs[:-4] + refs[-3:]
-        hat = pltpu.make_async_copy(refs[len(sources)], hat_hbm, refs[-1].at[0, len(sources)])
+def result_kernel(sources, more, width, solve_ref, left_ref, m_ref, *refs):
+    refs, (error_ref, q_ref, sems) = refs[:-3], refs[-3:]
+    if more == "hat":
+        hat = pltpu.make_async_copy(refs[len(sources)], refs[-1], sems.at[0, len(sources)])
         hat.start()
-    error_hbm, q_hbm, token_ref, error_ref, q_ref, sems = refs[-6:]
-    token_ref[...] = jnp.zeros_like(token_ref)
+    if more == "token":
+        refs[-1][...] = jnp.zeros_like(refs[-1])
+    error_hbm, q_hbm = refs[-3:-1] if more else refs[-2:]
     rank = solve_ref.shape[0]
     columns = q_ref.shape[2]
     left = left_ref[...]
@@ -477,27 +476,25 @@
     for n, base in enumerate(bases):
         for c in copies(n, base, 0, columns):
             c.wait()
-    if last:
+    if more == "hat":
         hat.wait()
 
 
-def result(sources, totals, merged, solve, left, before, p_hat=None):
+def result(sources, totals, merged, solve, left, before, p_hat=None, token=False):
     rank = solve.shape[0]
     rows, columns = merged.shape
     quarter = columns // 2 // QUARTERS
     n = len(sources)
     held = [] if before is None else list(before)
     last = [] if p_hat is None else [p_hat]
-    return pl.pallas_call(
-        functools.partial(result_kernel, sources, bool(last), quarter // 2),
-        out_shape=[
-            pltpu.HBM((rows, columns), BF16),
-            pltpu.HBM((rank, columns), F32),
-            pltpu.VMEM((ROWS, 128), F32),
-        ]
-        + [pltpu.HBM(a.shape, F32) for a in last],
+    more = "hat" if last else "token" if token else ""
+    return pl.pallas_call(
+        functools.partial(result_kernel, sources, more, quarter // 2),
+        out_shape=[pltpu.HBM((rows, columns), BF16), pltpu.HBM((rank, columns), F32)]
+        + [pltpu.HBM(a.shape, F32) for a in last]
+        + [pltpu.VMEM((ROWS, 128), F32)] * token,
         in_specs=[WHOLE] * (3 + n + len(last)) + [ANY] * len(held),
-        out_specs=[ANY, ANY, WHOLE] + [ANY] * len(last),
+        out_specs=[ANY, ANY] + [ANY] * len(last) + [WHOLE] * token,
         scratch_shapes=[
             pltpu.VMEM((n, rows, quarter), BF16),
             pltpu.VMEM((n, rank, quarter), F32),
@@ -505,7 +502,7 @@
         ],
         input_output_aliases={3 + n + len(last) + i: i for i in range(len(held))},
         compiler_params=params(12),
-        cost_estimate=cost(1<<33, 1<<20),
+        cost_estimate=cost(1 << 33, 1 << 20),
         name="result",
     )(solve, left, merged, *totals, *last, *held)
 
@@ -545,23 +542,23 @@
     *near, own = next_pair(kept, got_next, weight)
     own, *sent = add_quarters((own, *ring(near, 0, (1, 3)), two), ext)
     extra = ext.shape[0]
-    part, _ = across(1, (own, *ring(sent, 1)), extra, True)
+    (part,) = across(1, (own, *ring(sent, 1)), extra, True)
     total, ext = across(0, (part, *ring([part] * 3, 2)), extra, False)
     solve, left, p_hat = factor(ext, p_mean, replicas)
     total = assemble((total, *ring([total] * 3, 1)), solve)
     two, one, three = ring([total] * 3, 0, (2, 1, 3))
 
-    def write(sources, totals, *after):
-        return result(sources, totals, merged, solve, left, *after)
+    def write(sources, totals, *after, **more):
+        return result(sources, totals, merged, solve, left, *after, **more)
 
     own, other = True, False
-    *out, _ = write(((own, 0),), (total,), None)
-    *out, token = write(((other, 0),), (swap(total),), out)
+    out = write(((own, 0),), (total,), None)
+    *out, token = write(((other, 0),), (swap(total),), out, token=True)
     two = tie(two, token)
-    *out, token = write(((own, 2),), (two,), out)
+    *out, token = write(((own, 2),), (two,), out, token=True)
     one, three = tie(one, token), tie(three, token)
-    *out, _ = write(((own, 1), (own, 3), (other, 2)), (one, three, swap(two)), out)
-    new_error, q_new, _, p_hat = write(
+    out = write(((own, 1), (own, 3), (other, 2)), (one, three, swap(two)), out)
+    new_error, q_new, p_hat = write(
         ((other, 1), (other, 3)), (swap(one), swap(three)), out, p_hat
     )
     return (new_error[None], p_hat, q_new)

time: 89.6 us -> 87.9 us (0.981)
  Pallas kernels: 23.6 us -> 21.2 us
    pallas_call x7, Pallas kernels: 12 us -> 9.62 us  [the longest x5 9.48 us: result(): pl.pallas_call(functools.partial(result_kernel, sources, more, quarter //...]
  transfers between devices with their start and end apart: 27 -> 27, of which waited for: 16 -> 16; matrix products, arithmetic and copies ran while one was open for 0% -> 0% of each run, Pallas kernels for 15% -> 14%
where the time goes in v13:
time: 87.9 us; the launch traced here: 87.8 us
  starting transfers between devices  39 us (44%)
  waiting for transfers between devices  26.5 us (30%)
  Pallas kernels  21.2 us (24%)
  between operations  0.98 us (1%)
    ppermute x21, starting transfers between devices, ring(): out.append(lax.ppermute(value, AXES, pairs))  30.7 us
    ppermute x21, waiting for transfers between devices, ring(): out.append(lax.ppermute(value, AXES, pairs))  26.5 us
    pallas_call x5, Pallas kernels, result(): pl.pallas_call(functools.partial(result_kernel, sources, more, quarter //...  9.48 us
    ppermute x6, starting transfers between devices, swap(): return lax.ppermute(value, 'c', [(0, 1), (1, 0)])  8.35 us
    pallas_call x1, Pallas kernels, merge(): pl.pallas_call(functools.partial(merge_kernel, cuts), out_shape=[pltpu.VM...  6.21 us
    pallas_call x3, Pallas kernels, next_right(): pl.pallas_call(functools.partial(next_right_kernel, own, turns), out_shap...  2.25 us
    pallas_call x1, Pallas kernels, factor(): pl.pallas_call(functools.partial(factor_kernel, replicas), out_shape=[jax...  2.01 us
  transfers between devices with their start and end apart: 27, of which 16 were waited for; matrix products, arithmetic and copies ran while one was open for 0% of the time, Pallas kernels for 14%

profile of v13, /device:TPU:1, one launch (start us, length us, event | category | flops | bytes accessed | tf_op | source)
XLA Modules:
  0.0 87.8 jit_solution(7754146645745404688)
XLA Ops:
  0.6 6.2 %merge.1 = (bf16[320,10240]{1,0:T(8,128)(2,1)S(1)}, f32[160,128]{1,0:T(8,128)S(1)}) custom-call(bf16[320,10240]{1,0:T(8,128)(2,1)} %bitcast.3, bf16[320,10240]{1,0:T(8,128)(2,1)} %bitcast.4, bf16[64,10240]{1,0:T(8,128)(2,1)} %q_hbm.1), custom_call_target="tpu_custom_call" | custom-call | flops 419430400 | bytes 13107200 | tf_op jit(solution)/shard_map/merge/pallas_call | solution.py:138
  6.8 2.5 %collective-permute-start = (f32[160,128]{1,0:T(8,128)S(1)}, f32[160,128]{1,0:T(8,128)S(1)}, u32[]{:S(2)}, u32[]{:S(2)}) collective-permute-start(f32[160,128]{1,0:T(8,128)S(1)} %get-tuple-element.37), channel_id=1, source_target_pairs={{0,8},{1,33},{2,10},{3,35},{4,12},{5,37},{6,14},{7,39},{8,16},{9,4... | collective-permute-start | bytes 245768 | tf_op jit(solution)/shard_map/ppermute | solution.py:77
  9.4 2.2 %collective-permute-start.1 = (f32[160,128]{1,0:T(8,128)S(1)}, f32[160,128]{1,0:T(8,128)S(1)}, u32[]{:S(2)}, u32[]{:S(2)}) collective-permute-start(f32[160,128]{1,0:T(8,128)S(1)} %get-tuple-element.37), channel_id=1, source_target_pairs={{0,24},{1,97},{2,26},{3,99},{4,28},{5,101},{6,30},{7,103},{8,0},{9... | collective-permute-start | bytes 245768 | tf_op jit(solution)/shard_map/ppermute | solution.py:77
  11.6 1.2 %collective-permute-start.2 = (f32[160,128]{1,0:T(8,128)S(1)}, f32[160,128]{1,0:T(8,128)S(1)}, u32[]{:S(2)}, u32[]{:S(2)}) collective-permute-start(f32[160,128]{1,0:T(8,128)S(1)} %get-tuple-element.37), channel_id=1, source_target_pairs={{0,16},{1,65},{2,18},{3,67},{4,20},{5,69},{6,22},{7,71},{8,24},{9,... | collective-permute-start | bytes 245768 | tf_op jit(solution)/shard_map/ppermute | solution.py:77
  12.8 0.8 collective-permute-done
  13.6 0.0 collective-permute-done.1
  13.6 3.1 %collective-permute-done.2 = f32[160,128]{1,0:T(8,128)S(1)} collective-permute-done((f32[160,128]{1,0:T(8,128)S(1)}, f32[160,128]{1,0:T(8,128)S(1)}, u32[]{:S(2)}, u32[]{:S(2)}) %collective-permute-start.2) | collective-permute-done | bytes 81952 | tf_op jit(solution)/shard_map/ppermute | solution.py:77
  16.7 1.0 %collective-permute-start.3 = (f32[160,128]{1,0:T(8,128)S(1)}, f32[160,128]{1,0:T(8,128)S(1)}, u32[]{:S(2)}, u32[]{:S(2)}) collective-permute-start(f32[160,128]{1,0:T(8,128)S(1)} %add_add_fusion.a_ref), channel_id=1, source_target_pairs={{0,32},{1,9},{2,34},{3,11},{4,36},{5,13},{6,38},{7,15},{8,40},{9,1... | collective-permute-start | bytes 245768 | tf_op jit(solution)/shard_map/ppermute | solution.py:77
  17.7 1.8 %collective-permute-start.4 = (f32[160,128]{1,0:T(8,128)S(1)}, f32[160,128]{1,0:T(8,128)S(1)}, u32[]{:S(2)}, u32[]{:S(2)}) collective-permute-start(f32[160,128]{1,0:T(8,128)S(1)} %add_add_fusion.a_ref), channel_id=1, source_target_pairs={{0,96},{1,25},{2,98},{3,27},{4,100},{5,29},{6,102},{7,31},{8,104},... | collective-permute-start | bytes 245768 | tf_op jit(solution)/shard_map/ppermute | solution.py:77
  19.4 1.2 %collective-permute-start.5 = (f32[160,128]{1,0:T(8,128)S(1)}, f32[160,128]{1,0:T(8,128)S(1)}, u32[]{:S(2)}, u32[]{:S(2)}) collective-permute-start(f32[160,128]{1,0:T(8,128)S(1)} %add_add_fusion.a_ref), channel_id=1, source_target_pairs={{0,64},{1,17},{2,66},{3,19},{4,68},{5,21},{6,70},{7,23},{8,72},{9,... | collective-permute-start | bytes 245768 | tf_op jit(solution)/shard_map/ppermute | solution.py:77
  20.7 0.6 collective-permute-done.3.b_ref
  21.3 0.0 collective-permute-done.4.c_ref
  21.3 3.0 %collective-permute-done.5.d_ref = f32[160,128]{1,0:T(8,128)S(1)} collective-permute-done((f32[160,128]{1,0:T(8,128)S(1)}, f32[160,128]{1,0:T(8,128)S(1)}, u32[]{:S(2)}, u32[]{:S(2)}) %collective-permute-start.5) | collective-permute-done | bytes 81952 | tf_op jit(solution)/shard_map/ppermute | solution.py:77
  24.2 0.7 first_right.1
  24.9 3.5 %collective-permute-start.6 = (f32[680,128]{1,0:T(8,128)S(1)}, f32[680,128]{1,0:T(8,128)S(1)}, u32[]{:S(2)}, u32[]{:S(2)}) collective-permute-start(f32[680,128]{1,0:T(8,128)S(1)} %get-tuple-element.41), channel_id=1, source_target_pairs={{0,1},{1,0},{2,3},{3,2},{4,5},{5,4},{6,7},{7,6},{8,9},{9,8},{10,11... | collective-permute-start | bytes 1044488 | tf_op jit(solution)/shard_map/ppermute | solution.py:82
  28.5 0.9 %next_right.3.after_ref = f32[1920,128]{1,0:T(8,128)S(1)} custom-call(bf16[192,320]{1,0:T(8,128)(2,1)S(1)} %get-tuple-element.39.pieces_ref, bf16[320,10240]{1,0:T(8,128)(2,1)S(1)} %get-tuple-element.38.m_ref, f32[40,128]{1,0:T(8,128)S(1)} %get-tuple-element.40.after_ref.ext_ref), custom_call_target="tpu_custom_call" | custom-call | flops 8589934592 | bytes 1048576 | tf_op jit(solution)/shard_map/next_right/pallas_call | solution.py:233
  29.4 0.1 collective-permute-start.7
  29.5 0.4 next_right.4.kept_ref
  29.9 0.0 collective-permute-done.6.got_ref
  30.0 0.1 first_pair.1
  30.1 1.6 %collective-permute-start.10 = (f32[640,128]{1,0:T(8,128)S(1)}, f32[640,128]{1,0:T(8,128)S(1)}, u32[]{:S(2)}, u32[]{:S(2)}) collective-permute-start(f32[640,128]{1,0:T(8,128)S(1)} %get-tuple-element.46), channel_id=1, source_target_pairs={{0,16},{1,65},{2,66},{3,19},{4,20},{5,69},{6,70},{7,23},{8,72},{9,... | collective-permute-start | bytes 983048 | tf_op jit(solution)/shard_map/ppermute | solution.py:77
  31.6 0.9 %next_right.5.kept_ref = f32[1920,128]{1,0:T(8,128)S(1)} custom-call(bf16[192,320]{1,0:T(8,128)(2,1)S(1)} %get-tuple-element.39.pieces_ref, bf16[320,10240]{1,0:T(8,128)(2,1)S(1)} %get-tuple-element.38.m_ref, f32[16,128]{1,0:T(8,128)S(1)} %get-tuple-element.42.after_ref.weight_ref), custom_call_target="tpu_custom_call" | custom-call | flops 8589934592 | bytes 1048576 | tf_op jit(solution)/shard_map/next_right/pallas_call | solution.py:233
  32.6 0.0 collective-permute-done.7.got_ref
  32.6 0.2 next_pair.1
  32.8 1.4 %collective-permute-start.8 = (f32[640,128]{1,0:T(8,128)S(1)}, f32[640,128]{1,0:T(8,128)S(1)}, u32[]{:S(2)}, u32[]{:S(2)}) collective-permute-start(f32[640,128]{1,0:T(8,128)S(1)} %get-tuple-element.44), channel_id=1, source_target_pairs={{0,9},{1,32},{2,35},{3,10},{4,13},{5,36},{6,39},{7,14},{8,41},{9,1... | collective-permute-start | bytes 983048 | tf_op jit(solution)/shard_map/ppermute | solution.py:77
  34.3 1.6 %collective-permute-start.9 = (f32[640,128]{1,0:T(8,128)S(1)}, f32[640,128]{1,0:T(8,128)S(1)}, u32[]{:S(2)}, u32[]{:S(2)}) collective-permute-start(f32[640,128]{1,0:T(8,128)S(1)} %get-tuple-element.45), channel_id=1, source_target_pairs={{0,25},{1,96},{2,99},{3,26},{4,29},{5,100},{6,103},{7,30},{8,105},... | collective-permute-start | bytes 983048 | tf_op jit(solution)/shard_map/ppermute | solution.py:77
  35.8 2.0 %collective-permute-done.10.d_ref = f32[640,128]{1,0:T(8,128)S(1)} collective-permute-done((f32[640,128]{1,0:T(8,128)S(1)}, f32[640,128]{1,0:T(8,128)S(1)}, u32[]{:S(2)}, u32[]{:S(2)}) %collective-permute-start.10) | collective-permute-done | bytes 327712 | tf_op jit(solution)/shard_map/ppermute | solution.py:77
  37.9 3.5 %collective-permute-done.8.b_ref = f32[640,128]{1,0:T(8,128)S(1)} collective-permute-done((f32[640,128]{1,0:T(8,128)S(1)}, f32[640,128]{1,0:T(8,128)S(1)}, u32[]{:S(2)}, u32[]{:S(2)}) %collective-permute-start.8) | collective-permute-done | bytes 327712 | tf_op jit(solution)/shard_map/ppermute | solution.py:77
  41.4 0.2 collective-permute-done.9.c_ref
  41.6 0.1 add_quarters.1
  41.7 2.4 %collective-permute-start.11 = (f32[200,128]{1,0:T(8,128)S(1)}, f32[200,128]{1,0:T(8,128)S(1)}, u32[]{:S(2)}, u32[]{:S(2)}) collective-permute-start(f32[200,128]{1,0:T(8,128)S(1)} %get-tuple-element.49), channel_id=1, source_target_pairs={{0,33},{1,2},{2,5},{3,34},{4,37},{5,6},{6,1},{7,38},{8,11},{9,40},... | collective-permute-start | bytes 307208 | tf_op jit(solution)/shard_map/ppermute | solution.py:77
  44.0 1.5 %collective-permute-start.12 = (f32[200,128]{1,0:T(8,128)S(1)}, f32[200,128]{1,0:T(8,128)S(1)}, u32[]{:S(2)}, u32[]{:S(2)}) collective-permute-start(f32[200,128]{1,0:T(8,128)S(1)} %get-tuple-element.50), channel_id=1, source_target_pairs={{0,97},{1,6},{2,1},{3,98},{4,101},{5,2},{6,5},{7,102},{8,15},{9,10... | collective-permute-start | bytes 307208 | tf_op jit(solution)/shard_map/ppermute | solution.py:77
  45.6 1.1 %collective-permute-start.13 = (f32[200,128]{1,0:T(8,128)S(1)}, f32[200,128]{1,0:T(8,128)S(1)}, u32[]{:S(2)}, u32[]{:S(2)}) collective-permute-start(f32[200,128]{1,0:T(8,128)S(1)} %get-tuple-element.51), channel_id=1, source_target_pairs={{0,64},{1,5},{2,6},{3,67},{4,68},{5,1},{6,2},{7,71},{8,12},{9,73},... | collective-permute-start | bytes 307208 | tf_op jit(solution)/shard_map/ppermute | solution.py:77
  46.7 1.2 %collective-permute-done.11.b_ref = f32[200,128]{1,0:T(8,128)S(1)} collective-permute-done((f32[200,128]{1,0:T(8,128)S(1)}, f32[200,128]{1,0:T(8,128)S(1)}, u32[]{:S(2)}, u32[]{:S(2)}) %collective-permute-start.11) | collective-permute-done | bytes 102432 | tf_op jit(solution)/shard_map/ppermute | solution.py:77
  47.8 0.3 collective-permute-done.12.c_ref
  48.1 2.8 %collective-permute-done.13.d_ref = f32[200,128]{1,0:T(8,128)S(1)} collective-permute-done((f32[200,128]{1,0:T(8,128)S(1)}, f32[200,128]{1,0:T(8,128)S(1)}, u32[]{:S(2)}, u32[]{:S(2)}) %collective-permute-start.13) | collective-permute-done | bytes 102432 | tf_op jit(solution)/shard_map/ppermute | solution.py:77
  50.9 0.1 across.2.a_ref
  51.0 1.1 %collective-permute-start.14 = (f32[200,128]{1,0:T(8,128)S(1)}, f32[200,128]{1,0:T(8,128)S(1)}, u32[]{:S(2)}, u32[]{:S(2)}) collective-permute-start(f32[200,128]{1,0:T(8,128)S(1)} %across.2.a_ref), channel_id=1, source_target_pairs={{0,3},{1,8},{2,11},{3,4},{4,7},{5,12},{6,15},{7,0},{8,17},{9,10},{... | collective-permute-start | bytes 307208 | tf_op jit(solution)/shard_map/ppermute | solution.py:77
  52.0 2.0 %collective-permute-start.15 = (f32[200,128]{1,0:T(8,128)S(1)}, f32[200,128]{1,0:T(8,128)S(1)}, u32[]{:S(2)}, u32[]{:S(2)}) collective-permute-start(f32[200,128]{1,0:T(8,128)S(1)} %across.2.a_ref), channel_id=1, source_target_pairs={{0,7},{1,24},{2,27},{3,0},{4,3},{5,28},{6,31},{7,4},{8,1},{9,14},{... | collective-permute-start | bytes 307208 | tf_op jit(solution)/shard_map/ppermute | solution.py:77
  54.0 0.5 collective-permute-start.16
  54.5 2.1 %collective-permute-done.14.b_ref = f32[200,128]{1,0:T(8,128)S(1)} collective-permute-done((f32[200,128]{1,0:T(8,128)S(1)}, f32[200,128]{1,0:T(8,128)S(1)}, u32[]{:S(2)}, u32[]{:S(2)}) %collective-permute-start.14) | collective-permute-done | bytes 102432 | tf_op jit(solution)/shard_map/ppermute | solution.py:77
  56.6 2.4 %collective-permute-done.16.d_ref = f32[200,128]{1,0:T(8,128)S(1)} collective-permute-done((f32[200,128]{1,0:T(8,128)S(1)}, f32[200,128]{1,0:T(8,128)S(1)}, u32[]{:S(2)}, u32[]{:S(2)}) %collective-permute-start.16) | collective-permute-done | bytes 102432 | tf_op jit(solution)/shard_map/ppermute | solution.py:77
  59.0 0.1 across.3
  59.1 2.5 %collective-permute-start.17 = (f32[160,128]{1,0:T(8,128)S(1)}, f32[160,128]{1,0:T(8,128)S(1)}, u32[]{:S(2)}, u32[]{:S(2)}) collective-permute-start(f32[160,128]{1,0:T(8,128)S(1)} %get-tuple-element.56.a_ref), channel_id=1, source_target_pairs={{0,33},{1,2},{2,5},{3,34},{4,37},{5,6},{6,1},{7,38},{8,11},{9,40},... | collective-permute-start | bytes 245768 | tf_op jit(solution)/shard_map/ppermute | solution.py:77
  61.6 1.5 %collective-permute-start.18 = (f32[160,128]{1,0:T(8,128)S(1)}, f32[160,128]{1,0:T(8,128)S(1)}, u32[]{:S(2)}, u32[]{:S(2)}) collective-permute-start(f32[160,128]{1,0:T(8,128)S(1)} %get-tuple-element.56.a_ref), channel_id=1, source_target_pairs={{0,97},{1,6},{2,1},{3,98},{4,101},{5,2},{6,5},{7,102},{8,15},{9,10... | collective-permute-start | bytes 245768 | tf_op jit(solution)/shard_map/ppermute | solution.py:77
  63.1 1.1 %collective-permute-start.19 = (f32[160,128]{1,0:T(8,128)S(1)}, f32[160,128]{1,0:T(8,128)S(1)}, u32[]{:S(2)}, u32[]{:S(2)}) collective-permute-start(f32[160,128]{1,0:T(8,128)S(1)} %get-tuple-element.56.a_ref), channel_id=1, source_target_pairs={{0,64},{1,5},{2,6},{3,67},{4,68},{5,1},{6,2},{7,71},{8,12},{9,73},... | collective-permute-start | bytes 245768 | tf_op jit(solution)/shard_map/ppermute | solution.py:77
  64.2 2.0 %factor.1 = (bf16[64,384]{1,0:T(8,128)(2,1)S(1)}, bf16[320,64]{1,0:T(8,128)(2,1)S(1)}, f32[64,320]{1,0:T(8,128)S(1)}) custom-call(f32[40,128]{1,0:T(8,128)S(1)} %get-tuple-element.52.ext_ref, f32[64,320]{1,0:T(8,128)S(1)} %get-tuple-element.53.p_ref), custom_call_target="tpu_custom_call" | custom-call | flops 4294967296 | bytes 1048576 | tf_op jit(solution)/shard_map/factor/pallas_call | solution.py:411
  66.2 0.0 collective-permute-done.18.c_ref
  66.2 1.7 %collective-permute-done.19.d_ref = f32[160,128]{1,0:T(8,128)S(1)} collective-permute-done((f32[160,128]{1,0:T(8,128)S(1)}, f32[160,128]{1,0:T(8,128)S(1)}, u32[]{:S(2)}, u32[]{:S(2)}) %collective-permute-start.19) | collective-permute-done | bytes 81952 | tf_op jit(solution)/shard_map/ppermute | solution.py:77
  67.9 2.7 %collective-permute-start.22 = (f32[640,128]{1,0:T(8,128)S(1)}, f32[640,128]{1,0:T(8,128)S(1)}, u32[]{:S(2)}, u32[]{:S(2)}) collective-permute-start(f32[640,128]{1,0:T(8,128)S(1)} %assemble.1.refs_0_), channel_id=1, source_target_pairs={{0,1},{1,0},{2,3},{3,2},{4,5},{5,4},{6,7},{7,6},{8,9},{9,8},{10,11... | collective-permute-start | bytes 983048 | tf_op jit(solution)/shard_map/ppermute | solution.py:82
  70.6 2.5 %collective-permute-start.24 = (f32[640,128]{1,0:T(8,128)S(1)}, f32[640,128]{1,0:T(8,128)S(1)}, u32[]{:S(2)}, u32[]{:S(2)}) collective-permute-start(f32[640,128]{1,0:T(8,128)S(1)} %assemble.1.refs_0_), channel_id=1, source_target_pairs={{0,25},{1,96},{2,99},{3,26},{4,29},{5,100},{6,103},{7,30},{8,105},... | collective-permute-start | bytes 983048 | tf_op jit(solution)/shard_map/ppermute | solution.py:77
  73.1 1.6 %result.5 = (bf16[320,10240]{1,0:T(8,128)(2,1)}, f32[64,10240]{1,0:T(8,128)}) custom-call(bf16[64,384]{1,0:T(8,128)(2,1)S(1)} %get-tuple-element.54.after_ref.solve_ref, bf16[320,64]{1,0:T(8,128)(2,1)S(1)} %get-tuple-element.55.left_ref, bf16[320,10240]{1,0:T(8,128)(2,1)S(1)} %get-tuple-element.38.m_ref, f32[640,128]{1,0:T(8,128)S(1)} %assemble.1.refs_0_), custom_call_target="tpu_custom_call" | custom-call | flops 8589934592 | bytes 1048576 | tf_op jit(solution)/shard_map/result/pallas_call | solution.py:491
  74.7 0.0 collective-permute-done.22.refs_0_
  74.7 1.6 %result.6 = (bf16[320,10240]{1,0:T(8,128)(2,1)}, f32[64,10240]{1,0:T(8,128)}, f32[8,128]{1,0:T(8,128)S(1)}) custom-call(bf16[64,384]{1,0:T(8,128)(2,1)S(1)} %get-tuple-element.54.after_ref.solve_ref, bf16[320,64]{1,0:T(8,128)(2,1)S(1)} %get-tuple-element.55.left_ref, ...), custom_call_target="tpu_custom_call", output_to_operand_aliasing={{0}: (4, {}), {1}: (5, {})} | custom-call | flops 8589934592 | bytes 1048576 | tf_op jit(solution)/shard_map/result/pallas_call | solution.py:491
  76.3 2.1 %collective-permute-done.21.value_ref = f32[640,128]{1,0:T(8,128)S(1)} collective-permute-done((f32[640,128]{1,0:T(8,128)S(1)}, f32[640,128]{1,0:T(8,128)S(1)}, u32[]{:S(2)}, u32[]{:S(2)}) %collective-permute-start.21) | collective-permute-done | bytes 327712 | tf_op jit(solution)/shard_map/ppermute | solution.py:77
  78.3 1.1 %collective-permute-start.26 = (f32[640,128]{1,0:T(8,128)S(1)}, f32[640,128]{1,0:T(8,128)S(1)}, u32[]{:S(2)}, u32[]{:S(2)}) collective-permute-start(f32[640,128]{1,0:T(8,128)S(1)} %tie.3.refs_0_), channel_id=1, source_target_pairs={{0,1},{1,0},{2,3},{3,2},{4,5},{5,4},{6,7},{7,6},{8,9},{9,8},{10,11... | collective-permute-start | bytes 983048 | tf_op jit(solution)/shard_map/ppermute | solution.py:82
  79.4 1.6 %result.7 = (bf16[320,10240]{1,0:T(8,128)(2,1)}, f32[64,10240]{1,0:T(8,128)}, f32[8,128]{1,0:T(8,128)S(1)}) custom-call(bf16[64,384]{1,0:T(8,128)(2,1)S(1)} %get-tuple-element.54.after_ref.solve_ref, bf16[320,64]{1,0:T(8,128)(2,1)S(1)} %get-tuple-element.55.left_ref, ...), custom_call_target="tpu_custom_call", output_to_operand_aliasing={{0}: (4, {}), {1}: (5, {})} | custom-call | flops 8589934592 | bytes 1048576 | tf_op jit(solution)/shard_map/result/pallas_call | solution.py:491
  81.0 0.7 collective-permute-done.24.value_ref
  81.7 0.0 collective-permute-start.25
  81.7 0.1 collective-permute-done.20.value_ref
  81.9 0.9 %collective-permute-start.23 = (f32[640,128]{1,0:T(8,128)S(1)}, f32[640,128]{1,0:T(8,128)S(1)}, u32[]{:S(2)}, u32[]{:S(2)}) collective-permute-start(f32[640,128]{1,0:T(8,128)S(1)} %tie.4.refs_0_), channel_id=1, source_target_pairs={{0,1},{1,0},{2,3},{3,2},{4,5},{5,4},{6,7},{7,6},{8,9},{9,8},{10,11... | collective-permute-start | bytes 983048 | tf_op jit(solution)/shard_map/ppermute | solution.py:82
  82.8 2.7 %result.8 = (bf16[320,10240]{1,0:T(8,128)(2,1)}, f32[64,10240]{1,0:T(8,128)}) custom-call(bf16[64,384]{1,0:T(8,128)(2,1)S(1)} %get-tuple-element.54.after_ref.solve_ref, bf16[320,64]{1,0:T(8,128)(2,1)S(1)} %get-tuple-element.55.left_ref, bf16[320,10240]{1,0:T(8,128)(2,1)S(1)} %get-tuple-element.38.m_ref, ...), custom_call_target="tpu_custom_call", output_to_operand_aliasing={{0}: (6, {}), {1}: (7, {})} | custom-call | flops 8589934592 | bytes 1048576 | tf_op jit(solution)/shard_map/result/pallas_call | solution.py:491
  85.5 0.0 collective-permute-done.25.refs_1_
  85.5 2.1 %result.9 = (bf16[320,10240]{1,0:T(8,128)(2,1)}, f32[64,10240]{1,0:T(8,128)}, f32[64,320]{1,0:T(8,128)}) custom-call(bf16[64,384]{1,0:T(8,128)(2,1)S(1)} %get-tuple-element.54.after_ref.solve_ref, bf16[320,64]{1,0:T(8,128)(2,1)S(1)} %get-tuple-element.55.left_ref, ...), custom_call_target="tpu_custom_call", output_to_operand_aliasing={{0}: (6, {}), {1}: (7, {})} | custom-call | flops 8589934592 | bytes 1048576 | tf_op jit(solution)/shard_map/result/pallas_call | solution.py:491
  (11 shorter events, 0.1 us)
Async XLA Ops:
  6.8 6.7 %collective-permute-start = (f32[160,128]{1,0:T(8,128)S(1)}, f32[160,128]{1,0:T(8,128)S(1)}, u32[]{:S(2)}, u32[]{:S(2)}) collective-permute-start(f32[160,128]{1,0:T(8,128)S(1)} %get-tuple-element.37), channel_id=1, source_target_pairs={{0,8},{1,33},{2,10},{3,35},{4,12},{5,37},{6,14},{7,39},{8,16},{9,4... | collective-permute-start | bytes 245768 | tf_op jit(solution)/shard_map/ppermute | solution.py:77
  9.4 4.2 %collective-permute-start.1 = (f32[160,128]{1,0:T(8,128)S(1)}, f32[160,128]{1,0:T(8,128)S(1)}, u32[]{:S(2)}, u32[]{:S(2)}) collective-permute-start(f32[160,128]{1,0:T(8,128)S(1)} %get-tuple-element.37), channel_id=1, source_target_pairs={{0,24},{1,97},{2,26},{3,99},{4,28},{5,101},{6,30},{7,103},{8,0},{9... | collective-permute-start | bytes 245768 | tf_op jit(solution)/shard_map/ppermute | solution.py:77
  11.6 5.1 %collective-permute-start.2 = (f32[160,128]{1,0:T(8,128)S(1)}, f32[160,128]{1,0:T(8,128)S(1)}, u32[]{:S(2)}, u32[]{:S(2)}) collective-permute-start(f32[160,128]{1,0:T(8,128)S(1)} %get-tuple-element.37), channel_id=1, source_target_pairs={{0,16},{1,65},{2,18},{3,67},{4,20},{5,69},{6,22},{7,71},{8,24},{9,... | collective-permute-start | bytes 245768 | tf_op jit(solution)/shard_map/ppermute | solution.py:77
  16.7 4.6 %collective-permute-start.3 = (f32[160,128]{1,0:T(8,128)S(1)}, f32[160,128]{1,0:T(8,128)S(1)}, u32[]{:S(2)}, u32[]{:S(2)}) collective-permute-start(f32[160,128]{1,0:T(8,128)S(1)} %add_add_fusion.a_ref), channel_id=1, source_target_pairs={{0,32},{1,9},{2,34},{3,11},{4,36},{5,13},{6,38},{7,15},{8,40},{9,1... | collective-permute-start | bytes 245768 | tf_op jit(solution)/shard_map/ppermute | solution.py:77
  17.7 3.6 %collective-permute-start.4 = (f32[160,128]{1,0:T(8,128)S(1)}, f32[160,128]{1,0:T(8,128)S(1)}, u32[]{:S(2)}, u32[]{:S(2)}) collective-permute-start(f32[160,128]{1,0:T(8,128)S(1)} %add_add_fusion.a_ref), channel_id=1, source_target_pairs={{0,96},{1,25},{2,98},{3,27},{4,100},{5,29},{6,102},{7,31},{8,104},... | collective-permute-start | bytes 245768 | tf_op jit(solution)/shard_map/ppermute | solution.py:77
  19.4 4.8 %collective-permute-start.5 = (f32[160,128]{1,0:T(8,128)S(1)}, f32[160,128]{1,0:T(8,128)S(1)}, u32[]{:S(2)}, u32[]{:S(2)}) collective-permute-start(f32[160,128]{1,0:T(8,128)S(1)} %add_add_fusion.a_ref), channel_id=1, source_target_pairs={{0,64},{1,17},{2,66},{3,19},{4,68},{5,21},{6,70},{7,23},{8,72},{9,... | collective-permute-start | bytes 245768 | tf_op jit(solution)/shard_map/ppermute | solution.py:77
  24.9 5.0 %collective-permute-start.6 = (f32[680,128]{1,0:T(8,128)S(1)}, f32[680,128]{1,0:T(8,128)S(1)}, u32[]{:S(2)}, u32[]{:S(2)}) collective-permute-start(f32[680,128]{1,0:T(8,128)S(1)} %get-tuple-element.41), channel_id=1, source_target_pairs={{0,1},{1,0},{2,3},{3,2},{4,5},{5,4},{6,7},{7,6},{8,9},{9,8},{10,11... | collective-permute-start | bytes 1044488 | tf_op jit(solution)/shard_map/ppermute | solution.py:82
  29.4 3.2 %collective-permute-start.7 = (f32[1920,128]{1,0:T(8,128)S(1)}, f32[1920,128]{1,0:T(8,128)S(1)}, u32[]{:S(2)}, u32[]{:S(2)}) collective-permute-start(f32[1920,128]{1,0:T(8,128)S(1)} %next_right.3.after_ref), channel_id=1, source_target_pairs={{0,1},{1,0},{2,3},{3,2},{4,5},{5,4},{6,7},{7,6},{8,9},{9,8},{10,11... | collective-permute-start | bytes 2949128 | tf_op jit(solution)/shard_map/ppermute | solution.py:82
  30.1 7.8 %collective-permute-start.10 = (f32[640,128]{1,0:T(8,128)S(1)}, f32[640,128]{1,0:T(8,128)S(1)}, u32[]{:S(2)}, u32[]{:S(2)}) collective-permute-start(f32[640,128]{1,0:T(8,128)S(1)} %get-tuple-element.46), channel_id=1, source_target_pairs={{0,16},{1,65},{2,66},{3,19},{4,20},{5,69},{6,70},{7,23},{8,72},{9,... | collective-permute-start | bytes 983048 | tf_op jit(solution)/shard_map/ppermute | solution.py:77
  32.8 8.6 %collective-permute-start.8 = (f32[640,128]{1,0:T(8,128)S(1)}, f32[640,128]{1,0:T(8,128)S(1)}, u32[]{:S(2)}, u32[]{:S(2)}) collective-permute-start(f32[640,128]{1,0:T(8,128)S(1)} %get-tuple-element.44), channel_id=1, source_target_pairs={{0,9},{1,32},{2,35},{3,10},{4,13},{5,36},{6,39},{7,14},{8,41},{9,1... | collective-permute-start | bytes 983048 | tf_op jit(solution)/shard_map/ppermute | solution.py:77
  34.3 7.3 %collective-permute-start.9 = (f32[640,128]{1,0:T(8,128)S(1)}, f32[640,128]{1,0:T(8,128)S(1)}, u32[]{:S(2)}, u32[]{:S(2)}) collective-permute-start(f32[640,128]{1,0:T(8,128)S(1)} %get-tuple-element.45), channel_id=1, source_target_pairs={{0,25},{1,96},{2,99},{3,26},{4,29},{5,100},{6,103},{7,30},{8,105},... | collective-permute-start | bytes 983048 | tf_op jit(solution)/shard_map/ppermute | solution.py:77
  41.7 6.2 %collective-permute-start.11 = (f32[200,128]{1,0:T(8,128)S(1)}, f32[200,128]{1,0:T(8,128)S(1)}, u32[]{:S(2)}, u32[]{:S(2)}) collective-permute-start(f32[200,128]{1,0:T(8,128)S(1)} %get-tuple-element.49), channel_id=1, source_target_pairs={{0,33},{1,2},{2,5},{3,34},{4,37},{5,6},{6,1},{7,38},{8,11},{9,40},... | collective-permute-start | bytes 307208 | tf_op jit(solution)/shard_map/ppermute | solution.py:77
  44.0 4.1 %collective-permute-start.12 = (f32[200,128]{1,0:T(8,128)S(1)}, f32[200,128]{1,0:T(8,128)S(1)}, u32[]{:S(2)}, u32[]{:S(2)}) collective-permute-start(f32[200,128]{1,0:T(8,128)S(1)} %get-tuple-element.50), channel_id=1, source_target_pairs={{0,97},{1,6},{2,1},{3,98},{4,101},{5,2},{6,5},{7,102},{8,15},{9,10... | collective-permute-start | bytes 307208 | tf_op jit(solution)/shard_map/ppermute | solution.py:77
  45.6 5.3 %collective-permute-start.13 = (f32[200,128]{1,0:T(8,128)S(1)}, f32[200,128]{1,0:T(8,128)S(1)}, u32[]{:S(2)}, u32[]{:S(2)}) collective-permute-start(f32[200,128]{1,0:T(8,128)S(1)} %get-tuple-element.51), channel_id=1, source_target_pairs={{0,64},{1,5},{2,6},{3,67},{4,68},{5,1},{6,2},{7,71},{8,12},{9,73},... | collective-permute-start | bytes 307208 | tf_op jit(solution)/shard_map/ppermute | solution.py:77
  51.0 5.7 %collective-permute-start.14 = (f32[200,128]{1,0:T(8,128)S(1)}, f32[200,128]{1,0:T(8,128)S(1)}, u32[]{:S(2)}, u32[]{:S(2)}) collective-permute-start(f32[200,128]{1,0:T(8,128)S(1)} %across.2.a_ref), channel_id=1, source_target_pairs={{0,3},{1,8},{2,11},{3,4},{4,7},{5,12},{6,15},{7,0},{8,17},{9,10},{... | collective-permute-start | bytes 307208 | tf_op jit(solution)/shard_map/ppermute | solution.py:77
  52.0 4.6 %collective-permute-start.15 = (f32[200,128]{1,0:T(8,128)S(1)}, f32[200,128]{1,0:T(8,128)S(1)}, u32[]{:S(2)}, u32[]{:S(2)}) collective-permute-start(f32[200,128]{1,0:T(8,128)S(1)} %across.2.a_ref), channel_id=1, source_target_pairs={{0,7},{1,24},{2,27},{3,0},{4,3},{5,28},{6,31},{7,4},{8,1},{9,14},{... | collective-permute-start | bytes 307208 | tf_op jit(solution)/shard_map/ppermute | solution.py:77
  54.0 5.0 %collective-permute-start.16 = (f32[200,128]{1,0:T(8,128)S(1)}, f32[200,128]{1,0:T(8,128)S(1)}, u32[]{:S(2)}, u32[]{:S(2)}) collective-permute-start(f32[200,128]{1,0:T(8,128)S(1)} %across.2.a_ref), channel_id=1, source_target_pairs={{0,4},{1,17},{2,18},{3,7},{4,0},{5,21},{6,22},{7,3},{8,24},{9,13},... | collective-permute-start | bytes 307208 | tf_op jit(solution)/shard_map/ppermute | solution.py:77
  59.1 7.1 %collective-permute-start.17 = (f32[160,128]{1,0:T(8,128)S(1)}, f32[160,128]{1,0:T(8,128)S(1)}, u32[]{:S(2)}, u32[]{:S(2)}) collective-permute-start(f32[160,128]{1,0:T(8,128)S(1)} %get-tuple-element.56.a_ref), channel_id=1, source_target_pairs={{0,33},{1,2},{2,5},{3,34},{4,37},{5,6},{6,1},{7,38},{8,11},{9,40},... | collective-permute-start | bytes 245768 | tf_op jit(solution)/shard_map/ppermute | solution.py:77
  61.6 4.7 %collective-permute-start.18 = (f32[160,128]{1,0:T(8,128)S(1)}, f32[160,128]{1,0:T(8,128)S(1)}, u32[]{:S(2)}, u32[]{:S(2)}) collective-permute-start(f32[160,128]{1,0:T(8,128)S(1)} %get-tuple-element.56.a_ref), channel_id=1, source_target_pairs={{0,97},{1,6},{2,1},{3,98},{4,101},{5,2},{6,5},{7,102},{8,15},{9,10... | collective-permute-start | bytes 245768 | tf_op jit(solution)/shard_map/ppermute | solution.py:77
  63.1 4.8 %collective-permute-start.19 = (f32[160,128]{1,0:T(8,128)S(1)}, f32[160,128]{1,0:T(8,128)S(1)}, u32[]{:S(2)}, u32[]{:S(2)}) collective-permute-start(f32[160,128]{1,0:T(8,128)S(1)} %get-tuple-element.56.a_ref), channel_id=1, source_target_pairs={{0,64},{1,5},{2,6},{3,67},{4,68},{5,1},{6,2},{7,71},{8,12},{9,73},... | collective-permute-start | bytes 245768 | tf_op jit(solution)/shard_map/ppermute | solution.py:77
  67.9 6.7 %collective-permute-start.22 = (f32[640,128]{1,0:T(8,128)S(1)}, f32[640,128]{1,0:T(8,128)S(1)}, u32[]{:S(2)}, u32[]{:S(2)}) collective-permute-start(f32[640,128]{1,0:T(8,128)S(1)} %assemble.1.refs_0_), channel_id=1, source_target_pairs={{0,1},{1,0},{2,3},{3,2},{4,5},{5,4},{6,7},{7,6},{8,9},{9,8},{10,11... | collective-permute-start | bytes 983048 | tf_op jit(solution)/shard_map/ppermute | solution.py:82
  70.6 7.7 %collective-permute-start.21 = (f32[640,128]{1,0:T(8,128)S(1)}, f32[640,128]{1,0:T(8,128)S(1)}, u32[]{:S(2)}, u32[]{:S(2)}) collective-permute-start(f32[640,128]{1,0:T(8,128)S(1)} %assemble.1.refs_0_), channel_id=1, source_target_pairs={{0,16},{1,65},{2,66},{3,19},{4,20},{5,69},{6,70},{7,23},{8,72},{9,... | collective-permute-start | bytes 983048 | tf_op jit(solution)/shard_map/ppermute | solution.py:77
  70.6 11.1 %collective-permute-start.24 = (f32[640,128]{1,0:T(8,128)S(1)}, f32[640,128]{1,0:T(8,128)S(1)}, u32[]{:S(2)}, u32[]{:S(2)}) collective-permute-start(f32[640,128]{1,0:T(8,128)S(1)} %assemble.1.refs_0_), channel_id=1, source_target_pairs={{0,25},{1,96},{2,99},{3,26},{4,29},{5,100},{6,103},{7,30},{8,105},... | collective-permute-start | bytes 983048 | tf_op jit(solution)/shard_map/ppermute | solution.py:77
  73.1 8.7 %collective-permute-start.20 = (f32[640,128]{1,0:T(8,128)S(1)}, f32[640,128]{1,0:T(8,128)S(1)}, u32[]{:S(2)}, u32[]{:S(2)}) collective-permute-start(f32[640,128]{1,0:T(8,128)S(1)} %assemble.1.refs_0_), channel_id=1, source_target_pairs={{0,9},{1,32},{2,35},{3,10},{4,13},{5,36},{6,39},{7,14},{8,41},{9,1... | collective-permute-start | bytes 983048 | tf_op jit(solution)/shard_map/ppermute | solution.py:77
  78.3 4.5 %collective-permute-start.26 = (f32[640,128]{1,0:T(8,128)S(1)}, f32[640,128]{1,0:T(8,128)S(1)}, u32[]{:S(2)}, u32[]{:S(2)}) collective-permute-start(f32[640,128]{1,0:T(8,128)S(1)} %tie.3.refs_0_), channel_id=1, source_target_pairs={{0,1},{1,0},{2,3},{3,2},{4,5},{5,4},{6,7},{7,6},{8,9},{9,8},{10,11... | collective-permute-start | bytes 983048 | tf_op jit(solution)/shard_map/ppermute | solution.py:82
  81.7 3.8 %collective-permute-start.25 = (f32[640,128]{1,0:T(8,128)S(1)}, f32[640,128]{1,0:T(8,128)S(1)}, u32[]{:S(2)}, u32[]{:S(2)}) collective-permute-start(f32[640,128]{1,0:T(8,128)S(1)} %tie.5.refs_1_), channel_id=1, source_target_pairs={{0,1},{1,0},{2,3},{3,2},{4,5},{5,4},{6,7},{7,6},{8,9},{9,8},{10,11... | collective-permute-start | bytes 983048 | tf_op jit(solution)/shard_map/ppermute | solution.py:82
  81.9 3.7 %collective-permute-start.23 = (f32[640,128]{1,0:T(8,128)S(1)}, f32[640,128]{1,0:T(8,128)S(1)}, u32[]{:S(2)}, u32[]{:S(2)}) collective-permute-start(f32[640,128]{1,0:T(8,128)S(1)} %tie.4.refs_0_), channel_id=1, source_target_pairs={{0,1},{1,0},{2,3},{3,2},{4,5},{5,4},{6,7},{7,6},{8,9},{9,8},{10,11... | collective-permute-start | bytes 983048 | tf_op jit(solution)/shard_map/ppermute | solution.py:82

commit v14 on v13

--- a/solution.py
+++ b/solution.py
@@ -16,6 +16,7 @@
 MIB = 1 << 20
 ROWS = 8
 QUARTERS = 4
+SHRINK = 2.0**-16
 RIGHT = 1 << 33
 SHIFTS = (1, 3, 2)
 ANY = pl.BlockSpec(memory_space=pl.ANY)
@@ -184,7 +185,7 @@
     peak = jnp.where(peak > 0, peak, 1.0)
     p = unpack(p, rank)
     p_ref[...] = p
-    pieces = jnp.concatenate(split(p / peak), axis=0)
+    pieces = jnp.concatenate(split(p / peak * SHRINK), axis=0)
     pieces_ref[...] = pieces
     right_tiles(quarters_of(False, turns), pieces, m_ref, out_ref)
     gram = lax.dot_general(
@@ -399,7 +400,8 @@
         inverse.append(blocks[g][:, rank:] / jnp.sqrt(diagonal))
     inverse = jnp.concatenate(inverse, axis=0)
     grams = ext_ref.shape[0] - ROWS
-    s1, s2, s3 = split(inverse * (ext_ref[grams : grams + 1, :1] * (1.0 / replicas)))
+    solve = inverse * ext_ref[grams : grams + 1, :1] * (1.0 / (replicas * SHRINK))
+    s1, s2, s3 = split(solve)
     solve_ref[...] = jnp.concatenate([s1, s1, s2, s2, s1, s3], axis=1)
     hat = jnp.dot(inverse, p_ref[...], precision=HIGHEST, preferred_element_type=F32)
     hat_ref[...] = hat

time: 87.9 us -> 87.9 us (level)
  no operation moved by 1% of the time
where the time goes in v14:
time: 87.9 us; the launch traced here: 87.8 us
  starting transfers between devices  39.1 us (44%)
  waiting for transfers between devices  26.5 us (30%)
  Pallas kernels  21.3 us (24%)
  between operations  0.98 us (1%)
    ppermute x21, starting transfers between devices, ring(): out.append(lax.ppermute(value, AXES, pairs))  30.7 us
    ppermute x21, waiting for transfers between devices, ring(): out.append(lax.ppermute(value, AXES, pairs))  26.5 us
    pallas_call x5, Pallas kernels, result(): pl.pallas_call(functools.partial(result_kernel, sources, more, quarter //...  9.5 us
    ppermute x6, starting transfers between devices, swap(): return lax.ppermute(value, 'c', [(0, 1), (1, 0)])  8.36 us
    pallas_call x1, Pallas kernels, merge(): pl.pallas_call(functools.partial(merge_kernel, cuts), out_shape=[pltpu.VM...  6.21 us
    pallas_call x3, Pallas kernels, next_right(): pl.pallas_call(functools.partial(next_right_kernel, own, turns), out_shap...  2.25 us
    pallas_call x1, Pallas kernels, factor(): pl.pallas_call(functools.partial(factor_kernel, replicas), out_shape=[jax...  2.01 us
  transfers between devices with their start and end apart: 27, of which 16 were waited for; matrix products, arithmetic and copies ran while one was open for 0% of the time, Pallas kernels for 14%

profile of v14, /device:TPU:1, one launch (start us, length us, event | category | flops | bytes accessed | tf_op | source)
XLA Modules:
  0.0 87.8 jit_solution(8483967396656695447)
XLA Ops:
  0.6 6.2 %merge.1 = (bf16[320,10240]{1,0:T(8,128)(2,1)S(1)}, f32[160,128]{1,0:T(8,128)S(1)}) custom-call(bf16[320,10240]{1,0:T(8,128)(2,1)} %bitcast.3, bf16[320,10240]{1,0:T(8,128)(2,1)} %bitcast.4, bf16[64,10240]{1,0:T(8,128)(2,1)} %q_hbm.1), custom_call_target="tpu_custom_call" | custom-call | flops 419430400 | bytes 13107200 | tf_op jit(solution)/shard_map/merge/pallas_call | solution.py:139
  6.8 2.5 %collective-permute-start = (f32[160,128]{1,0:T(8,128)S(1)}, f32[160,128]{1,0:T(8,128)S(1)}, u32[]{:S(2)}, u32[]{:S(2)}) collective-permute-start(f32[160,128]{1,0:T(8,128)S(1)} %get-tuple-element.37), channel_id=1, source_target_pairs={{0,8},{1,33},{2,10},{3,35},{4,12},{5,37},{6,14},{7,39},{8,16},{9,4... | collective-permute-start | bytes 245768 | tf_op jit(solution)/shard_map/ppermute | solution.py:78
  9.4 2.2 %collective-permute-start.1 = (f32[160,128]{1,0:T(8,128)S(1)}, f32[160,128]{1,0:T(8,128)S(1)}, u32[]{:S(2)}, u32[]{:S(2)}) collective-permute-start(f32[160,128]{1,0:T(8,128)S(1)} %get-tuple-element.37), channel_id=1, source_target_pairs={{0,24},{1,97},{2,26},{3,99},{4,28},{5,101},{6,30},{7,103},{8,0},{9... | collective-permute-start | bytes 245768 | tf_op jit(solution)/shard_map/ppermute | solution.py:78
  11.6 1.2 %collective-permute-start.2 = (f32[160,128]{1,0:T(8,128)S(1)}, f32[160,128]{1,0:T(8,128)S(1)}, u32[]{:S(2)}, u32[]{:S(2)}) collective-permute-start(f32[160,128]{1,0:T(8,128)S(1)} %get-tuple-element.37), channel_id=1, source_target_pairs={{0,16},{1,65},{2,18},{3,67},{4,20},{5,69},{6,22},{7,71},{8,24},{9,... | collective-permute-start | bytes 245768 | tf_op jit(solution)/shard_map/ppermute | solution.py:78
  12.8 0.8 collective-permute-done
  13.6 0.0 collective-permute-done.1
  13.6 3.1 %collective-permute-done.2 = f32[160,128]{1,0:T(8,128)S(1)} collective-permute-done((f32[160,128]{1,0:T(8,128)S(1)}, f32[160,128]{1,0:T(8,128)S(1)}, u32[]{:S(2)}, u32[]{:S(2)}) %collective-permute-start.2) | collective-permute-done | bytes 81952 | tf_op jit(solution)/shard_map/ppermute | solution.py:78
  16.7 1.0 %collective-permute-start.3 = (f32[160,128]{1,0:T(8,128)S(1)}, f32[160,128]{1,0:T(8,128)S(1)}, u32[]{:S(2)}, u32[]{:S(2)}) collective-permute-start(f32[160,128]{1,0:T(8,128)S(1)} %add_add_fusion.a_ref), channel_id=1, source_target_pairs={{0,32},{1,9},{2,34},{3,11},{4,36},{5,13},{6,38},{7,15},{8,40},{9,1... | collective-permute-start | bytes 245768 | tf_op jit(solution)/shard_map/ppermute | solution.py:78
  17.7 1.8 %collective-permute-start.4 = (f32[160,128]{1,0:T(8,128)S(1)}, f32[160,128]{1,0:T(8,128)S(1)}, u32[]{:S(2)}, u32[]{:S(2)}) collective-permute-start(f32[160,128]{1,0:T(8,128)S(1)} %add_add_fusion.a_ref), channel_id=1, source_target_pairs={{0,96},{1,25},{2,98},{3,27},{4,100},{5,29},{6,102},{7,31},{8,104},... | collective-permute-start | bytes 245768 | tf_op jit(solution)/shard_map/ppermute | solution.py:78
  19.4 1.2 %collective-permute-start.5 = (f32[160,128]{1,0:T(8,128)S(1)}, f32[160,128]{1,0:T(8,128)S(1)}, u32[]{:S(2)}, u32[]{:S(2)}) collective-permute-start(f32[160,128]{1,0:T(8,128)S(1)} %add_add_fusion.a_ref), channel_id=1, source_target_pairs={{0,64},{1,17},{2,66},{3,19},{4,68},{5,21},{6,70},{7,23},{8,72},{9,... | collective-permute-start | bytes 245768 | tf_op jit(solution)/shard_map/ppermute | solution.py:78
  20.7 0.6 collective-permute-done.3.b_ref
  21.3 0.0 collective-permute-done.4.c_ref
  21.3 3.0 %collective-permute-done.5.d_ref = f32[160,128]{1,0:T(8,128)S(1)} collective-permute-done((f32[160,128]{1,0:T(8,128)S(1)}, f32[160,128]{1,0:T(8,128)S(1)}, u32[]{:S(2)}, u32[]{:S(2)}) %collective-permute-start.5) | collective-permute-done | bytes 81952 | tf_op jit(solution)/shard_map/ppermute | solution.py:78
  24.2 0.7 first_right.1
  24.9 3.5 %collective-permute-start.6 = (f32[680,128]{1,0:T(8,128)S(1)}, f32[680,128]{1,0:T(8,128)S(1)}, u32[]{:S(2)}, u32[]{:S(2)}) collective-permute-start(f32[680,128]{1,0:T(8,128)S(1)} %get-tuple-element.41), channel_id=1, source_target_pairs={{0,1},{1,0},{2,3},{3,2},{4,5},{5,4},{6,7},{7,6},{8,9},{9,8},{10,11... | collective-permute-start | bytes 1044488 | tf_op jit(solution)/shard_map/ppermute | solution.py:83
  28.5 0.9 %next_right.3.after_ref = f32[1920,128]{1,0:T(8,128)S(1)} custom-call(bf16[192,320]{1,0:T(8,128)(2,1)S(1)} %get-tuple-element.39.pieces_ref, bf16[320,10240]{1,0:T(8,128)(2,1)S(1)} %get-tuple-element.38.m_ref, f32[40,128]{1,0:T(8,128)S(1)} %get-tuple-element.40.after_ref.ext_ref), custom_call_target="tpu_custom_call" | custom-call | flops 8589934592 | bytes 1048576 | tf_op jit(solution)/shard_map/next_right/pallas_call | solution.py:234
  29.4 0.1 collective-permute-start.7
  29.5 0.4 next_right.4.kept_ref
  29.9 0.0 collective-permute-done.6.got_ref
  30.0 0.1 first_pair.1
  30.1 1.6 %collective-permute-start.10 = (f32[640,128]{1,0:T(8,128)S(1)}, f32[640,128]{1,0:T(8,128)S(1)}, u32[]{:S(2)}, u32[]{:S(2)}) collective-permute-start(f32[640,128]{1,0:T(8,128)S(1)} %get-tuple-element.46), channel_id=1, source_target_pairs={{0,16},{1,65},{2,66},{3,19},{4,20},{5,69},{6,70},{7,23},{8,72},{9,... | collective-permute-start | bytes 983048 | tf_op jit(solution)/shard_map/ppermute | solution.py:78
  31.7 0.9 %next_right.5.kept_ref = f32[1920,128]{1,0:T(8,128)S(1)} custom-call(bf16[192,320]{1,0:T(8,128)(2,1)S(1)} %get-tuple-element.39.pieces_ref, bf16[320,10240]{1,0:T(8,128)(2,1)S(1)} %get-tuple-element.38.m_ref, f32[16,128]{1,0:T(8,128)S(1)} %get-tuple-element.42.after_ref.weight_ref), custom_call_target="tpu_custom_call" | custom-call | flops 8589934592 | bytes 1048576 | tf_op jit(solution)/shard_map/next_right/pallas_call | solution.py:234
  32.6 0.0 collective-permute-done.7.got_ref
  32.6 0.2 next_pair.1
  32.8 1.4 %collective-permute-start.8 = (f32[640,128]{1,0:T(8,128)S(1)}, f32[640,128]{1,0:T(8,128)S(1)}, u32[]{:S(2)}, u32[]{:S(2)}) collective-permute-start(f32[640,128]{1,0:T(8,128)S(1)} %get-tuple-element.44), channel_id=1, source_target_pairs={{0,9},{1,32},{2,35},{3,10},{4,13},{5,36},{6,39},{7,14},{8,41},{9,1... | collective-permute-start | bytes 983048 | tf_op jit(solution)/shard_map/ppermute | solution.py:78
  34.3 1.6 %collective-permute-start.9 = (f32[640,128]{1,0:T(8,128)S(1)}, f32[640,128]{1,0:T(8,128)S(1)}, u32[]{:S(2)}, u32[]{:S(2)}) collective-permute-start(f32[640,128]{1,0:T(8,128)S(1)} %get-tuple-element.45), channel_id=1, source_target_pairs={{0,25},{1,96},{2,99},{3,26},{4,29},{5,100},{6,103},{7,30},{8,105},... | collective-permute-start | bytes 983048 | tf_op jit(solution)/shard_map/ppermute | solution.py:78
  35.9 2.0 %collective-permute-done.10.d_ref = f32[640,128]{1,0:T(8,128)S(1)} collective-permute-done((f32[640,128]{1,0:T(8,128)S(1)}, f32[640,128]{1,0:T(8,128)S(1)}, u32[]{:S(2)}, u32[]{:S(2)}) %collective-permute-start.10) | collective-permute-done | bytes 327712 | tf_op jit(solution)/shard_map/ppermute | solution.py:78
  37.9 3.5 %collective-permute-done.8.b_ref = f32[640,128]{1,0:T(8,128)S(1)} collective-permute-done((f32[640,128]{1,0:T(8,128)S(1)}, f32[640,128]{1,0:T(8,128)S(1)}, u32[]{:S(2)}, u32[]{:S(2)}) %collective-permute-start.8) | collective-permute-done | bytes 327712 | tf_op jit(solution)/shard_map/ppermute | solution.py:78
  41.4 0.2 collective-permute-done.9.c_ref
  41.6 0.1 add_quarters.1
  41.7 2.4 %collective-permute-start.11 = (f32[200,128]{1,0:T(8,128)S(1)}, f32[200,128]{1,0:T(8,128)S(1)}, u32[]{:S(2)}, u32[]{:S(2)}) collective-permute-start(f32[200,128]{1,0:T(8,128)S(1)} %get-tuple-element.49), channel_id=1, source_target_pairs={{0,33},{1,2},{2,5},{3,34},{4,37},{5,6},{6,1},{7,38},{8,11},{9,40},... | collective-permute-start | bytes 307208 | tf_op jit(solution)/shard_map/ppermute | solution.py:78
  44.1 1.5 %collective-permute-start.12 = (f32[200,128]{1,0:T(8,128)S(1)}, f32[200,128]{1,0:T(8,128)S(1)}, u32[]{:S(2)}, u32[]{:S(2)}) collective-permute-start(f32[200,128]{1,0:T(8,128)S(1)} %get-tuple-element.50), channel_id=1, source_target_pairs={{0,97},{1,6},{2,1},{3,98},{4,101},{5,2},{6,5},{7,102},{8,15},{9,10... | collective-permute-start | bytes 307208 | tf_op jit(solution)/shard_map/ppermute | solution.py:78
  45.6 1.1 %collective-permute-start.13 = (f32[200,128]{1,0:T(8,128)S(1)}, f32[200,128]{1,0:T(8,128)S(1)}, u32[]{:S(2)}, u32[]{:S(2)}) collective-permute-start(f32[200,128]{1,0:T(8,128)S(1)} %get-tuple-element.51), channel_id=1, source_target_pairs={{0,64},{1,5},{2,6},{3,67},{4,68},{5,1},{6,2},{7,71},{8,12},{9,73},... | collective-permute-start | bytes 307208 | tf_op jit(solution)/shard_map/ppermute | solution.py:78
  46.7 1.2 %collective-permute-done.11.b_ref = f32[200,128]{1,0:T(8,128)S(1)} collective-permute-done((f32[200,128]{1,0:T(8,128)S(1)}, f32[200,128]{1,0:T(8,128)S(1)}, u32[]{:S(2)}, u32[]{:S(2)}) %collective-permute-start.11) | collective-permute-done | bytes 102432 | tf_op jit(solution)/shard_map/ppermute | solution.py:78
  47.8 0.3 collective-permute-done.12.c_ref
  48.1 2.7 %collective-permute-done.13.d_ref = f32[200,128]{1,0:T(8,128)S(1)} collective-permute-done((f32[200,128]{1,0:T(8,128)S(1)}, f32[200,128]{1,0:T(8,128)S(1)}, u32[]{:S(2)}, u32[]{:S(2)}) %collective-permute-start.13) | collective-permute-done | bytes 102432 | tf_op jit(solution)/shard_map/ppermute | solution.py:78
  50.9 0.1 across.2.a_ref
  51.0 1.1 %collective-permute-start.14 = (f32[200,128]{1,0:T(8,128)S(1)}, f32[200,128]{1,0:T(8,128)S(1)}, u32[]{:S(2)}, u32[]{:S(2)}) collective-permute-start(f32[200,128]{1,0:T(8,128)S(1)} %across.2.a_ref), channel_id=1, source_target_pairs={{0,3},{1,8},{2,11},{3,4},{4,7},{5,12},{6,15},{7,0},{8,17},{9,10},{... | collective-permute-start | bytes 307208 | tf_op jit(solution)/shard_map/ppermute | solution.py:78
  52.0 2.0 %collective-permute-start.15 = (f32[200,128]{1,0:T(8,128)S(1)}, f32[200,128]{1,0:T(8,128)S(1)}, u32[]{:S(2)}, u32[]{:S(2)}) collective-permute-start(f32[200,128]{1,0:T(8,128)S(1)} %across.2.a_ref), channel_id=1, source_target_pairs={{0,7},{1,24},{2,27},{3,0},{4,3},{5,28},{6,31},{7,4},{8,1},{9,14},{... | collective-permute-start | bytes 307208 | tf_op jit(solution)/shard_map/ppermute | solution.py:78
  54.0 0.5 collective-permute-start.16
  54.5 2.1 %collective-permute-done.14.b_ref = f32[200,128]{1,0:T(8,128)S(1)} collective-permute-done((f32[200,128]{1,0:T(8,128)S(1)}, f32[200,128]{1,0:T(8,128)S(1)}, u32[]{:S(2)}, u32[]{:S(2)}) %collective-permute-start.14) | collective-permute-done | bytes 102432 | tf_op jit(solution)/shard_map/ppermute | solution.py:78
  56.6 0.0 collective-permute-done.15.c_ref
  56.6 2.4 %collective-permute-done.16.d_ref = f32[200,128]{1,0:T(8,128)S(1)} collective-permute-done((f32[200,128]{1,0:T(8,128)S(1)}, f32[200,128]{1,0:T(8,128)S(1)}, u32[]{:S(2)}, u32[]{:S(2)}) %collective-permute-start.16) | collective-permute-done | bytes 102432 | tf_op jit(solution)/shard_map/ppermute | solution.py:78
  59.0 0.1 across.3
  59.1 2.5 %collective-permute-start.17 = (f32[160,128]{1,0:T(8,128)S(1)}, f32[160,128]{1,0:T(8,128)S(1)}, u32[]{:S(2)}, u32[]{:S(2)}) collective-permute-start(f32[160,128]{1,0:T(8,128)S(1)} %get-tuple-element.56.a_ref), channel_id=1, source_target_pairs={{0,33},{1,2},{2,5},{3,34},{4,37},{5,6},{6,1},{7,38},{8,11},{9,40},... | collective-permute-start | bytes 245768 | tf_op jit(solution)/shard_map/ppermute | solution.py:78
  61.6 1.5 %collective-permute-start.18 = (f32[160,128]{1,0:T(8,128)S(1)}, f32[160,128]{1,0:T(8,128)S(1)}, u32[]{:S(2)}, u32[]{:S(2)}) collective-permute-start(f32[160,128]{1,0:T(8,128)S(1)} %get-tuple-element.56.a_ref), channel_id=1, source_target_pairs={{0,97},{1,6},{2,1},{3,98},{4,101},{5,2},{6,5},{7,102},{8,15},{9,10... | collective-permute-start | bytes 245768 | tf_op jit(solution)/shard_map/ppermute | solution.py:78
  63.1 1.1 %collective-permute-start.19 = (f32[160,128]{1,0:T(8,128)S(1)}, f32[160,128]{1,0:T(8,128)S(1)}, u32[]{:S(2)}, u32[]{:S(2)}) collective-permute-start(f32[160,128]{1,0:T(8,128)S(1)} %get-tuple-element.56.a_ref), channel_id=1, source_target_pairs={{0,64},{1,5},{2,6},{3,67},{4,68},{5,1},{6,2},{7,71},{8,12},{9,73},... | collective-permute-start | bytes 245768 | tf_op jit(solution)/shard_map/ppermute | solution.py:78
  64.2 2.0 %factor.1 = (bf16[64,384]{1,0:T(8,128)(2,1)S(1)}, bf16[320,64]{1,0:T(8,128)(2,1)S(1)}, f32[64,320]{1,0:T(8,128)S(1)}) custom-call(f32[40,128]{1,0:T(8,128)S(1)} %get-tuple-element.52.ext_ref, f32[64,320]{1,0:T(8,128)S(1)} %get-tuple-element.53.p_ref), custom_call_target="tpu_custom_call" | custom-call | flops 4294967296 | bytes 1048576 | tf_op jit(solution)/shard_map/factor/pallas_call | solution.py:413
  66.2 1.7 %collective-permute-done.19.d_ref = f32[160,128]{1,0:T(8,128)S(1)} collective-permute-done((f32[160,128]{1,0:T(8,128)S(1)}, f32[160,128]{1,0:T(8,128)S(1)}, u32[]{:S(2)}, u32[]{:S(2)}) %collective-permute-start.19) | collective-permute-done | bytes 81952 | tf_op jit(solution)/shard_map/ppermute | solution.py:78
  67.9 2.7 %collective-permute-start.22 = (f32[640,128]{1,0:T(8,128)S(1)}, f32[640,128]{1,0:T(8,128)S(1)}, u32[]{:S(2)}, u32[]{:S(2)}) collective-permute-start(f32[640,128]{1,0:T(8,128)S(1)} %assemble.1.refs_0_), channel_id=1, source_target_pairs={{0,1},{1,0},{2,3},{3,2},{4,5},{5,4},{6,7},{7,6},{8,9},{9,8},{10,11... | collective-permute-start | bytes 983048 | tf_op jit(solution)/shard_map/ppermute | solution.py:83
  70.6 2.5 %collective-permute-start.24 = (f32[640,128]{1,0:T(8,128)S(1)}, f32[640,128]{1,0:T(8,128)S(1)}, u32[]{:S(2)}, u32[]{:S(2)}) collective-permute-start(f32[640,128]{1,0:T(8,128)S(1)} %assemble.1.refs_0_), channel_id=1, source_target_pairs={{0,25},{1,96},{2,99},{3,26},{4,29},{5,100},{6,103},{7,30},{8,105},... | collective-permute-start | bytes 983048 | tf_op jit(solution)/shard_map/ppermute | solution.py:78
  73.1 0.0 collective-permute-start.20
  73.1 1.6 %result.5 = (bf16[320,10240]{1,0:T(8,128)(2,1)}, f32[64,10240]{1,0:T(8,128)}) custom-call(bf16[64,384]{1,0:T(8,128)(2,1)S(1)} %get-tuple-element.54.after_ref.solve_ref, bf16[320,64]{1,0:T(8,128)(2,1)S(1)} %get-tuple-element.55.left_ref, bf16[320,10240]{1,0:T(8,128)(2,1)S(1)} %get-tuple-element.38.m_ref, f32[640,128]{1,0:T(8,128)S(1)} %assemble.1.refs_0_), custom_call_target="tpu_custom_call" | custom-call | flops 8589934592 | bytes 1048576 | tf_op jit(solution)/shard_map/result/pallas_call | solution.py:493
  74.7 0.0 collective-permute-done.22.refs_0_
  74.7 1.6 %result.6 = (bf16[320,10240]{1,0:T(8,128)(2,1)}, f32[64,10240]{1,0:T(8,128)}, f32[8,128]{1,0:T(8,128)S(1)}) custom-call(bf16[64,384]{1,0:T(8,128)(2,1)S(1)} %get-tuple-element.54.after_ref.solve_ref, bf16[320,64]{1,0:T(8,128)(2,1)S(1)} %get-tuple-element.55.left_ref, ...), custom_call_target="tpu_custom_call", output_to_operand_aliasing={{0}: (4, {}), {1}: (5, {})} | custom-call | flops 8589934592 | bytes 1048576 | tf_op jit(solution)/shard_map/result/pallas_call | solution.py:493
  76.3 2.1 %collective-permute-done.21.value_ref = f32[640,128]{1,0:T(8,128)S(1)} collective-permute-done((f32[640,128]{1,0:T(8,128)S(1)}, f32[640,128]{1,0:T(8,128)S(1)}, u32[]{:S(2)}, u32[]{:S(2)}) %collective-permute-start.21) | collective-permute-done | bytes 327712 | tf_op jit(solution)/shard_map/ppermute | solution.py:78
  78.4 1.1 %collective-permute-start.26 = (f32[640,128]{1,0:T(8,128)S(1)}, f32[640,128]{1,0:T(8,128)S(1)}, u32[]{:S(2)}, u32[]{:S(2)}) collective-permute-start(f32[640,128]{1,0:T(8,128)S(1)} %tie.3.refs_0_), channel_id=1, source_target_pairs={{0,1},{1,0},{2,3},{3,2},{4,5},{5,4},{6,7},{7,6},{8,9},{9,8},{10,11... | collective-permute-start | bytes 983048 | tf_op jit(solution)/shard_map/ppermute | solution.py:83
  79.4 1.6 %result.7 = (bf16[320,10240]{1,0:T(8,128)(2,1)}, f32[64,10240]{1,0:T(8,128)}, f32[8,128]{1,0:T(8,128)S(1)}) custom-call(bf16[64,384]{1,0:T(8,128)(2,1)S(1)} %get-tuple-element.54.after_ref.solve_ref, bf16[320,64]{1,0:T(8,128)(2,1)S(1)} %get-tuple-element.55.left_ref, ...), custom_call_target="tpu_custom_call", output_to_operand_aliasing={{0}: (4, {}), {1}: (5, {})} | custom-call | flops 8589934592 | bytes 1048576 | tf_op jit(solution)/shard_map/result/pallas_call | solution.py:493
  81.0 0.7 collective-permute-done.24.value_ref
  81.7 0.2 collective-permute-done.20.value_ref
  81.9 0.9 %collective-permute-start.23 = (f32[640,128]{1,0:T(8,128)S(1)}, f32[640,128]{1,0:T(8,128)S(1)}, u32[]{:S(2)}, u32[]{:S(2)}) collective-permute-start(f32[640,128]{1,0:T(8,128)S(1)} %tie.4.refs_0_), channel_id=1, source_target_pairs={{0,1},{1,0},{2,3},{3,2},{4,5},{5,4},{6,7},{7,6},{8,9},{9,8},{10,11... | collective-permute-start | bytes 983048 | tf_op jit(solution)/shard_map/ppermute | solution.py:83
  82.8 2.7 %result.8 = (bf16[320,10240]{1,0:T(8,128)(2,1)}, f32[64,10240]{1,0:T(8,128)}) custom-call(bf16[64,384]{1,0:T(8,128)(2,1)S(1)} %get-tuple-element.54.after_ref.solve_ref, bf16[320,64]{1,0:T(8,128)(2,1)S(1)} %get-tuple-element.55.left_ref, bf16[320,10240]{1,0:T(8,128)(2,1)S(1)} %get-tuple-element.38.m_ref, ...), custom_call_target="tpu_custom_call", output_to_operand_aliasing={{0}: (6, {}), {1}: (7, {})} | custom-call | flops 8589934592 | bytes 1048576 | tf_op jit(solution)/shard_map/result/pallas_call | solution.py:493
  85.5 0.0 collective-permute-done.23.refs_0_
  85.5 2.1 %result.9 = (bf16[320,10240]{1,0:T(8,128)(2,1)}, f32[64,10240]{1,0:T(8,128)}, f32[64,320]{1,0:T(8,128)}) custom-call(bf16[64,384]{1,0:T(8,128)(2,1)S(1)} %get-tuple-element.54.after_ref.solve_ref, bf16[320,64]{1,0:T(8,128)(2,1)S(1)} %get-tuple-element.55.left_ref, ...), custom_call_target="tpu_custom_call", output_to_operand_aliasing={{0}: (6, {}), {1}: (7, {})} | custom-call | flops 8589934592 | bytes 1048576 | tf_op jit(solution)/shard_map/result/pallas_call | solution.py:493
  (11 shorter events, 0.1 us)
Async XLA Ops:
  6.8 6.7 %collective-permute-start = (f32[160,128]{1,0:T(8,128)S(1)}, f32[160,128]{1,0:T(8,128)S(1)}, u32[]{:S(2)}, u32[]{:S(2)}) collective-permute-start(f32[160,128]{1,0:T(8,128)S(1)} %get-tuple-element.37), channel_id=1, source_target_pairs={{0,8},{1,33},{2,10},{3,35},{4,12},{5,37},{6,14},{7,39},{8,16},{9,4... | collective-permute-start | bytes 245768 | tf_op jit(solution)/shard_map/ppermute | solution.py:78
  9.4 4.2 %collective-permute-start.1 = (f32[160,128]{1,0:T(8,128)S(1)}, f32[160,128]{1,0:T(8,128)S(1)}, u32[]{:S(2)}, u32[]{:S(2)}) collective-permute-start(f32[160,128]{1,0:T(8,128)S(1)} %get-tuple-element.37), channel_id=1, source_target_pairs={{0,24},{1,97},{2,26},{3,99},{4,28},{5,101},{6,30},{7,103},{8,0},{9... | collective-permute-start | bytes 245768 | tf_op jit(solution)/shard_map/ppermute | solution.py:78
  11.6 5.1 %collective-permute-start.2 = (f32[160,128]{1,0:T(8,128)S(1)}, f32[160,128]{1,0:T(8,128)S(1)}, u32[]{:S(2)}, u32[]{:S(2)}) collective-permute-start(f32[160,128]{1,0:T(8,128)S(1)} %get-tuple-element.37), channel_id=1, source_target_pairs={{0,16},{1,65},{2,18},{3,67},{4,20},{5,69},{6,22},{7,71},{8,24},{9,... | collective-permute-start | bytes 245768 | tf_op jit(solution)/shard_map/ppermute | solution.py:78
  16.7 4.6 %collective-permute-start.3 = (f32[160,128]{1,0:T(8,128)S(1)}, f32[160,128]{1,0:T(8,128)S(1)}, u32[]{:S(2)}, u32[]{:S(2)}) collective-permute-start(f32[160,128]{1,0:T(8,128)S(1)} %add_add_fusion.a_ref), channel_id=1, source_target_pairs={{0,32},{1,9},{2,34},{3,11},{4,36},{5,13},{6,38},{7,15},{8,40},{9,1... | collective-permute-start | bytes 245768 | tf_op jit(solution)/shard_map/ppermute | solution.py:78
  17.7 3.6 %collective-permute-start.4 = (f32[160,128]{1,0:T(8,128)S(1)}, f32[160,128]{1,0:T(8,128)S(1)}, u32[]{:S(2)}, u32[]{:S(2)}) collective-permute-start(f32[160,128]{1,0:T(8,128)S(1)} %add_add_fusion.a_ref), channel_id=1, source_target_pairs={{0,96},{1,25},{2,98},{3,27},{4,100},{5,29},{6,102},{7,31},{8,104},... | collective-permute-start | bytes 245768 | tf_op jit(solution)/shard_map/ppermute | solution.py:78
  19.4 4.8 %collective-permute-start.5 = (f32[160,128]{1,0:T(8,128)S(1)}, f32[160,128]{1,0:T(8,128)S(1)}, u32[]{:S(2)}, u32[]{:S(2)}) collective-permute-start(f32[160,128]{1,0:T(8,128)S(1)} %add_add_fusion.a_ref), channel_id=1, source_target_pairs={{0,64},{1,17},{2,66},{3,19},{4,68},{5,21},{6,70},{7,23},{8,72},{9,... | collective-permute-start | bytes 245768 | tf_op jit(solution)/shard_map/ppermute | solution.py:78
  24.9 5.0 %collective-permute-start.6 = (f32[680,128]{1,0:T(8,128)S(1)}, f32[680,128]{1,0:T(8,128)S(1)}, u32[]{:S(2)}, u32[]{:S(2)}) collective-permute-start(f32[680,128]{1,0:T(8,128)S(1)} %get-tuple-element.41), channel_id=1, source_target_pairs={{0,1},{1,0},{2,3},{3,2},{4,5},{5,4},{6,7},{7,6},{8,9},{9,8},{10,11... | collective-permute-start | bytes 1044488 | tf_op jit(solution)/shard_map/ppermute | solution.py:83
  29.4 3.2 %collective-permute-start.7 = (f32[1920,128]{1,0:T(8,128)S(1)}, f32[1920,128]{1,0:T(8,128)S(1)}, u32[]{:S(2)}, u32[]{:S(2)}) collective-permute-start(f32[1920,128]{1,0:T(8,128)S(1)} %next_right.3.after_ref), channel_id=1, source_target_pairs={{0,1},{1,0},{2,3},{3,2},{4,5},{5,4},{6,7},{7,6},{8,9},{9,8},{10,11... | collective-permute-start | bytes 2949128 | tf_op jit(solution)/shard_map/ppermute | solution.py:83
  30.1 7.8 %collective-permute-start.10 = (f32[640,128]{1,0:T(8,128)S(1)}, f32[640,128]{1,0:T(8,128)S(1)}, u32[]{:S(2)}, u32[]{:S(2)}) collective-permute-start(f32[640,128]{1,0:T(8,128)S(1)} %get-tuple-element.46), channel_id=1, source_target_pairs={{0,16},{1,65},{2,66},{3,19},{4,20},{5,69},{6,70},{7,23},{8,72},{9,... | collective-permute-start | bytes 983048 | tf_op jit(solution)/shard_map/ppermute | solution.py:78
  32.8 8.6 %collective-permute-start.8 = (f32[640,128]{1,0:T(8,128)S(1)}, f32[640,128]{1,0:T(8,128)S(1)}, u32[]{:S(2)}, u32[]{:S(2)}) collective-permute-start(f32[640,128]{1,0:T(8,128)S(1)} %get-tuple-element.44), channel_id=1, source_target_pairs={{0,9},{1,32},{2,35},{3,10},{4,13},{5,36},{6,39},{7,14},{8,41},{9,1... | collective-permute-start | bytes 983048 | tf_op jit(solution)/shard_map/ppermute | solution.py:78
  34.3 7.3 %collective-permute-start.9 = (f32[640,128]{1,0:T(8,128)S(1)}, f32[640,128]{1,0:T(8,128)S(1)}, u32[]{:S(2)}, u32[]{:S(2)}) collective-permute-start(f32[640,128]{1,0:T(8,128)S(1)} %get-tuple-element.45), channel_id=1, source_target_pairs={{0,25},{1,96},{2,99},{3,26},{4,29},{5,100},{6,103},{7,30},{8,105},... | collective-permute-start | bytes 983048 | tf_op jit(solution)/shard_map/ppermute | solution.py:78
  41.7 6.2 %collective-permute-start.11 = (f32[200,128]{1,0:T(8,128)S(1)}, f32[200,128]{1,0:T(8,128)S(1)}, u32[]{:S(2)}, u32[]{:S(2)}) collective-permute-start(f32[200,128]{1,0:T(8,128)S(1)} %get-tuple-element.49), channel_id=1, source_target_pairs={{0,33},{1,2},{2,5},{3,34},{4,37},{5,6},{6,1},{7,38},{8,11},{9,40},... | collective-permute-start | bytes 307208 | tf_op jit(solution)/shard_map/ppermute | solution.py:78
  44.1 4.1 %collective-permute-start.12 = (f32[200,128]{1,0:T(8,128)S(1)}, f32[200,128]{1,0:T(8,128)S(1)}, u32[]{:S(2)}, u32[]{:S(2)}) collective-permute-start(f32[200,128]{1,0:T(8,128)S(1)} %get-tuple-element.50), channel_id=1, source_target_pairs={{0,97},{1,6},{2,1},{3,98},{4,101},{5,2},{6,5},{7,102},{8,15},{9,10... | collective-permute-start | bytes 307208 | tf_op jit(solution)/shard_map/ppermute | solution.py:78
  45.6 5.3 %collective-permute-start.13 = (f32[200,128]{1,0:T(8,128)S(1)}, f32[200,128]{1,0:T(8,128)S(1)}, u32[]{:S(2)}, u32[]{:S(2)}) collective-permute-start(f32[200,128]{1,0:T(8,128)S(1)} %get-tuple-element.51), channel_id=1, source_target_pairs={{0,64},{1,5},{2,6},{3,67},{4,68},{5,1},{6,2},{7,71},{8,12},{9,73},... | collective-permute-start | bytes 307208 | tf_op jit(solution)/shard_map/ppermute | solution.py:78
  51.0 5.7 %collective-permute-start.14 = (f32[200,128]{1,0:T(8,128)S(1)}, f32[200,128]{1,0:T(8,128)S(1)}, u32[]{:S(2)}, u32[]{:S(2)}) collective-permute-start(f32[200,128]{1,0:T(8,128)S(1)} %across.2.a_ref), channel_id=1, source_target_pairs={{0,3},{1,8},{2,11},{3,4},{4,7},{5,12},{6,15},{7,0},{8,17},{9,10},{... | collective-permute-start | bytes 307208 | tf_op jit(solution)/shard_map/ppermute | solution.py:78
  52.0 4.6 %collective-permute-start.15 = (f32[200,128]{1,0:T(8,128)S(1)}, f32[200,128]{1,0:T(8,128)S(1)}, u32[]{:S(2)}, u32[]{:S(2)}) collective-permute-start(f32[200,128]{1,0:T(8,128)S(1)} %across.2.a_ref), channel_id=1, source_target_pairs={{0,7},{1,24},{2,27},{3,0},{4,3},{5,28},{6,31},{7,4},{8,1},{9,14},{... | collective-permute-start | bytes 307208 | tf_op jit(solution)/shard_map/ppermute | solution.py:78
  54.0 5.0 %collective-permute-start.16 = (f32[200,128]{1,0:T(8,128)S(1)}, f32[200,128]{1,0:T(8,128)S(1)}, u32[]{:S(2)}, u32[]{:S(2)}) collective-permute-start(f32[200,128]{1,0:T(8,128)S(1)} %across.2.a_ref), channel_id=1, source_target_pairs={{0,4},{1,17},{2,18},{3,7},{4,0},{5,21},{6,22},{7,3},{8,24},{9,13},... | collective-permute-start | bytes 307208 | tf_op jit(solution)/shard_map/ppermute | solution.py:78
  59.1 7.1 %collective-permute-start.17 = (f32[160,128]{1,0:T(8,128)S(1)}, f32[160,128]{1,0:T(8,128)S(1)}, u32[]{:S(2)}, u32[]{:S(2)}) collective-permute-start(f32[160,128]{1,0:T(8,128)S(1)} %get-tuple-element.56.a_ref), channel_id=1, source_target_pairs={{0,33},{1,2},{2,5},{3,34},{4,37},{5,6},{6,1},{7,38},{8,11},{9,40},... | collective-permute-start | bytes 245768 | tf_op jit(solution)/shard_map/ppermute | solution.py:78
  61.6 4.7 %collective-permute-start.18 = (f32[160,128]{1,0:T(8,128)S(1)}, f32[160,128]{1,0:T(8,128)S(1)}, u32[]{:S(2)}, u32[]{:S(2)}) collective-permute-start(f32[160,128]{1,0:T(8,128)S(1)} %get-tuple-element.56.a_ref), channel_id=1, source_target_pairs={{0,97},{1,6},{2,1},{3,98},{4,101},{5,2},{6,5},{7,102},{8,15},{9,10... | collective-permute-start | bytes 245768 | tf_op jit(solution)/shard_map/ppermute | solution.py:78
  63.1 4.8 %collective-permute-start.19 = (f32[160,128]{1,0:T(8,128)S(1)}, f32[160,128]{1,0:T(8,128)S(1)}, u32[]{:S(2)}, u32[]{:S(2)}) collective-permute-start(f32[160,128]{1,0:T(8,128)S(1)} %get-tuple-element.56.a_ref), channel_id=1, source_target_pairs={{0,64},{1,5},{2,6},{3,67},{4,68},{5,1},{6,2},{7,71},{8,12},{9,73},... | collective-permute-start | bytes 245768 | tf_op jit(solution)/shard_map/ppermute | solution.py:78
  67.9 6.8 %collective-permute-start.22 = (f32[640,128]{1,0:T(8,128)S(1)}, f32[640,128]{1,0:T(8,128)S(1)}, u32[]{:S(2)}, u32[]{:S(2)}) collective-permute-start(f32[640,128]{1,0:T(8,128)S(1)} %assemble.1.refs_0_), channel_id=1, source_target_pairs={{0,1},{1,0},{2,3},{3,2},{4,5},{5,4},{6,7},{7,6},{8,9},{9,8},{10,11... | collective-permute-start | bytes 983048 | tf_op jit(solution)/shard_map/ppermute | solution.py:83
  70.6 7.7 %collective-permute-start.21 = (f32[640,128]{1,0:T(8,128)S(1)}, f32[640,128]{1,0:T(8,128)S(1)}, u32[]{:S(2)}, u32[]{:S(2)}) collective-permute-start(f32[640,128]{1,0:T(8,128)S(1)} %assemble.1.refs_0_), channel_id=1, source_target_pairs={{0,16},{1,65},{2,66},{3,19},{4,20},{5,69},{6,70},{7,23},{8,72},{9,... | collective-permute-start | bytes 983048 | tf_op jit(solution)/shard_map/ppermute | solution.py:78
  70.6 11.1 %collective-permute-start.24 = (f32[640,128]{1,0:T(8,128)S(1)}, f32[640,128]{1,0:T(8,128)S(1)}, u32[]{:S(2)}, u32[]{:S(2)}) collective-permute-start(f32[640,128]{1,0:T(8,128)S(1)} %assemble.1.refs_0_), channel_id=1, source_target_pairs={{0,25},{1,96},{2,99},{3,26},{4,29},{5,100},{6,103},{7,30},{8,105},... | collective-permute-start | bytes 983048 | tf_op jit(solution)/shard_map/ppermute | solution.py:78
  73.1 8.7 %collective-permute-start.20 = (f32[640,128]{1,0:T(8,128)S(1)}, f32[640,128]{1,0:T(8,128)S(1)}, u32[]{:S(2)}, u32[]{:S(2)}) collective-permute-start(f32[640,128]{1,0:T(8,128)S(1)} %assemble.1.refs_0_), channel_id=1, source_target_pairs={{0,9},{1,32},{2,35},{3,10},{4,13},{5,36},{6,39},{7,14},{8,41},{9,1... | collective-permute-start | bytes 983048 | tf_op jit(solution)/shard_map/ppermute | solution.py:78
  78.4 4.5 %collective-permute-start.26 = (f32[640,128]{1,0:T(8,128)S(1)}, f32[640,128]{1,0:T(8,128)S(1)}, u32[]{:S(2)}, u32[]{:S(2)}) collective-permute-start(f32[640,128]{1,0:T(8,128)S(1)} %tie.3.refs_0_), channel_id=1, source_target_pairs={{0,1},{1,0},{2,3},{3,2},{4,5},{5,4},{6,7},{7,6},{8,9},{9,8},{10,11... | collective-permute-start | bytes 983048 | tf_op jit(solution)/shard_map/ppermute | solution.py:83
  81.7 3.8 %collective-permute-start.25 = (f32[640,128]{1,0:T(8,128)S(1)}, f32[640,128]{1,0:T(8,128)S(1)}, u32[]{:S(2)}, u32[]{:S(2)}) collective-permute-start(f32[640,128]{1,0:T(8,128)S(1)} %tie.5.refs_1_), channel_id=1, source_target_pairs={{0,1},{1,0},{2,3},{3,2},{4,5},{5,4},{6,7},{7,6},{8,9},{9,8},{10,11... | collective-permute-start | bytes 983048 | tf_op jit(solution)/shard_map/ppermute | solution.py:83
  81.9 3.7 %collective-permute-start.23 = (f32[640,128]{1,0:T(8,128)S(1)}, f32[640,128]{1,0:T(8,128)S(1)}, u32[]{:S(2)}, u32[]{:S(2)}) collective-permute-start(f32[640,128]{1,0:T(8,128)S(1)} %tie.4.refs_0_), channel_id=1, source_target_pairs={{0,1},{1,0},{2,3},{3,2},{4,5},{5,4},{6,7},{7,6},{8,9},{9,8},{10,11... | collective-permute-start | bytes 983048 | tf_op jit(solution)/shard_map/ppermute | solution.py:83

commit v15 on v14

--- a/solution.py
+++ b/solution.py
@@ -156,11 +156,18 @@
 def right_tiles(quarters, pieces, m_ref, out_ref):
     rank = pieces.shape[0] // 3
     width = m_ref.shape[1] // 2 // QUARTERS
+    main = pieces.shape[1] // 256 * 256
+    rest = jnp.concatenate(
+        [pieces[i : i + rank, main:] for i in range(0, 3 * rank, rank)], axis=1
+    )
     to = 0
     for quarter in quarters:
         at = pl.multiple_of(quarter * width, width)
-        t = jnp.dot(pieces, m_ref[:, pl.ds(at, width)], preferred_element_type=F32)
+        m = m_ref[:, pl.ds(at, width)]
+        t = jnp.dot(pieces[:, :main], m[:main], preferred_element_type=F32)
         t = t[:rank] + (t[rank : 2 * rank] + t[2 * rank :])
+        m = jnp.concatenate([m[main:]] * 3, axis=0)
+        t = t + jnp.dot(rest, m, preferred_element_type=F32)
         for g in range(rank // ROWS):
             for n in range(width // 128):
                 out_ref[to : to + ROWS, :] = t[g * ROWS : (g + 1) * ROWS, n * 128 : (n + 1) * 128]
@@ -509,6 +516,22 @@
     )(solve, left, merged, *totals, *last, *held)
 
 
+def again_kernel(value_ref, out_ref):
+    out_ref[...] = value_ref[...]
+
+
+def again(value):
+    return pl.pallas_call(
+        again_kernel,
+        out_shape=jax.ShapeDtypeStruct(value.shape, value.dtype),
+        in_specs=[WHOLE],
+        out_specs=WHOLE,
+        compiler_params=params(4),
+        cost_estimate=cost(RIGHT, 1 << 20),
+        name="again",
+    )(value)
+
+
 def tie_kernel(value_ref, after_ref, out_ref):
     del value_ref, after_ref, out_ref
 
@@ -554,6 +577,7 @@
         return result(sources, totals, merged, solve, left, *after, **more)
 
     own, other = True, False
+    total = again(total)
     out = write(((own, 0),), (total,), None)
     *out, token = write(((other, 0),), (swap(total),), out, token=True)
     two = tie(two, token)

time: 87.9 us -> 87.6 us (level)
  starting transfers between devices: 39.1 us -> 41.2 us
  waiting for transfers between devices: 26.5 us -> 24.4 us
    ppermute x21, starting transfers between devices: 30.7 us -> 33.3 us  [ring(): out.append(lax.ppermute(value, AXES, pairs))]
    ppermute x21, waiting for transfers between devices: 26.5 us -> 24.4 us  [ring(): out.append(lax.ppermute(value, AXES, pairs))]
  transfers between devices with their start and end apart: 27 -> 27, of which waited for: 16 -> 14; matrix products, arithmetic and copies ran while one was open for 0% -> 0% of each run, Pallas kernels for 14% -> 13%
where the time goes in v15:
time: 87.6 us; the launch traced here: 87.5 us
  starting transfers between devices  41.2 us (47%)
  waiting for transfers between devices  24.4 us (28%)
  Pallas kernels  20.9 us (24%)
  between operations  1 us (1%)
    ppermute x21, starting transfers between devices, ring(): out.append(lax.ppermute(value, AXES, pairs))  33.3 us
    ppermute x21, waiting for transfers between devices, ring(): out.append(lax.ppermute(value, AXES, pairs))  24.4 us
    pallas_call x5, Pallas kernels, result(): pl.pallas_call(functools.partial(result_kernel, sources, more, quarter //...  9.49 us
    ppermute x6, starting transfers between devices, swap(): return lax.ppermute(value, 'c', [(0, 1), (1, 0)])  7.87 us
    pallas_call x1, Pallas kernels, merge(): pl.pallas_call(functools.partial(merge_kernel, cuts), out_shape=[pltpu.VM...  6.21 us
    pallas_call x1, Pallas kernels, factor(): pl.pallas_call(functools.partial(factor_kernel, replicas), out_shape=[jax...  2.01 us
    pallas_call x3, Pallas kernels, next_right(): pl.pallas_call(functools.partial(next_right_kernel, own, turns), out_shap...  1.95 us
  transfers between devices with their start and end apart: 27, of which 14 were waited for; matrix products, arithmetic and copies ran while one was open for 0% of the time, Pallas kernels for 13%

profile of v15, /device:TPU:1, one launch (start us, length us, event | category | flops | bytes accessed | tf_op | source)
XLA Modules:
  0.0 87.5 jit_solution(10547380278579718886)
XLA Ops:
  0.6 6.2 %merge.1 = (bf16[320,10240]{1,0:T(8,128)(2,1)S(1)}, f32[160,128]{1,0:T(8,128)S(1)}) custom-call(bf16[320,10240]{1,0:T(8,128)(2,1)} %bitcast.3, bf16[320,10240]{1,0:T(8,128)(2,1)} %bitcast.4, bf16[64,10240]{1,0:T(8,128)(2,1)} %q_hbm.1), custom_call_target="tpu_custom_call" | custom-call | flops 419430400 | bytes 13107200 | tf_op jit(solution)/shard_map/merge/pallas_call | solution.py:139
  6.8 2.5 %collective-permute-start = (f32[160,128]{1,0:T(8,128)S(1)}, f32[160,128]{1,0:T(8,128)S(1)}, u32[]{:S(2)}, u32[]{:S(2)}) collective-permute-start(f32[160,128]{1,0:T(8,128)S(1)} %get-tuple-element.37), channel_id=1, source_target_pairs={{0,8},{1,33},{2,10},{3,35},{4,12},{5,37},{6,14},{7,39},{8,16},{9,4... | collective-permute-start | bytes 245768 | tf_op jit(solution)/shard_map/ppermute | solution.py:78
  9.4 2.2 %collective-permute-start.1 = (f32[160,128]{1,0:T(8,128)S(1)}, f32[160,128]{1,0:T(8,128)S(1)}, u32[]{:S(2)}, u32[]{:S(2)}) collective-permute-start(f32[160,128]{1,0:T(8,128)S(1)} %get-tuple-element.37), channel_id=1, source_target_pairs={{0,24},{1,97},{2,26},{3,99},{4,28},{5,101},{6,30},{7,103},{8,0},{9... | collective-permute-start | bytes 245768 | tf_op jit(solution)/shard_map/ppermute | solution.py:78
  11.6 1.2 %collective-permute-start.2 = (f32[160,128]{1,0:T(8,128)S(1)}, f32[160,128]{1,0:T(8,128)S(1)}, u32[]{:S(2)}, u32[]{:S(2)}) collective-permute-start(f32[160,128]{1,0:T(8,128)S(1)} %get-tuple-element.37), channel_id=1, source_target_pairs={{0,16},{1,65},{2,18},{3,67},{4,20},{5,69},{6,22},{7,71},{8,24},{9,... | collective-permute-start | bytes 245768 | tf_op jit(solution)/shard_map/ppermute | solution.py:78
  12.8 0.8 collective-permute-done
  13.6 0.0 collective-permute-done.1
  13.6 3.1 %collective-permute-done.2 = f32[160,128]{1,0:T(8,128)S(1)} collective-permute-done((f32[160,128]{1,0:T(8,128)S(1)}, f32[160,128]{1,0:T(8,128)S(1)}, u32[]{:S(2)}, u32[]{:S(2)}) %collective-permute-start.2) | collective-permute-done | bytes 81952 | tf_op jit(solution)/shard_map/ppermute | solution.py:78
  16.7 1.0 %collective-permute-start.3 = (f32[160,128]{1,0:T(8,128)S(1)}, f32[160,128]{1,0:T(8,128)S(1)}, u32[]{:S(2)}, u32[]{:S(2)}) collective-permute-start(f32[160,128]{1,0:T(8,128)S(1)} %add_add_fusion.a_ref), channel_id=1, source_target_pairs={{0,32},{1,9},{2,34},{3,11},{4,36},{5,13},{6,38},{7,15},{8,40},{9,1... | collective-permute-start | bytes 245768 | tf_op jit(solution)/shard_map/ppermute | solution.py:78
  17.7 1.8 %collective-permute-start.4 = (f32[160,128]{1,0:T(8,128)S(1)}, f32[160,128]{1,0:T(8,128)S(1)}, u32[]{:S(2)}, u32[]{:S(2)}) collective-permute-start(f32[160,128]{1,0:T(8,128)S(1)} %add_add_fusion.a_ref), channel_id=1, source_target_pairs={{0,96},{1,25},{2,98},{3,27},{4,100},{5,29},{6,102},{7,31},{8,104},... | collective-permute-start | bytes 245768 | tf_op jit(solution)/shard_map/ppermute | solution.py:78
  19.4 1.2 %collective-permute-start.5 = (f32[160,128]{1,0:T(8,128)S(1)}, f32[160,128]{1,0:T(8,128)S(1)}, u32[]{:S(2)}, u32[]{:S(2)}) collective-permute-start(f32[160,128]{1,0:T(8,128)S(1)} %add_add_fusion.a_ref), channel_id=1, source_target_pairs={{0,64},{1,17},{2,66},{3,19},{4,68},{5,21},{6,70},{7,23},{8,72},{9,... | collective-permute-start | bytes 245768 | tf_op jit(solution)/shard_map/ppermute | solution.py:78
  20.7 0.6 collective-permute-done.3.b_ref
  21.3 3.0 %collective-permute-done.5.d_ref = f32[160,128]{1,0:T(8,128)S(1)} collective-permute-done((f32[160,128]{1,0:T(8,128)S(1)}, f32[160,128]{1,0:T(8,128)S(1)}, u32[]{:S(2)}, u32[]{:S(2)}) %collective-permute-start.5) | collective-permute-done | bytes 81952 | tf_op jit(solution)/shard_map/ppermute | solution.py:78
  24.2 0.6 first_right.1
  24.9 3.5 %collective-permute-start.6 = (f32[680,128]{1,0:T(8,128)S(1)}, f32[680,128]{1,0:T(8,128)S(1)}, u32[]{:S(2)}, u32[]{:S(2)}) collective-permute-start(f32[680,128]{1,0:T(8,128)S(1)} %get-tuple-element.41), channel_id=1, source_target_pairs={{0,1},{1,0},{2,3},{3,2},{4,5},{5,4},{6,7},{7,6},{8,9},{9,8},{10,11... | collective-permute-start | bytes 1044488 | tf_op jit(solution)/shard_map/ppermute | solution.py:83
  28.4 0.8 next_right.3.after_ref
  29.2 0.1 collective-permute-start.7
  29.4 0.4 next_right.4.kept_ref
  29.7 0.0 collective-permute-done.6.got_ref
  29.7 0.1 first_pair.1
  29.8 1.6 %collective-permute-start.10 = (f32[640,128]{1,0:T(8,128)S(1)}, f32[640,128]{1,0:T(8,128)S(1)}, u32[]{:S(2)}, u32[]{:S(2)}) collective-permute-start(f32[640,128]{1,0:T(8,128)S(1)} %get-tuple-element.46), channel_id=1, source_target_pairs={{0,16},{1,65},{2,66},{3,19},{4,20},{5,69},{6,70},{7,23},{8,72},{9,... | collective-permute-start | bytes 983048 | tf_op jit(solution)/shard_map/ppermute | solution.py:78
  31.5 0.8 next_right.5.kept_ref
  32.2 0.0 collective-permute-done.7.got_ref
  32.3 0.2 next_pair.1
  32.5 1.4 %collective-permute-start.8 = (f32[640,128]{1,0:T(8,128)S(1)}, f32[640,128]{1,0:T(8,128)S(1)}, u32[]{:S(2)}, u32[]{:S(2)}) collective-permute-start(f32[640,128]{1,0:T(8,128)S(1)} %get-tuple-element.44), channel_id=1, source_target_pairs={{0,9},{1,32},{2,35},{3,10},{4,13},{5,36},{6,39},{7,14},{8,41},{9,1... | collective-permute-start | bytes 983048 | tf_op jit(solution)/shard_map/ppermute | solution.py:78
  33.9 1.6 %collective-permute-start.9 = (f32[640,128]{1,0:T(8,128)S(1)}, f32[640,128]{1,0:T(8,128)S(1)}, u32[]{:S(2)}, u32[]{:S(2)}) collective-permute-start(f32[640,128]{1,0:T(8,128)S(1)} %get-tuple-element.45), channel_id=1, source_target_pairs={{0,25},{1,96},{2,99},{3,26},{4,29},{5,100},{6,103},{7,30},{8,105},... | collective-permute-start | bytes 983048 | tf_op jit(solution)/shard_map/ppermute | solution.py:78
  35.5 2.1 %collective-permute-done.10.d_ref = f32[640,128]{1,0:T(8,128)S(1)} collective-permute-done((f32[640,128]{1,0:T(8,128)S(1)}, f32[640,128]{1,0:T(8,128)S(1)}, u32[]{:S(2)}, u32[]{:S(2)}) %collective-permute-start.10) | collective-permute-done | bytes 327712 | tf_op jit(solution)/shard_map/ppermute | solution.py:78
  37.7 3.5 %collective-permute-done.8.b_ref = f32[640,128]{1,0:T(8,128)S(1)} collective-permute-done((f32[640,128]{1,0:T(8,128)S(1)}, f32[640,128]{1,0:T(8,128)S(1)}, u32[]{:S(2)}, u32[]{:S(2)}) %collective-permute-start.8) | collective-permute-done | bytes 327712 | tf_op jit(solution)/shard_map/ppermute | solution.py:78
  41.2 0.2 collective-permute-done.9.c_ref
  41.4 0.1 add_quarters.1
  41.4 2.4 %collective-permute-start.11 = (f32[200,128]{1,0:T(8,128)S(1)}, f32[200,128]{1,0:T(8,128)S(1)}, u32[]{:S(2)}, u32[]{:S(2)}) collective-permute-start(f32[200,128]{1,0:T(8,128)S(1)} %get-tuple-element.49), channel_id=1, source_target_pairs={{0,33},{1,2},{2,5},{3,34},{4,37},{5,6},{6,1},{7,38},{8,11},{9,40},... | collective-permute-start | bytes 307208 | tf_op jit(solution)/shard_map/ppermute | solution.py:78
  43.8 1.5 %collective-permute-start.12 = (f32[200,128]{1,0:T(8,128)S(1)}, f32[200,128]{1,0:T(8,128)S(1)}, u32[]{:S(2)}, u32[]{:S(2)}) collective-permute-start(f32[200,128]{1,0:T(8,128)S(1)} %get-tuple-element.50), channel_id=1, source_target_pairs={{0,97},{1,6},{2,1},{3,98},{4,101},{5,2},{6,5},{7,102},{8,15},{9,10... | collective-permute-start | bytes 307208 | tf_op jit(solution)/shard_map/ppermute | solution.py:78
  45.4 1.1 %collective-permute-start.13 = (f32[200,128]{1,0:T(8,128)S(1)}, f32[200,128]{1,0:T(8,128)S(1)}, u32[]{:S(2)}, u32[]{:S(2)}) collective-permute-start(f32[200,128]{1,0:T(8,128)S(1)} %get-tuple-element.51), channel_id=1, source_target_pairs={{0,64},{1,5},{2,6},{3,67},{4,68},{5,1},{6,2},{7,71},{8,12},{9,73},... | collective-permute-start | bytes 307208 | tf_op jit(solution)/shard_map/ppermute | solution.py:78
  46.5 1.2 %collective-permute-done.11.b_ref = f32[200,128]{1,0:T(8,128)S(1)} collective-permute-done((f32[200,128]{1,0:T(8,128)S(1)}, f32[200,128]{1,0:T(8,128)S(1)}, u32[]{:S(2)}, u32[]{:S(2)}) %collective-permute-start.11) | collective-permute-done | bytes 102432 | tf_op jit(solution)/shard_map/ppermute | solution.py:78
  47.6 0.3 collective-permute-done.12.c_ref
  47.9 2.7 %collective-permute-done.13.d_ref = f32[200,128]{1,0:T(8,128)S(1)} collective-permute-done((f32[200,128]{1,0:T(8,128)S(1)}, f32[200,128]{1,0:T(8,128)S(1)}, u32[]{:S(2)}, u32[]{:S(2)}) %collective-permute-start.13) | collective-permute-done | bytes 102432 | tf_op jit(solution)/shard_map/ppermute | solution.py:78
  50.7 0.1 across.2.a_ref
  50.7 1.1 %collective-permute-start.14 = (f32[200,128]{1,0:T(8,128)S(1)}, f32[200,128]{1,0:T(8,128)S(1)}, u32[]{:S(2)}, u32[]{:S(2)}) collective-permute-start(f32[200,128]{1,0:T(8,128)S(1)} %across.2.a_ref), channel_id=1, source_target_pairs={{0,3},{1,8},{2,11},{3,4},{4,7},{5,12},{6,15},{7,0},{8,17},{9,10},{... | collective-permute-start | bytes 307208 | tf_op jit(solution)/shard_map/ppermute | solution.py:78
  51.8 2.0 %collective-permute-start.15 = (f32[200,128]{1,0:T(8,128)S(1)}, f32[200,128]{1,0:T(8,128)S(1)}, u32[]{:S(2)}, u32[]{:S(2)}) collective-permute-start(f32[200,128]{1,0:T(8,128)S(1)} %across.2.a_ref), channel_id=1, source_target_pairs={{0,7},{1,24},{2,27},{3,0},{4,3},{5,28},{6,31},{7,4},{8,1},{9,14},{... | collective-permute-start | bytes 307208 | tf_op jit(solution)/shard_map/ppermute | solution.py:78
  53.8 0.5 collective-permute-start.16
  54.3 2.1 %collective-permute-done.14.b_ref = f32[200,128]{1,0:T(8,128)S(1)} collective-permute-done((f32[200,128]{1,0:T(8,128)S(1)}, f32[200,128]{1,0:T(8,128)S(1)}, u32[]{:S(2)}, u32[]{:S(2)}) %collective-permute-start.14) | collective-permute-done | bytes 102432 | tf_op jit(solution)/shard_map/ppermute | solution.py:78
  56.4 2.4 %collective-permute-done.16.d_ref = f32[200,128]{1,0:T(8,128)S(1)} collective-permute-done((f32[200,128]{1,0:T(8,128)S(1)}, f32[200,128]{1,0:T(8,128)S(1)}, u32[]{:S(2)}, u32[]{:S(2)}) %collective-permute-start.16) | collective-permute-done | bytes 102432 | tf_op jit(solution)/shard_map/ppermute | solution.py:78
  58.8 0.1 across.3
  58.9 2.5 %collective-permute-start.17 = (f32[160,128]{1,0:T(8,128)S(1)}, f32[160,128]{1,0:T(8,128)S(1)}, u32[]{:S(2)}, u32[]{:S(2)}) collective-permute-start(f32[160,128]{1,0:T(8,128)S(1)} %get-tuple-element.56.a_ref), channel_id=1, source_target_pairs={{0,33},{1,2},{2,5},{3,34},{4,37},{5,6},{6,1},{7,38},{8,11},{9,40},... | collective-permute-start | bytes 245768 | tf_op jit(solution)/shard_map/ppermute | solution.py:78
  61.4 1.5 %collective-permute-start.18 = (f32[160,128]{1,0:T(8,128)S(1)}, f32[160,128]{1,0:T(8,128)S(1)}, u32[]{:S(2)}, u32[]{:S(2)}) collective-permute-start(f32[160,128]{1,0:T(8,128)S(1)} %get-tuple-element.56.a_ref), channel_id=1, source_target_pairs={{0,97},{1,6},{2,1},{3,98},{4,101},{5,2},{6,5},{7,102},{8,15},{9,10... | collective-permute-start | bytes 245768 | tf_op jit(solution)/shard_map/ppermute | solution.py:78
  62.9 1.1 %collective-permute-start.19 = (f32[160,128]{1,0:T(8,128)S(1)}, f32[160,128]{1,0:T(8,128)S(1)}, u32[]{:S(2)}, u32[]{:S(2)}) collective-permute-start(f32[160,128]{1,0:T(8,128)S(1)} %get-tuple-element.56.a_ref), channel_id=1, source_target_pairs={{0,64},{1,5},{2,6},{3,67},{4,68},{5,1},{6,2},{7,71},{8,12},{9,73},... | collective-permute-start | bytes 245768 | tf_op jit(solution)/shard_map/ppermute | solution.py:78
  64.0 2.0 %factor.1 = (bf16[64,384]{1,0:T(8,128)(2,1)S(1)}, bf16[320,64]{1,0:T(8,128)(2,1)S(1)}, f32[64,320]{1,0:T(8,128)S(1)}) custom-call(f32[40,128]{1,0:T(8,128)S(1)} %get-tuple-element.52.ext_ref, f32[64,320]{1,0:T(8,128)S(1)} %get-tuple-element.53.p_ref), custom_call_target="tpu_custom_call" | custom-call | flops 4294967296 | bytes 1048576 | tf_op jit(solution)/shard_map/factor/pallas_call | solution.py:420
  66.0 0.0 collective-permute-done.17.b_ref
  66.0 1.7 %collective-permute-done.19.d_ref = f32[160,128]{1,0:T(8,128)S(1)} collective-permute-done((f32[160,128]{1,0:T(8,128)S(1)}, f32[160,128]{1,0:T(8,128)S(1)}, u32[]{:S(2)}, u32[]{:S(2)}) %collective-permute-start.19) | collective-permute-done | bytes 81952 | tf_op jit(solution)/shard_map/ppermute | solution.py:78
  67.7 1.6 %collective-permute-start.21 = (f32[640,128]{1,0:T(8,128)S(1)}, f32[640,128]{1,0:T(8,128)S(1)}, u32[]{:S(2)}, u32[]{:S(2)}) collective-permute-start(f32[640,128]{1,0:T(8,128)S(1)} %assemble.1.value_ref), channel_id=1, source_target_pairs={{0,16},{1,65},{2,66},{3,19},{4,20},{5,69},{6,70},{7,23},{8,72},{9,... | collective-permute-start | bytes 983048 | tf_op jit(solution)/shard_map/ppermute | solution.py:78
  69.3 3.5 %collective-permute-start.24 = (f32[640,128]{1,0:T(8,128)S(1)}, f32[640,128]{1,0:T(8,128)S(1)}, u32[]{:S(2)}, u32[]{:S(2)}) collective-permute-start(f32[640,128]{1,0:T(8,128)S(1)} %assemble.1.value_ref), channel_id=1, source_target_pairs={{0,25},{1,96},{2,99},{3,26},{4,29},{5,100},{6,103},{7,30},{8,105},... | collective-permute-start | bytes 983048 | tf_op jit(solution)/shard_map/ppermute | solution.py:78
  72.8 0.0 collective-permute-start.20
  72.8 1.2 %collective-permute-start.22 = (f32[640,128]{1,0:T(8,128)S(1)}, f32[640,128]{1,0:T(8,128)S(1)}, u32[]{:S(2)}, u32[]{:S(2)}) collective-permute-start(f32[640,128]{1,0:T(8,128)S(1)} %again.1.refs_0_), channel_id=1, source_target_pairs={{0,1},{1,0},{2,3},{3,2},{4,5},{5,4},{6,7},{7,6},{8,9},{9,8},{10,11... | collective-permute-start | bytes 983048 | tf_op jit(solution)/shard_map/ppermute | solution.py:83
  74.0 1.6 %result.5 = (bf16[320,10240]{1,0:T(8,128)(2,1)}, f32[64,10240]{1,0:T(8,128)}) custom-call(bf16[64,384]{1,0:T(8,128)(2,1)S(1)} %get-tuple-element.54.after_ref.solve_ref, bf16[320,64]{1,0:T(8,128)(2,1)S(1)} %get-tuple-element.55.left_ref, bf16[320,10240]{1,0:T(8,128)(2,1)S(1)} %get-tuple-element.38.m_ref, f32[640,128]{1,0:T(8,128)S(1)} %again.1.refs_0_), custom_call_target="tpu_custom_call" | custom-call | flops 8589934592 | bytes 1048576 | tf_op jit(solution)/shard_map/result/pallas_call | solution.py:500
  75.6 0.0 collective-permute-done.22.refs_0_
  75.6 1.6 %result.6 = (bf16[320,10240]{1,0:T(8,128)(2,1)}, f32[64,10240]{1,0:T(8,128)}, f32[8,128]{1,0:T(8,128)S(1)}) custom-call(bf16[64,384]{1,0:T(8,128)(2,1)S(1)} %get-tuple-element.54.after_ref.solve_ref, bf16[320,64]{1,0:T(8,128)(2,1)S(1)} %get-tuple-element.55.left_ref, ...), custom_call_target="tpu_custom_call", output_to_operand_aliasing={{0}: (4, {}), {1}: (5, {})} | custom-call | flops 8589934592 | bytes 1048576 | tf_op jit(solution)/shard_map/result/pallas_call | solution.py:500
  77.2 1.9 %collective-permute-start.26 = (f32[640,128]{1,0:T(8,128)S(1)}, f32[640,128]{1,0:T(8,128)S(1)}, u32[]{:S(2)}, u32[]{:S(2)}) collective-permute-start(f32[640,128]{1,0:T(8,128)S(1)} %tie.3.refs_0_), channel_id=1, source_target_pairs={{0,1},{1,0},{2,3},{3,2},{4,5},{5,4},{6,7},{7,6},{8,9},{9,8},{10,11... | collective-permute-start | bytes 983048 | tf_op jit(solution)/shard_map/ppermute | solution.py:83
  79.1 1.6 %result.7 = (bf16[320,10240]{1,0:T(8,128)(2,1)}, f32[64,10240]{1,0:T(8,128)}, f32[8,128]{1,0:T(8,128)S(1)}) custom-call(bf16[64,384]{1,0:T(8,128)(2,1)S(1)} %get-tuple-element.54.after_ref.solve_ref, bf16[320,64]{1,0:T(8,128)(2,1)S(1)} %get-tuple-element.55.left_ref, ...), custom_call_target="tpu_custom_call", output_to_operand_aliasing={{0}: (4, {}), {1}: (5, {})} | custom-call | flops 8589934592 | bytes 1048576 | tf_op jit(solution)/shard_map/result/pallas_call | solution.py:500
  80.7 0.7 collective-permute-done.24.value_ref
  81.4 0.0 collective-permute-start.25
  81.4 0.0 collective-permute-done.20.value_ref
  81.4 1.1 %collective-permute-start.23 = (f32[640,128]{1,0:T(8,128)S(1)}, f32[640,128]{1,0:T(8,128)S(1)}, u32[]{:S(2)}, u32[]{:S(2)}) collective-permute-start(f32[640,128]{1,0:T(8,128)S(1)} %tie.4.refs_0_), channel_id=1, source_target_pairs={{0,1},{1,0},{2,3},{3,2},{4,5},{5,4},{6,7},{7,6},{8,9},{9,8},{10,11... | collective-permute-start | bytes 983048 | tf_op jit(solution)/shard_map/ppermute | solution.py:83
  82.5 0.0 collective-permute-done.26.refs_2_
  82.5 2.7 %result.8 = (bf16[320,10240]{1,0:T(8,128)(2,1)}, f32[64,10240]{1,0:T(8,128)}) custom-call(bf16[64,384]{1,0:T(8,128)(2,1)S(1)} %get-tuple-element.54.after_ref.solve_ref, bf16[320,64]{1,0:T(8,128)(2,1)S(1)} %get-tuple-element.55.left_ref, bf16[320,10240]{1,0:T(8,128)(2,1)S(1)} %get-tuple-element.38.m_ref, ...), custom_call_target="tpu_custom_call", output_to_operand_aliasing={{0}: (6, {}), {1}: (7, {})} | custom-call | flops 8589934592 | bytes 1048576 | tf_op jit(solution)/shard_map/result/pallas_call | solution.py:500
  85.3 2.1 %result.9 = (bf16[320,10240]{1,0:T(8,128)(2,1)}, f32[64,10240]{1,0:T(8,128)}, f32[64,320]{1,0:T(8,128)}) custom-call(bf16[64,384]{1,0:T(8,128)(2,1)S(1)} %get-tuple-element.54.after_ref.solve_ref, bf16[320,64]{1,0:T(8,128)(2,1)S(1)} %get-tuple-element.55.left_ref, ...), custom_call_target="tpu_custom_call", output_to_operand_aliasing={{0}: (6, {}), {1}: (7, {})} | custom-call | flops 8589934592 | bytes 1048576 | tf_op jit(solution)/shard_map/result/pallas_call | solution.py:500
  (12 shorter events, 0.1 us)
Async XLA Ops:
  6.8 6.7 %collective-permute-start = (f32[160,128]{1,0:T(8,128)S(1)}, f32[160,128]{1,0:T(8,128)S(1)}, u32[]{:S(2)}, u32[]{:S(2)}) collective-permute-start(f32[160,128]{1,0:T(8,128)S(1)} %get-tuple-element.37), channel_id=1, source_target_pairs={{0,8},{1,33},{2,10},{3,35},{4,12},{5,37},{6,14},{7,39},{8,16},{9,4... | collective-permute-start | bytes 245768 | tf_op jit(solution)/shard_map/ppermute | solution.py:78
  9.4 4.2 %collective-permute-start.1 = (f32[160,128]{1,0:T(8,128)S(1)}, f32[160,128]{1,0:T(8,128)S(1)}, u32[]{:S(2)}, u32[]{:S(2)}) collective-permute-start(f32[160,128]{1,0:T(8,128)S(1)} %get-tuple-element.37), channel_id=1, source_target_pairs={{0,24},{1,97},{2,26},{3,99},{4,28},{5,101},{6,30},{7,103},{8,0},{9... | collective-permute-start | bytes 245768 | tf_op jit(solution)/shard_map/ppermute | solution.py:78
  11.6 5.1 %collective-permute-start.2 = (f32[160,128]{1,0:T(8,128)S(1)}, f32[160,128]{1,0:T(8,128)S(1)}, u32[]{:S(2)}, u32[]{:S(2)}) collective-permute-start(f32[160,128]{1,0:T(8,128)S(1)} %get-tuple-element.37), channel_id=1, source_target_pairs={{0,16},{1,65},{2,18},{3,67},{4,20},{5,69},{6,22},{7,71},{8,24},{9,... | collective-permute-start | bytes 245768 | tf_op jit(solution)/shard_map/ppermute | solution.py:78
  16.7 4.6 %collective-permute-start.3 = (f32[160,128]{1,0:T(8,128)S(1)}, f32[160,128]{1,0:T(8,128)S(1)}, u32[]{:S(2)}, u32[]{:S(2)}) collective-permute-start(f32[160,128]{1,0:T(8,128)S(1)} %add_add_fusion.a_ref), channel_id=1, source_target_pairs={{0,32},{1,9},{2,34},{3,11},{4,36},{5,13},{6,38},{7,15},{8,40},{9,1... | collective-permute-start | bytes 245768 | tf_op jit(solution)/shard_map/ppermute | solution.py:78
  17.7 3.6 %collective-permute-start.4 = (f32[160,128]{1,0:T(8,128)S(1)}, f32[160,128]{1,0:T(8,128)S(1)}, u32[]{:S(2)}, u32[]{:S(2)}) collective-permute-start(f32[160,128]{1,0:T(8,128)S(1)} %add_add_fusion.a_ref), channel_id=1, source_target_pairs={{0,96},{1,25},{2,98},{3,27},{4,100},{5,29},{6,102},{7,31},{8,104},... | collective-permute-start | bytes 245768 | tf_op jit(solution)/shard_map/ppermute | solution.py:78
  19.4 4.8 %collective-permute-start.5 = (f32[160,128]{1,0:T(8,128)S(1)}, f32[160,128]{1,0:T(8,128)S(1)}, u32[]{:S(2)}, u32[]{:S(2)}) collective-permute-start(f32[160,128]{1,0:T(8,128)S(1)} %add_add_fusion.a_ref), channel_id=1, source_target_pairs={{0,64},{1,17},{2,66},{3,19},{4,68},{5,21},{6,70},{7,23},{8,72},{9,... | collective-permute-start | bytes 245768 | tf_op jit(solution)/shard_map/ppermute | solution.py:78
  24.9 4.8 %collective-permute-start.6 = (f32[680,128]{1,0:T(8,128)S(1)}, f32[680,128]{1,0:T(8,128)S(1)}, u32[]{:S(2)}, u32[]{:S(2)}) collective-permute-start(f32[680,128]{1,0:T(8,128)S(1)} %get-tuple-element.41), channel_id=1, source_target_pairs={{0,1},{1,0},{2,3},{3,2},{4,5},{5,4},{6,7},{7,6},{8,9},{9,8},{10,11... | collective-permute-start | bytes 1044488 | tf_op jit(solution)/shard_map/ppermute | solution.py:83
  29.2 3.0 %collective-permute-start.7 = (f32[1920,128]{1,0:T(8,128)S(1)}, f32[1920,128]{1,0:T(8,128)S(1)}, u32[]{:S(2)}, u32[]{:S(2)}) collective-permute-start(f32[1920,128]{1,0:T(8,128)S(1)} %next_right.3.after_ref), channel_id=1, source_target_pairs={{0,1},{1,0},{2,3},{3,2},{4,5},{5,4},{6,7},{7,6},{8,9},{9,8},{10,11... | collective-permute-start | bytes 2949128 | tf_op jit(solution)/shard_map/ppermute | solution.py:83
  29.8 7.8 %collective-permute-start.10 = (f32[640,128]{1,0:T(8,128)S(1)}, f32[640,128]{1,0:T(8,128)S(1)}, u32[]{:S(2)}, u32[]{:S(2)}) collective-permute-start(f32[640,128]{1,0:T(8,128)S(1)} %get-tuple-element.46), channel_id=1, source_target_pairs={{0,16},{1,65},{2,66},{3,19},{4,20},{5,69},{6,70},{7,23},{8,72},{9,... | collective-permute-start | bytes 983048 | tf_op jit(solution)/shard_map/ppermute | solution.py:78
  32.5 8.7 %collective-permute-start.8 = (f32[640,128]{1,0:T(8,128)S(1)}, f32[640,128]{1,0:T(8,128)S(1)}, u32[]{:S(2)}, u32[]{:S(2)}) collective-permute-start(f32[640,128]{1,0:T(8,128)S(1)} %get-tuple-element.44), channel_id=1, source_target_pairs={{0,9},{1,32},{2,35},{3,10},{4,13},{5,36},{6,39},{7,14},{8,41},{9,1... | collective-permute-start | bytes 983048 | tf_op jit(solution)/shard_map/ppermute | solution.py:78
  33.9 7.5 %collective-permute-start.9 = (f32[640,128]{1,0:T(8,128)S(1)}, f32[640,128]{1,0:T(8,128)S(1)}, u32[]{:S(2)}, u32[]{:S(2)}) collective-permute-start(f32[640,128]{1,0:T(8,128)S(1)} %get-tuple-element.45), channel_id=1, source_target_pairs={{0,25},{1,96},{2,99},{3,26},{4,29},{5,100},{6,103},{7,30},{8,105},... | collective-permute-start | bytes 983048 | tf_op jit(solution)/shard_map/ppermute | solution.py:78
  41.4 6.2 %collective-permute-start.11 = (f32[200,128]{1,0:T(8,128)S(1)}, f32[200,128]{1,0:T(8,128)S(1)}, u32[]{:S(2)}, u32[]{:S(2)}) collective-permute-start(f32[200,128]{1,0:T(8,128)S(1)} %get-tuple-element.49), channel_id=1, source_target_pairs={{0,33},{1,2},{2,5},{3,34},{4,37},{5,6},{6,1},{7,38},{8,11},{9,40},... | collective-permute-start | bytes 307208 | tf_op jit(solution)/shard_map/ppermute | solution.py:78
  43.8 4.1 %collective-permute-start.12 = (f32[200,128]{1,0:T(8,128)S(1)}, f32[200,128]{1,0:T(8,128)S(1)}, u32[]{:S(2)}, u32[]{:S(2)}) collective-permute-start(f32[200,128]{1,0:T(8,128)S(1)} %get-tuple-element.50), channel_id=1, source_target_pairs={{0,97},{1,6},{2,1},{3,98},{4,101},{5,2},{6,5},{7,102},{8,15},{9,10... | collective-permute-start | bytes 307208 | tf_op jit(solution)/shard_map/ppermute | solution.py:78
  45.4 5.3 %collective-permute-start.13 = (f32[200,128]{1,0:T(8,128)S(1)}, f32[200,128]{1,0:T(8,128)S(1)}, u32[]{:S(2)}, u32[]{:S(2)}) collective-permute-start(f32[200,128]{1,0:T(8,128)S(1)} %get-tuple-element.51), channel_id=1, source_target_pairs={{0,64},{1,5},{2,6},{3,67},{4,68},{5,1},{6,2},{7,71},{8,12},{9,73},... | collective-permute-start | bytes 307208 | tf_op jit(solution)/shard_map/ppermute | solution.py:78
  50.7 5.7 %collective-permute-start.14 = (f32[200,128]{1,0:T(8,128)S(1)}, f32[200,128]{1,0:T(8,128)S(1)}, u32[]{:S(2)}, u32[]{:S(2)}) collective-permute-start(f32[200,128]{1,0:T(8,128)S(1)} %across.2.a_ref), channel_id=1, source_target_pairs={{0,3},{1,8},{2,11},{3,4},{4,7},{5,12},{6,15},{7,0},{8,17},{9,10},{... | collective-permute-start | bytes 307208 | tf_op jit(solution)/shard_map/ppermute | solution.py:78
  51.8 4.6 %collective-permute-start.15 = (f32[200,128]{1,0:T(8,128)S(1)}, f32[200,128]{1,0:T(8,128)S(1)}, u32[]{:S(2)}, u32[]{:S(2)}) collective-permute-start(f32[200,128]{1,0:T(8,128)S(1)} %across.2.a_ref), channel_id=1, source_target_pairs={{0,7},{1,24},{2,27},{3,0},{4,3},{5,28},{6,31},{7,4},{8,1},{9,14},{... | collective-permute-start | bytes 307208 | tf_op jit(solution)/shard_map/ppermute | solution.py:78
  53.8 5.0 %collective-permute-start.16 = (f32[200,128]{1,0:T(8,128)S(1)}, f32[200,128]{1,0:T(8,128)S(1)}, u32[]{:S(2)}, u32[]{:S(2)}) collective-permute-start(f32[200,128]{1,0:T(8,128)S(1)} %across.2.a_ref), channel_id=1, source_target_pairs={{0,4},{1,17},{2,18},{3,7},{4,0},{5,21},{6,22},{7,3},{8,24},{9,13},... | collective-permute-start | bytes 307208 | tf_op jit(solution)/shard_map/ppermute | solution.py:78
  58.9 7.1 %collective-permute-start.17 = (f32[160,128]{1,0:T(8,128)S(1)}, f32[160,128]{1,0:T(8,128)S(1)}, u32[]{:S(2)}, u32[]{:S(2)}) collective-permute-start(f32[160,128]{1,0:T(8,128)S(1)} %get-tuple-element.56.a_ref), channel_id=1, source_target_pairs={{0,33},{1,2},{2,5},{3,34},{4,37},{5,6},{6,1},{7,38},{8,11},{9,40},... | collective-permute-start | bytes 245768 | tf_op jit(solution)/shard_map/ppermute | solution.py:78
  61.4 4.7 %collective-permute-start.18 = (f32[160,128]{1,0:T(8,128)S(1)}, f32[160,128]{1,0:T(8,128)S(1)}, u32[]{:S(2)}, u32[]{:S(2)}) collective-permute-start(f32[160,128]{1,0:T(8,128)S(1)} %get-tuple-element.56.a_ref), channel_id=1, source_target_pairs={{0,97},{1,6},{2,1},{3,98},{4,101},{5,2},{6,5},{7,102},{8,15},{9,10... | collective-permute-start | bytes 245768 | tf_op jit(solution)/shard_map/ppermute | solution.py:78
  62.9 4.8 %collective-permute-start.19 = (f32[160,128]{1,0:T(8,128)S(1)}, f32[160,128]{1,0:T(8,128)S(1)}, u32[]{:S(2)}, u32[]{:S(2)}) collective-permute-start(f32[160,128]{1,0:T(8,128)S(1)} %get-tuple-element.56.a_ref), channel_id=1, source_target_pairs={{0,64},{1,5},{2,6},{3,67},{4,68},{5,1},{6,2},{7,71},{8,12},{9,73},... | collective-permute-start | bytes 245768 | tf_op jit(solution)/shard_map/ppermute | solution.py:78
  67.7 9.4 %collective-permute-start.21 = (f32[640,128]{1,0:T(8,128)S(1)}, f32[640,128]{1,0:T(8,128)S(1)}, u32[]{:S(2)}, u32[]{:S(2)}) collective-permute-start(f32[640,128]{1,0:T(8,128)S(1)} %assemble.1.value_ref), channel_id=1, source_target_pairs={{0,16},{1,65},{2,66},{3,19},{4,20},{5,69},{6,70},{7,23},{8,72},{9,... | collective-permute-start | bytes 983048 | tf_op jit(solution)/shard_map/ppermute | solution.py:78
  69.3 12.1 %collective-permute-start.24 = (f32[640,128]{1,0:T(8,128)S(1)}, f32[640,128]{1,0:T(8,128)S(1)}, u32[]{:S(2)}, u32[]{:S(2)}) collective-permute-start(f32[640,128]{1,0:T(8,128)S(1)} %assemble.1.value_ref), channel_id=1, source_target_pairs={{0,25},{1,96},{2,99},{3,26},{4,29},{5,100},{6,103},{7,30},{8,105},... | collective-permute-start | bytes 983048 | tf_op jit(solution)/shard_map/ppermute | solution.py:78
  72.8 8.6 %collective-permute-start.20 = (f32[640,128]{1,0:T(8,128)S(1)}, f32[640,128]{1,0:T(8,128)S(1)}, u32[]{:S(2)}, u32[]{:S(2)}) collective-permute-start(f32[640,128]{1,0:T(8,128)S(1)} %assemble.1.value_ref), channel_id=1, source_target_pairs={{0,9},{1,32},{2,35},{3,10},{4,13},{5,36},{6,39},{7,14},{8,41},{9,1... | collective-permute-start | bytes 983048 | tf_op jit(solution)/shard_map/ppermute | solution.py:78
  72.8 2.7 %collective-permute-start.22 = (f32[640,128]{1,0:T(8,128)S(1)}, f32[640,128]{1,0:T(8,128)S(1)}, u32[]{:S(2)}, u32[]{:S(2)}) collective-permute-start(f32[640,128]{1,0:T(8,128)S(1)} %again.1.refs_0_), channel_id=1, source_target_pairs={{0,1},{1,0},{2,3},{3,2},{4,5},{5,4},{6,7},{7,6},{8,9},{9,8},{10,11... | collective-permute-start | bytes 983048 | tf_op jit(solution)/shard_map/ppermute | solution.py:83
  77.2 5.3 %collective-permute-start.26 = (f32[640,128]{1,0:T(8,128)S(1)}, f32[640,128]{1,0:T(8,128)S(1)}, u32[]{:S(2)}, u32[]{:S(2)}) collective-permute-start(f32[640,128]{1,0:T(8,128)S(1)} %tie.3.refs_0_), channel_id=1, source_target_pairs={{0,1},{1,0},{2,3},{3,2},{4,5},{5,4},{6,7},{7,6},{8,9},{9,8},{10,11... | collective-permute-start | bytes 983048 | tf_op jit(solution)/shard_map/ppermute | solution.py:83
  81.4 3.8 %collective-permute-start.25 = (f32[640,128]{1,0:T(8,128)S(1)}, f32[640,128]{1,0:T(8,128)S(1)}, u32[]{:S(2)}, u32[]{:S(2)}) collective-permute-start(f32[640,128]{1,0:T(8,128)S(1)} %tie.5.refs_1_), channel_id=1, source_target_pairs={{0,1},{1,0},{2,3},{3,2},{4,5},{5,4},{6,7},{7,6},{8,9},{9,8},{10,11... | collective-permute-start | bytes 983048 | tf_op jit(solution)/shard_map/ppermute | solution.py:83
  81.4 3.8 %collective-permute-start.23 = (f32[640,128]{1,0:T(8,128)S(1)}, f32[640,128]{1,0:T(8,128)S(1)}, u32[]{:S(2)}, u32[]{:S(2)}) collective-permute-start(f32[640,128]{1,0:T(8,128)S(1)} %tie.4.refs_0_), channel_id=1, source_target_pairs={{0,1},{1,0},{2,3},{3,2},{4,5},{5,4},{6,7},{7,6},{8,9},{9,8},{10,11... | collective-permute-start | bytes 983048 | tf_op jit(solution)/shard_map/ppermute | solution.py:83

commit v16 on v15

--- a/solution.py
+++ b/solution.py
@@ -18,7 +18,7 @@
 QUARTERS = 4
 SHRINK = 2.0**-16
 RIGHT = 1 << 33
-SHIFTS = (1, 3, 2)
+TURNS = (1, 2, 3)
 ANY = pl.BlockSpec(memory_space=pl.ANY)
 WHOLE = pl.BlockSpec(memory_space=pltpu.VMEM)
 
@@ -37,18 +37,31 @@
 
 def core_of(x, y, z, c):
     return c
+
+
+def half_of(x, y, z, c):
+    return (x + y + z + c) % 2
+
+
+MASKS = (1, 3)
+
+
+def corner(kind, x, z):
+    if kind == 0:
+        return ((x ^ (x >> 1)) & 1) + 2 * ((z ^ (z >> 1)) & 1)
+    return (x >> 1) + 2 * (z >> 1)
 
 
 def place():
     x, y, z, c = (lax.axis_index(a) for a in ("x", "y", "z", "c"))
     half = half_of(x, y, z, c)
-    return half, jnp.where(half == 0, x, z), jnp.where(half == 0, z, y)
+    zero, one = corner(0, x, z), corner(1, x, z)
+    return half, jnp.where(half == 0, zero, one), jnp.where(half == 0, one, zero)
 
 
 def other_place():
-    x, y, z, c = (lax.axis_index(a) for a in ("x", "y", "z", "c"))
-    half = 1 - half_of(x, y, z, c)
-    return half, jnp.where(half == 0, x, z), jnp.where(half == 0, z, y)
+    half, first, second = place()
+    return 1 - half, second, first
 
 
 def index(z, x, y, c):
@@ -65,16 +78,26 @@
     ]
 
 
-def ring(values, phase, shifts=SHIFTS, orders=("xzy", "zyx"), group=half_of):
+def square(values, phase, turns, group=half_of):
     out = []
-    for k, value in zip(shifts, values):
+    for k, value in zip(turns, values):
         pairs = []
         for z, x, y, c in everyone():
-            to = {"z": z, "x": x, "y": y}
-            axis = orders[group(x, y, z, c)][phase]
-            to[axis] = (to[axis] + k) % SIZES[AXES.index(axis)]
-            core = c if group is core_of else (c + k) % 2
-            pairs.append((index(z, x, y, c), index(*to.values(), core)))
+            mask = MASKS[(group(x, y, z, c) + phase) % 2]
+            to_x, to_z = x ^ (mask if k & 1 else 0), z ^ (mask if k & 2 else 0)
+            core = c if group is core_of else (c + x + to_x + z + to_z) % 2
+            pairs.append((index(z, x, y, c), index(to_z, to_x, y, core)))
+        out.append(lax.ppermute(value, AXES, pairs))
+    return out
+
+
+def ring_y(value):
+    out = []
+    for k in (1, 3, 2):
+        pairs = [
+            (index(z, x, y, c), index(z, x, (y + k) % SIZES[2], (c + k) % 2))
+            for z, x, y, c in everyone()
+        ]
         out.append(lax.ppermute(value, AXES, pairs))
     return out
 
@@ -176,7 +199,7 @@
 
 def quarters_of(own, turns):
     half, turn, _ = place() if own else other_place()
-    return [half * QUARTERS + (turn + k) % QUARTERS for k in turns]
+    return [half * QUARTERS + (turn ^ k) for k in turns]
 
 
 def split(n):
@@ -297,51 +320,64 @@
     )(kept, got, weight)
 
 
-def add_quarters_kernel(a_ref, b_ref, c_ref, d_ref, ext_ref, *out):
+def add_quarters_kernel(a_ref, b_ref, c_ref, d_ref, *out):
     size = a_ref.shape[0] // QUARTERS
-    for k, ref in zip((0,) + SHIFTS, out):
-        at = pl.ds(pl.multiple_of((place()[2] + k) % QUARTERS * size, size), size)
-        ref[:size] = (a_ref[at] + b_ref[at]) + (c_ref[at] + d_ref[at])
-        ref[size:] = ext_ref[...]
-
-
-def add_quarters(parts, ext):
+    for k, ref in zip((0,) + TURNS, out):
+        at = pl.ds(pl.multiple_of((place()[2] ^ k) * size, size), size)
+        ref[...] = (a_ref[at] + b_ref[at]) + (c_ref[at] + d_ref[at])
+
+
+def add_quarters(parts):
     size = parts[0].shape[0] // QUARTERS
     return pl.pallas_call(
         add_quarters_kernel,
-        out_shape=[jax.ShapeDtypeStruct((size + ext.shape[0], 128), F32)] * QUARTERS,
-        in_specs=[WHOLE] * (QUARTERS + 1),
+        out_shape=[jax.ShapeDtypeStruct((size, 128), F32)] * QUARTERS,
+        in_specs=[WHOLE] * QUARTERS,
         out_specs=[WHOLE] * QUARTERS,
         compiler_params=params(8),
         name="add_quarters",
+    )(*parts)
+
+
+def add_parts_kernel(a_ref, b_ref, c_ref, d_ref, ext_ref, out_ref):
+    size = a_ref.shape[0]
+    out_ref[:size] = (a_ref[...] + b_ref[...]) + (c_ref[...] + d_ref[...])
+    out_ref[size:] = ext_ref[...]
+
+
+def add_parts(parts, ext):
+    return pl.pallas_call(
+        add_parts_kernel,
+        out_shape=jax.ShapeDtypeStruct((parts[0].shape[0] + ext.shape[0], 128), F32),
+        in_specs=[WHOLE] * 5,
+        out_specs=WHOLE,
+        compiler_params=params(8),
+        name="add_parts",
     )(*parts, ext)
 
 
-def across_kernel(half_along_y, extra, a_ref, b_ref, c_ref, d_ref, out_ref, *ext_ref):
-    grams = extra - ROWS
-    size = a_ref.shape[0] - extra
+def across_kernel(a_ref, b_ref, c_ref, d_ref, out_ref, ext_ref):
+    size = out_ref.shape[0]
+    grams = ext_ref.shape[0] - ROWS
     refs = (a_ref, b_ref, c_ref, d_ref)
     peaks = [r[size + grams : size + grams + 1, :1] for r in refs]
     top = jnp.maximum(jnp.maximum(peaks[0], peaks[1]), jnp.maximum(peaks[2], peaks[3]))
     a, b, c, d = (r[:size] * (k / top) for r, k in zip(refs, peaks))
-    out_ref[:size] = (a + b) + (c + d)
+    out_ref[...] = (a + b) + (c + d)
     a, b, c, d = (r[size : size + grams] for r in refs)
-    gram = jnp.where(place()[0] == half_along_y, (a + b) + (c + d), a)
-    ext = out_ref.at[size:] if not ext_ref else ext_ref[0]
-    ext[:grams] = gram
-    ext[grams:] = jnp.broadcast_to(top, (ROWS, 128))
-
-
-def across(half_along_y, parts, extra, keep):
-    rows = parts[0].shape[0]
-    out = [jax.ShapeDtypeStruct((rows, 128), F32)]
-    if not keep:
-        out = [jax.ShapeDtypeStruct((rows - extra, 128), F32), pltpu.VMEM((extra, 128), F32)]
-    return pl.pallas_call(
-        functools.partial(across_kernel, half_along_y, extra),
-        out_shape=out,
+    ext_ref[:grams] = (a + b) + (c + d)
+    ext_ref[grams:] = jnp.broadcast_to(top, (ROWS, 128))
+
+
+def across(parts, extra):
+    return pl.pallas_call(
+        across_kernel,
+        out_shape=[
+            jax.ShapeDtypeStruct((parts[0].shape[0] - extra, 128), F32),
+            pltpu.VMEM((extra, 128), F32),
+        ],
         in_specs=[WHOLE] * 4,
-        out_specs=[WHOLE] * len(out),
+        out_specs=[WHOLE] * 2,
         compiler_params=params(8),
         name="across",
     )(*parts)
@@ -350,8 +386,8 @@
 def assemble_kernel(a_ref, b_ref, c_ref, d_ref, after_ref, out_ref):
     del after_ref
     size = a_ref.shape[0]
-    for k, ref in zip((0,) + SHIFTS, (a_ref, b_ref, c_ref, d_ref)):
-        at = pl.multiple_of((place()[2] + QUARTERS - k) % QUARTERS * size, size)
+    for k, ref in zip((0,) + TURNS, (a_ref, b_ref, c_ref, d_ref)):
+        at = pl.multiple_of((place()[2] ^ k) * size, size)
         out_ref[pl.ds(at, size)] = ref[...]
 
 
@@ -456,8 +492,7 @@
     for n, (own, k) in enumerate(sources):
         t_ref = refs[n]
         half, turn, _ = place() if own else other_place()
-        quarter = (turn + QUARTERS - k) % QUARTERS
-        base = (half * QUARTERS + quarter) * columns
+        base = (half * QUARTERS + (turn ^ k)) * columns
         bases.append(base)
         for at in range(0, columns, width):
             t = jnp.concatenate(
@@ -552,26 +587,25 @@
     rank = q_start.shape[0]
     replicas = SIZES[0] * SIZES[1]
     merged, p = merge(gradient[0], error[0], q_start)
-    a, b, c = ring([p] * 3, 0, orders=("xz", "zx"), group=core_of)
+    a, b, c = square([p] * 3, 0, TURNS, core_of)
     p = (p + a) + (b + c)
     sent, ext, p_mean, pieces = first_right(
-        (2,), (p, *ring([p] * 3, 1, orders=("xz", "zx"), group=core_of)), merged, rank, replicas
+        (3,), (p, *square([p] * 3, 1, TURNS, core_of)), merged, rank, replicas
     )
     got = swap(sent)
-    sent = next_right(False, (1, 3, 0), pieces, merged, ext)
+    sent = next_right(False, (1, 2, 0), pieces, merged, ext)
     got_next = swap(sent)
-    kept = next_right(True, (2,), pieces, merged, sent)
-    two, ext, weight = first_pair(kept, got, ext)
-    (two,) = ring((two,), 0, (2,))
-    kept = next_right(True, (1, 3, 0), pieces, merged, weight)
+    kept = next_right(True, (3,), pieces, merged, sent)
+    far, ext, weight = first_pair(kept, got, ext)
+    (far,) = square((far,), 0, (3,))
+    kept = next_right(True, (1, 2, 0), pieces, merged, weight)
     *near, own = next_pair(kept, got_next, weight)
-    own, *sent = add_quarters((own, *ring(near, 0, (1, 3)), two), ext)
-    extra = ext.shape[0]
-    (part,) = across(1, (own, *ring(sent, 1)), extra, True)
-    total, ext = across(0, (part, *ring([part] * 3, 2)), extra, False)
+    own, *sent = add_quarters((own, *square(near, 0, (1, 2)), far))
+    part = add_parts((own, *square(sent, 1, TURNS)), ext)
+    total, ext = across((part, *ring_y(part)), ext.shape[0])
     solve, left, p_hat = factor(ext, p_mean, replicas)
-    total = assemble((total, *ring([total] * 3, 1)), solve)
-    two, one, three = ring([total] * 3, 0, (2, 1, 3))
+    total = assemble((total, *square([total] * 3, 1, TURNS)), solve)
+    three, one, two = square([total] * 3, 0, (3, 1, 2))
 
     def write(sources, totals, *after, **more):
         return result(sources, totals, merged, solve, left, *after, **more)
@@ -580,12 +614,12 @@
     total = again(total)
     out = write(((own, 0),), (total,), None)
     *out, token = write(((other, 0),), (swap(total),), out, token=True)
-    two = tie(two, token)
-    *out, token = write(((own, 2),), (two,), out, token=True)
-    one, three = tie(one, token), tie(three, token)
-    out = write(((own, 1), (own, 3), (other, 2)), (one, three, swap(two)), out)
+    three = tie(three, token)
+    *out, token = write(((own, 3),), (three,), out, token=True)
+    one, two = tie(one, token), tie(two, token)
+    out = write(((own, 1), (own, 2), (other, 3)), (one, two, swap(three)), out)
     new_error, q_new, p_hat = write(
-        ((other, 1), (other, 3)), (swap(one), swap(three)), out, p_hat
+        ((other, 1), (other, 2)), (swap(one), swap(two)), out, p_hat
     )
     return (new_error[None], p_hat, q_new)
 

time: 87.6 us -> 91.1 us (1.040)
  starting transfers between devices: 41.2 us -> 46 us
  waiting for transfers between devices: 24.4 us -> 23.1 us
    ppermute x6, starting transfers between devices: 7.87 us -> 12.4 us  [swap(): return lax.ppermute(value, 'c', [(0, 1), (1, 0)])]
    ppermute x21, waiting for transfers between devices: 24.4 us -> 22.9 us  [the longest x18 18.7 us: square(): out.append(lax.ppermute(value, AXES, pairs))]
  transfers between devices with their start and end apart: 27 -> 27, of which waited for: 14 -> 16; matrix products, arithmetic and copies ran while one was open for 0% -> 0% of each run, Pallas kernels for 13% -> 13%
where the time goes in v16:
time: 91.1 us; the launch traced here: 91 us
  starting transfers between devices  46 us (50%)
  waiting for transfers between devices  23.1 us (25%)
  Pallas kernels  20.9 us (23%)
  between operations  1.02 us (1%)
    ppermute x18, starting transfers between devices, square(): out.append(lax.ppermute(value, AXES, pairs))  27.3 us
    ppermute x18, waiting for transfers between devices, square(): out.append(lax.ppermute(value, AXES, pairs))  18.7 us
    ppermute x6, starting transfers between devices, swap(): return lax.ppermute(value, 'c', [(0, 1), (1, 0)])  12.4 us
    pallas_call x5, Pallas kernels, result(): pl.pallas_call(functools.partial(result_kernel, sources, more, quarter //...  9.47 us
    ppermute x3, starting transfers between devices, ring_y(): out.append(lax.ppermute(value, AXES, pairs))  6.29 us
    pallas_call x1, Pallas kernels, merge(): pl.pallas_call(functools.partial(merge_kernel, cuts), out_shape=[pltpu.VM...  6.21 us
    ppermute x3, waiting for transfers between devices, ring_y(): out.append(lax.ppermute(value, AXES, pairs))  4.23 us
    pallas_call x1, Pallas kernels, factor(): pl.pallas_call(functools.partial(factor_kernel, replicas), out_shape=[jax...  2.01 us
  transfers between devices with their start and end apart: 27, of which 16 were waited for; matrix products, arithmetic and copies ran while one was open for 0% of the time, Pallas kernels for 13%

profile of v16, /device:TPU:1, one launch (start us, length us, event | category | flops | bytes accessed | tf_op | source)
XLA Modules:
  0.0 91.0 jit_solution(462175060646072272)
XLA Ops:
  0.6 6.2 %merge.1 = (bf16[320,10240]{1,0:T(8,128)(2,1)S(1)}, f32[160,128]{1,0:T(8,128)S(1)}) custom-call(bf16[320,10240]{1,0:T(8,128)(2,1)} %bitcast.3, bf16[320,10240]{1,0:T(8,128)(2,1)} %bitcast.4, bf16[64,10240]{1,0:T(8,128)(2,1)} %q_hbm.1), custom_call_target="tpu_custom_call" | custom-call | flops 419430400 | bytes 13107200 | tf_op jit(solution)/shard_map/merge/pallas_call | solution.py:162
  6.8 3.4 %collective-permute-start = (f32[160,128]{1,0:T(8,128)S(1)}, f32[160,128]{1,0:T(8,128)S(1)}, u32[]{:S(2)}, u32[]{:S(2)}) collective-permute-start(f32[160,128]{1,0:T(8,128)S(1)} %get-tuple-element.37), channel_id=1, source_target_pairs={{0,8},{1,25},{2,10},{3,27},{4,12},{5,29},{6,14},{7,31},{8,0},{9,17... | collective-permute-start | bytes 245768 | tf_op jit(solution)/shard_map/ppermute | solution.py:90
  10.2 3.8 %collective-permute-start.1 = (f32[160,128]{1,0:T(8,128)S(1)}, f32[160,128]{1,0:T(8,128)S(1)}, u32[]{:S(2)}, u32[]{:S(2)}) collective-permute-start(f32[160,128]{1,0:T(8,128)S(1)} %get-tuple-element.37), channel_id=1, source_target_pairs={{0,32},{1,97},{2,34},{3,99},{4,36},{5,101},{6,38},{7,103},{8,40},{... | collective-permute-start | bytes 245768 | tf_op jit(solution)/shard_map/ppermute | solution.py:90
  14.0 0.0 collective-permute-start.2
  14.0 0.0 collective-permute-done
  14.0 2.0 %collective-permute-done.1 = f32[160,128]{1,0:T(8,128)S(1)} collective-permute-done((f32[160,128]{1,0:T(8,128)S(1)}, f32[160,128]{1,0:T(8,128)S(1)}, u32[]{:S(2)}, u32[]{:S(2)}) %collective-permute-start.1) | collective-permute-done | bytes 81952 | tf_op jit(solution)/shard_map/ppermute | solution.py:90
  16.0 4.6 %collective-permute-done.2 = f32[160,128]{1,0:T(8,128)S(1)} collective-permute-done((f32[160,128]{1,0:T(8,128)S(1)}, f32[160,128]{1,0:T(8,128)S(1)}, u32[]{:S(2)}, u32[]{:S(2)}) %collective-permute-start.2) | collective-permute-done | bytes 81952 | tf_op jit(solution)/shard_map/ppermute | solution.py:90
  20.6 0.1 collective-permute-start.3
  20.7 0.1 collective-permute-start.4
  20.8 2.5 %collective-permute-start.5 = (f32[160,128]{1,0:T(8,128)S(1)}, f32[160,128]{1,0:T(8,128)S(1)}, u32[]{:S(2)}, u32[]{:S(2)}) collective-permute-start(f32[160,128]{1,0:T(8,128)S(1)} %add_add_fusion.a_ref), channel_id=1, source_target_pairs={{0,120},{1,41},{2,122},{3,43},{4,124},{5,45},{6,126},{7,47},{8,112... | collective-permute-start | bytes 245768 | tf_op jit(solution)/shard_map/ppermute | solution.py:90
  23.4 0.9 %collective-permute-done.3.b_ref = f32[160,128]{1,0:T(8,128)S(1)} collective-permute-done((f32[160,128]{1,0:T(8,128)S(1)}, f32[160,128]{1,0:T(8,128)S(1)}, u32[]{:S(2)}, u32[]{:S(2)}) %collective-permute-start.3) | collective-permute-done | bytes 81952 | tf_op jit(solution)/shard_map/ppermute | solution.py:90
  24.3 0.1 collective-permute-done.4.c_ref
  24.4 0.8 collective-permute-done.5.d_ref
  25.2 0.6 first_right.1
  25.8 4.5 %collective-permute-start.6 = (f32[680,128]{1,0:T(8,128)S(1)}, f32[680,128]{1,0:T(8,128)S(1)}, u32[]{:S(2)}, u32[]{:S(2)}) collective-permute-start(f32[680,128]{1,0:T(8,128)S(1)} %get-tuple-element.41), channel_id=1, source_target_pairs={{0,1},{1,0},{2,3},{3,2},{4,5},{5,4},{6,7},{7,6},{8,9},{9,8},{10,11... | collective-permute-start | bytes 1044488 | tf_op jit(solution)/shard_map/ppermute | solution.py:106
  30.3 0.8 next_right.3.after_ref
  31.1 0.1 collective-permute-start.7
  31.3 0.4 next_right.4.kept_ref
  31.6 0.0 collective-permute-done.6.got_ref
  31.6 0.1 first_pair.1
  31.8 1.1 %collective-permute-start.10 = (f32[640,128]{1,0:T(8,128)S(1)}, f32[640,128]{1,0:T(8,128)S(1)}, u32[]{:S(2)}, u32[]{:S(2)}) collective-permute-start(f32[640,128]{1,0:T(8,128)S(1)} %get-tuple-element.46), channel_id=1, source_target_pairs={{0,40},{1,121},{2,122},{3,43},{4,44},{5,125},{6,126},{7,47},{8,112... | collective-permute-start | bytes 983048 | tf_op jit(solution)/shard_map/ppermute | solution.py:90
  32.9 0.8 next_right.5.kept_ref
  33.7 0.1 collective-permute-done.7.got_ref
  33.8 0.2 next_pair.1
  34.0 2.4 %collective-permute-start.8 = (f32[640,128]{1,0:T(8,128)S(1)}, f32[640,128]{1,0:T(8,128)S(1)}, u32[]{:S(2)}, u32[]{:S(2)}) collective-permute-start(f32[640,128]{1,0:T(8,128)S(1)} %get-tuple-element.44), channel_id=1, source_target_pairs={{0,9},{1,24},{2,27},{3,10},{4,13},{5,28},{6,31},{7,14},{8,17},{9,0... | collective-permute-start | bytes 983048 | tf_op jit(solution)/shard_map/ppermute | solution.py:90
  36.4 1.9 %collective-permute-start.9 = (f32[640,128]{1,0:T(8,128)S(1)}, f32[640,128]{1,0:T(8,128)S(1)}, u32[]{:S(2)}, u32[]{:S(2)}) collective-permute-start(f32[640,128]{1,0:T(8,128)S(1)} %get-tuple-element.45), channel_id=1, source_target_pairs={{0,33},{1,96},{2,99},{3,34},{4,37},{5,100},{6,103},{7,38},{8,105},... | collective-permute-start | bytes 983048 | tf_op jit(solution)/shard_map/ppermute | solution.py:90
  38.3 2.8 %collective-permute-done.10.d_ref = f32[640,128]{1,0:T(8,128)S(1)} collective-permute-done((f32[640,128]{1,0:T(8,128)S(1)}, f32[640,128]{1,0:T(8,128)S(1)}, u32[]{:S(2)}, u32[]{:S(2)}) %collective-permute-start.10) | collective-permute-done | bytes 327712 | tf_op jit(solution)/shard_map/ppermute | solution.py:90
  41.1 2.4 %collective-permute-done.8.b_ref = f32[640,128]{1,0:T(8,128)S(1)} collective-permute-done((f32[640,128]{1,0:T(8,128)S(1)}, f32[640,128]{1,0:T(8,128)S(1)}, u32[]{:S(2)}, u32[]{:S(2)}) %collective-permute-start.8) | collective-permute-done | bytes 327712 | tf_op jit(solution)/shard_map/ppermute | solution.py:90
  43.6 1.0 %collective-permute-done.9.c_ref = f32[640,128]{1,0:T(8,128)S(1)} collective-permute-done((f32[640,128]{1,0:T(8,128)S(1)}, f32[640,128]{1,0:T(8,128)S(1)}, u32[]{:S(2)}, u32[]{:S(2)}) %collective-permute-start.9) | collective-permute-done | bytes 327712 | tf_op jit(solution)/shard_map/ppermute | solution.py:90
  44.6 0.1 add_quarters.1
  44.7 0.1 collective-permute-start.11
  44.8 0.1 collective-permute-start.12
  44.8 2.8 %collective-permute-start.13 = (f32[160,128]{1,0:T(8,128)S(1)}, f32[160,128]{1,0:T(8,128)S(1)}, u32[]{:S(2)}, u32[]{:S(2)}) collective-permute-start(f32[160,128]{1,0:T(8,128)S(1)} %get-tuple-element.50), channel_id=1, source_target_pairs={{0,120},{1,41},{2,42},{3,123},{4,124},{5,45},{6,46},{7,127},{8,32}... | collective-permute-start | bytes 245768 | tf_op jit(solution)/shard_map/ppermute | solution.py:90
  47.7 1.0 %collective-permute-done.11.b_ref = f32[160,128]{1,0:T(8,128)S(1)} collective-permute-done((f32[160,128]{1,0:T(8,128)S(1)}, f32[160,128]{1,0:T(8,128)S(1)}, u32[]{:S(2)}, u32[]{:S(2)}) %collective-permute-start.11) | collective-permute-done | bytes 81952 | tf_op jit(solution)/shard_map/ppermute | solution.py:90
  48.7 0.0 collective-permute-done.12.c_ref
  48.7 0.9 collective-permute-done.13.d_ref
  49.6 3.7 %collective-permute-start.14 = (f32[200,128]{1,0:T(8,128)S(1)}, f32[200,128]{1,0:T(8,128)S(1)}, u32[]{:S(2)}, u32[]{:S(2)}) collective-permute-start(f32[200,128]{1,0:T(8,128)S(1)} %add_parts.1.a_ref), channel_id=1, source_target_pairs={{0,3},{1,2},{2,5},{3,4},{4,7},{5,6},{6,1},{7,0},{8,11},{9,10},{10,... | collective-permute-start | bytes 307208 | tf_op jit(solution)/shard_map/ppermute | solution.py:101
  53.3 1.5 %collective-permute-start.15 = (f32[200,128]{1,0:T(8,128)S(1)}, f32[200,128]{1,0:T(8,128)S(1)}, u32[]{:S(2)}, u32[]{:S(2)}) collective-permute-start(f32[200,128]{1,0:T(8,128)S(1)} %add_parts.1.a_ref), channel_id=1, source_target_pairs={{0,7},{1,6},{2,1},{3,0},{4,3},{5,2},{6,5},{7,4},{8,15},{9,14},{10,... | collective-permute-start | bytes 307208 | tf_op jit(solution)/shard_map/ppermute | solution.py:101
  54.8 1.1 %collective-permute-start.16 = (f32[200,128]{1,0:T(8,128)S(1)}, f32[200,128]{1,0:T(8,128)S(1)}, u32[]{:S(2)}, u32[]{:S(2)}) collective-permute-start(f32[200,128]{1,0:T(8,128)S(1)} %add_parts.1.a_ref), channel_id=1, source_target_pairs={{0,4},{1,5},{2,6},{3,7},{4,0},{5,1},{6,2},{7,3},{8,12},{9,13},{10,... | collective-permute-start | bytes 307208 | tf_op jit(solution)/shard_map/ppermute | solution.py:101
  55.9 1.6 %collective-permute-done.14.b_ref = f32[200,128]{1,0:T(8,128)S(1)} collective-permute-done((f32[200,128]{1,0:T(8,128)S(1)}, f32[200,128]{1,0:T(8,128)S(1)}, u32[]{:S(2)}, u32[]{:S(2)}) %collective-permute-start.14) | collective-permute-done | bytes 102432 | tf_op jit(solution)/shard_map/ppermute | solution.py:101
  57.5 0.8 collective-permute-done.15.c_ref
  58.3 1.9 %collective-permute-done.16.d_ref = f32[200,128]{1,0:T(8,128)S(1)} collective-permute-done((f32[200,128]{1,0:T(8,128)S(1)}, f32[200,128]{1,0:T(8,128)S(1)}, u32[]{:S(2)}, u32[]{:S(2)}) %collective-permute-start.16) | collective-permute-done | bytes 102432 | tf_op jit(solution)/shard_map/ppermute | solution.py:101
  60.1 0.1 across.1
  60.2 1.8 %collective-permute-start.17 = (f32[160,128]{1,0:T(8,128)S(1)}, f32[160,128]{1,0:T(8,128)S(1)}, u32[]{:S(2)}, u32[]{:S(2)}) collective-permute-start(f32[160,128]{1,0:T(8,128)S(1)} %get-tuple-element.56.a_ref), channel_id=1, source_target_pairs={{0,25},{1,8},{2,11},{3,26},{4,29},{5,12},{6,15},{7,30},{8,1},{9,16... | collective-permute-start | bytes 245768 | tf_op jit(solution)/shard_map/ppermute | solution.py:90
  62.0 1.2 %collective-permute-start.18 = (f32[160,128]{1,0:T(8,128)S(1)}, f32[160,128]{1,0:T(8,128)S(1)}, u32[]{:S(2)}, u32[]{:S(2)}) collective-permute-start(f32[160,128]{1,0:T(8,128)S(1)} %get-tuple-element.56.a_ref), channel_id=1, source_target_pairs={{0,97},{1,32},{2,35},{3,98},{4,101},{5,36},{6,39},{7,102},{8,41},{... | collective-permute-start | bytes 245768 | tf_op jit(solution)/shard_map/ppermute | solution.py:90
  63.2 0.1 collective-permute-start.19
  63.3 2.0 %factor.1 = (bf16[64,384]{1,0:T(8,128)(2,1)S(1)}, bf16[320,64]{1,0:T(8,128)(2,1)S(1)}, f32[64,320]{1,0:T(8,128)S(1)}) custom-call(f32[40,128]{1,0:T(8,128)S(1)} %get-tuple-element.52.ext_ref, f32[64,320]{1,0:T(8,128)S(1)} %get-tuple-element.53.p_ref), custom_call_target="tpu_custom_call" | custom-call | flops 4294967296 | bytes 1048576 | tf_op jit(solution)/shard_map/factor/pallas_call | solution.py:456
  65.3 0.0 collective-permute-done.17.b_ref
  65.3 0.6 collective-permute-done.18.c_ref
  65.8 1.5 %collective-permute-done.19.d_ref = f32[160,128]{1,0:T(8,128)S(1)} collective-permute-done((f32[160,128]{1,0:T(8,128)S(1)}, f32[160,128]{1,0:T(8,128)S(1)}, u32[]{:S(2)}, u32[]{:S(2)}) %collective-permute-start.19) | collective-permute-done | bytes 81952 | tf_op jit(solution)/shard_map/ppermute | solution.py:90
  67.4 1.8 %collective-permute-start.21 = (f32[640,128]{1,0:T(8,128)S(1)}, f32[640,128]{1,0:T(8,128)S(1)}, u32[]{:S(2)}, u32[]{:S(2)}) collective-permute-start(f32[640,128]{1,0:T(8,128)S(1)} %assemble.1.value_ref), channel_id=1, source_target_pairs={{0,40},{1,121},{2,122},{3,43},{4,44},{5,125},{6,126},{7,47},{8,112... | collective-permute-start | bytes 983048 | tf_op jit(solution)/shard_map/ppermute | solution.py:90
  69.2 4.3 %collective-permute-start.24 = (f32[640,128]{1,0:T(8,128)S(1)}, f32[640,128]{1,0:T(8,128)S(1)}, u32[]{:S(2)}, u32[]{:S(2)}) collective-permute-start(f32[640,128]{1,0:T(8,128)S(1)} %assemble.1.value_ref), channel_id=1, source_target_pairs={{0,33},{1,96},{2,99},{3,34},{4,37},{5,100},{6,103},{7,38},{8,105},... | collective-permute-start | bytes 983048 | tf_op jit(solution)/shard_map/ppermute | solution.py:90
  73.5 5.5 %collective-permute-start.22 = (f32[640,128]{1,0:T(8,128)S(1)}, f32[640,128]{1,0:T(8,128)S(1)}, u32[]{:S(2)}, u32[]{:S(2)}) collective-permute-start(f32[640,128]{1,0:T(8,128)S(1)} %again.1.refs_0_), channel_id=1, source_target_pairs={{0,1},{1,0},{2,3},{3,2},{4,5},{5,4},{6,7},{7,6},{8,9},{9,8},{10,11... | collective-permute-start | bytes 983048 | tf_op jit(solution)/shard_map/ppermute | solution.py:106
  78.9 1.6 %result.5 = (bf16[320,10240]{1,0:T(8,128)(2,1)}, f32[64,10240]{1,0:T(8,128)}) custom-call(bf16[64,384]{1,0:T(8,128)(2,1)S(1)} %get-tuple-element.54.after_ref.solve_ref, bf16[320,64]{1,0:T(8,128)(2,1)S(1)} %get-tuple-element.55.left_ref, bf16[320,10240]{1,0:T(8,128)(2,1)S(1)} %get-tuple-element.38.m_ref, f32[640,128]{1,0:T(8,128)S(1)} %again.1.refs_0_), custom_call_target="tpu_custom_call" | custom-call | flops 8589934592 | bytes 1048576 | tf_op jit(solution)/shard_map/result/pallas_call | solution.py:535
  80.5 0.0 collective-permute-done.22.refs_0_
  80.5 1.6 %result.6 = (bf16[320,10240]{1,0:T(8,128)(2,1)}, f32[64,10240]{1,0:T(8,128)}, f32[8,128]{1,0:T(8,128)S(1)}) custom-call(bf16[64,384]{1,0:T(8,128)(2,1)S(1)} %get-tuple-element.54.after_ref.solve_ref, bf16[320,64]{1,0:T(8,128)(2,1)S(1)} %get-tuple-element.55.left_ref, ...), custom_call_target="tpu_custom_call", output_to_operand_aliasing={{0}: (4, {}), {1}: (5, {})} | custom-call | flops 8589934592 | bytes 1048576 | tf_op jit(solution)/shard_map/result/pallas_call | solution.py:535
  82.1 1.7 %collective-permute-start.26 = (f32[640,128]{1,0:T(8,128)S(1)}, f32[640,128]{1,0:T(8,128)S(1)}, u32[]{:S(2)}, u32[]{:S(2)}) collective-permute-start(f32[640,128]{1,0:T(8,128)S(1)} %tie.3.refs_0_), channel_id=1, source_target_pairs={{0,1},{1,0},{2,3},{3,2},{4,5},{5,4},{6,7},{7,6},{8,9},{9,8},{10,11... | collective-permute-start | bytes 983048 | tf_op jit(solution)/shard_map/ppermute | solution.py:106
  83.8 1.6 %result.7 = (bf16[320,10240]{1,0:T(8,128)(2,1)}, f32[64,10240]{1,0:T(8,128)}, f32[8,128]{1,0:T(8,128)S(1)}) custom-call(bf16[64,384]{1,0:T(8,128)(2,1)S(1)} %get-tuple-element.54.after_ref.solve_ref, bf16[320,64]{1,0:T(8,128)(2,1)S(1)} %get-tuple-element.55.left_ref, ...), custom_call_target="tpu_custom_call", output_to_operand_aliasing={{0}: (4, {}), {1}: (5, {})} | custom-call | flops 8589934592 | bytes 1048576 | tf_op jit(solution)/shard_map/result/pallas_call | solution.py:535
  85.4 0.4 collective-permute-start.25
  85.8 0.0 collective-permute-done.20.value_ref
  85.8 0.1 collective-permute-start.23
  86.0 0.0 collective-permute-done.26.refs_2_
  86.0 2.7 %result.8 = (bf16[320,10240]{1,0:T(8,128)(2,1)}, f32[64,10240]{1,0:T(8,128)}) custom-call(bf16[64,384]{1,0:T(8,128)(2,1)S(1)} %get-tuple-element.54.after_ref.solve_ref, bf16[320,64]{1,0:T(8,128)(2,1)S(1)} %get-tuple-element.55.left_ref, bf16[320,10240]{1,0:T(8,128)(2,1)S(1)} %get-tuple-element.38.m_ref, ...), custom_call_target="tpu_custom_call", output_to_operand_aliasing={{0}: (6, {}), {1}: (7, {})} | custom-call | flops 8589934592 | bytes 1048576 | tf_op jit(solution)/shard_map/result/pallas_call | solution.py:535
  88.7 2.1 %result.9 = (bf16[320,10240]{1,0:T(8,128)(2,1)}, f32[64,10240]{1,0:T(8,128)}, f32[64,320]{1,0:T(8,128)}) custom-call(bf16[64,384]{1,0:T(8,128)(2,1)S(1)} %get-tuple-element.54.after_ref.solve_ref, bf16[320,64]{1,0:T(8,128)(2,1)S(1)} %get-tuple-element.55.left_ref, ...), custom_call_target="tpu_custom_call", output_to_operand_aliasing={{0}: (6, {}), {1}: (7, {})} | custom-call | flops 8589934592 | bytes 1048576 | tf_op jit(solution)/shard_map/result/pallas_call | solution.py:535
  (12 shorter events, 0.1 us)
Async XLA Ops:
  6.8 7.2 %collective-permute-start = (f32[160,128]{1,0:T(8,128)S(1)}, f32[160,128]{1,0:T(8,128)S(1)}, u32[]{:S(2)}, u32[]{:S(2)}) collective-permute-start(f32[160,128]{1,0:T(8,128)S(1)} %get-tuple-element.37), channel_id=1, source_target_pairs={{0,8},{1,25},{2,10},{3,27},{4,12},{5,29},{6,14},{7,31},{8,0},{9,17... | collective-permute-start | bytes 245768 | tf_op jit(solution)/shard_map/ppermute | solution.py:90
  10.2 5.7 %collective-permute-start.1 = (f32[160,128]{1,0:T(8,128)S(1)}, f32[160,128]{1,0:T(8,128)S(1)}, u32[]{:S(2)}, u32[]{:S(2)}) collective-permute-start(f32[160,128]{1,0:T(8,128)S(1)} %get-tuple-element.37), channel_id=1, source_target_pairs={{0,32},{1,97},{2,34},{3,99},{4,36},{5,101},{6,38},{7,103},{8,40},{... | collective-permute-start | bytes 245768 | tf_op jit(solution)/shard_map/ppermute | solution.py:90
  14.0 6.6 %collective-permute-start.2 = (f32[160,128]{1,0:T(8,128)S(1)}, f32[160,128]{1,0:T(8,128)S(1)}, u32[]{:S(2)}, u32[]{:S(2)}) collective-permute-start(f32[160,128]{1,0:T(8,128)S(1)} %get-tuple-element.37), channel_id=1, source_target_pairs={{0,40},{1,121},{2,42},{3,123},{4,44},{5,125},{6,46},{7,127},{8,32}... | collective-permute-start | bytes 245768 | tf_op jit(solution)/shard_map/ppermute | solution.py:90
  20.6 3.7 %collective-permute-start.3 = (f32[160,128]{1,0:T(8,128)S(1)}, f32[160,128]{1,0:T(8,128)S(1)}, u32[]{:S(2)}, u32[]{:S(2)}) collective-permute-start(f32[160,128]{1,0:T(8,128)S(1)} %add_add_fusion.a_ref), channel_id=1, source_target_pairs={{0,24},{1,9},{2,26},{3,11},{4,28},{5,13},{6,30},{7,15},{8,16},{9,1... | collective-permute-start | bytes 245768 | tf_op jit(solution)/shard_map/ppermute | solution.py:90
  20.7 3.7 %collective-permute-start.4 = (f32[160,128]{1,0:T(8,128)S(1)}, f32[160,128]{1,0:T(8,128)S(1)}, u32[]{:S(2)}, u32[]{:S(2)}) collective-permute-start(f32[160,128]{1,0:T(8,128)S(1)} %add_add_fusion.a_ref), channel_id=1, source_target_pairs={{0,96},{1,33},{2,98},{3,35},{4,100},{5,37},{6,102},{7,39},{8,104},... | collective-permute-start | bytes 245768 | tf_op jit(solution)/shard_map/ppermute | solution.py:90
  20.8 4.4 %collective-permute-start.5 = (f32[160,128]{1,0:T(8,128)S(1)}, f32[160,128]{1,0:T(8,128)S(1)}, u32[]{:S(2)}, u32[]{:S(2)}) collective-permute-start(f32[160,128]{1,0:T(8,128)S(1)} %add_add_fusion.a_ref), channel_id=1, source_target_pairs={{0,120},{1,41},{2,122},{3,43},{4,124},{5,45},{6,126},{7,47},{8,112... | collective-permute-start | bytes 245768 | tf_op jit(solution)/shard_map/ppermute | solution.py:90
  25.8 5.8 %collective-permute-start.6 = (f32[680,128]{1,0:T(8,128)S(1)}, f32[680,128]{1,0:T(8,128)S(1)}, u32[]{:S(2)}, u32[]{:S(2)}) collective-permute-start(f32[680,128]{1,0:T(8,128)S(1)} %get-tuple-element.41), channel_id=1, source_target_pairs={{0,1},{1,0},{2,3},{3,2},{4,5},{5,4},{6,7},{7,6},{8,9},{9,8},{10,11... | collective-permute-start | bytes 1044488 | tf_op jit(solution)/shard_map/ppermute | solution.py:106
  31.1 2.6 %collective-permute-start.7 = (f32[1920,128]{1,0:T(8,128)S(1)}, f32[1920,128]{1,0:T(8,128)S(1)}, u32[]{:S(2)}, u32[]{:S(2)}) collective-permute-start(f32[1920,128]{1,0:T(8,128)S(1)} %next_right.3.after_ref), channel_id=1, source_target_pairs={{0,1},{1,0},{2,3},{3,2},{4,5},{5,4},{6,7},{7,6},{8,9},{9,8},{10,11... | collective-permute-start | bytes 2949128 | tf_op jit(solution)/shard_map/ppermute | solution.py:106
  31.8 9.4 %collective-permute-start.10 = (f32[640,128]{1,0:T(8,128)S(1)}, f32[640,128]{1,0:T(8,128)S(1)}, u32[]{:S(2)}, u32[]{:S(2)}) collective-permute-start(f32[640,128]{1,0:T(8,128)S(1)} %get-tuple-element.46), channel_id=1, source_target_pairs={{0,40},{1,121},{2,122},{3,43},{4,44},{5,125},{6,126},{7,47},{8,112... | collective-permute-start | bytes 983048 | tf_op jit(solution)/shard_map/ppermute | solution.py:90
  34.0 9.5 %collective-permute-start.8 = (f32[640,128]{1,0:T(8,128)S(1)}, f32[640,128]{1,0:T(8,128)S(1)}, u32[]{:S(2)}, u32[]{:S(2)}) collective-permute-start(f32[640,128]{1,0:T(8,128)S(1)} %get-tuple-element.44), channel_id=1, source_target_pairs={{0,9},{1,24},{2,27},{3,10},{4,13},{5,28},{6,31},{7,14},{8,17},{9,0... | collective-permute-start | bytes 983048 | tf_op jit(solution)/shard_map/ppermute | solution.py:90
  36.4 8.2 %collective-permute-start.9 = (f32[640,128]{1,0:T(8,128)S(1)}, f32[640,128]{1,0:T(8,128)S(1)}, u32[]{:S(2)}, u32[]{:S(2)}) collective-permute-start(f32[640,128]{1,0:T(8,128)S(1)} %get-tuple-element.45), channel_id=1, source_target_pairs={{0,33},{1,96},{2,99},{3,34},{4,37},{5,100},{6,103},{7,38},{8,105},... | collective-permute-start | bytes 983048 | tf_op jit(solution)/shard_map/ppermute | solution.py:90
  44.7 4.1 %collective-permute-start.11 = (f32[160,128]{1,0:T(8,128)S(1)}, f32[160,128]{1,0:T(8,128)S(1)}, u32[]{:S(2)}, u32[]{:S(2)}) collective-permute-start(f32[160,128]{1,0:T(8,128)S(1)} %get-tuple-element.48), channel_id=1, source_target_pairs={{0,25},{1,8},{2,11},{3,26},{4,29},{5,12},{6,15},{7,30},{8,1},{9,16... | collective-permute-start | bytes 245768 | tf_op jit(solution)/shard_map/ppermute | solution.py:90
  44.8 4.0 %collective-permute-start.12 = (f32[160,128]{1,0:T(8,128)S(1)}, f32[160,128]{1,0:T(8,128)S(1)}, u32[]{:S(2)}, u32[]{:S(2)}) collective-permute-start(f32[160,128]{1,0:T(8,128)S(1)} %get-tuple-element.49), channel_id=1, source_target_pairs={{0,97},{1,32},{2,35},{3,98},{4,101},{5,36},{6,39},{7,102},{8,41},{... | collective-permute-start | bytes 245768 | tf_op jit(solution)/shard_map/ppermute | solution.py:90
  44.8 4.7 %collective-permute-start.13 = (f32[160,128]{1,0:T(8,128)S(1)}, f32[160,128]{1,0:T(8,128)S(1)}, u32[]{:S(2)}, u32[]{:S(2)}) collective-permute-start(f32[160,128]{1,0:T(8,128)S(1)} %get-tuple-element.50), channel_id=1, source_target_pairs={{0,120},{1,41},{2,42},{3,123},{4,124},{5,45},{6,46},{7,127},{8,32}... | collective-permute-start | bytes 245768 | tf_op jit(solution)/shard_map/ppermute | solution.py:90
  49.6 7.9 %collective-permute-start.14 = (f32[200,128]{1,0:T(8,128)S(1)}, f32[200,128]{1,0:T(8,128)S(1)}, u32[]{:S(2)}, u32[]{:S(2)}) collective-permute-start(f32[200,128]{1,0:T(8,128)S(1)} %add_parts.1.a_ref), channel_id=1, source_target_pairs={{0,3},{1,2},{2,5},{3,4},{4,7},{5,6},{6,1},{7,0},{8,11},{9,10},{10,... | collective-permute-start | bytes 307208 | tf_op jit(solution)/shard_map/ppermute | solution.py:101
  53.3 5.0 %collective-permute-start.15 = (f32[200,128]{1,0:T(8,128)S(1)}, f32[200,128]{1,0:T(8,128)S(1)}, u32[]{:S(2)}, u32[]{:S(2)}) collective-permute-start(f32[200,128]{1,0:T(8,128)S(1)} %add_parts.1.a_ref), channel_id=1, source_target_pairs={{0,7},{1,6},{2,1},{3,0},{4,3},{5,2},{6,5},{7,4},{8,15},{9,14},{10,... | collective-permute-start | bytes 307208 | tf_op jit(solution)/shard_map/ppermute | solution.py:101
  54.8 5.3 %collective-permute-start.16 = (f32[200,128]{1,0:T(8,128)S(1)}, f32[200,128]{1,0:T(8,128)S(1)}, u32[]{:S(2)}, u32[]{:S(2)}) collective-permute-start(f32[200,128]{1,0:T(8,128)S(1)} %add_parts.1.a_ref), channel_id=1, source_target_pairs={{0,4},{1,5},{2,6},{3,7},{4,0},{5,1},{6,2},{7,3},{8,12},{9,13},{10,... | collective-permute-start | bytes 307208 | tf_op jit(solution)/shard_map/ppermute | solution.py:101
  60.2 5.1 %collective-permute-start.17 = (f32[160,128]{1,0:T(8,128)S(1)}, f32[160,128]{1,0:T(8,128)S(1)}, u32[]{:S(2)}, u32[]{:S(2)}) collective-permute-start(f32[160,128]{1,0:T(8,128)S(1)} %get-tuple-element.56.a_ref), channel_id=1, source_target_pairs={{0,25},{1,8},{2,11},{3,26},{4,29},{5,12},{6,15},{7,30},{8,1},{9,16... | collective-permute-start | bytes 245768 | tf_op jit(solution)/shard_map/ppermute | solution.py:90
  62.0 3.9 %collective-permute-start.18 = (f32[160,128]{1,0:T(8,128)S(1)}, f32[160,128]{1,0:T(8,128)S(1)}, u32[]{:S(2)}, u32[]{:S(2)}) collective-permute-start(f32[160,128]{1,0:T(8,128)S(1)} %get-tuple-element.56.a_ref), channel_id=1, source_target_pairs={{0,97},{1,32},{2,35},{3,98},{4,101},{5,36},{6,39},{7,102},{8,41},{... | collective-permute-start | bytes 245768 | tf_op jit(solution)/shard_map/ppermute | solution.py:90
  63.2 4.2 %collective-permute-start.19 = (f32[160,128]{1,0:T(8,128)S(1)}, f32[160,128]{1,0:T(8,128)S(1)}, u32[]{:S(2)}, u32[]{:S(2)}) collective-permute-start(f32[160,128]{1,0:T(8,128)S(1)} %get-tuple-element.56.a_ref), channel_id=1, source_target_pairs={{0,120},{1,41},{2,42},{3,123},{4,124},{5,45},{6,46},{7,127},{8,32}... | collective-permute-start | bytes 245768 | tf_op jit(solution)/shard_map/ppermute | solution.py:90
  67.4 14.7 %collective-permute-start.21 = (f32[640,128]{1,0:T(8,128)S(1)}, f32[640,128]{1,0:T(8,128)S(1)}, u32[]{:S(2)}, u32[]{:S(2)}) collective-permute-start(f32[640,128]{1,0:T(8,128)S(1)} %assemble.1.value_ref), channel_id=1, source_target_pairs={{0,40},{1,121},{2,122},{3,43},{4,44},{5,125},{6,126},{7,47},{8,112... | collective-permute-start | bytes 983048 | tf_op jit(solution)/shard_map/ppermute | solution.py:90
  69.2 16.2 %collective-permute-start.24 = (f32[640,128]{1,0:T(8,128)S(1)}, f32[640,128]{1,0:T(8,128)S(1)}, u32[]{:S(2)}, u32[]{:S(2)}) collective-permute-start(f32[640,128]{1,0:T(8,128)S(1)} %assemble.1.value_ref), channel_id=1, source_target_pairs={{0,33},{1,96},{2,99},{3,34},{4,37},{5,100},{6,103},{7,38},{8,105},... | collective-permute-start | bytes 983048 | tf_op jit(solution)/shard_map/ppermute | solution.py:90
  73.5 12.4 %collective-permute-start.20 = (f32[640,128]{1,0:T(8,128)S(1)}, f32[640,128]{1,0:T(8,128)S(1)}, u32[]{:S(2)}, u32[]{:S(2)}) collective-permute-start(f32[640,128]{1,0:T(8,128)S(1)} %assemble.1.value_ref), channel_id=1, source_target_pairs={{0,9},{1,24},{2,27},{3,10},{4,13},{5,28},{6,31},{7,14},{8,17},{9,0... | collective-permute-start | bytes 983048 | tf_op jit(solution)/shard_map/ppermute | solution.py:90
  73.5 7.0 %collective-permute-start.22 = (f32[640,128]{1,0:T(8,128)S(1)}, f32[640,128]{1,0:T(8,128)S(1)}, u32[]{:S(2)}, u32[]{:S(2)}) collective-permute-start(f32[640,128]{1,0:T(8,128)S(1)} %again.1.refs_0_), channel_id=1, source_target_pairs={{0,1},{1,0},{2,3},{3,2},{4,5},{5,4},{6,7},{7,6},{8,9},{9,8},{10,11... | collective-permute-start | bytes 983048 | tf_op jit(solution)/shard_map/ppermute | solution.py:106
  82.1 3.9 %collective-permute-start.26 = (f32[640,128]{1,0:T(8,128)S(1)}, f32[640,128]{1,0:T(8,128)S(1)}, u32[]{:S(2)}, u32[]{:S(2)}) collective-permute-start(f32[640,128]{1,0:T(8,128)S(1)} %tie.3.refs_0_), channel_id=1, source_target_pairs={{0,1},{1,0},{2,3},{3,2},{4,5},{5,4},{6,7},{7,6},{8,9},{9,8},{10,11... | collective-permute-start | bytes 983048 | tf_op jit(solution)/shard_map/ppermute | solution.py:106
  85.4 3.3 %collective-permute-start.25 = (f32[640,128]{1,0:T(8,128)S(1)}, f32[640,128]{1,0:T(8,128)S(1)}, u32[]{:S(2)}, u32[]{:S(2)}) collective-permute-start(f32[640,128]{1,0:T(8,128)S(1)} %tie.5.refs_1_), channel_id=1, source_target_pairs={{0,1},{1,0},{2,3},{3,2},{4,5},{5,4},{6,7},{7,6},{8,9},{9,8},{10,11... | collective-permute-start | bytes 983048 | tf_op jit(solution)/shard_map/ppermute | solution.py:106
  85.8 2.9 %collective-permute-start.23 = (f32[640,128]{1,0:T(8,128)S(1)}, f32[640,128]{1,0:T(8,128)S(1)}, u32[]{:S(2)}, u32[]{:S(2)}) collective-permute-start(f32[640,128]{1,0:T(8,128)S(1)} %tie.4.refs_0_), channel_id=1, source_target_pairs={{0,1},{1,0},{2,3},{3,2},{4,5},{5,4},{6,7},{7,6},{8,9},{9,8},{10,11... | collective-permute-start | bytes 983048 | tf_op jit(solution)/shard_map/ppermute | solution.py:106

commit v17 on v15

--- a/solution.py
+++ b/solution.py
@@ -581,9 +581,10 @@
     out = write(((own, 0),), (total,), None)
     *out, token = write(((other, 0),), (swap(total),), out, token=True)
     two = tie(two, token)
-    *out, token = write(((own, 2),), (two,), out, token=True)
+    out = write(((own, 2),), (two,), out)
+    *out, token = write(((other, 2),), (swap(two),), out, token=True)
     one, three = tie(one, token), tie(three, token)
-    out = write(((own, 1), (own, 3), (other, 2)), (one, three, swap(two)), out)
+    out = write(((own, 1), (own, 3)), (one, three), out)
     new_error, q_new, p_hat = write(
         ((other, 1), (other, 3)), (swap(one), swap(three)), out, p_hat
     )

time: 87.6 us -> 87.4 us (level)
  Pallas kernels: 20.9 us -> 21.9 us
    pallas_call x5 -> x6, Pallas kernels: 9.49 us -> 10.5 us  [result(): pl.pallas_call(functools.partial(result_kernel, sources, more, quarter //...]
  transfers between devices with their start and end apart: 27 -> 27, of which waited for: 14 -> 13; matrix products, arithmetic and copies ran while one was open for 0% -> 0% of each run, Pallas kernels for 13% -> 14%
where the time goes in v17:
time: 87.4 us; the launch traced here: 87.3 us
  starting transfers between devices  40.7 us (47%)
  waiting for transfers between devices  23.7 us (27%)
  Pallas kernels  21.9 us (25%)
  between operations  1.03 us (1%)
    ppermute x21, starting transfers between devices, ring(): out.append(lax.ppermute(value, AXES, pairs))  33.3 us
    ppermute x21, waiting for transfers between devices, ring(): out.append(lax.ppermute(value, AXES, pairs))  23.7 us
    pallas_call x6, Pallas kernels, result(): pl.pallas_call(functools.partial(result_kernel, sources, more, quarter //...  10.5 us
    ppermute x6, starting transfers between devices, swap(): return lax.ppermute(value, 'c', [(0, 1), (1, 0)])  7.37 us
    pallas_call x1, Pallas kernels, merge(): pl.pallas_call(functools.partial(merge_kernel, cuts), out_shape=[pltpu.VM...  6.21 us
    pallas_call x1, Pallas kernels, factor(): pl.pallas_call(functools.partial(factor_kernel, replicas), out_shape=[jax...  2.01 us
    pallas_call x3, Pallas kernels, next_right(): pl.pallas_call(functools.partial(next_right_kernel, own, turns), out_shap...  1.95 us
  transfers between devices with their start and end apart: 27, of which 13 were waited for; matrix products, arithmetic and copies ran while one was open for 0% of the time, Pallas kernels for 14%

profile of v17, /device:TPU:1, one launch (start us, length us, event | category | flops | bytes accessed | tf_op | source)
XLA Modules:
  0.0 87.3 jit_solution(14188141265657186820)
XLA Ops:
  0.6 6.2 %merge.1 = (bf16[320,10240]{1,0:T(8,128)(2,1)S(1)}, f32[160,128]{1,0:T(8,128)S(1)}) custom-call(bf16[320,10240]{1,0:T(8,128)(2,1)} %bitcast.3, bf16[320,10240]{1,0:T(8,128)(2,1)} %bitcast.4, bf16[64,10240]{1,0:T(8,128)(2,1)} %q_hbm.1), custom_call_target="tpu_custom_call" | custom-call | flops 419430400 | bytes 13107200 | tf_op jit(solution)/shard_map/merge/pallas_call | solution.py:139
  6.8 2.5 %collective-permute-start = (f32[160,128]{1,0:T(8,128)S(1)}, f32[160,128]{1,0:T(8,128)S(1)}, u32[]{:S(2)}, u32[]{:S(2)}) collective-permute-start(f32[160,128]{1,0:T(8,128)S(1)} %get-tuple-element.39), channel_id=1, source_target_pairs={{0,8},{1,33},{2,10},{3,35},{4,12},{5,37},{6,14},{7,39},{8,16},{9,4... | collective-permute-start | bytes 245768 | tf_op jit(solution)/shard_map/ppermute | solution.py:78
  9.4 2.2 %collective-permute-start.1 = (f32[160,128]{1,0:T(8,128)S(1)}, f32[160,128]{1,0:T(8,128)S(1)}, u32[]{:S(2)}, u32[]{:S(2)}) collective-permute-start(f32[160,128]{1,0:T(8,128)S(1)} %get-tuple-element.39), channel_id=1, source_target_pairs={{0,24},{1,97},{2,26},{3,99},{4,28},{5,101},{6,30},{7,103},{8,0},{9... | collective-permute-start | bytes 245768 | tf_op jit(solution)/shard_map/ppermute | solution.py:78
  11.6 1.2 %collective-permute-start.2 = (f32[160,128]{1,0:T(8,128)S(1)}, f32[160,128]{1,0:T(8,128)S(1)}, u32[]{:S(2)}, u32[]{:S(2)}) collective-permute-start(f32[160,128]{1,0:T(8,128)S(1)} %get-tuple-element.39), channel_id=1, source_target_pairs={{0,16},{1,65},{2,18},{3,67},{4,20},{5,69},{6,22},{7,71},{8,24},{9,... | collective-permute-start | bytes 245768 | tf_op jit(solution)/shard_map/ppermute | solution.py:78
  12.8 0.8 collective-permute-done
  13.6 0.0 collective-permute-done.1
  13.6 3.1 %collective-permute-done.2 = f32[160,128]{1,0:T(8,128)S(1)} collective-permute-done((f32[160,128]{1,0:T(8,128)S(1)}, f32[160,128]{1,0:T(8,128)S(1)}, u32[]{:S(2)}, u32[]{:S(2)}) %collective-permute-start.2) | collective-permute-done | bytes 81952 | tf_op jit(solution)/shard_map/ppermute | solution.py:78
  16.7 1.0 %collective-permute-start.3 = (f32[160,128]{1,0:T(8,128)S(1)}, f32[160,128]{1,0:T(8,128)S(1)}, u32[]{:S(2)}, u32[]{:S(2)}) collective-permute-start(f32[160,128]{1,0:T(8,128)S(1)} %add_add_fusion.a_ref), channel_id=1, source_target_pairs={{0,32},{1,9},{2,34},{3,11},{4,36},{5,13},{6,38},{7,15},{8,40},{9,1... | collective-permute-start | bytes 245768 | tf_op jit(solution)/shard_map/ppermute | solution.py:78
  17.7 1.8 %collective-permute-start.4 = (f32[160,128]{1,0:T(8,128)S(1)}, f32[160,128]{1,0:T(8,128)S(1)}, u32[]{:S(2)}, u32[]{:S(2)}) collective-permute-start(f32[160,128]{1,0:T(8,128)S(1)} %add_add_fusion.a_ref), channel_id=1, source_target_pairs={{0,96},{1,25},{2,98},{3,27},{4,100},{5,29},{6,102},{7,31},{8,104},... | collective-permute-start | bytes 245768 | tf_op jit(solution)/shard_map/ppermute | solution.py:78
  19.4 1.2 %collective-permute-start.5 = (f32[160,128]{1,0:T(8,128)S(1)}, f32[160,128]{1,0:T(8,128)S(1)}, u32[]{:S(2)}, u32[]{:S(2)}) collective-permute-start(f32[160,128]{1,0:T(8,128)S(1)} %add_add_fusion.a_ref), channel_id=1, source_target_pairs={{0,64},{1,17},{2,66},{3,19},{4,68},{5,21},{6,70},{7,23},{8,72},{9,... | collective-permute-start | bytes 245768 | tf_op jit(solution)/shard_map/ppermute | solution.py:78
  20.7 0.6 collective-permute-done.3.b_ref
  21.3 0.0 collective-permute-done.4.c_ref
  21.3 3.0 %collective-permute-done.5.d_ref = f32[160,128]{1,0:T(8,128)S(1)} collective-permute-done((f32[160,128]{1,0:T(8,128)S(1)}, f32[160,128]{1,0:T(8,128)S(1)}, u32[]{:S(2)}, u32[]{:S(2)}) %collective-permute-start.5) | collective-permute-done | bytes 81952 | tf_op jit(solution)/shard_map/ppermute | solution.py:78
  24.2 0.6 first_right.1
  24.9 3.5 %collective-permute-start.6 = (f32[680,128]{1,0:T(8,128)S(1)}, f32[680,128]{1,0:T(8,128)S(1)}, u32[]{:S(2)}, u32[]{:S(2)}) collective-permute-start(f32[680,128]{1,0:T(8,128)S(1)} %get-tuple-element.43), channel_id=1, source_target_pairs={{0,1},{1,0},{2,3},{3,2},{4,5},{5,4},{6,7},{7,6},{8,9},{9,8},{10,11... | collective-permute-start | bytes 1044488 | tf_op jit(solution)/shard_map/ppermute | solution.py:83
  28.4 0.8 next_right.3.after_ref
  29.2 0.1 collective-permute-start.7
  29.4 0.4 next_right.4.kept_ref
  29.7 0.0 collective-permute-done.6.got_ref
  29.7 0.1 first_pair.1
  29.8 1.6 %collective-permute-start.10 = (f32[640,128]{1,0:T(8,128)S(1)}, f32[640,128]{1,0:T(8,128)S(1)}, u32[]{:S(2)}, u32[]{:S(2)}) collective-permute-start(f32[640,128]{1,0:T(8,128)S(1)} %get-tuple-element.48), channel_id=1, source_target_pairs={{0,16},{1,65},{2,66},{3,19},{4,20},{5,69},{6,70},{7,23},{8,72},{9,... | collective-permute-start | bytes 983048 | tf_op jit(solution)/shard_map/ppermute | solution.py:78
  31.5 0.8 next_right.5.kept_ref
  32.3 0.2 next_pair.1
  32.5 1.4 %collective-permute-start.8 = (f32[640,128]{1,0:T(8,128)S(1)}, f32[640,128]{1,0:T(8,128)S(1)}, u32[]{:S(2)}, u32[]{:S(2)}) collective-permute-start(f32[640,128]{1,0:T(8,128)S(1)} %get-tuple-element.46), channel_id=1, source_target_pairs={{0,9},{1,32},{2,35},{3,10},{4,13},{5,36},{6,39},{7,14},{8,41},{9,1... | collective-permute-start | bytes 983048 | tf_op jit(solution)/shard_map/ppermute | solution.py:78
  33.9 1.6 %collective-permute-start.9 = (f32[640,128]{1,0:T(8,128)S(1)}, f32[640,128]{1,0:T(8,128)S(1)}, u32[]{:S(2)}, u32[]{:S(2)}) collective-permute-start(f32[640,128]{1,0:T(8,128)S(1)} %get-tuple-element.47), channel_id=1, source_target_pairs={{0,25},{1,96},{2,99},{3,26},{4,29},{5,100},{6,103},{7,30},{8,105},... | collective-permute-start | bytes 983048 | tf_op jit(solution)/shard_map/ppermute | solution.py:78
  35.5 2.1 %collective-permute-done.10.d_ref = f32[640,128]{1,0:T(8,128)S(1)} collective-permute-done((f32[640,128]{1,0:T(8,128)S(1)}, f32[640,128]{1,0:T(8,128)S(1)}, u32[]{:S(2)}, u32[]{:S(2)}) %collective-permute-start.10) | collective-permute-done | bytes 327712 | tf_op jit(solution)/shard_map/ppermute | solution.py:78
  37.7 3.5 %collective-permute-done.8.b_ref = f32[640,128]{1,0:T(8,128)S(1)} collective-permute-done((f32[640,128]{1,0:T(8,128)S(1)}, f32[640,128]{1,0:T(8,128)S(1)}, u32[]{:S(2)}, u32[]{:S(2)}) %collective-permute-start.8) | collective-permute-done | bytes 327712 | tf_op jit(solution)/shard_map/ppermute | solution.py:78
  41.2 0.2 collective-permute-done.9.c_ref
  41.4 0.1 add_quarters.1
  41.4 2.4 %collective-permute-start.11 = (f32[200,128]{1,0:T(8,128)S(1)}, f32[200,128]{1,0:T(8,128)S(1)}, u32[]{:S(2)}, u32[]{:S(2)}) collective-permute-start(f32[200,128]{1,0:T(8,128)S(1)} %get-tuple-element.51), channel_id=1, source_target_pairs={{0,33},{1,2},{2,5},{3,34},{4,37},{5,6},{6,1},{7,38},{8,11},{9,40},... | collective-permute-start | bytes 307208 | tf_op jit(solution)/shard_map/ppermute | solution.py:78
  43.8 1.5 %collective-permute-start.12 = (f32[200,128]{1,0:T(8,128)S(1)}, f32[200,128]{1,0:T(8,128)S(1)}, u32[]{:S(2)}, u32[]{:S(2)}) collective-permute-start(f32[200,128]{1,0:T(8,128)S(1)} %get-tuple-element.52), channel_id=1, source_target_pairs={{0,97},{1,6},{2,1},{3,98},{4,101},{5,2},{6,5},{7,102},{8,15},{9,10... | collective-permute-start | bytes 307208 | tf_op jit(solution)/shard_map/ppermute | solution.py:78
  45.4 1.1 %collective-permute-start.13 = (f32[200,128]{1,0:T(8,128)S(1)}, f32[200,128]{1,0:T(8,128)S(1)}, u32[]{:S(2)}, u32[]{:S(2)}) collective-permute-start(f32[200,128]{1,0:T(8,128)S(1)} %get-tuple-element.53), channel_id=1, source_target_pairs={{0,64},{1,5},{2,6},{3,67},{4,68},{5,1},{6,2},{7,71},{8,12},{9,73},... | collective-permute-start | bytes 307208 | tf_op jit(solution)/shard_map/ppermute | solution.py:78
  46.5 1.2 %collective-permute-done.11.b_ref = f32[200,128]{1,0:T(8,128)S(1)} collective-permute-done((f32[200,128]{1,0:T(8,128)S(1)}, f32[200,128]{1,0:T(8,128)S(1)}, u32[]{:S(2)}, u32[]{:S(2)}) %collective-permute-start.11) | collective-permute-done | bytes 102432 | tf_op jit(solution)/shard_map/ppermute | solution.py:78
  47.6 0.3 collective-permute-done.12.c_ref
  47.9 2.7 %collective-permute-done.13.d_ref = f32[200,128]{1,0:T(8,128)S(1)} collective-permute-done((f32[200,128]{1,0:T(8,128)S(1)}, f32[200,128]{1,0:T(8,128)S(1)}, u32[]{:S(2)}, u32[]{:S(2)}) %collective-permute-start.13) | collective-permute-done | bytes 102432 | tf_op jit(solution)/shard_map/ppermute | solution.py:78
  50.7 0.1 across.2.a_ref
  50.7 1.1 %collective-permute-start.14 = (f32[200,128]{1,0:T(8,128)S(1)}, f32[200,128]{1,0:T(8,128)S(1)}, u32[]{:S(2)}, u32[]{:S(2)}) collective-permute-start(f32[200,128]{1,0:T(8,128)S(1)} %across.2.a_ref), channel_id=1, source_target_pairs={{0,3},{1,8},{2,11},{3,4},{4,7},{5,12},{6,15},{7,0},{8,17},{9,10},{... | collective-permute-start | bytes 307208 | tf_op jit(solution)/shard_map/ppermute | solution.py:78
  51.8 2.0 %collective-permute-start.15 = (f32[200,128]{1,0:T(8,128)S(1)}, f32[200,128]{1,0:T(8,128)S(1)}, u32[]{:S(2)}, u32[]{:S(2)}) collective-permute-start(f32[200,128]{1,0:T(8,128)S(1)} %across.2.a_ref), channel_id=1, source_target_pairs={{0,7},{1,24},{2,27},{3,0},{4,3},{5,28},{6,31},{7,4},{8,1},{9,14},{... | collective-permute-start | bytes 307208 | tf_op jit(solution)/shard_map/ppermute | solution.py:78
  53.8 0.5 collective-permute-start.16
  54.3 2.1 %collective-permute-done.14.b_ref = f32[200,128]{1,0:T(8,128)S(1)} collective-permute-done((f32[200,128]{1,0:T(8,128)S(1)}, f32[200,128]{1,0:T(8,128)S(1)}, u32[]{:S(2)}, u32[]{:S(2)}) %collective-permute-start.14) | collective-permute-done | bytes 102432 | tf_op jit(solution)/shard_map/ppermute | solution.py:78
  56.4 2.4 %collective-permute-done.16.d_ref = f32[200,128]{1,0:T(8,128)S(1)} collective-permute-done((f32[200,128]{1,0:T(8,128)S(1)}, f32[200,128]{1,0:T(8,128)S(1)}, u32[]{:S(2)}, u32[]{:S(2)}) %collective-permute-start.16) | collective-permute-done | bytes 102432 | tf_op jit(solution)/shard_map/ppermute | solution.py:78
  58.8 0.1 across.3
  58.9 2.5 %collective-permute-start.17 = (f32[160,128]{1,0:T(8,128)S(1)}, f32[160,128]{1,0:T(8,128)S(1)}, u32[]{:S(2)}, u32[]{:S(2)}) collective-permute-start(f32[160,128]{1,0:T(8,128)S(1)} %get-tuple-element.58.a_ref), channel_id=1, source_target_pairs={{0,33},{1,2},{2,5},{3,34},{4,37},{5,6},{6,1},{7,38},{8,11},{9,40},... | collective-permute-start | bytes 245768 | tf_op jit(solution)/shard_map/ppermute | solution.py:78
  61.4 1.5 %collective-permute-start.18 = (f32[160,128]{1,0:T(8,128)S(1)}, f32[160,128]{1,0:T(8,128)S(1)}, u32[]{:S(2)}, u32[]{:S(2)}) collective-permute-start(f32[160,128]{1,0:T(8,128)S(1)} %get-tuple-element.58.a_ref), channel_id=1, source_target_pairs={{0,97},{1,6},{2,1},{3,98},{4,101},{5,2},{6,5},{7,102},{8,15},{9,10... | collective-permute-start | bytes 245768 | tf_op jit(solution)/shard_map/ppermute | solution.py:78
  62.9 1.1 %collective-permute-start.19 = (f32[160,128]{1,0:T(8,128)S(1)}, f32[160,128]{1,0:T(8,128)S(1)}, u32[]{:S(2)}, u32[]{:S(2)}) collective-permute-start(f32[160,128]{1,0:T(8,128)S(1)} %get-tuple-element.58.a_ref), channel_id=1, source_target_pairs={{0,64},{1,5},{2,6},{3,67},{4,68},{5,1},{6,2},{7,71},{8,12},{9,73},... | collective-permute-start | bytes 245768 | tf_op jit(solution)/shard_map/ppermute | solution.py:78
  64.0 2.0 %factor.1 = (bf16[64,384]{1,0:T(8,128)(2,1)S(1)}, bf16[320,64]{1,0:T(8,128)(2,1)S(1)}, f32[64,320]{1,0:T(8,128)S(1)}) custom-call(f32[40,128]{1,0:T(8,128)S(1)} %get-tuple-element.54.ext_ref, f32[64,320]{1,0:T(8,128)S(1)} %get-tuple-element.55.p_ref), custom_call_target="tpu_custom_call" | custom-call | flops 4294967296 | bytes 1048576 | tf_op jit(solution)/shard_map/factor/pallas_call | solution.py:420
  66.0 0.0 collective-permute-done.18.c_ref
  66.0 1.7 %collective-permute-done.19.d_ref = f32[160,128]{1,0:T(8,128)S(1)} collective-permute-done((f32[160,128]{1,0:T(8,128)S(1)}, f32[160,128]{1,0:T(8,128)S(1)}, u32[]{:S(2)}, u32[]{:S(2)}) %collective-permute-start.19) | collective-permute-done | bytes 81952 | tf_op jit(solution)/shard_map/ppermute | solution.py:78
  67.7 1.6 %collective-permute-start.21 = (f32[640,128]{1,0:T(8,128)S(1)}, f32[640,128]{1,0:T(8,128)S(1)}, u32[]{:S(2)}, u32[]{:S(2)}) collective-permute-start(f32[640,128]{1,0:T(8,128)S(1)} %assemble.1.value_ref), channel_id=1, source_target_pairs={{0,16},{1,65},{2,66},{3,19},{4,20},{5,69},{6,70},{7,23},{8,72},{9,... | collective-permute-start | bytes 983048 | tf_op jit(solution)/shard_map/ppermute | solution.py:78
  69.3 3.5 %collective-permute-start.25 = (f32[640,128]{1,0:T(8,128)S(1)}, f32[640,128]{1,0:T(8,128)S(1)}, u32[]{:S(2)}, u32[]{:S(2)}) collective-permute-start(f32[640,128]{1,0:T(8,128)S(1)} %assemble.1.value_ref), channel_id=1, source_target_pairs={{0,25},{1,96},{2,99},{3,26},{4,29},{5,100},{6,103},{7,30},{8,105},... | collective-permute-start | bytes 983048 | tf_op jit(solution)/shard_map/ppermute | solution.py:78
  72.8 1.2 %collective-permute-start.22 = (f32[640,128]{1,0:T(8,128)S(1)}, f32[640,128]{1,0:T(8,128)S(1)}, u32[]{:S(2)}, u32[]{:S(2)}) collective-permute-start(f32[640,128]{1,0:T(8,128)S(1)} %again.1.refs_0_), channel_id=1, source_target_pairs={{0,1},{1,0},{2,3},{3,2},{4,5},{5,4},{6,7},{7,6},{8,9},{9,8},{10,11... | collective-permute-start | bytes 983048 | tf_op jit(solution)/shard_map/ppermute | solution.py:83
  74.0 1.6 %result.6 = (bf16[320,10240]{1,0:T(8,128)(2,1)}, f32[64,10240]{1,0:T(8,128)}) custom-call(bf16[64,384]{1,0:T(8,128)(2,1)S(1)} %get-tuple-element.56.after_ref.solve_ref, bf16[320,64]{1,0:T(8,128)(2,1)S(1)} %get-tuple-element.57.left_ref, bf16[320,10240]{1,0:T(8,128)(2,1)S(1)} %get-tuple-element.40.m_ref, f32[640,128]{1,0:T(8,128)S(1)} %again.1.refs_0_), custom_call_target="tpu_custom_call" | custom-call | flops 8589934592 | bytes 1048576 | tf_op jit(solution)/shard_map/result/pallas_call | solution.py:500
  75.6 0.0 collective-permute-done.22.refs_0_
  75.6 1.6 %result.7 = (bf16[320,10240]{1,0:T(8,128)(2,1)}, f32[64,10240]{1,0:T(8,128)}, f32[8,128]{1,0:T(8,128)S(1)}) custom-call(bf16[64,384]{1,0:T(8,128)(2,1)S(1)} %get-tuple-element.56.after_ref.solve_ref, bf16[320,64]{1,0:T(8,128)(2,1)S(1)} %get-tuple-element.57.left_ref, ...), custom_call_target="tpu_custom_call", output_to_operand_aliasing={{0}: (4, {}), {1}: (5, {})} | custom-call | flops 8589934592 | bytes 1048576 | tf_op jit(solution)/shard_map/result/pallas_call | solution.py:500
  77.2 0.0 collective-permute-done.21.value_ref
  77.2 1.9 %collective-permute-start.23 = (f32[640,128]{1,0:T(8,128)S(1)}, f32[640,128]{1,0:T(8,128)S(1)}, u32[]{:S(2)}, u32[]{:S(2)}) collective-permute-start(f32[640,128]{1,0:T(8,128)S(1)} %tie.3.refs_0_), channel_id=1, source_target_pairs={{0,1},{1,0},{2,3},{3,2},{4,5},{5,4},{6,7},{7,6},{8,9},{9,8},{10,11... | collective-permute-start | bytes 983048 | tf_op jit(solution)/shard_map/ppermute | solution.py:83
  79.1 1.6 %result.8 = (bf16[320,10240]{1,0:T(8,128)(2,1)}, f32[64,10240]{1,0:T(8,128)}) custom-call(bf16[64,384]{1,0:T(8,128)(2,1)S(1)} %get-tuple-element.56.after_ref.solve_ref, bf16[320,64]{1,0:T(8,128)(2,1)S(1)} %get-tuple-element.57.left_ref, bf16[320,10240]{1,0:T(8,128)(2,1)S(1)} %get-tuple-element.40.m_ref, ...), custom_call_target="tpu_custom_call", output_to_operand_aliasing={{0}: (4, {}), {1}: (5, {})} | custom-call | flops 8589934592 | bytes 1048576 | tf_op jit(solution)/shard_map/result/pallas_call | solution.py:500
  80.7 1.6 %result.9 = (bf16[320,10240]{1,0:T(8,128)(2,1)}, f32[64,10240]{1,0:T(8,128)}, f32[8,128]{1,0:T(8,128)S(1)}) custom-call(bf16[64,384]{1,0:T(8,128)(2,1)S(1)} %get-tuple-element.56.after_ref.solve_ref, bf16[320,64]{1,0:T(8,128)(2,1)S(1)} %get-tuple-element.57.left_ref, ...), custom_call_target="tpu_custom_call", output_to_operand_aliasing={{0}: (4, {}), {1}: (5, {})} | custom-call | flops 8589934592 | bytes 1048576 | tf_op jit(solution)/shard_map/result/pallas_call | solution.py:500
  82.3 0.0 collective-permute-done.25.value_ref
  82.3 0.1 collective-permute-start.26
  82.4 0.5 collective-permute-start.24
  82.9 2.1 %result.10 = (bf16[320,10240]{1,0:T(8,128)(2,1)}, f32[64,10240]{1,0:T(8,128)}) custom-call(bf16[64,384]{1,0:T(8,128)(2,1)S(1)} %get-tuple-element.56.after_ref.solve_ref, bf16[320,64]{1,0:T(8,128)(2,1)S(1)} %get-tuple-element.57.left_ref, bf16[320,10240]{1,0:T(8,128)(2,1)S(1)} %get-tuple-element.40.m_ref, ...), custom_call_target="tpu_custom_call", output_to_operand_aliasing={{0}: (5, {}), {1}: (6, {})} | custom-call | flops 8589934592 | bytes 1048576 | tf_op jit(solution)/shard_map/result/pallas_call | solution.py:500
  85.0 0.0 collective-permute-done.26.refs_1_
  85.0 2.1 %result.11 = (bf16[320,10240]{1,0:T(8,128)(2,1)}, f32[64,10240]{1,0:T(8,128)}, f32[64,320]{1,0:T(8,128)}) custom-call(bf16[64,384]{1,0:T(8,128)(2,1)S(1)} %get-tuple-element.56.after_ref.solve_ref, bf16[320,64]{1,0:T(8,128)(2,1)S(1)} %get-tuple-element.57.left_ref, ...), custom_call_target="tpu_custom_call", output_to_operand_aliasing={{0}: (6, {}), {1}: (7, {})} | custom-call | flops 8589934592 | bytes 1048576 | tf_op jit(solution)/shard_map/result/pallas_call | solution.py:500
  (13 shorter events, 0.1 us)
Async XLA Ops:
  6.8 6.7 %collective-permute-start = (f32[160,128]{1,0:T(8,128)S(1)}, f32[160,128]{1,0:T(8,128)S(1)}, u32[]{:S(2)}, u32[]{:S(2)}) collective-permute-start(f32[160,128]{1,0:T(8,128)S(1)} %get-tuple-element.39), channel_id=1, source_target_pairs={{0,8},{1,33},{2,10},{3,35},{4,12},{5,37},{6,14},{7,39},{8,16},{9,4... | collective-permute-start | bytes 245768 | tf_op jit(solution)/shard_map/ppermute | solution.py:78
  9.4 4.2 %collective-permute-start.1 = (f32[160,128]{1,0:T(8,128)S(1)}, f32[160,128]{1,0:T(8,128)S(1)}, u32[]{:S(2)}, u32[]{:S(2)}) collective-permute-start(f32[160,128]{1,0:T(8,128)S(1)} %get-tuple-element.39), channel_id=1, source_target_pairs={{0,24},{1,97},{2,26},{3,99},{4,28},{5,101},{6,30},{7,103},{8,0},{9... | collective-permute-start | bytes 245768 | tf_op jit(solution)/shard_map/ppermute | solution.py:78
  11.6 5.1 %collective-permute-start.2 = (f32[160,128]{1,0:T(8,128)S(1)}, f32[160,128]{1,0:T(8,128)S(1)}, u32[]{:S(2)}, u32[]{:S(2)}) collective-permute-start(f32[160,128]{1,0:T(8,128)S(1)} %get-tuple-element.39), channel_id=1, source_target_pairs={{0,16},{1,65},{2,18},{3,67},{4,20},{5,69},{6,22},{7,71},{8,24},{9,... | collective-permute-start | bytes 245768 | tf_op jit(solution)/shard_map/ppermute | solution.py:78
  16.7 4.6 %collective-permute-start.3 = (f32[160,128]{1,0:T(8,128)S(1)}, f32[160,128]{1,0:T(8,128)S(1)}, u32[]{:S(2)}, u32[]{:S(2)}) collective-permute-start(f32[160,128]{1,0:T(8,128)S(1)} %add_add_fusion.a_ref), channel_id=1, source_target_pairs={{0,32},{1,9},{2,34},{3,11},{4,36},{5,13},{6,38},{7,15},{8,40},{9,1... | collective-permute-start | bytes 245768 | tf_op jit(solution)/shard_map/ppermute | solution.py:78
  17.7 3.6 %collective-permute-start.4 = (f32[160,128]{1,0:T(8,128)S(1)}, f32[160,128]{1,0:T(8,128)S(1)}, u32[]{:S(2)}, u32[]{:S(2)}) collective-permute-start(f32[160,128]{1,0:T(8,128)S(1)} %add_add_fusion.a_ref), channel_id=1, source_target_pairs={{0,96},{1,25},{2,98},{3,27},{4,100},{5,29},{6,102},{7,31},{8,104},... | collective-permute-start | bytes 245768 | tf_op jit(solution)/shard_map/ppermute | solution.py:78
  19.4 4.8 %collective-permute-start.5 = (f32[160,128]{1,0:T(8,128)S(1)}, f32[160,128]{1,0:T(8,128)S(1)}, u32[]{:S(2)}, u32[]{:S(2)}) collective-permute-start(f32[160,128]{1,0:T(8,128)S(1)} %add_add_fusion.a_ref), channel_id=1, source_target_pairs={{0,64},{1,17},{2,66},{3,19},{4,68},{5,21},{6,70},{7,23},{8,72},{9,... | collective-permute-start | bytes 245768 | tf_op jit(solution)/shard_map/ppermute | solution.py:78
  24.9 4.8 %collective-permute-start.6 = (f32[680,128]{1,0:T(8,128)S(1)}, f32[680,128]{1,0:T(8,128)S(1)}, u32[]{:S(2)}, u32[]{:S(2)}) collective-permute-start(f32[680,128]{1,0:T(8,128)S(1)} %get-tuple-element.43), channel_id=1, source_target_pairs={{0,1},{1,0},{2,3},{3,2},{4,5},{5,4},{6,7},{7,6},{8,9},{9,8},{10,11... | collective-permute-start | bytes 1044488 | tf_op jit(solution)/shard_map/ppermute | solution.py:83
  29.2 3.0 %collective-permute-start.7 = (f32[1920,128]{1,0:T(8,128)S(1)}, f32[1920,128]{1,0:T(8,128)S(1)}, u32[]{:S(2)}, u32[]{:S(2)}) collective-permute-start(f32[1920,128]{1,0:T(8,128)S(1)} %next_right.3.after_ref), channel_id=1, source_target_pairs={{0,1},{1,0},{2,3},{3,2},{4,5},{5,4},{6,7},{7,6},{8,9},{9,8},{10,11... | collective-permute-start | bytes 2949128 | tf_op jit(solution)/shard_map/ppermute | solution.py:83
  29.8 7.8 %collective-permute-start.10 = (f32[640,128]{1,0:T(8,128)S(1)}, f32[640,128]{1,0:T(8,128)S(1)}, u32[]{:S(2)}, u32[]{:S(2)}) collective-permute-start(f32[640,128]{1,0:T(8,128)S(1)} %get-tuple-element.48), channel_id=1, source_target_pairs={{0,16},{1,65},{2,66},{3,19},{4,20},{5,69},{6,70},{7,23},{8,72},{9,... | collective-permute-start | bytes 983048 | tf_op jit(solution)/shard_map/ppermute | solution.py:78
  32.5 8.7 %collective-permute-start.8 = (f32[640,128]{1,0:T(8,128)S(1)}, f32[640,128]{1,0:T(8,128)S(1)}, u32[]{:S(2)}, u32[]{:S(2)}) collective-permute-start(f32[640,128]{1,0:T(8,128)S(1)} %get-tuple-element.46), channel_id=1, source_target_pairs={{0,9},{1,32},{2,35},{3,10},{4,13},{5,36},{6,39},{7,14},{8,41},{9,1... | collective-permute-start | bytes 983048 | tf_op jit(solution)/shard_map/ppermute | solution.py:78
  33.9 7.5 %collective-permute-start.9 = (f32[640,128]{1,0:T(8,128)S(1)}, f32[640,128]{1,0:T(8,128)S(1)}, u32[]{:S(2)}, u32[]{:S(2)}) collective-permute-start(f32[640,128]{1,0:T(8,128)S(1)} %get-tuple-element.47), channel_id=1, source_target_pairs={{0,25},{1,96},{2,99},{3,26},{4,29},{5,100},{6,103},{7,30},{8,105},... | collective-permute-start | bytes 983048 | tf_op jit(solution)/shard_map/ppermute | solution.py:78
  41.4 6.2 %collective-permute-start.11 = (f32[200,128]{1,0:T(8,128)S(1)}, f32[200,128]{1,0:T(8,128)S(1)}, u32[]{:S(2)}, u32[]{:S(2)}) collective-permute-start(f32[200,128]{1,0:T(8,128)S(1)} %get-tuple-element.51), channel_id=1, source_target_pairs={{0,33},{1,2},{2,5},{3,34},{4,37},{5,6},{6,1},{7,38},{8,11},{9,40},... | collective-permute-start | bytes 307208 | tf_op jit(solution)/shard_map/ppermute | solution.py:78
  43.8 4.1 %collective-permute-start.12 = (f32[200,128]{1,0:T(8,128)S(1)}, f32[200,128]{1,0:T(8,128)S(1)}, u32[]{:S(2)}, u32[]{:S(2)}) collective-permute-start(f32[200,128]{1,0:T(8,128)S(1)} %get-tuple-element.52), channel_id=1, source_target_pairs={{0,97},{1,6},{2,1},{3,98},{4,101},{5,2},{6,5},{7,102},{8,15},{9,10... | collective-permute-start | bytes 307208 | tf_op jit(solution)/shard_map/ppermute | solution.py:78
  45.4 5.3 %collective-permute-start.13 = (f32[200,128]{1,0:T(8,128)S(1)}, f32[200,128]{1,0:T(8,128)S(1)}, u32[]{:S(2)}, u32[]{:S(2)}) collective-permute-start(f32[200,128]{1,0:T(8,128)S(1)} %get-tuple-element.53), channel_id=1, source_target_pairs={{0,64},{1,5},{2,6},{3,67},{4,68},{5,1},{6,2},{7,71},{8,12},{9,73},... | collective-permute-start | bytes 307208 | tf_op jit(solution)/shard_map/ppermute | solution.py:78
  50.7 5.7 %collective-permute-start.14 = (f32[200,128]{1,0:T(8,128)S(1)}, f32[200,128]{1,0:T(8,128)S(1)}, u32[]{:S(2)}, u32[]{:S(2)}) collective-permute-start(f32[200,128]{1,0:T(8,128)S(1)} %across.2.a_ref), channel_id=1, source_target_pairs={{0,3},{1,8},{2,11},{3,4},{4,7},{5,12},{6,15},{7,0},{8,17},{9,10},{... | collective-permute-start | bytes 307208 | tf_op jit(solution)/shard_map/ppermute | solution.py:78
  51.8 4.6 %collective-permute-start.15 = (f32[200,128]{1,0:T(8,128)S(1)}, f32[200,128]{1,0:T(8,128)S(1)}, u32[]{:S(2)}, u32[]{:S(2)}) collective-permute-start(f32[200,128]{1,0:T(8,128)S(1)} %across.2.a_ref), channel_id=1, source_target_pairs={{0,7},{1,24},{2,27},{3,0},{4,3},{5,28},{6,31},{7,4},{8,1},{9,14},{... | collective-permute-start | bytes 307208 | tf_op jit(solution)/shard_map/ppermute | solution.py:78
  53.8 5.0 %collective-permute-start.16 = (f32[200,128]{1,0:T(8,128)S(1)}, f32[200,128]{1,0:T(8,128)S(1)}, u32[]{:S(2)}, u32[]{:S(2)}) collective-permute-start(f32[200,128]{1,0:T(8,128)S(1)} %across.2.a_ref), channel_id=1, source_target_pairs={{0,4},{1,17},{2,18},{3,7},{4,0},{5,21},{6,22},{7,3},{8,24},{9,13},... | collective-permute-start | bytes 307208 | tf_op jit(solution)/shard_map/ppermute | solution.py:78
  58.9 7.1 %collective-permute-start.17 = (f32[160,128]{1,0:T(8,128)S(1)}, f32[160,128]{1,0:T(8,128)S(1)}, u32[]{:S(2)}, u32[]{:S(2)}) collective-permute-start(f32[160,128]{1,0:T(8,128)S(1)} %get-tuple-element.58.a_ref), channel_id=1, source_target_pairs={{0,33},{1,2},{2,5},{3,34},{4,37},{5,6},{6,1},{7,38},{8,11},{9,40},... | collective-permute-start | bytes 245768 | tf_op jit(solution)/shard_map/ppermute | solution.py:78
  61.4 4.7 %collective-permute-start.18 = (f32[160,128]{1,0:T(8,128)S(1)}, f32[160,128]{1,0:T(8,128)S(1)}, u32[]{:S(2)}, u32[]{:S(2)}) collective-permute-start(f32[160,128]{1,0:T(8,128)S(1)} %get-tuple-element.58.a_ref), channel_id=1, source_target_pairs={{0,97},{1,6},{2,1},{3,98},{4,101},{5,2},{6,5},{7,102},{8,15},{9,10... | collective-permute-start | bytes 245768 | tf_op jit(solution)/shard_map/ppermute | solution.py:78
  62.9 4.8 %collective-permute-start.19 = (f32[160,128]{1,0:T(8,128)S(1)}, f32[160,128]{1,0:T(8,128)S(1)}, u32[]{:S(2)}, u32[]{:S(2)}) collective-permute-start(f32[160,128]{1,0:T(8,128)S(1)} %get-tuple-element.58.a_ref), channel_id=1, source_target_pairs={{0,64},{1,5},{2,6},{3,67},{4,68},{5,1},{6,2},{7,71},{8,12},{9,73},... | collective-permute-start | bytes 245768 | tf_op jit(solution)/shard_map/ppermute | solution.py:78
  67.7 9.4 %collective-permute-start.21 = (f32[640,128]{1,0:T(8,128)S(1)}, f32[640,128]{1,0:T(8,128)S(1)}, u32[]{:S(2)}, u32[]{:S(2)}) collective-permute-start(f32[640,128]{1,0:T(8,128)S(1)} %assemble.1.value_ref), channel_id=1, source_target_pairs={{0,16},{1,65},{2,66},{3,19},{4,20},{5,69},{6,70},{7,23},{8,72},{9,... | collective-permute-start | bytes 983048 | tf_op jit(solution)/shard_map/ppermute | solution.py:78
  69.3 12.9 %collective-permute-start.25 = (f32[640,128]{1,0:T(8,128)S(1)}, f32[640,128]{1,0:T(8,128)S(1)}, u32[]{:S(2)}, u32[]{:S(2)}) collective-permute-start(f32[640,128]{1,0:T(8,128)S(1)} %assemble.1.value_ref), channel_id=1, source_target_pairs={{0,25},{1,96},{2,99},{3,26},{4,29},{5,100},{6,103},{7,30},{8,105},... | collective-permute-start | bytes 983048 | tf_op jit(solution)/shard_map/ppermute | solution.py:78
  72.8 9.6 %collective-permute-start.20 = (f32[640,128]{1,0:T(8,128)S(1)}, f32[640,128]{1,0:T(8,128)S(1)}, u32[]{:S(2)}, u32[]{:S(2)}) collective-permute-start(f32[640,128]{1,0:T(8,128)S(1)} %assemble.1.value_ref), channel_id=1, source_target_pairs={{0,9},{1,32},{2,35},{3,10},{4,13},{5,36},{6,39},{7,14},{8,41},{9,1... | collective-permute-start | bytes 983048 | tf_op jit(solution)/shard_map/ppermute | solution.py:78
  72.8 2.7 %collective-permute-start.22 = (f32[640,128]{1,0:T(8,128)S(1)}, f32[640,128]{1,0:T(8,128)S(1)}, u32[]{:S(2)}, u32[]{:S(2)}) collective-permute-start(f32[640,128]{1,0:T(8,128)S(1)} %again.1.refs_0_), channel_id=1, source_target_pairs={{0,1},{1,0},{2,3},{3,2},{4,5},{5,4},{6,7},{7,6},{8,9},{9,8},{10,11... | collective-permute-start | bytes 983048 | tf_op jit(solution)/shard_map/ppermute | solution.py:83
  77.2 3.5 %collective-permute-start.23 = (f32[640,128]{1,0:T(8,128)S(1)}, f32[640,128]{1,0:T(8,128)S(1)}, u32[]{:S(2)}, u32[]{:S(2)}) collective-permute-start(f32[640,128]{1,0:T(8,128)S(1)} %tie.3.refs_0_), channel_id=1, source_target_pairs={{0,1},{1,0},{2,3},{3,2},{4,5},{5,4},{6,7},{7,6},{8,9},{9,8},{10,11... | collective-permute-start | bytes 983048 | tf_op jit(solution)/shard_map/ppermute | solution.py:83
  82.3 2.7 %collective-permute-start.26 = (f32[640,128]{1,0:T(8,128)S(1)}, f32[640,128]{1,0:T(8,128)S(1)}, u32[]{:S(2)}, u32[]{:S(2)}) collective-permute-start(f32[640,128]{1,0:T(8,128)S(1)} %tie.5.refs_1_), channel_id=1, source_target_pairs={{0,1},{1,0},{2,3},{3,2},{4,5},{5,4},{6,7},{7,6},{8,9},{9,8},{10,11... | collective-permute-start | bytes 983048 | tf_op jit(solution)/shard_map/ppermute | solution.py:83
  82.4 2.6 %collective-permute-start.24 = (f32[640,128]{1,0:T(8,128)S(1)}, f32[640,128]{1,0:T(8,128)S(1)}, u32[]{:S(2)}, u32[]{:S(2)}) collective-permute-start(f32[640,128]{1,0:T(8,128)S(1)} %tie.4.refs_0_), channel_id=1, source_target_pairs={{0,1},{1,0},{2,3},{3,2},{4,5},{5,4},{6,7},{7,6},{8,9},{9,8},{10,11... | collective-permute-start | bytes 983048 | tf_op jit(solution)/shard_map/ppermute | solution.py:83

commit v18 on v17

--- a/solution.py
+++ b/solution.py
@@ -32,7 +32,7 @@
 
 
 def half_of(x, y, z, c):
-    return (x + y + z + c) % 2
+    return c
 
 
 def core_of(x, y, z, c):
@@ -73,7 +73,7 @@
             to = {"z": z, "x": x, "y": y}
             axis = orders[group(x, y, z, c)][phase]
             to[axis] = (to[axis] + k) % SIZES[AXES.index(axis)]
-            core = c if group is core_of else (c + k) % 2
+            core = c
             pairs.append((index(z, x, y, c), index(*to.values(), core)))
         out.append(lax.ppermute(value, AXES, pairs))
     return out

time: 87.4 us -> 89.4 us (1.023)
  starting transfers between devices: 40.7 us -> 42.4 us
    ppermute x6, starting transfers between devices: 7.37 us -> 14.3 us  [swap(): return lax.ppermute(value, 'c', [(0, 1), (1, 0)])]
    ppermute x21, starting transfers between devices: 33.3 us -> 28.1 us  [ring(): out.append(lax.ppermute(value, AXES, pairs))]
where the time goes in v18:
time: 89.4 us; the launch traced here: 89.3 us
  starting transfers between devices  42.4 us (47%)
  waiting for transfers between devices  23.9 us (27%)
  Pallas kernels  21.9 us (24%)
  between operations  1.04 us (1%)
    ppermute x21, starting transfers between devices, ring(): out.append(lax.ppermute(value, AXES, pairs))  28.1 us
    ppermute x21, waiting for transfers between devices, ring(): out.append(lax.ppermute(value, AXES, pairs))  23.9 us
    ppermute x6, starting transfers between devices, swap(): return lax.ppermute(value, 'c', [(0, 1), (1, 0)])  14.3 us
    pallas_call x6, Pallas kernels, result(): pl.pallas_call(functools.partial(result_kernel, sources, more, quarter //...  10.5 us
    pallas_call x1, Pallas kernels, merge(): pl.pallas_call(functools.partial(merge_kernel, cuts), out_shape=[pltpu.VM...  6.21 us
    pallas_call x1, Pallas kernels, factor(): pl.pallas_call(functools.partial(factor_kernel, replicas), out_shape=[jax...  2.01 us
    pallas_call x3, Pallas kernels, next_right(): pl.pallas_call(functools.partial(next_right_kernel, own, turns), out_shap...  1.95 us
  transfers between devices with their start and end apart: 27, of which 13 were waited for; matrix products, arithmetic and copies ran while one was open for 0% of the time, Pallas kernels for 14%

profile of v18, /device:TPU:1, one launch (start us, length us, event | category | flops | bytes accessed | tf_op | source)
XLA Modules:
  0.0 89.3 jit_solution(13571270775226183409)
XLA Ops:
  0.6 6.2 %merge.1 = (bf16[320,10240]{1,0:T(8,128)(2,1)S(1)}, f32[160,128]{1,0:T(8,128)S(1)}) custom-call(bf16[320,10240]{1,0:T(8,128)(2,1)} %bitcast.3, bf16[320,10240]{1,0:T(8,128)(2,1)} %bitcast.4, bf16[64,10240]{1,0:T(8,128)(2,1)} %q_hbm.1), custom_call_target="tpu_custom_call" | custom-call | flops 419430400 | bytes 13107200 | tf_op jit(solution)/shard_map/merge/pallas_call | solution.py:139
  6.8 2.5 %collective-permute-start = (f32[160,128]{1,0:T(8,128)S(1)}, f32[160,128]{1,0:T(8,128)S(1)}, u32[]{:S(2)}, u32[]{:S(2)}) collective-permute-start(f32[160,128]{1,0:T(8,128)S(1)} %get-tuple-element.39), channel_id=1, source_target_pairs={{0,8},{1,33},{2,10},{3,35},{4,12},{5,37},{6,14},{7,39},{8,16},{9,4... | collective-permute-start | bytes 245768 | tf_op jit(solution)/shard_map/ppermute | solution.py:78
  9.4 2.2 %collective-permute-start.1 = (f32[160,128]{1,0:T(8,128)S(1)}, f32[160,128]{1,0:T(8,128)S(1)}, u32[]{:S(2)}, u32[]{:S(2)}) collective-permute-start(f32[160,128]{1,0:T(8,128)S(1)} %get-tuple-element.39), channel_id=1, source_target_pairs={{0,24},{1,97},{2,26},{3,99},{4,28},{5,101},{6,30},{7,103},{8,0},{9... | collective-permute-start | bytes 245768 | tf_op jit(solution)/shard_map/ppermute | solution.py:78
  11.6 1.2 %collective-permute-start.2 = (f32[160,128]{1,0:T(8,128)S(1)}, f32[160,128]{1,0:T(8,128)S(1)}, u32[]{:S(2)}, u32[]{:S(2)}) collective-permute-start(f32[160,128]{1,0:T(8,128)S(1)} %get-tuple-element.39), channel_id=1, source_target_pairs={{0,16},{1,65},{2,18},{3,67},{4,20},{5,69},{6,22},{7,71},{8,24},{9,... | collective-permute-start | bytes 245768 | tf_op jit(solution)/shard_map/ppermute | solution.py:78
  12.8 0.8 collective-permute-done
  13.6 3.1 %collective-permute-done.2 = f32[160,128]{1,0:T(8,128)S(1)} collective-permute-done((f32[160,128]{1,0:T(8,128)S(1)}, f32[160,128]{1,0:T(8,128)S(1)}, u32[]{:S(2)}, u32[]{:S(2)}) %collective-permute-start.2) | collective-permute-done | bytes 81952 | tf_op jit(solution)/shard_map/ppermute | solution.py:78
  16.7 1.0 %collective-permute-start.3 = (f32[160,128]{1,0:T(8,128)S(1)}, f32[160,128]{1,0:T(8,128)S(1)}, u32[]{:S(2)}, u32[]{:S(2)}) collective-permute-start(f32[160,128]{1,0:T(8,128)S(1)} %add_add_fusion.a_ref), channel_id=1, source_target_pairs={{0,32},{1,9},{2,34},{3,11},{4,36},{5,13},{6,38},{7,15},{8,40},{9,1... | collective-permute-start | bytes 245768 | tf_op jit(solution)/shard_map/ppermute | solution.py:78
  17.7 1.8 %collective-permute-start.4 = (f32[160,128]{1,0:T(8,128)S(1)}, f32[160,128]{1,0:T(8,128)S(1)}, u32[]{:S(2)}, u32[]{:S(2)}) collective-permute-start(f32[160,128]{1,0:T(8,128)S(1)} %add_add_fusion.a_ref), channel_id=1, source_target_pairs={{0,96},{1,25},{2,98},{3,27},{4,100},{5,29},{6,102},{7,31},{8,104},... | collective-permute-start | bytes 245768 | tf_op jit(solution)/shard_map/ppermute | solution.py:78
  19.4 1.2 %collective-permute-start.5 = (f32[160,128]{1,0:T(8,128)S(1)}, f32[160,128]{1,0:T(8,128)S(1)}, u32[]{:S(2)}, u32[]{:S(2)}) collective-permute-start(f32[160,128]{1,0:T(8,128)S(1)} %add_add_fusion.a_ref), channel_id=1, source_target_pairs={{0,64},{1,17},{2,66},{3,19},{4,68},{5,21},{6,70},{7,23},{8,72},{9,... | collective-permute-start | bytes 245768 | tf_op jit(solution)/shard_map/ppermute | solution.py:78
  20.7 0.6 collective-permute-done.3.b_ref
  21.3 0.0 collective-permute-done.4.c_ref
  21.3 3.0 %collective-permute-done.5.d_ref = f32[160,128]{1,0:T(8,128)S(1)} collective-permute-done((f32[160,128]{1,0:T(8,128)S(1)}, f32[160,128]{1,0:T(8,128)S(1)}, u32[]{:S(2)}, u32[]{:S(2)}) %collective-permute-start.5) | collective-permute-done | bytes 81952 | tf_op jit(solution)/shard_map/ppermute | solution.py:78
  24.2 0.6 first_right.1
  24.9 3.5 %collective-permute-start.6 = (f32[680,128]{1,0:T(8,128)S(1)}, f32[680,128]{1,0:T(8,128)S(1)}, u32[]{:S(2)}, u32[]{:S(2)}) collective-permute-start(f32[680,128]{1,0:T(8,128)S(1)} %get-tuple-element.43), channel_id=1, source_target_pairs={{0,1},{1,0},{2,3},{3,2},{4,5},{5,4},{6,7},{7,6},{8,9},{9,8},{10,11... | collective-permute-start | bytes 1044488 | tf_op jit(solution)/shard_map/ppermute | solution.py:83
  28.4 0.8 next_right.3.after_ref
  29.2 0.1 collective-permute-start.7
  29.3 0.4 next_right.4.kept_ref
  29.7 0.1 first_pair.1
  29.8 1.6 %collective-permute-start.10 = (f32[640,128]{1,0:T(8,128)S(1)}, f32[640,128]{1,0:T(8,128)S(1)}, u32[]{:S(2)}, u32[]{:S(2)}) collective-permute-start(f32[640,128]{1,0:T(8,128)S(1)} %get-tuple-element.48), channel_id=1, source_target_pairs={{0,16},{1,65},{2,18},{3,67},{4,20},{5,69},{6,22},{7,71},{8,24},{9,... | collective-permute-start | bytes 983048 | tf_op jit(solution)/shard_map/ppermute | solution.py:78
  31.4 0.8 next_right.5.kept_ref
  32.2 0.2 next_pair.1
  32.5 0.8 collective-permute-start.8
  33.3 1.9 %collective-permute-start.9 = (f32[640,128]{1,0:T(8,128)S(1)}, f32[640,128]{1,0:T(8,128)S(1)}, u32[]{:S(2)}, u32[]{:S(2)}) collective-permute-start(f32[640,128]{1,0:T(8,128)S(1)} %get-tuple-element.47), channel_id=1, source_target_pairs={{0,24},{1,97},{2,26},{3,99},{4,28},{5,101},{6,30},{7,103},{8,0},{9... | collective-permute-start | bytes 983048 | tf_op jit(solution)/shard_map/ppermute | solution.py:78
  35.2 2.4 %collective-permute-done.10.d_ref = f32[640,128]{1,0:T(8,128)S(1)} collective-permute-done((f32[640,128]{1,0:T(8,128)S(1)}, f32[640,128]{1,0:T(8,128)S(1)}, u32[]{:S(2)}, u32[]{:S(2)}) %collective-permute-start.10) | collective-permute-done | bytes 327712 | tf_op jit(solution)/shard_map/ppermute | solution.py:78
  37.6 3.5 %collective-permute-done.8.b_ref = f32[640,128]{1,0:T(8,128)S(1)} collective-permute-done((f32[640,128]{1,0:T(8,128)S(1)}, f32[640,128]{1,0:T(8,128)S(1)}, u32[]{:S(2)}, u32[]{:S(2)}) %collective-permute-start.8) | collective-permute-done | bytes 327712 | tf_op jit(solution)/shard_map/ppermute | solution.py:78
  41.2 0.1 add_quarters.1
  41.2 1.4 %collective-permute-start.11 = (f32[200,128]{1,0:T(8,128)S(1)}, f32[200,128]{1,0:T(8,128)S(1)}, u32[]{:S(2)}, u32[]{:S(2)}) collective-permute-start(f32[200,128]{1,0:T(8,128)S(1)} %get-tuple-element.51), channel_id=1, source_target_pairs={{0,32},{1,3},{2,34},{3,5},{4,36},{5,7},{6,38},{7,1},{8,40},{9,11},... | collective-permute-start | bytes 307208 | tf_op jit(solution)/shard_map/ppermute | solution.py:78
  42.6 1.5 %collective-permute-start.12 = (f32[200,128]{1,0:T(8,128)S(1)}, f32[200,128]{1,0:T(8,128)S(1)}, u32[]{:S(2)}, u32[]{:S(2)}) collective-permute-start(f32[200,128]{1,0:T(8,128)S(1)} %get-tuple-element.52), channel_id=1, source_target_pairs={{0,96},{1,7},{2,98},{3,1},{4,100},{5,3},{6,102},{7,5},{8,104},{9,1... | collective-permute-start | bytes 307208 | tf_op jit(solution)/shard_map/ppermute | solution.py:78
  44.1 1.6 %collective-permute-start.13 = (f32[200,128]{1,0:T(8,128)S(1)}, f32[200,128]{1,0:T(8,128)S(1)}, u32[]{:S(2)}, u32[]{:S(2)}) collective-permute-start(f32[200,128]{1,0:T(8,128)S(1)} %get-tuple-element.53), channel_id=1, source_target_pairs={{0,64},{1,5},{2,66},{3,7},{4,68},{5,1},{6,70},{7,3},{8,72},{9,13},... | collective-permute-start | bytes 307208 | tf_op jit(solution)/shard_map/ppermute | solution.py:78
  45.7 0.4 collective-permute-done.11.b_ref
  46.1 0.3 collective-permute-done.12.c_ref
  46.4 2.7 %collective-permute-done.13.d_ref = f32[200,128]{1,0:T(8,128)S(1)} collective-permute-done((f32[200,128]{1,0:T(8,128)S(1)}, f32[200,128]{1,0:T(8,128)S(1)}, u32[]{:S(2)}, u32[]{:S(2)}) %collective-permute-start.13) | collective-permute-done | bytes 102432 | tf_op jit(solution)/shard_map/ppermute | solution.py:78
  49.2 0.1 across.2.a_ref
  49.2 0.1 collective-permute-start.14
  49.3 2.7 %collective-permute-start.15 = (f32[200,128]{1,0:T(8,128)S(1)}, f32[200,128]{1,0:T(8,128)S(1)}, u32[]{:S(2)}, u32[]{:S(2)}) collective-permute-start(f32[200,128]{1,0:T(8,128)S(1)} %across.2.a_ref), channel_id=1, source_target_pairs={{0,6},{1,25},{2,0},{3,27},{4,2},{5,29},{6,4},{7,31},{8,14},{9,1},{... | collective-permute-start | bytes 307208 | tf_op jit(solution)/shard_map/ppermute | solution.py:78
  52.0 0.0 collective-permute-start.16
  52.0 2.0 %collective-permute-done.14.b_ref = f32[200,128]{1,0:T(8,128)S(1)} collective-permute-done((f32[200,128]{1,0:T(8,128)S(1)}, f32[200,128]{1,0:T(8,128)S(1)}, u32[]{:S(2)}, u32[]{:S(2)}) %collective-permute-start.14) | collective-permute-done | bytes 102432 | tf_op jit(solution)/shard_map/ppermute | solution.py:78
  54.0 0.7 collective-permute-done.15.c_ref
  54.7 2.3 %collective-permute-done.16.d_ref = f32[200,128]{1,0:T(8,128)S(1)} collective-permute-done((f32[200,128]{1,0:T(8,128)S(1)}, f32[200,128]{1,0:T(8,128)S(1)}, u32[]{:S(2)}, u32[]{:S(2)}) %collective-permute-start.16) | collective-permute-done | bytes 102432 | tf_op jit(solution)/shard_map/ppermute | solution.py:78
  57.0 0.1 across.3
  57.1 0.5 collective-permute-start.17
  57.6 2.4 %collective-permute-start.18 = (f32[160,128]{1,0:T(8,128)S(1)}, f32[160,128]{1,0:T(8,128)S(1)}, u32[]{:S(2)}, u32[]{:S(2)}) collective-permute-start(f32[160,128]{1,0:T(8,128)S(1)} %get-tuple-element.58.a_ref), channel_id=1, source_target_pairs={{0,96},{1,7},{2,98},{3,1},{4,100},{5,3},{6,102},{7,5},{8,104},{9,1... | collective-permute-start | bytes 245768 | tf_op jit(solution)/shard_map/ppermute | solution.py:78
  60.0 0.6 collective-permute-start.19
  60.6 2.0 %factor.1 = (bf16[64,384]{1,0:T(8,128)(2,1)S(1)}, bf16[320,64]{1,0:T(8,128)(2,1)S(1)}, f32[64,320]{1,0:T(8,128)S(1)}) custom-call(f32[40,128]{1,0:T(8,128)S(1)} %get-tuple-element.54.ext_ref, f32[64,320]{1,0:T(8,128)S(1)} %get-tuple-element.55.p_ref), custom_call_target="tpu_custom_call" | custom-call | flops 4294967296 | bytes 1048576 | tf_op jit(solution)/shard_map/factor/pallas_call | solution.py:420
  62.7 0.0 collective-permute-done.17.b_ref
  62.7 2.1 %collective-permute-done.19.d_ref = f32[160,128]{1,0:T(8,128)S(1)} collective-permute-done((f32[160,128]{1,0:T(8,128)S(1)}, f32[160,128]{1,0:T(8,128)S(1)}, u32[]{:S(2)}, u32[]{:S(2)}) %collective-permute-start.19) | collective-permute-done | bytes 81952 | tf_op jit(solution)/shard_map/ppermute | solution.py:78
  64.9 1.6 %collective-permute-start.21 = (f32[640,128]{1,0:T(8,128)S(1)}, f32[640,128]{1,0:T(8,128)S(1)}, u32[]{:S(2)}, u32[]{:S(2)}) collective-permute-start(f32[640,128]{1,0:T(8,128)S(1)} %assemble.1.value_ref), channel_id=1, source_target_pairs={{0,16},{1,65},{2,18},{3,67},{4,20},{5,69},{6,22},{7,71},{8,24},{9,... | collective-permute-start | bytes 983048 | tf_op jit(solution)/shard_map/ppermute | solution.py:78
  66.5 0.9 %collective-permute-start.25 = (f32[640,128]{1,0:T(8,128)S(1)}, f32[640,128]{1,0:T(8,128)S(1)}, u32[]{:S(2)}, u32[]{:S(2)}) collective-permute-start(f32[640,128]{1,0:T(8,128)S(1)} %assemble.1.value_ref), channel_id=1, source_target_pairs={{0,24},{1,97},{2,26},{3,99},{4,28},{5,101},{6,30},{7,103},{8,0},{9... | collective-permute-start | bytes 983048 | tf_op jit(solution)/shard_map/ppermute | solution.py:78
  67.4 0.5 collective-permute-start.20
  67.9 8.6 %collective-permute-start.22 = (f32[640,128]{1,0:T(8,128)S(1)}, f32[640,128]{1,0:T(8,128)S(1)}, u32[]{:S(2)}, u32[]{:S(2)}) collective-permute-start(f32[640,128]{1,0:T(8,128)S(1)} %again.1.refs_0_), channel_id=1, source_target_pairs={{0,1},{1,0},{2,3},{3,2},{4,5},{5,4},{6,7},{7,6},{8,9},{9,8},{10,11... | collective-permute-start | bytes 983048 | tf_op jit(solution)/shard_map/ppermute | solution.py:83
  76.5 1.6 %result.6 = (bf16[320,10240]{1,0:T(8,128)(2,1)}, f32[64,10240]{1,0:T(8,128)}) custom-call(bf16[64,384]{1,0:T(8,128)(2,1)S(1)} %get-tuple-element.56.after_ref.solve_ref, bf16[320,64]{1,0:T(8,128)(2,1)S(1)} %get-tuple-element.57.left_ref, bf16[320,10240]{1,0:T(8,128)(2,1)S(1)} %get-tuple-element.40.m_ref, f32[640,128]{1,0:T(8,128)S(1)} %again.1.refs_0_), custom_call_target="tpu_custom_call" | custom-call | flops 8589934592 | bytes 1048576 | tf_op jit(solution)/shard_map/result/pallas_call | solution.py:500
  78.1 0.0 collective-permute-done.22.refs_0_
  78.1 1.6 %result.7 = (bf16[320,10240]{1,0:T(8,128)(2,1)}, f32[64,10240]{1,0:T(8,128)}, f32[8,128]{1,0:T(8,128)S(1)}) custom-call(bf16[64,384]{1,0:T(8,128)(2,1)S(1)} %get-tuple-element.56.after_ref.solve_ref, bf16[320,64]{1,0:T(8,128)(2,1)S(1)} %get-tuple-element.57.left_ref, ...), custom_call_target="tpu_custom_call", output_to_operand_aliasing={{0}: (4, {}), {1}: (5, {})} | custom-call | flops 8589934592 | bytes 1048576 | tf_op jit(solution)/shard_map/result/pallas_call | solution.py:500
  79.7 0.0 collective-permute-done.21.value_ref
  79.7 1.1 %collective-permute-start.23 = (f32[640,128]{1,0:T(8,128)S(1)}, f32[640,128]{1,0:T(8,128)S(1)}, u32[]{:S(2)}, u32[]{:S(2)}) collective-permute-start(f32[640,128]{1,0:T(8,128)S(1)} %tie.3.refs_0_), channel_id=1, source_target_pairs={{0,1},{1,0},{2,3},{3,2},{4,5},{5,4},{6,7},{7,6},{8,9},{9,8},{10,11... | collective-permute-start | bytes 983048 | tf_op jit(solution)/shard_map/ppermute | solution.py:83
  80.8 1.6 %result.8 = (bf16[320,10240]{1,0:T(8,128)(2,1)}, f32[64,10240]{1,0:T(8,128)}) custom-call(bf16[64,384]{1,0:T(8,128)(2,1)S(1)} %get-tuple-element.56.after_ref.solve_ref, bf16[320,64]{1,0:T(8,128)(2,1)S(1)} %get-tuple-element.57.left_ref, bf16[320,10240]{1,0:T(8,128)(2,1)S(1)} %get-tuple-element.40.m_ref, ...), custom_call_target="tpu_custom_call", output_to_operand_aliasing={{0}: (4, {}), {1}: (5, {})} | custom-call | flops 8589934592 | bytes 1048576 | tf_op jit(solution)/shard_map/result/pallas_call | solution.py:500
  82.4 0.0 collective-permute-done.23.refs_0_
  82.4 1.6 %result.9 = (bf16[320,10240]{1,0:T(8,128)(2,1)}, f32[64,10240]{1,0:T(8,128)}, f32[8,128]{1,0:T(8,128)S(1)}) custom-call(bf16[64,384]{1,0:T(8,128)(2,1)S(1)} %get-tuple-element.56.after_ref.solve_ref, bf16[320,64]{1,0:T(8,128)(2,1)S(1)} %get-tuple-element.57.left_ref, ...), custom_call_target="tpu_custom_call", output_to_operand_aliasing={{0}: (4, {}), {1}: (5, {})} | custom-call | flops 8589934592 | bytes 1048576 | tf_op jit(solution)/shard_map/result/pallas_call | solution.py:500
  84.0 0.9 collective-permute-start.26
  84.8 0.0 collective-permute-done.20.value_ref
  84.8 0.1 collective-permute-start.24
  84.9 2.1 %result.10 = (bf16[320,10240]{1,0:T(8,128)(2,1)}, f32[64,10240]{1,0:T(8,128)}) custom-call(bf16[64,384]{1,0:T(8,128)(2,1)S(1)} %get-tuple-element.56.after_ref.solve_ref, bf16[320,64]{1,0:T(8,128)(2,1)S(1)} %get-tuple-element.57.left_ref, bf16[320,10240]{1,0:T(8,128)(2,1)S(1)} %get-tuple-element.40.m_ref, ...), custom_call_target="tpu_custom_call", output_to_operand_aliasing={{0}: (5, {}), {1}: (6, {})} | custom-call | flops 8589934592 | bytes 1048576 | tf_op jit(solution)/shard_map/result/pallas_call | solution.py:500
  87.0 0.0 collective-permute-done.24.refs_0_
  87.0 2.1 %result.11 = (bf16[320,10240]{1,0:T(8,128)(2,1)}, f32[64,10240]{1,0:T(8,128)}, f32[64,320]{1,0:T(8,128)}) custom-call(bf16[64,384]{1,0:T(8,128)(2,1)S(1)} %get-tuple-element.56.after_ref.solve_ref, bf16[320,64]{1,0:T(8,128)(2,1)S(1)} %get-tuple-element.57.left_ref, ...), custom_call_target="tpu_custom_call", output_to_operand_aliasing={{0}: (6, {}), {1}: (7, {})} | custom-call | flops 8589934592 | bytes 1048576 | tf_op jit(solution)/shard_map/result/pallas_call | solution.py:500
  (13 shorter events, 0.1 us)
Async XLA Ops:
  6.8 6.7 %collective-permute-start = (f32[160,128]{1,0:T(8,128)S(1)}, f32[160,128]{1,0:T(8,128)S(1)}, u32[]{:S(2)}, u32[]{:S(2)}) collective-permute-start(f32[160,128]{1,0:T(8,128)S(1)} %get-tuple-element.39), channel_id=1, source_target_pairs={{0,8},{1,33},{2,10},{3,35},{4,12},{5,37},{6,14},{7,39},{8,16},{9,4... | collective-permute-start | bytes 245768 | tf_op jit(solution)/shard_map/ppermute | solution.py:78
  9.4 4.2 %collective-permute-start.1 = (f32[160,128]{1,0:T(8,128)S(1)}, f32[160,128]{1,0:T(8,128)S(1)}, u32[]{:S(2)}, u32[]{:S(2)}) collective-permute-start(f32[160,128]{1,0:T(8,128)S(1)} %get-tuple-element.39), channel_id=1, source_target_pairs={{0,24},{1,97},{2,26},{3,99},{4,28},{5,101},{6,30},{7,103},{8,0},{9... | collective-permute-start | bytes 245768 | tf_op jit(solution)/shard_map/ppermute | solution.py:78
  11.6 5.1 %collective-permute-start.2 = (f32[160,128]{1,0:T(8,128)S(1)}, f32[160,128]{1,0:T(8,128)S(1)}, u32[]{:S(2)}, u32[]{:S(2)}) collective-permute-start(f32[160,128]{1,0:T(8,128)S(1)} %get-tuple-element.39), channel_id=1, source_target_pairs={{0,16},{1,65},{2,18},{3,67},{4,20},{5,69},{6,22},{7,71},{8,24},{9,... | collective-permute-start | bytes 245768 | tf_op jit(solution)/shard_map/ppermute | solution.py:78
  16.7 4.6 %collective-permute-start.3 = (f32[160,128]{1,0:T(8,128)S(1)}, f32[160,128]{1,0:T(8,128)S(1)}, u32[]{:S(2)}, u32[]{:S(2)}) collective-permute-start(f32[160,128]{1,0:T(8,128)S(1)} %add_add_fusion.a_ref), channel_id=1, source_target_pairs={{0,32},{1,9},{2,34},{3,11},{4,36},{5,13},{6,38},{7,15},{8,40},{9,1... | collective-permute-start | bytes 245768 | tf_op jit(solution)/shard_map/ppermute | solution.py:78
  17.7 3.6 %collective-permute-start.4 = (f32[160,128]{1,0:T(8,128)S(1)}, f32[160,128]{1,0:T(8,128)S(1)}, u32[]{:S(2)}, u32[]{:S(2)}) collective-permute-start(f32[160,128]{1,0:T(8,128)S(1)} %add_add_fusion.a_ref), channel_id=1, source_target_pairs={{0,96},{1,25},{2,98},{3,27},{4,100},{5,29},{6,102},{7,31},{8,104},... | collective-permute-start | bytes 245768 | tf_op jit(solution)/shard_map/ppermute | solution.py:78
  19.4 4.8 %collective-permute-start.5 = (f32[160,128]{1,0:T(8,128)S(1)}, f32[160,128]{1,0:T(8,128)S(1)}, u32[]{:S(2)}, u32[]{:S(2)}) collective-permute-start(f32[160,128]{1,0:T(8,128)S(1)} %add_add_fusion.a_ref), channel_id=1, source_target_pairs={{0,64},{1,17},{2,66},{3,19},{4,68},{5,21},{6,70},{7,23},{8,72},{9,... | collective-permute-start | bytes 245768 | tf_op jit(solution)/shard_map/ppermute | solution.py:78
  24.9 4.8 %collective-permute-start.6 = (f32[680,128]{1,0:T(8,128)S(1)}, f32[680,128]{1,0:T(8,128)S(1)}, u32[]{:S(2)}, u32[]{:S(2)}) collective-permute-start(f32[680,128]{1,0:T(8,128)S(1)} %get-tuple-element.43), channel_id=1, source_target_pairs={{0,1},{1,0},{2,3},{3,2},{4,5},{5,4},{6,7},{7,6},{8,9},{9,8},{10,11... | collective-permute-start | bytes 1044488 | tf_op jit(solution)/shard_map/ppermute | solution.py:83
  29.2 3.0 %collective-permute-start.7 = (f32[1920,128]{1,0:T(8,128)S(1)}, f32[1920,128]{1,0:T(8,128)S(1)}, u32[]{:S(2)}, u32[]{:S(2)}) collective-permute-start(f32[1920,128]{1,0:T(8,128)S(1)} %next_right.3.after_ref), channel_id=1, source_target_pairs={{0,1},{1,0},{2,3},{3,2},{4,5},{5,4},{6,7},{7,6},{8,9},{9,8},{10,11... | collective-permute-start | bytes 2949128 | tf_op jit(solution)/shard_map/ppermute | solution.py:83
  29.8 7.8 %collective-permute-start.10 = (f32[640,128]{1,0:T(8,128)S(1)}, f32[640,128]{1,0:T(8,128)S(1)}, u32[]{:S(2)}, u32[]{:S(2)}) collective-permute-start(f32[640,128]{1,0:T(8,128)S(1)} %get-tuple-element.48), channel_id=1, source_target_pairs={{0,16},{1,65},{2,18},{3,67},{4,20},{5,69},{6,22},{7,71},{8,24},{9,... | collective-permute-start | bytes 983048 | tf_op jit(solution)/shard_map/ppermute | solution.py:78
  32.5 8.7 %collective-permute-start.8 = (f32[640,128]{1,0:T(8,128)S(1)}, f32[640,128]{1,0:T(8,128)S(1)}, u32[]{:S(2)}, u32[]{:S(2)}) collective-permute-start(f32[640,128]{1,0:T(8,128)S(1)} %get-tuple-element.46), channel_id=1, source_target_pairs={{0,8},{1,33},{2,10},{3,35},{4,12},{5,37},{6,14},{7,39},{8,16},{9,4... | collective-permute-start | bytes 983048 | tf_op jit(solution)/shard_map/ppermute | solution.py:78
  33.3 7.9 %collective-permute-start.9 = (f32[640,128]{1,0:T(8,128)S(1)}, f32[640,128]{1,0:T(8,128)S(1)}, u32[]{:S(2)}, u32[]{:S(2)}) collective-permute-start(f32[640,128]{1,0:T(8,128)S(1)} %get-tuple-element.47), channel_id=1, source_target_pairs={{0,24},{1,97},{2,26},{3,99},{4,28},{5,101},{6,30},{7,103},{8,0},{9... | collective-permute-start | bytes 983048 | tf_op jit(solution)/shard_map/ppermute | solution.py:78
  41.2 4.9 %collective-permute-start.11 = (f32[200,128]{1,0:T(8,128)S(1)}, f32[200,128]{1,0:T(8,128)S(1)}, u32[]{:S(2)}, u32[]{:S(2)}) collective-permute-start(f32[200,128]{1,0:T(8,128)S(1)} %get-tuple-element.51), channel_id=1, source_target_pairs={{0,32},{1,3},{2,34},{3,5},{4,36},{5,7},{6,38},{7,1},{8,40},{9,11},... | collective-permute-start | bytes 307208 | tf_op jit(solution)/shard_map/ppermute | solution.py:78
  42.6 3.8 %collective-permute-start.12 = (f32[200,128]{1,0:T(8,128)S(1)}, f32[200,128]{1,0:T(8,128)S(1)}, u32[]{:S(2)}, u32[]{:S(2)}) collective-permute-start(f32[200,128]{1,0:T(8,128)S(1)} %get-tuple-element.52), channel_id=1, source_target_pairs={{0,96},{1,7},{2,98},{3,1},{4,100},{5,3},{6,102},{7,5},{8,104},{9,1... | collective-permute-start | bytes 307208 | tf_op jit(solution)/shard_map/ppermute | solution.py:78
  44.1 5.0 %collective-permute-start.13 = (f32[200,128]{1,0:T(8,128)S(1)}, f32[200,128]{1,0:T(8,128)S(1)}, u32[]{:S(2)}, u32[]{:S(2)}) collective-permute-start(f32[200,128]{1,0:T(8,128)S(1)} %get-tuple-element.53), channel_id=1, source_target_pairs={{0,64},{1,5},{2,66},{3,7},{4,68},{5,1},{6,70},{7,3},{8,72},{9,13},... | collective-permute-start | bytes 307208 | tf_op jit(solution)/shard_map/ppermute | solution.py:78
  49.2 4.8 %collective-permute-start.14 = (f32[200,128]{1,0:T(8,128)S(1)}, f32[200,128]{1,0:T(8,128)S(1)}, u32[]{:S(2)}, u32[]{:S(2)}) collective-permute-start(f32[200,128]{1,0:T(8,128)S(1)} %across.2.a_ref), channel_id=1, source_target_pairs={{0,2},{1,9},{2,4},{3,11},{4,6},{5,13},{6,0},{7,15},{8,10},{9,17},{... | collective-permute-start | bytes 307208 | tf_op jit(solution)/shard_map/ppermute | solution.py:78
  49.3 5.4 %collective-permute-start.15 = (f32[200,128]{1,0:T(8,128)S(1)}, f32[200,128]{1,0:T(8,128)S(1)}, u32[]{:S(2)}, u32[]{:S(2)}) collective-permute-start(f32[200,128]{1,0:T(8,128)S(1)} %across.2.a_ref), channel_id=1, source_target_pairs={{0,6},{1,25},{2,0},{3,27},{4,2},{5,29},{6,4},{7,31},{8,14},{9,1},{... | collective-permute-start | bytes 307208 | tf_op jit(solution)/shard_map/ppermute | solution.py:78
  52.0 5.0 %collective-permute-start.16 = (f32[200,128]{1,0:T(8,128)S(1)}, f32[200,128]{1,0:T(8,128)S(1)}, u32[]{:S(2)}, u32[]{:S(2)}) collective-permute-start(f32[200,128]{1,0:T(8,128)S(1)} %across.2.a_ref), channel_id=1, source_target_pairs={{0,4},{1,17},{2,6},{3,19},{4,0},{5,21},{6,2},{7,23},{8,12},{9,25},... | collective-permute-start | bytes 307208 | tf_op jit(solution)/shard_map/ppermute | solution.py:78
  57.1 5.6 %collective-permute-start.17 = (f32[160,128]{1,0:T(8,128)S(1)}, f32[160,128]{1,0:T(8,128)S(1)}, u32[]{:S(2)}, u32[]{:S(2)}) collective-permute-start(f32[160,128]{1,0:T(8,128)S(1)} %get-tuple-element.58.a_ref), channel_id=1, source_target_pairs={{0,32},{1,3},{2,34},{3,5},{4,36},{5,7},{6,38},{7,1},{8,40},{9,11},... | collective-permute-start | bytes 245768 | tf_op jit(solution)/shard_map/ppermute | solution.py:78
  57.6 5.1 %collective-permute-start.18 = (f32[160,128]{1,0:T(8,128)S(1)}, f32[160,128]{1,0:T(8,128)S(1)}, u32[]{:S(2)}, u32[]{:S(2)}) collective-permute-start(f32[160,128]{1,0:T(8,128)S(1)} %get-tuple-element.58.a_ref), channel_id=1, source_target_pairs={{0,96},{1,7},{2,98},{3,1},{4,100},{5,3},{6,102},{7,5},{8,104},{9,1... | collective-permute-start | bytes 245768 | tf_op jit(solution)/shard_map/ppermute | solution.py:78
  60.0 4.8 %collective-permute-start.19 = (f32[160,128]{1,0:T(8,128)S(1)}, f32[160,128]{1,0:T(8,128)S(1)}, u32[]{:S(2)}, u32[]{:S(2)}) collective-permute-start(f32[160,128]{1,0:T(8,128)S(1)} %get-tuple-element.58.a_ref), channel_id=1, source_target_pairs={{0,64},{1,5},{2,66},{3,7},{4,68},{5,1},{6,70},{7,3},{8,72},{9,13},... | collective-permute-start | bytes 245768 | tf_op jit(solution)/shard_map/ppermute | solution.py:78
  64.9 14.8 %collective-permute-start.21 = (f32[640,128]{1,0:T(8,128)S(1)}, f32[640,128]{1,0:T(8,128)S(1)}, u32[]{:S(2)}, u32[]{:S(2)}) collective-permute-start(f32[640,128]{1,0:T(8,128)S(1)} %assemble.1.value_ref), channel_id=1, source_target_pairs={{0,16},{1,65},{2,18},{3,67},{4,20},{5,69},{6,22},{7,71},{8,24},{9,... | collective-permute-start | bytes 983048 | tf_op jit(solution)/shard_map/ppermute | solution.py:78
  66.5 17.5 %collective-permute-start.25 = (f32[640,128]{1,0:T(8,128)S(1)}, f32[640,128]{1,0:T(8,128)S(1)}, u32[]{:S(2)}, u32[]{:S(2)}) collective-permute-start(f32[640,128]{1,0:T(8,128)S(1)} %assemble.1.value_ref), channel_id=1, source_target_pairs={{0,24},{1,97},{2,26},{3,99},{4,28},{5,101},{6,30},{7,103},{8,0},{9... | collective-permute-start | bytes 983048 | tf_op jit(solution)/shard_map/ppermute | solution.py:78
  67.4 17.4 %collective-permute-start.20 = (f32[640,128]{1,0:T(8,128)S(1)}, f32[640,128]{1,0:T(8,128)S(1)}, u32[]{:S(2)}, u32[]{:S(2)}) collective-permute-start(f32[640,128]{1,0:T(8,128)S(1)} %assemble.1.value_ref), channel_id=1, source_target_pairs={{0,8},{1,33},{2,10},{3,35},{4,12},{5,37},{6,14},{7,39},{8,16},{9,4... | collective-permute-start | bytes 983048 | tf_op jit(solution)/shard_map/ppermute | solution.py:78
  67.9 10.2 %collective-permute-start.22 = (f32[640,128]{1,0:T(8,128)S(1)}, f32[640,128]{1,0:T(8,128)S(1)}, u32[]{:S(2)}, u32[]{:S(2)}) collective-permute-start(f32[640,128]{1,0:T(8,128)S(1)} %again.1.refs_0_), channel_id=1, source_target_pairs={{0,1},{1,0},{2,3},{3,2},{4,5},{5,4},{6,7},{7,6},{8,9},{9,8},{10,11... | collective-permute-start | bytes 983048 | tf_op jit(solution)/shard_map/ppermute | solution.py:83
  79.7 2.6 %collective-permute-start.23 = (f32[640,128]{1,0:T(8,128)S(1)}, f32[640,128]{1,0:T(8,128)S(1)}, u32[]{:S(2)}, u32[]{:S(2)}) collective-permute-start(f32[640,128]{1,0:T(8,128)S(1)} %tie.3.refs_0_), channel_id=1, source_target_pairs={{0,1},{1,0},{2,3},{3,2},{4,5},{5,4},{6,7},{7,6},{8,9},{9,8},{10,11... | collective-permute-start | bytes 983048 | tf_op jit(solution)/shard_map/ppermute | solution.py:83
  84.0 3.1 %collective-permute-start.26 = (f32[640,128]{1,0:T(8,128)S(1)}, f32[640,128]{1,0:T(8,128)S(1)}, u32[]{:S(2)}, u32[]{:S(2)}) collective-permute-start(f32[640,128]{1,0:T(8,128)S(1)} %tie.5.refs_1_), channel_id=1, source_target_pairs={{0,1},{1,0},{2,3},{3,2},{4,5},{5,4},{6,7},{7,6},{8,9},{9,8},{10,11... | collective-permute-start | bytes 983048 | tf_op jit(solution)/shard_map/ppermute | solution.py:83
  84.8 2.2 %collective-permute-start.24 = (f32[640,128]{1,0:T(8,128)S(1)}, f32[640,128]{1,0:T(8,128)S(1)}, u32[]{:S(2)}, u32[]{:S(2)}) collective-permute-start(f32[640,128]{1,0:T(8,128)S(1)} %tie.4.refs_0_), channel_id=1, source_target_pairs={{0,1},{1,0},{2,3},{3,2},{4,5},{5,4},{6,7},{7,6},{8,9},{9,8},{10,11... | collective-permute-start | bytes 983048 | tf_op jit(solution)/shard_map/ppermute | solution.py:83
